TPU v7x, 32 devices: a whole 2x2x4 slice. The times are simulated.
32 devices in a mesh: seq: 2 (over x), exp: 16 (over z, y, core).
Axes of the slice: x: 2, y: 2, z: 4, core: 2. Of those that a mesh axis runs over, the one named last changes fastest.
Arguments:
- tokens: bfloat16 [4096, 4096], P(('seq', 'exp')), may hold values from -6 to 6
- cotangent: bfloat16 [4096, 4096], P(('seq', 'exp')), may hold values from -3 to 3
- factors: bfloat16 [16, 3, 4, 1024, 128], P('exp', None, None, 'seq'), may hold values from -0.09375 to 0.09375
- mix: float32 [16, 3, 4, 4, 4], P('exp'), may hold values from -3 to 3
- selection: int32 [16, 4, 64], P('exp', 'seq'), may hold values from 0 to 1023, as said below
- scores: int32 [16, 4, 64], P('exp', 'seq'), may hold values from -192 to 191
Outputs:
- token_grad: bfloat16 [4096, 4096], P(('seq', 'exp'))
- factor_grad: float32 [16, 3, 4, 1024, 128], P('exp', None, None, 'seq')
- mix_grad: float32 [16, 3, 4, 4, 4], P('exp')
- gate_grad: float32 [16, 4, 64], P('exp', 'seq')
Inputs may be any that keep to these rules, and one draw needn't show every extreme that they name: `selection`: for every expert and block the 64 positions are distinct and ascending; at most 12 of them lie among the 128 positions of one device (aligned runs of 128), and for every expert and block some device holds exactly 12 of them.
All inputs are finite; a program needn't handle non-finite values.
Results may differ from a plain program's by a relative error of at most 0.015.
Values may be sent and summed in bfloat16 or wider, within the bound.
No kernel may reach another device: no remote copies, remote signals or barrier semaphores. Data moves between devices by JAX's collectives and lax.ppermute only.
A program may use at most 64 MiB of HBM per device.

v0:
```python
import jax
import jax.numpy as jnp
from jax import lax
from jax.sharding import PartitionSpec as P

C = 64
PICKS = 1


PRECISE = lax.Precision.HIGHEST


def expand(mixing, factor_set):
    count_f, rows_f, cols_f = factor_set.shape
    total = jnp.zeros((count_f, rows_f, count_f, cols_f), jnp.float32)
    for number in range(count_f):
        total = (
            total
            + mixing[number][:, None, :, None]
            * factor_set[number].astype(jnp.float32)[None, :, None, :]
        )
    return total.reshape(count_f * rows_f, count_f * cols_f).astype(jnp.bfloat16)


def factored_grads(mixing, factor_set, left, right):
    count_f, rows_f, cols_f = factor_set.shape
    slots = left.shape[0]
    left_view = left.reshape(slots, count_f, rows_f)
    right_view = right.reshape(slots, count_f, cols_f)
    mixed_right = jnp.einsum(
        "iab,rbq->riaq", mixing, right_view.astype(jnp.float32), precision=PRECISE
    )
    factor_out = jnp.einsum(
        "rap,riaq->ipq", left_view.astype(jnp.float32), mixed_right, precision=PRECISE
    )
    through = jnp.einsum("rap,ipq->riaq", left_view, factor_set, preferred_element_type=jnp.float32)
    mixing_out = jnp.einsum(
        "riaq,rbq->iab", through, right_view.astype(jnp.float32), precision=PRECISE
    )
    return (factor_out, mixing_out)


def silu_parts(preact):
    sigmoid_val = jax.nn.sigmoid(preact)
    return (preact * sigmoid_val, sigmoid_val + preact * sigmoid_val * (1.0 - sigmoid_val))


def contract(left, right):
    return lax.dot_general(
        left, right, (((0,), (0,)), ((), ())), preferred_element_type=jnp.float32
    )


def transposed(left, kernel):
    return lax.dot_general(
        left, kernel, (((1,), (1,)), ((), ())), preferred_element_type=jnp.float32
    )


def shards(tokens, cotangent, factors, mix, selection, scores):
    peer_count = lax.axis_size("exp")
    own_rows = tokens.shape[0]
    model_width = tokens.shape[1]
    slot_cap = 3 * PICKS * own_rows // (2 * peer_count)
    block_len = peer_count * C // PICKS
    slot_total = peer_count * slot_cap
    chosen = selection[0]
    position = (jnp.arange(chosen.shape[0], dtype=jnp.int32)[:, None] * block_len + chosen).reshape(
        -1
    )
    owner_idx = position // own_rows
    local_row = position % own_rows
    row_count = position.shape[0]
    earlier = jnp.sum((owner_idx[None, :] < owner_idx[:, None]).astype(jnp.int32), axis=1)
    slot_of = owner_idx * slot_cap + jnp.arange(row_count, dtype=jnp.int32) - earlier
    slot_hits = slot_of[:, None] == jnp.arange(slot_total, dtype=jnp.int32)[None, :]
    wanted = jnp.sum(jnp.where(slot_hits, local_row[:, None] + 1, 0), axis=0) - 1
    requested = lax.all_to_all(
        wanted.reshape(peer_count, slot_cap), "exp", split_axis=0, concat_axis=0, tiled=True
    )
    pick_rows = (
        requested.reshape(-1)[:, None] == jnp.arange(own_rows, dtype=jnp.int32)[None, :]
    ).astype(jnp.bfloat16)
    send_rows = (
        jnp.dot(pick_rows, tokens, preferred_element_type=jnp.float32)
        .astype(jnp.bfloat16)
        .reshape(peer_count, slot_cap, model_width)
    )
    send_grads = (
        jnp.dot(pick_rows, cotangent, preferred_element_type=jnp.float32)
        .astype(jnp.bfloat16)
        .reshape(peer_count, slot_cap, model_width)
    )
    gathered = lax.all_gather(factors, "seq", axis=3, tiled=True)[0]
    kernels = [expand(mix[0, number], gathered[number]) for number in range(3)]
    gate_val = jax.nn.sigmoid(scores[0].reshape(-1).astype(jnp.float32) / 64.0)
    got_rows, got_grads = (
        lax.all_to_all(send_rows, "exp", split_axis=0, concat_axis=0, tiled=True),
        lax.all_to_all(send_grads, "exp", split_axis=0, concat_axis=0, tiled=True),
    )
    sel_rows = jnp.take(got_rows.reshape(slot_total, model_width), slot_of, axis=0)
    pre_gate = jnp.dot(sel_rows, kernels[0], preferred_element_type=jnp.float32)
    pre_up = jnp.dot(sel_rows, kernels[1], preferred_element_type=jnp.float32)
    gate_act, gate_slope = silu_parts(pre_gate)
    hidden = (gate_act * pre_up).astype(jnp.bfloat16)
    expert_out = transposed(hidden, kernels[2])
    sel_grads = jnp.take(got_grads.reshape(slot_total, model_width), slot_of, axis=0)
    gate_in = jnp.sum(sel_grads.astype(jnp.float32) * expert_out, axis=1)
    gate_grad = gate_in * gate_val * (1.0 - gate_val)
    out_grad = (gate_val[:, None] * sel_grads.astype(jnp.float32)).astype(jnp.bfloat16)
    hidden_grad = jnp.dot(out_grad, kernels[2], preferred_element_type=jnp.float32)
    gate_pre = (hidden_grad * pre_up * gate_slope).astype(jnp.bfloat16)
    up_pre = (hidden_grad * gate_act).astype(jnp.bfloat16)
    row_grad = (transposed(gate_pre, kernels[0]) + transposed(up_pre, kernels[1])).astype(
        jnp.bfloat16
    )
    back_rows = (
        contract(slot_hits.astype(jnp.bfloat16), row_grad)
        .astype(jnp.bfloat16)
        .reshape(peer_count, slot_cap, model_width)
    )
    returned = lax.all_to_all(back_rows, "exp", split_axis=0, concat_axis=0, tiled=True)
    token_grad = contract(pick_rows, returned.reshape(slot_total, model_width)).astype(jnp.bfloat16)
    operand_pairs = [(sel_rows, gate_pre), (sel_rows, up_pre), (out_grad, hidden)]
    projected = [
        factored_grads(
            mix[0, number], gathered[number], operand_pairs[number][0], operand_pairs[number][1]
        )
        for number in range(3)
    ]
    factor_part = jnp.stack([item[0] for item in projected])[None]
    mix_part = jnp.stack([item[1] for item in projected])[None]
    factor_grad = lax.psum_scatter(
        factor_part.astype(jnp.bfloat16), "seq", scatter_dimension=3, tiled=True
    ).astype(jnp.float32)
    mix_grad = lax.psum(mix_part, "seq")
    return (token_grad, factor_grad, mix_grad, gate_grad.reshape(1, -1, C))


def solution(mesh):
    return jax.shard_map(
        shards,
        mesh=mesh,
        in_specs=(
            P(("seq", "exp"), None),
            P(("seq", "exp"), None),
            P("exp", None, None, "seq", None),
            P("exp", None, None, None, None),
            P("exp", "seq", None),
            P("exp", "seq", None),
        ),
        out_specs=(
            P(("seq", "exp"), None),
            P("exp", None, None, "seq", None),
            P("exp", None, None, None, None),
            P("exp", "seq", None),
        ),
        check_vma=False,
    )
```

profile of v0, /device:TPU:13, one launch (start us, length us, event | category | flops | bytes accessed | tf_op | source)
XLA Modules:
  0.0 261.7 jit_solution(8252747110568266650)
XLA Ops:
  8.6 10.2 %all_to_all.21 = s32[16,1,12]{2,1,0:T(1,128)S(1)} all-to-all(s32[16,1,12]{2,1,0:T(1,128)S(1)} %bitcast.250), channel_id=1, replica_groups=mesh['seq'=2,'exp'=16] {'exp'}, dimensions={0} | all-to-all | bytes 1536 | tf_op jit(solution)/shard_map/all_to_all | solution.py:78
  22.2 6.2 %all-to-all-start.2 = ((bf16[16,12,4096]{2,1,0:T(8,128)(2,1)}), bf16[16,12,4096]{2,1,0:T(8,128)(2,1)S(1)}, u32[]{:S(2)}, u32[]{:S(2)}) async-start(bf16[16,12,4096]{2,1,0:T(8,128)(2,1)} %reshape.423), calls=%async_computation.2 | async-start | bytes 4194304 | tf_op jit(solution)/shard_map/all_to_all | solution.py:98
  30.2 3.4 %reshape.421 = bf16[16,12,4096]{2,1,0:T(8,128)(2,1)} reshape(bf16[192,4096]{1,0:T(8,128)(2,1)} %convolution_convert_fusion.2) | data formatting | bytes 3145728 | tf_op jit(solution)/shard_map/reshape | solution.py:92
  33.7 42.2 %all-to-all-done.2 = bf16[16,12,4096]{2,1,0:T(8,128)(2,1)S(1)} async-done(((bf16[16,12,4096]{2,1,0:T(8,128)(2,1)}), bf16[16,12,4096]{2,1,0:T(8,128)(2,1)S(1)}, u32[]{:S(2)}, u32[]{:S(2)}) %all-to-all-start.2) | async-done | bytes 1572896 | tf_op jit(solution)/shard_map/all_to_all | solution.py:98
  75.9 4.9 %all-to-all-start.1 = ((bf16[16,12,4096]{2,1,0:T(8,128)(2,1)}), bf16[16,12,4096]{2,1,0:T(8,128)(2,1)}, u32[]{:S(2)}, u32[]{:S(2)}) async-start(bf16[16,12,4096]{2,1,0:T(8,128)(2,1)} %reshape.421), calls=%async_computation.1 | async-start | bytes 4194304 | tf_op jit(solution)/shard_map/all_to_all | solution.py:99
  81.6 2.5 reshape.424
  86.2 42.3 %all-to-all-done.1 = bf16[16,12,4096]{2,1,0:T(8,128)(2,1)} async-done(((bf16[16,12,4096]{2,1,0:T(8,128)(2,1)}), bf16[16,12,4096]{2,1,0:T(8,128)(2,1)}, u32[]{:S(2)}, u32[]{:S(2)}) %all-to-all-start.1) | async-done | bytes 1572896 | tf_op jit(solution)/shard_map/all_to_all | solution.py:99
  128.6 2.5 reshape.422
  134.6 3.3 %fusion.49 = (f32[1024,128]{1,0:T(8,128)S(1)}, f32[1024,128]{1,0:T(8,128)S(1)}, f32[1024,128]{1,0:T(8,128)S(1)}, f32[1024,128]{1,0:T(8,128)S(1)}, f32[1024,128]{...) fusion(bf16[1,3,4,1024,128]{4,3,2,1,0:T(8,128)(2,1)} %all-gathe, ...), kind=kLoop, calls=%fused_computation.89 | loop fusion | flops 1572864 | bytes 9437184 | tf_op jit(solution)/shard_map/convert_element_type | solution.py:20
  138.0 9.1 %add_convert_fusion = (bf16[4,1024,4,128]{3,2,1,0:T(4,128)(2,1)S(1)}, bf16[4,1024,4,128]{3,2,1,0:T(4,128)(2,1)S(1)}) fusion(f32[1024,128]{1,0:T(8,128)S(1)} %get-tuple-element.28, f32[4,4]{1,0:T(4,128)S(1)} %get-tuple-element.42, f32[1024,128]{1,0:T(8,128)S(1)} %get-tuple-element.29, f32[4,4]{1,0:T(4,128)S(1)} %get-tuple-element.43, ...), kind=kLoop, calls=%fused_computation.2 | loop fusion | flops 33554432 | bytes 12583424 | tf_op jit(solution)/shard_map/convert.21
  150.5 5.9 %add_convert_fusion.2 = bf16[4,1024,4,128]{3,2,1,0:T(4,128)(2,1)S(1)} fusion(f32[1024,128]{1,0:T(8,128)S(1)} %get-tuple-element.36, f32[4,4]{1,0:T(4,128)S(1)} %get-tuple-element.50, f32[1024,128]{1,0:T(8,128)} %get-tuple-element.37, f32[4,4]{1,0:T(4,128)S(1)} %get-tuple-element.51, f32[1024,128]{1,0:T(8,128)} %get-tuple-element.38, ...), kind=kLoop, calls=%fused_computation.4 | loop fusion | flops 16777216 | bytes 6291712 | tf_op jit(solution)/shard_map/convert.23
  162.1 3.7 %multiply_convert_fusion.1 = (bf16[128,512]{1,0:T(8,128)(2,1)S(1)}, bf16[128,512]{1,0:T(8,128)(2,1)}) fusion(f32[128,512]{1,0:T(8,128)} %copy-done.14, f32[128,512]{1,0:T(8,128)} %get-tuple-element.54, bf16[128,4096]{1,0:T(8,128)(2,1)S(1)} %fusion.17, bf16[512,8,4,128]{3,2,1,0:T(4,128)(2,1)} %bitcast.246), kind=kOutput, calls=%fused_computation.91 | convolution fusion | flops 537657344 | bytes 6029312 | tf_op jit(solution)/shard_map/dot_general | solution.py:111
  165.8 2.6 %convolution_bitcast_fusion.4 = f32[128,4,4,128]{3,2,1,0:T(4,128)} fusion(bf16[128,4,128,1]{2,1,0,3:T(4,128)(2,1)S(1)} %reshape.474, f32[1,3,4,4,4]{4,3,2,1,0:T(4,128)} %param.11), kind=kOutput, calls=%fused_computation.41 | convolution fusion | flops 12582912 | bytes 1187840 | tf_op jit(solution)/shard_map/iab,rbq->riaq/dot_general | solution.py:30
  171.0 3.2 %fusion.21 = bf16[1,1,4,1024,128]{3,4,2,1,0:T(8,128)(2,1)S(1)} fusion(f32[128,4,4,128]{3,2,1,0:T(4,128)} %convolution_bitcast_fusion.4, bf16[16,4,8,1024]{3,2,1,0:T(8,128)(2,1)S(1)} %bitcast.238), kind=kOutput, calls=%fused_computation.35 | convolution fusion | flops 3221749760 | bytes 3145728 | tf_op jit(solution)/shard_map/rap,riaq->ipq/dot_general | solution.py:33
  180.2 5.1 %fusion.1 = f32[128,4096]{1,0:T(8,128)} fusion(bf16[128,512]{1,0:T(8,128)(2,1)S(1)} %copy-done.11, bf16[512,8,4,128]{3,2,1,0:T(4,128)(2,1)} %bitcast.243), kind=kOutput, calls=%fused_computation.12 | convolution fusion | flops 536870912 | bytes 6422528 | tf_op jit(solution)/shard_map/dot_general | solution.py:55
  185.3 7.2 %convolution_convert_fusion = bf16[192,4096]{1,0:T(8,128)(2,1)} fusion(f32[128,4096]{1,0:T(8,128)} %fusion.1, bf16[128,512]{1,0:T(8,128)(2,1)S(1)} %get-tuple-element.39, bf16[512,8,4,128]{3,2,1,0:T(4,128)(2,1)} %bitcast.241, s32[128]{0:T(128)S(1)} %get-tuple-element.24), kind=kOutput, calls=%fused_computation.5 | convolution fusion | flops 740057088 | bytes 7995904 | tf_op jit(solution)/shard_map/dot_general | solution.py:49
  192.5 3.4 %reshape.425 = bf16[16,12,4096]{2,1,0:T(8,128)(2,1)} reshape(bf16[192,4096]{1,0:T(8,128)(2,1)} %convolution_convert_fusion) | data formatting | bytes 3145728 | tf_op jit(solution)/shard_map/reshape | solution.py:120
  195.9 4.3 %all-to-all-start.3 = ((bf16[16,12,4096]{2,1,0:T(8,128)(2,1)}), bf16[16,12,4096]{2,1,0:T(8,128)(2,1)}, u32[]{:S(2)}, u32[]{:S(2)}) async-start(bf16[16,12,4096]{2,1,0:T(8,128)(2,1)} %reshape.425), calls=%async_computation.3 | async-start | bytes 4194304 | tf_op jit(solution)/shard_map/all_to_all | solution.py:122
  204.0 2.2 convolution_bitcast_fusion.6
  209.8 2.2 convolution_bitcast_fusion.8
  212.0 8.0 %psum.7 = f32[1,3,4,4,4]{4,3,2,1,0:T(4,128)} all-reduce(f32[1,3,4,4,4]{4,3,2,1,0:T(4,128)S(1)} %maximum_bitcast_fusion), channel_id=1, replica_groups=mesh['seq'=2,'exp'=16] {'seq'}, use_global_device_ids=true, to_apply=%region_3.5 | all-reduce | flops 192 | bytes 1536 | tf_op jit(solution)/shard_map/psum | solution.py:136
  220.0 27.6 %all-to-all-done.3 = bf16[16,12,4096]{2,1,0:T(8,128)(2,1)} async-done(((bf16[16,12,4096]{2,1,0:T(8,128)(2,1)}), bf16[16,12,4096]{2,1,0:T(8,128)(2,1)}, u32[]{:S(2)}, u32[]{:S(2)}) %all-to-all-start.3) | async-done | bytes 1572896 | tf_op jit(solution)/shard_map/all_to_all | solution.py:122
  247.7 2.5 reshape.426
  251.7 3.1 %copy.54 = f32[1,3,4,512,128]{4,3,2,1,0:T(8,128)} copy(bf16[1,3,4,512,128]{3,4,2,1,0:T(8,128)(2,1)} %reduce-scatter.2.cloned.1.call-done) | data formatting | bytes 4718592
  (82 shorter events, 39.6 us)
Async XLA Ops:
  7.2 12.9 %copy-start = (bf16[128,4096]{1,0:T(8,128)(2,1)S(1)}, bf16[128,4096]{1,0:T(8,128)(2,1)}, u32[]{:S(2)}) copy-start(bf16[128,4096]{1,0:T(8,128)(2,1)} %param.8) | copy-start | bytes 3145732
  20.7 7.8 %copy-start.8 = (bf16[128,4096]{1,0:T(8,128)(2,1)S(1)}, bf16[128,4096]{1,0:T(8,128)(2,1)}, u32[]{:S(2)}) copy-start(bf16[128,4096]{1,0:T(8,128)(2,1)} %param.9) | copy-start | bytes 3145732
  22.2 53.7 %all-to-all-start.2 = ((bf16[16,12,4096]{2,1,0:T(8,128)(2,1)}), bf16[16,12,4096]{2,1,0:T(8,128)(2,1)S(1)}, u32[]{:S(2)}, u32[]{:S(2)}) async-start(bf16[16,12,4096]{2,1,0:T(8,128)(2,1)} %reshape.423), calls=%async_computation.2 | async-start | bytes 4194304 | tf_op jit(solution)/shard_map/all_to_all | solution.py:98
  30.2 51.4 %copy-start.12 = (f32[1,3,4,4,4]{4,3,2,1,0:T(4,128)S(1)}, f32[1,3,4,4,4]{4,3,2,1,0:T(4,128)}, u32[]{:S(2)}) copy-start(f32[1,3,4,4,4]{4,3,2,1,0:T(4,128)} %param.11) | copy-start | bytes 2308
  75.9 5.7 %copy-start.4 = (bf16[16,12,4096]{2,1,0:T(8,128)(2,1)}, bf16[16,12,4096]{2,1,0:T(8,128)(2,1)S(1)}, u32[]{:S(2)}) copy-start(bf16[16,12,4096]{2,1,0:T(8,128)(2,1)S(1)} %all-to-all-done.2) | copy-start | bytes 4718596
  75.9 52.7 %all-to-all-start.1 = ((bf16[16,12,4096]{2,1,0:T(8,128)(2,1)}), bf16[16,12,4096]{2,1,0:T(8,128)(2,1)}, u32[]{:S(2)}, u32[]{:S(2)}) async-start(bf16[16,12,4096]{2,1,0:T(8,128)(2,1)} %reshape.421), calls=%async_computation.1 | async-start | bytes 4194304 | tf_op jit(solution)/shard_map/all_to_all | solution.py:99
  80.8 53.9 %all-gather.2.cloned.1.call-start = ((), (), s32[]{:S(2)}) async-start(), calls=%async_computation.5 | async-start | bytes 4718592 | tf_op jit(solution)/shard_map/all_gather | solution.py:94
  81.5 170.2 %reduce-scatter.2.cloned.1.call-start = ((), (), s32[]{:S(2)}) async-start(), calls=%async_computation.6 | async-start | bytes 4718592 | tf_op jit(solution)/shard_map/reduce_scatter | solution.py:133
  147.0 3.4 %copy-start.2 = (bf16[4,1024,4,128]{3,2,1,0:T(4,128)(2,1)}, bf16[4,1024,4,128]{3,2,1,0:T(4,128)(2,1)S(1)}, u32[]{:S(2)}) copy-start(bf16[4,1024,4,128]{3,2,1,0:T(4,128)(2,1)S(1)} %get-tuple-element.56) | copy-start | bytes 12582916
  147.0 3.4 %copy-start.3 = (bf16[4,1024,4,128]{3,2,1,0:T(4,128)(2,1)}, bf16[4,1024,4,128]{3,2,1,0:T(4,128)(2,1)S(1)}, u32[]{:S(2)}) copy-start(bf16[4,1024,4,128]{3,2,1,0:T(4,128)(2,1)S(1)} %get-tuple-element.55) | copy-start | bytes 12582916
  147.8 1.2 copy-start.14
  150.5 7.9 %copy-start.6 = (bf16[128,4096]{1,0:T(8,128)(2,1)S(1)}, bf16[128,4096]{1,0:T(8,128)(2,1)}, u32[]{:S(2)}) copy-start(bf16[128,4096]{1,0:T(8,128)(2,1)} %gather_fusion) | copy-start | bytes 3145732
  156.4 2.0 copy-start.5
  156.4 3.7 %copy-start.13 = (s32[1,2,64]{2,1,0:T(2,128)S(1)}, s32[1,2,64]{2,1,0:T(2,128)}, u32[]{:S(2)}) copy-start(s32[1,2,64]{2,1,0:T(2,128)} %param.13) | copy-start | bytes 1540
  165.8 2.7 %copy-start.9 = (bf16[128,4,128,1]{2,1,0,3:T(4,128)(2,1)}, bf16[128,4,128,1]{2,1,0,3:T(4,128)(2,1)S(1)}, u32[]{:S(2)}) copy-start(bf16[128,4,128,1]{2,1,0,3:T(4,128)(2,1)S(1)} %reshape.474) | copy-start | bytes 393220
  178.2 2.0 copy-start.11
  195.9 51.8 %all-to-all-start.3 = ((bf16[16,12,4096]{2,1,0:T(8,128)(2,1)}), bf16[16,12,4096]{2,1,0:T(8,128)(2,1)}, u32[]{:S(2)}, u32[]{:S(2)}) async-start(bf16[16,12,4096]{2,1,0:T(8,128)(2,1)} %reshape.425), calls=%async_computation.3 | async-start | bytes 4194304 | tf_op jit(solution)/shard_map/all_to_all | solution.py:122
  201.9 4.3 %copy-start.7 = (bf16[1,3,4,1024,128]{4,3,2,1,0:T(8,128)(2,1)S(1)}, bf16[1,3,4,1024,128]{4,3,2,1,0:T(8,128)(2,1)}, u32[]{:S(2)}) copy-start(bf16[1,3,4,1024,128]{4,3,2,1,0:T(8,128)(2,1)} %all-gather.2.cloned.1.call-done) | copy-start | bytes 9437188
  201.9 5.0 %copy-start.10 = (bf16[128,4,128,1]{2,1,0,3:T(4,128)(2,1)S(1)}, bf16[128,4,128,1]{2,1,0,3:T(4,128)(2,1)}, u32[]{:S(2)}) copy-start(bf16[128,4,128,1]{2,1,0,3:T(4,128)(2,1)} %copy-done.9) | copy-start | bytes 393220
  247.7 7.1 %copy-start.1 = (bf16[128,4096]{1,0:T(8,128)(2,1)S(1)}, bf16[128,4096]{1,0:T(8,128)(2,1)}, u32[]{:S(2)}) copy-start(bf16[128,4096]{1,0:T(8,128)(2,1)} %param.8) | copy-start | bytes 3145732
Sparse Core Ops, SparseCore 0:
  83.1 45.4 all-gather.1
  180.4 43.0 reduce-scatter.1
where the time goes:
time: 263 us; the launch traced here: 262 us
  waiting for transfers between devices  113 us (43%)
  matrix products  46.1 us (18%)
  local copies, waits for them, and re-layouts  30.9 us (12%)
  other arithmetic  23.6 us (9%)
  blocking collectives  18.2 us (7%)
  starting transfers between devices  15.5 us (6%)
  between operations  14.4 us (5%)
    all_to_all x1, waiting for transfers between devices, shards(): lax.all_to_all(send_grads, 'exp', split_axis=0, concat_axis=0, tiled=True)  42.3 us
    all_to_all x1, waiting for transfers between devices, shards(): lax.all_to_all(send_rows, 'exp', split_axis=0, concat_axis=0, tiled=True)  42.2 us
    all_to_all x1, waiting for transfers between devices, shards(): lax.all_to_all(back_rows, 'exp', split_axis=0, concat_axis=0, tiled=True)  27.6 us
    another operation x2, other arithmetic  15 us
    all_to_all x1, blocking collectives, shards(): lax.all_to_all(wanted.reshape(peer_count, slot_cap), 'exp', split_axis=0,...  10.2 us
    dot_general x2, matrix products, contract(): lax.dot_general(left, right, (((0,), (0,)), ((), ())), preferred_element_...  8.68 us
    psum x1, blocking collectives, shards(): mix_grad = lax.psum(mix_part, 'seq')  8.03 us
    dot_general x3, matrix products, factored_grads(): jnp.einsum('rap,riaq->ipq', left_view.astype(jnp.float32), mixed_right, p...  7.17 us
  transfers between devices with their start and end apart: 5, of which 3 were waited for; matrix products, arithmetic and copies ran while one was open for 18% of the time, Pallas kernels for 0%

commit v1 on v0

v1 whole, which is shorter than its diff:
```python
import functools

import jax
import jax.numpy as jnp
from jax import lax
from jax.experimental import pallas as pl
from jax.experimental.pallas import tpu as pltpu
from jax.sharding import PartitionSpec as P

SELECTED = 64
NPHM = 4
VMEM_LIMIT = 32 * 1024 * 1024
F32 = jnp.float32
BF16 = jnp.bfloat16


def iota(shape, dim):
    return lax.broadcasted_iota(jnp.int32, shape, dim)


def dot(left, right):
    return jnp.dot(left, right, preferred_element_type=F32)


def dot_tn(left, right):
    return lax.dot_general(left, right, (((0,), (0,)), ((), ())), preferred_element_type=F32)


def dot_nt(left, right):
    return lax.dot_general(left, right, (((1,), (1,)), ((), ())), preferred_element_type=F32)


def call(body, outs, ins, name, flops, scratch=(), smem=(), **extra):
    vmem = pl.BlockSpec(memory_space=pltpu.VMEM)
    scalar = pl.BlockSpec(memory_space=pltpu.SMEM)
    single = not isinstance(outs, (list, tuple))
    moved = sum(x.size * x.dtype.itemsize for x in ins)
    moved += sum(x.size * x.dtype.itemsize for x in ([outs] if single else outs))
    return pl.pallas_call(
        body,
        out_shape=outs,
        in_specs=[scalar if n in smem else vmem for n in range(len(ins))],
        out_specs=vmem if single else [vmem] * len(outs),
        scratch_shapes=list(scratch),
        compiler_params=pltpu.CompilerParams(vmem_limit_bytes=VMEM_LIMIT),
        cost_estimate=pl.CostEstimate(flops=flops, bytes_accessed=moved, transcendentals=0),
        name=name,
        **extra,
    )(*ins)


def shaped(shape, dtype):
    return jax.ShapeDtypeStruct(shape, dtype)


def index_body(cap, pieces, own_rows, block_len, chosen_ref, wanted_ref, slot_ref):
    peers, lanes = wanted_ref.shape
    rows = slot_ref.shape[1]
    position = jnp.concatenate(
        [chosen_ref[b : b + 1, :] + b * block_len for b in range(chosen_ref.shape[0])], axis=1
    )
    owner = lax.shift_right_logical(position, own_rows.bit_length() - 1)
    local = position & (own_rows - 1)
    peer = iota((peers, rows), 0)
    mine = (peer == owner).astype(F32)
    count = jnp.sum(mine, axis=1, keepdims=True)
    earlier = jnp.sum(jnp.where(peer < owner, count, 0.0), axis=0, keepdims=True).astype(jnp.int32)
    rank = iota((1, rows), 1) - earlier
    slot_ref[...] = owner * (cap * pieces) + rank
    lane = iota((lanes, rows), 0)
    hit = jnp.zeros((lanes, rows), F32)
    for j in range(pieces):
        hit = hit + (lane == rank + j * cap).astype(F32)
    marked = mine * (local + 1).astype(F32)
    wanted_ref[...] = dot_nt(marked.astype(BF16), hit.astype(BF16)).astype(jnp.int32)


def pick_matrix(cap, pieces, own_rows, requested):
    peers, lanes = requested.shape
    group = cap * pieces
    slots = peers * group
    peer = iota((peers, group, peers), 0).reshape(slots, peers)
    spread = dot(
        (peer == iota((slots, peers), 1)).astype(BF16), requested.astype(F32).astype(BF16)
    )
    place = iota((peers, group, lanes), 1).reshape(slots, lanes)
    row = jnp.sum(
        jnp.where(place == iota((slots, lanes), 1), spread, 0.0), axis=1, keepdims=True
    ).astype(jnp.int32)
    piece = iota((peers, group, 1), 1).reshape(slots, 1)
    shift = jnp.zeros((slots, 1), jnp.int32)
    for j in range(1, pieces):
        shift = shift + jnp.where(piece >= j * cap, own_rows, 0)
    target = jnp.where(row > 0, row - 1 + shift, -1)
    return (target == iota((slots, pieces * own_rows), 1)).astype(BF16)


def pick_body(cap, pieces, own_rows, requested_ref, *refs):
    columns, out_ref, pick_ref = refs[:pieces], refs[pieces], refs[pieces + 1]

    @pl.when(pl.program_id(0) == 0)
    def _():
        pick_ref[...] = pick_matrix(cap, pieces, own_rows, requested_ref[...])

    stacked = jnp.concatenate([ref[...] for ref in columns], axis=0)
    out_ref[...] = dot(pick_ref[...], stacked).astype(BF16)


def pick_rows(cap, pieces, requested, source, name):
    own_rows, width = source.shape
    part = width // pieces
    chunk = min(part, 512)
    steps = part // chunk
    slots = requested.shape[0] * cap * pieces
    specs = [
        pl.BlockSpec((own_rows, chunk), functools.partial(lambda j, c: (0, j * steps + c), j))
        for j in range(pieces)
    ]
    return pl.pallas_call(
        functools.partial(pick_body, cap, pieces, own_rows),
        out_shape=shaped((slots, part), BF16),
        grid=(steps,),
        in_specs=[pl.BlockSpec(requested.shape, lambda c: (0, 0))] + specs,
        out_specs=pl.BlockSpec((slots, chunk), lambda c: (0, c)),
        scratch_shapes=[pltpu.VMEM((slots, pieces * own_rows), BF16)],
        compiler_params=pltpu.CompilerParams(vmem_limit_bytes=VMEM_LIMIT),
        cost_estimate=pl.CostEstimate(
            flops=2 * slots * pieces * own_rows * part,
            bytes_accessed=4 * slots * part,
            transcendentals=0,
        ),
        name=name,
    )(requested, *([source] * pieces))


def place_body(cap, pieces, own_rows, requested_ref, returned_ref, out_ref, pick_ref):
    @pl.when(pl.program_id(0) == 0)
    def _():
        pick_ref[...] = pick_matrix(cap, pieces, own_rows, requested_ref[...])

    total = dot_tn(pick_ref[...], returned_ref[...]).astype(BF16)
    for j in range(pieces):
        out_ref[:, j, :] = total[j * own_rows : (j + 1) * own_rows]


def sum_rows(cap, pieces, own_rows, requested, returned):
    slots, part = returned.shape

    def body(requested_ref, returned_ref, out_ref):
        pick = pick_matrix(cap, pieces, own_rows, requested_ref[...])
        chunk = min(part, 512)
        for c in range(part // chunk):
            total = dot_tn(pick, returned_ref[:, c * chunk : (c + 1) * chunk]).astype(BF16)
            for j in range(pieces):
                start = j * part + c * chunk
                out_ref[:, start : start + chunk] = total[j * own_rows : (j + 1) * own_rows]

    return call(
        body,
        shaped((own_rows, part * pieces), BF16),
        [requested, returned],
        "sum_rows",
        2 * slots * pieces * own_rows * part,
    )


def assemble_body(order_ref, *refs):
    parts, out_ref = refs[:-1], refs[-1]
    for n, part in enumerate(parts):
        weights, count, rows, cols = part.shape
        start = pl.multiple_of(order_ref[n] * rows, rows)
        for m in range(weights):
            for i in range(count):
                out_ref[m, pl.ds(start, rows), i * cols : (i + 1) * cols] = part[m, i]


def place_matrix(cap, pieces, slots, slot):
    wide = jnp.concatenate([slot + j * cap for j in range(pieces)], axis=1)
    return (iota((slots, wide.shape[1]), 0) == wide).astype(BF16)


def stack_rows(pieces, place, got_ref, out_ref):
    part = got_ref.shape[1]
    rows, depth = out_ref.shape[0] // NPHM, out_ref.shape[1]
    chunk = min(part, 512)
    for c in range(part // chunk):
        block = dot_tn(place, got_ref[:, c * chunk : (c + 1) * chunk]).astype(BF16)
        for j in range(pieces):
            column = j * part + c * chunk
            a, start = column // depth, column % depth
            out_ref[a * rows : (a + 1) * rows, start : start + chunk] = block[
                j * rows : (j + 1) * rows
            ]


STRIP = 32


def mix_in(mix_ref, m, y_ref, emit):
    rows, cols = y_ref.shape[0] // NPHM, y_ref.shape[1] // NPHM

    def strip(n, carry):
        start = pl.multiple_of(n * STRIP, STRIP)
        total = [jnp.zeros((STRIP, cols), F32)] * NPHM
        for a in range(NPHM):
            for i in range(NPHM):
                block = y_ref[pl.ds(a * rows + start, STRIP), i * cols : (i + 1) * cols]
                for b in range(NPHM):
                    total[b] = total[b] + mix_ref[m * 64 + i * 16 + a * 4 + b] * block
        emit(start, total)
        return carry

    lax.fori_loop(0, rows // STRIP, strip, 0)


def mix_out(mix_ref, m, d_ref, z_ref):
    rows, cols = d_ref.shape[0], d_ref.shape[1] // NPHM

    def strip(n, carry):
        start = pl.multiple_of(n * STRIP, STRIP)
        blocks = [
            d_ref[pl.ds(start, STRIP), b * cols : (b + 1) * cols].astype(F32) for b in range(NPHM)
        ]
        for a in range(NPHM):
            for i in range(NPHM):
                total = mix_ref[m * 64 + i * 16 + a * 4] * blocks[0]
                for b in range(1, NPHM):
                    total = total + mix_ref[m * 64 + i * 16 + a * 4 + b] * blocks[b]
                z_ref[pl.ds(a * rows + start, STRIP), i * cols : (i + 1) * cols] = total.astype(
                    z_ref.dtype
                )
        return carry

    lax.fori_loop(0, rows // STRIP, strip, 0)


def forward_body(
    cap, pieces, slot_ref, mix_ref, got_ref, factor_ref, x_ref, yg_ref, yu_ref, act_ref, slope_ref, hid_ref, pre_ref
):
    place = place_matrix(cap, pieces, got_ref.shape[0], slot_ref[...])
    stack_rows(pieces, place, got_ref, x_ref)
    yg_ref[...] = dot(x_ref[...], factor_ref[0])
    yu_ref[...] = dot(x_ref[...], factor_ref[1])
    cols = yg_ref.shape[1] // NPHM

    def keep(start, total):
        for b in range(NPHM):
            pre_ref[pl.ds(start, STRIP), b * cols : (b + 1) * cols] = total[b]

    def finish(start, total):
        for b in range(NPHM):
            at = (pl.ds(start, STRIP), slice(b * cols, (b + 1) * cols))
            gate = pre_ref[at]
            sig = jax.nn.sigmoid(gate)
            act = gate * sig
            act_ref[at] = act
            slope_ref[at] = total[b] * (sig + act * (1.0 - sig))
            hid_ref[at] = act * total[b]

    mix_in(mix_ref, 0, yg_ref, keep)
    mix_in(mix_ref, 1, yu_ref, finish)


def backward_body(
    cap, pieces, slot_ref, mix_ref, got_ref, factor_ref, act_ref, slope_ref, hid_ref, gate_ref,
    back_ref, x_ref, y_ref, dg_ref, du_ref, dd_ref, zg_ref, zu_ref, part_ref, grad_ref,
):
    place = place_matrix(cap, pieces, got_ref.shape[0], slot_ref[...])
    stack_rows(pieces, place, got_ref, x_ref)
    y_ref[...] = dot(x_ref[...], factor_ref[2])
    cols = y_ref.shape[1] // NPHM

    def finish(start, total):
        gate = gate_ref[pl.ds(start, STRIP), :]
        inner = jnp.zeros((STRIP, cols), F32)
        for b in range(NPHM):
            at = (pl.ds(start, STRIP), slice(b * cols, (b + 1) * cols))
            hidden = hid_ref[at]
            inner = inner + hidden * total[b]
            hidden_grad = gate * total[b]
            dg_ref[at] = (hidden_grad * slope_ref[at]).astype(dg_ref.dtype)
            du_ref[at] = (hidden_grad * act_ref[at]).astype(du_ref.dtype)
            dd_ref[at] = (hidden * gate).astype(dd_ref.dtype)
        part_ref[pl.ds(start, STRIP), :] = inner

    mix_in(mix_ref, 2, y_ref, finish)
    mix_out(mix_ref, 0, dg_ref, zg_ref)
    mix_out(mix_ref, 1, du_ref, zu_ref)
    grad = dot_nt(zg_ref[...], factor_ref[0]) + dot_nt(zu_ref[...], factor_ref[1])
    grad_ref[...] = grad.astype(BF16)
    part = back_ref.shape[1]
    rows, depth = x_ref.shape[0] // NPHM, x_ref.shape[1]
    chunk = min(part, 512)
    for c in range(part // chunk):
        blocks = []
        for j in range(pieces):
            column = j * part + c * chunk
            a, start = column // depth, column % depth
            blocks.append(grad_ref[a * rows : (a + 1) * rows, start : start + chunk])
        back_ref[:, c * chunk : (c + 1) * chunk] = dot(
            place, jnp.concatenate(blocks, axis=0)
        ).astype(BF16)


def factor_body(swap, order_ref, mix_ref, xr_ref, xg_ref, zg_ref, zu_ref, dd_ref, *refs):
    zd_ref = refs[-1]
    mix_out(mix_ref, 2, dd_ref, zd_ref)
    pairs = ((xr_ref, zg_ref), (xr_ref, zu_ref), (xg_ref, zd_ref))
    if swap:
        other_ref, own_ref = refs[0], refs[1]
        half = own_ref.shape[1]
        for ref, n in ((other_ref, 1), (own_ref, 0)):
            start = pl.multiple_of(order_ref[n] * half, half)
            for m, (x_ref, z_ref) in enumerate(pairs):
                ref[m] = dot_tn(x_ref[:, pl.ds(start, half)], z_ref[...]).astype(ref.dtype)
    else:
        for m, (x_ref, z_ref) in enumerate(pairs):
            refs[0][m] = dot_tn(x_ref[...], z_ref[...]).astype(BF16)


def mix_grad_body(yg_ref, yu_ref, yd_ref, dg_ref, du_ref, dd_ref, out_ref):
    rows, cols = dg_ref.shape[0], dg_ref.shape[1] // NPHM
    for m, (y_ref, d_ref) in enumerate(((yg_ref, dg_ref), (yu_ref, du_ref), (yd_ref, dd_ref))):
        for a in range(NPHM):
            for i in range(NPHM):
                block = y_ref[a * rows : (a + 1) * rows, i * cols : (i + 1) * cols]
                for b in range(NPHM):
                    at = m * 64 + i * 16 + a * 4 + b
                    other = d_ref[:, b * cols : (b + 1) * cols].astype(F32)
                    out_ref[at : at + 1, :] = jnp.sum(block * other, axis=0, keepdims=True)


def combine_body(*refs):
    parts, out_ref = refs[:-1], refs[-1]
    weights, count, _, cols = out_ref.shape
    for m in range(weights):
        for i in range(count):
            at = slice(i * cols, (i + 1) * cols)
            out_ref[m, i] = sum(part[m, :, at].astype(F32) for part in parts)


def shards(tokens, cotangent, factors, mix, selection, scores):
    peers = lax.axis_size("exp")
    groups = lax.axis_size("seq")
    group = lax.axis_index("seq")
    own_rows, width = tokens.shape
    _, weights, count, depth_own, cols = factors.shape
    depth = depth_own * groups
    hidden = count * cols
    cap = 3 * own_rows // (2 * peers)
    pieces = 1
    while (cap * pieces) % 8:
        pieces *= 2
    lanes = 128
    slots = peers * cap * pieces
    part = width // pieces
    block_len = peers * SELECTED
    rows = selection.shape[1] * selection.shape[2]
    swap = groups == 2
    pair = [(0, 1), (1, 0)]
    mixing = mix.reshape(-1)
    order = jnp.stack([group, 1 - group]).astype(jnp.int32)

    if swap:
        factor_parts = [factors[0], lax.ppermute(factors, "seq", pair)[0]]
    else:
        factor_parts = [lax.all_gather(factors, "seq", axis=3, tiled=True)[0]]

    wanted, slot = call(
        functools.partial(index_body, cap, pieces, own_rows, block_len),
        [shaped((peers, lanes), jnp.int32), shaped((1, rows), jnp.int32)],
        [selection[0]],
        "wanted_rows",
        1 << 20,
    )
    requested = lax.all_to_all(wanted, "exp", split_axis=0, concat_axis=0, tiled=True)

    def exchange(array):
        array = array.reshape(peers, cap * pieces, part)
        array = lax.all_to_all(array, "exp", split_axis=0, concat_axis=0, tiled=True)
        return array.reshape(slots, part)

    got_rows = exchange(pick_rows(cap, pieces, requested, tokens, "pick_tokens"))
    got_grads = exchange(pick_rows(cap, pieces, requested, cotangent, "pick_cotangent"))

    factor_order = order if swap else jnp.zeros((2,), jnp.int32)
    side = call(
        assemble_body,
        shaped((weights, depth, hidden), BF16),
        [factor_order] + factor_parts,
        "assemble_factors",
        1 << 20,
        smem=(0,),
    )
    gate = jax.nn.sigmoid(scores[0].reshape(-1).astype(F32) / 64.0)
    gate_wide = jnp.broadcast_to(gate[:, None], (rows, cols))

    product = 2 * count * rows * depth * hidden
    stack = shaped((count * rows, depth), BF16)
    mixed = shaped((count * rows, hidden), F32)
    mixed_low = shaped((count * rows, hidden), BF16)
    flat = shaped((rows, hidden), F32)
    flat_low = shaped((rows, hidden), BF16)
    x_rows, y_gate, y_up, act, slope, hid = call(
        functools.partial(forward_body, cap, pieces),
        [stack, mixed, mixed, flat, flat, flat],
        [slot, mixing, got_rows, side],
        "forward",
        2 * product,
        scratch=[pltpu.VMEM((rows, hidden), F32)],
        smem=(1,),
    )
    back, x_grads, y_down, d_gate, d_up, d_down, z_gate, z_up, inner = call(
        functools.partial(backward_body, cap, pieces),
        [shaped((slots, part), BF16), stack, mixed, flat_low, flat_low, flat_low, mixed_low, mixed_low]
        + [shaped((rows, cols), F32)],
        [slot, mixing, got_grads, side, act, slope, hid, gate_wide],
        "backward",
        3 * product,
        scratch=[pltpu.VMEM((count * rows, depth), BF16)],
        smem=(1,),
    )
    returned = exchange(back)

    if swap:
        outs = [shaped((weights, depth_own, hidden), BF16), shaped((weights, depth_own, hidden), F32)]
    else:
        outs = [shaped((weights, depth, hidden), BF16)]
    partial = call(
        functools.partial(factor_body, swap),
        outs,
        [order, mixing, x_rows, x_grads, z_gate, z_up, d_down],
        "factor_partials",
        3 * product,
        scratch=[pltpu.VMEM((count * rows, hidden), BF16)],
        smem=(0, 1),
    )
    mix_rows = call(
        mix_grad_body,
        shaped((mixing.size, cols), F32),
        [y_gate, y_up, y_down, d_gate, d_up, d_down],
        "mix_partials",
        weights * 64 * 2 * rows * cols,
    )
    mix_part = jnp.sum(mix_rows, axis=1).reshape(mix.shape)
    if swap:
        halves = [partial[1], lax.ppermute(partial[0], "seq", pair)]
        mix_grad = mix_part + lax.ppermute(mix_part, "seq", pair)
    else:
        halves = [lax.psum_scatter(partial[0], "seq", scatter_dimension=1, tiled=True)]
        mix_grad = lax.psum(mix_part, "seq")
    gate_grad = (jnp.sum(inner, axis=1) * gate * (1.0 - gate)).reshape(selection.shape)
    factor_grad = call(
        combine_body,
        shaped((weights, count, depth_own, cols), F32),
        halves,
        "factor_grad",
        1 << 20,
    )[None]
    token_grad = sum_rows(cap, pieces, own_rows, requested, returned)
    return token_grad, factor_grad, mix_grad, gate_grad


def solution(mesh):
    return jax.shard_map(
        shards,
        mesh=mesh,
        in_specs=(
            P(("seq", "exp"), None),
            P(("seq", "exp"), None),
            P("exp", None, None, "seq", None),
            P("exp", None, None, None, None),
            P("exp", "seq", None),
            P("exp", "seq", None),
        ),
        out_specs=(
            P(("seq", "exp"), None),
            P("exp", None, None, "seq", None),
            P("exp", None, None, None, None),
            P("exp", "seq", None),
        ),
        check_vma=False,
    )
```

time: 263 us -> 189 us (0.72)
  matrix products: 46.1 us -> 0 us
  Pallas kernels: 0 us -> 24.5 us
  other arithmetic: 23.6 us -> 2.33 us
  waiting for transfers between devices: 113 us -> 99.3 us
  between operations: 14.4 us -> 0.79 us
  blocking collectives: 18.2 us -> 10.2 us
  starting transfers between devices: 15.5 us -> 20.9 us
    all_to_all x3, waiting for transfers between devices: 112 us -> 33.5 us  [exchange(): lax.all_to_all(array, 'exp', split_axis=0, concat_axis=0, tiled=True)]
    ppermute x0 -> x3, waiting for transfers between devices: none -> 65.8 us  [the longest x1 34.2 us: shards(): factor_parts = [factors[0], lax.ppermute(factors, 'seq', pair)[0]]]
    dot_general x21 -> x0, matrix products: 46.1 us -> none  [the longest x2 8.68 us: contract(): lax.dot_general(left, right, (((0,), (0,)), ((), ())), preferred_element_...]
    pallas_call x0 -> x10, Pallas kernels: none -> 24.5 us  [the longest x8 19.1 us: call(): pl.pallas_call(body, out_shape=outs, in_specs=[scalar if n in smem else v...]
    unnamed x31 -> x76, local copies, waits for them, and re-layouts: 6.25 us -> 28.1 us
    reshape x11 -> x2, local copies, waits for them, and re-layouts: 18.4 us -> 0.23 us  [the longest x1 0.12 us: shards(): mix_part = jnp.sum(mix_rows, axis=1).reshape(mix.shape)]
    another operation x3 -> x1, other arithmetic: 17 us -> 0.07 us  [shards(): order = jnp.stack([group, 1 - group]).astype(jnp.int32)]
    psum x1 -> x0, blocking collectives: 8.03 us -> none  [shards(): mix_grad = lax.psum(mix_part, 'seq')]
  transfers between devices with their start and end apart: 5 -> 6, of which waited for: 3 -> 3; matrix products, arithmetic and copies ran while one was open for 18% -> 1% of each run, Pallas kernels for 0% -> 7%
where the time goes in v1:
time: 189 us; the launch traced here: 187 us
  waiting for transfers between devices  99.3 us (53%)
  local copies, waits for them, and re-layouts  28.6 us (15%)
  Pallas kernels  24.5 us (13%)
  starting transfers between devices  20.9 us (11%)
  blocking collectives  10.2 us (5%)
  other arithmetic  2.33 us (1%)
    ppermute x1, waiting for transfers between devices, shards(): factor_parts = [factors[0], lax.ppermute(factors, 'seq', pair)[0]]  34.2 us
    all_to_all x3, waiting for transfers between devices, exchange(): lax.all_to_all(array, 'exp', split_axis=0, concat_axis=0, tiled=True)  33.5 us
    ppermute x1, waiting for transfers between devices, shards(): mix_grad = mix_part + lax.ppermute(mix_part, 'seq', pair)  31.6 us
    unnamed x76, local copies, waits for them, and re-layouts  28.1 us
    pallas_call x8, Pallas kernels, call(): pl.pallas_call(body, out_shape=outs, in_specs=[scalar if n in smem else v...  19.1 us
    all_to_all x3, starting transfers between devices, exchange(): lax.all_to_all(array, 'exp', split_axis=0, concat_axis=0, tiled=True)  18.1 us
    all_to_all x1, blocking collectives, shards(): lax.all_to_all(wanted, 'exp', split_axis=0, concat_axis=0, tiled=True)  10.2 us
    pallas_call x2, Pallas kernels, pick_rows(): pl.pallas_call(functools.partial(pick_body, cap, pieces, own_rows), out_s...  5.46 us
  transfers between devices with their start and end apart: 6, of which 3 were waited for; matrix products, arithmetic and copies ran while one was open for 1% of the time, Pallas kernels for 7%

profile of v1, /device:TPU:13, one launch (start us, length us, event | category | flops | bytes accessed | tf_op | source)
XLA Modules:
  0.0 186.6 jit_solution(10489643032086294052)
XLA Ops:
  1.6 10.2 %all_to_all.26 = s32[16,1,128]{2,1,0:T(1,128)S(1)} all-to-all(s32[16,1,128]{2,1,0:T(1,128)S(1)} %bitcast.24), channel_id=1, replica_groups=mesh['seq'=2,'exp'=16] {'exp'}, dimensions={0} | all-to-all | bytes 16384 | tf_op jit(solution)/shard_map/all_to_all | solution.py:376
  11.8 1.2 copy-done.2
  13.0 2.8 %pick_tokens.1 = bf16[384,2048]{1,0:T(8,128)(2,1)} custom-call(s32[16,128]{1,0:T(8,128)S(1)} %bitcast.21, bf16[128,4096]{1,0:T(8,128)(2,1)S(1)} %copy-done.2, bf16[128,4096]{1,0:T(8,128)(2,1)S(1)} %copy-done.2), custom_call_target="tpu_custom_call" | custom-call | flops 402653184 | bytes 3145728 | tf_op jit(solution)/shard_map/pick_tokens/pallas_call | solution.py:119
  15.8 6.4 %all-to-all-start.2 = ((bf16[16,24,2048]{2,1,0:T(8,128)(2,1)}), bf16[16,24,2048]{2,1,0:T(8,128)(2,1)S(1)}, u32[]{:S(2)}, u32[]{:S(2)}) async-start(bf16[16,24,2048]{2,1,0:T(8,128)(2,1)} %bitcast.10), calls=%async_computation.2 | async-start | bytes 3145728 | tf_op jit(solution)/shard_map/all_to_all | solution.py:380
  22.2 2.7 %pick_cotangent.1 = bf16[384,2048]{1,0:T(8,128)(2,1)} custom-call(s32[16,128]{1,0:T(8,128)S(1)} %bitcast.22, bf16[128,4096]{1,0:T(8,128)(2,1)S(1)} %copy-done.3, bf16[128,4096]{1,0:T(8,128)(2,1)S(1)} %copy-done.3), custom_call_target="tpu_custom_call" | custom-call | flops 402653184 | bytes 3145728 | tf_op jit(solution)/shard_map/pick_cotangent/pallas_call | solution.py:119
  24.8 33.5 %all-to-all-done.2 = bf16[16,24,2048]{2,1,0:T(8,128)(2,1)S(1)} async-done(((bf16[16,24,2048]{2,1,0:T(8,128)(2,1)}), bf16[16,24,2048]{2,1,0:T(8,128)(2,1)S(1)}, u32[]{:S(2)}, u32[]{:S(2)}) %all-to-all-start.2) | async-done | bytes 1572896 | tf_op jit(solution)/shard_map/all_to_all | solution.py:380
  58.4 1.2 copy-done
  59.5 4.9 %all-to-all-start.1 = ((bf16[16,24,2048]{2,1,0:T(8,128)(2,1)}), bf16[16,24,2048]{2,1,0:T(8,128)(2,1)}, u32[]{:S(2)}, u32[]{:S(2)}) async-start(bf16[16,24,2048]{2,1,0:T(8,128)(2,1)} %bitcast.4), calls=%async_computation.1 | async-start | bytes 3145728 | tf_op jit(solution)/shard_map/all_to_all | solution.py:380
  64.4 1.3 collective-permute-start
  66.0 34.2 %collective-permute-done = bf16[1,3,4,512,128]{4,3,2,1,0:T(8,128)(2,1)S(1)} collective-permute-done((bf16[1,3,4,512,128]{4,3,2,1,0:T(8,128)(2,1)S(1)}, bf16[1,3,4,512,128]{4,3,2,1,0:T(8,128)(2,1)S(1)}, u32[]{:S(2)}, u32[]{:S(2)}) %collective-permute-start) | collective-permute-done | bytes 1572896 | tf_op jit(solution)/shard_map/ppermute | solution.py:365
  101.4 1.4 copy-done.8
  102.8 1.4 copy-done.10
  105.6 3.1 %forward.1 = (bf16[512,1024]{1,0:T(8,128)(2,1)S(1)}, f32[512,512]{1,0:T(8,128)S(1)}, f32[512,512]{1,0:T(8,128)S(1)}, f32[128,512]{1,0:T(8,128)S(1)}, f32[128,512]{1,0:T(8,128)S(1)}, /*index=5*/f32[128,512]{1,0:T(8,128)S(1)}) custom-call(s32[1,128]{1,0:T(1,128)S(1)} %get-tuple-element.24.slot_ref, f32[192]{0:T(256)S(1)} %reshape.51.mix_ref, ...), custom_call_target="tpu_custom_call" | custom-call | flops 1073741824 | bytes 8652032 | tf_op jit(solution)/shard_map/forward/pallas_call | solution.py:39
  116.7 5.5 %backward.1 = (bf16[384,2048]{1,0:T(8,128)(2,1)S(1)}, bf16[512,1024]{1,0:T(8,128)(2,1)S(1)}, f32[512,512]{1,0:T(8,128)S(1)}, bf16[128,512]{1,0:T(8,128)(2,1)S(1)...) custom-call(s32[1,128]{1,0:T(1,128)S(1)} %get-tuple-element.24.slot_, ...), custom_call_target="tpu_custom_call" | custom-call | flops 1610612736 | bytes 10749184 | tf_op jit(solution)/shard_map/backward/pallas_call | solution.py:39
  128.2 6.9 %all-to-all-start.3 = ((bf16[16,24,2048]{2,1,0:T(8,128)(2,1)}), bf16[16,24,2048]{2,1,0:T(8,128)(2,1)S(1)}, u32[]{:S(2)}, u32[]{:S(2)}) async-start(bf16[16,24,2048]{2,1,0:T(8,128)(2,1)} %bitcast.18), calls=%async_computation.3 | async-start | bytes 3145728 | tf_op jit(solution)/shard_map/all_to_all | solution.py:380
  135.1 1.2 copy-done.31
  138.4 3.6 %factor_partials.1 = (bf16[3,512,512]{2,1,0:T(8,128)(2,1)}, f32[3,512,512]{2,1,0:T(8,128)S(1)}) custom-call(s32[2]{0:T(128)S(1)} %pad_add_fusion.order_ref, f32[192]{0:T(256)S(1)} %reshape.51.mix_ref, bf16[512,1024]{1,0:T(8,128)(2,1)S(1)} %copy-done.22, bf16[512,1024]{1,0:T(8,128)(2,1)S(1)} %copy-done.31, bf16[512,512]{1,0:T(8,128)(2,1)S(1)} %copy-done.33, ...), custom_call_target="tpu_custom_call" | custom-call | flops 1610612736 | bytes 7996168 | tf_op jit(solution)/shard_map/factor_partials/pallas_call | solution.py:39
  142.1 1.7 copy-done.4
  143.7 1.2 collective-permute-start.1
  144.9 1.4 mix_partials.1
  148.5 31.6 %collective-permute-done.2 = f32[1,3,4,4,4]{4,3,2,1,0:T(4,128)S(1)} collective-permute-done((f32[1,3,4,4,4]{4,3,2,1,0:T(4,128)S(1)}, f32[1,3,4,4,4]{4,3,2,1,0:T(4,128)S(1)}, u32[]{:S(2)}, u32[]{:S(2)}) %collective-permute-start.2) | collective-permute-done | bytes 800 | tf_op jit(solution)/shard_map/ppermute | solution.py:448
  180.7 1.9 %copy-done.5 = f32[3,512,512]{2,1,0:T(8,128)S(1)} copy-done((f32[3,512,512]{2,1,0:T(8,128)S(1)}, f32[3,512,512]{2,1,0:T(8,128)}, u32[]{:S(2)}) %copy-start.5) | copy-done | bytes 3145752
  182.6 2.1 %factor_grad.1 = f32[3,4,512,128]{3,2,1,0:T(8,128)} custom-call(f32[3,512,512]{2,1,0:T(8,128)S(1)} %copy-done.5, bf16[3,512,512]{2,1,0:T(8,128)(2,1)S(1)} %collective-permute-done.1.refs_1_), custom_call_target="tpu_custom_call" | custom-call | flops 1048576 | bytes 7864320 | tf_op jit(solution)/shard_map/factor_grad/pallas_call | solution.py:39
  184.7 2.0 %sum_rows.1 = bf16[128,4096]{1,0:T(8,128)(2,1)} custom-call(s32[16,128]{1,0:T(8,128)S(1)} %bitcast.23, bf16[384,2048]{1,0:T(8,128)(2,1)S(1)} %bitcast.16), custom_call_target="tpu_custom_call" | custom-call | flops 402653184 | bytes 2629632 | tf_op jit(solution)/shard_map/sum_rows/pallas_call | solution.py:39
  (86 shorter events, 22.6 us)
Async XLA Ops:
  11.8 1.2 copy-start.2
  15.8 6.4 %copy-start.3 = (bf16[128,4096]{1,0:T(8,128)(2,1)S(1)}, bf16[128,4096]{1,0:T(8,128)(2,1)}, u32[]{:S(2)}) copy-start(bf16[128,4096]{1,0:T(8,128)(2,1)} %refs_1_.2) | copy-start | bytes 3145732
  15.8 42.6 %all-to-all-start.2 = ((bf16[16,24,2048]{2,1,0:T(8,128)(2,1)}), bf16[16,24,2048]{2,1,0:T(8,128)(2,1)S(1)}, u32[]{:S(2)}, u32[]{:S(2)}) async-start(bf16[16,24,2048]{2,1,0:T(8,128)(2,1)} %bitcast.10), calls=%async_computation.2 | async-start | bytes 3145728 | tf_op jit(solution)/shard_map/all_to_all | solution.py:380
  58.3 1.2 copy-start
  58.4 6.1 %copy-start.7 = (bf16[1,3,4,512,128]{4,3,2,1,0:T(8,128)(2,1)S(1)}, bf16[1,3,4,512,128]{4,3,2,1,0:T(8,128)(2,1)}, u32[]{:S(2)}) copy-start(bf16[1,3,4,512,128]{4,3,2,1,0:T(8,128)(2,1)} %param.8) | copy-start | bytes 4718596
  58.4 7.3 %copy-start.36 = (f32[1,3,4,4,4]{4,3,2,1,0:T(4,128)S(1)}, f32[1,3,4,4,4]{4,3,2,1,0:T(4,128)}, u32[]{:S(2)}) copy-start(f32[1,3,4,4,4]{4,3,2,1,0:T(4,128)} %param.9) | copy-start | bytes 2308
  58.4 7.4 %copy-start.37 = (s32[1,2,64]{2,1,0:T(2,128)S(1)}, s32[1,2,64]{2,1,0:T(2,128)}, u32[]{:S(2)}) copy-start(s32[1,2,64]{2,1,0:T(2,128)} %param.11) | copy-start | bytes 1540
  59.5 54.3 %all-to-all-start.1 = ((bf16[16,24,2048]{2,1,0:T(8,128)(2,1)}), bf16[16,24,2048]{2,1,0:T(8,128)(2,1)}, u32[]{:S(2)}, u32[]{:S(2)}) async-start(bf16[16,24,2048]{2,1,0:T(8,128)(2,1)} %bitcast.4), calls=%async_computation.1 | async-start | bytes 3145728 | tf_op jit(solution)/shard_map/all_to_all | solution.py:380
  64.4 35.8 %collective-permute-start = (bf16[1,3,4,512,128]{4,3,2,1,0:T(8,128)(2,1)S(1)}, bf16[1,3,4,512,128]{4,3,2,1,0:T(8,128)(2,1)S(1)}, u32[]{:S(2)}, u32[]{:S(2)}) collective-permute-start(bf16[1,3,4,512,128]{4,3,2,1,0:T(8,128)(2,1)S(1)} %copy-done.7), channel_id=1, source_target_pairs={{0,16},{16,0},{1,17},{17,1},{2,18},{18,2},{3,19},{19,3},{4,20},{20... | collective-permute-start | bytes 4718600 | tf_op jit(solution)/shard_map/ppermute | solution.py:365
  101.4 1.4 copy-start.8
  102.8 1.4 copy-start.10
  104.2 1.4 copy-start.1
  128.2 6.9 %copy-start.18 = (bf16[128,512]{1,0:T(8,128)(2,1)S(1)}, bf16[128,512]{1,0:T(8,128)(2,1)}, u32[]{:S(2)}) copy-start(bf16[128,512]{1,0:T(8,128)(2,1)} %copy-done.17) | copy-start | bytes 393220
  128.2 6.9 %copy-start.22 = (bf16[512,1024]{1,0:T(8,128)(2,1)S(1)}, bf16[512,1024]{1,0:T(8,128)(2,1)}, u32[]{:S(2)}) copy-start(bf16[512,1024]{1,0:T(8,128)(2,1)} %copy-done.21) | copy-start | bytes 3145732
  128.2 56.4 %all-to-all-start.3 = ((bf16[16,24,2048]{2,1,0:T(8,128)(2,1)}), bf16[16,24,2048]{2,1,0:T(8,128)(2,1)S(1)}, u32[]{:S(2)}, u32[]{:S(2)}) async-start(bf16[16,24,2048]{2,1,0:T(8,128)(2,1)} %bitcast.18), calls=%async_computation.3 | async-start | bytes 3145728 | tf_op jit(solution)/shard_map/all_to_all | solution.py:380
  135.1 1.2 copy-start.31
  138.4 6.5 %copy-start.12 = (f32[512,512]{1,0:T(8,128)S(1)}, f32[512,512]{1,0:T(8,128)}, u32[]{:S(2)}) copy-start(f32[512,512]{1,0:T(8,128)} %copy-done.11) | copy-start | bytes 3145732
  138.4 6.5 %copy-start.14 = (f32[512,512]{1,0:T(8,128)S(1)}, f32[512,512]{1,0:T(8,128)}, u32[]{:S(2)}) copy-start(f32[512,512]{1,0:T(8,128)} %copy-done.13) | copy-start | bytes 3145732
  138.4 6.5 %copy-start.16 = (f32[512,512]{1,0:T(8,128)S(1)}, f32[512,512]{1,0:T(8,128)}, u32[]{:S(2)}) copy-start(f32[512,512]{1,0:T(8,128)} %copy-done.15) | copy-start | bytes 3145732
  138.4 6.5 %copy-start.19 = (bf16[128,512]{1,0:T(8,128)(2,1)S(1)}, bf16[128,512]{1,0:T(8,128)(2,1)}, u32[]{:S(2)}) copy-start(bf16[128,512]{1,0:T(8,128)(2,1)} %copy-done.17) | copy-start | bytes 393220
  142.1 1.7 copy-start.4
  143.7 37.0 %collective-permute-start.1 = (bf16[3,512,512]{2,1,0:T(8,128)(2,1)}, bf16[3,512,512]{2,1,0:T(8,128)(2,1)S(1)}, u32[]{:S(2)}, u32[]{:S(2)}) collective-permute-start(bf16[3,512,512]{2,1,0:T(8,128)(2,1)} %get-tuple-element.35), channel_id=1, source_target_pairs={{0,16},{16,0},{1,17},{17,1},{2,18},{18,2},{3,19},{19,3},{4,20},{20... | collective-permute-start | bytes 4718600 | tf_op jit(solution)/shard_map/ppermute | solution.py:447
  147.6 32.5 %collective-permute-start.2 = (f32[1,3,4,4,4]{4,3,2,1,0:T(4,128)S(1)}, f32[1,3,4,4,4]{4,3,2,1,0:T(4,128)S(1)}, u32[]{:S(2)}, u32[]{:S(2)}) collective-permute-start(f32[1,3,4,4,4]{4,3,2,1,0:T(4,128)S(1)} %reshape.58), channel_id=1, source_target_pairs={{0,16},{16,0},{1,17},{17,1},{2,18},{18,2},{3,19},{19,3},{4,20},{20... | collective-permute-start | bytes 2312 | tf_op jit(solution)/shard_map/ppermute | solution.py:448
  180.7 1.9 %copy-start.5 = (f32[3,512,512]{2,1,0:T(8,128)S(1)}, f32[3,512,512]{2,1,0:T(8,128)}, u32[]{:S(2)}) copy-start(f32[3,512,512]{2,1,0:T(8,128)} %copy-done.4) | copy-start | bytes 9437188
  (20 other events, 17.8 us)

commit v2 on v1

v2 whole, which is shorter than its diff:
```python
import functools

import jax
import jax.numpy as jnp
from jax import lax
from jax.experimental import pallas as pl
from jax.experimental.pallas import tpu as pltpu
from jax.sharding import PartitionSpec as P

SELECTED = 64
NPHM = 4
VMEM_LIMIT = 32 * 1024 * 1024
F32 = jnp.float32
BF16 = jnp.bfloat16


def iota(shape, dim):
    return lax.broadcasted_iota(jnp.int32, shape, dim)


def dot(left, right):
    return jnp.dot(left, right, preferred_element_type=F32)


def dot_tn(left, right):
    return lax.dot_general(left, right, (((0,), (0,)), ((), ())), preferred_element_type=F32)


def dot_nt(left, right):
    return lax.dot_general(left, right, (((1,), (1,)), ((), ())), preferred_element_type=F32)


HBM = pl.BlockSpec(memory_space=pltpu.HBM)
VMEM = pl.BlockSpec(memory_space=pltpu.VMEM)
SMEM = pl.BlockSpec(memory_space=pltpu.SMEM)


def call(body, outs, ins, name, flops, scratch=()):
    moved = sum(x.size * x.dtype.itemsize for x, _ in list(ins) + list(outs))
    return pl.pallas_call(
        body,
        out_shape=[x for x, _ in outs],
        in_specs=[place for _, place in ins],
        out_specs=[place for _, place in outs],
        scratch_shapes=list(scratch),
        compiler_params=pltpu.CompilerParams(vmem_limit_bytes=VMEM_LIMIT),
        cost_estimate=pl.CostEstimate(flops=flops, bytes_accessed=moved, transcendentals=0),
        name=name,
    )(*[x for x, _ in ins])


def begin(source, target, sem):
    copy = pltpu.make_async_copy(source, target, sem)
    copy.start()
    return copy


def shaped(shape, dtype):
    return jax.ShapeDtypeStruct(shape, dtype)


def scratch_like(shape, dtype):
    return pltpu.VMEM(shape, dtype)


def chunks_of(part):
    chunk = min(part, 512)
    return [slice(c * chunk, (c + 1) * chunk) for c in range(part // chunk)]


def index_body(cap, pieces, own_rows, block_len, chosen_ref, wanted_ref, slot_ref):
    peers, lanes = wanted_ref.shape
    rows = slot_ref.shape[1]
    position = jnp.concatenate(
        [chosen_ref[b : b + 1, :] + b * block_len for b in range(chosen_ref.shape[0])], axis=1
    )
    owner = lax.shift_right_logical(position, own_rows.bit_length() - 1)
    local = position & (own_rows - 1)
    peer = iota((peers, rows), 0)
    mine = (peer == owner).astype(F32)
    count = jnp.sum(mine, axis=1, keepdims=True)
    earlier = jnp.sum(jnp.where(peer < owner, count, 0.0), axis=0, keepdims=True).astype(jnp.int32)
    rank = iota((1, rows), 1) - earlier
    slot_ref[...] = owner * (cap * pieces) + rank
    lane = iota((lanes, rows), 0)
    hit = jnp.zeros((lanes, rows), F32)
    for j in range(pieces):
        hit = hit + (lane == rank + j * cap).astype(F32)
    marked = mine * (local + 1).astype(F32)
    wanted_ref[...] = dot_nt(marked.astype(BF16), hit.astype(BF16)).astype(jnp.int32)


def pick_matrix(cap, pieces, own_rows, requested):
    peers, lanes = requested.shape
    group = cap * pieces
    slots = peers * group
    peer = iota((peers, group, peers), 0).reshape(slots, peers)
    spread = dot(
        (peer == iota((slots, peers), 1)).astype(BF16), requested.astype(F32).astype(BF16)
    )
    place = iota((peers, group, lanes), 1).reshape(slots, lanes)
    row = jnp.sum(
        jnp.where(place == iota((slots, lanes), 1), spread, 0.0), axis=1, keepdims=True
    ).astype(jnp.int32)
    piece = iota((peers, group, 1), 1).reshape(slots, 1)
    shift = jnp.zeros((slots, 1), jnp.int32)
    for j in range(1, pieces):
        shift = shift + jnp.where(piece >= j * cap, own_rows, 0)
    target = jnp.where(row > 0, row - 1 + shift, -1)
    return (target == iota((slots, pieces * own_rows), 1)).astype(BF16)


def pick_rows(cap, pieces, requested, source, after, name):
    own_rows, width = source.shape
    part = width // pieces
    slots = requested.shape[0] * cap * pieces
    columns = chunks_of(part)

    def body(requested_ref, source_ref, *refs):
        out_ref, rows_ref, sent_ref, in_sem, out_sem = refs[len(after) :]
        loads = []
        for n, at in enumerate(columns):
            for j in range(pieces):
                wide = slice(j * part + at.start, j * part + at.stop)
                target = rows_ref.at[j * own_rows : (j + 1) * own_rows, at]
                loads.append(begin(source_ref.at[:, wide], target, in_sem.at[n, j]))
        pick = pick_matrix(cap, pieces, own_rows, requested_ref[...])
        stores = []
        for n, at in enumerate(columns):
            for load in loads[n * pieces : (n + 1) * pieces]:
                load.wait()
            sent_ref[:, at] = dot(pick, rows_ref[:, at]).astype(BF16)
            stores.append(begin(sent_ref.at[:, at], out_ref.at[:, at], out_sem.at[n]))
        for store in stores:
            store.wait()

    return call(
        body,
        [(shaped((slots, part), BF16), HBM)],
        [(requested, VMEM), (source, HBM)] + [(x, HBM) for x in after],
        name,
        2 * slots * pieces * own_rows * part,
        [
            scratch_like((pieces * own_rows, part), BF16),
            scratch_like((slots, part), BF16),
            pltpu.SemaphoreType.DMA((len(columns), pieces)),
            pltpu.SemaphoreType.DMA((len(columns),)),
        ],
    )[0]


def sum_rows(cap, pieces, own_rows, requested, returned):
    slots, part = returned.shape
    columns = chunks_of(part)

    def body(requested_ref, returned_ref, out_ref, got_ref, sum_ref, in_sem, out_sem):
        loads = [
            begin(returned_ref.at[:, at], got_ref.at[:, at], in_sem.at[n])
            for n, at in enumerate(columns)
        ]
        pick = pick_matrix(cap, pieces, own_rows, requested_ref[...])
        stores = []
        for n, at in enumerate(columns):
            loads[n].wait()
            total = dot_tn(pick, got_ref[:, at]).astype(BF16)
            for j in range(pieces):
                wide = slice(j * part + at.start, j * part + at.stop)
                sum_ref[:, wide] = total[j * own_rows : (j + 1) * own_rows]
                stores.append(
                    begin(sum_ref.at[:, wide], out_ref.at[:, wide], out_sem.at[n, j])
                )
        for store in stores:
            store.wait()

    return call(
        body,
        [(shaped((own_rows, part * pieces), BF16), HBM)],
        [(requested, VMEM), (returned, HBM)],
        "sum_rows",
        2 * slots * pieces * own_rows * part,
        [
            scratch_like((slots, part), BF16),
            scratch_like((own_rows, part * pieces), BF16),
            pltpu.SemaphoreType.DMA((len(columns),)),
            pltpu.SemaphoreType.DMA((len(columns), pieces)),
        ],
    )[0]


def load_factor(order_ref, parts, m, target, sems):
    copies = []
    for n, part in enumerate(parts):
        _, count, rows, cols = part.shape
        start = pl.multiple_of(order_ref[n] * rows, rows)
        for i in range(count):
            at = target.at[pl.ds(start, rows), i * cols : (i + 1) * cols]
            copies.append(begin(part.at[m, i], at, sems.at[n, i]))
    return copies


def wait_all(copies):
    for copy in copies:
        copy.wait()


def place_matrix(cap, pieces, slots, slot):
    wide = jnp.concatenate([slot + j * cap for j in range(pieces)], axis=1)
    return (iota((slots, wide.shape[1]), 0) == wide).astype(BF16)


def load_rows(got_hbm, got_ref, sems):
    return [
        begin(got_hbm.at[:, at], got_ref.at[:, at], sems.at[n])
        for n, at in enumerate(chunks_of(got_ref.shape[1]))
    ]


def stack_rows(pieces, place, loads, got_ref, out_ref):
    part = got_ref.shape[1]
    rows, depth = out_ref.shape[0] // NPHM, out_ref.shape[1]
    for load, at in zip(loads, chunks_of(part)):
        load.wait()
        block = dot_tn(place, got_ref[:, at]).astype(BF16)
        for j in range(pieces):
            column = j * part + at.start
            a, start = column // depth, column % depth
            out_ref[a * rows : (a + 1) * rows, start : start + at.stop - at.start] = block[
                j * rows : (j + 1) * rows
            ]


def store_parts(order_ref, source_ref, outs, sems):
    copies = []
    for n, out in enumerate(outs):
        size = out.shape[1]
        start = pl.multiple_of(order_ref[n] * size, size)
        copies.append(begin(source_ref.at[:, pl.ds(start, size)], out, sems.at[n]))
    return copies


STRIP = 32


def mix_in(mix_ref, m, y_ref, emit):
    rows, cols = y_ref.shape[0] // NPHM, y_ref.shape[1] // NPHM

    def strip(n, carry):
        start = pl.multiple_of(n * STRIP, STRIP)
        total = [jnp.zeros((STRIP, cols), F32)] * NPHM
        for a in range(NPHM):
            for i in range(NPHM):
                block = y_ref[pl.ds(a * rows + start, STRIP), i * cols : (i + 1) * cols]
                for b in range(NPHM):
                    total[b] = total[b] + mix_ref[m * 64 + i * 16 + a * 4 + b] * block
        emit(start, total)
        return carry

    lax.fori_loop(0, rows // STRIP, strip, 0)


def mix_out(mix_ref, m, d_ref, z_ref):
    rows, cols = d_ref.shape[0], d_ref.shape[1] // NPHM

    def strip(n, carry):
        start = pl.multiple_of(n * STRIP, STRIP)
        blocks = [
            d_ref[pl.ds(start, STRIP), b * cols : (b + 1) * cols].astype(F32) for b in range(NPHM)
        ]
        for a in range(NPHM):
            for i in range(NPHM):
                total = mix_ref[m * 64 + i * 16 + a * 4] * blocks[0]
                for b in range(1, NPHM):
                    total = total + mix_ref[m * 64 + i * 16 + a * 4 + b] * blocks[b]
                z_ref[pl.ds(a * rows + start, STRIP), i * cols : (i + 1) * cols] = total.astype(
                    z_ref.dtype
                )
        return carry

    lax.fori_loop(0, rows // STRIP, strip, 0)


def forward_body(
    cap, pieces, sides, slot_ref, mix_ref, order_ref, got_hbm, *refs
):
    parts, refs = refs[:sides], refs[sides:]
    x_outs, refs = refs[:sides], refs[sides:]
    yg_hbm, yu_hbm, act_hbm, slope_hbm, hid_hbm = refs[:5]
    got_ref, side_ref, x_ref, yg_ref, yu_ref, pre_ref, act_ref, slope_ref, hid_ref = refs[5:14]
    got_sem, side_sem, out_sem = refs[14:]
    loads = load_rows(got_hbm, got_ref, got_sem)
    sides_in = [
        load_factor(order_ref, parts, m, side_ref.at[m], side_sem.at[m]) for m in range(2)
    ]
    place = place_matrix(cap, pieces, got_ref.shape[0], slot_ref[...])
    stack_rows(pieces, place, loads, got_ref, x_ref)
    stores = store_parts(order_ref, x_ref, x_outs, out_sem)
    wait_all(sides_in[0])
    yg_ref[...] = dot(x_ref[...], side_ref[0])
    stores.append(begin(yg_ref, yg_hbm, out_sem.at[2]))
    wait_all(sides_in[1])
    yu_ref[...] = dot(x_ref[...], side_ref[1])
    stores.append(begin(yu_ref, yu_hbm, out_sem.at[3]))
    cols = yg_ref.shape[1] // NPHM

    def keep(start, total):
        for b in range(NPHM):
            pre_ref[pl.ds(start, STRIP), b * cols : (b + 1) * cols] = total[b]

    def finish(start, total):
        for b in range(NPHM):
            at = (pl.ds(start, STRIP), slice(b * cols, (b + 1) * cols))
            gate = pre_ref[at]
            sig = jax.nn.sigmoid(gate)
            act = gate * sig
            act_ref[at] = act
            slope_ref[at] = total[b] * (sig + act * (1.0 - sig))
            hid_ref[at] = act * total[b]

    mix_in(mix_ref, 0, yg_ref, keep)
    mix_in(mix_ref, 1, yu_ref, finish)
    stores.append(begin(act_ref, act_hbm, out_sem.at[4]))
    stores.append(begin(slope_ref, slope_hbm, out_sem.at[5]))
    stores.append(begin(hid_ref, hid_hbm, out_sem.at[6]))
    wait_all(stores)


def backward_body(
    cap, pieces, sides, after, slot_ref, mix_ref, order_ref, gate_ref, got_hbm, act_hbm, slope_hbm, hid_hbm,
    *refs,
):
    parts, refs = refs[:sides], refs[sides + after :]
    back_hbm, x_outs, refs = refs[0], refs[1 : 1 + sides], refs[1 + sides :]
    y_hbm, d_hbm, inner_ref = refs[:3]
    (
        got_ref, side_ref, x_ref, y_ref, d_ref, act_ref, slope_ref, hid_ref, zg_ref, zu_ref, grad_ref,
        back_ref, got_sem, side_sem, in_sem, out_sem,
    ) = refs[3:]
    loads = load_rows(got_hbm, got_ref, got_sem)
    down_in = load_factor(order_ref, parts, 2, side_ref.at[2], side_sem.at[2])
    flat_in = [
        begin(source, target, in_sem.at[n])
        for n, (source, target) in enumerate(
            ((act_hbm, act_ref), (slope_hbm, slope_ref), (hid_hbm, hid_ref))
        )
    ]
    sides_in = [
        load_factor(order_ref, parts, m, side_ref.at[m], side_sem.at[m]) for m in range(2)
    ]
    place = place_matrix(cap, pieces, got_ref.shape[0], slot_ref[...])
    stack_rows(pieces, place, loads, got_ref, x_ref)
    stores = store_parts(order_ref, x_ref, x_outs, out_sem)
    wait_all(down_in)
    y_ref[...] = dot(x_ref[...], side_ref[2])
    stores.append(begin(y_ref, y_hbm, out_sem.at[2]))
    cols = y_ref.shape[1] // NPHM
    wait_all(flat_in)

    def finish(start, total):
        gate = gate_ref[pl.ds(start, STRIP), :]
        inner = jnp.zeros((STRIP, cols), F32)
        for b in range(NPHM):
            at = (pl.ds(start, STRIP), slice(b * cols, (b + 1) * cols))
            hidden = hid_ref[at]
            inner = inner + hidden * total[b]
            hidden_grad = gate * total[b]
            d_ref[(0,) + at] = (hidden_grad * slope_ref[at]).astype(BF16)
            d_ref[(1,) + at] = (hidden_grad * act_ref[at]).astype(BF16)
            d_ref[(2,) + at] = (hidden * gate).astype(BF16)
        inner_ref[pl.ds(start, STRIP), :] = inner

    mix_in(mix_ref, 2, y_ref, finish)
    stores.append(begin(d_ref, d_hbm, out_sem.at[3]))
    mix_out(mix_ref, 0, d_ref.at[0], zg_ref)
    mix_out(mix_ref, 1, d_ref.at[1], zu_ref)
    wait_all(sides_in[0])
    wait_all(sides_in[1])
    grad = dot_nt(zg_ref[...], side_ref[0]) + dot_nt(zu_ref[...], side_ref[1])
    grad_ref[...] = grad.astype(BF16)
    part = back_ref.shape[1]
    rows, depth = x_ref.shape[0] // NPHM, x_ref.shape[1]
    for n, at in enumerate(chunks_of(part)):
        blocks = []
        for j in range(pieces):
            column = j * part + at.start
            a, start = column // depth, column % depth
            blocks.append(
                grad_ref[a * rows : (a + 1) * rows, start : start + at.stop - at.start]
            )
        back_ref[:, at] = dot(place, jnp.concatenate(blocks, axis=0)).astype(BF16)
        stores.append(begin(back_ref.at[:, at], back_hbm.at[:, at], out_sem.at[4 + n]))
    wait_all(stores)


def factor_body(count_groups, mix_ref, *refs):
    rows_in, refs = refs[: 3 * count_groups], refs[3 * count_groups :]
    out_hbm, x_ref, g_ref, d_ref, z_ref, sum_ref, in_sem, out_sem = refs
    loads = []
    for n in range(count_groups):
        for k, target in enumerate((x_ref, g_ref, d_ref)):
            loads.append(begin(rows_in[3 * n + k], target.at[n], in_sem.at[n, k]))
    stores = []
    cols = out_hbm.shape[3]
    wait_all(loads)
    for m in (2, 0, 1):
        for n in range(count_groups):
            mix_out(mix_ref, m, d_ref.at[n, m], z_ref.at[n])
        left = g_ref if m == 2 else x_ref
        sum_ref[m] = sum(dot_tn(left[n], z_ref[n]) for n in range(count_groups))
        for i in range(NPHM):
            at = sum_ref.at[m, :, i * cols : (i + 1) * cols]
            stores.append(begin(at, out_hbm.at[m, i], out_sem.at[m, i]))
    wait_all(stores)


def mix_grad_body(yg_hbm, yu_hbm, yd_hbm, d_hbm, out_ref, y_ref, d_ref, sems):
    loads = [begin(d_hbm, d_ref, sems.at[3])]
    for m, source in enumerate((yg_hbm, yu_hbm, yd_hbm)):
        loads.append(begin(source, y_ref.at[m], sems.at[m]))
    wait_all(loads)
    rows, cols = d_ref.shape[1], d_ref.shape[2] // NPHM
    for m in range(3):
        for a in range(NPHM):
            for i in range(NPHM):
                block = y_ref[m, a * rows : (a + 1) * rows, i * cols : (i + 1) * cols]
                for b in range(NPHM):
                    at = m * 64 + i * 16 + a * 4 + b
                    other = d_ref[m, :, b * cols : (b + 1) * cols].astype(F32)
                    out_ref[at : at + 1, :] = jnp.sum(block * other, axis=0, keepdims=True)


def shards(tokens, cotangent, factors, mix, selection, scores):
    peers = lax.axis_size("exp")
    groups = lax.axis_size("seq")
    group = lax.axis_index("seq")
    own_rows, width = tokens.shape
    _, weights, count, depth_own, cols = factors.shape
    depth = depth_own * groups
    hidden = count * cols
    cap = 3 * own_rows // (2 * peers)
    pieces = 1
    while (cap * pieces) % 8:
        pieces *= 2
    lanes = 128
    slots = peers * cap * pieces
    part = width // pieces
    steps = len(chunks_of(part))
    block_len = peers * SELECTED
    rows = selection.shape[1] * selection.shape[2]
    stacked = count * rows
    swap = groups == 2
    pair = [(0, 1), (1, 0)]
    mixing = mix.reshape(-1)
    dma = pltpu.SemaphoreType.DMA

    def across(array):
        return lax.ppermute(array, "seq", pair)

    if swap:
        factor_parts = [factors[0], across(factors)[0]]
        order = jnp.stack([group, 1 - group]).astype(jnp.int32)
    else:
        factor_parts = [lax.all_gather(factors, "seq", axis=3, tiled=True)[0]]
        order = jnp.zeros((2,), jnp.int32)
    sides = len(factor_parts)
    sides_in = [(x, HBM) for x in factor_parts]

    wanted, slot = call(
        functools.partial(index_body, cap, pieces, own_rows, block_len),
        [(shaped((peers, lanes), jnp.int32), VMEM), (shaped((1, rows), jnp.int32), VMEM)],
        [(selection[0], VMEM)],
        "wanted_rows",
        1 << 20,
    )
    requested = lax.all_to_all(wanted, "exp", split_axis=0, concat_axis=0, tiled=True)

    def exchange(array):
        array = array.reshape(peers, cap * pieces, part)
        array = lax.all_to_all(array, "exp", split_axis=0, concat_axis=0, tiled=True)
        return array.reshape(slots, part)

    got_rows = exchange(pick_rows(cap, pieces, requested, tokens, [], "pick_tokens"))
    got_grads = exchange(
        pick_rows(cap, pieces, requested, cotangent, factor_parts[1:], "pick_cotangent")
    )

    gate = jax.nn.sigmoid(scores[0].reshape(-1).astype(F32) / 64.0)
    gate_wide = jnp.broadcast_to(gate[:, None], (rows, cols))

    product = 2 * stacked * depth * hidden
    split = [(shaped((stacked, depth // sides), BF16), HBM)] * sides
    mixed = (shaped((stacked, hidden), F32), HBM)
    flat = (shaped((rows, hidden), F32), HBM)
    got_scratch = scratch_like((slots, part), BF16)
    stack_scratch = scratch_like((stacked, depth), BF16)
    mixed_scratch = scratch_like((stacked, hidden), F32)
    low_scratch = scratch_like((stacked, hidden), BF16)
    flat_scratch = scratch_like((rows, hidden), F32)
    outs = call(
        functools.partial(forward_body, cap, pieces, sides),
        split + [mixed, mixed, flat, flat, flat],
        [(slot, VMEM), (mixing, SMEM), (order, SMEM), (got_rows, HBM)] + sides_in,
        "forward",
        2 * product,
        [got_scratch, scratch_like((2, depth, hidden), BF16), stack_scratch, mixed_scratch, mixed_scratch]
        + [flat_scratch] * 4
        + [dma((steps,)), dma((2, sides, count)), dma((7,))],
    )
    x_parts, (y_gate, y_up, act, slope, hid) = outs[:sides], outs[sides:]
    x_rows = [x_parts[0]] + [across(x) for x in x_parts[1:]]
    after = x_rows[1:]
    outs = call(
        functools.partial(backward_body, cap, pieces, sides, len(after)),
        [(shaped((slots, part), BF16), HBM)]
        + split
        + [mixed, (shaped((weights, rows, hidden), BF16), HBM), (shaped((rows, cols), F32), VMEM)],
        [(slot, VMEM), (mixing, SMEM), (order, SMEM), (gate_wide, VMEM), (got_grads, HBM)]
        + [(x, HBM) for x in (act, slope, hid)]
        + sides_in
        + [(x, HBM) for x in after],
        "backward",
        3 * product,
        [got_scratch, scratch_like((weights, depth, hidden), BF16), stack_scratch, mixed_scratch]
        + [scratch_like((weights, rows, hidden), BF16)]
        + [flat_scratch] * 3
        + [low_scratch] * 2
        + [stack_scratch, got_scratch]
        + [dma((steps,)), dma((weights, sides, count)), dma((3,)), dma((4 + steps,))],
    )
    back, g_parts, (y_down, d_own, inner) = outs[0], outs[1 : 1 + sides], outs[1 + sides :]
    returned = exchange(back)

    d_rows = [d_own] + [across(d_own) for _ in x_parts[1:]]
    g_rows = [g_parts[0]] + [across(x) for x in g_parts[1:]]
    depth_here = depth // sides
    factor_grad = call(
        functools.partial(factor_body, sides),
        [(shaped((weights, count, depth_here, cols), F32), HBM)],
        [(mixing, SMEM)]
        + [(x, HBM) for n in range(sides) for x in (x_rows[n], g_rows[n], d_rows[n])],
        "factor_grad",
        3 * product,
        [scratch_like((sides, stacked, depth_here), BF16)] * 2
        + [
            scratch_like((sides, weights, rows, hidden), BF16),
            scratch_like((sides, stacked, hidden), BF16),
            scratch_like((weights, depth_here, hidden), F32),
            dma((sides, 3)),
            dma((weights, count)),
        ],
    )[0]
    mix_rows = call(
        mix_grad_body,
        [(shaped((mixing.size, cols), F32), VMEM)],
        [(x, HBM) for x in (y_gate, y_up, y_down, d_own)],
        "mix_partials",
        weights * 64 * 2 * rows * cols,
        [
            scratch_like((weights, stacked, hidden), F32),
            scratch_like((weights, rows, hidden), BF16),
            dma((4,)),
        ],
    )[0]
    mix_part = jnp.sum(mix_rows, axis=1).reshape(mix.shape)
    if swap:
        mix_grad = mix_part + across(mix_part)
    else:
        factor_grad = lax.psum_scatter(
            factor_grad.astype(BF16), "seq", scatter_dimension=2, tiled=True
        ).astype(F32)
        mix_grad = lax.psum(mix_part, "seq")
    gate_grad = (jnp.sum(inner, axis=1) * gate * (1.0 - gate)).reshape(selection.shape)
    token_grad = sum_rows(cap, pieces, own_rows, requested, returned)
    return token_grad, factor_grad[None], mix_grad, gate_grad


def solution(mesh):
    return jax.shard_map(
        shards,
        mesh=mesh,
        in_specs=(
            P(("seq", "exp"), None),
            P(("seq", "exp"), None),
            P("exp", None, None, "seq", None),
            P("exp", None, None, None, None),
            P("exp", "seq", None),
            P("exp", "seq", None),
        ),
        out_specs=(
            P(("seq", "exp"), None),
            P("exp", None, None, "seq", None),
            P("exp", None, None, None, None),
            P("exp", "seq", None),
        ),
        check_vma=False,
    )
```

time: 189 us -> 167 us (0.88)
  waiting for transfers between devices: 99.3 us -> 73 us
  Pallas kernels: 24.5 us -> 28.9 us
  starting transfers between devices: 20.9 us -> 23.5 us
  local copies, waits for them, and re-layouts: 28.6 us -> 26.2 us
    all_to_all x3, waiting for transfers between devices: 33.5 us -> 14.2 us  [exchange(): lax.all_to_all(array, 'exp', split_axis=0, concat_axis=0, tiled=True)]
    ppermute x3 -> x5, waiting for transfers between devices: 65.8 us -> 58.8 us  [across(): return lax.ppermute(array, 'seq', pair)]
    pallas_call x10 -> x8, Pallas kernels: 24.5 us -> 28.9 us  [call(): pl.pallas_call(body, out_shape=[x for x, _ in outs], in_specs=[place for...]
    ppermute x3 -> x5, starting transfers between devices: 2.8 us -> 5.22 us  [across(): return lax.ppermute(array, 'seq', pair)]
    unnamed x76 -> x64, local copies, waits for them, and re-layouts: 28.1 us -> 25.7 us
  transfers between devices with their start and end apart: 6 -> 8, of which waited for: 3 -> 5; matrix products, arithmetic and copies ran while one was open for 1% -> 2% of each run, Pallas kernels for 7% -> 10%
where the time goes in v2:
time: 167 us; the launch traced here: 166 us
  waiting for transfers between devices  73 us (44%)
  Pallas kernels  28.9 us (17%)
  local copies, waits for them, and re-layouts  26.2 us (16%)
  starting transfers between devices  23.5 us (14%)
  blocking collectives  10.2 us (6%)
  other arithmetic  3.22 us (2%)
    ppermute x5, waiting for transfers between devices, across(): return lax.ppermute(array, 'seq', pair)  58.8 us
    pallas_call x8, Pallas kernels, call(): pl.pallas_call(body, out_shape=[x for x, _ in outs], in_specs=[place for...  28.9 us
    unnamed x64, local copies, waits for them, and re-layouts  25.7 us
    all_to_all x3, starting transfers between devices, exchange(): lax.all_to_all(array, 'exp', split_axis=0, concat_axis=0, tiled=True)  18.3 us
    all_to_all x3, waiting for transfers between devices, exchange(): lax.all_to_all(array, 'exp', split_axis=0, concat_axis=0, tiled=True)  14.2 us
    all_to_all x1, blocking collectives, shards(): lax.all_to_all(wanted, 'exp', split_axis=0, concat_axis=0, tiled=True)  10.2 us
    ppermute x5, starting transfers between devices, across(): return lax.ppermute(array, 'seq', pair)  5.22 us
  transfers between devices with their start and end apart: 8, of which 5 were waited for; matrix products, arithmetic and copies ran while one was open for 2% of the time, Pallas kernels for 10%

profile of v2, /device:TPU:13, one launch (start us, length us, event | category | flops | bytes accessed | tf_op | source)
XLA Modules:
  0.0 166.0 jit_solution(5523667622491102016)
XLA Ops:
  1.6 10.2 %all_to_all.26 = s32[16,1,128]{2,1,0:T(1,128)S(1)} all-to-all(s32[16,1,128]{2,1,0:T(1,128)S(1)} %bitcast.29), channel_id=1, replica_groups=mesh['seq'=2,'exp'=16] {'exp'}, dimensions={0} | all-to-all | bytes 16384 | tf_op jit(solution)/shard_map/all_to_all | solution.py:474
  11.8 1.2 copy-done.12
  13.0 2.4 %pick_tokens.1 = bf16[384,2048]{1,0:T(8,128)(2,1)} custom-call(s32[16,128]{1,0:T(8,128)S(1)} %bitcast.26, bf16[128,4096]{1,0:T(8,128)(2,1)S(1)} %copy-done.12), custom_call_target="tpu_custom_call" | custom-call | flops 402653184 | bytes 2629632 | tf_op jit(solution)/shard_map/pick_tokens/pallas_call | solution.py:40
  15.4 6.2 %all-to-all-start.2 = ((bf16[16,24,2048]{2,1,0:T(8,128)(2,1)}), bf16[16,24,2048]{2,1,0:T(8,128)(2,1)S(1)}, u32[]{:S(2)}, u32[]{:S(2)}) async-start(bf16[16,24,2048]{2,1,0:T(8,128)(2,1)} %bitcast.9), calls=%async_computation.2 | async-start | bytes 3145728 | tf_op jit(solution)/shard_map/all_to_all | solution.py:478
  22.9 34.6 %collective-permute-done = bf16[1,3,4,512,128]{4,3,2,1,0:T(8,128)(2,1)S(1)} collective-permute-done((bf16[1,3,4,512,128]{4,3,2,1,0:T(8,128)(2,1)}, bf16[1,3,4,512,128]{4,3,2,1,0:T(8,128)(2,1)S(1)}, u32[]{:S(2)}, u32[]{:S(2)}) %collective-permute-start) | collective-permute-done | bytes 1572896 | tf_op jit(solution)/shard_map/ppermute | solution.py:456
  57.5 1.2 copy-done.13
  58.7 1.8 %pick_cotangent.1 = bf16[384,2048]{1,0:T(8,128)(2,1)S(1)} custom-call(s32[16,128]{1,0:T(8,128)S(1)} %bitcast.27, bf16[128,4096]{1,0:T(8,128)(2,1)S(1)} %copy-done.13, bf16[3,4,512,128]{3,2,1,0:T(8,128)(2,1)S(1)} %bitcast.16), custom_call_target="tpu_custom_call" | custom-call | flops 402653184 | bytes 4202496 | tf_op jit(solution)/shard_map/pick_cotangent/pallas_call | solution.py:40
  62.9 7.0 %all-to-all-start.1 = ((bf16[16,24,2048]{2,1,0:T(8,128)(2,1)}), bf16[16,24,2048]{2,1,0:T(8,128)(2,1)S(1)}, u32[]{:S(2)}, u32[]{:S(2)}) async-start(bf16[16,24,2048]{2,1,0:T(8,128)(2,1)} %bitcast.22), calls=%async_computation.1 | async-start | bytes 3145728 | tf_op jit(solution)/shard_map/all_to_all | solution.py:478
  70.1 1.4 copy-done.1
  71.5 1.4 copy-done.3
  72.9 5.2 %forward.1 = (bf16[512,512]{1,0:T(8,128)(2,1)S(1)}, bf16[512,512]{1,0:T(8,128)(2,1)}, f32[512,512]{1,0:T(8,128)S(1)}, f32[512,512]{1,0:T(8,128)S(1)}, f32[128,51...) custom-call(s32[1,128]{1,0:T(1,128)S(1)} %get-tuple-element.20.slot_ref, f32[192]{0:T(256)S(1)} %reshape.51.mix_ref, ...), custom_call_target="tpu_custom_call" | custom-call | flops 1073741824 | bytes 8652040 | tf_op jit(solution)/shard_map/forward/pallas_call | solution.py:40
  84.3 12.2 %collective-permute-done.1.refs_2_.refs_3_ = bf16[512,512]{1,0:T(8,128)(2,1)} collective-permute-done((bf16[512,512]{1,0:T(8,128)(2,1)}, bf16[512,512]{1,0:T(8,128)(2,1)}, u32[]{:S(2)}, u32[]{:S(2)}) %collective-permute-start.1) | collective-permute-done | bytes 524320 | tf_op jit(solution)/shard_map/ppermute | solution.py:456
  96.4 9.7 %all-to-all-done.1 = bf16[16,24,2048]{2,1,0:T(8,128)(2,1)S(1)} async-done(((bf16[16,24,2048]{2,1,0:T(8,128)(2,1)}), bf16[16,24,2048]{2,1,0:T(8,128)(2,1)S(1)}, u32[]{:S(2)}, u32[]{:S(2)}) %all-to-all-start.1) | async-done | bytes 1572896 | tf_op jit(solution)/shard_map/all_to_all | solution.py:478
  106.2 1.4 copy-done.4
  111.1 7.5 %backward.1 = (bf16[384,2048]{1,0:T(8,128)(2,1)S(1)}, bf16[512,512]{1,0:T(8,128)(2,1)S(1)}, bf16[512,512]{1,0:T(8,128)(2,1)}, f32[512,512]{1,0:T(8,128)S(1)}, bf...) custom-call(s32[1,128]{1,0:T(1,128)S(1)} %get-tuple-element.20.slot_ref, f32[192]{0:T(256)S(1)} %reshape.51.mix_ref, ...), custom_call_target="tpu_custom_call" | custom-call | flops 1610612736 | bytes 10224904 | tf_op jit(solution)/shard_map/backward/pallas_call | solution.py:40
  122.2 5.0 %all-to-all-start.3 = ((bf16[16,24,2048]{2,1,0:T(8,128)(2,1)}), bf16[16,24,2048]{2,1,0:T(8,128)(2,1)S(1)}, u32[]{:S(2)}, u32[]{:S(2)}) async-start(bf16[16,24,2048]{2,1,0:T(8,128)(2,1)} %bitcast.25), calls=%async_computation.3 | async-start | bytes 3145728 | tf_op jit(solution)/shard_map/all_to_all | solution.py:478
  127.2 1.3 collective-permute-start.2
  128.8 1.2 copy-done.9
  131.3 1.8 %mix_partials.1 = f32[192,128]{1,0:T(8,128)S(1)} custom-call(f32[512,512]{1,0:T(8,128)S(1)} %copy-done.7, f32[512,512]{1,0:T(8,128)S(1)} %copy-done.9, f32[512,512]{1,0:T(8,128)S(1)} %copy-done.11, bf16[3,128,512]{2,1,0:T(8,128)(2,1)S(1)} %get-tuple-element.28.refs_2_.d_hbm), custom_call_target="tpu_custom_call" | custom-call | flops 6291456 | bytes 3637248 | tf_op jit(solution)/shard_map/mix_partials/pallas_call | solution.py:40
  135.8 1.3 collective-permute-start.4
  137.7 12.1 %collective-permute-done.4 = f32[1,3,4,4,4]{4,3,2,1,0:T(4,128)S(1)} collective-permute-done((f32[1,3,4,4,4]{4,3,2,1,0:T(4,128)S(1)}, f32[1,3,4,4,4]{4,3,2,1,0:T(4,128)S(1)}, u32[]{:S(2)}, u32[]{:S(2)}) %collective-permute-start.4) | collective-permute-done | bytes 800 | tf_op jit(solution)/shard_map/ppermute | solution.py:456
  151.4 7.5 %factor_grad.1 = f32[3,4,512,128]{3,2,1,0:T(8,128)} custom-call(f32[192]{0:T(256)S(1)} %reshape.51.mix_ref, bf16[512,512]{1,0:T(8,128)(2,1)S(1)} %copy-done.15, bf16[512,512]{1,0:T(8,128)(2,1)S(1)} %copy-done.17, bf16[3,128,512]{2,1,0:T(8,128)(2,1)S(1)} %get-tuple-element.28.refs_2_.d_hbm, bf16[512,512]{1,0:T(8,128)(2,1)} %collective-permute-done.1.refs_2_.refs_3_, ...), custom_call_target="tpu_custom_call" | custom-call | flops 1610612736 | bytes 6030080 | tf_op jit(solution)/shard_map/factor_grad/pallas_call | solution.py:40
  158.9 4.5 %all-to-all-done.3 = bf16[16,24,2048]{2,1,0:T(8,128)(2,1)S(1)} async-done(((bf16[16,24,2048]{2,1,0:T(8,128)(2,1)}), bf16[16,24,2048]{2,1,0:T(8,128)(2,1)S(1)}, u32[]{:S(2)}, u32[]{:S(2)}) %all-to-all-start.3) | async-done | bytes 1572896 | tf_op jit(solution)/shard_map/all_to_all | solution.py:478
  163.4 2.4 %sum_rows.1 = bf16[128,4096]{1,0:T(8,128)(2,1)} custom-call(s32[16,128]{1,0:T(8,128)S(1)} %bitcast.28, bf16[384,2048]{1,0:T(8,128)(2,1)S(1)} %bitcast.19), custom_call_target="tpu_custom_call" | custom-call | flops 402653184 | bytes 2629632 | tf_op jit(solution)/shard_map/sum_rows/pallas_call | solution.py:40
  (76 shorter events, 24.5 us)
Async XLA Ops:
  11.8 1.2 copy-start.12
  15.4 46.3 %all-to-all-start.2 = ((bf16[16,24,2048]{2,1,0:T(8,128)(2,1)}), bf16[16,24,2048]{2,1,0:T(8,128)(2,1)S(1)}, u32[]{:S(2)}, u32[]{:S(2)}) async-start(bf16[16,24,2048]{2,1,0:T(8,128)(2,1)} %bitcast.9), calls=%async_computation.2 | async-start | bytes 3145728 | tf_op jit(solution)/shard_map/all_to_all | solution.py:478
  21.7 35.8 %collective-permute-start = (bf16[1,3,4,512,128]{4,3,2,1,0:T(8,128)(2,1)}, bf16[1,3,4,512,128]{4,3,2,1,0:T(8,128)(2,1)S(1)}, u32[]{:S(2)}, u32[]{:S(2)}) collective-permute-start(bf16[1,3,4,512,128]{4,3,2,1,0:T(8,128)(2,1)} %param.8), channel_id=1, source_target_pairs={{0,16},{16,0},{1,17},{17,1},{2,18},{18,2},{3,19},{19,3},{4,20},{20... | collective-permute-start | bytes 4718600 | tf_op jit(solution)/shard_map/ppermute | solution.py:456
  57.5 1.2 copy-start.13
  60.6 1.1 copy-start.2
  61.7 1.2 copy-start
  62.9 7.0 %copy-start.29 = (f32[1,3,4,4,4]{4,3,2,1,0:T(4,128)S(1)}, f32[1,3,4,4,4]{4,3,2,1,0:T(4,128)}, u32[]{:S(2)}) copy-start(f32[1,3,4,4,4]{4,3,2,1,0:T(4,128)} %param.9) | copy-start | bytes 2308
  62.9 43.2 %all-to-all-start.1 = ((bf16[16,24,2048]{2,1,0:T(8,128)(2,1)}), bf16[16,24,2048]{2,1,0:T(8,128)(2,1)S(1)}, u32[]{:S(2)}, u32[]{:S(2)}) async-start(bf16[16,24,2048]{2,1,0:T(8,128)(2,1)} %bitcast.22), calls=%async_computation.1 | async-start | bytes 3145728 | tf_op jit(solution)/shard_map/all_to_all | solution.py:478
  70.1 8.0 %copy-start.26 = (s32[2]{0:T(128)}, s32[2]{0:T(128)S(1)}, u32[]{:S(2)}) copy-start(s32[2]{0:T(128)S(1)} %pad_add_fusion.order_ref) | copy-start | bytes 28
  70.1 1.4 copy-start.1
  71.5 1.4 copy-start.3
  72.9 11.2 %copy-start.30 = (s32[1,2,64]{2,1,0:T(2,128)S(1)}, s32[1,2,64]{2,1,0:T(2,128)}, u32[]{:S(2)}) copy-start(s32[1,2,64]{2,1,0:T(2,128)} %param.11) | copy-start | bytes 1540
  83.0 13.5 %collective-permute-start.1 = (bf16[512,512]{1,0:T(8,128)(2,1)}, bf16[512,512]{1,0:T(8,128)(2,1)}, u32[]{:S(2)}, u32[]{:S(2)}) collective-permute-start(bf16[512,512]{1,0:T(8,128)(2,1)} %get-tuple-element.24), channel_id=1, source_target_pairs={{0,16},{16,0},{1,17},{17,1},{2,18},{18,2},{3,19},{19,3},{4,20},{20... | collective-permute-start | bytes 1572872 | tf_op jit(solution)/shard_map/ppermute | solution.py:456
  106.2 1.4 copy-start.4
  118.6 1.2 copy-start.5
  122.2 6.6 %copy-start.7 = (f32[512,512]{1,0:T(8,128)S(1)}, f32[512,512]{1,0:T(8,128)}, u32[]{:S(2)}) copy-start(f32[512,512]{1,0:T(8,128)} %copy-done.6) | copy-start | bytes 3145732
  122.2 41.2 %all-to-all-start.3 = ((bf16[16,24,2048]{2,1,0:T(8,128)(2,1)}), bf16[16,24,2048]{2,1,0:T(8,128)(2,1)S(1)}, u32[]{:S(2)}, u32[]{:S(2)}) async-start(bf16[16,24,2048]{2,1,0:T(8,128)(2,1)} %bitcast.25), calls=%async_computation.3 | async-start | bytes 3145728 | tf_op jit(solution)/shard_map/all_to_all | solution.py:478
  127.2 23.1 %collective-permute-start.2 = (bf16[512,512]{1,0:T(8,128)(2,1)}, bf16[512,512]{1,0:T(8,128)(2,1)}, u32[]{:S(2)}, u32[]{:S(2)}) collective-permute-start(bf16[512,512]{1,0:T(8,128)(2,1)} %get-tuple-element.29), channel_id=1, source_target_pairs={{0,16},{16,0},{1,17},{17,1},{2,18},{18,2},{3,19},{19,3},{4,20},{20... | collective-permute-start | bytes 1572872 | tf_op jit(solution)/shard_map/ppermute | solution.py:456
  128.5 21.8 %collective-permute-start.3 = (bf16[3,128,512]{2,1,0:T(8,128)(2,1)S(1)}, bf16[3,128,512]{2,1,0:T(8,128)(2,1)}, u32[]{:S(2)}, u32[]{:S(2)}) collective-permute-start(bf16[3,128,512]{2,1,0:T(8,128)(2,1)S(1)} %get-tuple-element.28.refs_2_.d_hbm), channel_id=1, source_target_pairs={{0,16},{16,0},{1,17},{17,1},{2,18},{18,2},{3,19},{19,3},{4,20},{20... | collective-permute-start | bytes 1179656 | tf_op jit(solution)/shard_map/ppermute | solution.py:456
  128.8 1.2 copy-start.9
  130.0 1.2 copy-start.11
  131.2 5.8 %copy-start.31 = (s32[1,2,64]{2,1,0:T(2,128)S(1)}, s32[1,2,64]{2,1,0:T(2,128)}, u32[]{:S(2)}) copy-start(s32[1,2,64]{2,1,0:T(2,128)} %param.11) | copy-start | bytes 1540
  131.2 19.1 %copy-start.15 = (bf16[512,512]{1,0:T(8,128)(2,1)S(1)}, bf16[512,512]{1,0:T(8,128)(2,1)}, u32[]{:S(2)}) copy-start(bf16[512,512]{1,0:T(8,128)(2,1)} %copy-done.14) | copy-start | bytes 1572868
  135.8 13.9 %collective-permute-start.4 = (f32[1,3,4,4,4]{4,3,2,1,0:T(4,128)S(1)}, f32[1,3,4,4,4]{4,3,2,1,0:T(4,128)S(1)}, u32[]{:S(2)}, u32[]{:S(2)}) collective-permute-start(f32[1,3,4,4,4]{4,3,2,1,0:T(4,128)S(1)} %reshape.58), channel_id=1, source_target_pairs={{0,16},{16,0},{1,17},{17,1},{2,18},{18,2},{3,19},{19,3},{4,20},{20... | collective-permute-start | bytes 2312 | tf_op jit(solution)/shard_map/ppermute | solution.py:456
  (16 other events, 13.1 us)

commit v3 on v2

--- a/solution.py
+++ b/solution.py
@@ -9,7 +9,7 @@
 
 SELECTED = 64
 NPHM = 4
-VMEM_LIMIT = 32 * 1024 * 1024
+VMEM_LIMIT = 63 * 1024 * 1024
 F32 = jnp.float32
 BF16 = jnp.bfloat16
 
@@ -189,13 +189,24 @@
 
 def load_factor(order_ref, parts, m, target, sems):
     copies = []
-    for n, part in enumerate(parts):
+    for n, side in enumerate(parts):
+        held = m
+        for part in side:
+            if held < part.shape[0]:
+                break
+            held -= part.shape[0]
         _, count, rows, cols = part.shape
         start = pl.multiple_of(order_ref[n] * rows, rows)
         for i in range(count):
             at = target.at[pl.ds(start, rows), i * cols : (i + 1) * cols]
-            copies.append(begin(part.at[m, i], at, sems.at[n, i]))
+            copies.append(begin(part.at[held, i], at, sems.at[n, i]))
     return copies
+
+
+def sides_of(sides, refs):
+    if sides == 1:
+        return [refs[:1]], refs[1:]
+    return [refs[:1], refs[1:3]], refs[3:]
 
 
 def wait_all(copies):
@@ -282,7 +293,7 @@
 def forward_body(
     cap, pieces, sides, slot_ref, mix_ref, order_ref, got_hbm, *refs
 ):
-    parts, refs = refs[:sides], refs[sides:]
+    parts, refs = sides_of(sides, refs)
     x_outs, refs = refs[:sides], refs[sides:]
     yg_hbm, yu_hbm, act_hbm, slope_hbm, hid_hbm = refs[:5]
     got_ref, side_ref, x_ref, yg_ref, yu_ref, pre_ref, act_ref, slope_ref, hid_ref = refs[5:14]
@@ -328,7 +339,8 @@
     cap, pieces, sides, after, slot_ref, mix_ref, order_ref, gate_ref, got_hbm, act_hbm, slope_hbm, hid_hbm,
     *refs,
 ):
-    parts, refs = refs[:sides], refs[sides + after :]
+    parts, refs = sides_of(sides, refs)
+    refs = refs[after:]
     back_hbm, x_outs, refs = refs[0], refs[1 : 1 + sides], refs[1 + sides :]
     y_hbm, d_hbm, inner_ref = refs[:3]
     (
@@ -456,13 +468,15 @@
         return lax.ppermute(array, "seq", pair)
 
     if swap:
-        factor_parts = [factors[0], across(factors)[0]]
+        early, late = across(factors[0, :1]), across(factors[0, 1:])
+        factor_parts = [[factors[0]], [early, late]]
         order = jnp.stack([group, 1 - group]).astype(jnp.int32)
     else:
-        factor_parts = [lax.all_gather(factors, "seq", axis=3, tiled=True)[0]]
+        early = late = None
+        factor_parts = [[lax.all_gather(factors, "seq", axis=3, tiled=True)[0]]]
         order = jnp.zeros((2,), jnp.int32)
     sides = len(factor_parts)
-    sides_in = [(x, HBM) for x in factor_parts]
+    sides_in = [(x, HBM) for side in factor_parts for x in side]
 
     wanted, slot = call(
         functools.partial(index_body, cap, pieces, own_rows, block_len),
@@ -478,9 +492,9 @@
         array = lax.all_to_all(array, "exp", split_axis=0, concat_axis=0, tiled=True)
         return array.reshape(slots, part)
 
-    got_rows = exchange(pick_rows(cap, pieces, requested, tokens, [], "pick_tokens"))
+    got_rows = exchange(pick_rows(cap, pieces, requested, tokens, [early] if swap else [], "pick_tokens"))
     got_grads = exchange(
-        pick_rows(cap, pieces, requested, cotangent, factor_parts[1:], "pick_cotangent")
+        pick_rows(cap, pieces, requested, cotangent, [late] if swap else [], "pick_cotangent")
     )
 
     gate = jax.nn.sigmoid(scores[0].reshape(-1).astype(F32) / 64.0)

time: 167 us -> 161 us (0.964)
  local copies, waits for them, and re-layouts: 26.2 us -> 5.24 us
  Pallas kernels: 28.9 us -> 40.6 us
  waiting for transfers between devices: 73 us -> 75.7 us
    unnamed x64 -> x16, local copies, waits for them, and re-layouts: 25.7 us -> 1.62 us
    all_to_all x3, waiting for transfers between devices: 14.2 us -> 27.1 us  [exchange(): lax.all_to_all(array, 'exp', split_axis=0, concat_axis=0, tiled=True)]
    pallas_call x8, Pallas kernels: 28.9 us -> 40.6 us  [call(): pl.pallas_call(body, out_shape=[x for x, _ in outs], in_specs=[place for...]
    ppermute x5 -> x6, waiting for transfers between devices: 58.8 us -> 48.7 us  [across(): return lax.ppermute(array, 'seq', pair)]
    squeeze x0 -> x2, local copies, waits for them, and re-layouts: none -> 1.94 us  [shards(): early, late = (across(factors[0, :1]), across(factors[0, 1:]))]
    ppermute x5 -> x6, starting transfers between devices: 5.22 us -> 6.55 us  [across(): return lax.ppermute(array, 'seq', pair)]
  transfers between devices with their start and end apart: 8 -> 9, of which waited for: 5 -> 6; matrix products, arithmetic and copies ran while one was open for 2% -> 3% of each run, Pallas kernels for 10% -> 15%
where the time goes in v3:
time: 161 us; the launch traced here: 160 us
  waiting for transfers between devices  75.7 us (47%)
  Pallas kernels  40.6 us (25%)
  starting transfers between devices  23.9 us (15%)
  blocking collectives  10.5 us (7%)
  local copies, waits for them, and re-layouts  5.24 us (3%)
  other arithmetic  3.63 us (2%)
    ppermute x6, waiting for transfers between devices, across(): return lax.ppermute(array, 'seq', pair)  48.7 us
    pallas_call x8, Pallas kernels, call(): pl.pallas_call(body, out_shape=[x for x, _ in outs], in_specs=[place for...  40.6 us
    all_to_all x3, waiting for transfers between devices, exchange(): lax.all_to_all(array, 'exp', split_axis=0, concat_axis=0, tiled=True)  27.1 us
    all_to_all x3, starting transfers between devices, exchange(): lax.all_to_all(array, 'exp', split_axis=0, concat_axis=0, tiled=True)  17.4 us
    all_to_all x1, blocking collectives, shards(): lax.all_to_all(wanted, 'exp', split_axis=0, concat_axis=0, tiled=True)  10.5 us
    ppermute x6, starting transfers between devices, across(): return lax.ppermute(array, 'seq', pair)  6.55 us
  transfers between devices with their start and end apart: 9, of which 6 were waited for; matrix products, arithmetic and copies ran while one was open for 3% of the time, Pallas kernels for 15%

profile of v3, /device:TPU:13, one launch (start us, length us, event | category | flops | bytes accessed | tf_op | source)
XLA Modules:
  0.0 160.5 jit_solution(2076644098000861801)
XLA Ops:
  0.6 1.9 %slice_bitcast_fusion.1 = bf16[1,4,512,128]{3,2,1,0:T(8,128)(2,1)} fusion(bf16[1,3,4,512,128]{4,3,2,1,0:T(8,128)(2,1)} %param.8), kind=kLoop, calls=%fused_computation.1 | loop fusion | bytes 1048576 | tf_op jit(solution)/shard_map/squeeze | solution.py:471
  3.7 1.6 wanted_rows.1
  5.3 10.5 %all_to_all.26 = s32[16,1,128]{2,1,0:T(1,128)} all-to-all(s32[16,1,128]{2,1,0:T(1,128)} %bitcast.28), channel_id=1, replica_groups=mesh['seq'=2,'exp'=16] {'exp'}, dimensions={0} | all-to-all | bytes 16384 | tf_op jit(solution)/shard_map/all_to_all | solution.py:488
  16.6 3.6 %pick_tokens.1 = bf16[384,2048]{1,0:T(8,128)(2,1)} custom-call(s32[16,128]{1,0:T(8,128)} %bitcast.25, bf16[128,4096]{1,0:T(8,128)(2,1)} %source_ref.3, bf16[1,4,512,128]{3,2,1,0:T(8,128)(2,1)} %copy-done.1), custom_call_target="tpu_custom_call" | custom-call | flops 402653184 | bytes 3153920 | tf_op jit(solution)/shard_map/pick_tokens/pallas_call | solution.py:40
  20.3 7.3 %all-to-all-start.2 = ((bf16[16,24,2048]{2,1,0:T(8,128)(2,1)}), bf16[16,24,2048]{2,1,0:T(8,128)(2,1)}, u32[]{:S(2)}, u32[]{:S(2)}) async-start(bf16[16,24,2048]{2,1,0:T(8,128)(2,1)} %bitcast.22), calls=%async_computation.2 | async-start | bytes 3145728 | tf_op jit(solution)/shard_map/all_to_all | solution.py:492
  27.6 1.3 collective-permute-start
  28.9 23.3 %collective-permute-done.refs_0_.refs_2_ = bf16[2,4,512,128]{3,2,1,0:T(8,128)(2,1)} collective-permute-done((bf16[2,4,512,128]{3,2,1,0:T(8,128)(2,1)S(1)}, bf16[2,4,512,128]{3,2,1,0:T(8,128)(2,1)}, u32[]{:S(2)}, u32[]{:S(2)}) %collective-permute-start) | collective-permute-done | bytes 1048608 | tf_op jit(solution)/shard_map/ppermute | solution.py:468
  52.2 3.6 %pick_cotangent.1 = bf16[384,2048]{1,0:T(8,128)(2,1)} custom-call(s32[16,128]{1,0:T(8,128)} %bitcast.26, bf16[128,4096]{1,0:T(8,128)(2,1)} %source_ref.2, bf16[2,4,512,128]{3,2,1,0:T(8,128)(2,1)} %collective-permute-done.refs_0_.refs_2_), custom_call_target="tpu_custom_call" | custom-call | flops 402653184 | bytes 3678208 | tf_op jit(solution)/shard_map/pick_cotangent/pallas_call | solution.py:40
  55.8 8.1 %all-to-all-done.2 = bf16[16,24,2048]{2,1,0:T(8,128)(2,1)} async-done(((bf16[16,24,2048]{2,1,0:T(8,128)(2,1)}), bf16[16,24,2048]{2,1,0:T(8,128)(2,1)}, u32[]{:S(2)}, u32[]{:S(2)}) %all-to-all-start.2) | async-done | bytes 1572896 | tf_op jit(solution)/shard_map/all_to_all | solution.py:492
  63.8 5.0 %all-to-all-start.1 = ((bf16[16,24,2048]{2,1,0:T(8,128)(2,1)}), bf16[16,24,2048]{2,1,0:T(8,128)(2,1)}, u32[]{:S(2)}, u32[]{:S(2)}) async-start(bf16[16,24,2048]{2,1,0:T(8,128)(2,1)} %bitcast.21), calls=%async_computation.1 | async-start | bytes 3145728 | tf_op jit(solution)/shard_map/all_to_all | solution.py:492
  70.2 7.0 %forward.1 = (bf16[512,512]{1,0:T(8,128)(2,1)}, bf16[512,512]{1,0:T(8,128)(2,1)}, f32[512,512]{1,0:T(8,128)}, f32[512,512]{1,0:T(8,128)}, f32[128,512]{1,0:T(8,1...) custom-call(s32[1,128]{1,0:T(1,128)} %get-tuple-element.20.slot_ref, f32[192]{0:T(256)} %reshape.51.mix_ref, ...), custom_call_target="tpu_custom_call" | custom-call | flops 1073741824 | bytes 8652040 | tf_op jit(solution)/shard_map/forward/pallas_call | solution.py:40
  77.2 1.3 collective-permute-start.2
  78.5 12.2 %collective-permute-done.2.refs_3_ = bf16[512,512]{1,0:T(8,128)(2,1)S(1)} collective-permute-done((bf16[512,512]{1,0:T(8,128)(2,1)}, bf16[512,512]{1,0:T(8,128)(2,1)S(1)}, u32[]{:S(2)}, u32[]{:S(2)}) %collective-permute-start.2) | collective-permute-done | bytes 524320 | tf_op jit(solution)/shard_map/ppermute | solution.py:468
  90.7 14.5 %all-to-all-done.1 = bf16[16,24,2048]{2,1,0:T(8,128)(2,1)} async-done(((bf16[16,24,2048]{2,1,0:T(8,128)(2,1)}), bf16[16,24,2048]{2,1,0:T(8,128)(2,1)}, u32[]{:S(2)}, u32[]{:S(2)}) %all-to-all-start.1) | async-done | bytes 1572896 | tf_op jit(solution)/shard_map/all_to_all | solution.py:492
  105.8 9.4 %backward.1 = (bf16[384,2048]{1,0:T(8,128)(2,1)}, bf16[512,512]{1,0:T(8,128)(2,1)}, bf16[512,512]{1,0:T(8,128)(2,1)}, f32[512,512]{1,0:T(8,128)}, bf16[3,128,512]{2,1,0:T(8,128)(2,1)}, /*index=5*/f32[128,128]{1,0:T(8,128)}) custom-call(s32[1,128]{1,0:T(1,128)} %get-tuple-element.20.slot_ref, f32[192]{0:T(256)} %reshape.51.mix_ref, s32[2]{0:T(128)} %pad_add_fusion.order_ref, ...), custom_call_target="tpu_custom_call" | custom-call | flops 1610612736 | bytes 10224904 | tf_op jit(solution)/shard_map/backward/pallas_call | solution.py:40
  115.2 5.1 %all-to-all-start.3 = ((bf16[16,24,2048]{2,1,0:T(8,128)(2,1)}), bf16[16,24,2048]{2,1,0:T(8,128)(2,1)}, u32[]{:S(2)}, u32[]{:S(2)}) async-start(bf16[16,24,2048]{2,1,0:T(8,128)(2,1)} %bitcast.24), calls=%async_computation.3 | async-start | bytes 3145728 | tf_op jit(solution)/shard_map/all_to_all | solution.py:492
  120.3 1.3 collective-permute-start.3
  121.9 3.9 %mix_partials.1 = f32[192,128]{1,0:T(8,128)} custom-call(f32[512,512]{1,0:T(8,128)} %get-tuple-element.30.yg_hbm, f32[512,512]{1,0:T(8,128)} %get-tuple-element.31.yu_hbm, f32[512,512]{1,0:T(8,128)} %get-tuple-element.32.yd_hbm, bf16[3,128,512]{2,1,0:T(8,128)(2,1)} %get-tuple-element.28.refs_2_.d_hbm), custom_call_target="tpu_custom_call" | custom-call | flops 6291456 | bytes 3637248 | tf_op jit(solution)/shard_map/mix_partials/pallas_call | solution.py:40
  127.1 1.3 collective-permute-start.5
  128.3 1.3 subtract_multiply_fusion
  129.6 13.2 %collective-permute-done.5 = f32[1,3,4,4,4]{4,3,2,1,0:T(4,128)S(1)} collective-permute-done((f32[1,3,4,4,4]{4,3,2,1,0:T(4,128)S(1)}, f32[1,3,4,4,4]{4,3,2,1,0:T(4,128)S(1)}, u32[]{:S(2)}, u32[]{:S(2)}) %collective-permute-start.5) | collective-permute-done | bytes 800 | tf_op jit(solution)/shard_map/ppermute | solution.py:468
  144.2 7.8 %factor_grad.1 = f32[3,4,512,128]{3,2,1,0:T(8,128)} custom-call(f32[192]{0:T(256)} %reshape.51.mix_ref, bf16[512,512]{1,0:T(8,128)(2,1)} %get-tuple-element.26.refs_0_, bf16[512,512]{1,0:T(8,128)(2,1)} %get-tuple-element.27.refs_1_, bf16[3,128,512]{2,1,0:T(8,128)(2,1)} %get-tuple-element.28.refs_2_.d_hbm, bf16[512,512]{1,0:T(8,128)(2,1)} %copy-done.2, ...), custom_call_target="tpu_custom_call" | custom-call | flops 1610612736 | bytes 6030080 | tf_op jit(solution)/shard_map/factor_grad/pallas_call | solution.py:40
  152.1 4.5 %all-to-all-done.3 = bf16[16,24,2048]{2,1,0:T(8,128)(2,1)} async-done(((bf16[16,24,2048]{2,1,0:T(8,128)(2,1)}), bf16[16,24,2048]{2,1,0:T(8,128)(2,1)}, u32[]{:S(2)}, u32[]{:S(2)}) %all-to-all-start.3) | async-done | bytes 1572896 | tf_op jit(solution)/shard_map/all_to_all | solution.py:492
  156.6 3.7 %sum_rows.1 = bf16[128,4096]{1,0:T(8,128)(2,1)} custom-call(s32[16,128]{1,0:T(8,128)} %bitcast.27, bf16[384,2048]{1,0:T(8,128)(2,1)} %bitcast.14.returned_ref), custom_call_target="tpu_custom_call" | custom-call | flops 402653184 | bytes 2629632 | tf_op jit(solution)/shard_map/sum_rows/pallas_call | solution.py:40
  (32 shorter events, 7.2 us)
Async XLA Ops:
  2.5 13.3 %collective-permute-start.1 = (bf16[1,4,512,128]{3,2,1,0:T(8,128)(2,1)}, bf16[1,4,512,128]{3,2,1,0:T(8,128)(2,1)S(1)}, u32[]{:S(2)}, u32[]{:S(2)}) collective-permute-start(bf16[1,4,512,128]{3,2,1,0:T(8,128)(2,1)} %slice_bitcast_fusion.1), channel_id=1, source_target_pairs={{0,16},{16,0},{1,17},{17,1},{2,18},{18,2},{3,19},{19,3},{4,20},{20... | collective-permute-start | bytes 1572872 | tf_op jit(solution)/shard_map/ppermute | solution.py:468
  15.8 0.8 copy-start.1
  20.2 7.3 %copy-start = (bf16[1,3,4,512,128]{4,3,2,1,0:T(8,128)(2,1)S(1)}, bf16[1,3,4,512,128]{4,3,2,1,0:T(8,128)(2,1)}, u32[]{:S(2)}) copy-start(bf16[1,3,4,512,128]{4,3,2,1,0:T(8,128)(2,1)} %param.8) | copy-start | bytes 4718596
  20.3 43.6 %all-to-all-start.2 = ((bf16[16,24,2048]{2,1,0:T(8,128)(2,1)}), bf16[16,24,2048]{2,1,0:T(8,128)(2,1)}, u32[]{:S(2)}, u32[]{:S(2)}) async-start(bf16[16,24,2048]{2,1,0:T(8,128)(2,1)} %bitcast.22), calls=%async_computation.2 | async-start | bytes 3145728 | tf_op jit(solution)/shard_map/all_to_all | solution.py:492
  27.6 24.6 %collective-permute-start = (bf16[2,4,512,128]{3,2,1,0:T(8,128)(2,1)S(1)}, bf16[2,4,512,128]{3,2,1,0:T(8,128)(2,1)}, u32[]{:S(2)}, u32[]{:S(2)}) collective-permute-start(bf16[2,4,512,128]{3,2,1,0:T(8,128)(2,1)S(1)} %slice_bitcast_fusion), channel_id=1, source_target_pairs={{0,16},{16,0},{1,17},{17,1},{2,18},{18,2},{3,19},{19,3},{4,20},{20... | collective-permute-start | bytes 3145736 | tf_op jit(solution)/shard_map/ppermute | solution.py:468
  63.8 5.0 %copy-start.6 = (f32[1,3,4,4,4]{4,3,2,1,0:T(4,128)S(1)}, f32[1,3,4,4,4]{4,3,2,1,0:T(4,128)}, u32[]{:S(2)}) copy-start(f32[1,3,4,4,4]{4,3,2,1,0:T(4,128)} %param.9) | copy-start | bytes 2308
  63.8 41.3 %all-to-all-start.1 = ((bf16[16,24,2048]{2,1,0:T(8,128)(2,1)}), bf16[16,24,2048]{2,1,0:T(8,128)(2,1)}, u32[]{:S(2)}, u32[]{:S(2)}) async-start(bf16[16,24,2048]{2,1,0:T(8,128)(2,1)} %bitcast.21), calls=%async_computation.1 | async-start | bytes 3145728 | tf_op jit(solution)/shard_map/all_to_all | solution.py:492
  70.2 8.2 %copy-start.7 = (s32[1,2,64]{2,1,0:T(2,128)S(1)}, s32[1,2,64]{2,1,0:T(2,128)}, u32[]{:S(2)}) copy-start(s32[1,2,64]{2,1,0:T(2,128)} %param.11) | copy-start | bytes 1540
  77.2 13.5 %collective-permute-start.2 = (bf16[512,512]{1,0:T(8,128)(2,1)}, bf16[512,512]{1,0:T(8,128)(2,1)S(1)}, u32[]{:S(2)}, u32[]{:S(2)}) collective-permute-start(bf16[512,512]{1,0:T(8,128)(2,1)} %get-tuple-element.24), channel_id=1, source_target_pairs={{0,16},{16,0},{1,17},{17,1},{2,18},{18,2},{3,19},{19,3},{4,20},{20... | collective-permute-start | bytes 1572872 | tf_op jit(solution)/shard_map/ppermute | solution.py:468
  90.7 15.2 %copy-start.2 = (bf16[512,512]{1,0:T(8,128)(2,1)}, bf16[512,512]{1,0:T(8,128)(2,1)S(1)}, u32[]{:S(2)}) copy-start(bf16[512,512]{1,0:T(8,128)(2,1)S(1)} %collective-permute-done.2.refs_3_) | copy-start | bytes 1572868
  115.2 6.3 %copy-start.3 = (bf16[3,128,512]{2,1,0:T(8,128)(2,1)S(1)}, bf16[3,128,512]{2,1,0:T(8,128)(2,1)}, u32[]{:S(2)}) copy-start(bf16[3,128,512]{2,1,0:T(8,128)(2,1)} %get-tuple-element.28.refs_2_.d_hbm) | copy-start | bytes 1179652
  115.2 41.3 %all-to-all-start.3 = ((bf16[16,24,2048]{2,1,0:T(8,128)(2,1)}), bf16[16,24,2048]{2,1,0:T(8,128)(2,1)}, u32[]{:S(2)}, u32[]{:S(2)}) async-start(bf16[16,24,2048]{2,1,0:T(8,128)(2,1)} %bitcast.24), calls=%async_computation.3 | async-start | bytes 3145728 | tf_op jit(solution)/shard_map/all_to_all | solution.py:492
  120.3 23.1 %collective-permute-start.3 = (bf16[512,512]{1,0:T(8,128)(2,1)}, bf16[512,512]{1,0:T(8,128)(2,1)S(1)}, u32[]{:S(2)}, u32[]{:S(2)}) collective-permute-start(bf16[512,512]{1,0:T(8,128)(2,1)} %get-tuple-element.29), channel_id=1, source_target_pairs={{0,16},{16,0},{1,17},{17,1},{2,18},{18,2},{3,19},{19,3},{4,20},{20... | collective-permute-start | bytes 1572872 | tf_op jit(solution)/shard_map/ppermute | solution.py:468
  121.6 21.8 %collective-permute-start.4 = (bf16[3,128,512]{2,1,0:T(8,128)(2,1)S(1)}, bf16[3,128,512]{2,1,0:T(8,128)(2,1)}, u32[]{:S(2)}, u32[]{:S(2)}) collective-permute-start(bf16[3,128,512]{2,1,0:T(8,128)(2,1)S(1)} %copy-done.3), channel_id=1, source_target_pairs={{0,16},{16,0},{1,17},{17,1},{2,18},{18,2},{3,19},{19,3},{4,20},{20... | collective-permute-start | bytes 1179656 | tf_op jit(solution)/shard_map/ppermute | solution.py:468
  121.9 4.9 %copy-start.5 = (f32[128,128]{1,0:T(8,128)S(1)}, f32[128,128]{1,0:T(8,128)}, u32[]{:S(2)}) copy-start(f32[128,128]{1,0:T(8,128)} %get-tuple-element.33) | copy-start | bytes 196612
  127.1 15.7 %collective-permute-start.5 = (f32[1,3,4,4,4]{4,3,2,1,0:T(4,128)S(1)}, f32[1,3,4,4,4]{4,3,2,1,0:T(4,128)S(1)}, u32[]{:S(2)}, u32[]{:S(2)}) collective-permute-start(f32[1,3,4,4,4]{4,3,2,1,0:T(4,128)S(1)} %reshape.58), channel_id=1, source_target_pairs={{0,16},{16,0},{1,17},{17,1},{2,18},{18,2},{3,19},{19,3},{4,20},{20... | collective-permute-start | bytes 2312 | tf_op jit(solution)/shard_map/ppermute | solution.py:468
  143.4 0.8 copy-start.4

commit v4 on v3

--- a/solution.py
+++ b/solution.py
@@ -68,7 +68,7 @@
     return [slice(c * chunk, (c + 1) * chunk) for c in range(part // chunk)]
 
 
-def index_body(cap, pieces, own_rows, block_len, chosen_ref, wanted_ref, slot_ref):
+def index_body(cap, pieces, own_rows, block_len, me_ref, chosen_ref, wanted_ref, slot_ref):
     peers, lanes = wanted_ref.shape
     rows = slot_ref.shape[1]
     position = jnp.concatenate(
@@ -81,7 +81,7 @@
     count = jnp.sum(mine, axis=1, keepdims=True)
     earlier = jnp.sum(jnp.where(peer < owner, count, 0.0), axis=0, keepdims=True).astype(jnp.int32)
     rank = iota((1, rows), 1) - earlier
-    slot_ref[...] = owner * (cap * pieces) + rank
+    slot_ref[...] = (owner ^ me_ref[0]) * (cap * pieces) + rank
     lane = iota((lanes, rows), 0)
     hit = jnp.zeros((lanes, rows), F32)
     for j in range(pieces):
@@ -90,11 +90,11 @@
     wanted_ref[...] = dot_nt(marked.astype(BF16), hit.astype(BF16)).astype(jnp.int32)
 
 
-def pick_matrix(cap, pieces, own_rows, requested):
+def pick_matrix(cap, pieces, own_rows, me, requested):
     peers, lanes = requested.shape
     group = cap * pieces
     slots = peers * group
-    peer = iota((peers, group, peers), 0).reshape(slots, peers)
+    peer = iota((peers, group, peers), 0).reshape(slots, peers) ^ me
     spread = dot(
         (peer == iota((slots, peers), 1)).astype(BF16), requested.astype(F32).astype(BF16)
     )
@@ -110,58 +110,75 @@
     return (target == iota((slots, pieces * own_rows), 1)).astype(BF16)
 
 
-def pick_rows(cap, pieces, requested, source, after, name):
+def slab_specs(count, slots, part):
+    return [(shaped((slots // count, part), BF16), HBM)] * count
+
+
+def store_slabs(source_ref, at, outs, sems):
+    size = outs[0].shape[0]
+    return [
+        begin(source_ref.at[k * size : (k + 1) * size, at], out.at[:, at], sems.at[k])
+        for k, out in enumerate(outs)
+    ]
+
+
+def load_slabs(slabs, target_ref, sems):
+    size = slabs[0].shape[0]
+    return [
+        begin(slab, target_ref.at[k * size : (k + 1) * size], sems.at[k])
+        for k, slab in enumerate(slabs)
+    ]
+
+
+def pick_rows(cap, pieces, count, me, requested, source, name):
     own_rows, width = source.shape
     part = width // pieces
     slots = requested.shape[0] * cap * pieces
     columns = chunks_of(part)
 
-    def body(requested_ref, source_ref, *refs):
-        out_ref, rows_ref, sent_ref, in_sem, out_sem = refs[len(after) :]
+    def body(me_ref, requested_ref, source_ref, *refs):
+        outs, (rows_ref, sent_ref, in_sem, out_sem) = refs[:count], refs[count:]
         loads = []
         for n, at in enumerate(columns):
             for j in range(pieces):
                 wide = slice(j * part + at.start, j * part + at.stop)
                 target = rows_ref.at[j * own_rows : (j + 1) * own_rows, at]
                 loads.append(begin(source_ref.at[:, wide], target, in_sem.at[n, j]))
-        pick = pick_matrix(cap, pieces, own_rows, requested_ref[...])
+        pick = pick_matrix(cap, pieces, own_rows, me_ref[0], requested_ref[...])
         stores = []
         for n, at in enumerate(columns):
-            for load in loads[n * pieces : (n + 1) * pieces]:
-                load.wait()
+            wait_all(loads[n * pieces : (n + 1) * pieces])
             sent_ref[:, at] = dot(pick, rows_ref[:, at]).astype(BF16)
-            stores.append(begin(sent_ref.at[:, at], out_ref.at[:, at], out_sem.at[n]))
-        for store in stores:
-            store.wait()
+            stores += store_slabs(sent_ref, at, outs, out_sem.at[n])
+        wait_all(stores)
 
     return call(
         body,
-        [(shaped((slots, part), BF16), HBM)],
-        [(requested, VMEM), (source, HBM)] + [(x, HBM) for x in after],
+        slab_specs(count, slots, part),
+        [(me, SMEM), (requested, VMEM), (source, HBM)],
         name,
         2 * slots * pieces * own_rows * part,
         [
             scratch_like((pieces * own_rows, part), BF16),
             scratch_like((slots, part), BF16),
             pltpu.SemaphoreType.DMA((len(columns), pieces)),
-            pltpu.SemaphoreType.DMA((len(columns),)),
+            pltpu.SemaphoreType.DMA((len(columns), count)),
         ],
-    )[0]
-
-
-def sum_rows(cap, pieces, own_rows, requested, returned):
-    slots, part = returned.shape
+    )
+
+
+def sum_rows(cap, pieces, own_rows, me, requested, returned):
+    count, part = len(returned), returned[0].shape[1]
+    slots = count * returned[0].shape[0]
     columns = chunks_of(part)
 
-    def body(requested_ref, returned_ref, out_ref, got_ref, sum_ref, in_sem, out_sem):
-        loads = [
-            begin(returned_ref.at[:, at], got_ref.at[:, at], in_sem.at[n])
-            for n, at in enumerate(columns)
-        ]
-        pick = pick_matrix(cap, pieces, own_rows, requested_ref[...])
+    def body(me_ref, requested_ref, *refs):
+        slabs, (out_ref, got_ref, sum_ref, in_sem, out_sem) = refs[:count], refs[count:]
+        loads = load_slabs(slabs, got_ref, in_sem)
+        pick = pick_matrix(cap, pieces, own_rows, me_ref[0], requested_ref[...])
+        wait_all(loads)
         stores = []
         for n, at in enumerate(columns):
-            loads[n].wait()
             total = dot_tn(pick, got_ref[:, at]).astype(BF16)
             for j in range(pieces):
                 wide = slice(j * part + at.start, j * part + at.stop)
@@ -169,19 +186,18 @@
                 stores.append(
                     begin(sum_ref.at[:, wide], out_ref.at[:, wide], out_sem.at[n, j])
                 )
-        for store in stores:
-            store.wait()
+        wait_all(stores)
 
     return call(
         body,
         [(shaped((own_rows, part * pieces), BF16), HBM)],
-        [(requested, VMEM), (returned, HBM)],
+        [(me, SMEM), (requested, VMEM)] + [(x, HBM) for x in returned],
         "sum_rows",
         2 * slots * pieces * own_rows * part,
         [
             scratch_like((slots, part), BF16),
             scratch_like((own_rows, part * pieces), BF16),
-            pltpu.SemaphoreType.DMA((len(columns),)),
+            pltpu.SemaphoreType.DMA((count,)),
             pltpu.SemaphoreType.DMA((len(columns), pieces)),
         ],
     )[0]
@@ -206,7 +222,7 @@
 def sides_of(sides, refs):
     if sides == 1:
         return [refs[:1]], refs[1:]
-    return [refs[:1], refs[1:3]], refs[3:]
+    return [refs[:1], refs[1:2]], refs[2:]
 
 
 def wait_all(copies):
@@ -219,18 +235,10 @@
     return (iota((slots, wide.shape[1]), 0) == wide).astype(BF16)
 
 
-def load_rows(got_hbm, got_ref, sems):
-    return [
-        begin(got_hbm.at[:, at], got_ref.at[:, at], sems.at[n])
-        for n, at in enumerate(chunks_of(got_ref.shape[1]))
-    ]
-
-
-def stack_rows(pieces, place, loads, got_ref, out_ref):
+def stack_rows(pieces, place, got_ref, out_ref):
     part = got_ref.shape[1]
     rows, depth = out_ref.shape[0] // NPHM, out_ref.shape[1]
-    for load, at in zip(loads, chunks_of(part)):
-        load.wait()
+    for at in chunks_of(part):
         block = dot_tn(place, got_ref[:, at]).astype(BF16)
         for j in range(pieces):
             column = j * part + at.start
@@ -291,19 +299,21 @@
 
 
 def forward_body(
-    cap, pieces, sides, slot_ref, mix_ref, order_ref, got_hbm, *refs
+    cap, pieces, sides, count, slot_ref, mix_ref, order_ref, *refs
 ):
+    slabs, refs = refs[:count], refs[count:]
     parts, refs = sides_of(sides, refs)
     x_outs, refs = refs[:sides], refs[sides:]
     yg_hbm, yu_hbm, act_hbm, slope_hbm, hid_hbm = refs[:5]
     got_ref, side_ref, x_ref, yg_ref, yu_ref, pre_ref, act_ref, slope_ref, hid_ref = refs[5:14]
     got_sem, side_sem, out_sem = refs[14:]
-    loads = load_rows(got_hbm, got_ref, got_sem)
+    loads = load_slabs(slabs, got_ref, got_sem)
     sides_in = [
         load_factor(order_ref, parts, m, side_ref.at[m], side_sem.at[m]) for m in range(2)
     ]
     place = place_matrix(cap, pieces, got_ref.shape[0], slot_ref[...])
-    stack_rows(pieces, place, loads, got_ref, x_ref)
+    wait_all(loads)
+    stack_rows(pieces, place, got_ref, x_ref)
     stores = store_parts(order_ref, x_ref, x_outs, out_sem)
     wait_all(sides_in[0])
     yg_ref[...] = dot(x_ref[...], side_ref[0])
@@ -336,18 +346,20 @@
 
 
 def backward_body(
-    cap, pieces, sides, after, slot_ref, mix_ref, order_ref, gate_ref, got_hbm, act_hbm, slope_hbm, hid_hbm,
+    cap, pieces, sides, after, count, slot_ref, mix_ref, order_ref, gate_ref, act_hbm, slope_hbm, hid_hbm,
     *refs,
 ):
+    slabs, refs = refs[:count], refs[count:]
     parts, refs = sides_of(sides, refs)
     refs = refs[after:]
-    back_hbm, x_outs, refs = refs[0], refs[1 : 1 + sides], refs[1 + sides :]
+    backs, refs = refs[:count], refs[count:]
+    x_outs, refs = refs[:sides], refs[sides:]
     y_hbm, d_hbm, inner_ref = refs[:3]
     (
         got_ref, side_ref, x_ref, y_ref, d_ref, act_ref, slope_ref, hid_ref, zg_ref, zu_ref, grad_ref,
-        back_ref, got_sem, side_sem, in_sem, out_sem,
+        back_ref, got_sem, side_sem, in_sem, out_sem, back_sem,
     ) = refs[3:]
-    loads = load_rows(got_hbm, got_ref, got_sem)
+    loads = load_slabs(slabs, got_ref, got_sem)
     down_in = load_factor(order_ref, parts, 2, side_ref.at[2], side_sem.at[2])
     flat_in = [
         begin(source, target, in_sem.at[n])
@@ -359,7 +371,8 @@
         load_factor(order_ref, parts, m, side_ref.at[m], side_sem.at[m]) for m in range(2)
     ]
     place = place_matrix(cap, pieces, got_ref.shape[0], slot_ref[...])
-    stack_rows(pieces, place, loads, got_ref, x_ref)
+    wait_all(loads)
+    stack_rows(pieces, place, got_ref, x_ref)
     stores = store_parts(order_ref, x_ref, x_outs, out_sem)
     wait_all(down_in)
     y_ref[...] = dot(x_ref[...], side_ref[2])
@@ -399,7 +412,7 @@
                 grad_ref[a * rows : (a + 1) * rows, start : start + at.stop - at.start]
             )
         back_ref[:, at] = dot(place, jnp.concatenate(blocks, axis=0)).astype(BF16)
-        stores.append(begin(back_ref.at[:, at], back_hbm.at[:, at], out_sem.at[4 + n]))
+        stores += store_slabs(back_ref, at, backs, back_sem.at[n])
     wait_all(stores)
 
 
@@ -450,7 +463,7 @@
     hidden = count * cols
     cap = 3 * own_rows // (2 * peers)
     pieces = 1
-    while (cap * pieces) % 8:
+    while (cap * pieces) % 16:
         pieces *= 2
     lanes = 128
     slots = peers * cap * pieces
@@ -468,34 +481,42 @@
         return lax.ppermute(array, "seq", pair)
 
     if swap:
-        early, late = across(factors[0, :1]), across(factors[0, 1:])
-        factor_parts = [[factors[0]], [early, late]]
+        factor_parts = [[factors[0]], [across(factors)[0]]]
         order = jnp.stack([group, 1 - group]).astype(jnp.int32)
     else:
-        early = late = None
         factor_parts = [[lax.all_gather(factors, "seq", axis=3, tiled=True)[0]]]
         order = jnp.zeros((2,), jnp.int32)
     sides = len(factor_parts)
+    direct = peers <= 16
+    count_slabs = peers if direct else 1
+    me = lax.axis_index("exp").astype(jnp.int32) if direct else jnp.int32(0)
+    me = me.reshape(1)
     sides_in = [(x, HBM) for side in factor_parts for x in side]
 
     wanted, slot = call(
         functools.partial(index_body, cap, pieces, own_rows, block_len),
         [(shaped((peers, lanes), jnp.int32), VMEM), (shaped((1, rows), jnp.int32), VMEM)],
-        [(selection[0], VMEM)],
+        [(me, SMEM), (selection[0], VMEM)],
         "wanted_rows",
         1 << 20,
     )
     requested = lax.all_to_all(wanted, "exp", split_axis=0, concat_axis=0, tiled=True)
 
-    def exchange(array):
-        array = array.reshape(peers, cap * pieces, part)
+    def exchange(slabs):
+        if direct:
+            return [slabs[0]] + [
+                lax.ppermute(slabs[k], "exp", [(n, n ^ k) for n in range(peers)])
+                for k in range(1, peers)
+            ]
+        array = slabs[0].reshape(peers, cap * pieces, part)
         array = lax.all_to_all(array, "exp", split_axis=0, concat_axis=0, tiled=True)
-        return array.reshape(slots, part)
-
-    got_rows = exchange(pick_rows(cap, pieces, requested, tokens, [early] if swap else [], "pick_tokens"))
-    got_grads = exchange(
-        pick_rows(cap, pieces, requested, cotangent, [late] if swap else [], "pick_cotangent")
-    )
+        return [array.reshape(slots, part)]
+
+    def picked(source, name):
+        return pick_rows(cap, pieces, count_slabs, me, requested, source, name)
+
+    got_rows = exchange(picked(tokens, "pick_tokens"))
+    got_grads = exchange(picked(cotangent, "pick_cotangent"))
 
     gate = jax.nn.sigmoid(scores[0].reshape(-1).astype(F32) / 64.0)
     gate_wide = jnp.broadcast_to(gate[:, None], (rows, cols))
@@ -510,25 +531,27 @@
     low_scratch = scratch_like((stacked, hidden), BF16)
     flat_scratch = scratch_like((rows, hidden), F32)
     outs = call(
-        functools.partial(forward_body, cap, pieces, sides),
+        functools.partial(forward_body, cap, pieces, sides, count_slabs),
         split + [mixed, mixed, flat, flat, flat],
-        [(slot, VMEM), (mixing, SMEM), (order, SMEM), (got_rows, HBM)] + sides_in,
+        [(slot, VMEM), (mixing, SMEM), (order, SMEM)]
+        + [(x, HBM) for x in got_rows]
+        + sides_in,
         "forward",
         2 * product,
         [got_scratch, scratch_like((2, depth, hidden), BF16), stack_scratch, mixed_scratch, mixed_scratch]
         + [flat_scratch] * 4
-        + [dma((steps,)), dma((2, sides, count)), dma((7,))],
+        + [dma((count_slabs,)), dma((2, sides, count)), dma((7,))],
     )
     x_parts, (y_gate, y_up, act, slope, hid) = outs[:sides], outs[sides:]
     x_rows = [x_parts[0]] + [across(x) for x in x_parts[1:]]
     after = x_rows[1:]
     outs = call(
-        functools.partial(backward_body, cap, pieces, sides, len(after)),
-        [(shaped((slots, part), BF16), HBM)]
+        functools.partial(backward_body, cap, pieces, sides, len(after), count_slabs),
+        slab_specs(count_slabs, slots, part)
         + split
         + [mixed, (shaped((weights, rows, hidden), BF16), HBM), (shaped((rows, cols), F32), VMEM)],
-        [(slot, VMEM), (mixing, SMEM), (order, SMEM), (gate_wide, VMEM), (got_grads, HBM)]
-        + [(x, HBM) for x in (act, slope, hid)]
+        [(slot, VMEM), (mixing, SMEM), (order, SMEM), (gate_wide, VMEM)]
+        + [(x, HBM) for x in [act, slope, hid] + got_grads]
         + sides_in
         + [(x, HBM) for x in after],
         "backward",
@@ -538,9 +561,11 @@
         + [flat_scratch] * 3
         + [low_scratch] * 2
         + [stack_scratch, got_scratch]
-        + [dma((steps,)), dma((weights, sides, count)), dma((3,)), dma((4 + steps,))],
+        + [dma((count_slabs,)), dma((weights, sides, count)), dma((3,)), dma((4,))]
+        + [dma((steps, count_slabs))],
     )
-    back, g_parts, (y_down, d_own, inner) = outs[0], outs[1 : 1 + sides], outs[1 + sides :]
+    back, outs = outs[:count_slabs], outs[count_slabs:]
+    g_parts, (y_down, d_own, inner) = outs[:sides], outs[sides:]
     returned = exchange(back)
 
     d_rows = [d_own] + [across(d_own) for _ in x_parts[1:]]
@@ -583,7 +608,7 @@
         ).astype(F32)
         mix_grad = lax.psum(mix_part, "seq")
     gate_grad = (jnp.sum(inner, axis=1) * gate * (1.0 - gate)).reshape(selection.shape)
-    token_grad = sum_rows(cap, pieces, own_rows, requested, returned)
+    token_grad = sum_rows(cap, pieces, own_rows, me, requested, returned)
     return token_grad, factor_grad[None], mix_grad, gate_grad
 
 

time: 161 us -> 205 us (1.27)
  starting transfers between devices: 23.9 us -> 66.1 us
  Pallas kernels: 40.6 us -> 44.2 us
  waiting for transfers between devices: 75.7 us -> 72.6 us
    ppermute x0 -> x45, waiting for transfers between devices: none -> 70.8 us  [exchange(): lax.ppermute(slabs[k], 'exp', [(n, n ^ k) for n in range(peers)])]
    ppermute x0 -> x45, starting transfers between devices: none -> 61.8 us  [exchange(): lax.ppermute(slabs[k], 'exp', [(n, n ^ k) for n in range(peers)])]
    ppermute x6 -> x5, waiting for transfers between devices: 48.7 us -> 1.78 us  [across(): return lax.ppermute(array, 'seq', pair)]
    all_to_all x3 -> x0, waiting for transfers between devices: 27.1 us -> none  [exchange(): lax.all_to_all(array, 'exp', split_axis=0, concat_axis=0, tiled=True)]
    all_to_all x3 -> x0, starting transfers between devices: 17.4 us -> none  [exchange(): lax.all_to_all(array, 'exp', split_axis=0, concat_axis=0, tiled=True)]
    pallas_call x8, Pallas kernels: 40.6 us -> 44.2 us  [call(): pl.pallas_call(body, out_shape=[x for x, _ in outs], in_specs=[place for...]
    ppermute x6 -> x5, starting transfers between devices: 6.55 us -> 4.33 us  [across(): return lax.ppermute(array, 'seq', pair)]
  transfers between devices with their start and end apart: 9 -> 50, of which waited for: 6 -> 29; matrix products, arithmetic and copies ran while one was open for 3% -> 3% of each run, Pallas kernels for 15% -> 9%
where the time goes in v4:
time: 205 us; the launch traced here: 203 us
  waiting for transfers between devices  72.6 us (35%)
  starting transfers between devices  66.1 us (32%)
  Pallas kernels  44.2 us (22%)
  blocking collectives  10.7 us (5%)
  local copies, waits for them, and re-layouts  4.69 us (2%)
  other arithmetic  3.67 us (2%)
    ppermute x45, waiting for transfers between devices, exchange(): lax.ppermute(slabs[k], 'exp', [(n, n ^ k) for n in range(peers)])  70.8 us
    ppermute x45, starting transfers between devices, exchange(): lax.ppermute(slabs[k], 'exp', [(n, n ^ k) for n in range(peers)])  61.8 us
    pallas_call x8, Pallas kernels, call(): pl.pallas_call(body, out_shape=[x for x, _ in outs], in_specs=[place for...  44.2 us
    all_to_all x1, blocking collectives, shards(): lax.all_to_all(wanted, 'exp', split_axis=0, concat_axis=0, tiled=True)  10.7 us
    ppermute x5, starting transfers between devices, across(): return lax.ppermute(array, 'seq', pair)  4.33 us
  transfers between devices with their start and end apart: 50, of which 29 were waited for; matrix products, arithmetic and copies ran while one was open for 3% of the time, Pallas kernels for 9%

profile of v4, /device:TPU:13, one launch (start us, length us, event | category | flops | bytes accessed | tf_op | source)
XLA Modules:
  0.0 203.0 jit_solution(9033097691259670203)
XLA Ops:
  3.5 10.7 %all_to_all.11 = s32[16,1,128]{2,1,0:T(1,128)} all-to-all(s32[16,1,128]{2,1,0:T(1,128)} %bitcast.17), channel_id=1, replica_groups=mesh['seq'=2,'exp'=16] {'exp'}, dimensions={0} | all-to-all | bytes 16384 | tf_op jit(solution)/shard_map/all_to_all | solution.py:503
  14.2 4.2 %pick_tokens.1 = (bf16[48,1024]{1,0:T(8,128)(2,1)}, bf16[48,1024]{1,0:T(8,128)(2,1)}, bf16[48,1024]{1,0:T(8,128)(2,1)}, bf16[48,1024]{1,0:T(8,128)(2,1)}, bf16[4...) custom-call(s32[1]{0:T(128)} %bitcast.me_ref, ...), custom_call_target="tpu_custom_call" | custom-call | flops 805306368 | bytes 2629636 | tf_op jit(solution)/shard_map/pick_tokens/pallas_call | solution.py:40
  28.3 3.0 %collective-permute-start.8 = (bf16[48,1024]{1,0:T(8,128)(2,1)}, bf16[48,1024]{1,0:T(8,128)(2,1)S(1)}, u32[]{:S(2)}, u32[]{:S(2)}) collective-permute-start(bf16[48,1024]{1,0:T(8,128)(2,1)} %get-tuple-element.77), channel_id=1, source_target_pairs={{0,9},{1,8},{2,11},{3,10},{4,13},{5,12},{6,15},{7,14},{8,1},{9,0},... | collective-permute-start | bytes 294920 | tf_op jit(solution)/shard_map/ppermute | solution.py:508
  32.6 2.8 %collective-permute-start.10 = (bf16[48,1024]{1,0:T(8,128)(2,1)}, bf16[48,1024]{1,0:T(8,128)(2,1)}, u32[]{:S(2)}, u32[]{:S(2)}) collective-permute-start(bf16[48,1024]{1,0:T(8,128)(2,1)} %get-tuple-element.79), channel_id=1, source_target_pairs={{0,11},{1,10},{2,9},{3,8},{4,15},{5,14},{6,13},{7,12},{8,3},{9,2},... | collective-permute-start | bytes 294920 | tf_op jit(solution)/shard_map/ppermute | solution.py:508
  37.9 4.0 %collective-permute-done.8.refs_9_ = bf16[48,1024]{1,0:T(8,128)(2,1)S(1)} collective-permute-done((bf16[48,1024]{1,0:T(8,128)(2,1)}, bf16[48,1024]{1,0:T(8,128)(2,1)S(1)}, u32[]{:S(2)}, u32[]{:S(2)}) %collective-permute-start.8) | collective-permute-done | bytes 98336 | tf_op jit(solution)/shard_map/ppermute | solution.py:508
  46.2 4.1 %collective-permute-done.10.refs_11_ = bf16[48,1024]{1,0:T(8,128)(2,1)} collective-permute-done((bf16[48,1024]{1,0:T(8,128)(2,1)}, bf16[48,1024]{1,0:T(8,128)(2,1)}, u32[]{:S(2)}, u32[]{:S(2)}) %collective-permute-start.10) | collective-permute-done | bytes 98336 | tf_op jit(solution)/shard_map/ppermute | solution.py:508
  50.3 4.3 %collective-permute-start.14 = (bf16[48,1024]{1,0:T(8,128)(2,1)}, bf16[48,1024]{1,0:T(8,128)(2,1)}, u32[]{:S(2)}, u32[]{:S(2)}) collective-permute-start(bf16[48,1024]{1,0:T(8,128)(2,1)} %get-tuple-element.83), channel_id=1, source_target_pairs={{0,15},{1,14},{2,13},{3,12},{4,11},{5,10},{6,9},{7,8},{8,7},{9,6},... | collective-permute-start | bytes 294920 | tf_op jit(solution)/shard_map/ppermute | solution.py:508
  55.8 5.8 %collective-permute-done.12.refs_13_ = bf16[48,1024]{1,0:T(8,128)(2,1)} collective-permute-done((bf16[48,1024]{1,0:T(8,128)(2,1)}, bf16[48,1024]{1,0:T(8,128)(2,1)}, u32[]{:S(2)}, u32[]{:S(2)}) %collective-permute-start.12) | collective-permute-done | bytes 98336 | tf_op jit(solution)/shard_map/ppermute | solution.py:508
  65.9 7.3 %forward.1 = (bf16[512,512]{1,0:T(8,128)(2,1)}, bf16[512,512]{1,0:T(8,128)(2,1)}, f32[512,512]{1,0:T(8,128)}, f32[512,512]{1,0:T(8,128)}, f32[128,512]{1,0:T(8,1...) custom-call(s32[1,128]{1,0:T(1,128)} %get-tuple-element.67.slot_ref, f32[192]{0:T(256)} %reshape.37.mix_ref, ...), custom_call_target="tpu_custom_call" | custom-call | flops 1073741824 | bytes 8652040 | tf_op jit(solution)/shard_map/forward/pallas_call | solution.py:40
  73.5 4.3 %pick_cotangent.1 = (bf16[48,1024]{1,0:T(8,128)(2,1)}, bf16[48,1024]{1,0:T(8,128)(2,1)}, bf16[48,1024]{1,0:T(8,128)(2,1)}, bf16[48,1024]{1,0:T(8,128)(2,1)}, bf1...) custom-call(s32[1]{0:T(128)} %bitcast.me_ref, ...), custom_call_target="tpu_custom_call" | custom-call | flops 805306368 | bytes 2629636 | tf_op jit(solution)/shard_map/pick_cotangent/pallas_call | solution.py:40
  83.3 2.7 %collective-permute-done.18.refs_3_ = bf16[48,1024]{1,0:T(8,128)(2,1)S(1)} collective-permute-done((bf16[48,1024]{1,0:T(8,128)(2,1)}, bf16[48,1024]{1,0:T(8,128)(2,1)S(1)}, u32[]{:S(2)}, u32[]{:S(2)}) %collective-permute-start.18) | collective-permute-done | bytes 98336 | tf_op jit(solution)/shard_map/ppermute | solution.py:508
  95.9 5.1 %collective-permute-done.24.refs_9_ = bf16[48,1024]{1,0:T(8,128)(2,1)} collective-permute-done((bf16[48,1024]{1,0:T(8,128)(2,1)}, bf16[48,1024]{1,0:T(8,128)(2,1)}, u32[]{:S(2)}, u32[]{:S(2)}) %collective-permute-start.24) | collective-permute-done | bytes 98336 | tf_op jit(solution)/shard_map/ppermute | solution.py:508
  101.0 2.9 %collective-permute-start.28 = (bf16[48,1024]{1,0:T(8,128)(2,1)}, bf16[48,1024]{1,0:T(8,128)(2,1)S(1)}, u32[]{:S(2)}, u32[]{:S(2)}) collective-permute-start(bf16[48,1024]{1,0:T(8,128)(2,1)} %get-tuple-element.100), channel_id=1, source_target_pairs={{0,13},{1,12},{2,15},{3,14},{4,9},{5,8},{6,11},{7,10},{8,5},{9,4},... | collective-permute-start | bytes 294920 | tf_op jit(solution)/shard_map/ppermute | solution.py:508
  106.3 6.8 %collective-permute-start.30 = (bf16[48,1024]{1,0:T(8,128)(2,1)}, bf16[48,1024]{1,0:T(8,128)(2,1)S(1)}, u32[]{:S(2)}, u32[]{:S(2)}) collective-permute-start(bf16[48,1024]{1,0:T(8,128)(2,1)} %get-tuple-element.102), channel_id=1, source_target_pairs={{0,15},{1,14},{2,13},{3,12},{4,11},{5,10},{6,9},{7,8},{8,7},{9,6},... | collective-permute-start | bytes 294920 | tf_op jit(solution)/shard_map/ppermute | solution.py:508
  113.2 6.6 %collective-permute-done.28.refs_13_ = bf16[48,1024]{1,0:T(8,128)(2,1)S(1)} collective-permute-done((bf16[48,1024]{1,0:T(8,128)(2,1)}, bf16[48,1024]{1,0:T(8,128)(2,1)S(1)}, u32[]{:S(2)}, u32[]{:S(2)}) %collective-permute-start.28) | collective-permute-done | bytes 98336 | tf_op jit(solution)/shard_map/ppermute | solution.py:508
  125.0 11.0 %backward.1 = (bf16[48,1024]{1,0:T(8,128)(2,1)}, bf16[48,1024]{1,0:T(8,128)(2,1)}, bf16[48,1024]{1,0:T(8,128)(2,1)}, bf16[48,1024]{1,0:T(8,128)(2,1)}, bf16[48,1...) custom-call(s32[1,128]{1,0:T(1,128)} %get-tuple-element.67.slot_ref,, ...), custom_call_target="tpu_custom_call" | custom-call | flops 1610612736 | bytes 10224904 | tf_op jit(solution)/shard_map/backward/pallas_call | solution.py:40
  138.2 3.9 %mix_partials.1 = f32[192,128]{1,0:T(8,128)} custom-call(f32[512,512]{1,0:T(8,128)} %get-tuple-element.124.yg_hbm, f32[512,512]{1,0:T(8,128)} %get-tuple-element.125.yu_hbm, f32[512,512]{1,0:T(8,128)} %get-tuple-element.126.yd_hbm, bf16[3,128,512]{2,1,0:T(8,128)(2,1)} %get-tuple-element.122.refs_2_.d_hbm), custom_call_target="tpu_custom_call" | custom-call | flops 6291456 | bytes 3637248 | tf_op jit(solution)/shard_map/mix_partials/pallas_call | solution.py:40
  152.9 2.8 %collective-permute-start.40 = (bf16[48,1024]{1,0:T(8,128)(2,1)}, bf16[48,1024]{1,0:T(8,128)(2,1)S(1)}, u32[]{:S(2)}, u32[]{:S(2)}) collective-permute-start(bf16[48,1024]{1,0:T(8,128)(2,1)} %get-tuple-element.113), channel_id=1, source_target_pairs={{0,9},{1,8},{2,11},{3,10},{4,13},{5,12},{6,15},{7,14},{8,1},{9,0},... | collective-permute-start | bytes 294920 | tf_op jit(solution)/shard_map/ppermute | solution.py:508
  160.3 5.4 %collective-permute-start.43 = (bf16[48,1024]{1,0:T(8,128)(2,1)}, bf16[48,1024]{1,0:T(8,128)(2,1)S(1)}, u32[]{:S(2)}, u32[]{:S(2)}) collective-permute-start(bf16[48,1024]{1,0:T(8,128)(2,1)} %get-tuple-element.116), channel_id=1, source_target_pairs={{0,12},{1,13},{2,14},{3,15},{4,8},{5,9},{6,10},{7,11},{8,4},{9,5},... | collective-permute-start | bytes 294920 | tf_op jit(solution)/shard_map/ppermute | solution.py:508
  167.5 3.6 %collective-permute-done.41.refs_10_ = bf16[48,1024]{1,0:T(8,128)(2,1)S(1)} collective-permute-done((bf16[48,1024]{1,0:T(8,128)(2,1)}, bf16[48,1024]{1,0:T(8,128)(2,1)S(1)}, u32[]{:S(2)}, u32[]{:S(2)}) %collective-permute-start.41) | collective-permute-done | bytes 98336 | tf_op jit(solution)/shard_map/ppermute | solution.py:508
  173.3 5.8 %collective-permute-done.43.refs_12_ = bf16[48,1024]{1,0:T(8,128)(2,1)S(1)} collective-permute-done((bf16[48,1024]{1,0:T(8,128)(2,1)}, bf16[48,1024]{1,0:T(8,128)(2,1)S(1)}, u32[]{:S(2)}, u32[]{:S(2)}) %collective-permute-start.43) | collective-permute-done | bytes 98336 | tf_op jit(solution)/shard_map/ppermute | solution.py:508
  181.1 4.4 %collective-permute-done.44.refs_13_ = bf16[48,1024]{1,0:T(8,128)(2,1)S(1)} collective-permute-done((bf16[48,1024]{1,0:T(8,128)(2,1)}, bf16[48,1024]{1,0:T(8,128)(2,1)S(1)}, u32[]{:S(2)}, u32[]{:S(2)}) %collective-permute-start.44) | collective-permute-done | bytes 98336 | tf_op jit(solution)/shard_map/ppermute | solution.py:508
  190.2 4.1 %sum_rows.1 = bf16[128,4096]{1,0:T(8,128)(2,1)} custom-call(s32[1]{0:T(128)} %bitcast.me_ref, s32[16,128]{1,0:T(8,128)} %bitcast.16, bf16[48,1024]{1,0:T(8,128)(2,1)} %get-tuple-element.104.refs_0_, bf16[48,1024]{1,0:T(8,128)(2,1)} %copy-done.23, bf16[48,1024]{1,0:T(8,128)(2,1)} %collective-permute-done.33.refs_2_, ...), custom_call_target="tpu_custom_call" | custom-call | flops 805306368 | bytes 2629636 | tf_op jit(solution)/shard_map/sum_rows/pallas_call | solution.py:40
  195.0 7.8 %factor_grad.1 = f32[3,4,512,128]{3,2,1,0:T(8,128)} custom-call(f32[192]{0:T(256)} %reshape.37.mix_ref, bf16[512,512]{1,0:T(8,128)(2,1)} %get-tuple-element.120.refs_0_, bf16[512,512]{1,0:T(8,128)(2,1)} %get-tuple-element.121.refs_1_, bf16[3,128,512]{2,1,0:T(8,128)(2,1)} %get-tuple-element.122.refs_2_.d_hbm, bf16[512,512]{1,0:T(8,128)(2,1)} %copy-done, ...), custom_call_target="tpu_custom_call" | custom-call | flops 1610612736 | bytes 6030080 | tf_op jit(solution)/shard_map/factor_grad/pallas_call | solution.py:40
  (166 shorter events, 78.5 us)
Async XLA Ops:
  0.6 65.2 %collective-permute-start.15 = (bf16[1,3,4,512,128]{4,3,2,1,0:T(8,128)(2,1)}, bf16[1,3,4,512,128]{4,3,2,1,0:T(8,128)(2,1)}, u32[]{:S(2)}, u32[]{:S(2)}) collective-permute-start(bf16[1,3,4,512,128]{4,3,2,1,0:T(8,128)(2,1)} %param.8), channel_id=1, source_target_pairs={{0,16},{16,0},{1,17},{17,1},{2,18},{18,2},{3,19},{19,3},{4,20},{20... | collective-permute-start | bytes 4718600 | tf_op jit(solution)/shard_map/ppermute | solution.py:481
  31.3 13.8 %collective-permute-start.9 = (bf16[48,1024]{1,0:T(8,128)(2,1)}, bf16[48,1024]{1,0:T(8,128)(2,1)S(1)}, u32[]{:S(2)}, u32[]{:S(2)}) collective-permute-start(bf16[48,1024]{1,0:T(8,128)(2,1)} %get-tuple-element.78), channel_id=1, source_target_pairs={{0,10},{1,11},{2,8},{3,9},{4,14},{5,15},{6,12},{7,13},{8,2},{9,3},... | collective-permute-start | bytes 294920 | tf_op jit(solution)/shard_map/ppermute | solution.py:508
  32.6 17.7 %collective-permute-start.10 = (bf16[48,1024]{1,0:T(8,128)(2,1)}, bf16[48,1024]{1,0:T(8,128)(2,1)}, u32[]{:S(2)}, u32[]{:S(2)}) collective-permute-start(bf16[48,1024]{1,0:T(8,128)(2,1)} %get-tuple-element.79), channel_id=1, source_target_pairs={{0,11},{1,10},{2,9},{3,8},{4,15},{5,14},{6,13},{7,12},{8,3},{9,2},... | collective-permute-start | bytes 294920 | tf_op jit(solution)/shard_map/ppermute | solution.py:508
  36.9 18.9 %collective-permute-start.11 = (bf16[48,1024]{1,0:T(8,128)(2,1)}, bf16[48,1024]{1,0:T(8,128)(2,1)}, u32[]{:S(2)}, u32[]{:S(2)}) collective-permute-start(bf16[48,1024]{1,0:T(8,128)(2,1)} %get-tuple-element.80), channel_id=1, source_target_pairs={{0,12},{1,13},{2,14},{3,15},{4,8},{5,9},{6,10},{7,11},{8,4},{9,5},... | collective-permute-start | bytes 294920 | tf_op jit(solution)/shard_map/ppermute | solution.py:508
  41.9 19.7 %collective-permute-start.12 = (bf16[48,1024]{1,0:T(8,128)(2,1)}, bf16[48,1024]{1,0:T(8,128)(2,1)}, u32[]{:S(2)}, u32[]{:S(2)}) collective-permute-start(bf16[48,1024]{1,0:T(8,128)(2,1)} %get-tuple-element.81), channel_id=1, source_target_pairs={{0,13},{1,12},{2,15},{3,14},{4,9},{5,8},{6,11},{7,10},{8,5},{9,4},... | collective-permute-start | bytes 294920 | tf_op jit(solution)/shard_map/ppermute | solution.py:508
  45.0 18.6 %collective-permute-start.13 = (bf16[48,1024]{1,0:T(8,128)(2,1)}, bf16[48,1024]{1,0:T(8,128)(2,1)}, u32[]{:S(2)}, u32[]{:S(2)}) collective-permute-start(bf16[48,1024]{1,0:T(8,128)(2,1)} %get-tuple-element.82), channel_id=1, source_target_pairs={{0,14},{1,15},{2,12},{3,13},{4,10},{5,11},{6,8},{7,9},{8,6},{9,7},... | collective-permute-start | bytes 294920 | tf_op jit(solution)/shard_map/ppermute | solution.py:508
  50.3 15.5 %collective-permute-start.14 = (bf16[48,1024]{1,0:T(8,128)(2,1)}, bf16[48,1024]{1,0:T(8,128)(2,1)}, u32[]{:S(2)}, u32[]{:S(2)}) collective-permute-start(bf16[48,1024]{1,0:T(8,128)(2,1)} %get-tuple-element.83), channel_id=1, source_target_pairs={{0,15},{1,14},{2,13},{3,12},{4,11},{5,10},{6,9},{7,8},{8,7},{9,6},... | collective-permute-start | bytes 294920 | tf_op jit(solution)/shard_map/ppermute | solution.py:508
  73.2 50.9 %collective-permute-start.31 = (bf16[512,512]{1,0:T(8,128)(2,1)}, bf16[512,512]{1,0:T(8,128)(2,1)S(1)}, u32[]{:S(2)}, u32[]{:S(2)}) collective-permute-start(bf16[512,512]{1,0:T(8,128)(2,1)} %get-tuple-element.103), channel_id=1, source_target_pairs={{0,16},{16,0},{1,17},{17,1},{2,18},{18,2},{3,19},{19,3},{4,20},{20... | collective-permute-start | bytes 1572872 | tf_op jit(solution)/shard_map/ppermute | solution.py:481
  88.9 15.0 %collective-permute-start.25 = (bf16[48,1024]{1,0:T(8,128)(2,1)}, bf16[48,1024]{1,0:T(8,128)(2,1)}, u32[]{:S(2)}, u32[]{:S(2)}) collective-permute-start(bf16[48,1024]{1,0:T(8,128)(2,1)} %get-tuple-element.97), channel_id=1, source_target_pairs={{0,10},{1,11},{2,8},{3,9},{4,14},{5,15},{6,12},{7,13},{8,2},{9,3},... | collective-permute-start | bytes 294920 | tf_op jit(solution)/shard_map/ppermute | solution.py:508
  95.1 18.0 %collective-permute-start.27 = (bf16[48,1024]{1,0:T(8,128)(2,1)}, bf16[48,1024]{1,0:T(8,128)(2,1)S(1)}, u32[]{:S(2)}, u32[]{:S(2)}) collective-permute-start(bf16[48,1024]{1,0:T(8,128)(2,1)} %get-tuple-element.99), channel_id=1, source_target_pairs={{0,12},{1,13},{2,14},{3,15},{4,8},{5,9},{6,10},{7,11},{8,4},{9,5},... | collective-permute-start | bytes 294920 | tf_op jit(solution)/shard_map/ppermute | solution.py:508
  101.0 18.8 %collective-permute-start.28 = (bf16[48,1024]{1,0:T(8,128)(2,1)}, bf16[48,1024]{1,0:T(8,128)(2,1)S(1)}, u32[]{:S(2)}, u32[]{:S(2)}) collective-permute-start(bf16[48,1024]{1,0:T(8,128)(2,1)} %get-tuple-element.100), channel_id=1, source_target_pairs={{0,13},{1,12},{2,15},{3,14},{4,9},{5,8},{6,11},{7,10},{8,5},{9,4},... | collective-permute-start | bytes 294920 | tf_op jit(solution)/shard_map/ppermute | solution.py:508
  104.0 17.5 %collective-permute-start.29 = (bf16[48,1024]{1,0:T(8,128)(2,1)}, bf16[48,1024]{1,0:T(8,128)(2,1)S(1)}, u32[]{:S(2)}, u32[]{:S(2)}) collective-permute-start(bf16[48,1024]{1,0:T(8,128)(2,1)} %get-tuple-element.101), channel_id=1, source_target_pairs={{0,14},{1,15},{2,12},{3,13},{4,10},{5,11},{6,8},{7,9},{8,6},{9,7},... | collective-permute-start | bytes 294920 | tf_op jit(solution)/shard_map/ppermute | solution.py:508
  106.3 17.8 %collective-permute-start.30 = (bf16[48,1024]{1,0:T(8,128)(2,1)}, bf16[48,1024]{1,0:T(8,128)(2,1)S(1)}, u32[]{:S(2)}, u32[]{:S(2)}) collective-permute-start(bf16[48,1024]{1,0:T(8,128)(2,1)} %get-tuple-element.102), channel_id=1, source_target_pairs={{0,15},{1,14},{2,13},{3,12},{4,11},{5,10},{6,9},{7,8},{8,7},{9,6},... | collective-permute-start | bytes 294920 | tf_op jit(solution)/shard_map/ppermute | solution.py:508
  136.0 14.3 %collective-permute-start.33 = (bf16[48,1024]{1,0:T(8,128)(2,1)}, bf16[48,1024]{1,0:T(8,128)(2,1)}, u32[]{:S(2)}, u32[]{:S(2)}) collective-permute-start(bf16[48,1024]{1,0:T(8,128)(2,1)} %get-tuple-element.106), channel_id=1, source_target_pairs={{0,2},{1,3},{2,0},{3,1},{4,6},{5,7},{6,4},{7,5},{8,10},{9,11},{10,... | collective-permute-start | bytes 294920 | tf_op jit(solution)/shard_map/ppermute | solution.py:508
  136.3 14.1 %collective-permute-start.34 = (bf16[48,1024]{1,0:T(8,128)(2,1)}, bf16[48,1024]{1,0:T(8,128)(2,1)}, u32[]{:S(2)}, u32[]{:S(2)}) collective-permute-start(bf16[48,1024]{1,0:T(8,128)(2,1)} %get-tuple-element.107), channel_id=1, source_target_pairs={{0,3},{1,2},{2,1},{3,0},{4,7},{5,6},{6,5},{7,4},{8,11},{9,10},{10,... | collective-permute-start | bytes 294920 | tf_op jit(solution)/shard_map/ppermute | solution.py:508
  138.2 14.3 %collective-permute-start.35 = (bf16[48,1024]{1,0:T(8,128)(2,1)}, bf16[48,1024]{1,0:T(8,128)(2,1)}, u32[]{:S(2)}, u32[]{:S(2)}) collective-permute-start(bf16[48,1024]{1,0:T(8,128)(2,1)} %get-tuple-element.108), channel_id=1, source_target_pairs={{0,4},{1,5},{2,6},{3,7},{4,0},{5,1},{6,2},{7,3},{8,12},{9,13},{10,... | collective-permute-start | bytes 294920 | tf_op jit(solution)/shard_map/ppermute | solution.py:508
  149.2 45.0 %collective-permute-start.47 = (bf16[512,512]{1,0:T(8,128)(2,1)}, bf16[512,512]{1,0:T(8,128)(2,1)S(1)}, u32[]{:S(2)}, u32[]{:S(2)}) collective-permute-start(bf16[512,512]{1,0:T(8,128)(2,1)} %get-tuple-element.123), channel_id=1, source_target_pairs={{0,16},{16,0},{1,17},{17,1},{2,18},{18,2},{3,19},{19,3},{4,20},{20... | collective-permute-start | bytes 1572872 | tf_op jit(solution)/shard_map/ppermute | solution.py:481
  152.9 14.1 %collective-permute-start.40 = (bf16[48,1024]{1,0:T(8,128)(2,1)}, bf16[48,1024]{1,0:T(8,128)(2,1)S(1)}, u32[]{:S(2)}, u32[]{:S(2)}) collective-permute-start(bf16[48,1024]{1,0:T(8,128)(2,1)} %get-tuple-element.113), channel_id=1, source_target_pairs={{0,9},{1,8},{2,11},{3,10},{4,13},{5,12},{6,15},{7,14},{8,1},{9,0},... | collective-permute-start | bytes 294920 | tf_op jit(solution)/shard_map/ppermute | solution.py:508
  156.3 14.8 %collective-permute-start.41 = (bf16[48,1024]{1,0:T(8,128)(2,1)}, bf16[48,1024]{1,0:T(8,128)(2,1)S(1)}, u32[]{:S(2)}, u32[]{:S(2)}) collective-permute-start(bf16[48,1024]{1,0:T(8,128)(2,1)} %get-tuple-element.114), channel_id=1, source_target_pairs={{0,10},{1,11},{2,8},{3,9},{4,14},{5,15},{6,12},{7,13},{8,2},{9,3},... | collective-permute-start | bytes 294920 | tf_op jit(solution)/shard_map/ppermute | solution.py:508
  158.5 14.9 %collective-permute-start.42 = (bf16[48,1024]{1,0:T(8,128)(2,1)}, bf16[48,1024]{1,0:T(8,128)(2,1)S(1)}, u32[]{:S(2)}, u32[]{:S(2)}) collective-permute-start(bf16[48,1024]{1,0:T(8,128)(2,1)} %get-tuple-element.115), channel_id=1, source_target_pairs={{0,11},{1,10},{2,9},{3,8},{4,15},{5,14},{6,13},{7,12},{8,3},{9,2},... | collective-permute-start | bytes 294920 | tf_op jit(solution)/shard_map/ppermute | solution.py:508
  160.3 18.8 %collective-permute-start.43 = (bf16[48,1024]{1,0:T(8,128)(2,1)}, bf16[48,1024]{1,0:T(8,128)(2,1)S(1)}, u32[]{:S(2)}, u32[]{:S(2)}) collective-permute-start(bf16[48,1024]{1,0:T(8,128)(2,1)} %get-tuple-element.116), channel_id=1, source_target_pairs={{0,12},{1,13},{2,14},{3,15},{4,8},{5,9},{6,10},{7,11},{8,4},{9,5},... | collective-permute-start | bytes 294920 | tf_op jit(solution)/shard_map/ppermute | solution.py:508
  167.0 27.2 %collective-permute-start.48 = (bf16[3,128,512]{2,1,0:T(8,128)(2,1)S(1)}, bf16[3,128,512]{2,1,0:T(8,128)(2,1)}, u32[]{:S(2)}, u32[]{:S(2)}) collective-permute-start(bf16[3,128,512]{2,1,0:T(8,128)(2,1)S(1)} %copy-done.1), channel_id=1, source_target_pairs={{0,16},{16,0},{1,17},{17,1},{2,18},{18,2},{3,19},{19,3},{4,20},{20... | collective-permute-start | bytes 1179656 | tf_op jit(solution)/shard_map/ppermute | solution.py:481
  171.1 14.4 %collective-permute-start.44 = (bf16[48,1024]{1,0:T(8,128)(2,1)}, bf16[48,1024]{1,0:T(8,128)(2,1)S(1)}, u32[]{:S(2)}, u32[]{:S(2)}) collective-permute-start(bf16[48,1024]{1,0:T(8,128)(2,1)} %get-tuple-element.117), channel_id=1, source_target_pairs={{0,13},{1,12},{2,15},{3,14},{4,9},{5,8},{6,11},{7,10},{8,5},{9,4},... | collective-permute-start | bytes 294920 | tf_op jit(solution)/shard_map/ppermute | solution.py:508
  173.3 14.0 %collective-permute-start.45 = (bf16[48,1024]{1,0:T(8,128)(2,1)}, bf16[48,1024]{1,0:T(8,128)(2,1)S(1)}, u32[]{:S(2)}, u32[]{:S(2)}) collective-permute-start(bf16[48,1024]{1,0:T(8,128)(2,1)} %get-tuple-element.118), channel_id=1, source_target_pairs={{0,14},{1,15},{2,12},{3,13},{4,10},{5,11},{6,8},{7,9},{8,6},{9,7},... | collective-permute-start | bytes 294920 | tf_op jit(solution)/shard_map/ppermute | solution.py:508
  (61 other events, 988.1 us)

commit v5 on v4

--- a/solution.py
+++ b/solution.py
@@ -68,7 +68,15 @@
     return [slice(c * chunk, (c + 1) * chunk) for c in range(part // chunk)]
 
 
-def index_body(cap, pieces, own_rows, block_len, me_ref, chosen_ref, wanted_ref, slot_ref):
+def position_of(peers, direct, me, peer):
+    if not direct:
+        return peer
+    half = peers // 2
+    apart = peer ^ me
+    return jnp.where(apart < half, peer & (half - 1), apart)
+
+
+def index_body(cap, pieces, own_rows, block_len, direct, me_ref, chosen_ref, wanted_ref, slot_ref):
     peers, lanes = wanted_ref.shape
     rows = slot_ref.shape[1]
     position = jnp.concatenate(
@@ -81,7 +89,8 @@
     count = jnp.sum(mine, axis=1, keepdims=True)
     earlier = jnp.sum(jnp.where(peer < owner, count, 0.0), axis=0, keepdims=True).astype(jnp.int32)
     rank = iota((1, rows), 1) - earlier
-    slot_ref[...] = (owner ^ me_ref[0]) * (cap * pieces) + rank
+    place = position_of(peers, direct, me_ref[0], owner)
+    slot_ref[...] = place * (cap * pieces) + rank
     lane = iota((lanes, rows), 0)
     hit = jnp.zeros((lanes, rows), F32)
     for j in range(pieces):
@@ -90,19 +99,18 @@
     wanted_ref[...] = dot_nt(marked.astype(BF16), hit.astype(BF16)).astype(jnp.int32)
 
 
-def pick_matrix(cap, pieces, own_rows, me, requested):
+def pick_matrix(cap, pieces, own_rows, direct, me, requested, first, count):
     peers, lanes = requested.shape
     group = cap * pieces
-    slots = peers * group
-    peer = iota((peers, group, peers), 0).reshape(slots, peers) ^ me
-    spread = dot(
-        (peer == iota((slots, peers), 1)).astype(BF16), requested.astype(F32).astype(BF16)
-    )
-    place = iota((peers, group, lanes), 1).reshape(slots, lanes)
+    slots = count * group
+    place = iota((count, group, peers), 0).reshape(slots, peers) + first
+    peer = position_of(peers, direct, me, iota((slots, peers), 1))
+    spread = dot((peer == place).astype(BF16), requested.astype(F32).astype(BF16))
+    rank = iota((count, group, lanes), 1).reshape(slots, lanes)
     row = jnp.sum(
-        jnp.where(place == iota((slots, lanes), 1), spread, 0.0), axis=1, keepdims=True
+        jnp.where(rank == iota((slots, lanes), 1), spread, 0.0), axis=1, keepdims=True
     ).astype(jnp.int32)
-    piece = iota((peers, group, 1), 1).reshape(slots, 1)
+    piece = iota((count, group, 1), 1).reshape(slots, 1)
     shift = jnp.zeros((slots, 1), jnp.int32)
     for j in range(1, pieces):
         shift = shift + jnp.where(piece >= j * cap, own_rows, 0)
@@ -110,41 +118,47 @@
     return (target == iota((slots, pieces * own_rows), 1)).astype(BF16)
 
 
-def slab_specs(count, slots, part):
-    return [(shaped((slots // count, part), BF16), HBM)] * count
+def slab_specs(sizes, part):
+    return [(shaped((size, part), BF16), HBM) for size in sizes]
 
 
 def store_slabs(source_ref, at, outs, sems):
-    size = outs[0].shape[0]
-    return [
-        begin(source_ref.at[k * size : (k + 1) * size, at], out.at[:, at], sems.at[k])
-        for k, out in enumerate(outs)
-    ]
+    copies, start = [], 0
+    for k, out in enumerate(outs):
+        stop = start + out.shape[0]
+        copies.append(begin(source_ref.at[start:stop, at], out.at[:, at], sems.at[k]))
+        start = stop
+    return copies
 
 
 def load_slabs(slabs, target_ref, sems):
-    size = slabs[0].shape[0]
-    return [
-        begin(slab, target_ref.at[k * size : (k + 1) * size], sems.at[k])
-        for k, slab in enumerate(slabs)
-    ]
-
-
-def pick_rows(cap, pieces, count, me, requested, source, name):
+    copies, start = [], 0
+    for k, slab in enumerate(slabs):
+        stop = start + slab.shape[0]
+        copies.append(begin(slab, target_ref.at[start:stop], sems.at[k]))
+        start = stop
+    return copies
+
+
+def pick_rows(cap, pieces, direct, first, sizes, me, requested, source, after, name):
     own_rows, width = source.shape
     part = width // pieces
-    slots = requested.shape[0] * cap * pieces
+    slots = sum(sizes)
+    peers = slots // (cap * pieces)
     columns = chunks_of(part)
 
     def body(me_ref, requested_ref, source_ref, *refs):
-        outs, (rows_ref, sent_ref, in_sem, out_sem) = refs[:count], refs[count:]
+        refs = refs[len(after) :]
+        outs, (rows_ref, sent_ref, in_sem, out_sem) = refs[: len(sizes)], refs[len(sizes) :]
         loads = []
         for n, at in enumerate(columns):
             for j in range(pieces):
                 wide = slice(j * part + at.start, j * part + at.stop)
                 target = rows_ref.at[j * own_rows : (j + 1) * own_rows, at]
                 loads.append(begin(source_ref.at[:, wide], target, in_sem.at[n, j]))
-        pick = pick_matrix(cap, pieces, own_rows, me_ref[0], requested_ref[...])
+        pick = pick_matrix(
+            cap, pieces, own_rows, direct, me_ref[0], requested_ref[...], first, peers
+        )
         stores = []
         for n, at in enumerate(columns):
             wait_all(loads[n * pieces : (n + 1) * pieces])
@@ -154,28 +168,29 @@
 
     return call(
         body,
-        slab_specs(count, slots, part),
-        [(me, SMEM), (requested, VMEM), (source, HBM)],
+        slab_specs(sizes, part),
+        [(me, SMEM), (requested, VMEM), (source, HBM)] + [(x, HBM) for x in after],
         name,
         2 * slots * pieces * own_rows * part,
         [
             scratch_like((pieces * own_rows, part), BF16),
             scratch_like((slots, part), BF16),
             pltpu.SemaphoreType.DMA((len(columns), pieces)),
-            pltpu.SemaphoreType.DMA((len(columns), count)),
+            pltpu.SemaphoreType.DMA((len(columns), len(sizes))),
         ],
     )
 
 
-def sum_rows(cap, pieces, own_rows, me, requested, returned):
+def sum_rows(cap, pieces, own_rows, direct, me, requested, returned):
     count, part = len(returned), returned[0].shape[1]
-    slots = count * returned[0].shape[0]
+    slots = sum(x.shape[0] for x in returned)
+    peers = slots // (cap * pieces)
     columns = chunks_of(part)
 
     def body(me_ref, requested_ref, *refs):
         slabs, (out_ref, got_ref, sum_ref, in_sem, out_sem) = refs[:count], refs[count:]
         loads = load_slabs(slabs, got_ref, in_sem)
-        pick = pick_matrix(cap, pieces, own_rows, me_ref[0], requested_ref[...])
+        pick = pick_matrix(cap, pieces, own_rows, direct, me_ref[0], requested_ref[...], 0, peers)
         wait_all(loads)
         stores = []
         for n, at in enumerate(columns):
@@ -299,10 +314,11 @@
 
 
 def forward_body(
-    cap, pieces, sides, count, slot_ref, mix_ref, order_ref, *refs
+    cap, pieces, sides, after, count, slot_ref, mix_ref, order_ref, *refs
 ):
     slabs, refs = refs[:count], refs[count:]
     parts, refs = sides_of(sides, refs)
+    refs = refs[after:]
     x_outs, refs = refs[:sides], refs[sides:]
     yg_hbm, yu_hbm, act_hbm, slope_hbm, hid_hbm = refs[:5]
     got_ref, side_ref, x_ref, yg_ref, yu_ref, pre_ref, act_ref, slope_ref, hid_ref = refs[5:14]
@@ -487,14 +503,17 @@
         factor_parts = [[lax.all_gather(factors, "seq", axis=3, tiled=True)[0]]]
         order = jnp.zeros((2,), jnp.int32)
     sides = len(factor_parts)
-    direct = peers <= 16
-    count_slabs = peers if direct else 1
+    direct = peers == 16
+    half, slab = peers // 2, cap * pieces
+    near, far = (half, half) if direct else (peers, 0)
+    sizes = [near * slab] + [slab] * far
+    count_slabs = len(sizes)
     me = lax.axis_index("exp").astype(jnp.int32) if direct else jnp.int32(0)
     me = me.reshape(1)
     sides_in = [(x, HBM) for side in factor_parts for x in side]
 
     wanted, slot = call(
-        functools.partial(index_body, cap, pieces, own_rows, block_len),
+        functools.partial(index_body, cap, pieces, own_rows, block_len, direct),
         [(shaped((peers, lanes), jnp.int32), VMEM), (shaped((1, rows), jnp.int32), VMEM)],
         [(me, SMEM), (selection[0], VMEM)],
         "wanted_rows",
@@ -502,21 +521,47 @@
     )
     requested = lax.all_to_all(wanted, "exp", split_axis=0, concat_axis=0, tiled=True)
 
-    def exchange(slabs):
-        if direct:
-            return [slabs[0]] + [
-                lax.ppermute(slabs[k], "exp", [(n, n ^ k) for n in range(peers)])
-                for k in range(1, peers)
+    halves = [list(range(half)), list(range(half, peers))] if direct else None
+
+    def exchange_near(array):
+        array = array.reshape(near, slab, part)
+        array = lax.all_to_all(
+            array, "exp", split_axis=0, concat_axis=0, axis_index_groups=halves, tiled=True
+        )
+        return array.reshape(near * slab, part)
+
+    def exchange_far(slabs):
+        return [
+            lax.ppermute(x, "exp", [(n, n ^ (half + k)) for n in range(peers)])
+            for k, x in enumerate(slabs)
+        ]
+
+    if direct:
+        far_sizes = [slab] * far
+        pick_of = functools.partial(pick_rows, cap, pieces, direct)
+        far_rows = exchange_far(
+            pick_of(half, far_sizes, me, requested, tokens, [], "pick_tokens_far")
+        )
+        near_rows = pick_of(0, sizes[:1], me, requested, tokens, far_rows[:1], "pick_tokens_near")
+        got_rows = [exchange_near(near_rows[0])] + far_rows
+        far_grads = exchange_far(
+            pick_of(half, far_sizes, me, requested, cotangent, far_rows[1:2], "pick_cotangent_far")
+        )
+        near_grads = pick_of(
+            0, sizes[:1], me, requested, cotangent, far_rows[4:5], "pick_cotangent_near"
+        )
+        got_grads = [exchange_near(near_grads[0])] + far_grads
+        before_forward = far_grads[:4]
+    else:
+        got_rows, got_grads = [
+            [
+                exchange_near(
+                    pick_rows(cap, pieces, direct, 0, sizes, me, requested, source, [], name)[0]
+                )
             ]
-        array = slabs[0].reshape(peers, cap * pieces, part)
-        array = lax.all_to_all(array, "exp", split_axis=0, concat_axis=0, tiled=True)
-        return [array.reshape(slots, part)]
-
-    def picked(source, name):
-        return pick_rows(cap, pieces, count_slabs, me, requested, source, name)
-
-    got_rows = exchange(picked(tokens, "pick_tokens"))
-    got_grads = exchange(picked(cotangent, "pick_cotangent"))
+            for source, name in ((tokens, "pick_tokens"), (cotangent, "pick_cotangent"))
+        ]
+        before_forward = []
 
     gate = jax.nn.sigmoid(scores[0].reshape(-1).astype(F32) / 64.0)
     gate_wide = jnp.broadcast_to(gate[:, None], (rows, cols))
@@ -531,11 +576,12 @@
     low_scratch = scratch_like((stacked, hidden), BF16)
     flat_scratch = scratch_like((rows, hidden), F32)
     outs = call(
-        functools.partial(forward_body, cap, pieces, sides, count_slabs),
+        functools.partial(forward_body, cap, pieces, sides, len(before_forward), count_slabs),
         split + [mixed, mixed, flat, flat, flat],
         [(slot, VMEM), (mixing, SMEM), (order, SMEM)]
         + [(x, HBM) for x in got_rows]
-        + sides_in,
+        + sides_in
+        + [(x, HBM) for x in before_forward],
         "forward",
         2 * product,
         [got_scratch, scratch_like((2, depth, hidden), BF16), stack_scratch, mixed_scratch, mixed_scratch]
@@ -547,7 +593,7 @@
     after = x_rows[1:]
     outs = call(
         functools.partial(backward_body, cap, pieces, sides, len(after), count_slabs),
-        slab_specs(count_slabs, slots, part)
+        slab_specs(sizes, part)
         + split
         + [mixed, (shaped((weights, rows, hidden), BF16), HBM), (shaped((rows, cols), F32), VMEM)],
         [(slot, VMEM), (mixing, SMEM), (order, SMEM), (gate_wide, VMEM)]
@@ -566,7 +612,7 @@
     )
     back, outs = outs[:count_slabs], outs[count_slabs:]
     g_parts, (y_down, d_own, inner) = outs[:sides], outs[sides:]
-    returned = exchange(back)
+    returned = [exchange_near(back[0])] + exchange_far(back[1:])
 
     d_rows = [d_own] + [across(d_own) for _ in x_parts[1:]]
     g_rows = [g_parts[0]] + [across(x) for x in g_parts[1:]]
@@ -608,7 +654,7 @@
         ).astype(F32)
         mix_grad = lax.psum(mix_part, "seq")
     gate_grad = (jnp.sum(inner, axis=1) * gate * (1.0 - gate)).reshape(selection.shape)
-    token_grad = sum_rows(cap, pieces, own_rows, me, requested, returned)
+    token_grad = sum_rows(cap, pieces, own_rows, direct, me, requested, returned)
     return token_grad, factor_grad[None], mix_grad, gate_grad
 
 

time: 205 us -> 203 us (level)
  waiting for transfers between devices: 72.6 us -> 67.7 us
  Pallas kernels: 44.2 us -> 48.8 us
  starting transfers between devices: 66.1 us -> 62.6 us
    ppermute x45 -> x24, starting transfers between devices: 61.8 us -> 33.5 us  [exchange_far(): lax.ppermute(x, 'exp', [(n, n ^ half + k) for n in range(peers)])]
    all_to_all x0 -> x3, starting transfers between devices: none -> 24.8 us  [exchange_near(): lax.all_to_all(array, 'exp', split_axis=0, concat_axis=0, axis_index_grou...]
    ppermute x45 -> x24, waiting for transfers between devices: 70.8 us -> 54.7 us  [exchange_far(): lax.ppermute(x, 'exp', [(n, n ^ half + k) for n in range(peers)])]
    ppermute x5, waiting for transfers between devices: 1.78 us -> 12.4 us  [across(): return lax.ppermute(array, 'seq', pair)]
    pallas_call x8 -> x10, Pallas kernels: 44.2 us -> 48.8 us  [call(): pl.pallas_call(body, out_shape=[x for x, _ in outs], in_specs=[place for...]
  transfers between devices with their start and end apart: 50 -> 32, of which waited for: 29 -> 16; matrix products, arithmetic and copies ran while one was open for 3% -> 3% of each run, Pallas kernels for 9% -> 13%
where the time goes in v5:
time: 203 us; the launch traced here: 200 us
  waiting for transfers between devices  67.7 us (33%)
  starting transfers between devices  62.6 us (31%)
  Pallas kernels  48.8 us (24%)
  blocking collectives  10.4 us (5%)
  local copies, waits for them, and re-layouts  5.22 us (3%)
  other arithmetic  4.28 us (2%)
    ppermute x24, waiting for transfers between devices, exchange_far(): lax.ppermute(x, 'exp', [(n, n ^ half + k) for n in range(peers)])  54.7 us
    pallas_call x10, Pallas kernels, call(): pl.pallas_call(body, out_shape=[x for x, _ in outs], in_specs=[place for...  48.8 us
    ppermute x24, starting transfers between devices, exchange_far(): lax.ppermute(x, 'exp', [(n, n ^ half + k) for n in range(peers)])  33.5 us
    all_to_all x3, starting transfers between devices, exchange_near(): lax.all_to_all(array, 'exp', split_axis=0, concat_axis=0, axis_index_grou...  24.8 us
    ppermute x5, waiting for transfers between devices, across(): return lax.ppermute(array, 'seq', pair)  12.4 us
    all_to_all x1, blocking collectives, shards(): lax.all_to_all(wanted, 'exp', split_axis=0, concat_axis=0, tiled=True)  10.4 us
    ppermute x5, starting transfers between devices, across(): return lax.ppermute(array, 'seq', pair)  4.34 us
  transfers between devices with their start and end apart: 32, of which 16 were waited for; matrix products, arithmetic and copies ran while one was open for 3% of the time, Pallas kernels for 13%

profile of v5, /device:TPU:13, one launch (start us, length us, event | category | flops | bytes accessed | tf_op | source)
XLA Modules:
  0.0 200.0 jit_solution(9456788631075662691)
XLA Ops:
  2.2 10.4 %all_to_all.26 = s32[16,1,128]{2,1,0:T(1,128)} all-to-all(s32[16,1,128]{2,1,0:T(1,128)} %bitcast.27), channel_id=1, replica_groups=mesh['seq'=2,'exp'=16] {'exp'}, dimensions={0} | all-to-all | bytes 16384 | tf_op jit(solution)/shard_map/all_to_all | solution.py:522
  12.6 3.5 %pick_tokens_far.1 = (bf16[48,1024]{1,0:T(8,128)(2,1)}, bf16[48,1024]{1,0:T(8,128)(2,1)}, bf16[48,1024]{1,0:T(8,128)(2,1)}, bf16[48,1024]{1,0:T(8,128)(2,1)}, bf...) custom-call(s32[1]{0:T(128)} %bitcast.me_ref, ...), custom_call_target="tpu_custom_call" | custom-call | flops 402653184 | bytes 1843204 | tf_op jit(solution)/shard_map/pick_tokens_far/pallas_call | solution.py:40
  16.5 4.7 %collective-permute-done.refs_0_.refs_1_ = bf16[48,1024]{1,0:T(8,128)(2,1)S(1)} collective-permute-done((bf16[48,1024]{1,0:T(8,128)(2,1)}, bf16[48,1024]{1,0:T(8,128)(2,1)S(1)}, u32[]{:S(2)}, u32[]{:S(2)}) %collective-permute-start) | collective-permute-done | bytes 98336 | tf_op jit(solution)/shard_map/ppermute | solution.py:535
  21.8 3.4 %pick_tokens_near.1 = bf16[384,1024]{1,0:T(8,128)(2,1)} custom-call(s32[1]{0:T(128)} %bitcast.me_ref, s32[16,128]{1,0:T(8,128)} %bitcast.23, bf16[128,4096]{1,0:T(8,128)(2,1)} %source_ref.5, bf16[48,1024]{1,0:T(8,128)(2,1)} %copy-done.4), custom_call_target="tpu_custom_call" | custom-call | flops 402653184 | bytes 1941508 | tf_op jit(solution)/shard_map/pick_tokens_near/pallas_call | solution.py:40
  25.2 8.9 %all-to-all-start.1 = ((bf16[8,48,1024]{2,1,0:T(8,128)(2,1)}), bf16[8,48,1024]{2,1,0:T(8,128)(2,1)S(1)}, u32[]{:S(2)}, u32[]{:S(2)}) async-start(bf16[8,48,1024]{2,1,0:T(8,128)(2,1)} %bitcast.20), calls=%async_computation.1 | async-start | bytes 1572864 | tf_op jit(solution)/shard_map/all_to_all | solution.py:528
  35.3 3.9 %collective-permute-done.4.refs_5_.refs_0_ = bf16[48,1024]{1,0:T(8,128)(2,1)S(1)} collective-permute-done((bf16[48,1024]{1,0:T(8,128)(2,1)S(1)}, bf16[48,1024]{1,0:T(8,128)(2,1)S(1)}, u32[]{:S(2)}, u32[]{:S(2)}) %collective-permute-start.4) | collective-permute-done | bytes 98336 | tf_op jit(solution)/shard_map/ppermute | solution.py:535
  39.8 3.4 %pick_cotangent_near.1 = bf16[384,1024]{1,0:T(8,128)(2,1)} custom-call(s32[1]{0:T(128)} %bitcast.me_ref, s32[16,128]{1,0:T(8,128)} %bitcast.24, bf16[128,4096]{1,0:T(8,128)(2,1)} %source_ref.7, bf16[48,1024]{1,0:T(8,128)(2,1)} %copy-done.5), custom_call_target="tpu_custom_call" | custom-call | flops 402653184 | bytes 1941508 | tf_op jit(solution)/shard_map/pick_cotangent_near/pallas_call | solution.py:40
  43.9 11.4 %all-to-all-start.2 = ((bf16[8,48,1024]{2,1,0:T(8,128)(2,1)}), bf16[8,48,1024]{2,1,0:T(8,128)(2,1)}, u32[]{:S(2)}, u32[]{:S(2)}) async-start(bf16[8,48,1024]{2,1,0:T(8,128)(2,1)} %bitcast.19), calls=%async_computation.2 | async-start | bytes 1572864 | tf_op jit(solution)/shard_map/all_to_all | solution.py:528
  57.9 2.7 %collective-permute-start.3 = (bf16[48,1024]{1,0:T(8,128)(2,1)}, bf16[48,1024]{1,0:T(8,128)(2,1)S(1)}, u32[]{:S(2)}, u32[]{:S(2)}) collective-permute-start(bf16[48,1024]{1,0:T(8,128)(2,1)} %get-tuple-element.48), channel_id=1, source_target_pairs={{0,11},{1,10},{2,9},{3,8},{4,15},{5,14},{6,13},{7,12},{8,3},{9,2},... | collective-permute-start | bytes 294920 | tf_op jit(solution)/shard_map/ppermute | solution.py:535
  60.6 8.4 %collective-permute-done.1.refs_0_.refs_2_ = bf16[48,1024]{1,0:T(8,128)(2,1)S(1)} collective-permute-done((bf16[48,1024]{1,0:T(8,128)(2,1)}, bf16[48,1024]{1,0:T(8,128)(2,1)S(1)}, u32[]{:S(2)}, u32[]{:S(2)}) %collective-permute-start.1) | collective-permute-done | bytes 98336 | tf_op jit(solution)/shard_map/ppermute | solution.py:535
  74.1 3.5 %pick_cotangent_far.1 = (bf16[48,1024]{1,0:T(8,128)(2,1)}, bf16[48,1024]{1,0:T(8,128)(2,1)}, bf16[48,1024]{1,0:T(8,128)(2,1)}, bf16[48,1024]{1,0:T(8,128)(2,1)},...) custom-call(s32[1]{0:T(128)} %bitcast.me_ref, ...), custom_call_target="tpu_custom_call" | custom-call | flops 402653184 | bytes 1941508 | tf_op jit(solution)/shard_map/pick_cotangent_far/pallas_call | solution.py:40
  79.9 5.9 %collective-permute-done.6.refs_7_ = bf16[48,1024]{1,0:T(8,128)(2,1)} collective-permute-done((bf16[48,1024]{1,0:T(8,128)(2,1)}, bf16[48,1024]{1,0:T(8,128)(2,1)}, u32[]{:S(2)}, u32[]{:S(2)}) %collective-permute-start.6) | collective-permute-done | bytes 98336 | tf_op jit(solution)/shard_map/ppermute | solution.py:535
  91.1 4.5 %collective-permute-done.10.refs_12_.refs_2_ = bf16[48,1024]{1,0:T(8,128)(2,1)S(1)} collective-permute-done((bf16[48,1024]{1,0:T(8,128)(2,1)}, bf16[48,1024]{1,0:T(8,128)(2,1)S(1)}, u32[]{:S(2)}, u32[]{:S(2)}) %collective-permute-start.10) | collective-permute-done | bytes 98336 | tf_op jit(solution)/shard_map/ppermute | solution.py:535
  99.8 7.3 %forward.1 = (bf16[512,512]{1,0:T(8,128)(2,1)}, bf16[512,512]{1,0:T(8,128)(2,1)}, f32[512,512]{1,0:T(8,128)}, f32[512,512]{1,0:T(8,128)}, f32[128,512]{1,0:T(8,1...) custom-call(s32[1,128]{1,0:T(1,128)} %get-tuple-element.44.slot_ref, f32[192]{0:T(256)} %reshape.55.mix_ref, ...), custom_call_target="tpu_custom_call" | custom-call | flops 1073741824 | bytes 9045256 | tf_op jit(solution)/shard_map/forward/pallas_call | solution.py:40
  113.5 11.9 %collective-permute-done.14.refs_6_ = bf16[48,1024]{1,0:T(8,128)(2,1)S(1)} collective-permute-done((bf16[48,1024]{1,0:T(8,128)(2,1)}, bf16[48,1024]{1,0:T(8,128)(2,1)S(1)}, u32[]{:S(2)}, u32[]{:S(2)}) %collective-permute-start.14) | collective-permute-done | bytes 98336 | tf_op jit(solution)/shard_map/ppermute | solution.py:535
  125.4 2.7 %collective-permute-done.16.refs_8_ = bf16[48,1024]{1,0:T(8,128)(2,1)S(1)} collective-permute-done((bf16[48,1024]{1,0:T(8,128)(2,1)}, bf16[48,1024]{1,0:T(8,128)(2,1)S(1)}, u32[]{:S(2)}, u32[]{:S(2)}) %collective-permute-start.16) | collective-permute-done | bytes 98336 | tf_op jit(solution)/shard_map/ppermute | solution.py:535
  129.0 10.6 %backward.1 = (bf16[384,1024]{1,0:T(8,128)(2,1)}, bf16[48,1024]{1,0:T(8,128)(2,1)}, bf16[48,1024]{1,0:T(8,128)(2,1)}, bf16[48,1024]{1,0:T(8,128)(2,1)}, bf16[48,...) custom-call(s32[1,128]{1,0:T(1,128)} %get-tuple-element.44.slot_ref,, ...), custom_call_target="tpu_custom_call" | custom-call | flops 1610612736 | bytes 10224904 | tf_op jit(solution)/shard_map/backward/pallas_call | solution.py:40
  139.6 4.5 %all-to-all-start.3 = ((bf16[8,48,1024]{2,1,0:T(8,128)(2,1)}), bf16[8,48,1024]{2,1,0:T(8,128)(2,1)}, u32[]{:S(2)}, u32[]{:S(2)}) async-start(bf16[8,48,1024]{2,1,0:T(8,128)(2,1)} %bitcast.21), calls=%async_computation.3 | async-start | bytes 1572864 | tf_op jit(solution)/shard_map/all_to_all | solution.py:528
  145.6 3.9 %mix_partials.1 = f32[192,128]{1,0:T(8,128)} custom-call(f32[512,512]{1,0:T(8,128)} %get-tuple-element.78.yg_hbm, f32[512,512]{1,0:T(8,128)} %get-tuple-element.79.yu_hbm, f32[512,512]{1,0:T(8,128)} %get-tuple-element.80.yd_hbm, bf16[3,128,512]{2,1,0:T(8,128)(2,1)} %get-tuple-element.76.refs_2_.d_hbm), custom_call_target="tpu_custom_call" | custom-call | flops 6291456 | bytes 3637248 | tf_op jit(solution)/shard_map/mix_partials/pallas_call | solution.py:40
  154.7 12.4 %collective-permute-done.28 = f32[1,3,4,4,4]{4,3,2,1,0:T(4,128)S(1)} collective-permute-done((f32[1,3,4,4,4]{4,3,2,1,0:T(4,128)S(1)}, f32[1,3,4,4,4]{4,3,2,1,0:T(4,128)S(1)}, u32[]{:S(2)}, u32[]{:S(2)}) %collective-permute-start.28) | collective-permute-done | bytes 800 | tf_op jit(solution)/shard_map/ppermute | solution.py:497
  175.6 6.7 %collective-permute-start.24 = (bf16[48,1024]{1,0:T(8,128)(2,1)}, bf16[48,1024]{1,0:T(8,128)(2,1)S(1)}, u32[]{:S(2)}, u32[]{:S(2)}) collective-permute-start(bf16[48,1024]{1,0:T(8,128)(2,1)} %get-tuple-element.72), channel_id=1, source_target_pairs={{0,14},{1,15},{2,12},{3,13},{4,10},{5,11},{6,8},{7,9},{8,6},{9,7},... | collective-permute-start | bytes 294920 | tf_op jit(solution)/shard_map/ppermute | solution.py:535
  183.1 7.8 %factor_grad.1 = f32[3,4,512,128]{3,2,1,0:T(8,128)} custom-call(f32[192]{0:T(256)} %reshape.55.mix_ref, bf16[512,512]{1,0:T(8,128)(2,1)} %get-tuple-element.74.refs_0_, bf16[512,512]{1,0:T(8,128)(2,1)} %get-tuple-element.75.refs_1_, bf16[3,128,512]{2,1,0:T(8,128)(2,1)} %get-tuple-element.76.refs_2_.d_hbm, bf16[512,512]{1,0:T(8,128)(2,1)} %copy-done.1, ...), custom_call_target="tpu_custom_call" | custom-call | flops 1610612736 | bytes 6030080 | tf_op jit(solution)/shard_map/factor_grad/pallas_call | solution.py:40
  191.5 2.8 %collective-permute-done.24.refs_7_ = bf16[48,1024]{1,0:T(8,128)(2,1)S(1)} collective-permute-done((bf16[48,1024]{1,0:T(8,128)(2,1)}, bf16[48,1024]{1,0:T(8,128)(2,1)S(1)}, u32[]{:S(2)}, u32[]{:S(2)}) %collective-permute-start.24) | collective-permute-done | bytes 98336 | tf_op jit(solution)/shard_map/ppermute | solution.py:535
  196.0 3.9 %sum_rows.1 = bf16[128,4096]{1,0:T(8,128)(2,1)} custom-call(s32[1]{0:T(128)} %bitcast.me_ref, s32[16,128]{1,0:T(8,128)} %bitcast.26, bf16[384,1024]{1,0:T(8,128)(2,1)} %bitcast.14.refs_0_, bf16[48,1024]{1,0:T(8,128)(2,1)} %copy-done.15, bf16[48,1024]{1,0:T(8,128)(2,1)} %copy-done.16, bf16[48,1024]{1,0:T(8,128)(2,1)} %copy-done.17, ...), custom_call_target="tpu_custom_call" | custom-call | flops 805306368 | bytes 2629636 | tf_op jit(solution)/shard_map/sum_rows/pallas_call | solution.py:40
  (104 shorter events, 50.1 us)
Async XLA Ops:
  25.2 18.6 %all-to-all-start.1 = ((bf16[8,48,1024]{2,1,0:T(8,128)(2,1)}), bf16[8,48,1024]{2,1,0:T(8,128)(2,1)S(1)}, u32[]{:S(2)}, u32[]{:S(2)}) async-start(bf16[8,48,1024]{2,1,0:T(8,128)(2,1)} %bitcast.20), calls=%async_computation.1 | async-start | bytes 1572864 | tf_op jit(solution)/shard_map/all_to_all | solution.py:528
  34.1 65.7 %collective-permute-start.8 = (bf16[1,3,4,512,128]{4,3,2,1,0:T(8,128)(2,1)}, bf16[1,3,4,512,128]{4,3,2,1,0:T(8,128)(2,1)}, u32[]{:S(2)}, u32[]{:S(2)}) collective-permute-start(bf16[1,3,4,512,128]{4,3,2,1,0:T(8,128)(2,1)} %param.8), channel_id=1, source_target_pairs={{0,16},{16,0},{1,17},{17,1},{2,18},{18,2},{3,19},{19,3},{4,20},{20... | collective-permute-start | bytes 4718600 | tf_op jit(solution)/shard_map/ppermute | solution.py:497
  43.9 84.2 %all-to-all-start.2 = ((bf16[8,48,1024]{2,1,0:T(8,128)(2,1)}), bf16[8,48,1024]{2,1,0:T(8,128)(2,1)}, u32[]{:S(2)}, u32[]{:S(2)}) async-start(bf16[8,48,1024]{2,1,0:T(8,128)(2,1)} %bitcast.19), calls=%async_computation.2 | async-start | bytes 1572864 | tf_op jit(solution)/shard_map/all_to_all | solution.py:528
  55.3 13.8 %collective-permute-start.1 = (bf16[48,1024]{1,0:T(8,128)(2,1)}, bf16[48,1024]{1,0:T(8,128)(2,1)S(1)}, u32[]{:S(2)}, u32[]{:S(2)}) collective-permute-start(bf16[48,1024]{1,0:T(8,128)(2,1)} %get-tuple-element.46), channel_id=1, source_target_pairs={{0,9},{1,8},{2,11},{3,10},{4,13},{5,12},{6,15},{7,14},{8,1},{9,0},... | collective-permute-start | bytes 294920 | tf_op jit(solution)/shard_map/ppermute | solution.py:535
  57.0 13.5 %collective-permute-start.2 = (bf16[48,1024]{1,0:T(8,128)(2,1)}, bf16[48,1024]{1,0:T(8,128)(2,1)}, u32[]{:S(2)}, u32[]{:S(2)}) collective-permute-start(bf16[48,1024]{1,0:T(8,128)(2,1)} %get-tuple-element.47), channel_id=1, source_target_pairs={{0,10},{1,11},{2,8},{3,9},{4,14},{5,15},{6,12},{7,13},{8,2},{9,3},... | collective-permute-start | bytes 294920 | tf_op jit(solution)/shard_map/ppermute | solution.py:535
  57.9 19.7 %collective-permute-start.3 = (bf16[48,1024]{1,0:T(8,128)(2,1)}, bf16[48,1024]{1,0:T(8,128)(2,1)S(1)}, u32[]{:S(2)}, u32[]{:S(2)}) collective-permute-start(bf16[48,1024]{1,0:T(8,128)(2,1)} %get-tuple-element.48), channel_id=1, source_target_pairs={{0,11},{1,10},{2,9},{3,8},{4,15},{5,14},{6,13},{7,12},{8,3},{9,2},... | collective-permute-start | bytes 294920 | tf_op jit(solution)/shard_map/ppermute | solution.py:535
  60.6 19.3 %collective-permute-start.5 = (bf16[48,1024]{1,0:T(8,128)(2,1)}, bf16[48,1024]{1,0:T(8,128)(2,1)}, u32[]{:S(2)}, u32[]{:S(2)}) collective-permute-start(bf16[48,1024]{1,0:T(8,128)(2,1)} %get-tuple-element.50), channel_id=1, source_target_pairs={{0,13},{1,12},{2,15},{3,14},{4,9},{5,8},{6,11},{7,10},{8,5},{9,4},... | collective-permute-start | bytes 294920 | tf_op jit(solution)/shard_map/ppermute | solution.py:535
  69.0 16.8 %collective-permute-start.6 = (bf16[48,1024]{1,0:T(8,128)(2,1)}, bf16[48,1024]{1,0:T(8,128)(2,1)}, u32[]{:S(2)}, u32[]{:S(2)}) collective-permute-start(bf16[48,1024]{1,0:T(8,128)(2,1)} %get-tuple-element.51), channel_id=1, source_target_pairs={{0,14},{1,15},{2,12},{3,13},{4,10},{5,11},{6,8},{7,9},{8,6},{9,7},... | collective-permute-start | bytes 294920 | tf_op jit(solution)/shard_map/ppermute | solution.py:535
  70.5 17.9 %collective-permute-start.7 = (bf16[48,1024]{1,0:T(8,128)(2,1)}, bf16[48,1024]{1,0:T(8,128)(2,1)}, u32[]{:S(2)}, u32[]{:S(2)}) collective-permute-start(bf16[48,1024]{1,0:T(8,128)(2,1)} %get-tuple-element.52), channel_id=1, source_target_pairs={{0,15},{1,14},{2,13},{3,12},{4,11},{5,10},{6,9},{7,8},{8,7},{9,6},... | collective-permute-start | bytes 294920 | tf_op jit(solution)/shard_map/ppermute | solution.py:535
  79.9 15.7 %collective-permute-start.10 = (bf16[48,1024]{1,0:T(8,128)(2,1)}, bf16[48,1024]{1,0:T(8,128)(2,1)S(1)}, u32[]{:S(2)}, u32[]{:S(2)}) collective-permute-start(bf16[48,1024]{1,0:T(8,128)(2,1)} %get-tuple-element.54), channel_id=1, source_target_pairs={{0,9},{1,8},{2,11},{3,10},{4,13},{5,12},{6,15},{7,14},{8,1},{9,0},... | collective-permute-start | bytes 294920 | tf_op jit(solution)/shard_map/ppermute | solution.py:535
  107.1 21.0 %collective-permute-start.17 = (bf16[512,512]{1,0:T(8,128)(2,1)}, bf16[512,512]{1,0:T(8,128)(2,1)S(1)}, u32[]{:S(2)}, u32[]{:S(2)}) collective-permute-start(bf16[512,512]{1,0:T(8,128)(2,1)} %get-tuple-element.64), channel_id=1, source_target_pairs={{0,16},{16,0},{1,17},{17,1},{2,18},{18,2},{3,19},{19,3},{4,20},{20... | collective-permute-start | bytes 1572872 | tf_op jit(solution)/shard_map/ppermute | solution.py:497
  108.4 17.0 %collective-permute-start.14 = (bf16[48,1024]{1,0:T(8,128)(2,1)}, bf16[48,1024]{1,0:T(8,128)(2,1)S(1)}, u32[]{:S(2)}, u32[]{:S(2)}) collective-permute-start(bf16[48,1024]{1,0:T(8,128)(2,1)} %get-tuple-element.61), channel_id=1, source_target_pairs={{0,13},{1,12},{2,15},{3,14},{4,9},{5,8},{6,11},{7,10},{8,5},{9,4},... | collective-permute-start | bytes 294920 | tf_op jit(solution)/shard_map/ppermute | solution.py:535
  110.9 14.4 %collective-permute-start.15 = (bf16[48,1024]{1,0:T(8,128)(2,1)}, bf16[48,1024]{1,0:T(8,128)(2,1)S(1)}, u32[]{:S(2)}, u32[]{:S(2)}) collective-permute-start(bf16[48,1024]{1,0:T(8,128)(2,1)} %get-tuple-element.62), channel_id=1, source_target_pairs={{0,14},{1,15},{2,12},{3,13},{4,10},{5,11},{6,8},{7,9},{8,6},{9,7},... | collective-permute-start | bytes 294920 | tf_op jit(solution)/shard_map/ppermute | solution.py:535
  111.1 17.0 %collective-permute-start.16 = (bf16[48,1024]{1,0:T(8,128)(2,1)}, bf16[48,1024]{1,0:T(8,128)(2,1)S(1)}, u32[]{:S(2)}, u32[]{:S(2)}) collective-permute-start(bf16[48,1024]{1,0:T(8,128)(2,1)} %get-tuple-element.63), channel_id=1, source_target_pairs={{0,15},{1,14},{2,13},{3,12},{4,11},{5,10},{6,9},{7,8},{8,7},{9,6},... | collective-permute-start | bytes 294920 | tf_op jit(solution)/shard_map/ppermute | solution.py:535
  139.6 55.8 %all-to-all-start.3 = ((bf16[8,48,1024]{2,1,0:T(8,128)(2,1)}), bf16[8,48,1024]{2,1,0:T(8,128)(2,1)}, u32[]{:S(2)}, u32[]{:S(2)}) async-start(bf16[8,48,1024]{2,1,0:T(8,128)(2,1)} %bitcast.21), calls=%async_computation.3 | async-start | bytes 1572864 | tf_op jit(solution)/shard_map/all_to_all | solution.py:528
  144.1 38.3 %collective-permute-start.26 = (bf16[512,512]{1,0:T(8,128)(2,1)}, bf16[512,512]{1,0:T(8,128)(2,1)S(1)}, u32[]{:S(2)}, u32[]{:S(2)}) collective-permute-start(bf16[512,512]{1,0:T(8,128)(2,1)} %get-tuple-element.77), channel_id=1, source_target_pairs={{0,16},{16,0},{1,17},{17,1},{2,18},{18,2},{3,19},{19,3},{4,20},{20... | collective-permute-start | bytes 1572872 | tf_op jit(solution)/shard_map/ppermute | solution.py:497
  144.4 31.3 %collective-permute-start.27 = (bf16[3,128,512]{2,1,0:T(8,128)(2,1)S(1)}, bf16[3,128,512]{2,1,0:T(8,128)(2,1)}, u32[]{:S(2)}, u32[]{:S(2)}) collective-permute-start(bf16[3,128,512]{2,1,0:T(8,128)(2,1)S(1)} %copy-done.2), channel_id=1, source_target_pairs={{0,16},{16,0},{1,17},{17,1},{2,18},{18,2},{3,19},{19,3},{4,20},{20... | collective-permute-start | bytes 1179656 | tf_op jit(solution)/shard_map/ppermute | solution.py:497
  150.6 16.5 %collective-permute-start.28 = (f32[1,3,4,4,4]{4,3,2,1,0:T(4,128)S(1)}, f32[1,3,4,4,4]{4,3,2,1,0:T(4,128)S(1)}, u32[]{:S(2)}, u32[]{:S(2)}) collective-permute-start(f32[1,3,4,4,4]{4,3,2,1,0:T(4,128)S(1)} %reshape.62), channel_id=1, source_target_pairs={{0,16},{16,0},{1,17},{17,1},{2,18},{18,2},{3,19},{19,3},{4,20},{20... | collective-permute-start | bytes 2312 | tf_op jit(solution)/shard_map/ppermute | solution.py:497
  151.1 19.7 %collective-permute-start.18 = (bf16[48,1024]{1,0:T(8,128)(2,1)}, bf16[48,1024]{1,0:T(8,128)(2,1)S(1)}, u32[]{:S(2)}, u32[]{:S(2)}) collective-permute-start(bf16[48,1024]{1,0:T(8,128)(2,1)} %get-tuple-element.66), channel_id=1, source_target_pairs={{0,8},{1,9},{2,10},{3,11},{4,12},{5,13},{6,14},{7,15},{8,0},{9,1},... | collective-permute-start | bytes 294920 | tf_op jit(solution)/shard_map/ppermute | solution.py:535
  153.6 19.4 %collective-permute-start.19 = (bf16[48,1024]{1,0:T(8,128)(2,1)}, bf16[48,1024]{1,0:T(8,128)(2,1)S(1)}, u32[]{:S(2)}, u32[]{:S(2)}) collective-permute-start(bf16[48,1024]{1,0:T(8,128)(2,1)} %get-tuple-element.67), channel_id=1, source_target_pairs={{0,9},{1,8},{2,11},{3,10},{4,13},{5,12},{6,15},{7,14},{8,1},{9,0},... | collective-permute-start | bytes 294920 | tf_op jit(solution)/shard_map/ppermute | solution.py:535
  170.8 20.1 %collective-permute-start.21 = (bf16[48,1024]{1,0:T(8,128)(2,1)}, bf16[48,1024]{1,0:T(8,128)(2,1)}, u32[]{:S(2)}, u32[]{:S(2)}) collective-permute-start(bf16[48,1024]{1,0:T(8,128)(2,1)} %get-tuple-element.69), channel_id=1, source_target_pairs={{0,11},{1,10},{2,9},{3,8},{4,15},{5,14},{6,13},{7,12},{8,3},{9,2},... | collective-permute-start | bytes 294920 | tf_op jit(solution)/shard_map/ppermute | solution.py:535
  172.9 18.0 %collective-permute-start.22 = (bf16[48,1024]{1,0:T(8,128)(2,1)}, bf16[48,1024]{1,0:T(8,128)(2,1)}, u32[]{:S(2)}, u32[]{:S(2)}) collective-permute-start(bf16[48,1024]{1,0:T(8,128)(2,1)} %get-tuple-element.70), channel_id=1, source_target_pairs={{0,12},{1,13},{2,14},{3,15},{4,8},{5,9},{6,10},{7,11},{8,4},{9,5},... | collective-permute-start | bytes 294920 | tf_op jit(solution)/shard_map/ppermute | solution.py:535
  174.4 17.1 %collective-permute-start.23 = (bf16[48,1024]{1,0:T(8,128)(2,1)}, bf16[48,1024]{1,0:T(8,128)(2,1)}, u32[]{:S(2)}, u32[]{:S(2)}) collective-permute-start(bf16[48,1024]{1,0:T(8,128)(2,1)} %get-tuple-element.71), channel_id=1, source_target_pairs={{0,13},{1,12},{2,15},{3,14},{4,9},{5,8},{6,11},{7,10},{8,5},{9,4},... | collective-permute-start | bytes 294920 | tf_op jit(solution)/shard_map/ppermute | solution.py:535
  175.6 18.7 %collective-permute-start.24 = (bf16[48,1024]{1,0:T(8,128)(2,1)}, bf16[48,1024]{1,0:T(8,128)(2,1)S(1)}, u32[]{:S(2)}, u32[]{:S(2)}) collective-permute-start(bf16[48,1024]{1,0:T(8,128)(2,1)} %get-tuple-element.72), channel_id=1, source_target_pairs={{0,14},{1,15},{2,12},{3,13},{4,10},{5,11},{6,8},{7,9},{8,6},{9,7},... | collective-permute-start | bytes 294920 | tf_op jit(solution)/shard_map/ppermute | solution.py:535
  (29 other events, 233.6 us)

commit v6 on v2

--- a/solution.py
+++ b/solution.py
@@ -9,7 +9,7 @@
 
 SELECTED = 64
 NPHM = 4
-VMEM_LIMIT = 32 * 1024 * 1024
+VMEM_LIMIT = 63 * 1024 * 1024
 F32 = jnp.float32
 BF16 = jnp.bfloat16
 
@@ -68,97 +68,119 @@
     return [slice(c * chunk, (c + 1) * chunk) for c in range(part // chunk)]
 
 
-def index_body(cap, pieces, own_rows, block_len, chosen_ref, wanted_ref, slot_ref):
-    peers, lanes = wanted_ref.shape
+def start_all(pairs, sems):
+    return [begin(source, target, sems.at[n]) for n, (source, target) in enumerate(pairs)]
+
+
+def spread_columns(places, source, half, direct, name):
+    own_rows, width = source.shape
+    part = width // half
+
+    def body(places_ref, source_ref, *refs):
+        outs, sems = refs[:-1], refs[-1]
+        copies = []
+        for k in range(half):
+            share = places_ref[1] ^ k if direct else k
+            at = source_ref.at[:, pl.ds(pl.multiple_of(share * part, part), part)]
+            out = outs[k] if direct else outs[0].at[k * own_rows : (k + 1) * own_rows]
+            copies.append(begin(at, out, sems.at[k]))
+        wait_all(copies)
+
+    if direct:
+        outs = [(shaped((own_rows, part), BF16), HBM)] * half
+    else:
+        outs = [(shaped((half * own_rows, part), BF16), HBM)]
+    ins = [(places, SMEM), (source, HBM)]
+    return call(body, outs, ins, name, 0, [pltpu.SemaphoreType.DMA((half,))])
+
+
+def pick_rows(places, chosen, shares, own_rows, name):
+    peers, _, picks = chosen.shape
+    part = shares[0].shape[1]
+    block = sum(x.shape[0] for x in shares)
+    batch = min(peers, 16)
+
+    def body(places_ref, chosen_ref, *refs):
+        parts, (out_ref, rows_ref, pick_ref, sent_ref, in_sem, out_sem) = (
+            refs[: len(shares)],
+            refs[len(shares) :],
+        )
+        loads = []
+        for k, share in enumerate(parts):
+            size = share.shape[0]
+            start = pl.multiple_of((places_ref[1] ^ k) * size if len(parts) > 1 else 0, 16)
+            loads.append(begin(share, rows_ref.at[pl.ds(start, size)], in_sem.at[k]))
+        stores = []
+        for first in range(0, peers, batch):
+            for e in range(batch):
+                wanted = chosen_ref[first + e, pl.ds(places_ref[2], 1), :]
+                same = iota((picks, picks), 0) == iota((picks, picks), 1)
+                column = jnp.sum(jnp.where(same, wanted, 0), axis=1, keepdims=True)
+                pick_ref[e * picks : (e + 1) * picks] = (
+                    column == iota((picks, block), 1)
+                ).astype(BF16)
+            if first == 0:
+                wait_all(loads)
+            at = slice(first * picks, (first + batch) * picks)
+            sent_ref[at] = dot(pick_ref[...], rows_ref[...]).astype(BF16)
+            stores.append(begin(sent_ref.at[at], out_ref.at[at], out_sem.at[first // batch]))
+        wait_all(stores)
+
+    return call(
+        body,
+        [(shaped((peers * picks, part), BF16), HBM)],
+        [(places, SMEM), (chosen, VMEM)] + [(x, HBM) for x in shares],
+        name,
+        2 * peers * picks * block * part,
+        [
+            scratch_like((block, part), BF16),
+            scratch_like((batch * picks, block), BF16),
+            scratch_like((peers * picks, part), BF16),
+            pltpu.SemaphoreType.DMA((len(shares),)),
+            pltpu.SemaphoreType.DMA((peers // batch,)),
+        ],
+    )[0]
+
+
+def slot_body(cap, pieces, own_rows, block_len, chosen_ref, slot_ref):
     rows = slot_ref.shape[1]
     position = jnp.concatenate(
         [chosen_ref[b : b + 1, :] + b * block_len for b in range(chosen_ref.shape[0])], axis=1
     )
     owner = lax.shift_right_logical(position, own_rows.bit_length() - 1)
-    local = position & (own_rows - 1)
+    peers = chosen_ref.shape[0] * block_len // own_rows
     peer = iota((peers, rows), 0)
-    mine = (peer == owner).astype(F32)
-    count = jnp.sum(mine, axis=1, keepdims=True)
+    count = jnp.sum((peer == owner).astype(F32), axis=1, keepdims=True)
     earlier = jnp.sum(jnp.where(peer < owner, count, 0.0), axis=0, keepdims=True).astype(jnp.int32)
-    rank = iota((1, rows), 1) - earlier
-    slot_ref[...] = owner * (cap * pieces) + rank
-    lane = iota((lanes, rows), 0)
-    hit = jnp.zeros((lanes, rows), F32)
-    for j in range(pieces):
-        hit = hit + (lane == rank + j * cap).astype(F32)
-    marked = mine * (local + 1).astype(F32)
-    wanted_ref[...] = dot_nt(marked.astype(BF16), hit.astype(BF16)).astype(jnp.int32)
-
-
-def pick_matrix(cap, pieces, own_rows, requested):
-    peers, lanes = requested.shape
+    slot_ref[...] = owner * (cap * pieces) + iota((1, rows), 1) - earlier
+
+
+def sum_rows(cap, pieces, own_rows, places, chosen, returned):
+    slots, part = returned.shape
+    peers, _, picks = chosen.shape
     group = cap * pieces
-    slots = peers * group
-    peer = iota((peers, group, peers), 0).reshape(slots, peers)
-    spread = dot(
-        (peer == iota((slots, peers), 1)).astype(BF16), requested.astype(F32).astype(BF16)
-    )
-    place = iota((peers, group, lanes), 1).reshape(slots, lanes)
-    row = jnp.sum(
-        jnp.where(place == iota((slots, lanes), 1), spread, 0.0), axis=1, keepdims=True
-    ).astype(jnp.int32)
-    piece = iota((peers, group, 1), 1).reshape(slots, 1)
-    shift = jnp.zeros((slots, 1), jnp.int32)
-    for j in range(1, pieces):
-        shift = shift + jnp.where(piece >= j * cap, own_rows, 0)
-    target = jnp.where(row > 0, row - 1 + shift, -1)
-    return (target == iota((slots, pieces * own_rows), 1)).astype(BF16)
-
-
-def pick_rows(cap, pieces, requested, source, after, name):
-    own_rows, width = source.shape
-    part = width // pieces
-    slots = requested.shape[0] * cap * pieces
     columns = chunks_of(part)
 
-    def body(requested_ref, source_ref, *refs):
-        out_ref, rows_ref, sent_ref, in_sem, out_sem = refs[len(after) :]
-        loads = []
-        for n, at in enumerate(columns):
-            for j in range(pieces):
-                wide = slice(j * part + at.start, j * part + at.stop)
-                target = rows_ref.at[j * own_rows : (j + 1) * own_rows, at]
-                loads.append(begin(source_ref.at[:, wide], target, in_sem.at[n, j]))
-        pick = pick_matrix(cap, pieces, own_rows, requested_ref[...])
-        stores = []
-        for n, at in enumerate(columns):
-            for load in loads[n * pieces : (n + 1) * pieces]:
-                load.wait()
-            sent_ref[:, at] = dot(pick, rows_ref[:, at]).astype(BF16)
-            stores.append(begin(sent_ref.at[:, at], out_ref.at[:, at], out_sem.at[n]))
-        for store in stores:
-            store.wait()
-
-    return call(
-        body,
-        [(shaped((slots, part), BF16), HBM)],
-        [(requested, VMEM), (source, HBM)] + [(x, HBM) for x in after],
-        name,
-        2 * slots * pieces * own_rows * part,
-        [
-            scratch_like((pieces * own_rows, part), BF16),
-            scratch_like((slots, part), BF16),
-            pltpu.SemaphoreType.DMA((len(columns), pieces)),
-            pltpu.SemaphoreType.DMA((len(columns),)),
-        ],
-    )[0]
-
-
-def sum_rows(cap, pieces, own_rows, requested, returned):
-    slots, part = returned.shape
-    columns = chunks_of(part)
-
-    def body(requested_ref, returned_ref, out_ref, got_ref, sum_ref, in_sem, out_sem):
+    def body(places_ref, chosen_ref, returned_ref, out_ref, got_ref, pick_ref, sum_ref, in_sem, out_sem):
         loads = [
             begin(returned_ref.at[:, at], got_ref.at[:, at], in_sem.at[n])
             for n, at in enumerate(columns)
         ]
-        pick = pick_matrix(cap, pieces, own_rows, requested_ref[...])
+        for e in range(peers):
+            local = chosen_ref[e, pl.ds(places_ref[2], 1), :] - places_ref[1] * own_rows
+            before = jnp.sum((local < 0).astype(F32), axis=1, keepdims=True).astype(jnp.int32)
+            rank = iota((1, picks), 1) - before
+            mine = jnp.where((local >= 0) & (local < own_rows), local + 1, 0)
+            place = iota((group, picks), 0)
+            column = jnp.zeros((group, 1), jnp.int32)
+            for j in range(pieces):
+                hit = jnp.where((place == rank + j * cap) & (rank >= 0) & (rank < cap), mine, 0)
+                row = jnp.sum(hit, axis=1, keepdims=True)
+                column = column + jnp.where(row > 0, row + j * own_rows, 0)
+            pick_ref[e * group : (e + 1) * group] = (
+                column == iota((group, pieces * own_rows), 1) + 1
+            ).astype(F32)
+        pick = pick_ref[...].astype(BF16)
         stores = []
         for n, at in enumerate(columns):
             loads[n].wait()
@@ -169,17 +191,17 @@
                 stores.append(
                     begin(sum_ref.at[:, wide], out_ref.at[:, wide], out_sem.at[n, j])
                 )
-        for store in stores:
-            store.wait()
+        wait_all(stores)
 
     return call(
         body,
         [(shaped((own_rows, part * pieces), BF16), HBM)],
-        [(requested, VMEM), (returned, HBM)],
+        [(places, SMEM), (chosen, VMEM), (returned, HBM)],
         "sum_rows",
         2 * slots * pieces * own_rows * part,
         [
             scratch_like((slots, part), BF16),
+            scratch_like((slots, pieces * own_rows), F32),
             scratch_like((own_rows, part * pieces), BF16),
             pltpu.SemaphoreType.DMA((len(columns),)),
             pltpu.SemaphoreType.DMA((len(columns), pieces)),
@@ -189,12 +211,12 @@
 
 def load_factor(order_ref, parts, m, target, sems):
     copies = []
-    for n, part in enumerate(parts):
-        _, count, rows, cols = part.shape
-        start = pl.multiple_of(order_ref[n] * rows, rows)
+    for n, side in enumerate(parts):
+        _, count, rows, cols = side.shape
+        start = pl.multiple_of(order_ref[3 + n] * rows, rows)
         for i in range(count):
             at = target.at[pl.ds(start, rows), i * cols : (i + 1) * cols]
-            copies.append(begin(part.at[m, i], at, sems.at[n, i]))
+            copies.append(begin(side.at[m, i], at, sems.at[n, i]))
     return copies
 
 
@@ -208,32 +230,26 @@
     return (iota((slots, wide.shape[1]), 0) == wide).astype(BF16)
 
 
-def load_rows(got_hbm, got_ref, sems):
-    return [
-        begin(got_hbm.at[:, at], got_ref.at[:, at], sems.at[n])
-        for n, at in enumerate(chunks_of(got_ref.shape[1]))
-    ]
-
-
-def stack_rows(pieces, place, loads, got_ref, out_ref):
-    part = got_ref.shape[1]
-    rows, depth = out_ref.shape[0] // NPHM, out_ref.shape[1]
-    for load, at in zip(loads, chunks_of(part)):
-        load.wait()
-        block = dot_tn(place, got_ref[:, at]).astype(BF16)
-        for j in range(pieces):
-            column = j * part + at.start
-            a, start = column // depth, column % depth
-            out_ref[a * rows : (a + 1) * rows, start : start + at.stop - at.start] = block[
-                j * rows : (j + 1) * rows
-            ]
+def load_rows(got_hbm, x_ref, sems):
+    rows, depth = x_ref.shape[0] // NPHM, x_ref.shape[1]
+    part = got_hbm.shape[1]
+    shares = NPHM * depth // part
+    picks = got_hbm.shape[0] * part // (NPHM * depth) // (rows // SELECTED)
+    copies = []
+    for n in range(got_hbm.shape[0] // picks):
+        block, share = divmod(n, shares)
+        a, start = share * part // depth, share * part % depth
+        first = a * rows + block * picks
+        at = x_ref.at[first : first + picks, start : start + part]
+        copies.append(begin(got_hbm.at[n * picks : (n + 1) * picks], at, sems.at[n]))
+    return copies
 
 
 def store_parts(order_ref, source_ref, outs, sems):
     copies = []
     for n, out in enumerate(outs):
         size = out.shape[1]
-        start = pl.multiple_of(order_ref[n] * size, size)
+        start = pl.multiple_of(order_ref[3 + n] * size, size)
         copies.append(begin(source_ref.at[:, pl.ds(start, size)], out, sems.at[n]))
     return copies
 
@@ -280,19 +296,18 @@
 
 
 def forward_body(
-    cap, pieces, sides, slot_ref, mix_ref, order_ref, got_hbm, *refs
+    sides, order_ref, mix_ref, got_hbm, *refs
 ):
     parts, refs = refs[:sides], refs[sides:]
     x_outs, refs = refs[:sides], refs[sides:]
     yg_hbm, yu_hbm, act_hbm, slope_hbm, hid_hbm = refs[:5]
-    got_ref, side_ref, x_ref, yg_ref, yu_ref, pre_ref, act_ref, slope_ref, hid_ref = refs[5:14]
-    got_sem, side_sem, out_sem = refs[14:]
-    loads = load_rows(got_hbm, got_ref, got_sem)
+    side_ref, x_ref, yg_ref, yu_ref, pre_ref, act_ref, slope_ref, hid_ref = refs[5:13]
+    got_sem, side_sem, out_sem = refs[13:]
+    loads = load_rows(got_hbm, x_ref, got_sem)
     sides_in = [
         load_factor(order_ref, parts, m, side_ref.at[m], side_sem.at[m]) for m in range(2)
     ]
-    place = place_matrix(cap, pieces, got_ref.shape[0], slot_ref[...])
-    stack_rows(pieces, place, loads, got_ref, x_ref)
+    wait_all(loads)
     stores = store_parts(order_ref, x_ref, x_outs, out_sem)
     wait_all(sides_in[0])
     yg_ref[...] = dot(x_ref[...], side_ref[0])
@@ -325,17 +340,17 @@
 
 
 def backward_body(
-    cap, pieces, sides, after, slot_ref, mix_ref, order_ref, gate_ref, got_hbm, act_hbm, slope_hbm, hid_hbm,
+    cap, pieces, sides, after, order_ref, mix_ref, slot_ref, gate_ref, got_hbm, act_hbm, slope_hbm, hid_hbm,
     *refs,
 ):
     parts, refs = refs[:sides], refs[sides + after :]
     back_hbm, x_outs, refs = refs[0], refs[1 : 1 + sides], refs[1 + sides :]
     y_hbm, d_hbm, inner_ref = refs[:3]
     (
-        got_ref, side_ref, x_ref, y_ref, d_ref, act_ref, slope_ref, hid_ref, zg_ref, zu_ref, grad_ref,
+        side_ref, x_ref, y_ref, d_ref, act_ref, slope_ref, hid_ref, zg_ref, zu_ref, grad_ref,
         back_ref, got_sem, side_sem, in_sem, out_sem,
     ) = refs[3:]
-    loads = load_rows(got_hbm, got_ref, got_sem)
+    loads = load_rows(got_hbm, x_ref, got_sem)
     down_in = load_factor(order_ref, parts, 2, side_ref.at[2], side_sem.at[2])
     flat_in = [
         begin(source, target, in_sem.at[n])
@@ -346,8 +361,7 @@
     sides_in = [
         load_factor(order_ref, parts, m, side_ref.at[m], side_sem.at[m]) for m in range(2)
     ]
-    place = place_matrix(cap, pieces, got_ref.shape[0], slot_ref[...])
-    stack_rows(pieces, place, loads, got_ref, x_ref)
+    wait_all(loads)
     stores = store_parts(order_ref, x_ref, x_outs, out_sem)
     wait_all(down_in)
     y_ref[...] = dot(x_ref[...], side_ref[2])
@@ -376,6 +390,7 @@
     wait_all(sides_in[1])
     grad = dot_nt(zg_ref[...], side_ref[0]) + dot_nt(zu_ref[...], side_ref[1])
     grad_ref[...] = grad.astype(BF16)
+    place = place_matrix(cap, pieces, back_ref.shape[0], slot_ref[...])
     part = back_ref.shape[1]
     rows, depth = x_ref.shape[0] // NPHM, x_ref.shape[1]
     for n, at in enumerate(chunks_of(part)):
@@ -440,7 +455,6 @@
     pieces = 1
     while (cap * pieces) % 8:
         pieces *= 2
-    lanes = 128
     slots = peers * cap * pieces
     part = width // pieces
     steps = len(chunks_of(part))
@@ -457,31 +471,48 @@
 
     if swap:
         factor_parts = [factors[0], across(factors)[0]]
-        order = jnp.stack([group, 1 - group]).astype(jnp.int32)
     else:
         factor_parts = [lax.all_gather(factors, "seq", axis=3, tiled=True)[0]]
-        order = jnp.zeros((2,), jnp.int32)
     sides = len(factor_parts)
     sides_in = [(x, HBM) for x in factor_parts]
 
-    wanted, slot = call(
-        functools.partial(index_body, cap, pieces, own_rows, block_len),
-        [(shaped((peers, lanes), jnp.int32), VMEM), (shaped((1, rows), jnp.int32), VMEM)],
+    half = peers // selection.shape[1]
+    direct = half == 8
+    me = lax.axis_index("exp")
+    first = group if swap else 0
+    places = jnp.stack([me, me % half, me // half, first, 1 - first]).astype(jnp.int32)
+    chosen = lax.all_gather(selection[0], "exp")
+    halves = [list(range(h, h + half)) for h in range(0, peers, half)]
+
+    def to_peers(array):
+        array = array.reshape(peers, -1, array.shape[1])
+        array = lax.all_to_all(array, "exp", split_axis=0, concat_axis=0, tiled=True)
+        return array.reshape(-1, array.shape[2])
+
+    def collect(source, name):
+        shares = spread_columns(places, source, half, direct, "spread_" + name)
+        if direct:
+            shares = [shares[0]] + [
+                lax.ppermute(shares[k], "exp", [(n, n ^ k) for n in range(peers)])
+                for k in range(1, half)
+            ]
+        else:
+            array = shares[0].reshape(half, own_rows, -1)
+            array = lax.all_to_all(
+                array, "exp", split_axis=0, concat_axis=0, axis_index_groups=halves, tiled=True
+            )
+            shares = [array.reshape(half * own_rows, -1)]
+        return to_peers(pick_rows(places, chosen, shares, own_rows, "pick_" + name))
+
+    got_rows = collect(tokens, "tokens")
+    got_grads = collect(cotangent, "cotangent")
+    slot = call(
+        functools.partial(slot_body, cap, pieces, own_rows, block_len),
+        [(shaped((1, rows), jnp.int32), VMEM)],
         [(selection[0], VMEM)],
-        "wanted_rows",
-        1 << 20,
-    )
-    requested = lax.all_to_all(wanted, "exp", split_axis=0, concat_axis=0, tiled=True)
-
-    def exchange(array):
-        array = array.reshape(peers, cap * pieces, part)
-        array = lax.all_to_all(array, "exp", split_axis=0, concat_axis=0, tiled=True)
-        return array.reshape(slots, part)
-
-    got_rows = exchange(pick_rows(cap, pieces, requested, tokens, [], "pick_tokens"))
-    got_grads = exchange(
-        pick_rows(cap, pieces, requested, cotangent, factor_parts[1:], "pick_cotangent")
-    )
+        "row_slots",
+        1 << 16,
+    )[0]
 
     gate = jax.nn.sigmoid(scores[0].reshape(-1).astype(F32) / 64.0)
     gate_wide = jnp.broadcast_to(gate[:, None], (rows, cols))
@@ -490,20 +521,21 @@
     split = [(shaped((stacked, depth // sides), BF16), HBM)] * sides
     mixed = (shaped((stacked, hidden), F32), HBM)
     flat = (shaped((rows, hidden), F32), HBM)
-    got_scratch = scratch_like((slots, part), BF16)
+    back_scratch = scratch_like((slots, part), BF16)
+    pieces_in = got_rows.shape[0] // SELECTED
     stack_scratch = scratch_like((stacked, depth), BF16)
     mixed_scratch = scratch_like((stacked, hidden), F32)
     low_scratch = scratch_like((stacked, hidden), BF16)
     flat_scratch = scratch_like((rows, hidden), F32)
     outs = call(
-        functools.partial(forward_body, cap, pieces, sides),
+        functools.partial(forward_body, sides),
         split + [mixed, mixed, flat, flat, flat],
-        [(slot, VMEM), (mixing, SMEM), (order, SMEM), (got_rows, HBM)] + sides_in,
+        [(places, SMEM), (mixing, SMEM), (got_rows, HBM)] + sides_in,
         "forward",
         2 * product,
-        [got_scratch, scratch_like((2, depth, hidden), BF16), stack_scratch, mixed_scratch, mixed_scratch]
+        [scratch_like((2, depth, hidden), BF16), stack_scratch, mixed_scratch, mixed_scratch]
         + [flat_scratch] * 4
-        + [dma((steps,)), dma((2, sides, count)), dma((7,))],
+        + [dma((pieces_in,)), dma((2, sides, count)), dma((7,))],
     )
     x_parts, (y_gate, y_up, act, slope, hid) = outs[:sides], outs[sides:]
     x_rows = [x_parts[0]] + [across(x) for x in x_parts[1:]]
@@ -513,21 +545,21 @@
         [(shaped((slots, part), BF16), HBM)]
         + split
         + [mixed, (shaped((weights, rows, hidden), BF16), HBM), (shaped((rows, cols), F32), VMEM)],
-        [(slot, VMEM), (mixing, SMEM), (order, SMEM), (gate_wide, VMEM), (got_grads, HBM)]
+        [(places, SMEM), (mixing, SMEM), (slot, VMEM), (gate_wide, VMEM), (got_grads, HBM)]
         + [(x, HBM) for x in (act, slope, hid)]
         + sides_in
         + [(x, HBM) for x in after],
         "backward",
         3 * product,
-        [got_scratch, scratch_like((weights, depth, hidden), BF16), stack_scratch, mixed_scratch]
+        [scratch_like((weights, depth, hidden), BF16), stack_scratch, mixed_scratch]
         + [scratch_like((weights, rows, hidden), BF16)]
         + [flat_scratch] * 3
         + [low_scratch] * 2
-        + [stack_scratch, got_scratch]
-        + [dma((steps,)), dma((weights, sides, count)), dma((3,)), dma((4 + steps,))],
+        + [stack_scratch, back_scratch]
+        + [dma((pieces_in,)), dma((weights, sides, count)), dma((3,)), dma((4 + steps,))],
     )
     back, g_parts, (y_down, d_own, inner) = outs[0], outs[1 : 1 + sides], outs[1 + sides :]
-    returned = exchange(back)
+    returned = to_peers(back)
 
     d_rows = [d_own] + [across(d_own) for _ in x_parts[1:]]
     g_rows = [g_parts[0]] + [across(x) for x in g_parts[1:]]
@@ -569,7 +601,7 @@
         ).astype(F32)
         mix_grad = lax.psum(mix_part, "seq")
     gate_grad = (jnp.sum(inner, axis=1) * gate * (1.0 - gate)).reshape(selection.shape)
-    token_grad = sum_rows(cap, pieces, own_rows, requested, returned)
+    token_grad = sum_rows(cap, pieces, own_rows, places, chosen, returned)
     return token_grad, factor_grad[None], mix_grad, gate_grad
 
 

time: 167 us -> 233 us (1.40)
  Pallas kernels: 28.9 us -> 108 us
  local copies, waits for them, and re-layouts: 26.2 us -> 4.69 us
  waiting for transfers between devices: 73 us -> 56.7 us
  starting transfers between devices: 23.5 us -> 36.7 us
  blocking collectives: 10.2 us -> 22.2 us
    pallas_call x8 -> x10, Pallas kernels: 28.9 us -> 108 us  [call(): pl.pallas_call(body, out_shape=[x for x, _ in outs], in_specs=[place for...]
    unnamed x64 -> x40, local copies, waits for them, and re-layouts: 25.7 us -> 2.2 us
    all_gather x0 -> x1, blocking collectives: none -> 22.2 us  [shards(): chosen = lax.all_gather(selection[0], 'exp')]
    ppermute x5, waiting for transfers between devices: 58.8 us -> 41 us  [across(): return lax.ppermute(array, 'seq', pair)]
    ppermute x0 -> x14, waiting for transfers between devices: none -> 11.2 us  [collect(): lax.ppermute(shares[k], 'exp', [(n, n ^ k) for n in range(peers)])]
    ppermute x0 -> x14, starting transfers between devices: none -> 10.5 us  [collect(): lax.ppermute(shares[k], 'exp', [(n, n ^ k) for n in range(peers)])]
    all_to_all x1 -> x0, blocking collectives: 10.2 us -> none  [shards(): lax.all_to_all(wanted, 'exp', split_axis=0, concat_axis=0, tiled=True)]
    all_to_all x3, waiting for transfers between devices: 14.2 us -> 4.55 us  [to_peers(): lax.all_to_all(array, 'exp', split_axis=0, concat_axis=0, tiled=True)]
  transfers between devices with their start and end apart: 8 -> 22, of which waited for: 5 -> 10; matrix products, arithmetic and copies ran while one was open for 2% -> 2% of each run, Pallas kernels for 10% -> 25%
where the time goes in v6:
time: 233 us; the launch traced here: 232 us
  Pallas kernels  108 us (46%)
  waiting for transfers between devices  56.7 us (24%)
  starting transfers between devices  36.7 us (16%)
  blocking collectives  22.2 us (10%)
  local copies, waits for them, and re-layouts  4.69 us (2%)
  other arithmetic  2.99 us (1%)
    pallas_call x10, Pallas kernels, call(): pl.pallas_call(body, out_shape=[x for x, _ in outs], in_specs=[place for...  108 us
    ppermute x5, waiting for transfers between devices, across(): return lax.ppermute(array, 'seq', pair)  41 us
    all_gather x1, blocking collectives, shards(): chosen = lax.all_gather(selection[0], 'exp')  22.2 us
    all_to_all x3, starting transfers between devices, to_peers(): lax.all_to_all(array, 'exp', split_axis=0, concat_axis=0, tiled=True)  20.9 us
    ppermute x14, waiting for transfers between devices, collect(): lax.ppermute(shares[k], 'exp', [(n, n ^ k) for n in range(peers)])  11.2 us
    ppermute x14, starting transfers between devices, collect(): lax.ppermute(shares[k], 'exp', [(n, n ^ k) for n in range(peers)])  10.5 us
    ppermute x5, starting transfers between devices, across(): return lax.ppermute(array, 'seq', pair)  5.28 us
  transfers between devices with their start and end apart: 22, of which 10 were waited for; matrix products, arithmetic and copies ran while one was open for 2% of the time, Pallas kernels for 25%

profile of v6, /device:TPU:13, one launch (start us, length us, event | category | flops | bytes accessed | tf_op | source)
XLA Modules:
  0.0 232.2 jit_solution(5809072181159415197)
XLA Ops:
  1.3 33.6 %spread_tokens.1 = (bf16[128,512]{1,0:T(8,128)(2,1)}, bf16[128,512]{1,0:T(8,128)(2,1)}, bf16[128,512]{1,0:T(8,128)(2,1)}, bf16[128,512]{1,0:T(8,128)(2,1)}, bf16...) custom-call(s32[5]{0:T(128)} %stack.23.places_ref.order_ref, ...), custom_call_target="tpu_custom_call" | custom-call | bytes 2097172 | tf_op jit(solution)/shard_map/spread_tokens/pallas_call | solution.py:40
  37.6 1.6 collective-permute-start.11
  39.2 1.8 collective-permute-done.8.refs_2_
  41.8 22.2 %all_gather.3.chosen_ref = s32[16,2,64]{2,1,0:T(2,128)} all-gather(s32[1,2,64]{2,1,0:T(2,128)} %param.10), channel_id=1, replica_groups=mesh['seq'=2,'exp'=16] {'exp'}, dimensions={0}, use_global_device_ids=true | all-gather | bytes 8704 | tf_op jit(solution)/shard_map/all_gather | solution.py:484
  64.9 4.6 %pick_tokens.1 = bf16[1024,512]{1,0:T(8,128)(2,1)} custom-call(s32[5]{0:T(128)} %stack.23.places_ref.order_ref, s32[16,2,64]{2,1,0:T(2,128)} %all_gather.3.chosen_ref, bf16[128,512]{1,0:T(8,128)(2,1)} %get-tuple-element.41.refs_0_, bf16[128,512]{1,0:T(8,128)(2,1)} %copy-done.7, bf16[128,512]{1,0:T(8,128)(2,1)} %copy-done.9, bf16[128,512]{1,0:T(8,128)(2,1)} %copy-done.11, ...), custom_call_target="tpu_custom_call" | custom-call | flops 1073741824 | bytes 2105364 | tf_op jit(solution)/shard_map/pick_tokens/pallas_call | solution.py:40
  69.4 7.5 %all-to-all-start.1 = ((bf16[16,64,512]{2,1,0:T(8,128)(2,1)}), bf16[16,64,512]{2,1,0:T(8,128)(2,1)}, u32[]{:S(2)}, u32[]{:S(2)}) async-start(bf16[16,64,512]{2,1,0:T(8,128)(2,1)} %bitcast.19), calls=%async_computation.1 | async-start | bytes 2097152 | tf_op jit(solution)/shard_map/all_to_all | solution.py:489
  76.9 33.6 %spread_cotangent.1 = (bf16[128,512]{1,0:T(8,128)(2,1)}, bf16[128,512]{1,0:T(8,128)(2,1)}, bf16[128,512]{1,0:T(8,128)(2,1)}, bf16[128,512]{1,0:T(8,128)(2,1)}, b...) custom-call(s32[5]{0:T(128)} %stack.23.places_ref.order_ref, ...), custom_call_target="tpu_custom_call" | custom-call | bytes 2097172 | tf_op jit(solution)/shard_map/spread_cotangent/pallas_call | solution.py:40
  111.2 1.5 collective-permute-start.2
  114.5 1.6 collective-permute-done.1.refs_2_
  117.6 1.9 collective-permute-done.2.refs_3_
  121.8 1.9 collective-permute-done.5.refs_6_
  123.6 3.0 %collective-permute-done.6.refs_7_ = bf16[128,512]{1,0:T(8,128)(2,1)S(1)} collective-permute-done((bf16[128,512]{1,0:T(8,128)(2,1)}, bf16[128,512]{1,0:T(8,128)(2,1)S(1)}, u32[]{:S(2)}, u32[]{:S(2)}) %collective-permute-start.6) | collective-permute-done | bytes 131104 | tf_op jit(solution)/shard_map/ppermute | solution.py:496
  127.3 4.6 %pick_cotangent.1 = bf16[1024,512]{1,0:T(8,128)(2,1)} custom-call(s32[5]{0:T(128)} %stack.23.places_ref.order_ref, s32[16,2,64]{2,1,0:T(2,128)} %all_gather.3.chosen_ref, bf16[128,512]{1,0:T(8,128)(2,1)} %get-tuple-element.33.refs_0_, bf16[128,512]{1,0:T(8,128)(2,1)} %copy-done.6, bf16[128,512]{1,0:T(8,128)(2,1)} %copy-done.8, bf16[128,512]{1,0:T(8,128)(2,1)} %copy-done.10, ...), custom_call_target="tpu_custom_call" | custom-call | flops 1073741824 | bytes 2105364 | tf_op jit(solution)/shard_map/pick_cotangent/pallas_call | solution.py:40
  131.9 6.0 %all-to-all-start = ((bf16[16,64,512]{2,1,0:T(8,128)(2,1)}), bf16[16,64,512]{2,1,0:T(8,128)(2,1)}, u32[]{:S(2)}, u32[]{:S(2)}) async-start(bf16[16,64,512]{2,1,0:T(8,128)(2,1)} %bitcast.20), calls=%async_computation | async-start | bytes 2097152 | tf_op jit(solution)/shard_map/all_to_all | solution.py:489
  138.5 17.4 %collective-permute-done.14 = bf16[1,3,4,512,128]{4,3,2,1,0:T(8,128)(2,1)} collective-permute-done((bf16[1,3,4,512,128]{4,3,2,1,0:T(8,128)(2,1)}, bf16[1,3,4,512,128]{4,3,2,1,0:T(8,128)(2,1)}, u32[]{:S(2)}, u32[]{:S(2)}) %collective-permute-start.14) | collective-permute-done | bytes 1572896 | tf_op jit(solution)/shard_map/ppermute | solution.py:470
  156.0 6.1 %forward.1 = (bf16[512,512]{1,0:T(8,128)(2,1)}, bf16[512,512]{1,0:T(8,128)(2,1)}, f32[512,512]{1,0:T(8,128)}, f32[512,512]{1,0:T(8,128)}, f32[128,512]{1,0:T(8,1...) custom-call(s32[5]{0:T(128)} %stack.23.places_ref.order_ref, f32[192]{0:T(256)} %reshape.49.mix_ref, ...), custom_call_target="tpu_custom_call" | custom-call | flops 1073741824 | bytes 8127252 | tf_op jit(solution)/shard_map/forward/pallas_call | solution.py:40
  164.8 10.3 %collective-permute-done.15.refs_2_.refs_3_ = bf16[512,512]{1,0:T(8,128)(2,1)S(1)} collective-permute-done((bf16[512,512]{1,0:T(8,128)(2,1)}, bf16[512,512]{1,0:T(8,128)(2,1)S(1)}, u32[]{:S(2)}, u32[]{:S(2)}) %collective-permute-start.15) | collective-permute-done | bytes 524320 | tf_op jit(solution)/shard_map/ppermute | solution.py:470
  176.0 8.7 %backward.1 = (bf16[384,2048]{1,0:T(8,128)(2,1)}, bf16[512,512]{1,0:T(8,128)(2,1)}, bf16[512,512]{1,0:T(8,128)(2,1)}, f32[512,512]{1,0:T(8,128)}, bf16[3,128,512]{2,1,0:T(8,128)(2,1)}, /*index=5*/f32[128,128]{1,0:T(8,128)}) custom-call(s32[5]{0:T(128)} %stack.23.places_ref.order_ref, f32[192]{0:T(256)} %reshape.49.mix_ref, s32[1,128]{1,0:T(1,128)} %row_slots.1.slot_ref, ...), custom_call_target="tpu_custom_call" | custom-call | flops 1610612736 | bytes 9700628 | tf_op jit(solution)/shard_map/backward/pallas_call | solution.py:40
  184.7 7.4 %all-to-all-start.2 = ((bf16[16,24,2048]{2,1,0:T(8,128)(2,1)}), bf16[16,24,2048]{2,1,0:T(8,128)(2,1)}, u32[]{:S(2)}, u32[]{:S(2)}) async-start(bf16[16,24,2048]{2,1,0:T(8,128)(2,1)} %bitcast.18), calls=%async_computation.2 | async-start | bytes 3145728 | tf_op jit(solution)/shard_map/all_to_all | solution.py:489
  193.6 3.9 %mix_partials.1 = f32[192,128]{1,0:T(8,128)} custom-call(f32[512,512]{1,0:T(8,128)} %get-tuple-element.58.yg_hbm, f32[512,512]{1,0:T(8,128)} %get-tuple-element.59.yu_hbm, f32[512,512]{1,0:T(8,128)} %get-tuple-element.60.yd_hbm, bf16[3,128,512]{2,1,0:T(8,128)(2,1)} %get-tuple-element.56.refs_2_.d_hbm), custom_call_target="tpu_custom_call" | custom-call | flops 6291456 | bytes 3637248 | tf_op jit(solution)/shard_map/mix_partials/pallas_call | solution.py:40
  201.4 13.2 %collective-permute-done.18 = f32[1,3,4,4,4]{4,3,2,1,0:T(4,128)S(1)} collective-permute-done((f32[1,3,4,4,4]{4,3,2,1,0:T(4,128)S(1)}, f32[1,3,4,4,4]{4,3,2,1,0:T(4,128)S(1)}, u32[]{:S(2)}, u32[]{:S(2)}) %collective-permute-start.18) | collective-permute-done | bytes 800 | tf_op jit(solution)/shard_map/ppermute | solution.py:470
  216.0 7.8 %factor_grad.1 = f32[3,4,512,128]{3,2,1,0:T(8,128)} custom-call(f32[192]{0:T(256)} %reshape.49.mix_ref, bf16[512,512]{1,0:T(8,128)(2,1)} %get-tuple-element.54.refs_0_, bf16[512,512]{1,0:T(8,128)(2,1)} %get-tuple-element.55.refs_1_, bf16[3,128,512]{2,1,0:T(8,128)(2,1)} %get-tuple-element.56.refs_2_.d_hbm, bf16[512,512]{1,0:T(8,128)(2,1)} %copy-done.1, ...), custom_call_target="tpu_custom_call" | custom-call | flops 1610612736 | bytes 6030080 | tf_op jit(solution)/shard_map/factor_grad/pallas_call | solution.py:40
  223.8 4.5 %all-to-all-done.2 = bf16[16,24,2048]{2,1,0:T(8,128)(2,1)} async-done(((bf16[16,24,2048]{2,1,0:T(8,128)(2,1)}), bf16[16,24,2048]{2,1,0:T(8,128)(2,1)}, u32[]{:S(2)}, u32[]{:S(2)}) %all-to-all-start.2) | async-done | bytes 1572896 | tf_op jit(solution)/shard_map/all_to_all | solution.py:489
  228.4 3.7 %sum_rows.1 = bf16[128,4096]{1,0:T(8,128)(2,1)} custom-call(s32[5]{0:T(128)} %stack.23.places_ref.order_ref, s32[16,2,64]{2,1,0:T(2,128)} %all_gather.3.chosen_ref, bf16[384,2048]{1,0:T(8,128)(2,1)} %bitcast.13.returned_ref), custom_call_target="tpu_custom_call" | custom-call | flops 402653184 | bytes 2629652 | tf_op jit(solution)/shard_map/sum_rows/pallas_call | solution.py:40
  (82 shorter events, 22.7 us)
Async XLA Ops:
  34.9 4.3 %collective-permute-start.7 = (bf16[128,512]{1,0:T(8,128)(2,1)}, bf16[128,512]{1,0:T(8,128)(2,1)S(1)}, u32[]{:S(2)}, u32[]{:S(2)}) collective-permute-start(bf16[128,512]{1,0:T(8,128)(2,1)} %get-tuple-element.42), channel_id=1, source_target_pairs={{0,1},{1,0},{2,3},{3,2},{4,5},{5,4},{6,7},{7,6},{8,9},{9,8},{10,11... | collective-permute-start | bytes 393224 | tf_op jit(solution)/shard_map/ppermute | solution.py:496
  35.7 5.3 %collective-permute-start.8 = (bf16[128,512]{1,0:T(8,128)(2,1)}, bf16[128,512]{1,0:T(8,128)(2,1)S(1)}, u32[]{:S(2)}, u32[]{:S(2)}) collective-permute-start(bf16[128,512]{1,0:T(8,128)(2,1)} %get-tuple-element.43), channel_id=1, source_target_pairs={{0,2},{1,3},{2,0},{3,1},{4,6},{5,7},{6,4},{7,5},{8,10},{9,11},{10,... | collective-permute-start | bytes 393224 | tf_op jit(solution)/shard_map/ppermute | solution.py:496
  35.9 28.1 %collective-permute-start.9 = (bf16[128,512]{1,0:T(8,128)(2,1)}, bf16[128,512]{1,0:T(8,128)(2,1)S(1)}, u32[]{:S(2)}, u32[]{:S(2)}) collective-permute-start(bf16[128,512]{1,0:T(8,128)(2,1)} %get-tuple-element.44), channel_id=1, source_target_pairs={{0,3},{1,2},{2,1},{3,0},{4,7},{5,6},{6,5},{7,4},{8,11},{9,10},{10,... | collective-permute-start | bytes 393224 | tf_op jit(solution)/shard_map/ppermute | solution.py:496
  37.4 26.6 %collective-permute-start.10 = (bf16[128,512]{1,0:T(8,128)(2,1)}, bf16[128,512]{1,0:T(8,128)(2,1)S(1)}, u32[]{:S(2)}, u32[]{:S(2)}) collective-permute-start(bf16[128,512]{1,0:T(8,128)(2,1)} %get-tuple-element.45), channel_id=1, source_target_pairs={{0,4},{1,5},{2,6},{3,7},{4,0},{5,1},{6,2},{7,3},{8,12},{9,13},{10,... | collective-permute-start | bytes 393224 | tf_op jit(solution)/shard_map/ppermute | solution.py:496
  37.6 26.5 %collective-permute-start.11 = (bf16[128,512]{1,0:T(8,128)(2,1)}, bf16[128,512]{1,0:T(8,128)(2,1)S(1)}, u32[]{:S(2)}, u32[]{:S(2)}) collective-permute-start(bf16[128,512]{1,0:T(8,128)(2,1)} %get-tuple-element.46), channel_id=1, source_target_pairs={{0,5},{1,4},{2,7},{3,6},{4,1},{5,0},{6,3},{7,2},{8,13},{9,12},{10,... | collective-permute-start | bytes 393224 | tf_op jit(solution)/shard_map/ppermute | solution.py:496
  39.2 24.9 %copy-start.7 = (bf16[128,512]{1,0:T(8,128)(2,1)}, bf16[128,512]{1,0:T(8,128)(2,1)S(1)}, u32[]{:S(2)}) copy-start(bf16[128,512]{1,0:T(8,128)(2,1)S(1)} %collective-permute-done.7.refs_1_) | copy-start | bytes 393220
  39.2 24.9 %collective-permute-start.12 = (bf16[128,512]{1,0:T(8,128)(2,1)}, bf16[128,512]{1,0:T(8,128)(2,1)S(1)}, u32[]{:S(2)}, u32[]{:S(2)}) collective-permute-start(bf16[128,512]{1,0:T(8,128)(2,1)} %get-tuple-element.47), channel_id=1, source_target_pairs={{0,6},{1,7},{2,4},{3,5},{4,2},{5,3},{6,0},{7,1},{8,14},{9,15},{10,... | collective-permute-start | bytes 393224 | tf_op jit(solution)/shard_map/ppermute | solution.py:496
  41.0 23.2 %copy-start.9 = (bf16[128,512]{1,0:T(8,128)(2,1)}, bf16[128,512]{1,0:T(8,128)(2,1)S(1)}, u32[]{:S(2)}) copy-start(bf16[128,512]{1,0:T(8,128)(2,1)S(1)} %collective-permute-done.8.refs_2_) | copy-start | bytes 393220
  41.0 23.1 %collective-permute-start.13 = (bf16[128,512]{1,0:T(8,128)(2,1)}, bf16[128,512]{1,0:T(8,128)(2,1)S(1)}, u32[]{:S(2)}, u32[]{:S(2)}) collective-permute-start(bf16[128,512]{1,0:T(8,128)(2,1)} %get-tuple-element.48), channel_id=1, source_target_pairs={{0,7},{1,6},{2,5},{3,4},{4,3},{5,2},{6,1},{7,0},{8,15},{9,14},{10,... | collective-permute-start | bytes 393224 | tf_op jit(solution)/shard_map/ppermute | solution.py:496
  69.4 62.4 %all-to-all-start.1 = ((bf16[16,64,512]{2,1,0:T(8,128)(2,1)}), bf16[16,64,512]{2,1,0:T(8,128)(2,1)}, u32[]{:S(2)}, u32[]{:S(2)}) async-start(bf16[16,64,512]{2,1,0:T(8,128)(2,1)} %bitcast.19), calls=%async_computation.1 | async-start | bytes 2097152 | tf_op jit(solution)/shard_map/all_to_all | solution.py:489
  110.5 3.9 %collective-permute-start = (bf16[128,512]{1,0:T(8,128)(2,1)}, bf16[128,512]{1,0:T(8,128)(2,1)S(1)}, u32[]{:S(2)}, u32[]{:S(2)}) collective-permute-start(bf16[128,512]{1,0:T(8,128)(2,1)} %get-tuple-element.34), channel_id=1, source_target_pairs={{0,1},{1,0},{2,3},{3,2},{4,5},{5,4},{6,7},{7,6},{8,9},{9,8},{10,11... | collective-permute-start | bytes 393224 | tf_op jit(solution)/shard_map/ppermute | solution.py:496
  111.0 5.2 %collective-permute-start.1 = (bf16[128,512]{1,0:T(8,128)(2,1)}, bf16[128,512]{1,0:T(8,128)(2,1)S(1)}, u32[]{:S(2)}, u32[]{:S(2)}) collective-permute-start(bf16[128,512]{1,0:T(8,128)(2,1)} %get-tuple-element.35), channel_id=1, source_target_pairs={{0,2},{1,3},{2,0},{3,1},{4,6},{5,7},{6,4},{7,5},{8,10},{9,11},{10,... | collective-permute-start | bytes 393224 | tf_op jit(solution)/shard_map/ppermute | solution.py:496
  111.2 8.3 %collective-permute-start.2 = (bf16[128,512]{1,0:T(8,128)(2,1)}, bf16[128,512]{1,0:T(8,128)(2,1)S(1)}, u32[]{:S(2)}, u32[]{:S(2)}) collective-permute-start(bf16[128,512]{1,0:T(8,128)(2,1)} %get-tuple-element.36), channel_id=1, source_target_pairs={{0,3},{1,2},{2,1},{3,0},{4,7},{5,6},{6,5},{7,4},{8,11},{9,10},{10,... | collective-permute-start | bytes 393224 | tf_op jit(solution)/shard_map/ppermute | solution.py:496
  112.8 8.0 %collective-permute-start.3 = (bf16[128,512]{1,0:T(8,128)(2,1)}, bf16[128,512]{1,0:T(8,128)(2,1)S(1)}, u32[]{:S(2)}, u32[]{:S(2)}) collective-permute-start(bf16[128,512]{1,0:T(8,128)(2,1)} %get-tuple-element.37), channel_id=1, source_target_pairs={{0,4},{1,5},{2,6},{3,7},{4,0},{5,1},{6,2},{7,3},{8,12},{9,13},{10,... | collective-permute-start | bytes 393224 | tf_op jit(solution)/shard_map/ppermute | solution.py:496
  113.0 8.7 %collective-permute-start.4 = (bf16[128,512]{1,0:T(8,128)(2,1)}, bf16[128,512]{1,0:T(8,128)(2,1)S(1)}, u32[]{:S(2)}, u32[]{:S(2)}) collective-permute-start(bf16[128,512]{1,0:T(8,128)(2,1)} %get-tuple-element.38), channel_id=1, source_target_pairs={{0,5},{1,4},{2,7},{3,6},{4,1},{5,0},{6,3},{7,2},{8,13},{9,12},{10,... | collective-permute-start | bytes 393224 | tf_op jit(solution)/shard_map/ppermute | solution.py:496
  114.5 9.2 %collective-permute-start.5 = (bf16[128,512]{1,0:T(8,128)(2,1)}, bf16[128,512]{1,0:T(8,128)(2,1)S(1)}, u32[]{:S(2)}, u32[]{:S(2)}) collective-permute-start(bf16[128,512]{1,0:T(8,128)(2,1)} %get-tuple-element.39), channel_id=1, source_target_pairs={{0,6},{1,7},{2,4},{3,5},{4,2},{5,3},{6,0},{7,1},{8,14},{9,15},{10,... | collective-permute-start | bytes 393224 | tf_op jit(solution)/shard_map/ppermute | solution.py:496
  116.1 10.5 %collective-permute-start.6 = (bf16[128,512]{1,0:T(8,128)(2,1)}, bf16[128,512]{1,0:T(8,128)(2,1)S(1)}, u32[]{:S(2)}, u32[]{:S(2)}) collective-permute-start(bf16[128,512]{1,0:T(8,128)(2,1)} %get-tuple-element.40), channel_id=1, source_target_pairs={{0,7},{1,6},{2,5},{3,4},{4,3},{5,2},{6,1},{7,0},{8,15},{9,14},{10,... | collective-permute-start | bytes 393224 | tf_op jit(solution)/shard_map/ppermute | solution.py:496
  119.5 36.4 %collective-permute-start.14 = (bf16[1,3,4,512,128]{4,3,2,1,0:T(8,128)(2,1)}, bf16[1,3,4,512,128]{4,3,2,1,0:T(8,128)(2,1)}, u32[]{:S(2)}, u32[]{:S(2)}) collective-permute-start(bf16[1,3,4,512,128]{4,3,2,1,0:T(8,128)(2,1)} %param.8), channel_id=1, source_target_pairs={{0,16},{16,0},{1,17},{17,1},{2,18},{18,2},{3,19},{19,3},{4,20},{20... | collective-permute-start | bytes 4718600 | tf_op jit(solution)/shard_map/ppermute | solution.py:470
  131.9 32.9 %all-to-all-start = ((bf16[16,64,512]{2,1,0:T(8,128)(2,1)}), bf16[16,64,512]{2,1,0:T(8,128)(2,1)}, u32[]{:S(2)}, u32[]{:S(2)}) async-start(bf16[16,64,512]{2,1,0:T(8,128)(2,1)} %bitcast.20), calls=%async_computation | async-start | bytes 2097152 | tf_op jit(solution)/shard_map/all_to_all | solution.py:489
  162.1 13.1 %collective-permute-start.15 = (bf16[512,512]{1,0:T(8,128)(2,1)}, bf16[512,512]{1,0:T(8,128)(2,1)S(1)}, u32[]{:S(2)}, u32[]{:S(2)}) collective-permute-start(bf16[512,512]{1,0:T(8,128)(2,1)} %get-tuple-element.52), channel_id=1, source_target_pairs={{0,16},{16,0},{1,17},{17,1},{2,18},{18,2},{3,19},{19,3},{4,20},{20... | collective-permute-start | bytes 1572872 | tf_op jit(solution)/shard_map/ppermute | solution.py:470
  184.7 43.7 %all-to-all-start.2 = ((bf16[16,24,2048]{2,1,0:T(8,128)(2,1)}), bf16[16,24,2048]{2,1,0:T(8,128)(2,1)}, u32[]{:S(2)}, u32[]{:S(2)}) async-start(bf16[16,24,2048]{2,1,0:T(8,128)(2,1)} %bitcast.18), calls=%async_computation.2 | async-start | bytes 3145728 | tf_op jit(solution)/shard_map/all_to_all | solution.py:489
  192.1 23.1 %collective-permute-start.16 = (bf16[512,512]{1,0:T(8,128)(2,1)}, bf16[512,512]{1,0:T(8,128)(2,1)S(1)}, u32[]{:S(2)}, u32[]{:S(2)}) collective-permute-start(bf16[512,512]{1,0:T(8,128)(2,1)} %get-tuple-element.57), channel_id=1, source_target_pairs={{0,16},{16,0},{1,17},{17,1},{2,18},{18,2},{3,19},{19,3},{4,20},{20... | collective-permute-start | bytes 1572872 | tf_op jit(solution)/shard_map/ppermute | solution.py:470
  193.3 21.8 %collective-permute-start.17 = (bf16[3,128,512]{2,1,0:T(8,128)(2,1)S(1)}, bf16[3,128,512]{2,1,0:T(8,128)(2,1)}, u32[]{:S(2)}, u32[]{:S(2)}) collective-permute-start(bf16[3,128,512]{2,1,0:T(8,128)(2,1)S(1)} %copy-done), channel_id=1, source_target_pairs={{0,16},{16,0},{1,17},{17,1},{2,18},{18,2},{3,19},{19,3},{4,20},{20... | collective-permute-start | bytes 1179656 | tf_op jit(solution)/shard_map/ppermute | solution.py:470
  198.8 15.7 %collective-permute-start.18 = (f32[1,3,4,4,4]{4,3,2,1,0:T(4,128)S(1)}, f32[1,3,4,4,4]{4,3,2,1,0:T(4,128)S(1)}, u32[]{:S(2)}, u32[]{:S(2)}) collective-permute-start(f32[1,3,4,4,4]{4,3,2,1,0:T(4,128)S(1)} %reshape.56), channel_id=1, source_target_pairs={{0,16},{16,0},{1,17},{17,1},{2,18},{18,2},{3,19},{19,3},{4,20},{20... | collective-permute-start | bytes 2312 | tf_op jit(solution)/shard_map/ppermute | solution.py:470
  (18 other events, 77.8 us)

commit v7 on v6

--- a/solution.py
+++ b/solution.py
@@ -72,35 +72,64 @@
     return [begin(source, target, sems.at[n]) for n, (source, target) in enumerate(pairs)]
 
 
-def spread_columns(places, source, half, direct, name):
+def spread_columns(me, source, half, direct, name, more=(), selection=None, cuts=None):
     own_rows, width = source.shape
     part = width // half
-
-    def body(places_ref, source_ref, *refs):
-        outs, sems = refs[:-1], refs[-1]
+    count = half if direct else 1
+    ahead = [] if cuts is None else [(selection, VMEM), (cuts, HBM)]
+
+    def body(me_ref, source_ref, *refs):
+        held_ref, sems = refs[-2:]
+        refs = refs[:-2]
+        load = begin(source_ref, held_ref.at[0], sems.at[0])
+        if ahead:
+            chosen_ref, cuts_ref, refs = refs[0], refs[1], refs[2:]
+            wanted_ref, pieces, refs = refs[0], refs[1 : 1 + cuts.shape[0]], refs[1 + cuts.shape[0] :]
+        outs, scratch = refs[:count], refs[count:]
         copies = []
+        if ahead:
+            cut_ref, cut_sems = scratch
+            cuts_in = [
+                begin(cuts_ref.at[m], cut_ref.at[m], cut_sems.at[0, m])
+                for m in range(cuts.shape[0])
+            ]
+            row = jnp.concatenate([chosen_ref[b : b + 1, :] for b in range(chosen_ref.shape[0])], axis=1)
+            wanted_ref[...] = jnp.broadcast_to(row, wanted_ref.shape)
+        load.wait()
+        low = me_ref[0] & (half - 1)
         for k in range(half):
-            share = places_ref[1] ^ k if direct else k
-            at = source_ref.at[:, pl.ds(pl.multiple_of(share * part, part), part)]
+            share = low ^ k if direct else k
+            at = held_ref.at[0, :, pl.ds(pl.multiple_of(share * part, part), part)]
             out = outs[k] if direct else outs[0].at[k * own_rows : (k + 1) * own_rows]
-            copies.append(begin(at, out, sems.at[k]))
+            copies.append(begin(at, out, sems.at[1 + k]))
+        if ahead:
+            for m, copy in enumerate(cuts_in):
+                copy.wait()
+                copies.append(begin(cut_ref.at[m], pieces[m], cut_sems.at[1, m]))
         wait_all(copies)
 
     if direct:
         outs = [(shaped((own_rows, part), BF16), HBM)] * half
     else:
         outs = [(shaped((half * own_rows, part), BF16), HBM)]
-    ins = [(places, SMEM), (source, HBM)]
-    return call(body, outs, ins, name, 0, [pltpu.SemaphoreType.DMA((half,))])
-
-
-def pick_rows(places, chosen, shares, own_rows, name):
-    peers, _, picks = chosen.shape
+    scratch = []
+    if ahead:
+        wanted = shaped((more[0], selection.size), jnp.int32)
+        outs = [(wanted, VMEM)] + [(shaped(cuts.shape[1:], BF16), HBM)] * cuts.shape[0] + outs
+        scratch = [scratch_like(cuts.shape, BF16), pltpu.SemaphoreType.DMA((2, cuts.shape[0]))]
+    scratch += [scratch_like((1, own_rows, width), BF16), pltpu.SemaphoreType.DMA((1 + half,))]
+    return call(body, outs, [(me, SMEM), (source, HBM)] + ahead, name, 0, scratch)
+
+
+def pick_rows(me, half, chosen, shares, after, name):
+    peers, total = chosen.shape
+    picks = total * half // peers
     part = shares[0].shape[1]
     block = sum(x.shape[0] for x in shares)
-    batch = min(peers, 16)
-
-    def body(places_ref, chosen_ref, *refs):
+    batch = min(peers, 8)
+
+    def body(me_ref, chosen_ref, *refs):
+        refs = refs[len(after) :]
         parts, (out_ref, rows_ref, pick_ref, sent_ref, in_sem, out_sem) = (
             refs[: len(shares)],
             refs[len(shares) :],
@@ -108,33 +137,35 @@
         loads = []
         for k, share in enumerate(parts):
             size = share.shape[0]
-            start = pl.multiple_of((places_ref[1] ^ k) * size if len(parts) > 1 else 0, 16)
+            place = (me_ref[0] & (half - 1)) ^ k if len(parts) > 1 else 0
+            start = pl.multiple_of(place * size, 16)
             loads.append(begin(share, rows_ref.at[pl.ds(start, size)], in_sem.at[k]))
+        block_at = lax.shift_right_logical(me_ref[0], half.bit_length() - 1)
+        same = iota((picks, total), 0) + block_at * picks == iota((picks, total), 1)
         stores = []
         for first in range(0, peers, batch):
             for e in range(batch):
-                wanted = chosen_ref[first + e, pl.ds(places_ref[2], 1), :]
-                same = iota((picks, picks), 0) == iota((picks, picks), 1)
+                wanted = chosen_ref[first + e : first + e + 1, :]
                 column = jnp.sum(jnp.where(same, wanted, 0), axis=1, keepdims=True)
-                pick_ref[e * picks : (e + 1) * picks] = (
+                pick_ref[first // batch % 2, e * picks : (e + 1) * picks] = (
                     column == iota((picks, block), 1)
                 ).astype(BF16)
             if first == 0:
                 wait_all(loads)
             at = slice(first * picks, (first + batch) * picks)
-            sent_ref[at] = dot(pick_ref[...], rows_ref[...]).astype(BF16)
+            sent_ref[at] = dot(pick_ref[first // batch % 2], rows_ref[...]).astype(BF16)
             stores.append(begin(sent_ref.at[at], out_ref.at[at], out_sem.at[first // batch]))
         wait_all(stores)
 
     return call(
         body,
         [(shaped((peers * picks, part), BF16), HBM)],
-        [(places, SMEM), (chosen, VMEM)] + [(x, HBM) for x in shares],
+        [(me, SMEM), (chosen, VMEM)] + [(x, HBM) for x in list(after) + list(shares)],
         name,
         2 * peers * picks * block * part,
         [
             scratch_like((block, part), BF16),
-            scratch_like((batch * picks, block), BF16),
+            scratch_like((2, batch * picks, block), BF16),
             scratch_like((peers * picks, part), BF16),
             pltpu.SemaphoreType.DMA((len(shares),)),
             pltpu.SemaphoreType.DMA((peers // batch,)),
@@ -155,23 +186,29 @@
     slot_ref[...] = owner * (cap * pieces) + iota((1, rows), 1) - earlier
 
 
-def sum_rows(cap, pieces, own_rows, places, chosen, returned):
+def sum_rows(cap, pieces, own_rows, me, half, chosen, returned):
     slots, part = returned.shape
-    peers, _, picks = chosen.shape
+    peers, total = chosen.shape
+    picks = total * half // peers
     group = cap * pieces
     columns = chunks_of(part)
 
-    def body(places_ref, chosen_ref, returned_ref, out_ref, got_ref, pick_ref, sum_ref, in_sem, out_sem):
+    def body(me_ref, chosen_ref, returned_ref, out_ref, got_ref, pick_ref, sum_ref, in_sem, out_sem):
         loads = [
             begin(returned_ref.at[:, at], got_ref.at[:, at], in_sem.at[n])
             for n, at in enumerate(columns)
         ]
+        low = me_ref[0] & (half - 1)
+        block_at = lax.shift_right_logical(me_ref[0], half.bit_length() - 1)
+        lane = iota((peers, total), 1) - block_at * picks
+        here = (lane >= 0) & (lane < picks)
+        local = jnp.where(here, chosen_ref[...] - low * own_rows, own_rows)
+        before = jnp.sum((local < 0).astype(F32), axis=1, keepdims=True).astype(jnp.int32)
+        ranks = lane - before
+        owned = jnp.where((local >= 0) & (local < own_rows), local + 1, 0)
+        place = iota((group, total), 0)
         for e in range(peers):
-            local = chosen_ref[e, pl.ds(places_ref[2], 1), :] - places_ref[1] * own_rows
-            before = jnp.sum((local < 0).astype(F32), axis=1, keepdims=True).astype(jnp.int32)
-            rank = iota((1, picks), 1) - before
-            mine = jnp.where((local >= 0) & (local < own_rows), local + 1, 0)
-            place = iota((group, picks), 0)
+            rank, mine = ranks[e : e + 1], owned[e : e + 1]
             column = jnp.zeros((group, 1), jnp.int32)
             for j in range(pieces):
                 hit = jnp.where((place == rank + j * cap) & (rank >= 0) & (rank < cap), mine, 0)
@@ -184,10 +221,10 @@
         stores = []
         for n, at in enumerate(columns):
             loads[n].wait()
-            total = dot_tn(pick, got_ref[:, at]).astype(BF16)
+            summed = dot_tn(pick, got_ref[:, at]).astype(BF16)
             for j in range(pieces):
                 wide = slice(j * part + at.start, j * part + at.stop)
-                sum_ref[:, wide] = total[j * own_rows : (j + 1) * own_rows]
+                sum_ref[:, wide] = summed[j * own_rows : (j + 1) * own_rows]
                 stores.append(
                     begin(sum_ref.at[:, wide], out_ref.at[:, wide], out_sem.at[n, j])
                 )
@@ -196,7 +233,7 @@
     return call(
         body,
         [(shaped((own_rows, part * pieces), BF16), HBM)],
-        [(places, SMEM), (chosen, VMEM), (returned, HBM)],
+        [(me, SMEM), (chosen, VMEM), (returned, HBM)],
         "sum_rows",
         2 * slots * pieces * own_rows * part,
         [
@@ -211,12 +248,13 @@
 
 def load_factor(order_ref, parts, m, target, sems):
     copies = []
-    for n, side in enumerate(parts):
-        _, count, rows, cols = side.shape
-        start = pl.multiple_of(order_ref[3 + n] * rows, rows)
+    for n, side in enumerate((parts[0].at[m], parts[1 + m]) if len(parts) > 1 else (parts[0].at[m],)):
+        count, rows, cols = side.shape
+        place = order_ref[0] ^ n if len(parts) > 1 else 0
+        start = pl.multiple_of(place * rows, rows)
         for i in range(count):
             at = target.at[pl.ds(start, rows), i * cols : (i + 1) * cols]
-            copies.append(begin(side.at[m, i], at, sems.at[n, i]))
+            copies.append(begin(side.at[i], at, sems.at[n, i]))
     return copies
 
 
@@ -249,7 +287,7 @@
     copies = []
     for n, out in enumerate(outs):
         size = out.shape[1]
-        start = pl.multiple_of(order_ref[3 + n] * size, size)
+        start = pl.multiple_of((order_ref[0] ^ n) * size if len(outs) > 1 else 0, size)
         copies.append(begin(source_ref.at[:, pl.ds(start, size)], out, sems.at[n]))
     return copies
 
@@ -298,7 +336,8 @@
 def forward_body(
     sides, order_ref, mix_ref, got_hbm, *refs
 ):
-    parts, refs = refs[:sides], refs[sides:]
+    held = 3 if sides > 1 else 1
+    parts, refs = refs[:held], refs[held:]
     x_outs, refs = refs[:sides], refs[sides:]
     yg_hbm, yu_hbm, act_hbm, slope_hbm, hid_hbm = refs[:5]
     side_ref, x_ref, yg_ref, yu_ref, pre_ref, act_ref, slope_ref, hid_ref = refs[5:13]
@@ -343,7 +382,8 @@
     cap, pieces, sides, after, order_ref, mix_ref, slot_ref, gate_ref, got_hbm, act_hbm, slope_hbm, hid_hbm,
     *refs,
 ):
-    parts, refs = refs[:sides], refs[sides + after :]
+    held = 4 if sides > 1 else 1
+    parts, refs = refs[:held], refs[held + after :]
     back_hbm, x_outs, refs = refs[0], refs[1 : 1 + sides], refs[1 + sides :]
     y_hbm, d_hbm, inner_ref = refs[:3]
     (
@@ -446,7 +486,6 @@
 def shards(tokens, cotangent, factors, mix, selection, scores):
     peers = lax.axis_size("exp")
     groups = lax.axis_size("seq")
-    group = lax.axis_index("seq")
     own_rows, width = tokens.shape
     _, weights, count, depth_own, cols = factors.shape
     depth = depth_own * groups
@@ -469,43 +508,52 @@
     def across(array):
         return lax.ppermute(array, "seq", pair)
 
-    if swap:
-        factor_parts = [factors[0], across(factors)[0]]
-    else:
-        factor_parts = [lax.all_gather(factors, "seq", axis=3, tiled=True)[0]]
-    sides = len(factor_parts)
-    sides_in = [(x, HBM) for x in factor_parts]
-
     half = peers // selection.shape[1]
     direct = half == 8
-    me = lax.axis_index("exp")
-    first = group if swap else 0
-    places = jnp.stack([me, me % half, me // half, first, 1 - first]).astype(jnp.int32)
-    chosen = lax.all_gather(selection[0], "exp")
+    me = lax.axis_index("exp").astype(jnp.int32).reshape(1)
+    group = lax.axis_index("seq").astype(jnp.int32).reshape(1)
     halves = [list(range(h, h + half)) for h in range(0, peers, half)]
+    near = [k for k in range(1, half) if k >= 4] + [k for k in range(1, half) if k < 4]
+
+    outs = spread_columns(
+        me, tokens, half, direct, "spread_tokens", (peers,), selection[0], factors[0]
+    )
+    wanted, cuts, token_shares = outs[0], outs[1 : 1 + weights], outs[1 + weights :]
+    if swap:
+        cuts = [across(x) for x in cuts]
+        factor_parts = [factors[0]] + cuts
+        sides = 2
+    else:
+        cuts = []
+        factor_parts = [lax.all_gather(factors, "seq", axis=3, tiled=True)[0]]
+        sides = 1
+    sides_in = [(x, HBM) for x in factor_parts]
+    chosen = lax.all_to_all(wanted, "exp", split_axis=0, concat_axis=0, tiled=True)
 
     def to_peers(array):
         array = array.reshape(peers, -1, array.shape[1])
         array = lax.all_to_all(array, "exp", split_axis=0, concat_axis=0, tiled=True)
         return array.reshape(-1, array.shape[2])
 
-    def collect(source, name):
-        shares = spread_columns(places, source, half, direct, "spread_" + name)
+    def collect(shares):
         if direct:
-            shares = [shares[0]] + [
-                lax.ppermute(shares[k], "exp", [(n, n ^ k) for n in range(peers)])
-                for k in range(1, half)
-            ]
-        else:
-            array = shares[0].reshape(half, own_rows, -1)
-            array = lax.all_to_all(
-                array, "exp", split_axis=0, concat_axis=0, axis_index_groups=halves, tiled=True
-            )
-            shares = [array.reshape(half * own_rows, -1)]
-        return to_peers(pick_rows(places, chosen, shares, own_rows, "pick_" + name))
-
-    got_rows = collect(tokens, "tokens")
-    got_grads = collect(cotangent, "cotangent")
+            moved = {
+                k: lax.ppermute(shares[k], "exp", [(n, n ^ k) for n in range(peers)]) for k in near
+            }
+            return [shares[0]] + [moved[k] for k in range(1, half)]
+        array = shares[0].reshape(half, own_rows, -1)
+        array = lax.all_to_all(
+            array, "exp", split_axis=0, concat_axis=0, axis_index_groups=halves, tiled=True
+        )
+        return [array.reshape(half * own_rows, -1)]
+
+    got_rows = to_peers(
+        pick_rows(me, half, chosen, collect(token_shares), cuts[:1], "pick_tokens")
+    )
+    grad_shares = spread_columns(me, cotangent, half, direct, "spread_cotangent")
+    got_grads = to_peers(
+        pick_rows(me, half, chosen, collect(grad_shares), cuts[1:2], "pick_cotangent")
+    )
     slot = call(
         functools.partial(slot_body, cap, pieces, own_rows, block_len),
         [(shaped((1, rows), jnp.int32), VMEM)],
@@ -530,7 +578,7 @@
     outs = call(
         functools.partial(forward_body, sides),
         split + [mixed, mixed, flat, flat, flat],
-        [(places, SMEM), (mixing, SMEM), (got_rows, HBM)] + sides_in,
+        [(group, SMEM), (mixing, SMEM), (got_rows, HBM)] + sides_in[:3],
         "forward",
         2 * product,
         [scratch_like((2, depth, hidden), BF16), stack_scratch, mixed_scratch, mixed_scratch]
@@ -545,7 +593,7 @@
         [(shaped((slots, part), BF16), HBM)]
         + split
         + [mixed, (shaped((weights, rows, hidden), BF16), HBM), (shaped((rows, cols), F32), VMEM)],
-        [(places, SMEM), (mixing, SMEM), (slot, VMEM), (gate_wide, VMEM), (got_grads, HBM)]
+        [(group, SMEM), (mixing, SMEM), (slot, VMEM), (gate_wide, VMEM), (got_grads, HBM)]
         + [(x, HBM) for x in (act, slope, hid)]
         + sides_in
         + [(x, HBM) for x in after],
@@ -601,7 +649,7 @@
         ).astype(F32)
         mix_grad = lax.psum(mix_part, "seq")
     gate_grad = (jnp.sum(inner, axis=1) * gate * (1.0 - gate)).reshape(selection.shape)
-    token_grad = sum_rows(cap, pieces, own_rows, places, chosen, returned)
+    token_grad = sum_rows(cap, pieces, own_rows, me, half, chosen, returned)
     return token_grad, factor_grad[None], mix_grad, gate_grad
 
 

time: 233 us -> 162 us (0.70)
  Pallas kernels: 108 us -> 46.7 us
  blocking collectives: 22.2 us -> 9.88 us
    pallas_call x10, Pallas kernels: 108 us -> 46.7 us  [call(): pl.pallas_call(body, out_shape=[x for x, _ in outs], in_specs=[place for...]
    ppermute x5 -> x7, waiting for transfers between devices: 41 us -> 17.8 us  [across(): return lax.ppermute(array, 'seq', pair)]
    all_gather x1 -> x0, blocking collectives: 22.2 us -> none  [shards(): chosen = lax.all_gather(selection[0], 'exp')]
    ppermute x14, waiting for transfers between devices: 11.2 us -> 23.2 us  [collect(): lax.ppermute(shares[k], 'exp', [(n, n ^ k) for n in range(peers)])]
    all_to_all x3, waiting for transfers between devices: 4.55 us -> 16.3 us  [to_peers(): lax.all_to_all(array, 'exp', split_axis=0, concat_axis=0, tiled=True)]
    all_to_all x0 -> x1, blocking collectives: none -> 9.88 us  [shards(): lax.all_to_all(wanted, 'exp', split_axis=0, concat_axis=0, tiled=True)]
    ppermute x14, starting transfers between devices: 10.5 us -> 14.5 us  [collect(): lax.ppermute(shares[k], 'exp', [(n, n ^ k) for n in range(peers)])]
    ppermute x5 -> x7, starting transfers between devices: 5.28 us -> 4.99 us  [across(): return lax.ppermute(array, 'seq', pair)]
  transfers between devices with their start and end apart: 22 -> 24, of which waited for: 10 -> 12; matrix products, arithmetic and copies ran while one was open for 2% -> 2% of each run, Pallas kernels for 25% -> 16%
where the time goes in v7:
time: 162 us; the launch traced here: 161 us
  waiting for transfers between devices  57.3 us (35%)
  Pallas kernels  46.7 us (29%)
  starting transfers between devices  38.3 us (24%)
  blocking collectives  9.88 us (6%)
  local copies, waits for them, and re-layouts  4.67 us (3%)
  other arithmetic  2.99 us (2%)
    pallas_call x10, Pallas kernels, call(): pl.pallas_call(body, out_shape=[x for x, _ in outs], in_specs=[place for...  46.7 us
    ppermute x14, waiting for transfers between devices, collect(): lax.ppermute(shares[k], 'exp', [(n, n ^ k) for n in range(peers)])  23.2 us
    all_to_all x3, starting transfers between devices, to_peers(): lax.all_to_all(array, 'exp', split_axis=0, concat_axis=0, tiled=True)  18.8 us
    ppermute x7, waiting for transfers between devices, across(): return lax.ppermute(array, 'seq', pair)  17.8 us
    all_to_all x3, waiting for transfers between devices, to_peers(): lax.all_to_all(array, 'exp', split_axis=0, concat_axis=0, tiled=True)  16.3 us
    ppermute x14, starting transfers between devices, collect(): lax.ppermute(shares[k], 'exp', [(n, n ^ k) for n in range(peers)])  14.5 us
    all_to_all x1, blocking collectives, shards(): lax.all_to_all(wanted, 'exp', split_axis=0, concat_axis=0, tiled=True)  9.88 us
    ppermute x7, starting transfers between devices, across(): return lax.ppermute(array, 'seq', pair)  4.99 us
  transfers between devices with their start and end apart: 24, of which 12 were waited for; matrix products, arithmetic and copies ran while one was open for 2% of the time, Pallas kernels for 16%

profile of v7, /device:TPU:13, one launch (start us, length us, event | category | flops | bytes accessed | tf_op | source)
XLA Modules:
  0.0 160.8 jit_solution(8020618249449400016)
XLA Ops:
  0.6 4.5 %spread_tokens.1 = (s32[16,128]{1,0:T(8,128)}, bf16[4,512,128]{2,1,0:T(8,128)(2,1)}, bf16[4,512,128]{2,1,0:T(8,128)(2,1)}, bf16[4,512,128]{2,1,0:T(8,128)(2,1)},...) custom-call(s32[1]{0:T(128)} %bitcast.me_ref, ...), custom_call_target="tpu_custom_call" | custom-call | bytes 5251588 | tf_op jit(solution)/shard_map/spread_tokens/pallas_call | solution.py:40
  12.8 3.1 %collective-permute-done.11.refs_4_ = bf16[128,512]{1,0:T(8,128)(2,1)S(1)} collective-permute-done((bf16[128,512]{1,0:T(8,128)(2,1)}, bf16[128,512]{1,0:T(8,128)(2,1)S(1)}, u32[]{:S(2)}, u32[]{:S(2)}) %collective-permute-start.11) | collective-permute-done | bytes 131104 | tf_op jit(solution)/shard_map/ppermute | solution.py:541
  16.4 9.9 %all_to_all.26 = s32[16,1,128]{2,1,0:T(1,128)} all-to-all(s32[16,1,128]{2,1,0:T(1,128)} %bitcast.25), channel_id=1, replica_groups=mesh['seq'=2,'exp'=16] {'exp'}, dimensions={0} | all-to-all | bytes 16384 | tf_op jit(solution)/shard_map/all_to_all | solution.py:531
  27.7 4.2 %pick_tokens.1 = bf16[1024,512]{1,0:T(8,128)(2,1)} custom-call(s32[1]{0:T(128)} %bitcast.me_ref, s32[16,128]{1,0:T(8,128)} %bitcast.22, bf16[4,512,128]{2,1,0:T(8,128)(2,1)} %copy-done.6, bf16[128,512]{1,0:T(8,128)(2,1)} %get-tuple-element.48.refs_1_, bf16[128,512]{1,0:T(8,128)(2,1)} %copy-done.8, bf16[128,512]{1,0:T(8,128)(2,1)} %copy-done.10, ...), custom_call_target="tpu_custom_call" | custom-call | flops 1073741824 | bytes 2629636 | tf_op jit(solution)/shard_map/pick_tokens/pallas_call | solution.py:40
  32.0 6.8 %all-to-all-start.2 = ((bf16[16,64,512]{2,1,0:T(8,128)(2,1)}), bf16[16,64,512]{2,1,0:T(8,128)(2,1)}, u32[]{:S(2)}, u32[]{:S(2)}) async-start(bf16[16,64,512]{2,1,0:T(8,128)(2,1)} %bitcast.20), calls=%async_computation.2 | async-start | bytes 2097152 | tf_op jit(solution)/shard_map/all_to_all | solution.py:535
  45.5 3.3 %collective-permute-done.2.refs_3_ = bf16[128,512]{1,0:T(8,128)(2,1)S(1)} collective-permute-done((bf16[128,512]{1,0:T(8,128)(2,1)}, bf16[128,512]{1,0:T(8,128)(2,1)S(1)}, u32[]{:S(2)}, u32[]{:S(2)}) %collective-permute-start.2) | collective-permute-done | bytes 131104 | tf_op jit(solution)/shard_map/ppermute | solution.py:541
  50.8 2.8 %collective-permute-done.3.refs_4_ = bf16[128,512]{1,0:T(8,128)(2,1)S(1)} collective-permute-done((bf16[128,512]{1,0:T(8,128)(2,1)}, bf16[128,512]{1,0:T(8,128)(2,1)S(1)}, u32[]{:S(2)}, u32[]{:S(2)}) %collective-permute-start.3) | collective-permute-done | bytes 131104 | tf_op jit(solution)/shard_map/ppermute | solution.py:541
  53.6 3.3 %collective-permute-start.7 = (bf16[128,512]{1,0:T(8,128)(2,1)}, bf16[128,512]{1,0:T(8,128)(2,1)S(1)}, u32[]{:S(2)}, u32[]{:S(2)}) collective-permute-start(bf16[128,512]{1,0:T(8,128)(2,1)} %get-tuple-element.46), channel_id=1, source_target_pairs={{0,7},{1,6},{2,5},{3,4},{4,3},{5,2},{6,1},{7,0},{8,15},{9,14},{10,... | collective-permute-start | bytes 393224 | tf_op jit(solution)/shard_map/ppermute | solution.py:541
  56.8 2.9 %collective-permute-done.4.refs_5_ = bf16[128,512]{1,0:T(8,128)(2,1)S(1)} collective-permute-done((bf16[128,512]{1,0:T(8,128)(2,1)}, bf16[128,512]{1,0:T(8,128)(2,1)S(1)}, u32[]{:S(2)}, u32[]{:S(2)}) %collective-permute-start.4) | collective-permute-done | bytes 131104 | tf_op jit(solution)/shard_map/ppermute | solution.py:541
  59.7 3.9 %collective-permute-done.5.refs_6_ = bf16[128,512]{1,0:T(8,128)(2,1)S(1)} collective-permute-done((bf16[128,512]{1,0:T(8,128)(2,1)}, bf16[128,512]{1,0:T(8,128)(2,1)S(1)}, u32[]{:S(2)}, u32[]{:S(2)}) %collective-permute-start.5) | collective-permute-done | bytes 131104 | tf_op jit(solution)/shard_map/ppermute | solution.py:541
  63.6 2.6 %collective-permute-done.6.refs_7_ = bf16[128,512]{1,0:T(8,128)(2,1)S(1)} collective-permute-done((bf16[128,512]{1,0:T(8,128)(2,1)}, bf16[128,512]{1,0:T(8,128)(2,1)S(1)}, u32[]{:S(2)}, u32[]{:S(2)}) %collective-permute-start.6) | collective-permute-done | bytes 131104 | tf_op jit(solution)/shard_map/ppermute | solution.py:541
  66.2 2.9 %collective-permute-done.7.refs_8_ = bf16[128,512]{1,0:T(8,128)(2,1)S(1)} collective-permute-done((bf16[128,512]{1,0:T(8,128)(2,1)}, bf16[128,512]{1,0:T(8,128)(2,1)S(1)}, u32[]{:S(2)}, u32[]{:S(2)}) %collective-permute-start.7) | collective-permute-done | bytes 131104 | tf_op jit(solution)/shard_map/ppermute | solution.py:541
  69.7 4.2 %pick_cotangent.1 = bf16[1024,512]{1,0:T(8,128)(2,1)} custom-call(s32[1]{0:T(128)} %bitcast.me_ref, s32[16,128]{1,0:T(8,128)} %bitcast.23, bf16[4,512,128]{2,1,0:T(8,128)(2,1)} %collective-permute-done.refs_0_.refs_2_, bf16[128,512]{1,0:T(8,128)(2,1)} %get-tuple-element.39.refs_1_, bf16[128,512]{1,0:T(8,128)(2,1)} %copy-done.9, bf16[128,512]{1,0:T(8,128)(2,1)} %copy-done.11, ...), custom_call_target="tpu_custom_call" | custom-call | flops 1073741824 | bytes 2629636 | tf_op jit(solution)/shard_map/pick_cotangent/pallas_call | solution.py:40
  74.0 5.5 %all-to-all-start.1 = ((bf16[16,64,512]{2,1,0:T(8,128)(2,1)}), bf16[16,64,512]{2,1,0:T(8,128)(2,1)}, u32[]{:S(2)}, u32[]{:S(2)}) async-start(bf16[16,64,512]{2,1,0:T(8,128)(2,1)} %bitcast.21), calls=%async_computation.1 | async-start | bytes 2097152 | tf_op jit(solution)/shard_map/all_to_all | solution.py:535
  80.5 6.1 %forward.1 = (bf16[512,512]{1,0:T(8,128)(2,1)}, bf16[512,512]{1,0:T(8,128)(2,1)}, f32[512,512]{1,0:T(8,128)}, f32[512,512]{1,0:T(8,128)}, f32[128,512]{1,0:T(8,1...) custom-call(s32[1]{0:T(128)} %bitcast.6.order_ref, f32[192]{0:T(256)} %reshape.59.mix_ref, ...), custom_call_target="tpu_custom_call" | custom-call | flops 1073741824 | bytes 7602948 | tf_op jit(solution)/shard_map/forward/pallas_call | solution.py:40
  89.3 3.7 %collective-permute-done.16.refs_3_ = bf16[4,512,128]{2,1,0:T(8,128)(2,1)} collective-permute-done((bf16[4,512,128]{2,1,0:T(8,128)(2,1)}, bf16[4,512,128]{2,1,0:T(8,128)(2,1)}, u32[]{:S(2)}, u32[]{:S(2)}) %collective-permute-start.16) | collective-permute-done | bytes 524320 | tf_op jit(solution)/shard_map/ppermute | solution.py:509
  93.0 11.7 %all-to-all-done.1 = bf16[16,64,512]{2,1,0:T(8,128)(2,1)} async-done(((bf16[16,64,512]{2,1,0:T(8,128)(2,1)}), bf16[16,64,512]{2,1,0:T(8,128)(2,1)}, u32[]{:S(2)}, u32[]{:S(2)}) %all-to-all-start.1) | async-done | bytes 1048608 | tf_op jit(solution)/shard_map/all_to_all | solution.py:535
  105.6 8.7 %backward.1 = (bf16[384,2048]{1,0:T(8,128)(2,1)}, bf16[512,512]{1,0:T(8,128)(2,1)}, bf16[512,512]{1,0:T(8,128)(2,1)}, f32[512,512]{1,0:T(8,128)}, bf16[3,128,512]{2,1,0:T(8,128)(2,1)}, /*index=5*/f32[128,128]{1,0:T(8,128)}) custom-call(s32[1]{0:T(128)} %bitcast.6.order_ref, f32[192]{0:T(256)} %reshape.59.mix_ref, s32[1,128]{1,0:T(1,128)} %row_slots.1.slot_ref, ...), custom_call_target="tpu_custom_call" | custom-call | flops 1610612736 | bytes 9700612 | tf_op jit(solution)/shard_map/backward/pallas_call | solution.py:40
  114.2 6.4 %all-to-all-start.3 = ((bf16[16,24,2048]{2,1,0:T(8,128)(2,1)}), bf16[16,24,2048]{2,1,0:T(8,128)(2,1)}, u32[]{:S(2)}, u32[]{:S(2)}) async-start(bf16[16,24,2048]{2,1,0:T(8,128)(2,1)} %bitcast.16), calls=%async_computation.3 | async-start | bytes 3145728 | tf_op jit(solution)/shard_map/all_to_all | solution.py:535
  122.2 3.9 %mix_partials.1 = f32[192,128]{1,0:T(8,128)} custom-call(f32[512,512]{1,0:T(8,128)} %get-tuple-element.66.yg_hbm, f32[512,512]{1,0:T(8,128)} %get-tuple-element.67.yu_hbm, f32[512,512]{1,0:T(8,128)} %get-tuple-element.68.yd_hbm, bf16[3,128,512]{2,1,0:T(8,128)(2,1)} %get-tuple-element.64.refs_2_.d_hbm), custom_call_target="tpu_custom_call" | custom-call | flops 6291456 | bytes 3637248 | tf_op jit(solution)/shard_map/mix_partials/pallas_call | solution.py:40
  129.0 14.1 %collective-permute-done.20 = f32[1,3,4,4,4]{4,3,2,1,0:T(4,128)S(1)} collective-permute-done((f32[1,3,4,4,4]{4,3,2,1,0:T(4,128)S(1)}, f32[1,3,4,4,4]{4,3,2,1,0:T(4,128)S(1)}, u32[]{:S(2)}, u32[]{:S(2)}) %collective-permute-start.20) | collective-permute-done | bytes 800 | tf_op jit(solution)/shard_map/ppermute | solution.py:509
  144.6 7.8 %factor_grad.1 = f32[3,4,512,128]{3,2,1,0:T(8,128)} custom-call(f32[192]{0:T(256)} %reshape.59.mix_ref, bf16[512,512]{1,0:T(8,128)(2,1)} %get-tuple-element.62.refs_0_, bf16[512,512]{1,0:T(8,128)(2,1)} %get-tuple-element.63.refs_1_, bf16[3,128,512]{2,1,0:T(8,128)(2,1)} %get-tuple-element.64.refs_2_.d_hbm, bf16[512,512]{1,0:T(8,128)(2,1)} %copy-done.1, ...), custom_call_target="tpu_custom_call" | custom-call | flops 1610612736 | bytes 6030080 | tf_op jit(solution)/shard_map/factor_grad/pallas_call | solution.py:40
  152.4 4.5 %all-to-all-done.3 = bf16[16,24,2048]{2,1,0:T(8,128)(2,1)} async-done(((bf16[16,24,2048]{2,1,0:T(8,128)(2,1)}), bf16[16,24,2048]{2,1,0:T(8,128)(2,1)}, u32[]{:S(2)}, u32[]{:S(2)}) %all-to-all-start.3) | async-done | bytes 1572896 | tf_op jit(solution)/shard_map/all_to_all | solution.py:535
  157.0 3.7 %sum_rows.1 = bf16[128,4096]{1,0:T(8,128)(2,1)} custom-call(s32[1]{0:T(128)} %bitcast.me_ref, s32[16,128]{1,0:T(8,128)} %bitcast.24, bf16[384,2048]{1,0:T(8,128)(2,1)} %bitcast.12.returned_ref), custom_call_target="tpu_custom_call" | custom-call | flops 402653184 | bytes 2629636 | tf_op jit(solution)/shard_map/sum_rows/pallas_call | solution.py:40
  (89 shorter events, 29.3 us)
Async XLA Ops:
  5.1 21.2 %collective-permute-start.8 = (bf16[4,512,128]{2,1,0:T(8,128)(2,1)}, bf16[4,512,128]{2,1,0:T(8,128)(2,1)S(1)}, u32[]{:S(2)}, u32[]{:S(2)}) collective-permute-start(bf16[4,512,128]{2,1,0:T(8,128)(2,1)} %get-tuple-element.47), channel_id=1, source_target_pairs={{0,16},{16,0},{1,17},{17,1},{2,18},{18,2},{3,19},{19,3},{4,20},{20... | collective-permute-start | bytes 1572872 | tf_op jit(solution)/shard_map/ppermute | solution.py:509
  6.4 2.8 %collective-permute-start.9 = (bf16[128,512]{1,0:T(8,128)(2,1)}, bf16[128,512]{1,0:T(8,128)(2,1)S(1)}, u32[]{:S(2)}, u32[]{:S(2)}) collective-permute-start(bf16[128,512]{1,0:T(8,128)(2,1)} %get-tuple-element.49), channel_id=1, source_target_pairs={{0,1},{1,0},{2,3},{3,2},{4,5},{5,4},{6,7},{7,6},{8,9},{9,8},{10,11... | collective-permute-start | bytes 393224 | tf_op jit(solution)/shard_map/ppermute | solution.py:541
  7.3 5.3 %collective-permute-start.10 = (bf16[128,512]{1,0:T(8,128)(2,1)}, bf16[128,512]{1,0:T(8,128)(2,1)S(1)}, u32[]{:S(2)}, u32[]{:S(2)}) collective-permute-start(bf16[128,512]{1,0:T(8,128)(2,1)} %get-tuple-element.50), channel_id=1, source_target_pairs={{0,2},{1,3},{2,0},{3,1},{4,6},{5,7},{6,4},{7,5},{8,10},{9,11},{10,... | collective-permute-start | bytes 393224 | tf_op jit(solution)/shard_map/ppermute | solution.py:541
  7.6 8.3 %collective-permute-start.11 = (bf16[128,512]{1,0:T(8,128)(2,1)}, bf16[128,512]{1,0:T(8,128)(2,1)S(1)}, u32[]{:S(2)}, u32[]{:S(2)}) collective-permute-start(bf16[128,512]{1,0:T(8,128)(2,1)} %get-tuple-element.51), channel_id=1, source_target_pairs={{0,3},{1,2},{2,1},{3,0},{4,7},{5,6},{6,5},{7,4},{8,11},{9,10},{10,... | collective-permute-start | bytes 393224 | tf_op jit(solution)/shard_map/ppermute | solution.py:541
  9.0 17.3 %collective-permute-start.12 = (bf16[128,512]{1,0:T(8,128)(2,1)}, bf16[128,512]{1,0:T(8,128)(2,1)S(1)}, u32[]{:S(2)}, u32[]{:S(2)}) collective-permute-start(bf16[128,512]{1,0:T(8,128)(2,1)} %get-tuple-element.52), channel_id=1, source_target_pairs={{0,4},{1,5},{2,6},{3,7},{4,0},{5,1},{6,2},{7,3},{8,12},{9,13},{10,... | collective-permute-start | bytes 393224 | tf_op jit(solution)/shard_map/ppermute | solution.py:541
  9.1 17.1 %collective-permute-start.13 = (bf16[128,512]{1,0:T(8,128)(2,1)}, bf16[128,512]{1,0:T(8,128)(2,1)S(1)}, u32[]{:S(2)}, u32[]{:S(2)}) collective-permute-start(bf16[128,512]{1,0:T(8,128)(2,1)} %get-tuple-element.53), channel_id=1, source_target_pairs={{0,5},{1,4},{2,7},{3,6},{4,1},{5,0},{6,3},{7,2},{8,13},{9,12},{10,... | collective-permute-start | bytes 393224 | tf_op jit(solution)/shard_map/ppermute | solution.py:541
  12.7 13.6 %collective-permute-start.14 = (bf16[128,512]{1,0:T(8,128)(2,1)}, bf16[128,512]{1,0:T(8,128)(2,1)S(1)}, u32[]{:S(2)}, u32[]{:S(2)}) collective-permute-start(bf16[128,512]{1,0:T(8,128)(2,1)} %get-tuple-element.54), channel_id=1, source_target_pairs={{0,6},{1,7},{2,4},{3,5},{4,2},{5,3},{6,0},{7,1},{8,14},{9,15},{10,... | collective-permute-start | bytes 393224 | tf_op jit(solution)/shard_map/ppermute | solution.py:541
  15.9 10.4 %collective-permute-start.15 = (bf16[128,512]{1,0:T(8,128)(2,1)}, bf16[128,512]{1,0:T(8,128)(2,1)S(1)}, u32[]{:S(2)}, u32[]{:S(2)}) collective-permute-start(bf16[128,512]{1,0:T(8,128)(2,1)} %get-tuple-element.55), channel_id=1, source_target_pairs={{0,7},{1,6},{2,5},{3,4},{4,3},{5,2},{6,1},{7,0},{8,15},{9,14},{10,... | collective-permute-start | bytes 393224 | tf_op jit(solution)/shard_map/ppermute | solution.py:541
  32.0 42.0 %all-to-all-start.2 = ((bf16[16,64,512]{2,1,0:T(8,128)(2,1)}), bf16[16,64,512]{2,1,0:T(8,128)(2,1)}, u32[]{:S(2)}, u32[]{:S(2)}) async-start(bf16[16,64,512]{2,1,0:T(8,128)(2,1)} %bitcast.20), calls=%async_computation.2 | async-start | bytes 2097152 | tf_op jit(solution)/shard_map/all_to_all | solution.py:535
  38.8 30.3 %collective-permute-start = (bf16[4,512,128]{2,1,0:T(8,128)(2,1)S(1)}, bf16[4,512,128]{2,1,0:T(8,128)(2,1)}, u32[]{:S(2)}, u32[]{:S(2)}) collective-permute-start(bf16[4,512,128]{2,1,0:T(8,128)(2,1)S(1)} %copy-done.7), channel_id=1, source_target_pairs={{0,16},{16,0},{1,17},{17,1},{2,18},{18,2},{3,19},{19,3},{4,20},{20... | collective-permute-start | bytes 1572872 | tf_op jit(solution)/shard_map/ppermute | solution.py:509
  41.3 2.7 %collective-permute-start.1 = (bf16[128,512]{1,0:T(8,128)(2,1)}, bf16[128,512]{1,0:T(8,128)(2,1)S(1)}, u32[]{:S(2)}, u32[]{:S(2)}) collective-permute-start(bf16[128,512]{1,0:T(8,128)(2,1)} %get-tuple-element.40), channel_id=1, source_target_pairs={{0,1},{1,0},{2,3},{3,2},{4,5},{5,4},{6,7},{7,6},{8,9},{9,8},{10,11... | collective-permute-start | bytes 393224 | tf_op jit(solution)/shard_map/ppermute | solution.py:541
  42.0 6.8 %collective-permute-start.2 = (bf16[128,512]{1,0:T(8,128)(2,1)}, bf16[128,512]{1,0:T(8,128)(2,1)S(1)}, u32[]{:S(2)}, u32[]{:S(2)}) collective-permute-start(bf16[128,512]{1,0:T(8,128)(2,1)} %get-tuple-element.41), channel_id=1, source_target_pairs={{0,2},{1,3},{2,0},{3,1},{4,6},{5,7},{6,4},{7,5},{8,10},{9,11},{10,... | collective-permute-start | bytes 393224 | tf_op jit(solution)/shard_map/ppermute | solution.py:541
  42.3 11.3 %collective-permute-start.3 = (bf16[128,512]{1,0:T(8,128)(2,1)}, bf16[128,512]{1,0:T(8,128)(2,1)S(1)}, u32[]{:S(2)}, u32[]{:S(2)}) collective-permute-start(bf16[128,512]{1,0:T(8,128)(2,1)} %get-tuple-element.42), channel_id=1, source_target_pairs={{0,3},{1,2},{2,1},{3,0},{4,7},{5,6},{6,5},{7,4},{8,11},{9,10},{10,... | collective-permute-start | bytes 393224 | tf_op jit(solution)/shard_map/ppermute | solution.py:541
  43.7 16.0 %collective-permute-start.4 = (bf16[128,512]{1,0:T(8,128)(2,1)}, bf16[128,512]{1,0:T(8,128)(2,1)S(1)}, u32[]{:S(2)}, u32[]{:S(2)}) collective-permute-start(bf16[128,512]{1,0:T(8,128)(2,1)} %get-tuple-element.43), channel_id=1, source_target_pairs={{0,4},{1,5},{2,6},{3,7},{4,0},{5,1},{6,2},{7,3},{8,12},{9,13},{10,... | collective-permute-start | bytes 393224 | tf_op jit(solution)/shard_map/ppermute | solution.py:541
  44.0 19.6 %collective-permute-start.5 = (bf16[128,512]{1,0:T(8,128)(2,1)}, bf16[128,512]{1,0:T(8,128)(2,1)S(1)}, u32[]{:S(2)}, u32[]{:S(2)}) collective-permute-start(bf16[128,512]{1,0:T(8,128)(2,1)} %get-tuple-element.44), channel_id=1, source_target_pairs={{0,5},{1,4},{2,7},{3,6},{4,1},{5,0},{6,3},{7,2},{8,13},{9,12},{10,... | collective-permute-start | bytes 393224 | tf_op jit(solution)/shard_map/ppermute | solution.py:541
  48.8 17.4 %collective-permute-start.6 = (bf16[128,512]{1,0:T(8,128)(2,1)}, bf16[128,512]{1,0:T(8,128)(2,1)S(1)}, u32[]{:S(2)}, u32[]{:S(2)}) collective-permute-start(bf16[128,512]{1,0:T(8,128)(2,1)} %get-tuple-element.45), channel_id=1, source_target_pairs={{0,6},{1,7},{2,4},{3,5},{4,2},{5,3},{6,0},{7,1},{8,14},{9,15},{10,... | collective-permute-start | bytes 393224 | tf_op jit(solution)/shard_map/ppermute | solution.py:541
  53.6 15.5 %collective-permute-start.7 = (bf16[128,512]{1,0:T(8,128)(2,1)}, bf16[128,512]{1,0:T(8,128)(2,1)S(1)}, u32[]{:S(2)}, u32[]{:S(2)}) collective-permute-start(bf16[128,512]{1,0:T(8,128)(2,1)} %get-tuple-element.46), channel_id=1, source_target_pairs={{0,7},{1,6},{2,5},{3,4},{4,3},{5,2},{6,1},{7,0},{8,15},{9,14},{10,... | collective-permute-start | bytes 393224 | tf_op jit(solution)/shard_map/ppermute | solution.py:541
  74.0 30.7 %all-to-all-start.1 = ((bf16[16,64,512]{2,1,0:T(8,128)(2,1)}), bf16[16,64,512]{2,1,0:T(8,128)(2,1)}, u32[]{:S(2)}, u32[]{:S(2)}) async-start(bf16[16,64,512]{2,1,0:T(8,128)(2,1)} %bitcast.21), calls=%async_computation.1 | async-start | bytes 2097152 | tf_op jit(solution)/shard_map/all_to_all | solution.py:535
  79.5 13.5 %collective-permute-start.16 = (bf16[4,512,128]{2,1,0:T(8,128)(2,1)}, bf16[4,512,128]{2,1,0:T(8,128)(2,1)}, u32[]{:S(2)}, u32[]{:S(2)}) collective-permute-start(bf16[4,512,128]{2,1,0:T(8,128)(2,1)} %get-tuple-element.59), channel_id=1, source_target_pairs={{0,16},{16,0},{1,17},{17,1},{2,18},{18,2},{3,19},{19,3},{4,20},{20... | collective-permute-start | bytes 1572872 | tf_op jit(solution)/shard_map/ppermute | solution.py:509
  86.6 18.1 %collective-permute-start.17 = (bf16[512,512]{1,0:T(8,128)(2,1)}, bf16[512,512]{1,0:T(8,128)(2,1)S(1)}, u32[]{:S(2)}, u32[]{:S(2)}) collective-permute-start(bf16[512,512]{1,0:T(8,128)(2,1)} %get-tuple-element.60), channel_id=1, source_target_pairs={{0,16},{16,0},{1,17},{17,1},{2,18},{18,2},{3,19},{19,3},{4,20},{20... | collective-permute-start | bytes 1572872 | tf_op jit(solution)/shard_map/ppermute | solution.py:509
  114.2 42.7 %all-to-all-start.3 = ((bf16[16,24,2048]{2,1,0:T(8,128)(2,1)}), bf16[16,24,2048]{2,1,0:T(8,128)(2,1)}, u32[]{:S(2)}, u32[]{:S(2)}) async-start(bf16[16,24,2048]{2,1,0:T(8,128)(2,1)} %bitcast.16), calls=%async_computation.3 | async-start | bytes 3145728 | tf_op jit(solution)/shard_map/all_to_all | solution.py:535
  120.7 23.1 %collective-permute-start.18 = (bf16[512,512]{1,0:T(8,128)(2,1)}, bf16[512,512]{1,0:T(8,128)(2,1)S(1)}, u32[]{:S(2)}, u32[]{:S(2)}) collective-permute-start(bf16[512,512]{1,0:T(8,128)(2,1)} %get-tuple-element.65), channel_id=1, source_target_pairs={{0,16},{16,0},{1,17},{17,1},{2,18},{18,2},{3,19},{19,3},{4,20},{20... | collective-permute-start | bytes 1572872 | tf_op jit(solution)/shard_map/ppermute | solution.py:509
  121.0 22.8 %collective-permute-start.19 = (bf16[3,128,512]{2,1,0:T(8,128)(2,1)S(1)}, bf16[3,128,512]{2,1,0:T(8,128)(2,1)}, u32[]{:S(2)}, u32[]{:S(2)}) collective-permute-start(bf16[3,128,512]{2,1,0:T(8,128)(2,1)S(1)} %copy-done), channel_id=1, source_target_pairs={{0,16},{16,0},{1,17},{17,1},{2,18},{18,2},{3,19},{19,3},{4,20},{20... | collective-permute-start | bytes 1179656 | tf_op jit(solution)/shard_map/ppermute | solution.py:509
  127.4 15.7 %collective-permute-start.20 = (f32[1,3,4,4,4]{4,3,2,1,0:T(4,128)S(1)}, f32[1,3,4,4,4]{4,3,2,1,0:T(4,128)S(1)}, u32[]{:S(2)}, u32[]{:S(2)}) collective-permute-start(f32[1,3,4,4,4]{4,3,2,1,0:T(4,128)S(1)} %reshape.66), channel_id=1, source_target_pairs={{0,16},{16,0},{1,17},{17,1},{2,18},{18,2},{3,19},{19,3},{4,20},{20... | collective-permute-start | bytes 2312 | tf_op jit(solution)/shard_map/ppermute | solution.py:509
  (22 other events, 162.9 us)

commit v8 on v7

--- a/solution.py
+++ b/solution.py
@@ -72,60 +72,74 @@
     return [begin(source, target, sems.at[n]) for n, (source, target) in enumerate(pairs)]
 
 
-def spread_columns(me, source, half, direct, name, more=(), selection=None, cuts=None):
-    own_rows, width = source.shape
+def spread_columns(me, sources, half, direct, name):
+    own_rows, width = sources[0].shape
+    count = len(sources)
     part = width // half
-    count = half if direct else 1
-    ahead = [] if cuts is None else [(selection, VMEM), (cuts, HBM)]
-
-    def body(me_ref, source_ref, *refs):
-        held_ref, sems = refs[-2:]
-        refs = refs[:-2]
-        load = begin(source_ref, held_ref.at[0], sems.at[0])
-        if ahead:
-            chosen_ref, cuts_ref, refs = refs[0], refs[1], refs[2:]
-            wanted_ref, pieces, refs = refs[0], refs[1 : 1 + cuts.shape[0]], refs[1 + cuts.shape[0] :]
-        outs, scratch = refs[:count], refs[count:]
+    tall = count * own_rows
+
+    def body(me_ref, *refs):
+        ins, outs = refs[:count], refs[count : -3]
+        held_ref, in_sem, out_sem = refs[-3:]
+        loads = [begin(ref, held_ref.at[n], in_sem.at[n]) for n, ref in enumerate(ins)]
+        low = me_ref[0] & (half - 1)
         copies = []
-        if ahead:
-            cut_ref, cut_sems = scratch
-            cuts_in = [
-                begin(cuts_ref.at[m], cut_ref.at[m], cut_sems.at[0, m])
-                for m in range(cuts.shape[0])
-            ]
-            row = jnp.concatenate([chosen_ref[b : b + 1, :] for b in range(chosen_ref.shape[0])], axis=1)
-            wanted_ref[...] = jnp.broadcast_to(row, wanted_ref.shape)
-        load.wait()
-        low = me_ref[0] & (half - 1)
-        for k in range(half):
-            share = low ^ k if direct else k
-            at = held_ref.at[0, :, pl.ds(pl.multiple_of(share * part, part), part)]
-            out = outs[k] if direct else outs[0].at[k * own_rows : (k + 1) * own_rows]
-            copies.append(begin(at, out, sems.at[1 + k]))
-        if ahead:
-            for m, copy in enumerate(cuts_in):
-                copy.wait()
-                copies.append(begin(cut_ref.at[m], pieces[m], cut_sems.at[1, m]))
+        for n, load in enumerate(loads):
+            load.wait()
+            for k in range(half):
+                share = low ^ k if direct else k
+                at = held_ref.at[n, :, pl.ds(pl.multiple_of(share * part, part), part)]
+                out, first = (outs[k], 0) if direct else (outs[0], k * tall)
+                rows = pl.ds(first + n * own_rows, own_rows)
+                copies.append(begin(at, out.at[rows], out_sem.at[n, k]))
         wait_all(copies)
 
     if direct:
-        outs = [(shaped((own_rows, part), BF16), HBM)] * half
+        outs = [(shaped((tall, part), BF16), HBM)] * half
     else:
-        outs = [(shaped((half * own_rows, part), BF16), HBM)]
-    scratch = []
-    if ahead:
-        wanted = shaped((more[0], selection.size), jnp.int32)
-        outs = [(wanted, VMEM)] + [(shaped(cuts.shape[1:], BF16), HBM)] * cuts.shape[0] + outs
-        scratch = [scratch_like(cuts.shape, BF16), pltpu.SemaphoreType.DMA((2, cuts.shape[0]))]
-    scratch += [scratch_like((1, own_rows, width), BF16), pltpu.SemaphoreType.DMA((1 + half,))]
-    return call(body, outs, [(me, SMEM), (source, HBM)] + ahead, name, 0, scratch)
-
-
-def pick_rows(me, half, chosen, shares, after, name):
+        outs = [(shaped((half * tall, part), BF16), HBM)]
+    scratch = [
+        scratch_like((count, own_rows, width), BF16),
+        pltpu.SemaphoreType.DMA((count,)),
+        pltpu.SemaphoreType.DMA((count, half)),
+    ]
+    return call(body, outs, [(me, SMEM)] + [(x, HBM) for x in sources], name, 0, scratch)
+
+
+def share_selection(chosen, peers):
+    def body(chosen_ref, out_ref):
+        blocks = [chosen_ref[b : b + 1, :] for b in range(chosen_ref.shape[0])]
+        out_ref[...] = jnp.broadcast_to(jnp.concatenate(blocks, axis=1), out_ref.shape)
+
+    out = (shaped((peers, chosen.size), jnp.int32), VMEM)
+    return call(body, [out], [(chosen, VMEM)], "share_selection", 0)[0]
+
+
+def cut_factors(factors):
+    weights = factors.shape[0]
+
+    def body(factors_ref, *refs):
+        outs, (held_ref, sems) = refs[:weights], refs[weights:]
+        loads = [
+            begin(factors_ref.at[m], held_ref.at[m], sems.at[0, m]) for m in range(weights)
+        ]
+        copies = []
+        for m, load in enumerate(loads):
+            load.wait()
+            copies.append(begin(held_ref.at[m], outs[m], sems.at[1, m]))
+        wait_all(copies)
+
+    outs = [(shaped(factors.shape[1:], BF16), HBM)] * weights
+    scratch = [scratch_like(factors.shape, BF16), pltpu.SemaphoreType.DMA((2, weights))]
+    return call(body, outs, [(factors, HBM)], "cut_factors", 0, scratch)
+
+
+def pick_rows(me, half, own_rows, which, chosen, shares, after, name):
     peers, total = chosen.shape
     picks = total * half // peers
     part = shares[0].shape[1]
-    block = sum(x.shape[0] for x in shares)
+    block = half * own_rows
+    tall = sum(x.shape[0] for x in shares) // half
     batch = min(peers, 8)
 
     def body(me_ref, chosen_ref, *refs):
@@ -135,11 +149,12 @@
             refs[len(shares) :],
         )
         loads = []
-        for k, share in enumerate(parts):
-            size = share.shape[0]
-            place = (me_ref[0] & (half - 1)) ^ k if len(parts) > 1 else 0
-            start = pl.multiple_of(place * size, 16)
-            loads.append(begin(share, rows_ref.at[pl.ds(start, size)], in_sem.at[k]))
+        for k in range(half):
+            place = (me_ref[0] & (half - 1)) ^ k if len(parts) > 1 else k
+            share, first = (parts[k], 0) if len(parts) > 1 else (parts[0], k * tall)
+            first += which * own_rows
+            target = rows_ref.at[pl.ds(pl.multiple_of(place * own_rows, own_rows), own_rows)]
+            loads.append(begin(share.at[first : first + own_rows], target, in_sem.at[k]))
         block_at = lax.shift_right_logical(me_ref[0], half.bit_length() - 1)
         same = iota((picks, total), 0) + block_at * picks == iota((picks, total), 1)
         stores = []
@@ -167,7 +182,7 @@
             scratch_like((block, part), BF16),
             scratch_like((2, batch * picks, block), BF16),
             scratch_like((peers * picks, part), BF16),
-            pltpu.SemaphoreType.DMA((len(shares),)),
+            pltpu.SemaphoreType.DMA((half,)),
             pltpu.SemaphoreType.DMA((peers // batch,)),
         ],
     )[0]
@@ -186,18 +201,12 @@
     slot_ref[...] = owner * (cap * pieces) + iota((1, rows), 1) - earlier
 
 
-def sum_rows(cap, pieces, own_rows, me, half, chosen, returned):
-    slots, part = returned.shape
+def place_rows(cap, pieces, own_rows, me, half, chosen):
     peers, total = chosen.shape
     picks = total * half // peers
     group = cap * pieces
-    columns = chunks_of(part)
-
-    def body(me_ref, chosen_ref, returned_ref, out_ref, got_ref, pick_ref, sum_ref, in_sem, out_sem):
-        loads = [
-            begin(returned_ref.at[:, at], got_ref.at[:, at], in_sem.at[n])
-            for n, at in enumerate(columns)
-        ]
+
+    def body(me_ref, chosen_ref, out_ref, pick_ref):
         low = me_ref[0] & (half - 1)
         block_at = lax.shift_right_logical(me_ref[0], half.bit_length() - 1)
         lane = iota((peers, total), 1) - block_at * picks
@@ -217,11 +226,34 @@
             pick_ref[e * group : (e + 1) * group] = (
                 column == iota((group, pieces * own_rows), 1) + 1
             ).astype(F32)
-        pick = pick_ref[...].astype(BF16)
+        out_ref[...] = jnp.transpose(pick_ref[...]).astype(BF16)
+
+    return call(
+        body,
+        [(shaped((pieces * own_rows, peers * group), BF16), VMEM)],
+        [(me, SMEM), (chosen, VMEM)],
+        "place_rows",
+        1 << 20,
+        [scratch_like((peers * group, pieces * own_rows), F32)],
+    )[0]
+
+
+def sum_rows(pieces, placed, returned):
+    slots, part = returned.shape
+    own_rows = placed.shape[0] // pieces
+    columns = chunks_of(part)
+
+    def body(placed_hbm, returned_ref, out_ref, place_ref, got_ref, sum_ref, in_sem, out_sem):
+        first = begin(placed_hbm, place_ref, in_sem.at[len(columns)])
+        loads = [
+            begin(returned_ref.at[:, at], got_ref.at[:, at], in_sem.at[n])
+            for n, at in enumerate(columns)
+        ]
+        first.wait()
         stores = []
         for n, at in enumerate(columns):
             loads[n].wait()
-            summed = dot_tn(pick, got_ref[:, at]).astype(BF16)
+            summed = dot(place_ref[...], got_ref[:, at]).astype(BF16)
             for j in range(pieces):
                 wide = slice(j * part + at.start, j * part + at.stop)
                 sum_ref[:, wide] = summed[j * own_rows : (j + 1) * own_rows]
@@ -233,14 +265,14 @@
     return call(
         body,
         [(shaped((own_rows, part * pieces), BF16), HBM)],
-        [(me, SMEM), (chosen, VMEM), (returned, HBM)],
+        [(placed, HBM), (returned, HBM)],
         "sum_rows",
         2 * slots * pieces * own_rows * part,
         [
+            scratch_like(placed.shape, BF16),
             scratch_like((slots, part), BF16),
-            scratch_like((slots, pieces * own_rows), F32),
             scratch_like((own_rows, part * pieces), BF16),
-            pltpu.SemaphoreType.DMA((len(columns),)),
+            pltpu.SemaphoreType.DMA((len(columns) + 1,)),
             pltpu.SemaphoreType.DMA((len(columns), pieces)),
         ],
     )[0]
@@ -379,7 +411,7 @@
 
 
 def backward_body(
-    cap, pieces, sides, after, order_ref, mix_ref, slot_ref, gate_ref, got_hbm, act_hbm, slope_hbm, hid_hbm,
+    cap, pieces, sides, after, order_ref, mix_ref, slot_ref, score_ref, got_hbm, act_hbm, slope_hbm, hid_hbm,
     *refs,
 ):
     held = 4 if sides > 1 else 1
@@ -388,7 +420,7 @@
     y_hbm, d_hbm, inner_ref = refs[:3]
     (
         side_ref, x_ref, y_ref, d_ref, act_ref, slope_ref, hid_ref, zg_ref, zu_ref, grad_ref,
-        back_ref, got_sem, side_sem, in_sem, out_sem,
+        back_ref, gate_ref, got_sem, side_sem, in_sem, out_sem,
     ) = refs[3:]
     loads = load_rows(got_hbm, x_ref, got_sem)
     down_in = load_factor(order_ref, parts, 2, side_ref.at[2], side_sem.at[2])
@@ -401,6 +433,11 @@
     sides_in = [
         load_factor(order_ref, parts, m, side_ref.at[m], side_sem.at[m]) for m in range(2)
     ]
+    score = jnp.concatenate([score_ref[b : b + 1, :] for b in range(score_ref.shape[0])], axis=1)
+    rows = score.shape[1]
+    same = iota((rows, rows), 0) == iota((rows, rows), 1)
+    score = jnp.sum(jnp.where(same, score.astype(F32), 0.0), axis=1, keepdims=True)
+    gate_ref[...] = jnp.broadcast_to(jax.nn.sigmoid(score / 64.0), gate_ref.shape)
     wait_all(loads)
     stores = store_parts(order_ref, x_ref, x_outs, out_sem)
     wait_all(down_in)
@@ -515,10 +552,9 @@
     halves = [list(range(h, h + half)) for h in range(0, peers, half)]
     near = [k for k in range(1, half) if k >= 4] + [k for k in range(1, half) if k < 4]
 
-    outs = spread_columns(
-        me, tokens, half, direct, "spread_tokens", (peers,), selection[0], factors[0]
-    )
-    wanted, cuts, token_shares = outs[0], outs[1 : 1 + weights], outs[1 + weights :]
+    shares = spread_columns(me, [tokens, cotangent], half, direct, "spread_columns")
+    cuts = cut_factors(factors[0])
+    wanted = share_selection(selection[0], peers)
     if swap:
         cuts = [across(x) for x in cuts]
         factor_parts = [factors[0]] + cuts
@@ -541,19 +577,17 @@
                 k: lax.ppermute(shares[k], "exp", [(n, n ^ k) for n in range(peers)]) for k in near
             }
             return [shares[0]] + [moved[k] for k in range(1, half)]
-        array = shares[0].reshape(half, own_rows, -1)
+        array = shares[0].reshape(half, -1, shares[0].shape[1])
         array = lax.all_to_all(
             array, "exp", split_axis=0, concat_axis=0, axis_index_groups=halves, tiled=True
         )
-        return [array.reshape(half * own_rows, -1)]
-
-    got_rows = to_peers(
-        pick_rows(me, half, chosen, collect(token_shares), cuts[:1], "pick_tokens")
-    )
-    grad_shares = spread_columns(me, cotangent, half, direct, "spread_cotangent")
-    got_grads = to_peers(
-        pick_rows(me, half, chosen, collect(grad_shares), cuts[1:2], "pick_cotangent")
-    )
+        return [array.reshape(shares[0].shape)]
+
+    shares = collect(shares)
+    pick = functools.partial(pick_rows, me, half, own_rows)
+    got_rows = to_peers(pick(0, chosen, shares, cuts[:1], "pick_tokens"))
+    got_grads = to_peers(pick(1, chosen, shares, cuts[1:2], "pick_cotangent"))
+    placed = place_rows(cap, pieces, own_rows, me, half, chosen)
     slot = call(
         functools.partial(slot_body, cap, pieces, own_rows, block_len),
         [(shaped((1, rows), jnp.int32), VMEM)],
@@ -563,7 +597,6 @@
     )[0]
 
     gate = jax.nn.sigmoid(scores[0].reshape(-1).astype(F32) / 64.0)
-    gate_wide = jnp.broadcast_to(gate[:, None], (rows, cols))
 
     product = 2 * stacked * depth * hidden
     split = [(shaped((stacked, depth // sides), BF16), HBM)] * sides
@@ -593,7 +626,7 @@
         [(shaped((slots, part), BF16), HBM)]
         + split
         + [mixed, (shaped((weights, rows, hidden), BF16), HBM), (shaped((rows, cols), F32), VMEM)],
-        [(group, SMEM), (mixing, SMEM), (slot, VMEM), (gate_wide, VMEM), (got_grads, HBM)]
+        [(group, SMEM), (mixing, SMEM), (slot, VMEM), (scores[0], VMEM), (got_grads, HBM)]
         + [(x, HBM) for x in (act, slope, hid)]
         + sides_in
         + [(x, HBM) for x in after],
@@ -603,7 +636,7 @@
         + [scratch_like((weights, rows, hidden), BF16)]
         + [flat_scratch] * 3
         + [low_scratch] * 2
-        + [stack_scratch, back_scratch]
+        + [stack_scratch, back_scratch, scratch_like((rows, cols), F32)]
         + [dma((pieces_in,)), dma((weights, sides, count)), dma((3,)), dma((4 + steps,))],
     )
     back, g_parts, (y_down, d_own, inner) = outs[0], outs[1 : 1 + sides], outs[1 + sides :]
@@ -649,7 +682,7 @@
         ).astype(F32)
         mix_grad = lax.psum(mix_part, "seq")
     gate_grad = (jnp.sum(inner, axis=1) * gate * (1.0 - gate)).reshape(selection.shape)
-    token_grad = sum_rows(cap, pieces, own_rows, me, half, chosen, returned)
+    token_grad = sum_rows(pieces, placed, returned)
     return token_grad, factor_grad[None], mix_grad, gate_grad
 
 

time: 162 us -> 159 us (0.981)
  starting transfers between devices: 38.3 us -> 27.9 us
  blocking collectives: 9.88 us -> 15.9 us
  waiting for transfers between devices: 57.3 us -> 59.1 us
    ppermute x14 -> x7, waiting for transfers between devices: 23.2 us -> 6.9 us  [collect(): lax.ppermute(shares[k], 'exp', [(n, n ^ k) for n in range(peers)])]
    ppermute x7, waiting for transfers between devices: 17.8 us -> 29.2 us  [across(): return lax.ppermute(array, 'seq', pair)]
    ppermute x14 -> x7, starting transfers between devices: 14.5 us -> 4.6 us  [collect(): lax.ppermute(shares[k], 'exp', [(n, n ^ k) for n in range(peers)])]
    all_to_all x3, waiting for transfers between devices: 16.3 us -> 23 us  [to_peers(): lax.all_to_all(array, 'exp', split_axis=0, concat_axis=0, tiled=True)]
    all_to_all x1, blocking collectives: 9.88 us -> 15.9 us  [shards(): lax.all_to_all(wanted, 'exp', split_axis=0, concat_axis=0, tiled=True)]
    pallas_call x10 -> x12, Pallas kernels: 46.7 us -> 47.2 us  [call(): pl.pallas_call(body, out_shape=[x for x, _ in outs], in_specs=[place for...]
  transfers between devices with their start and end apart: 24 -> 17, of which waited for: 12 -> 8; matrix products, arithmetic and copies ran while one was open for 2% -> 2% of each run, Pallas kernels for 16% -> 18%
where the time goes in v8:
time: 159 us; the launch traced here: 158 us
  waiting for transfers between devices  59.1 us (37%)
  Pallas kernels  47.2 us (30%)
  starting transfers between devices  27.9 us (18%)
  blocking collectives  15.9 us (10%)
  local copies, waits for them, and re-layouts  4.08 us (3%)
  other arithmetic  2.99 us (2%)
    pallas_call x12, Pallas kernels, call(): pl.pallas_call(body, out_shape=[x for x, _ in outs], in_specs=[place for...  47.2 us
    ppermute x7, waiting for transfers between devices, across(): return lax.ppermute(array, 'seq', pair)  29.2 us
    all_to_all x3, waiting for transfers between devices, to_peers(): lax.all_to_all(array, 'exp', split_axis=0, concat_axis=0, tiled=True)  23 us
    all_to_all x3, starting transfers between devices, to_peers(): lax.all_to_all(array, 'exp', split_axis=0, concat_axis=0, tiled=True)  18.3 us
    all_to_all x1, blocking collectives, shards(): lax.all_to_all(wanted, 'exp', split_axis=0, concat_axis=0, tiled=True)  15.9 us
    ppermute x7, waiting for transfers between devices, collect(): lax.ppermute(shares[k], 'exp', [(n, n ^ k) for n in range(peers)])  6.9 us
    ppermute x7, starting transfers between devices, across(): return lax.ppermute(array, 'seq', pair)  5 us
    ppermute x7, starting transfers between devices, collect(): lax.ppermute(shares[k], 'exp', [(n, n ^ k) for n in range(peers)])  4.6 us
  transfers between devices with their start and end apart: 17, of which 8 were waited for; matrix products, arithmetic and copies ran while one was open for 2% of the time, Pallas kernels for 18%

profile of v8, /device:TPU:13, one launch (start us, length us, event | category | flops | bytes accessed | tf_op | source)
XLA Modules:
  0.0 158.1 jit_solution(9126583594351506777)
XLA Ops:
  0.6 2.7 %spread_columns.1 = (bf16[256,512]{1,0:T(8,128)(2,1)}, bf16[256,512]{1,0:T(8,128)(2,1)}, bf16[256,512]{1,0:T(8,128)(2,1)}, bf16[256,512]{1,0:T(8,128)(2,1)}, bf1...) custom-call(s32[1]{0:T(128)} %bitcast.me_ref, ...), custom_call_target="tpu_custom_call" | custom-call | bytes 4194308 | tf_op jit(solution)/shard_map/spread_columns/pallas_call | solution.py:40
  4.3 1.5 collective-permute-start.3
  5.8 2.2 %cut_factors.1 = (bf16[4,512,128]{2,1,0:T(8,128)(2,1)}, bf16[4,512,128]{2,1,0:T(8,128)(2,1)}, bf16[4,512,128]{2,1,0:T(8,128)(2,1)}) custom-call(bf16[3,4,512,128]{3,2,1,0:T(8,128)(2,1)} %bitcast.17), custom_call_target="tpu_custom_call" | custom-call | bytes 3145728 | tf_op jit(solution)/shard_map/cut_factors/pallas_call | solution.py:40
  9.5 1.9 %collective-permute-start.5 = (bf16[256,512]{1,0:T(8,128)(2,1)}, bf16[256,512]{1,0:T(8,128)(2,1)}, u32[]{:S(2)}, u32[]{:S(2)}) collective-permute-start(bf16[256,512]{1,0:T(8,128)(2,1)} %get-tuple-element.34), channel_id=1, source_target_pairs={{0,5},{1,4},{2,7},{3,6},{4,1},{5,0},{6,3},{7,2},{8,13},{9,12},{10,... | collective-permute-start | bytes 786440 | tf_op jit(solution)/shard_map/ppermute | solution.py:577
  12.3 6.0 %collective-permute-done.3.refs_4_ = bf16[256,512]{1,0:T(8,128)(2,1)} collective-permute-done((bf16[256,512]{1,0:T(8,128)(2,1)}, bf16[256,512]{1,0:T(8,128)(2,1)}, u32[]{:S(2)}, u32[]{:S(2)}) %collective-permute-start.3) | collective-permute-done | bytes 262176 | tf_op jit(solution)/shard_map/ppermute | solution.py:577
  18.3 1.3 share_selection.1
  19.7 15.9 %all_to_all.26 = s32[16,1,128]{2,1,0:T(1,128)} all-to-all(s32[16,1,128]{2,1,0:T(1,128)} %bitcast.26), channel_id=1, replica_groups=mesh['seq'=2,'exp'=16] {'exp'}, dimensions={0} | all-to-all | bytes 16384 | tf_op jit(solution)/shard_map/all_to_all | solution.py:567
  36.4 4.2 %pick_tokens.1 = bf16[1024,512]{1,0:T(8,128)(2,1)} custom-call(s32[1]{0:T(128)} %bitcast.me_ref, s32[16,128]{1,0:T(8,128)} %bitcast.23, bf16[4,512,128]{2,1,0:T(8,128)(2,1)} %copy-done.5, bf16[256,512]{1,0:T(8,128)(2,1)} %get-tuple-element.29.refs_1_, bf16[256,512]{1,0:T(8,128)(2,1)} %copy-done.8, bf16[256,512]{1,0:T(8,128)(2,1)} %collective-permute-done.2.refs_3_, ...), custom_call_target="tpu_custom_call" | custom-call | flops 1073741824 | bytes 3678212 | tf_op jit(solution)/shard_map/pick_tokens/pallas_call | solution.py:40
  40.6 7.0 %all-to-all-start.2 = ((bf16[16,64,512]{2,1,0:T(8,128)(2,1)}), bf16[16,64,512]{2,1,0:T(8,128)(2,1)}, u32[]{:S(2)}, u32[]{:S(2)}) async-start(bf16[16,64,512]{2,1,0:T(8,128)(2,1)} %bitcast.22), calls=%async_computation.2 | async-start | bytes 2097152 | tf_op jit(solution)/shard_map/all_to_all | solution.py:571
  47.9 12.9 %collective-permute-done.refs_0_.refs_2_ = bf16[4,512,128]{2,1,0:T(8,128)(2,1)S(1)} collective-permute-done((bf16[4,512,128]{2,1,0:T(8,128)(2,1)S(1)}, bf16[4,512,128]{2,1,0:T(8,128)(2,1)S(1)}, u32[]{:S(2)}, u32[]{:S(2)}) %collective-permute-start) | collective-permute-done | bytes 524320 | tf_op jit(solution)/shard_map/ppermute | solution.py:546
  61.6 4.2 %pick_cotangent.1 = bf16[1024,512]{1,0:T(8,128)(2,1)} custom-call(s32[1]{0:T(128)} %bitcast.me_ref, s32[16,128]{1,0:T(8,128)} %bitcast.24, bf16[4,512,128]{2,1,0:T(8,128)(2,1)} %copy-done.6, bf16[256,512]{1,0:T(8,128)(2,1)} %get-tuple-element.29.refs_1_, bf16[256,512]{1,0:T(8,128)(2,1)} %copy-done.8, bf16[256,512]{1,0:T(8,128)(2,1)} %collective-permute-done.2.refs_3_, ...), custom_call_target="tpu_custom_call" | custom-call | flops 1073741824 | bytes 3678212 | tf_op jit(solution)/shard_map/pick_cotangent/pallas_call | solution.py:40
  65.9 6.7 %all-to-all-done.2 = bf16[16,64,512]{2,1,0:T(8,128)(2,1)} async-done(((bf16[16,64,512]{2,1,0:T(8,128)(2,1)}), bf16[16,64,512]{2,1,0:T(8,128)(2,1)}, u32[]{:S(2)}, u32[]{:S(2)}) %all-to-all-start.2) | async-done | bytes 1048608 | tf_op jit(solution)/shard_map/all_to_all | solution.py:571
  72.6 4.9 %all-to-all-start.1 = ((bf16[16,64,512]{2,1,0:T(8,128)(2,1)}), bf16[16,64,512]{2,1,0:T(8,128)(2,1)}, u32[]{:S(2)}, u32[]{:S(2)}) async-start(bf16[16,64,512]{2,1,0:T(8,128)(2,1)} %bitcast.21), calls=%async_computation.1 | async-start | bytes 2097152 | tf_op jit(solution)/shard_map/all_to_all | solution.py:571
  78.5 5.9 %forward.1 = (bf16[512,512]{1,0:T(8,128)(2,1)}, bf16[512,512]{1,0:T(8,128)(2,1)}, f32[512,512]{1,0:T(8,128)}, f32[512,512]{1,0:T(8,128)}, f32[128,512]{1,0:T(8,1...) custom-call(s32[1]{0:T(128)} %bitcast.5.order_ref, f32[192]{0:T(256)} %reshape.44.mix_ref, ...), custom_call_target="tpu_custom_call" | custom-call | flops 1073741824 | bytes 7602948 | tf_op jit(solution)/shard_map/forward/pallas_call | solution.py:40
  87.0 4.0 %collective-permute-done.9.refs_3_ = bf16[4,512,128]{2,1,0:T(8,128)(2,1)} collective-permute-done((bf16[4,512,128]{2,1,0:T(8,128)(2,1)}, bf16[4,512,128]{2,1,0:T(8,128)(2,1)}, u32[]{:S(2)}, u32[]{:S(2)}) %collective-permute-start.9) | collective-permute-done | bytes 524320 | tf_op jit(solution)/shard_map/ppermute | solution.py:546
  91.0 11.7 %all-to-all-done.1 = bf16[16,64,512]{2,1,0:T(8,128)(2,1)} async-done(((bf16[16,64,512]{2,1,0:T(8,128)(2,1)}), bf16[16,64,512]{2,1,0:T(8,128)(2,1)}, u32[]{:S(2)}, u32[]{:S(2)}) %all-to-all-start.1) | async-done | bytes 1048608 | tf_op jit(solution)/shard_map/all_to_all | solution.py:571
  103.5 8.6 %backward.1 = (bf16[384,2048]{1,0:T(8,128)(2,1)}, bf16[512,512]{1,0:T(8,128)(2,1)}, bf16[512,512]{1,0:T(8,128)(2,1)}, f32[512,512]{1,0:T(8,128)}, bf16[3,128,512]{2,1,0:T(8,128)(2,1)}, /*index=5*/f32[128,128]{1,0:T(8,128)}) custom-call(s32[1]{0:T(128)} %bitcast.5.order_ref, f32[192]{0:T(256)} %reshape.44.mix_ref, s32[1,128]{1,0:T(1,128)} %row_slots.1.slot_ref, ...), custom_call_target="tpu_custom_call" | custom-call | flops 1610612736 | bytes 9635588 | tf_op jit(solution)/shard_map/backward/pallas_call | solution.py:40
  112.1 6.4 %all-to-all-start.3 = ((bf16[16,24,2048]{2,1,0:T(8,128)(2,1)}), bf16[16,24,2048]{2,1,0:T(8,128)(2,1)}, u32[]{:S(2)}, u32[]{:S(2)}) async-start(bf16[16,24,2048]{2,1,0:T(8,128)(2,1)} %bitcast.20), calls=%async_computation.3 | async-start | bytes 3145728 | tf_op jit(solution)/shard_map/all_to_all | solution.py:571
  120.1 1.8 %place_rows.1.placed_hbm = bf16[256,384]{1,0:T(8,128)(2,1)} custom-call(s32[1]{0:T(128)} %bitcast.me_ref, s32[16,128]{1,0:T(8,128)} %bitcast.25), custom_call_target="tpu_custom_call" | custom-call | flops 1048576 | bytes 204804 | tf_op jit(solution)/shard_map/place_rows/pallas_call | solution.py:40
  121.9 3.9 %mix_partials.1 = f32[192,128]{1,0:T(8,128)} custom-call(f32[512,512]{1,0:T(8,128)} %get-tuple-element.48.yg_hbm, f32[512,512]{1,0:T(8,128)} %get-tuple-element.49.yu_hbm, f32[512,512]{1,0:T(8,128)} %get-tuple-element.50.yd_hbm, bf16[3,128,512]{2,1,0:T(8,128)(2,1)} %get-tuple-element.46.refs_2_.d_hbm), custom_call_target="tpu_custom_call" | custom-call | flops 6291456 | bytes 3637248 | tf_op jit(solution)/shard_map/mix_partials/pallas_call | solution.py:40
  128.7 12.3 %collective-permute-done.13 = f32[1,3,4,4,4]{4,3,2,1,0:T(4,128)S(1)} collective-permute-done((f32[1,3,4,4,4]{4,3,2,1,0:T(4,128)S(1)}, f32[1,3,4,4,4]{4,3,2,1,0:T(4,128)S(1)}, u32[]{:S(2)}, u32[]{:S(2)}) %collective-permute-start.13) | collective-permute-done | bytes 800 | tf_op jit(solution)/shard_map/ppermute | solution.py:546
  142.4 7.8 %factor_grad.1 = f32[3,4,512,128]{3,2,1,0:T(8,128)} custom-call(f32[192]{0:T(256)} %reshape.44.mix_ref, bf16[512,512]{1,0:T(8,128)(2,1)} %get-tuple-element.44.refs_0_, bf16[512,512]{1,0:T(8,128)(2,1)} %get-tuple-element.45.refs_1_, bf16[3,128,512]{2,1,0:T(8,128)(2,1)} %get-tuple-element.46.refs_2_.d_hbm, bf16[512,512]{1,0:T(8,128)(2,1)} %copy-done.1, ...), custom_call_target="tpu_custom_call" | custom-call | flops 1610612736 | bytes 6030080 | tf_op jit(solution)/shard_map/factor_grad/pallas_call | solution.py:40
  150.3 4.5 %all-to-all-done.3 = bf16[16,24,2048]{2,1,0:T(8,128)(2,1)} async-done(((bf16[16,24,2048]{2,1,0:T(8,128)(2,1)}), bf16[16,24,2048]{2,1,0:T(8,128)(2,1)}, u32[]{:S(2)}, u32[]{:S(2)}) %all-to-all-start.3) | async-done | bytes 1572896 | tf_op jit(solution)/shard_map/all_to_all | solution.py:571
  154.8 3.1 %sum_rows.1 = bf16[128,4096]{1,0:T(8,128)(2,1)} custom-call(bf16[256,384]{1,0:T(8,128)(2,1)} %place_rows.1.placed_hbm, bf16[384,2048]{1,0:T(8,128)(2,1)} %bitcast.13.returned_ref), custom_call_target="tpu_custom_call" | custom-call | flops 402653184 | bytes 2818048 | tf_op jit(solution)/shard_map/sum_rows/pallas_call | solution.py:40
  (48 shorter events, 15.5 us)
Async XLA Ops:
  3.3 6.1 %collective-permute-start.1 = (bf16[256,512]{1,0:T(8,128)(2,1)}, bf16[256,512]{1,0:T(8,128)(2,1)S(1)}, u32[]{:S(2)}, u32[]{:S(2)}) collective-permute-start(bf16[256,512]{1,0:T(8,128)(2,1)} %get-tuple-element.30), channel_id=1, source_target_pairs={{0,1},{1,0},{2,3},{3,2},{4,5},{5,4},{6,7},{7,6},{8,9},{9,8},{10,11... | collective-permute-start | bytes 786440 | tf_op jit(solution)/shard_map/ppermute | solution.py:577
  4.1 8.2 %collective-permute-start.2 = (bf16[256,512]{1,0:T(8,128)(2,1)}, bf16[256,512]{1,0:T(8,128)(2,1)}, u32[]{:S(2)}, u32[]{:S(2)}) collective-permute-start(bf16[256,512]{1,0:T(8,128)(2,1)} %get-tuple-element.31), channel_id=1, source_target_pairs={{0,2},{1,3},{2,0},{3,1},{4,6},{5,7},{6,4},{7,5},{8,10},{9,11},{10,... | collective-permute-start | bytes 786440 | tf_op jit(solution)/shard_map/ppermute | solution.py:577
  4.3 14.0 %collective-permute-start.3 = (bf16[256,512]{1,0:T(8,128)(2,1)}, bf16[256,512]{1,0:T(8,128)(2,1)}, u32[]{:S(2)}, u32[]{:S(2)}) collective-permute-start(bf16[256,512]{1,0:T(8,128)(2,1)} %get-tuple-element.32), channel_id=1, source_target_pairs={{0,3},{1,2},{2,1},{3,0},{4,7},{5,6},{6,5},{7,4},{8,11},{9,10},{10,... | collective-permute-start | bytes 786440 | tf_op jit(solution)/shard_map/ppermute | solution.py:577
  8.0 27.6 %collective-permute-start.8 = (bf16[4,512,128]{2,1,0:T(8,128)(2,1)}, bf16[4,512,128]{2,1,0:T(8,128)(2,1)S(1)}, u32[]{:S(2)}, u32[]{:S(2)}) collective-permute-start(bf16[4,512,128]{2,1,0:T(8,128)(2,1)} %get-tuple-element.37), channel_id=1, source_target_pairs={{0,16},{16,0},{1,17},{17,1},{2,18},{18,2},{3,19},{19,3},{4,20},{20... | collective-permute-start | bytes 1572872 | tf_op jit(solution)/shard_map/ppermute | solution.py:546
  9.3 26.3 %collective-permute-start.4 = (bf16[256,512]{1,0:T(8,128)(2,1)}, bf16[256,512]{1,0:T(8,128)(2,1)}, u32[]{:S(2)}, u32[]{:S(2)}) collective-permute-start(bf16[256,512]{1,0:T(8,128)(2,1)} %get-tuple-element.33), channel_id=1, source_target_pairs={{0,4},{1,5},{2,6},{3,7},{4,0},{5,1},{6,2},{7,3},{8,12},{9,13},{10,... | collective-permute-start | bytes 786440 | tf_op jit(solution)/shard_map/ppermute | solution.py:577
  9.5 26.1 %copy-start.8 = (bf16[256,512]{1,0:T(8,128)(2,1)}, bf16[256,512]{1,0:T(8,128)(2,1)S(1)}, u32[]{:S(2)}) copy-start(bf16[256,512]{1,0:T(8,128)(2,1)S(1)} %collective-permute-done.1.refs_2_) | copy-start | bytes 786436
  9.5 26.1 %collective-permute-start.5 = (bf16[256,512]{1,0:T(8,128)(2,1)}, bf16[256,512]{1,0:T(8,128)(2,1)}, u32[]{:S(2)}, u32[]{:S(2)}) collective-permute-start(bf16[256,512]{1,0:T(8,128)(2,1)} %get-tuple-element.34), channel_id=1, source_target_pairs={{0,5},{1,4},{2,7},{3,6},{4,1},{5,0},{6,3},{7,2},{8,13},{9,12},{10,... | collective-permute-start | bytes 786440 | tf_op jit(solution)/shard_map/ppermute | solution.py:577
  12.3 23.3 %collective-permute-start.6 = (bf16[256,512]{1,0:T(8,128)(2,1)}, bf16[256,512]{1,0:T(8,128)(2,1)}, u32[]{:S(2)}, u32[]{:S(2)}) collective-permute-start(bf16[256,512]{1,0:T(8,128)(2,1)} %get-tuple-element.35), channel_id=1, source_target_pairs={{0,6},{1,7},{2,4},{3,5},{4,2},{5,3},{6,0},{7,1},{8,14},{9,15},{10,... | collective-permute-start | bytes 786440 | tf_op jit(solution)/shard_map/ppermute | solution.py:577
  18.3 17.2 %collective-permute-start.7 = (bf16[256,512]{1,0:T(8,128)(2,1)}, bf16[256,512]{1,0:T(8,128)(2,1)}, u32[]{:S(2)}, u32[]{:S(2)}) collective-permute-start(bf16[256,512]{1,0:T(8,128)(2,1)} %get-tuple-element.36), channel_id=1, source_target_pairs={{0,7},{1,6},{2,5},{3,4},{4,3},{5,2},{6,1},{7,0},{8,15},{9,14},{10,... | collective-permute-start | bytes 786440 | tf_op jit(solution)/shard_map/ppermute | solution.py:577
  40.6 7.0 %copy-start.7 = (bf16[4,512,128]{2,1,0:T(8,128)(2,1)S(1)}, bf16[4,512,128]{2,1,0:T(8,128)(2,1)}, u32[]{:S(2)}) copy-start(bf16[4,512,128]{2,1,0:T(8,128)(2,1)} %get-tuple-element.28) | copy-start | bytes 1572868
  40.6 32.0 %all-to-all-start.2 = ((bf16[16,64,512]{2,1,0:T(8,128)(2,1)}), bf16[16,64,512]{2,1,0:T(8,128)(2,1)}, u32[]{:S(2)}, u32[]{:S(2)}) async-start(bf16[16,64,512]{2,1,0:T(8,128)(2,1)} %bitcast.22), calls=%async_computation.2 | async-start | bytes 2097152 | tf_op jit(solution)/shard_map/all_to_all | solution.py:571
  47.6 13.2 %collective-permute-start = (bf16[4,512,128]{2,1,0:T(8,128)(2,1)S(1)}, bf16[4,512,128]{2,1,0:T(8,128)(2,1)S(1)}, u32[]{:S(2)}, u32[]{:S(2)}) collective-permute-start(bf16[4,512,128]{2,1,0:T(8,128)(2,1)S(1)} %copy-done.7), channel_id=1, source_target_pairs={{0,16},{16,0},{1,17},{17,1},{2,18},{18,2},{3,19},{19,3},{4,20},{20... | collective-permute-start | bytes 1572872 | tf_op jit(solution)/shard_map/ppermute | solution.py:546
  60.8 0.8 copy-start.6
  65.9 11.9 %copy-start.4 = (f32[1,3,4,4,4]{4,3,2,1,0:T(4,128)S(1)}, f32[1,3,4,4,4]{4,3,2,1,0:T(4,128)}, u32[]{:S(2)}) copy-start(f32[1,3,4,4,4]{4,3,2,1,0:T(4,128)} %param.9) | copy-start | bytes 2308
  72.6 30.1 %all-to-all-start.1 = ((bf16[16,64,512]{2,1,0:T(8,128)(2,1)}), bf16[16,64,512]{2,1,0:T(8,128)(2,1)}, u32[]{:S(2)}, u32[]{:S(2)}) async-start(bf16[16,64,512]{2,1,0:T(8,128)(2,1)} %bitcast.21), calls=%async_computation.1 | async-start | bytes 2097152 | tf_op jit(solution)/shard_map/all_to_all | solution.py:571
  77.5 13.5 %collective-permute-start.9 = (bf16[4,512,128]{2,1,0:T(8,128)(2,1)}, bf16[4,512,128]{2,1,0:T(8,128)(2,1)}, u32[]{:S(2)}, u32[]{:S(2)}) collective-permute-start(bf16[4,512,128]{2,1,0:T(8,128)(2,1)} %get-tuple-element.41), channel_id=1, source_target_pairs={{0,16},{16,0},{1,17},{17,1},{2,18},{18,2},{3,19},{19,3},{4,20},{20... | collective-permute-start | bytes 1572872 | tf_op jit(solution)/shard_map/ppermute | solution.py:546
  84.4 18.3 %collective-permute-start.10 = (bf16[512,512]{1,0:T(8,128)(2,1)}, bf16[512,512]{1,0:T(8,128)(2,1)S(1)}, u32[]{:S(2)}, u32[]{:S(2)}) collective-permute-start(bf16[512,512]{1,0:T(8,128)(2,1)} %get-tuple-element.42), channel_id=1, source_target_pairs={{0,16},{16,0},{1,17},{17,1},{2,18},{18,2},{3,19},{19,3},{4,20},{20... | collective-permute-start | bytes 1572872 | tf_op jit(solution)/shard_map/ppermute | solution.py:546
  102.7 0.8 copy-start.1
  112.1 6.7 %copy-start = (bf16[3,128,512]{2,1,0:T(8,128)(2,1)S(1)}, bf16[3,128,512]{2,1,0:T(8,128)(2,1)}, u32[]{:S(2)}) copy-start(bf16[3,128,512]{2,1,0:T(8,128)(2,1)} %get-tuple-element.46.refs_2_.d_hbm) | copy-start | bytes 1179652
  112.1 42.7 %all-to-all-start.3 = ((bf16[16,24,2048]{2,1,0:T(8,128)(2,1)}), bf16[16,24,2048]{2,1,0:T(8,128)(2,1)}, u32[]{:S(2)}, u32[]{:S(2)}) async-start(bf16[16,24,2048]{2,1,0:T(8,128)(2,1)} %bitcast.20), calls=%async_computation.3 | async-start | bytes 3145728 | tf_op jit(solution)/shard_map/all_to_all | solution.py:571
  118.5 23.1 %collective-permute-start.11 = (bf16[512,512]{1,0:T(8,128)(2,1)}, bf16[512,512]{1,0:T(8,128)(2,1)S(1)}, u32[]{:S(2)}, u32[]{:S(2)}) collective-permute-start(bf16[512,512]{1,0:T(8,128)(2,1)} %get-tuple-element.47), channel_id=1, source_target_pairs={{0,16},{16,0},{1,17},{17,1},{2,18},{18,2},{3,19},{19,3},{4,20},{20... | collective-permute-start | bytes 1572872 | tf_op jit(solution)/shard_map/ppermute | solution.py:546
  118.8 22.8 %collective-permute-start.12 = (bf16[3,128,512]{2,1,0:T(8,128)(2,1)S(1)}, bf16[3,128,512]{2,1,0:T(8,128)(2,1)}, u32[]{:S(2)}, u32[]{:S(2)}) collective-permute-start(bf16[3,128,512]{2,1,0:T(8,128)(2,1)S(1)} %copy-done), channel_id=1, source_target_pairs={{0,16},{16,0},{1,17},{17,1},{2,18},{18,2},{3,19},{19,3},{4,20},{20... | collective-permute-start | bytes 1179656 | tf_op jit(solution)/shard_map/ppermute | solution.py:546
  121.9 5.4 %copy-start.3 = (f32[128,128]{1,0:T(8,128)S(1)}, f32[128,128]{1,0:T(8,128)}, u32[]{:S(2)}) copy-start(f32[128,128]{1,0:T(8,128)} %get-tuple-element.51) | copy-start | bytes 196612
  126.9 14.1 %collective-permute-start.13 = (f32[1,3,4,4,4]{4,3,2,1,0:T(4,128)S(1)}, f32[1,3,4,4,4]{4,3,2,1,0:T(4,128)S(1)}, u32[]{:S(2)}, u32[]{:S(2)}) collective-permute-start(f32[1,3,4,4,4]{4,3,2,1,0:T(4,128)S(1)} %reshape.51), channel_id=1, source_target_pairs={{0,16},{16,0},{1,17},{17,1},{2,18},{18,2},{3,19},{19,3},{4,20},{20... | collective-permute-start | bytes 2312 | tf_op jit(solution)/shard_map/ppermute | solution.py:546
  (2 other events, 1.6 us)

commit v9 on v8

--- a/solution.py
+++ b/solution.py
@@ -68,8 +68,86 @@
     return [slice(c * chunk, (c + 1) * chunk) for c in range(part // chunk)]
 
 
-def start_all(pairs, sems):
-    return [begin(source, target, sems.at[n]) for n, (source, target) in enumerate(pairs)]
+def index_body(cap, pieces, own_rows, block_len, chosen_ref, told_ref, slot_ref):
+    peers, rows = told_ref.shape[0] // 2, slot_ref.shape[1]
+    blocks = [chosen_ref[b : b + 1, :] for b in range(chosen_ref.shape[0])]
+    position = jnp.concatenate([x + b * block_len for b, x in enumerate(blocks)], axis=1)
+    owner = lax.shift_right_logical(position, own_rows.bit_length() - 1)
+    local = position & (own_rows - 1)
+    peer = iota((peers, rows), 0)
+    mine = (peer == owner).astype(F32)
+    count = jnp.sum(mine, axis=1, keepdims=True)
+    earlier = jnp.sum(jnp.where(peer < owner, count, 0.0), axis=0, keepdims=True).astype(jnp.int32)
+    rank = iota((1, rows), 1) - earlier
+    slot_ref[...] = owner * (cap * pieces) + rank
+    lane = iota((rows, rows), 0)
+    hit = jnp.zeros((rows, rows), F32)
+    for j in range(pieces):
+        hit = hit + (lane == rank + j * cap).astype(F32)
+    twice = iota((2 * peers, rows), 0)
+    marked = jnp.where(twice == 2 * owner, local + 1, 0).astype(F32)
+    asked = dot_nt(marked.astype(BF16), hit.astype(BF16)).astype(jnp.int32)
+    told_ref[...] = jnp.where((twice & 1) == 1, jnp.concatenate(blocks, axis=1), asked)
+
+
+def pick_matrix(cap, pieces, own_rows, requested):
+    told, lanes = requested.shape
+    peers = told // 2
+    group = cap * pieces
+    slots = peers * group
+    peer = 2 * iota((peers, group, told), 0).reshape(slots, told)
+    spread = dot(
+        (peer == iota((slots, told), 1)).astype(BF16), requested.astype(F32).astype(BF16)
+    )
+    place = iota((peers, group, lanes), 1).reshape(slots, lanes)
+    row = jnp.sum(
+        jnp.where(place == iota((slots, lanes), 1), spread, 0.0), axis=1, keepdims=True
+    ).astype(jnp.int32)
+    piece = iota((peers, group, 1), 1).reshape(slots, 1)
+    shift = jnp.zeros((slots, 1), jnp.int32)
+    for j in range(1, pieces):
+        shift = shift + jnp.where(piece >= j * cap, own_rows, 0)
+    target = jnp.where(row > 0, row - 1 + shift, -1)
+    return (target == iota((slots, pieces * own_rows), 1)).astype(BF16)
+
+
+def pick_slots(cap, pieces, requested, source, name):
+    own_rows, width = source.shape
+    part = width // pieces
+    slots = requested.shape[0] // 2 * cap * pieces
+    columns = chunks_of(part)
+
+    def body(requested_ref, source_ref, *refs):
+        out_ref, rows_ref, sent_ref, in_sem, out_sem = refs
+        loads = []
+        for n, at in enumerate(columns):
+            for j in range(pieces):
+                wide = slice(j * part + at.start, j * part + at.stop)
+                target = rows_ref.at[j * own_rows : (j + 1) * own_rows, at]
+                loads.append(begin(source_ref.at[:, wide], target, in_sem.at[n, j]))
+        pick = pick_matrix(cap, pieces, own_rows, requested_ref[...])
+        stores = []
+        for n, at in enumerate(columns):
+            for load in loads[n * pieces : (n + 1) * pieces]:
+                load.wait()
+            sent_ref[:, at] = dot(pick, rows_ref[:, at]).astype(BF16)
+            stores.append(begin(sent_ref.at[:, at], out_ref.at[:, at], out_sem.at[n]))
+        for store in stores:
+            store.wait()
+
+    return call(
+        body,
+        [(shaped((slots, part), BF16), HBM)],
+        [(requested, VMEM), (source, HBM)],
+        name,
+        2 * slots * pieces * own_rows * part,
+        [
+            scratch_like((pieces * own_rows, part), BF16),
+            scratch_like((slots, part), BF16),
+            pltpu.SemaphoreType.DMA((len(columns), pieces)),
+            pltpu.SemaphoreType.DMA((len(columns),)),
+        ],
+    )[0]
 
 
 def spread_columns(me, sources, half, direct, name):
@@ -106,36 +184,29 @@
     return call(body, outs, [(me, SMEM)] + [(x, HBM) for x in sources], name, 0, scratch)
 
 
-def share_selection(chosen, peers):
-    def body(chosen_ref, out_ref):
-        blocks = [chosen_ref[b : b + 1, :] for b in range(chosen_ref.shape[0])]
-        out_ref[...] = jnp.broadcast_to(jnp.concatenate(blocks, axis=1), out_ref.shape)
-
-    out = (shaped((peers, chosen.size), jnp.int32), VMEM)
-    return call(body, [out], [(chosen, VMEM)], "share_selection", 0)[0]
-
-
-def cut_factors(factors):
-    weights = factors.shape[0]
+def cut_factors(factors, first):
+    cuts = (slice(0, first), slice(first, factors.shape[0]))
 
     def body(factors_ref, *refs):
-        outs, (held_ref, sems) = refs[:weights], refs[weights:]
+        outs, (held_ref, sems) = refs[:2], refs[2:]
         loads = [
-            begin(factors_ref.at[m], held_ref.at[m], sems.at[0, m]) for m in range(weights)
+            begin(factors_ref.at[at], held_ref.at[at], sems.at[0, n]) for n, at in enumerate(cuts)
         ]
         copies = []
-        for m, load in enumerate(loads):
-            load.wait()
-            copies.append(begin(held_ref.at[m], outs[m], sems.at[1, m]))
+        for n, at in enumerate(cuts):
+            loads[n].wait()
+            copies.append(begin(held_ref.at[at], outs[n], sems.at[1, n]))
         wait_all(copies)
 
-    outs = [(shaped(factors.shape[1:], BF16), HBM)] * weights
-    scratch = [scratch_like(factors.shape, BF16), pltpu.SemaphoreType.DMA((2, weights))]
+    outs = [
+        (shaped((at.stop - at.start,) + factors.shape[1:], BF16), HBM) for at in cuts
+    ]
+    scratch = [scratch_like(factors.shape, BF16), pltpu.SemaphoreType.DMA((2, 2))]
     return call(body, outs, [(factors, HBM)], "cut_factors", 0, scratch)
 
 
 def pick_rows(me, half, own_rows, which, chosen, shares, after, name):
-    peers, total = chosen.shape
+    peers, total = chosen.shape[0] // 2, chosen.shape[1]
     picks = total * half // peers
     part = shares[0].shape[1]
     block = half * own_rows
@@ -160,7 +231,7 @@
         stores = []
         for first in range(0, peers, batch):
             for e in range(batch):
-                wanted = chosen_ref[first + e : first + e + 1, :]
+                wanted = chosen_ref[2 * (first + e) + 1 : 2 * (first + e) + 2, :]
                 column = jnp.sum(jnp.where(same, wanted, 0), axis=1, keepdims=True)
                 pick_ref[first // batch % 2, e * picks : (e + 1) * picks] = (
                     column == iota((picks, block), 1)
@@ -188,28 +259,15 @@
     )[0]
 
 
-def slot_body(cap, pieces, own_rows, block_len, chosen_ref, slot_ref):
-    rows = slot_ref.shape[1]
-    position = jnp.concatenate(
-        [chosen_ref[b : b + 1, :] + b * block_len for b in range(chosen_ref.shape[0])], axis=1
-    )
-    owner = lax.shift_right_logical(position, own_rows.bit_length() - 1)
-    peers = chosen_ref.shape[0] * block_len // own_rows
-    peer = iota((peers, rows), 0)
-    count = jnp.sum((peer == owner).astype(F32), axis=1, keepdims=True)
-    earlier = jnp.sum(jnp.where(peer < owner, count, 0.0), axis=0, keepdims=True).astype(jnp.int32)
-    slot_ref[...] = owner * (cap * pieces) + iota((1, rows), 1) - earlier
-
-
 def place_rows(cap, pieces, own_rows, me, half, chosen):
-    peers, total = chosen.shape
+    peers, total = chosen.shape[0] // 2, chosen.shape[1]
     picks = total * half // peers
     group = cap * pieces
 
     def body(me_ref, chosen_ref, out_ref, pick_ref):
         low = me_ref[0] & (half - 1)
         block_at = lax.shift_right_logical(me_ref[0], half.bit_length() - 1)
-        lane = iota((peers, total), 1) - block_at * picks
+        lane = iota((2 * peers, total), 1) - block_at * picks
         here = (lane >= 0) & (lane < picks)
         local = jnp.where(here, chosen_ref[...] - low * own_rows, own_rows)
         before = jnp.sum((local < 0).astype(F32), axis=1, keepdims=True).astype(jnp.int32)
@@ -217,7 +275,8 @@
         owned = jnp.where((local >= 0) & (local < own_rows), local + 1, 0)
         place = iota((group, total), 0)
         for e in range(peers):
-            rank, mine = ranks[e : e + 1], owned[e : e + 1]
+            at = slice(2 * e + 1, 2 * e + 2)
+            rank, mine = ranks[at], owned[at]
             column = jnp.zeros((group, 1), jnp.int32)
             for j in range(pieces):
                 hit = jnp.where((place == rank + j * cap) & (rank >= 0) & (rank < cap), mine, 0)
@@ -280,7 +339,11 @@
 
 def load_factor(order_ref, parts, m, target, sems):
     copies = []
-    for n, side in enumerate((parts[0].at[m], parts[1 + m]) if len(parts) > 1 else (parts[0].at[m],)):
+    sides = [parts[0].at[m]]
+    if len(parts) > 1:
+        first = parts[1].shape[0]
+        sides.append(parts[1].at[m] if m < first else parts[2].at[m - first])
+    for n, side in enumerate(sides):
         count, rows, cols = side.shape
         place = order_ref[0] ^ n if len(parts) > 1 else 0
         start = pl.multiple_of(place * rows, rows)
@@ -313,6 +376,27 @@
         at = x_ref.at[first : first + picks, start : start + part]
         copies.append(begin(got_hbm.at[n * picks : (n + 1) * picks], at, sems.at[n]))
     return copies
+
+
+def load_slots(got_hbm, got_ref, sems):
+    return [
+        begin(got_hbm.at[:, at], got_ref.at[:, at], sems.at[n])
+        for n, at in enumerate(chunks_of(got_ref.shape[1]))
+    ]
+
+
+def stack_rows(pieces, place, loads, got_ref, out_ref):
+    part = got_ref.shape[1]
+    rows, depth = out_ref.shape[0] // NPHM, out_ref.shape[1]
+    for load, at in zip(loads, chunks_of(part)):
+        load.wait()
+        block = dot_tn(place, got_ref[:, at]).astype(BF16)
+        for j in range(pieces):
+            column = j * part + at.start
+            a, start = column // depth, column % depth
+            out_ref[a * rows : (a + 1) * rows, start : start + at.stop - at.start] = block[
+                j * rows : (j + 1) * rows
+            ]
 
 
 def store_parts(order_ref, source_ref, outs, sems):
@@ -366,19 +450,20 @@
 
 
 def forward_body(
-    sides, order_ref, mix_ref, got_hbm, *refs
+    cap, pieces, sides, order_ref, mix_ref, slot_ref, got_hbm, *refs
 ):
-    held = 3 if sides > 1 else 1
+    held = 2 if sides > 1 else 1
     parts, refs = refs[:held], refs[held:]
     x_outs, refs = refs[:sides], refs[sides:]
     yg_hbm, yu_hbm, act_hbm, slope_hbm, hid_hbm = refs[:5]
-    side_ref, x_ref, yg_ref, yu_ref, pre_ref, act_ref, slope_ref, hid_ref = refs[5:13]
-    got_sem, side_sem, out_sem = refs[13:]
-    loads = load_rows(got_hbm, x_ref, got_sem)
+    got_ref, side_ref, x_ref, yg_ref, yu_ref, pre_ref, act_ref, slope_ref, hid_ref = refs[5:14]
+    got_sem, side_sem, out_sem = refs[14:]
+    loads = load_slots(got_hbm, got_ref, got_sem)
     sides_in = [
         load_factor(order_ref, parts, m, side_ref.at[m], side_sem.at[m]) for m in range(2)
     ]
-    wait_all(loads)
+    place = place_matrix(cap, pieces, got_ref.shape[0], slot_ref[...])
+    stack_rows(pieces, place, loads, got_ref, x_ref)
     stores = store_parts(order_ref, x_ref, x_outs, out_sem)
     wait_all(sides_in[0])
     yg_ref[...] = dot(x_ref[...], side_ref[0])
@@ -414,7 +499,7 @@
     cap, pieces, sides, after, order_ref, mix_ref, slot_ref, score_ref, got_hbm, act_hbm, slope_hbm, hid_hbm,
     *refs,
 ):
-    held = 4 if sides > 1 else 1
+    held = 3 if sides > 1 else 1
     parts, refs = refs[:held], refs[held + after :]
     back_hbm, x_outs, refs = refs[0], refs[1 : 1 + sides], refs[1 + sides :]
     y_hbm, d_hbm, inner_ref = refs[:3]
@@ -552,11 +637,8 @@
     halves = [list(range(h, h + half)) for h in range(0, peers, half)]
     near = [k for k in range(1, half) if k >= 4] + [k for k in range(1, half) if k < 4]
 
-    shares = spread_columns(me, [tokens, cotangent], half, direct, "spread_columns")
-    cuts = cut_factors(factors[0])
-    wanted = share_selection(selection[0], peers)
     if swap:
-        cuts = [across(x) for x in cuts]
+        cuts = [across(x) for x in cut_factors(factors[0], 2)]
         factor_parts = [factors[0]] + cuts
         sides = 2
     else:
@@ -564,7 +646,14 @@
         factor_parts = [lax.all_gather(factors, "seq", axis=3, tiled=True)[0]]
         sides = 1
     sides_in = [(x, HBM) for x in factor_parts]
-    chosen = lax.all_to_all(wanted, "exp", split_axis=0, concat_axis=0, tiled=True)
+    told, slot = call(
+        functools.partial(index_body, cap, pieces, own_rows, block_len),
+        [(shaped((2 * peers, rows), jnp.int32), VMEM), (shaped((1, rows), jnp.int32), VMEM)],
+        [(selection[0], VMEM)],
+        "wanted_rows",
+        1 << 20,
+    )
+    chosen = lax.all_to_all(told, "exp", split_axis=0, concat_axis=0, tiled=True)
 
     def to_peers(array):
         array = array.reshape(peers, -1, array.shape[1])
@@ -583,19 +672,11 @@
         )
         return [array.reshape(shares[0].shape)]
 
-    shares = collect(shares)
-    pick = functools.partial(pick_rows, me, half, own_rows)
-    got_rows = to_peers(pick(0, chosen, shares, cuts[:1], "pick_tokens"))
-    got_grads = to_peers(pick(1, chosen, shares, cuts[1:2], "pick_cotangent"))
+    got_rows = to_peers(pick_slots(cap, pieces, chosen, tokens, "pick_tokens"))
+    shares = collect(spread_columns(me, [cotangent], half, direct, "spread_cotangent"))
+    picked = pick_rows(me, half, own_rows, 0, chosen, shares, cuts[:1], "pick_cotangent")
+    got_grads = to_peers(picked)
     placed = place_rows(cap, pieces, own_rows, me, half, chosen)
-    slot = call(
-        functools.partial(slot_body, cap, pieces, own_rows, block_len),
-        [(shaped((1, rows), jnp.int32), VMEM)],
-        [(selection[0], VMEM)],
-        "row_slots",
-        1 << 16,
-    )[0]
-
     gate = jax.nn.sigmoid(scores[0].reshape(-1).astype(F32) / 64.0)
 
     product = 2 * stacked * depth * hidden
@@ -603,20 +684,20 @@
     mixed = (shaped((stacked, hidden), F32), HBM)
     flat = (shaped((rows, hidden), F32), HBM)
     back_scratch = scratch_like((slots, part), BF16)
-    pieces_in = got_rows.shape[0] // SELECTED
+    pieces_in = got_grads.shape[0] // SELECTED
     stack_scratch = scratch_like((stacked, depth), BF16)
     mixed_scratch = scratch_like((stacked, hidden), F32)
     low_scratch = scratch_like((stacked, hidden), BF16)
     flat_scratch = scratch_like((rows, hidden), F32)
     outs = call(
-        functools.partial(forward_body, sides),
+        functools.partial(forward_body, cap, pieces, sides),
         split + [mixed, mixed, flat, flat, flat],
-        [(group, SMEM), (mixing, SMEM), (got_rows, HBM)] + sides_in[:3],
+        [(group, SMEM), (mixing, SMEM), (slot, VMEM), (got_rows, HBM)] + sides_in[:2],
         "forward",
         2 * product,
-        [scratch_like((2, depth, hidden), BF16), stack_scratch, mixed_scratch, mixed_scratch]
+        [back_scratch, scratch_like((2, depth, hidden), BF16), stack_scratch, mixed_scratch, mixed_scratch]
         + [flat_scratch] * 4
-        + [dma((pieces_in,)), dma((2, sides, count)), dma((7,))],
+        + [dma((steps,)), dma((2, sides, count)), dma((7,))],
     )
     x_parts, (y_gate, y_up, act, slope, hid) = outs[:sides], outs[sides:]
     x_rows = [x_parts[0]] + [across(x) for x in x_parts[1:]]

time: 159 us -> 155 us (0.975)
  blocking collectives: 15.9 us -> 10.8 us
  starting transfers between devices: 27.9 us -> 30.1 us
    ppermute x7, waiting for transfers between devices: 6.9 us -> 28.2 us  [collect(): lax.ppermute(shares[k], 'exp', [(n, n ^ k) for n in range(peers)])]
    ppermute x7 -> x6, waiting for transfers between devices: 29.2 us -> 15.8 us  [across(): return lax.ppermute(array, 'seq', pair)]
    all_to_all x3, waiting for transfers between devices: 23 us -> 16.3 us  [to_peers(): lax.all_to_all(array, 'exp', split_axis=0, concat_axis=0, tiled=True)]
    all_to_all x1, blocking collectives: 15.9 us -> 10.8 us  [shards(): lax.all_to_all(told, 'exp', split_axis=0, concat_axis=0, tiled=True)]
    unnamed x18 -> x24, local copies, waits for them, and re-layouts: 3.19 us -> 2.22 us
    pallas_call x12 -> x11, Pallas kernels: 47.2 us -> 46.2 us  [call(): pl.pallas_call(body, out_shape=[x for x, _ in outs], in_specs=[place for...]
    ppermute x7 -> x6, starting transfers between devices: 5 us -> 5.61 us  [across(): return lax.ppermute(array, 'seq', pair)]
  transfers between devices with their start and end apart: 17 -> 16, of which waited for: 8 -> 10; matrix products, arithmetic and copies ran while one was open for 2% -> 3% of each run, Pallas kernels for 18% -> 19%
where the time goes in v9:
time: 155 us; the launch traced here: 154 us
  waiting for transfers between devices  60.2 us (39%)
  Pallas kernels  46.2 us (30%)
  starting transfers between devices  30.1 us (19%)
  blocking collectives  10.8 us (7%)
  local copies, waits for them, and re-layouts  3.12 us (2%)
  other arithmetic  2.99 us (2%)
    pallas_call x11, Pallas kernels, call(): pl.pallas_call(body, out_shape=[x for x, _ in outs], in_specs=[place for...  46.2 us
    ppermute x7, waiting for transfers between devices, collect(): lax.ppermute(shares[k], 'exp', [(n, n ^ k) for n in range(peers)])  28.2 us
    all_to_all x3, starting transfers between devices, to_peers(): lax.all_to_all(array, 'exp', split_axis=0, concat_axis=0, tiled=True)  18.6 us
    all_to_all x3, waiting for transfers between devices, to_peers(): lax.all_to_all(array, 'exp', split_axis=0, concat_axis=0, tiled=True)  16.3 us
    ppermute x6, waiting for transfers between devices, across(): return lax.ppermute(array, 'seq', pair)  15.8 us
    all_to_all x1, blocking collectives, shards(): lax.all_to_all(told, 'exp', split_axis=0, concat_axis=0, tiled=True)  10.8 us
    ppermute x7, starting transfers between devices, collect(): lax.ppermute(shares[k], 'exp', [(n, n ^ k) for n in range(peers)])  5.93 us
    ppermute x6, starting transfers between devices, across(): return lax.ppermute(array, 'seq', pair)  5.61 us
  transfers between devices with their start and end apart: 16, of which 10 were waited for; matrix products, arithmetic and copies ran while one was open for 3% of the time, Pallas kernels for 19%

profile of v9, /device:TPU:13, one launch (start us, length us, event | category | flops | bytes accessed | tf_op | source)
XLA Modules:
  0.0 154.4 jit_solution(2926861586013070504)
XLA Ops:
  2.2 10.8 %all_to_all.26 = s32[16,2,128]{2,1,0:T(2,128)} all-to-all(s32[16,2,128]{2,1,0:T(2,128)} %bitcast.24), channel_id=1, replica_groups=mesh['seq'=2,'exp'=16] {'exp'}, dimensions={0} | all-to-all | bytes 32768 | tf_op jit(solution)/shard_map/all_to_all | solution.py:656
  13.0 3.6 %pick_tokens.1 = bf16[384,2048]{1,0:T(8,128)(2,1)} custom-call(s32[32,128]{1,0:T(8,128)} %bitcast.21, bf16[128,4096]{1,0:T(8,128)(2,1)} %source_ref.1), custom_call_target="tpu_custom_call" | custom-call | flops 402653184 | bytes 2637824 | tf_op jit(solution)/shard_map/pick_tokens/pallas_call | solution.py:40
  16.6 6.7 %all-to-all-start.2 = ((bf16[16,24,2048]{2,1,0:T(8,128)(2,1)}), bf16[16,24,2048]{2,1,0:T(8,128)(2,1)}, u32[]{:S(2)}, u32[]{:S(2)}) async-start(bf16[16,24,2048]{2,1,0:T(8,128)(2,1)} %bitcast.14), calls=%async_computation.2 | async-start | bytes 3145728 | tf_op jit(solution)/shard_map/all_to_all | solution.py:660
  23.3 2.4 %cut_factors.1 = (bf16[2,4,512,128]{3,2,1,0:T(8,128)(2,1)}, bf16[1,4,512,128]{3,2,1,0:T(8,128)(2,1)}) custom-call(bf16[3,4,512,128]{3,2,1,0:T(8,128)(2,1)} %bitcast.15), custom_call_target="tpu_custom_call" | custom-call | bytes 3145728 | tf_op jit(solution)/shard_map/cut_factors/pallas_call | solution.py:40
  27.0 2.3 %spread_cotangent.1 = (bf16[128,512]{1,0:T(8,128)(2,1)}, bf16[128,512]{1,0:T(8,128)(2,1)}, bf16[128,512]{1,0:T(8,128)(2,1)}, bf16[128,512]{1,0:T(8,128)(2,1)}, b...) custom-call(s32[1]{0:T(128)} %bitcast.me_ref, ...), custom_call_target="tpu_custom_call" | custom-call | bytes 2097156 | tf_op jit(solution)/shard_map/spread_cotangent/pallas_call | solution.py:40
  33.5 4.2 %collective-permute-done.2.refs_3_ = bf16[128,512]{1,0:T(8,128)(2,1)S(1)} collective-permute-done((bf16[128,512]{1,0:T(8,128)(2,1)}, bf16[128,512]{1,0:T(8,128)(2,1)S(1)}, u32[]{:S(2)}, u32[]{:S(2)}) %collective-permute-start.2) | collective-permute-done | bytes 131104 | tf_op jit(solution)/shard_map/ppermute | solution.py:666
  38.1 4.7 %collective-permute-done.3.refs_4_ = bf16[128,512]{1,0:T(8,128)(2,1)S(1)} collective-permute-done((bf16[128,512]{1,0:T(8,128)(2,1)}, bf16[128,512]{1,0:T(8,128)(2,1)S(1)}, u32[]{:S(2)}, u32[]{:S(2)}) %collective-permute-start.3) | collective-permute-done | bytes 131104 | tf_op jit(solution)/shard_map/ppermute | solution.py:666
  44.0 8.9 %collective-permute-done.4.refs_5_ = bf16[128,512]{1,0:T(8,128)(2,1)S(1)} collective-permute-done((bf16[128,512]{1,0:T(8,128)(2,1)}, bf16[128,512]{1,0:T(8,128)(2,1)S(1)}, u32[]{:S(2)}, u32[]{:S(2)}) %collective-permute-start.4) | collective-permute-done | bytes 131104 | tf_op jit(solution)/shard_map/ppermute | solution.py:666
  52.9 3.8 %collective-permute-done.5.refs_6_ = bf16[128,512]{1,0:T(8,128)(2,1)S(1)} collective-permute-done((bf16[128,512]{1,0:T(8,128)(2,1)}, bf16[128,512]{1,0:T(8,128)(2,1)S(1)}, u32[]{:S(2)}, u32[]{:S(2)}) %collective-permute-start.5) | collective-permute-done | bytes 131104 | tf_op jit(solution)/shard_map/ppermute | solution.py:666
  56.7 2.5 %collective-permute-done.6.refs_7_ = bf16[128,512]{1,0:T(8,128)(2,1)S(1)} collective-permute-done((bf16[128,512]{1,0:T(8,128)(2,1)}, bf16[128,512]{1,0:T(8,128)(2,1)S(1)}, u32[]{:S(2)}, u32[]{:S(2)}) %collective-permute-start.6) | collective-permute-done | bytes 131104 | tf_op jit(solution)/shard_map/ppermute | solution.py:666
  59.1 4.2 %collective-permute-done.7.refs_8_ = bf16[128,512]{1,0:T(8,128)(2,1)S(1)} collective-permute-done((bf16[128,512]{1,0:T(8,128)(2,1)}, bf16[128,512]{1,0:T(8,128)(2,1)S(1)}, u32[]{:S(2)}, u32[]{:S(2)}) %collective-permute-start.7) | collective-permute-done | bytes 131104 | tf_op jit(solution)/shard_map/ppermute | solution.py:666
  64.0 4.2 %pick_cotangent.1 = bf16[1024,512]{1,0:T(8,128)(2,1)} custom-call(s32[1]{0:T(128)} %bitcast.me_ref, s32[32,128]{1,0:T(8,128)} %bitcast.22, bf16[2,4,512,128]{3,2,1,0:T(8,128)(2,1)} %collective-permute-done.refs_0_.refs_1_, bf16[128,512]{1,0:T(8,128)(2,1)} %get-tuple-element.32.refs_1_, bf16[128,512]{1,0:T(8,128)(2,1)} %copy-done.5, ...), custom_call_target="tpu_custom_call" | custom-call | flops 1073741824 | bytes 3162116 | tf_op jit(solution)/shard_map/pick_cotangent/pallas_call | solution.py:40
  68.3 5.5 %all-to-all-start.1 = ((bf16[16,64,512]{2,1,0:T(8,128)(2,1)}), bf16[16,64,512]{2,1,0:T(8,128)(2,1)}, u32[]{:S(2)}, u32[]{:S(2)}) async-start(bf16[16,64,512]{2,1,0:T(8,128)(2,1)} %bitcast.20), calls=%async_computation.1 | async-start | bytes 2097152 | tf_op jit(solution)/shard_map/all_to_all | solution.py:660
  75.7 6.8 %forward.1 = (bf16[512,512]{1,0:T(8,128)(2,1)}, bf16[512,512]{1,0:T(8,128)(2,1)}, f32[512,512]{1,0:T(8,128)}, f32[512,512]{1,0:T(8,128)}, f32[128,512]{1,0:T(8,1...) custom-call(s32[1]{0:T(128)} %bitcast.4.order_ref, f32[192]{0:T(256)} %reshape.44.mix_ref, ...), custom_call_target="tpu_custom_call" | custom-call | flops 1073741824 | bytes 8127748 | tf_op jit(solution)/shard_map/forward/pallas_call | solution.py:40
  82.9 4.4 %collective-permute-done.8.refs_2_ = bf16[1,4,512,128]{3,2,1,0:T(8,128)(2,1)} collective-permute-done((bf16[1,4,512,128]{3,2,1,0:T(8,128)(2,1)}, bf16[1,4,512,128]{3,2,1,0:T(8,128)(2,1)}, u32[]{:S(2)}, u32[]{:S(2)}) %collective-permute-start.8) | collective-permute-done | bytes 524320 | tf_op jit(solution)/shard_map/ppermute | solution.py:631
  87.3 11.7 %all-to-all-done.1 = bf16[16,64,512]{2,1,0:T(8,128)(2,1)} async-done(((bf16[16,64,512]{2,1,0:T(8,128)(2,1)}), bf16[16,64,512]{2,1,0:T(8,128)(2,1)}, u32[]{:S(2)}, u32[]{:S(2)}) %all-to-all-start.1) | async-done | bytes 1048608 | tf_op jit(solution)/shard_map/all_to_all | solution.py:660
  99.8 8.6 %backward.1 = (bf16[384,2048]{1,0:T(8,128)(2,1)}, bf16[512,512]{1,0:T(8,128)(2,1)}, bf16[512,512]{1,0:T(8,128)(2,1)}, f32[512,512]{1,0:T(8,128)}, bf16[3,128,512]{2,1,0:T(8,128)(2,1)}, /*index=5*/f32[128,128]{1,0:T(8,128)}) custom-call(s32[1]{0:T(128)} %bitcast.4.order_ref, f32[192]{0:T(256)} %reshape.44.mix_ref, s32[1,128]{1,0:T(1,128)} %get-tuple-element.30.slot_ref, ...), custom_call_target="tpu_custom_call" | custom-call | flops 1610612736 | bytes 9635588 | tf_op jit(solution)/shard_map/backward/pallas_call | solution.py:40
  108.5 6.4 %all-to-all-start.3 = ((bf16[16,24,2048]{2,1,0:T(8,128)(2,1)}), bf16[16,24,2048]{2,1,0:T(8,128)(2,1)}, u32[]{:S(2)}, u32[]{:S(2)}) async-start(bf16[16,24,2048]{2,1,0:T(8,128)(2,1)} %bitcast.19), calls=%async_computation.3 | async-start | bytes 3145728 | tf_op jit(solution)/shard_map/all_to_all | solution.py:660
  116.4 1.8 %place_rows.1.placed_hbm = bf16[256,384]{1,0:T(8,128)(2,1)} custom-call(s32[1]{0:T(128)} %bitcast.me_ref, s32[32,128]{1,0:T(8,128)} %bitcast.23), custom_call_target="tpu_custom_call" | custom-call | flops 1048576 | bytes 212996 | tf_op jit(solution)/shard_map/place_rows/pallas_call | solution.py:40
  118.3 3.9 %mix_partials.1 = f32[192,128]{1,0:T(8,128)} custom-call(f32[512,512]{1,0:T(8,128)} %get-tuple-element.50.yg_hbm, f32[512,512]{1,0:T(8,128)} %get-tuple-element.51.yu_hbm, f32[512,512]{1,0:T(8,128)} %get-tuple-element.52.yd_hbm, bf16[3,128,512]{2,1,0:T(8,128)(2,1)} %get-tuple-element.48.refs_2_.d_hbm), custom_call_target="tpu_custom_call" | custom-call | flops 6291456 | bytes 3637248 | tf_op jit(solution)/shard_map/mix_partials/pallas_call | solution.py:40
  126.0 11.3 %collective-permute-done.12 = f32[1,3,4,4,4]{4,3,2,1,0:T(4,128)S(1)} collective-permute-done((f32[1,3,4,4,4]{4,3,2,1,0:T(4,128)S(1)}, f32[1,3,4,4,4]{4,3,2,1,0:T(4,128)S(1)}, u32[]{:S(2)}, u32[]{:S(2)}) %collective-permute-start.12) | collective-permute-done | bytes 800 | tf_op jit(solution)/shard_map/ppermute | solution.py:631
  138.8 7.8 %factor_grad.1 = f32[3,4,512,128]{3,2,1,0:T(8,128)} custom-call(f32[192]{0:T(256)} %reshape.44.mix_ref, bf16[512,512]{1,0:T(8,128)(2,1)} %get-tuple-element.46.refs_0_, bf16[512,512]{1,0:T(8,128)(2,1)} %get-tuple-element.47.refs_1_, bf16[3,128,512]{2,1,0:T(8,128)(2,1)} %get-tuple-element.48.refs_2_.d_hbm, bf16[512,512]{1,0:T(8,128)(2,1)} %copy-done.1, ...), custom_call_target="tpu_custom_call" | custom-call | flops 1610612736 | bytes 6030080 | tf_op jit(solution)/shard_map/factor_grad/pallas_call | solution.py:40
  146.6 4.5 %all-to-all-done.3 = bf16[16,24,2048]{2,1,0:T(8,128)(2,1)} async-done(((bf16[16,24,2048]{2,1,0:T(8,128)(2,1)}), bf16[16,24,2048]{2,1,0:T(8,128)(2,1)}, u32[]{:S(2)}, u32[]{:S(2)}) %all-to-all-start.3) | async-done | bytes 1572896 | tf_op jit(solution)/shard_map/all_to_all | solution.py:660
  151.2 3.1 %sum_rows.1 = bf16[128,4096]{1,0:T(8,128)(2,1)} custom-call(bf16[256,384]{1,0:T(8,128)(2,1)} %place_rows.1.placed_hbm, bf16[384,2048]{1,0:T(8,128)(2,1)} %bitcast.12.returned_ref), custom_call_target="tpu_custom_call" | custom-call | flops 402653184 | bytes 2818048 | tf_op jit(solution)/shard_map/sum_rows/pallas_call | solution.py:40
  (51 shorter events, 19.3 us)
Async XLA Ops:
  16.6 51.7 %all-to-all-start.2 = ((bf16[16,24,2048]{2,1,0:T(8,128)(2,1)}), bf16[16,24,2048]{2,1,0:T(8,128)(2,1)}, u32[]{:S(2)}, u32[]{:S(2)}) async-start(bf16[16,24,2048]{2,1,0:T(8,128)(2,1)} %bitcast.14), calls=%async_computation.2 | async-start | bytes 3145728 | tf_op jit(solution)/shard_map/all_to_all | solution.py:660
  25.7 37.7 %collective-permute-start = (bf16[2,4,512,128]{3,2,1,0:T(8,128)(2,1)}, bf16[2,4,512,128]{3,2,1,0:T(8,128)(2,1)}, u32[]{:S(2)}, u32[]{:S(2)}) collective-permute-start(bf16[2,4,512,128]{3,2,1,0:T(8,128)(2,1)} %get-tuple-element.31), channel_id=1, source_target_pairs={{0,16},{16,0},{1,17},{17,1},{2,18},{18,2},{3,19},{19,3},{4,20},{20... | collective-permute-start | bytes 3145736 | tf_op jit(solution)/shard_map/ppermute | solution.py:631
  29.2 2.7 %collective-permute-start.1 = (bf16[128,512]{1,0:T(8,128)(2,1)}, bf16[128,512]{1,0:T(8,128)(2,1)S(1)}, u32[]{:S(2)}, u32[]{:S(2)}) collective-permute-start(bf16[128,512]{1,0:T(8,128)(2,1)} %get-tuple-element.33), channel_id=1, source_target_pairs={{0,1},{1,0},{2,3},{3,2},{4,5},{5,4},{6,7},{7,6},{8,9},{9,8},{10,11... | collective-permute-start | bytes 393224 | tf_op jit(solution)/shard_map/ppermute | solution.py:666
  29.9 7.7 %collective-permute-start.2 = (bf16[128,512]{1,0:T(8,128)(2,1)}, bf16[128,512]{1,0:T(8,128)(2,1)S(1)}, u32[]{:S(2)}, u32[]{:S(2)}) collective-permute-start(bf16[128,512]{1,0:T(8,128)(2,1)} %get-tuple-element.34), channel_id=1, source_target_pairs={{0,2},{1,3},{2,0},{3,1},{4,6},{5,7},{6,4},{7,5},{8,10},{9,11},{10,... | collective-permute-start | bytes 393224 | tf_op jit(solution)/shard_map/ppermute | solution.py:666
  30.2 12.6 %collective-permute-start.3 = (bf16[128,512]{1,0:T(8,128)(2,1)}, bf16[128,512]{1,0:T(8,128)(2,1)S(1)}, u32[]{:S(2)}, u32[]{:S(2)}) collective-permute-start(bf16[128,512]{1,0:T(8,128)(2,1)} %get-tuple-element.35), channel_id=1, source_target_pairs={{0,3},{1,2},{2,1},{3,0},{4,7},{5,6},{6,5},{7,4},{8,11},{9,10},{10,... | collective-permute-start | bytes 393224 | tf_op jit(solution)/shard_map/ppermute | solution.py:666
  31.6 21.2 %collective-permute-start.4 = (bf16[128,512]{1,0:T(8,128)(2,1)}, bf16[128,512]{1,0:T(8,128)(2,1)S(1)}, u32[]{:S(2)}, u32[]{:S(2)}) collective-permute-start(bf16[128,512]{1,0:T(8,128)(2,1)} %get-tuple-element.36), channel_id=1, source_target_pairs={{0,4},{1,5},{2,6},{3,7},{4,0},{5,1},{6,2},{7,3},{8,12},{9,13},{10,... | collective-permute-start | bytes 393224 | tf_op jit(solution)/shard_map/ppermute | solution.py:666
  31.9 31.5 %copy-start.5 = (bf16[128,512]{1,0:T(8,128)(2,1)}, bf16[128,512]{1,0:T(8,128)(2,1)S(1)}, u32[]{:S(2)}) copy-start(bf16[128,512]{1,0:T(8,128)(2,1)S(1)} %collective-permute-done.1.refs_2_) | copy-start | bytes 393220
  31.9 24.7 %collective-permute-start.5 = (bf16[128,512]{1,0:T(8,128)(2,1)}, bf16[128,512]{1,0:T(8,128)(2,1)S(1)}, u32[]{:S(2)}, u32[]{:S(2)}) collective-permute-start(bf16[128,512]{1,0:T(8,128)(2,1)} %get-tuple-element.37), channel_id=1, source_target_pairs={{0,5},{1,4},{2,7},{3,6},{4,1},{5,0},{6,3},{7,2},{8,13},{9,12},{10,... | collective-permute-start | bytes 393224 | tf_op jit(solution)/shard_map/ppermute | solution.py:666
  37.6 25.8 %copy-start.6 = (bf16[128,512]{1,0:T(8,128)(2,1)}, bf16[128,512]{1,0:T(8,128)(2,1)S(1)}, u32[]{:S(2)}) copy-start(bf16[128,512]{1,0:T(8,128)(2,1)S(1)} %collective-permute-done.2.refs_3_) | copy-start | bytes 393220
  37.6 21.5 %collective-permute-start.6 = (bf16[128,512]{1,0:T(8,128)(2,1)}, bf16[128,512]{1,0:T(8,128)(2,1)S(1)}, u32[]{:S(2)}, u32[]{:S(2)}) collective-permute-start(bf16[128,512]{1,0:T(8,128)(2,1)} %get-tuple-element.38), channel_id=1, source_target_pairs={{0,6},{1,7},{2,4},{3,5},{4,2},{5,3},{6,0},{7,1},{8,14},{9,15},{10,... | collective-permute-start | bytes 393224 | tf_op jit(solution)/shard_map/ppermute | solution.py:666
  42.8 20.6 %copy-start.7 = (bf16[128,512]{1,0:T(8,128)(2,1)}, bf16[128,512]{1,0:T(8,128)(2,1)S(1)}, u32[]{:S(2)}) copy-start(bf16[128,512]{1,0:T(8,128)(2,1)S(1)} %collective-permute-done.3.refs_4_) | copy-start | bytes 393220
  42.8 20.6 %collective-permute-start.7 = (bf16[128,512]{1,0:T(8,128)(2,1)}, bf16[128,512]{1,0:T(8,128)(2,1)S(1)}, u32[]{:S(2)}, u32[]{:S(2)}) collective-permute-start(bf16[128,512]{1,0:T(8,128)(2,1)} %get-tuple-element.39), channel_id=1, source_target_pairs={{0,7},{1,6},{2,5},{3,4},{4,3},{5,2},{6,1},{7,0},{8,15},{9,14},{10,... | collective-permute-start | bytes 393224 | tf_op jit(solution)/shard_map/ppermute | solution.py:666
  52.9 10.5 %copy-start.8 = (bf16[128,512]{1,0:T(8,128)(2,1)}, bf16[128,512]{1,0:T(8,128)(2,1)S(1)}, u32[]{:S(2)}) copy-start(bf16[128,512]{1,0:T(8,128)(2,1)S(1)} %collective-permute-done.4.refs_5_) | copy-start | bytes 393220
  56.7 6.8 %copy-start.9 = (bf16[128,512]{1,0:T(8,128)(2,1)}, bf16[128,512]{1,0:T(8,128)(2,1)S(1)}, u32[]{:S(2)}) copy-start(bf16[128,512]{1,0:T(8,128)(2,1)S(1)} %collective-permute-done.5.refs_6_) | copy-start | bytes 393220
  68.3 6.8 %copy-start.4 = (f32[1,3,4,4,4]{4,3,2,1,0:T(4,128)S(1)}, f32[1,3,4,4,4]{4,3,2,1,0:T(4,128)}, u32[]{:S(2)}) copy-start(f32[1,3,4,4,4]{4,3,2,1,0:T(4,128)} %param.9) | copy-start | bytes 2308
  68.3 30.7 %all-to-all-start.1 = ((bf16[16,64,512]{2,1,0:T(8,128)(2,1)}), bf16[16,64,512]{2,1,0:T(8,128)(2,1)}, u32[]{:S(2)}, u32[]{:S(2)}) async-start(bf16[16,64,512]{2,1,0:T(8,128)(2,1)} %bitcast.20), calls=%async_computation.1 | async-start | bytes 2097152 | tf_op jit(solution)/shard_map/all_to_all | solution.py:660
  73.8 13.5 %collective-permute-start.8 = (bf16[1,4,512,128]{3,2,1,0:T(8,128)(2,1)}, bf16[1,4,512,128]{3,2,1,0:T(8,128)(2,1)}, u32[]{:S(2)}, u32[]{:S(2)}) collective-permute-start(bf16[1,4,512,128]{3,2,1,0:T(8,128)(2,1)} %get-tuple-element.43), channel_id=1, source_target_pairs={{0,16},{16,0},{1,17},{17,1},{2,18},{18,2},{3,19},{19,3},{4,20},{20... | collective-permute-start | bytes 1572872 | tf_op jit(solution)/shard_map/ppermute | solution.py:631
  82.6 16.4 %collective-permute-start.9 = (bf16[512,512]{1,0:T(8,128)(2,1)}, bf16[512,512]{1,0:T(8,128)(2,1)S(1)}, u32[]{:S(2)}, u32[]{:S(2)}) collective-permute-start(bf16[512,512]{1,0:T(8,128)(2,1)} %get-tuple-element.44), channel_id=1, source_target_pairs={{0,16},{16,0},{1,17},{17,1},{2,18},{18,2},{3,19},{19,3},{4,20},{20... | collective-permute-start | bytes 1572872 | tf_op jit(solution)/shard_map/ppermute | solution.py:631
  108.5 7.7 %copy-start = (bf16[3,128,512]{2,1,0:T(8,128)(2,1)S(1)}, bf16[3,128,512]{2,1,0:T(8,128)(2,1)}, u32[]{:S(2)}) copy-start(bf16[3,128,512]{2,1,0:T(8,128)(2,1)} %get-tuple-element.48.refs_2_.d_hbm) | copy-start | bytes 1179652
  108.5 42.7 %all-to-all-start.3 = ((bf16[16,24,2048]{2,1,0:T(8,128)(2,1)}), bf16[16,24,2048]{2,1,0:T(8,128)(2,1)}, u32[]{:S(2)}, u32[]{:S(2)}) async-start(bf16[16,24,2048]{2,1,0:T(8,128)(2,1)} %bitcast.19), calls=%async_computation.3 | async-start | bytes 3145728 | tf_op jit(solution)/shard_map/all_to_all | solution.py:660
  114.9 23.1 %collective-permute-start.10 = (bf16[512,512]{1,0:T(8,128)(2,1)}, bf16[512,512]{1,0:T(8,128)(2,1)S(1)}, u32[]{:S(2)}, u32[]{:S(2)}) collective-permute-start(bf16[512,512]{1,0:T(8,128)(2,1)} %get-tuple-element.49), channel_id=1, source_target_pairs={{0,16},{16,0},{1,17},{17,1},{2,18},{18,2},{3,19},{19,3},{4,20},{20... | collective-permute-start | bytes 1572872 | tf_op jit(solution)/shard_map/ppermute | solution.py:631
  116.1 21.8 %collective-permute-start.11 = (bf16[3,128,512]{2,1,0:T(8,128)(2,1)S(1)}, bf16[3,128,512]{2,1,0:T(8,128)(2,1)}, u32[]{:S(2)}, u32[]{:S(2)}) collective-permute-start(bf16[3,128,512]{2,1,0:T(8,128)(2,1)S(1)} %copy-done), channel_id=1, source_target_pairs={{0,16},{16,0},{1,17},{17,1},{2,18},{18,2},{3,19},{19,3},{4,20},{20... | collective-permute-start | bytes 1179656 | tf_op jit(solution)/shard_map/ppermute | solution.py:631
  118.3 6.3 %copy-start.3 = (f32[128,128]{1,0:T(8,128)S(1)}, f32[128,128]{1,0:T(8,128)}, u32[]{:S(2)}) copy-start(f32[128,128]{1,0:T(8,128)} %get-tuple-element.53) | copy-start | bytes 196612
  123.3 14.1 %collective-permute-start.12 = (f32[1,3,4,4,4]{4,3,2,1,0:T(4,128)S(1)}, f32[1,3,4,4,4]{4,3,2,1,0:T(4,128)S(1)}, u32[]{:S(2)}, u32[]{:S(2)}) collective-permute-start(f32[1,3,4,4,4]{4,3,2,1,0:T(4,128)S(1)} %reshape.51), channel_id=1, source_target_pairs={{0,16},{16,0},{1,17},{17,1},{2,18},{18,2},{3,19},{19,3},{4,20},{20... | collective-permute-start | bytes 2312 | tf_op jit(solution)/shard_map/ppermute | solution.py:631
  (4 other events, 6.5 us)

commit v10 on v8

--- a/solution.py
+++ b/solution.py
@@ -72,26 +72,37 @@
     return [begin(source, target, sems.at[n]) for n, (source, target) in enumerate(pairs)]
 
 
-def spread_columns(me, sources, half, direct, name):
-    own_rows, width = sources[0].shape
-    count = len(sources)
+INFO = 16
+DIGIT = 6
+
+
+def spread_columns(me, source, chosen, half, direct, name):
+    own_rows, width = source.shape
     part = width // half
-    tall = count * own_rows
-
-    def body(me_ref, *refs):
-        ins, outs = refs[:count], refs[count : -3]
-        held_ref, in_sem, out_sem = refs[-3:]
-        loads = [begin(ref, held_ref.at[n], in_sem.at[n]) for n, ref in enumerate(ins)]
+    tall = own_rows + (INFO if chosen else 0)
+
+    def body(me_ref, source_ref, *refs):
+        chosen_refs, outs = refs[: len(chosen)], refs[len(chosen) : -4]
+        held_ref, info_ref, in_sem, out_sem = refs[-4:]
+        load = begin(source_ref, held_ref, in_sem)
+        if chosen:
+            digits = []
+            for ref in chosen_refs:
+                row = jnp.concatenate([ref[b : b + 1, :] for b in range(ref.shape[0])], axis=1)
+                digits += [lax.shift_right_logical(row, DIGIT), row & ((1 << DIGIT) - 1)]
+            info = jnp.concatenate(digits, axis=1).astype(F32)
+            info_ref[...] = jnp.broadcast_to(info, info_ref.shape).astype(BF16)
         low = me_ref[0] & (half - 1)
+        load.wait()
         copies = []
-        for n, load in enumerate(loads):
-            load.wait()
-            for k in range(half):
-                share = low ^ k if direct else k
-                at = held_ref.at[n, :, pl.ds(pl.multiple_of(share * part, part), part)]
-                out, first = (outs[k], 0) if direct else (outs[0], k * tall)
-                rows = pl.ds(first + n * own_rows, own_rows)
-                copies.append(begin(at, out.at[rows], out_sem.at[n, k]))
+        for k in range(half):
+            share = low ^ k if direct else k
+            at = held_ref.at[:, pl.ds(pl.multiple_of(share * part, part), part)]
+            out, first = (outs[k], 0) if direct else (outs[0], k * tall)
+            copies.append(begin(at, out.at[pl.ds(first, own_rows)], out_sem.at[0, k]))
+            if chosen:
+                at = out.at[pl.ds(first + own_rows, INFO)]
+                copies.append(begin(info_ref, at, out_sem.at[1, k]))
         wait_all(copies)
 
     if direct:
@@ -99,93 +110,145 @@
     else:
         outs = [(shaped((half * tall, part), BF16), HBM)]
     scratch = [
-        scratch_like((count, own_rows, width), BF16),
-        pltpu.SemaphoreType.DMA((count,)),
-        pltpu.SemaphoreType.DMA((count, half)),
+        scratch_like((own_rows, width), BF16),
+        scratch_like((INFO, part), BF16),
+        pltpu.SemaphoreType.DMA,
+        pltpu.SemaphoreType.DMA((2, half)),
     ]
-    return call(body, outs, [(me, SMEM)] + [(x, HBM) for x in sources], name, 0, scratch)
-
-
-def share_selection(chosen, peers):
-    def body(chosen_ref, out_ref):
-        blocks = [chosen_ref[b : b + 1, :] for b in range(chosen_ref.shape[0])]
-        out_ref[...] = jnp.broadcast_to(jnp.concatenate(blocks, axis=1), out_ref.shape)
-
-    out = (shaped((peers, chosen.size), jnp.int32), VMEM)
-    return call(body, [out], [(chosen, VMEM)], "share_selection", 0)[0]
-
-
-def cut_factors(factors):
-    weights = factors.shape[0]
+    ins = [(me, SMEM), (source, HBM)] + [(x, VMEM) for x in chosen]
+    return call(body, outs, ins, name, 0, scratch)
+
+
+def cut_factors(factors, first):
+    cuts = (slice(0, first), slice(first, factors.shape[0]))
 
     def body(factors_ref, *refs):
-        outs, (held_ref, sems) = refs[:weights], refs[weights:]
+        outs, (held_ref, sems) = refs[:2], refs[2:]
         loads = [
-            begin(factors_ref.at[m], held_ref.at[m], sems.at[0, m]) for m in range(weights)
+            begin(factors_ref.at[at], held_ref.at[at], sems.at[0, n]) for n, at in enumerate(cuts)
         ]
         copies = []
-        for m, load in enumerate(loads):
-            load.wait()
-            copies.append(begin(held_ref.at[m], outs[m], sems.at[1, m]))
+        for n, at in enumerate(cuts):
+            loads[n].wait()
+            copies.append(begin(held_ref.at[at], outs[n], sems.at[1, n]))
         wait_all(copies)
 
-    outs = [(shaped(factors.shape[1:], BF16), HBM)] * weights
-    scratch = [scratch_like(factors.shape, BF16), pltpu.SemaphoreType.DMA((2, weights))]
+    outs = [
+        (shaped((at.stop - at.start,) + factors.shape[1:], BF16), HBM) for at in cuts
+    ]
+    scratch = [scratch_like(factors.shape, BF16), pltpu.SemaphoreType.DMA((2, 2))]
     return call(body, outs, [(factors, HBM)], "cut_factors", 0, scratch)
 
 
-def pick_rows(me, half, own_rows, which, chosen, shares, after, name):
+def mark_rows(target_ref, first, count, picks, block, block_at, chosen_ref):
+    total = chosen_ref.shape[1]
+    same = iota((picks, total), 0) + block_at * picks == iota((picks, total), 1)
+    for e in range(count):
+        wanted = chosen_ref[first + e : first + e + 1, :]
+        column = jnp.sum(jnp.where(same, wanted, 0), axis=1, keepdims=True)
+        target_ref[e * picks : (e + 1) * picks] = (column == iota((picks, block), 1)).astype(BF16)
+
+
+def mark_all(me, half, own_rows, chosen):
     peers, total = chosen.shape
-    picks = total * half // peers
+    picks, block = total * half // peers, half * own_rows
+    batch = min(peers, 8)
+
+    def body(me_ref, chosen_ref, out_ref, mark_ref, sems):
+        block_at = lax.shift_right_logical(me_ref[0], half.bit_length() - 1)
+        copies = []
+        for n in range(peers // batch):
+            if n > 1:
+                copies[n - 2].wait()
+            slot = mark_ref.at[n % 2]
+            mark_rows(slot, n * batch, batch, picks, block, block_at, chosen_ref)
+            at = out_ref.at[n * batch * picks : (n + 1) * batch * picks]
+            copies.append(begin(slot, at, sems.at[n]))
+        wait_all(copies[-2:])
+
+    return call(
+        body,
+        [(shaped((peers * picks, block), BF16), HBM)],
+        [(me, SMEM), (chosen, VMEM)],
+        "mark_rows",
+        1 << 20,
+        [scratch_like((2, batch * picks, block), BF16), pltpu.SemaphoreType.DMA((peers // batch,))],
+    )[0]
+
+
+def pick_rows(me, half, own_rows, peers, total, shares, chosen, marks, after, name):
+    picks, block = total * half // peers, half * own_rows
     part = shares[0].shape[1]
-    block = half * own_rows
     tall = sum(x.shape[0] for x in shares) // half
     batch = min(peers, 8)
-
-    def body(me_ref, chosen_ref, *refs):
-        refs = refs[len(after) :]
-        parts, (out_ref, rows_ref, pick_ref, sent_ref, in_sem, out_sem) = (
-            refs[: len(shares)],
-            refs[len(shares) :],
-        )
-        loads = []
+    told = [] if chosen is None else [(chosen, VMEM)]
+    told = told if marks is None else [(marks, HBM)]
+
+    def body(me_ref, *refs):
+        told_refs, refs = refs[: len(told)], refs[len(told) + len(after) :]
+        parts, refs = refs[: len(shares)], refs[len(shares) :]
+        out_ref, refs = refs[0], refs[1:]
+        if not told:
+            chosen_ref, refs = refs[0], refs[1:]
+        elif marks is None:
+            chosen_ref = told_refs[0]
+        rows_ref, mark_ref, sent_ref, info_ref, in_sem, mark_sem, out_sem = refs
+        low = me_ref[0] & (half - 1)
+        block_at = lax.shift_right_logical(me_ref[0], half.bit_length() - 1)
+        infos, loads, marks_in = [], [], []
+        if not told:
+            for k in range(half):
+                at = parts[k].at[own_rows : own_rows + INFO]
+                infos.append(begin(at, info_ref.at[k], in_sem.at[1, k]))
         for k in range(half):
-            place = (me_ref[0] & (half - 1)) ^ k if len(parts) > 1 else k
+            place = low ^ k if len(parts) > 1 else k
             share, first = (parts[k], 0) if len(parts) > 1 else (parts[0], k * tall)
-            first += which * own_rows
             target = rows_ref.at[pl.ds(pl.multiple_of(place * own_rows, own_rows), own_rows)]
-            loads.append(begin(share.at[first : first + own_rows], target, in_sem.at[k]))
-        block_at = lax.shift_right_logical(me_ref[0], half.bit_length() - 1)
-        same = iota((picks, total), 0) + block_at * picks == iota((picks, total), 1)
+            loads.append(begin(share.at[first : first + own_rows], target, in_sem.at[0, k]))
+        if marks is not None:
+            for n in range(peers // batch):
+                at = slice(n * batch * picks, (n + 1) * batch * picks)
+                marks_in.append(begin(told_refs[0].at[at], mark_ref.at[at], mark_sem.at[n]))
+        for k, copy in enumerate(infos):
+            copy.wait()
+            info = info_ref[k].astype(F32)[0:1, :].astype(jnp.int32)
+            for n in range(2):
+                high = info[:, 2 * n * total : (2 * n + 1) * total]
+                rest = info[:, (2 * n + 1) * total : (2 * n + 2) * total]
+                expert = (low ^ k) + (block_at ^ n) * half
+                chosen_ref[pl.ds(expert, 1), :] = high * (1 << DIGIT) + rest
         stores = []
-        for first in range(0, peers, batch):
-            for e in range(batch):
-                wanted = chosen_ref[first + e : first + e + 1, :]
-                column = jnp.sum(jnp.where(same, wanted, 0), axis=1, keepdims=True)
-                pick_ref[first // batch % 2, e * picks : (e + 1) * picks] = (
-                    column == iota((picks, block), 1)
-                ).astype(BF16)
-            if first == 0:
+        for n in range(peers // batch):
+            at = slice(n * batch * picks, (n + 1) * batch * picks)
+            if marks is None:
+                mark_rows(mark_ref.at[at], n * batch, batch, picks, block, block_at, chosen_ref)
+            else:
+                marks_in[n].wait()
+            if n == 0:
                 wait_all(loads)
-            at = slice(first * picks, (first + batch) * picks)
-            sent_ref[at] = dot(pick_ref[first // batch % 2], rows_ref[...]).astype(BF16)
-            stores.append(begin(sent_ref.at[at], out_ref.at[at], out_sem.at[first // batch]))
+            sent_ref[at] = dot(mark_ref[at], rows_ref[...]).astype(BF16)
+            stores.append(begin(sent_ref.at[at], out_ref.at[at], out_sem.at[n]))
         wait_all(stores)
 
+    outs = [(shaped((peers * picks, part), BF16), HBM)]
+    if not told:
+        outs.append((shaped((peers, total), jnp.int32), VMEM))
     return call(
         body,
-        [(shaped((peers * picks, part), BF16), HBM)],
-        [(me, SMEM), (chosen, VMEM)] + [(x, HBM) for x in list(after) + list(shares)],
+        outs,
+        [(me, SMEM)] + told + [(x, HBM) for x in list(after) + list(shares)],
         name,
         2 * peers * picks * block * part,
         [
             scratch_like((block, part), BF16),
-            scratch_like((2, batch * picks, block), BF16),
+            scratch_like((peers * picks, block), BF16),
             scratch_like((peers * picks, part), BF16),
-            pltpu.SemaphoreType.DMA((half,)),
+            scratch_like((half, INFO, part), BF16),
+            pltpu.SemaphoreType.DMA((2, half)),
+            pltpu.SemaphoreType.DMA((peers // batch,)),
             pltpu.SemaphoreType.DMA((peers // batch,)),
         ],
-    )[0]
+    )
 
 
 def slot_body(cap, pieces, own_rows, block_len, chosen_ref, slot_ref):
@@ -280,7 +343,11 @@
 
 def load_factor(order_ref, parts, m, target, sems):
     copies = []
-    for n, side in enumerate((parts[0].at[m], parts[1 + m]) if len(parts) > 1 else (parts[0].at[m],)):
+    sides = [parts[0].at[m]]
+    if len(parts) > 1:
+        first = parts[1].shape[0]
+        sides.append(parts[1].at[m] if m < first else parts[2].at[m - first])
+    for n, side in enumerate(sides):
         count, rows, cols = side.shape
         place = order_ref[0] ^ n if len(parts) > 1 else 0
         start = pl.multiple_of(place * rows, rows)
@@ -324,7 +391,7 @@
     return copies
 
 
-STRIP = 32
+STRIP = 64
 
 
 def mix_in(mix_ref, m, y_ref, emit):
@@ -368,7 +435,7 @@
 def forward_body(
     sides, order_ref, mix_ref, got_hbm, *refs
 ):
-    held = 3 if sides > 1 else 1
+    held = 2 if sides > 1 else 1
     parts, refs = refs[:held], refs[held:]
     x_outs, refs = refs[:sides], refs[sides:]
     yg_hbm, yu_hbm, act_hbm, slope_hbm, hid_hbm = refs[:5]
@@ -414,7 +481,7 @@
     cap, pieces, sides, after, order_ref, mix_ref, slot_ref, score_ref, got_hbm, act_hbm, slope_hbm, hid_hbm,
     *refs,
 ):
-    held = 4 if sides > 1 else 1
+    held = 3 if sides > 1 else 1
     parts, refs = refs[:held], refs[held + after :]
     back_hbm, x_outs, refs = refs[0], refs[1 : 1 + sides], refs[1 + sides :]
     y_hbm, d_hbm, inner_ref = refs[:3]
@@ -552,11 +619,8 @@
     halves = [list(range(h, h + half)) for h in range(0, peers, half)]
     near = [k for k in range(1, half) if k >= 4] + [k for k in range(1, half) if k < 4]
 
-    shares = spread_columns(me, [tokens, cotangent], half, direct, "spread_columns")
-    cuts = cut_factors(factors[0])
-    wanted = share_selection(selection[0], peers)
     if swap:
-        cuts = [across(x) for x in cuts]
+        cuts = [across(x) for x in cut_factors(factors[0], 2)]
         factor_parts = [factors[0]] + cuts
         sides = 2
     else:
@@ -564,8 +628,6 @@
         factor_parts = [lax.all_gather(factors, "seq", axis=3, tiled=True)[0]]
         sides = 1
     sides_in = [(x, HBM) for x in factor_parts]
-    chosen = lax.all_to_all(wanted, "exp", split_axis=0, concat_axis=0, tiled=True)
-
     def to_peers(array):
         array = array.reshape(peers, -1, array.shape[1])
         array = lax.all_to_all(array, "exp", split_axis=0, concat_axis=0, tiled=True)
@@ -583,10 +645,22 @@
         )
         return [array.reshape(shares[0].shape)]
 
-    shares = collect(shares)
-    pick = functools.partial(pick_rows, me, half, own_rows)
-    got_rows = to_peers(pick(0, chosen, shares, cuts[:1], "pick_tokens"))
-    got_grads = to_peers(pick(1, chosen, shares, cuts[1:2], "pick_cotangent"))
+    spread = functools.partial(spread_columns, me, half=half, direct=direct)
+    pick = functools.partial(pick_rows, me, half, own_rows, peers, rows)
+    if direct:
+        mirror = lax.ppermute(selection, "exp", [(n, n ^ half) for n in range(peers)])
+        told = [selection[0], mirror[0]]
+        shares = collect(spread(tokens, told, name="spread_tokens"))
+        picked, chosen = pick(shares, None, None, [], "pick_tokens")
+        marks = mark_all(me, half, own_rows, chosen)
+    else:
+        told = jnp.broadcast_to(selection.reshape(1, rows), (peers, rows))
+        chosen = lax.all_to_all(told, "exp", split_axis=0, concat_axis=0, tiled=True)
+        shares = collect(spread(tokens, [], name="spread_tokens"))
+        (picked,), marks = pick(shares, chosen, None, [], "pick_tokens"), None
+    got_rows = to_peers(picked)
+    shares = collect(spread(cotangent, [], name="spread_cotangent"))
+    got_grads = to_peers(pick(shares, chosen, marks, cuts[:1], "pick_cotangent")[0])
     placed = place_rows(cap, pieces, own_rows, me, half, chosen)
     slot = call(
         functools.partial(slot_body, cap, pieces, own_rows, block_len),
@@ -611,7 +685,7 @@
     outs = call(
         functools.partial(forward_body, sides),
         split + [mixed, mixed, flat, flat, flat],
-        [(group, SMEM), (mixing, SMEM), (got_rows, HBM)] + sides_in[:3],
+        [(group, SMEM), (mixing, SMEM), (got_rows, HBM)] + sides_in[:2],
         "forward",
         2 * product,
         [scratch_like((2, depth, hidden), BF16), stack_scratch, mixed_scratch, mixed_scratch]

time: 159 us -> 159 us (level)
  blocking collectives: 15.9 us -> 0 us
  starting transfers between devices: 27.9 us -> 42 us
  Pallas kernels: 47.2 us -> 50.9 us
    ppermute x7 -> x14, waiting for transfers between devices: 6.9 us -> 25.3 us  [collect(): lax.ppermute(shares[k], 'exp', [(n, n ^ k) for n in range(peers)])]
    all_to_all x3, waiting for transfers between devices: 23 us -> 5.09 us  [to_peers(): lax.all_to_all(array, 'exp', split_axis=0, concat_axis=0, tiled=True)]
    all_to_all x1 -> x0, blocking collectives: 15.9 us -> none  [shards(): lax.all_to_all(wanted, 'exp', split_axis=0, concat_axis=0, tiled=True)]
    ppermute x7 -> x14, starting transfers between devices: 4.6 us -> 15.6 us  [collect(): lax.ppermute(shares[k], 'exp', [(n, n ^ k) for n in range(peers)])]
    pallas_call x12 -> x13, Pallas kernels: 47.2 us -> 50.9 us  [call(): pl.pallas_call(body, out_shape=[x for x, _ in outs], in_specs=[place for...]
    ppermute x7 -> x6, waiting for transfers between devices: 29.2 us -> 26.6 us  [across(): return lax.ppermute(array, 'seq', pair)]
    ppermute x0 -> x1, starting transfers between devices: none -> 2.37 us  [shards(): lax.ppermute(selection, 'exp', [(n, n ^ half) for n in range(peers)])]
    unnamed x18 -> x38, local copies, waits for them, and re-layouts: 3.19 us -> 2.41 us
  transfers between devices with their start and end apart: 17 -> 24, of which waited for: 8 -> 17; matrix products, arithmetic and copies ran while one was open for 2% -> 2% of each run, Pallas kernels for 18% -> 20%
where the time goes in v10:
time: 159 us; the launch traced here: 158 us
  waiting for transfers between devices  58.2 us (37%)
  Pallas kernels  50.9 us (32%)
  starting transfers between devices  42 us (26%)
  local copies, waits for them, and re-layouts  3.23 us (2%)
  other arithmetic  2.99 us (2%)
    pallas_call x13, Pallas kernels, call(): pl.pallas_call(body, out_shape=[x for x, _ in outs], in_specs=[place for...  50.9 us
    ppermute x6, waiting for transfers between devices, across(): return lax.ppermute(array, 'seq', pair)  26.6 us
    ppermute x14, waiting for transfers between devices, collect(): lax.ppermute(shares[k], 'exp', [(n, n ^ k) for n in range(peers)])  25.3 us
    all_to_all x3, starting transfers between devices, to_peers(): lax.all_to_all(array, 'exp', split_axis=0, concat_axis=0, tiled=True)  18.4 us
    ppermute x14, starting transfers between devices, collect(): lax.ppermute(shares[k], 'exp', [(n, n ^ k) for n in range(peers)])  15.6 us
    ppermute x6, starting transfers between devices, across(): return lax.ppermute(array, 'seq', pair)  5.62 us
    all_to_all x3, waiting for transfers between devices, to_peers(): lax.all_to_all(array, 'exp', split_axis=0, concat_axis=0, tiled=True)  5.09 us
  transfers between devices with their start and end apart: 24, of which 17 were waited for; matrix products, arithmetic and copies ran while one was open for 2% of the time, Pallas kernels for 20%

profile of v10, /device:TPU:13, one launch (start us, length us, event | category | flops | bytes accessed | tf_op | source)
XLA Modules:
  0.0 158.4 jit_solution(6111977277148007928)
XLA Ops:
  0.6 2.4 %collective-permute-start = (s32[1,2,64]{2,1,0:T(2,128)}, s32[1,2,64]{2,1,0:T(2,128)S(1)}, u32[]{:S(2)}, u32[]{:S(2)}) collective-permute-start(s32[1,2,64]{2,1,0:T(2,128)} %param.10), channel_id=1, source_target_pairs={{0,8},{1,9},{2,10},{3,11},{4,12},{5,13},{6,14},{7,15},{8,0},{9,1},... | collective-permute-start | bytes 1544 | tf_op jit(solution)/shard_map/ppermute | solution.py:651
  4.8 3.1 %spread_tokens.1 = (bf16[144,512]{1,0:T(8,128)(2,1)}, bf16[144,512]{1,0:T(8,128)(2,1)}, bf16[144,512]{1,0:T(8,128)(2,1)}, bf16[144,512]{1,0:T(8,128)(2,1)}, bf16...) custom-call(s32[1]{0:T(128)} %bitcast.me_ref, ...), custom_call_target="tpu_custom_call" | custom-call | bytes 2229252 | tf_op jit(solution)/shard_map/spread_tokens/pallas_call | solution.py:40
  16.3 2.7 %collective-permute-done.3.refs_3_ = bf16[144,512]{1,0:T(8,128)(2,1)S(1)} collective-permute-done((bf16[144,512]{1,0:T(8,128)(2,1)}, bf16[144,512]{1,0:T(8,128)(2,1)S(1)}, u32[]{:S(2)}, u32[]{:S(2)}) %collective-permute-start.3) | collective-permute-done | bytes 147488 | tf_op jit(solution)/shard_map/ppermute | solution.py:639
  23.2 3.6 %collective-permute-done.7.refs_7_ = bf16[144,512]{1,0:T(8,128)(2,1)} collective-permute-done((bf16[144,512]{1,0:T(8,128)(2,1)}, bf16[144,512]{1,0:T(8,128)(2,1)}, u32[]{:S(2)}, u32[]{:S(2)}) %collective-permute-start.7) | collective-permute-done | bytes 147488 | tf_op jit(solution)/shard_map/ppermute | solution.py:639
  26.8 4.3 %pick_tokens.1 = (bf16[1024,512]{1,0:T(8,128)(2,1)}, s32[16,128]{1,0:T(8,128)}) custom-call(s32[1]{0:T(128)} %bitcast.me_ref, bf16[144,512]{1,0:T(8,128)(2,1)} %get-tuple-element.37.refs_0_, bf16[144,512]{1,0:T(8,128)(2,1)} %copy-done.13, bf16[144,512]{1,0:T(8,128)(2,1)} %copy-done.14, bf16[144,512]{1,0:T(8,128)(2,1)} %copy-done.15, ...), custom_call_target="tpu_custom_call" | custom-call | flops 1073741824 | bytes 2236420 | tf_op jit(solution)/shard_map/pick_tokens/pallas_call | solution.py:40
  31.1 6.1 %all-to-all-start.1 = ((bf16[16,64,512]{2,1,0:T(8,128)(2,1)}), bf16[16,64,512]{2,1,0:T(8,128)(2,1)}, u32[]{:S(2)}, u32[]{:S(2)}) async-start(bf16[16,64,512]{2,1,0:T(8,128)(2,1)} %bitcast.19), calls=%async_computation.1 | async-start | bytes 2097152 | tf_op jit(solution)/shard_map/all_to_all | solution.py:633
  37.2 2.4 %cut_factors.1 = (bf16[2,4,512,128]{3,2,1,0:T(8,128)(2,1)}, bf16[1,4,512,128]{3,2,1,0:T(8,128)(2,1)}) custom-call(bf16[3,4,512,128]{3,2,1,0:T(8,128)(2,1)} %bitcast.15), custom_call_target="tpu_custom_call" | custom-call | bytes 3145728 | tf_op jit(solution)/shard_map/cut_factors/pallas_call | solution.py:40
  49.0 2.7 %collective-permute-start.14 = (bf16[128,512]{1,0:T(8,128)(2,1)}, bf16[128,512]{1,0:T(8,128)(2,1)S(1)}, u32[]{:S(2)}, u32[]{:S(2)}) collective-permute-start(bf16[128,512]{1,0:T(8,128)(2,1)} %get-tuple-element.53), channel_id=1, source_target_pairs={{0,6},{1,7},{2,4},{3,5},{4,2},{5,3},{6,0},{7,1},{8,14},{9,15},{10,... | collective-permute-start | bytes 393224 | tf_op jit(solution)/shard_map/ppermute | solution.py:639
  51.7 2.6 %collective-permute-done.11.refs_5_ = bf16[128,512]{1,0:T(8,128)(2,1)S(1)} collective-permute-done((bf16[128,512]{1,0:T(8,128)(2,1)}, bf16[128,512]{1,0:T(8,128)(2,1)S(1)}, u32[]{:S(2)}, u32[]{:S(2)}) %collective-permute-start.11) | collective-permute-done | bytes 131104 | tf_op jit(solution)/shard_map/ppermute | solution.py:639
  59.6 2.4 %mark_rows.1.refs_0_ = bf16[1024,1024]{1,0:T(8,128)(2,1)} custom-call(s32[1]{0:T(128)} %bitcast.me_ref, s32[16,128]{1,0:T(8,128)} %get-tuple-element.45.chosen_ref), custom_call_target="tpu_custom_call" | custom-call | flops 1048576 | bytes 2105348 | tf_op jit(solution)/shard_map/mark_rows/pallas_call | solution.py:40
  62.1 2.8 %collective-permute-done.14.refs_8_ = bf16[128,512]{1,0:T(8,128)(2,1)S(1)} collective-permute-done((bf16[128,512]{1,0:T(8,128)(2,1)}, bf16[128,512]{1,0:T(8,128)(2,1)S(1)}, u32[]{:S(2)}, u32[]{:S(2)}) %collective-permute-start.14) | collective-permute-done | bytes 131104 | tf_op jit(solution)/shard_map/ppermute | solution.py:639
  64.9 2.8 %collective-permute-done.15.refs_9_ = bf16[128,512]{1,0:T(8,128)(2,1)S(1)} collective-permute-done((bf16[128,512]{1,0:T(8,128)(2,1)}, bf16[128,512]{1,0:T(8,128)(2,1)S(1)}, u32[]{:S(2)}, u32[]{:S(2)}) %collective-permute-start.15) | collective-permute-done | bytes 131104 | tf_op jit(solution)/shard_map/ppermute | solution.py:639
  68.4 4.0 %pick_cotangent.1 = bf16[1024,512]{1,0:T(8,128)(2,1)} custom-call(s32[1]{0:T(128)} %bitcast.me_ref, bf16[1024,1024]{1,0:T(8,128)(2,1)} %mark_rows.1.refs_0_, bf16[2,4,512,128]{3,2,1,0:T(8,128)(2,1)} %collective-permute-done.8.refs_1_, bf16[128,512]{1,0:T(8,128)(2,1)} %get-tuple-element.47.refs_2_, bf16[128,512]{1,0:T(8,128)(2,1)} %copy-done.9, ...), custom_call_target="tpu_custom_call" | custom-call | flops 1073741824 | bytes 5242884 | tf_op jit(solution)/shard_map/pick_cotangent/pallas_call | solution.py:40
  72.5 5.4 %all-to-all-start = ((bf16[16,64,512]{2,1,0:T(8,128)(2,1)}), bf16[16,64,512]{2,1,0:T(8,128)(2,1)}, u32[]{:S(2)}, u32[]{:S(2)}) async-start(bf16[16,64,512]{2,1,0:T(8,128)(2,1)} %bitcast.13), calls=%async_computation | async-start | bytes 2097152 | tf_op jit(solution)/shard_map/all_to_all | solution.py:633
  79.7 5.9 %forward.1 = (bf16[512,512]{1,0:T(8,128)(2,1)}, bf16[512,512]{1,0:T(8,128)(2,1)}, f32[512,512]{1,0:T(8,128)}, f32[512,512]{1,0:T(8,128)}, f32[128,512]{1,0:T(8,1...) custom-call(s32[1]{0:T(128)} %bitcast.3.order_ref, f32[192]{0:T(256)} %reshape.42.mix_ref, ...), custom_call_target="tpu_custom_call" | custom-call | flops 1073741824 | bytes 7602948 | tf_op jit(solution)/shard_map/forward/pallas_call | solution.py:40
  87.3 4.0 %collective-permute-done.16.refs_2_ = bf16[1,4,512,128]{3,2,1,0:T(8,128)(2,1)} collective-permute-done((bf16[1,4,512,128]{3,2,1,0:T(8,128)(2,1)}, bf16[1,4,512,128]{3,2,1,0:T(8,128)(2,1)}, u32[]{:S(2)}, u32[]{:S(2)}) %collective-permute-start.16) | collective-permute-done | bytes 524320 | tf_op jit(solution)/shard_map/ppermute | solution.py:613
  91.4 11.2 %collective-permute-done.17.refs_3_ = bf16[512,512]{1,0:T(8,128)(2,1)S(1)} collective-permute-done((bf16[512,512]{1,0:T(8,128)(2,1)}, bf16[512,512]{1,0:T(8,128)(2,1)S(1)}, u32[]{:S(2)}, u32[]{:S(2)}) %collective-permute-start.17) | collective-permute-done | bytes 524320 | tf_op jit(solution)/shard_map/ppermute | solution.py:613
  103.4 8.5 %backward.1 = (bf16[384,2048]{1,0:T(8,128)(2,1)}, bf16[512,512]{1,0:T(8,128)(2,1)}, bf16[512,512]{1,0:T(8,128)(2,1)}, f32[512,512]{1,0:T(8,128)}, bf16[3,128,512]{2,1,0:T(8,128)(2,1)}, /*index=5*/f32[128,128]{1,0:T(8,128)}) custom-call(s32[1]{0:T(128)} %bitcast.3.order_ref, f32[192]{0:T(256)} %reshape.42.mix_ref, s32[1,128]{1,0:T(1,128)} %row_slots.1.slot_ref, ...), custom_call_target="tpu_custom_call" | custom-call | flops 1610612736 | bytes 9635588 | tf_op jit(solution)/shard_map/backward/pallas_call | solution.py:40
  111.9 6.9 %all-to-all-start.2 = ((bf16[16,24,2048]{2,1,0:T(8,128)(2,1)}), bf16[16,24,2048]{2,1,0:T(8,128)(2,1)}, u32[]{:S(2)}, u32[]{:S(2)}) async-start(bf16[16,24,2048]{2,1,0:T(8,128)(2,1)} %bitcast.18), calls=%async_computation.2 | async-start | bytes 3145728 | tf_op jit(solution)/shard_map/all_to_all | solution.py:633
  122.2 3.9 %mix_partials.1 = f32[192,128]{1,0:T(8,128)} custom-call(f32[512,512]{1,0:T(8,128)} %get-tuple-element.66.yg_hbm, f32[512,512]{1,0:T(8,128)} %get-tuple-element.67.yu_hbm, f32[512,512]{1,0:T(8,128)} %get-tuple-element.68.yd_hbm, bf16[3,128,512]{2,1,0:T(8,128)(2,1)} %get-tuple-element.64.refs_2_.d_hbm), custom_call_target="tpu_custom_call" | custom-call | flops 6291456 | bytes 3637248 | tf_op jit(solution)/shard_map/mix_partials/pallas_call | solution.py:40
  130.0 11.4 %collective-permute-done.20 = f32[1,3,4,4,4]{4,3,2,1,0:T(4,128)S(1)} collective-permute-done((f32[1,3,4,4,4]{4,3,2,1,0:T(4,128)S(1)}, f32[1,3,4,4,4]{4,3,2,1,0:T(4,128)S(1)}, u32[]{:S(2)}, u32[]{:S(2)}) %collective-permute-start.20) | collective-permute-done | bytes 800 | tf_op jit(solution)/shard_map/ppermute | solution.py:613
  142.8 7.8 %factor_grad.1 = f32[3,4,512,128]{3,2,1,0:T(8,128)} custom-call(f32[192]{0:T(256)} %reshape.42.mix_ref, bf16[512,512]{1,0:T(8,128)(2,1)} %get-tuple-element.62.refs_0_, bf16[512,512]{1,0:T(8,128)(2,1)} %get-tuple-element.63.refs_1_, bf16[3,128,512]{2,1,0:T(8,128)(2,1)} %get-tuple-element.64.refs_2_.d_hbm, bf16[512,512]{1,0:T(8,128)(2,1)} %copy-done.1, ...), custom_call_target="tpu_custom_call" | custom-call | flops 1610612736 | bytes 6030080 | tf_op jit(solution)/shard_map/factor_grad/pallas_call | solution.py:40
  150.5 4.6 %all-to-all-done.2 = bf16[16,24,2048]{2,1,0:T(8,128)(2,1)} async-done(((bf16[16,24,2048]{2,1,0:T(8,128)(2,1)}), bf16[16,24,2048]{2,1,0:T(8,128)(2,1)}, u32[]{:S(2)}, u32[]{:S(2)}) %all-to-all-start.2) | async-done | bytes 1572896 | tf_op jit(solution)/shard_map/all_to_all | solution.py:633
  155.2 3.1 %sum_rows.1 = bf16[128,4096]{1,0:T(8,128)(2,1)} custom-call(bf16[256,384]{1,0:T(8,128)(2,1)} %place_rows.1.placed_hbm, bf16[384,2048]{1,0:T(8,128)(2,1)} %bitcast.11.returned_ref), custom_call_target="tpu_custom_call" | custom-call | flops 402653184 | bytes 2818048 | tf_op jit(solution)/shard_map/sum_rows/pallas_call | solution.py:40
  (82 shorter events, 42.9 us)
Async XLA Ops:
  0.6 3.6 %collective-permute-start = (s32[1,2,64]{2,1,0:T(2,128)}, s32[1,2,64]{2,1,0:T(2,128)S(1)}, u32[]{:S(2)}, u32[]{:S(2)}) collective-permute-start(s32[1,2,64]{2,1,0:T(2,128)} %param.10), channel_id=1, source_target_pairs={{0,8},{1,9},{2,10},{3,11},{4,12},{5,13},{6,14},{7,15},{8,0},{9,1},... | collective-permute-start | bytes 1544 | tf_op jit(solution)/shard_map/ppermute | solution.py:651
  7.8 5.4 %collective-permute-start.1 = (bf16[144,512]{1,0:T(8,128)(2,1)}, bf16[144,512]{1,0:T(8,128)(2,1)S(1)}, u32[]{:S(2)}, u32[]{:S(2)}) collective-permute-start(bf16[144,512]{1,0:T(8,128)(2,1)} %get-tuple-element.38), channel_id=1, source_target_pairs={{0,1},{1,0},{2,3},{3,2},{4,5},{5,4},{6,7},{7,6},{8,9},{9,8},{10,11... | collective-permute-start | bytes 442376 | tf_op jit(solution)/shard_map/ppermute | solution.py:639
  9.7 5.6 %collective-permute-start.2 = (bf16[144,512]{1,0:T(8,128)(2,1)}, bf16[144,512]{1,0:T(8,128)(2,1)S(1)}, u32[]{:S(2)}, u32[]{:S(2)}) collective-permute-start(bf16[144,512]{1,0:T(8,128)(2,1)} %get-tuple-element.39), channel_id=1, source_target_pairs={{0,2},{1,3},{2,0},{3,1},{4,6},{5,7},{6,4},{7,5},{8,10},{9,11},{10,... | collective-permute-start | bytes 442376 | tf_op jit(solution)/shard_map/ppermute | solution.py:639
  10.0 9.0 %collective-permute-start.3 = (bf16[144,512]{1,0:T(8,128)(2,1)}, bf16[144,512]{1,0:T(8,128)(2,1)S(1)}, u32[]{:S(2)}, u32[]{:S(2)}) collective-permute-start(bf16[144,512]{1,0:T(8,128)(2,1)} %get-tuple-element.40), channel_id=1, source_target_pairs={{0,3},{1,2},{2,1},{3,0},{4,7},{5,6},{6,5},{7,4},{8,11},{9,10},{10,... | collective-permute-start | bytes 442376 | tf_op jit(solution)/shard_map/ppermute | solution.py:639
  11.5 7.5 %collective-permute-start.4 = (bf16[144,512]{1,0:T(8,128)(2,1)}, bf16[144,512]{1,0:T(8,128)(2,1)S(1)}, u32[]{:S(2)}, u32[]{:S(2)}) collective-permute-start(bf16[144,512]{1,0:T(8,128)(2,1)} %get-tuple-element.41), channel_id=1, source_target_pairs={{0,4},{1,5},{2,6},{3,7},{4,0},{5,1},{6,2},{7,3},{8,12},{9,13},{10,... | collective-permute-start | bytes 442376 | tf_op jit(solution)/shard_map/ppermute | solution.py:639
  11.6 9.6 %collective-permute-start.5 = (bf16[144,512]{1,0:T(8,128)(2,1)}, bf16[144,512]{1,0:T(8,128)(2,1)S(1)}, u32[]{:S(2)}, u32[]{:S(2)}) collective-permute-start(bf16[144,512]{1,0:T(8,128)(2,1)} %get-tuple-element.42), channel_id=1, source_target_pairs={{0,5},{1,4},{2,7},{3,6},{4,1},{5,0},{6,3},{7,2},{8,13},{9,12},{10,... | collective-permute-start | bytes 442376 | tf_op jit(solution)/shard_map/ppermute | solution.py:639
  13.3 10.0 %collective-permute-start.6 = (bf16[144,512]{1,0:T(8,128)(2,1)}, bf16[144,512]{1,0:T(8,128)(2,1)S(1)}, u32[]{:S(2)}, u32[]{:S(2)}) collective-permute-start(bf16[144,512]{1,0:T(8,128)(2,1)} %get-tuple-element.43), channel_id=1, source_target_pairs={{0,6},{1,7},{2,4},{3,5},{4,2},{5,3},{6,0},{7,1},{8,14},{9,15},{10,... | collective-permute-start | bytes 442376 | tf_op jit(solution)/shard_map/ppermute | solution.py:639
  15.4 11.4 %collective-permute-start.7 = (bf16[144,512]{1,0:T(8,128)(2,1)}, bf16[144,512]{1,0:T(8,128)(2,1)}, u32[]{:S(2)}, u32[]{:S(2)}) collective-permute-start(bf16[144,512]{1,0:T(8,128)(2,1)} %get-tuple-element.44), channel_id=1, source_target_pairs={{0,7},{1,6},{2,5},{3,4},{4,3},{5,2},{6,1},{7,0},{8,15},{9,14},{10,... | collective-permute-start | bytes 442376 | tf_op jit(solution)/shard_map/ppermute | solution.py:639
  31.1 41.4 %all-to-all-start.1 = ((bf16[16,64,512]{2,1,0:T(8,128)(2,1)}), bf16[16,64,512]{2,1,0:T(8,128)(2,1)}, u32[]{:S(2)}, u32[]{:S(2)}) async-start(bf16[16,64,512]{2,1,0:T(8,128)(2,1)} %bitcast.19), calls=%async_computation.1 | async-start | bytes 2097152 | tf_op jit(solution)/shard_map/all_to_all | solution.py:633
  39.6 28.1 %collective-permute-start.8 = (bf16[2,4,512,128]{3,2,1,0:T(8,128)(2,1)}, bf16[2,4,512,128]{3,2,1,0:T(8,128)(2,1)}, u32[]{:S(2)}, u32[]{:S(2)}) collective-permute-start(bf16[2,4,512,128]{3,2,1,0:T(8,128)(2,1)} %get-tuple-element.46), channel_id=1, source_target_pairs={{0,16},{16,0},{1,17},{17,1},{2,18},{18,2},{3,19},{19,3},{4,20},{20... | collective-permute-start | bytes 3145736 | tf_op jit(solution)/shard_map/ppermute | solution.py:613
  43.3 5.7 %collective-permute-start.10 = (bf16[128,512]{1,0:T(8,128)(2,1)}, bf16[128,512]{1,0:T(8,128)(2,1)S(1)}, u32[]{:S(2)}, u32[]{:S(2)}) collective-permute-start(bf16[128,512]{1,0:T(8,128)(2,1)} %get-tuple-element.49), channel_id=1, source_target_pairs={{0,2},{1,3},{2,0},{3,1},{4,6},{5,7},{6,4},{7,5},{8,10},{9,11},{10,... | collective-permute-start | bytes 393224 | tf_op jit(solution)/shard_map/ppermute | solution.py:639
  43.6 10.7 %collective-permute-start.11 = (bf16[128,512]{1,0:T(8,128)(2,1)}, bf16[128,512]{1,0:T(8,128)(2,1)S(1)}, u32[]{:S(2)}, u32[]{:S(2)}) collective-permute-start(bf16[128,512]{1,0:T(8,128)(2,1)} %get-tuple-element.50), channel_id=1, source_target_pairs={{0,3},{1,2},{2,1},{3,0},{4,7},{5,6},{6,5},{7,4},{8,11},{9,10},{10,... | collective-permute-start | bytes 393224 | tf_op jit(solution)/shard_map/ppermute | solution.py:639
  45.6 12.7 %collective-permute-start.12 = (bf16[128,512]{1,0:T(8,128)(2,1)}, bf16[128,512]{1,0:T(8,128)(2,1)S(1)}, u32[]{:S(2)}, u32[]{:S(2)}) collective-permute-start(bf16[128,512]{1,0:T(8,128)(2,1)} %get-tuple-element.51), channel_id=1, source_target_pairs={{0,4},{1,5},{2,6},{3,7},{4,0},{5,1},{6,2},{7,3},{8,12},{9,13},{10,... | collective-permute-start | bytes 393224 | tf_op jit(solution)/shard_map/ppermute | solution.py:639
  45.9 16.2 %collective-permute-start.13 = (bf16[128,512]{1,0:T(8,128)(2,1)}, bf16[128,512]{1,0:T(8,128)(2,1)S(1)}, u32[]{:S(2)}, u32[]{:S(2)}) collective-permute-start(bf16[128,512]{1,0:T(8,128)(2,1)} %get-tuple-element.52), channel_id=1, source_target_pairs={{0,5},{1,4},{2,7},{3,6},{4,1},{5,0},{6,3},{7,2},{8,13},{9,12},{10,... | collective-permute-start | bytes 393224 | tf_op jit(solution)/shard_map/ppermute | solution.py:639
  49.0 15.9 %collective-permute-start.14 = (bf16[128,512]{1,0:T(8,128)(2,1)}, bf16[128,512]{1,0:T(8,128)(2,1)S(1)}, u32[]{:S(2)}, u32[]{:S(2)}) collective-permute-start(bf16[128,512]{1,0:T(8,128)(2,1)} %get-tuple-element.53), channel_id=1, source_target_pairs={{0,6},{1,7},{2,4},{3,5},{4,2},{5,3},{6,0},{7,1},{8,14},{9,15},{10,... | collective-permute-start | bytes 393224 | tf_op jit(solution)/shard_map/ppermute | solution.py:639
  54.3 13.5 %collective-permute-start.15 = (bf16[128,512]{1,0:T(8,128)(2,1)}, bf16[128,512]{1,0:T(8,128)(2,1)S(1)}, u32[]{:S(2)}, u32[]{:S(2)}) collective-permute-start(bf16[128,512]{1,0:T(8,128)(2,1)} %get-tuple-element.54), channel_id=1, source_target_pairs={{0,7},{1,6},{2,5},{3,4},{4,3},{5,2},{6,1},{7,0},{8,15},{9,14},{10,... | collective-permute-start | bytes 393224 | tf_op jit(solution)/shard_map/ppermute | solution.py:639
  58.3 9.4 %collective-permute-start.9 = (bf16[128,512]{1,0:T(8,128)(2,1)}, bf16[128,512]{1,0:T(8,128)(2,1)S(1)}, u32[]{:S(2)}, u32[]{:S(2)}) collective-permute-start(bf16[128,512]{1,0:T(8,128)(2,1)} %get-tuple-element.48), channel_id=1, source_target_pairs={{0,1},{1,0},{2,3},{3,2},{4,5},{5,4},{6,7},{7,6},{8,9},{9,8},{10,11... | collective-permute-start | bytes 393224 | tf_op jit(solution)/shard_map/ppermute | solution.py:639
  72.5 30.6 %all-to-all-start = ((bf16[16,64,512]{2,1,0:T(8,128)(2,1)}), bf16[16,64,512]{2,1,0:T(8,128)(2,1)}, u32[]{:S(2)}, u32[]{:S(2)}) async-start(bf16[16,64,512]{2,1,0:T(8,128)(2,1)} %bitcast.13), calls=%async_computation | async-start | bytes 2097152 | tf_op jit(solution)/shard_map/all_to_all | solution.py:633
  77.9 13.5 %collective-permute-start.16 = (bf16[1,4,512,128]{3,2,1,0:T(8,128)(2,1)}, bf16[1,4,512,128]{3,2,1,0:T(8,128)(2,1)}, u32[]{:S(2)}, u32[]{:S(2)}) collective-permute-start(bf16[1,4,512,128]{3,2,1,0:T(8,128)(2,1)} %get-tuple-element.59), channel_id=1, source_target_pairs={{0,16},{16,0},{1,17},{17,1},{2,18},{18,2},{3,19},{19,3},{4,20},{20... | collective-permute-start | bytes 1572872 | tf_op jit(solution)/shard_map/ppermute | solution.py:613
  85.6 17.0 %collective-permute-start.17 = (bf16[512,512]{1,0:T(8,128)(2,1)}, bf16[512,512]{1,0:T(8,128)(2,1)S(1)}, u32[]{:S(2)}, u32[]{:S(2)}) collective-permute-start(bf16[512,512]{1,0:T(8,128)(2,1)} %get-tuple-element.60), channel_id=1, source_target_pairs={{0,16},{16,0},{1,17},{17,1},{2,18},{18,2},{3,19},{19,3},{4,20},{20... | collective-permute-start | bytes 1572872 | tf_op jit(solution)/shard_map/ppermute | solution.py:613
  111.9 43.2 %all-to-all-start.2 = ((bf16[16,24,2048]{2,1,0:T(8,128)(2,1)}), bf16[16,24,2048]{2,1,0:T(8,128)(2,1)}, u32[]{:S(2)}, u32[]{:S(2)}) async-start(bf16[16,24,2048]{2,1,0:T(8,128)(2,1)} %bitcast.18), calls=%async_computation.2 | async-start | bytes 3145728 | tf_op jit(solution)/shard_map/all_to_all | solution.py:633
  118.9 23.1 %collective-permute-start.18 = (bf16[512,512]{1,0:T(8,128)(2,1)}, bf16[512,512]{1,0:T(8,128)(2,1)S(1)}, u32[]{:S(2)}, u32[]{:S(2)}) collective-permute-start(bf16[512,512]{1,0:T(8,128)(2,1)} %get-tuple-element.65), channel_id=1, source_target_pairs={{0,16},{16,0},{1,17},{17,1},{2,18},{18,2},{3,19},{19,3},{4,20},{20... | collective-permute-start | bytes 1572872 | tf_op jit(solution)/shard_map/ppermute | solution.py:613
  120.1 21.8 %collective-permute-start.19 = (bf16[3,128,512]{2,1,0:T(8,128)(2,1)S(1)}, bf16[3,128,512]{2,1,0:T(8,128)(2,1)}, u32[]{:S(2)}, u32[]{:S(2)}) collective-permute-start(bf16[3,128,512]{2,1,0:T(8,128)(2,1)S(1)} %copy-done), channel_id=1, source_target_pairs={{0,16},{16,0},{1,17},{17,1},{2,18},{18,2},{3,19},{19,3},{4,20},{20... | collective-permute-start | bytes 1179656 | tf_op jit(solution)/shard_map/ppermute | solution.py:613
  127.3 14.1 %collective-permute-start.20 = (f32[1,3,4,4,4]{4,3,2,1,0:T(4,128)S(1)}, f32[1,3,4,4,4]{4,3,2,1,0:T(4,128)S(1)}, u32[]{:S(2)}, u32[]{:S(2)}) collective-permute-start(f32[1,3,4,4,4]{4,3,2,1,0:T(4,128)S(1)} %reshape.49), channel_id=1, source_target_pairs={{0,16},{16,0},{1,17},{17,1},{2,18},{18,2},{3,19},{19,3},{4,20},{20... | collective-permute-start | bytes 2312 | tf_op jit(solution)/shard_map/ppermute | solution.py:613
  (19 other events, 124.4 us)

commit v11 on v9

--- a/solution.py
+++ b/solution.py
@@ -111,20 +111,22 @@
     return (target == iota((slots, pieces * own_rows), 1)).astype(BF16)
 
 
-def pick_slots(cap, pieces, requested, source, name):
+def pick_slots(cap, pieces, requested, source, after, name):
     own_rows, width = source.shape
     part = width // pieces
     slots = requested.shape[0] // 2 * cap * pieces
     columns = chunks_of(part)
 
-    def body(requested_ref, source_ref, *refs):
-        out_ref, rows_ref, sent_ref, in_sem, out_sem = refs
+    def body(requested_hbm, source_ref, *refs):
+        out_ref, requested_ref, rows_ref, sent_ref, in_sem, out_sem = refs[len(after) :]
+        asked = begin(requested_hbm, requested_ref, in_sem.at[len(columns), 0])
         loads = []
         for n, at in enumerate(columns):
             for j in range(pieces):
                 wide = slice(j * part + at.start, j * part + at.stop)
                 target = rows_ref.at[j * own_rows : (j + 1) * own_rows, at]
                 loads.append(begin(source_ref.at[:, wide], target, in_sem.at[n, j]))
+        asked.wait()
         pick = pick_matrix(cap, pieces, own_rows, requested_ref[...])
         stores = []
         for n, at in enumerate(columns):
@@ -138,13 +140,14 @@
     return call(
         body,
         [(shaped((slots, part), BF16), HBM)],
-        [(requested, VMEM), (source, HBM)],
+        [(requested, HBM), (source, HBM)] + [(x, HBM) for x in after],
         name,
         2 * slots * pieces * own_rows * part,
         [
+            scratch_like(requested.shape, jnp.int32),
             scratch_like((pieces * own_rows, part), BF16),
             scratch_like((slots, part), BF16),
-            pltpu.SemaphoreType.DMA((len(columns), pieces)),
+            pltpu.SemaphoreType.DMA((len(columns) + 1, pieces)),
             pltpu.SemaphoreType.DMA((len(columns),)),
         ],
     )[0]
@@ -372,7 +375,7 @@
     for n in range(got_hbm.shape[0] // picks):
         block, share = divmod(n, shares)
         a, start = share * part // depth, share * part % depth
-        first = a * rows + block * picks
+        first = (block * NPHM + a) * picks
         at = x_ref.at[first : first + picks, start : start + part]
         copies.append(begin(got_hbm.at[n * picks : (n + 1) * picks], at, sems.at[n]))
     return copies
@@ -394,9 +397,11 @@
         for j in range(pieces):
             column = j * part + at.start
             a, start = column // depth, column % depth
-            out_ref[a * rows : (a + 1) * rows, start : start + at.stop - at.start] = block[
-                j * rows : (j + 1) * rows
-            ]
+            for n in range(rows // STRIP):
+                first = (n * NPHM + a) * STRIP
+                out_ref[first : first + STRIP, start : start + at.stop - at.start] = block[
+                    j * rows + n * STRIP : j * rows + (n + 1) * STRIP
+                ]
 
 
 def store_parts(order_ref, source_ref, outs, sems):
@@ -408,45 +413,40 @@
     return copies
 
 
-STRIP = 32
-
-
-def mix_in(mix_ref, m, y_ref, emit):
-    rows, cols = y_ref.shape[0] // NPHM, y_ref.shape[1] // NPHM
-
-    def strip(n, carry):
-        start = pl.multiple_of(n * STRIP, STRIP)
-        total = [jnp.zeros((STRIP, cols), F32)] * NPHM
-        for a in range(NPHM):
-            for i in range(NPHM):
-                block = y_ref[pl.ds(a * rows + start, STRIP), i * cols : (i + 1) * cols]
-                for b in range(NPHM):
-                    total[b] = total[b] + mix_ref[m * 64 + i * 16 + a * 4 + b] * block
-        emit(start, total)
-        return carry
-
-    lax.fori_loop(0, rows // STRIP, strip, 0)
-
-
-def mix_out(mix_ref, m, d_ref, z_ref):
-    rows, cols = d_ref.shape[0], d_ref.shape[1] // NPHM
-
-    def strip(n, carry):
-        start = pl.multiple_of(n * STRIP, STRIP)
-        blocks = [
-            d_ref[pl.ds(start, STRIP), b * cols : (b + 1) * cols].astype(F32) for b in range(NPHM)
-        ]
-        for a in range(NPHM):
-            for i in range(NPHM):
-                total = mix_ref[m * 64 + i * 16 + a * 4] * blocks[0]
-                for b in range(1, NPHM):
-                    total = total + mix_ref[m * 64 + i * 16 + a * 4 + b] * blocks[b]
-                z_ref[pl.ds(a * rows + start, STRIP), i * cols : (i + 1) * cols] = total.astype(
-                    z_ref.dtype
-                )
-        return carry
-
-    lax.fori_loop(0, rows // STRIP, strip, 0)
+STRIP = SELECTED
+
+
+def rows_of(n, a):
+    return slice((n * NPHM + a) * STRIP, (n * NPHM + a + 1) * STRIP)
+
+
+def mix_in(mix_ref, m, y_ref, n):
+    cols = y_ref.shape[1] // NPHM
+    total = [jnp.zeros((STRIP, cols), F32)] * NPHM
+    for a in range(NPHM):
+        for i in range(NPHM):
+            block = y_ref[rows_of(n, a), i * cols : (i + 1) * cols]
+            for b in range(NPHM):
+                total[b] = total[b] + mix_ref[m * 64 + i * 16 + a * 4 + b] * block
+    return total
+
+
+def mix_out(mix_ref, m, blocks, n, z_ref, offset=0):
+    cols = blocks[0].shape[1]
+    for a in range(NPHM):
+        for i in range(NPHM):
+            total = mix_ref[m * 64 + i * 16 + a * 4] * blocks[0]
+            for b in range(1, NPHM):
+                total = total + mix_ref[m * 64 + i * 16 + a * 4 + b] * blocks[b]
+            z_ref[rows_of(n, a), offset + i * cols : offset + (i + 1) * cols] = total.astype(
+                z_ref.dtype
+            )
+
+
+def blocks_of(d_ref, n):
+    cols = d_ref.shape[1] // NPHM
+    at = slice(n * STRIP, (n + 1) * STRIP)
+    return [d_ref[at, b * cols : (b + 1) * cols].astype(F32) for b in range(NPHM)]
 
 
 def forward_body(
@@ -456,8 +456,8 @@
     parts, refs = refs[:held], refs[held:]
     x_outs, refs = refs[:sides], refs[sides:]
     yg_hbm, yu_hbm, act_hbm, slope_hbm, hid_hbm = refs[:5]
-    got_ref, side_ref, x_ref, yg_ref, yu_ref, pre_ref, act_ref, slope_ref, hid_ref = refs[5:14]
-    got_sem, side_sem, out_sem = refs[14:]
+    got_ref, side_ref, x_ref, yg_ref, yu_ref, act_ref, slope_ref, hid_ref = refs[5:13]
+    got_sem, side_sem, out_sem = refs[13:]
     loads = load_slots(got_hbm, got_ref, got_sem)
     sides_in = [
         load_factor(order_ref, parts, m, side_ref.at[m], side_sem.at[m]) for m in range(2)
@@ -472,23 +472,16 @@
     yu_ref[...] = dot(x_ref[...], side_ref[1])
     stores.append(begin(yu_ref, yu_hbm, out_sem.at[3]))
     cols = yg_ref.shape[1] // NPHM
-
-    def keep(start, total):
+    for n in range(yg_ref.shape[0] // (NPHM * STRIP)):
+        gates = mix_in(mix_ref, 0, yg_ref, n)
+        ups = mix_in(mix_ref, 1, yu_ref, n)
         for b in range(NPHM):
-            pre_ref[pl.ds(start, STRIP), b * cols : (b + 1) * cols] = total[b]
-
-    def finish(start, total):
-        for b in range(NPHM):
-            at = (pl.ds(start, STRIP), slice(b * cols, (b + 1) * cols))
-            gate = pre_ref[at]
-            sig = jax.nn.sigmoid(gate)
-            act = gate * sig
+            at = (slice(n * STRIP, (n + 1) * STRIP), slice(b * cols, (b + 1) * cols))
+            sig = jax.nn.sigmoid(gates[b])
+            act = gates[b] * sig
             act_ref[at] = act
-            slope_ref[at] = total[b] * (sig + act * (1.0 - sig))
-            hid_ref[at] = act * total[b]
-
-    mix_in(mix_ref, 0, yg_ref, keep)
-    mix_in(mix_ref, 1, yu_ref, finish)
+            slope_ref[at] = ups[b] * (sig + act * (1.0 - sig))
+            hid_ref[at] = act * ups[b]
     stores.append(begin(act_ref, act_hbm, out_sem.at[4]))
     stores.append(begin(slope_ref, slope_hbm, out_sem.at[5]))
     stores.append(begin(hid_ref, hid_hbm, out_sem.at[6]))
@@ -496,75 +489,84 @@
 
 
 def backward_body(
-    cap, pieces, sides, after, order_ref, mix_ref, slot_ref, score_ref, got_hbm, act_hbm, slope_hbm, hid_hbm,
+    cap, pieces, sides, after, order_ref, mix_ref, slot_hbm, score_hbm, got_hbm, act_hbm, slope_hbm, hid_hbm,
     *refs,
 ):
     held = 3 if sides > 1 else 1
     parts, refs = refs[:held], refs[held + after :]
     back_hbm, x_outs, refs = refs[0], refs[1 : 1 + sides], refs[1 + sides :]
-    y_hbm, d_hbm, inner_ref = refs[:3]
+    y_hbm, d_hbm, inner_hbm = refs[:3]
     (
-        side_ref, x_ref, y_ref, d_ref, act_ref, slope_ref, hid_ref, zg_ref, zu_ref, grad_ref,
-        back_ref, gate_ref, got_sem, side_sem, in_sem, out_sem,
+        down_ref, side_ref, x_ref, y_ref, d_ref, act_ref, slope_ref, hid_ref, z_ref, grad_ref,
+        back_ref, inner_ref, slot_ref, score_ref, got_sem, side_sem, in_sem, out_sem,
     ) = refs[3:]
     loads = load_rows(got_hbm, x_ref, got_sem)
-    down_in = load_factor(order_ref, parts, 2, side_ref.at[2], side_sem.at[2])
+    down_in = load_factor(order_ref, parts, 2, down_ref, side_sem.at[2])
+    small_in = [
+        begin(source, target, in_sem.at[n])
+        for n, (source, target) in enumerate(((score_hbm, score_ref), (slot_hbm, slot_ref)))
+    ]
     flat_in = [
-        begin(source, target, in_sem.at[n])
+        begin(source, target, in_sem.at[2 + n])
         for n, (source, target) in enumerate(
             ((act_hbm, act_ref), (slope_hbm, slope_ref), (hid_hbm, hid_ref))
         )
     ]
-    sides_in = [
-        load_factor(order_ref, parts, m, side_ref.at[m], side_sem.at[m]) for m in range(2)
-    ]
+    hidden = d_ref.shape[2]
+    sides_in = []
+    for m in range(2):
+        target = side_ref.at[:, m * hidden : (m + 1) * hidden]
+        sides_in += load_factor(order_ref, parts, m, target, side_sem.at[m])
+    wait_all(small_in)
     score = jnp.concatenate([score_ref[b : b + 1, :] for b in range(score_ref.shape[0])], axis=1)
     rows = score.shape[1]
     same = iota((rows, rows), 0) == iota((rows, rows), 1)
     score = jnp.sum(jnp.where(same, score.astype(F32), 0.0), axis=1, keepdims=True)
-    gate_ref[...] = jnp.broadcast_to(jax.nn.sigmoid(score / 64.0), gate_ref.shape)
+    cols = hidden // NPHM
+    gates = jnp.broadcast_to(jax.nn.sigmoid(score / 64.0), (rows, cols))
+    place = place_matrix(cap, pieces, back_ref.shape[0], slot_ref[...])
+    strips = rows // STRIP
+    tall = NPHM * STRIP
     wait_all(loads)
     stores = store_parts(order_ref, x_ref, x_outs, out_sem)
     wait_all(down_in)
-    y_ref[...] = dot(x_ref[...], side_ref[2])
+    for n in range(strips):
+        y_ref[n * tall : (n + 1) * tall] = dot(x_ref[n * tall : (n + 1) * tall], down_ref[...])
     stores.append(begin(y_ref, y_hbm, out_sem.at[2]))
-    cols = y_ref.shape[1] // NPHM
     wait_all(flat_in)
-
-    def finish(start, total):
-        gate = gate_ref[pl.ds(start, STRIP), :]
+    wait_all(sides_in)
+    for n in range(strips):
+        down = mix_in(mix_ref, 2, y_ref, n)
+        strip = slice(n * STRIP, (n + 1) * STRIP)
+        gate = gates[strip]
         inner = jnp.zeros((STRIP, cols), F32)
+        d_gate, d_up = [], []
         for b in range(NPHM):
-            at = (pl.ds(start, STRIP), slice(b * cols, (b + 1) * cols))
-            hidden = hid_ref[at]
-            inner = inner + hidden * total[b]
-            hidden_grad = gate * total[b]
-            d_ref[(0,) + at] = (hidden_grad * slope_ref[at]).astype(BF16)
-            d_ref[(1,) + at] = (hidden_grad * act_ref[at]).astype(BF16)
-            d_ref[(2,) + at] = (hidden * gate).astype(BF16)
-        inner_ref[pl.ds(start, STRIP), :] = inner
-
-    mix_in(mix_ref, 2, y_ref, finish)
+            at = (strip, slice(b * cols, (b + 1) * cols))
+            inner = inner + hid_ref[at] * down[b]
+            hidden_grad = gate * down[b]
+            d_gate.append(hidden_grad * slope_ref[at])
+            d_up.append(hidden_grad * act_ref[at])
+            d_ref[(0,) + at] = d_gate[b].astype(BF16)
+            d_ref[(1,) + at] = d_up[b].astype(BF16)
+            d_ref[(2,) + at] = (hid_ref[at] * gate).astype(BF16)
+        inner_ref[strip] = inner
+        mix_out(mix_ref, 0, d_gate, n, z_ref)
+        mix_out(mix_ref, 1, d_up, n, z_ref, hidden)
+        at = slice(n * tall, (n + 1) * tall)
+        grad_ref[at] = dot_nt(z_ref[at], side_ref[...]).astype(BF16)
     stores.append(begin(d_ref, d_hbm, out_sem.at[3]))
-    mix_out(mix_ref, 0, d_ref.at[0], zg_ref)
-    mix_out(mix_ref, 1, d_ref.at[1], zu_ref)
-    wait_all(sides_in[0])
-    wait_all(sides_in[1])
-    grad = dot_nt(zg_ref[...], side_ref[0]) + dot_nt(zu_ref[...], side_ref[1])
-    grad_ref[...] = grad.astype(BF16)
-    place = place_matrix(cap, pieces, back_ref.shape[0], slot_ref[...])
-    part = back_ref.shape[1]
-    rows, depth = x_ref.shape[0] // NPHM, x_ref.shape[1]
-    for n, at in enumerate(chunks_of(part)):
+    stores.append(begin(inner_ref, inner_hbm, out_sem.at[4]))
+    part, depth = back_ref.shape[1], x_ref.shape[1]
+    for k, at in enumerate(chunks_of(part)):
         blocks = []
         for j in range(pieces):
             column = j * part + at.start
             a, start = column // depth, column % depth
-            blocks.append(
-                grad_ref[a * rows : (a + 1) * rows, start : start + at.stop - at.start]
-            )
+            wide = slice(start, start + at.stop - at.start)
+            blocks += [grad_ref[rows_of(n, a), wide] for n in range(strips)]
         back_ref[:, at] = dot(place, jnp.concatenate(blocks, axis=0)).astype(BF16)
-        stores.append(begin(back_ref.at[:, at], back_hbm.at[:, at], out_sem.at[4 + n]))
+        stores.append(begin(back_ref.at[:, at], back_hbm.at[:, at], out_sem.at[5 + k]))
     wait_all(stores)
 
 
@@ -580,7 +582,9 @@
     wait_all(loads)
     for m in (2, 0, 1):
         for n in range(count_groups):
-            mix_out(mix_ref, m, d_ref.at[n, m], z_ref.at[n])
+            for strip in range(d_ref.shape[2] // STRIP):
+                blocks = blocks_of(d_ref.at[n, m], strip)
+                mix_out(mix_ref, m, blocks, strip, z_ref.at[n])
         left = g_ref if m == 2 else x_ref
         sum_ref[m] = sum(dot_tn(left[n], z_ref[n]) for n in range(count_groups))
         for i in range(NPHM):
@@ -598,7 +602,9 @@
     for m in range(3):
         for a in range(NPHM):
             for i in range(NPHM):
-                block = y_ref[m, a * rows : (a + 1) * rows, i * cols : (i + 1) * cols]
+                at = slice(i * cols, (i + 1) * cols)
+                strips = range(rows // STRIP)
+                block = jnp.concatenate([y_ref[m, rows_of(n, a), at] for n in strips], axis=0)
                 for b in range(NPHM):
                     at = m * 64 + i * 16 + a * 4 + b
                     other = d_ref[m, :, b * cols : (b + 1) * cols].astype(F32)
@@ -672,8 +678,9 @@
         )
         return [array.reshape(shares[0].shape)]
 
-    got_rows = to_peers(pick_slots(cap, pieces, chosen, tokens, "pick_tokens"))
     shares = collect(spread_columns(me, [cotangent], half, direct, "spread_cotangent"))
+    early = shares[4:] if direct else []
+    got_rows = to_peers(pick_slots(cap, pieces, chosen, tokens, early, "pick_tokens"))
     picked = pick_rows(me, half, own_rows, 0, chosen, shares, cuts[:1], "pick_cotangent")
     got_grads = to_peers(picked)
     placed = place_rows(cap, pieces, own_rows, me, half, chosen)
@@ -696,7 +703,7 @@
         "forward",
         2 * product,
         [back_scratch, scratch_like((2, depth, hidden), BF16), stack_scratch, mixed_scratch, mixed_scratch]
-        + [flat_scratch] * 4
+        + [flat_scratch] * 3
         + [dma((steps,)), dma((2, sides, count)), dma((7,))],
     )
     x_parts, (y_gate, y_up, act, slope, hid) = outs[:sides], outs[sides:]
@@ -706,19 +713,20 @@
         functools.partial(backward_body, cap, pieces, sides, len(after)),
         [(shaped((slots, part), BF16), HBM)]
         + split
-        + [mixed, (shaped((weights, rows, hidden), BF16), HBM), (shaped((rows, cols), F32), VMEM)],
-        [(group, SMEM), (mixing, SMEM), (slot, VMEM), (scores[0], VMEM), (got_grads, HBM)]
+        + [mixed, (shaped((weights, rows, hidden), BF16), HBM), (shaped((rows, cols), F32), HBM)],
+        [(group, SMEM), (mixing, SMEM), (slot, HBM), (scores[0], HBM), (got_grads, HBM)]
         + [(x, HBM) for x in (act, slope, hid)]
         + sides_in
         + [(x, HBM) for x in after],
         "backward",
         3 * product,
-        [scratch_like((weights, depth, hidden), BF16), stack_scratch, mixed_scratch]
-        + [scratch_like((weights, rows, hidden), BF16)]
+        [scratch_like((depth, hidden), BF16), scratch_like((depth, 2 * hidden), BF16)]
+        + [stack_scratch, mixed_scratch, scratch_like((weights, rows, hidden), BF16)]
         + [flat_scratch] * 3
-        + [low_scratch] * 2
-        + [stack_scratch, back_scratch, scratch_like((rows, cols), F32)]
-        + [dma((pieces_in,)), dma((weights, sides, count)), dma((3,)), dma((4 + steps,))],
+        + [scratch_like((stacked, 2 * hidden), BF16), stack_scratch, back_scratch]
+        + [scratch_like((rows, cols), F32), scratch_like(slot.shape, jnp.int32)]
+        + [scratch_like(scores.shape[1:], jnp.int32)]
+        + [dma((pieces_in,)), dma((weights, sides, count)), dma((5,)), dma((5 + steps,))],
     )
     back, g_parts, (y_down, d_own, inner) = outs[0], outs[1 : 1 + sides], outs[1 + sides :]
     returned = to_peers(back)

time: 155 us -> 152 us (0.981)
  Pallas kernels: 46.2 us -> 43.6 us
    ppermute x7, waiting for transfers between devices: 28.2 us -> 9.78 us  [collect(): lax.ppermute(shares[k], 'exp', [(n, n ^ k) for n in range(peers)])]
    ppermute x6, waiting for transfers between devices: 15.8 us -> 27.1 us  [across(): return lax.ppermute(array, 'seq', pair)]
    all_to_all x3, waiting for transfers between devices: 16.3 us -> 22.1 us  [to_peers(): lax.all_to_all(array, 'exp', split_axis=0, concat_axis=0, tiled=True)]
    pallas_call x11, Pallas kernels: 46.2 us -> 43.6 us  [call(): pl.pallas_call(body, out_shape=[x for x, _ in outs], in_specs=[place for...]
  transfers between devices with their start and end apart: 16 -> 16, of which waited for: 10 -> 8; matrix products, arithmetic and copies ran while one was open for 3% -> 3% of each run, Pallas kernels for 19% -> 18%
where the time goes in v11:
time: 152 us; the launch traced here: 151 us
  waiting for transfers between devices  58.9 us (39%)
  Pallas kernels  43.6 us (29%)
  starting transfers between devices  30.3 us (20%)
  blocking collectives  10.8 us (7%)
  local copies, waits for them, and re-layouts  3.29 us (2%)
  other arithmetic  2.99 us (2%)
    pallas_call x11, Pallas kernels, call(): pl.pallas_call(body, out_shape=[x for x, _ in outs], in_specs=[place for...  43.6 us
    ppermute x6, waiting for transfers between devices, across(): return lax.ppermute(array, 'seq', pair)  27.1 us
    all_to_all x3, waiting for transfers between devices, to_peers(): lax.all_to_all(array, 'exp', split_axis=0, concat_axis=0, tiled=True)  22.1 us
    all_to_all x3, starting transfers between devices, to_peers(): lax.all_to_all(array, 'exp', split_axis=0, concat_axis=0, tiled=True)  18 us
    all_to_all x1, blocking collectives, shards(): lax.all_to_all(told, 'exp', split_axis=0, concat_axis=0, tiled=True)  10.8 us
    ppermute x7, waiting for transfers between devices, collect(): lax.ppermute(shares[k], 'exp', [(n, n ^ k) for n in range(peers)])  9.78 us
    ppermute x7, starting transfers between devices, collect(): lax.ppermute(shares[k], 'exp', [(n, n ^ k) for n in range(peers)])  6.8 us
    ppermute x6, starting transfers between devices, across(): return lax.ppermute(array, 'seq', pair)  5.59 us
  transfers between devices with their start and end apart: 16, of which 8 were waited for; matrix products, arithmetic and copies ran while one was open for 3% of the time, Pallas kernels for 18%

profile of v11, /device:TPU:13, one launch (start us, length us, event | category | flops | bytes accessed | tf_op | source)
XLA Modules:
  0.0 150.9 jit_solution(2081428241717322278)
XLA Ops:
  0.6 2.2 %spread_cotangent.1 = (bf16[128,512]{1,0:T(8,128)(2,1)}, bf16[128,512]{1,0:T(8,128)(2,1)}, bf16[128,512]{1,0:T(8,128)(2,1)}, bf16[128,512]{1,0:T(8,128)(2,1)}, b...) custom-call(s32[1]{0:T(128)} %bitcast.me_ref, ...), custom_call_target="tpu_custom_call" | custom-call | bytes 2097156 | tf_op jit(solution)/shard_map/spread_cotangent/pallas_call | solution.py:40
  3.1 2.1 %collective-permute-start.5 = (bf16[128,512]{1,0:T(8,128)(2,1)}, bf16[128,512]{1,0:T(8,128)(2,1)S(1)}, u32[]{:S(2)}, u32[]{:S(2)}) collective-permute-start(bf16[128,512]{1,0:T(8,128)(2,1)} %get-tuple-element.37), channel_id=1, source_target_pairs={{0,5},{1,4},{2,7},{3,6},{4,1},{5,0},{6,3},{7,2},{8,13},{9,12},{10,... | collective-permute-start | bytes 393224 | tf_op jit(solution)/shard_map/ppermute | solution.py:672
  5.3 2.1 %collective-permute-start.7 = (bf16[128,512]{1,0:T(8,128)(2,1)}, bf16[128,512]{1,0:T(8,128)(2,1)S(1)}, u32[]{:S(2)}, u32[]{:S(2)}) collective-permute-start(bf16[128,512]{1,0:T(8,128)(2,1)} %get-tuple-element.39), channel_id=1, source_target_pairs={{0,7},{1,6},{2,5},{3,4},{4,3},{5,2},{6,1},{7,0},{8,15},{9,14},{10,... | collective-permute-start | bytes 393224 | tf_op jit(solution)/shard_map/ppermute | solution.py:672
  8.9 10.8 %all_to_all.26 = s32[16,2,128]{2,1,0:T(2,128)} all-to-all(s32[16,2,128]{2,1,0:T(2,128)} %bitcast.24), channel_id=1, replica_groups=mesh['seq'=2,'exp'=16] {'exp'}, dimensions={0} | all-to-all | bytes 32768 | tf_op jit(solution)/shard_map/all_to_all | solution.py:662
  20.5 2.9 %pick_tokens.1 = bf16[384,2048]{1,0:T(8,128)(2,1)} custom-call(s32[32,128]{1,0:T(8,128)} %bitcast.21, bf16[128,4096]{1,0:T(8,128)(2,1)} %source_ref.1, bf16[128,512]{1,0:T(8,128)(2,1)} %copy-done.3, bf16[128,512]{1,0:T(8,128)(2,1)} %copy-done.4, bf16[128,512]{1,0:T(8,128)(2,1)} %copy-done.5, bf16[128,512]{1,0:T(8,128)(2,1)} %copy-done.6), custom_call_target="tpu_custom_call" | custom-call | flops 402653184 | bytes 3162112 | tf_op jit(solution)/shard_map/pick_tokens/pallas_call | solution.py:40
  23.5 6.7 %all-to-all-start.2 = ((bf16[16,24,2048]{2,1,0:T(8,128)(2,1)}), bf16[16,24,2048]{2,1,0:T(8,128)(2,1)}, u32[]{:S(2)}, u32[]{:S(2)}) async-start(bf16[16,24,2048]{2,1,0:T(8,128)(2,1)} %bitcast.14), calls=%async_computation.2 | async-start | bytes 3145728 | tf_op jit(solution)/shard_map/all_to_all | solution.py:666
  30.2 2.4 %cut_factors.1 = (bf16[2,4,512,128]{3,2,1,0:T(8,128)(2,1)}, bf16[1,4,512,128]{3,2,1,0:T(8,128)(2,1)}) custom-call(bf16[3,4,512,128]{3,2,1,0:T(8,128)(2,1)} %bitcast.15), custom_call_target="tpu_custom_call" | custom-call | bytes 3145728 | tf_op jit(solution)/shard_map/cut_factors/pallas_call | solution.py:40
  36.2 6.4 %collective-permute-done.2.refs_3_ = bf16[128,512]{1,0:T(8,128)(2,1)S(1)} collective-permute-done((bf16[128,512]{1,0:T(8,128)(2,1)S(1)}, bf16[128,512]{1,0:T(8,128)(2,1)S(1)}, u32[]{:S(2)}, u32[]{:S(2)}) %collective-permute-start.2) | collective-permute-done | bytes 131104 | tf_op jit(solution)/shard_map/ppermute | solution.py:672
  42.6 3.4 %collective-permute-done.3.refs_4_ = bf16[128,512]{1,0:T(8,128)(2,1)S(1)} collective-permute-done((bf16[128,512]{1,0:T(8,128)(2,1)S(1)}, bf16[128,512]{1,0:T(8,128)(2,1)S(1)}, u32[]{:S(2)}, u32[]{:S(2)}) %collective-permute-start.3) | collective-permute-done | bytes 131104 | tf_op jit(solution)/shard_map/ppermute | solution.py:672
  46.0 11.4 %collective-permute-done.refs_0_.refs_1_ = bf16[2,4,512,128]{3,2,1,0:T(8,128)(2,1)} collective-permute-done((bf16[2,4,512,128]{3,2,1,0:T(8,128)(2,1)}, bf16[2,4,512,128]{3,2,1,0:T(8,128)(2,1)}, u32[]{:S(2)}, u32[]{:S(2)}) %collective-permute-start) | collective-permute-done | bytes 1048608 | tf_op jit(solution)/shard_map/ppermute | solution.py:637
  57.4 4.2 %pick_cotangent.1 = bf16[1024,512]{1,0:T(8,128)(2,1)} custom-call(s32[1]{0:T(128)} %bitcast.me_ref, s32[32,128]{1,0:T(8,128)} %bitcast.22, bf16[2,4,512,128]{3,2,1,0:T(8,128)(2,1)} %collective-permute-done.refs_0_.refs_1_, bf16[128,512]{1,0:T(8,128)(2,1)} %get-tuple-element.32.refs_1_, bf16[128,512]{1,0:T(8,128)(2,1)} %copy-done.12, ...), custom_call_target="tpu_custom_call" | custom-call | flops 1073741824 | bytes 3162116 | tf_op jit(solution)/shard_map/pick_cotangent/pallas_call | solution.py:40
  61.7 4.8 %all-to-all-done.2 = bf16[16,24,2048]{2,1,0:T(8,128)(2,1)} async-done(((bf16[16,24,2048]{2,1,0:T(8,128)(2,1)}), bf16[16,24,2048]{2,1,0:T(8,128)(2,1)}, u32[]{:S(2)}, u32[]{:S(2)}) %all-to-all-start.2) | async-done | bytes 1572896 | tf_op jit(solution)/shard_map/all_to_all | solution.py:666
  66.5 4.9 %all-to-all-start.1 = ((bf16[16,64,512]{2,1,0:T(8,128)(2,1)}), bf16[16,64,512]{2,1,0:T(8,128)(2,1)}, u32[]{:S(2)}, u32[]{:S(2)}) async-start(bf16[16,64,512]{2,1,0:T(8,128)(2,1)} %bitcast.20), calls=%async_computation.1 | async-start | bytes 2097152 | tf_op jit(solution)/shard_map/all_to_all | solution.py:666
  73.3 6.9 %forward.1 = (bf16[512,512]{1,0:T(8,128)(2,1)}, bf16[512,512]{1,0:T(8,128)(2,1)}, f32[512,512]{1,0:T(8,128)}, f32[512,512]{1,0:T(8,128)}, f32[128,512]{1,0:T(8,1...) custom-call(s32[1]{0:T(128)} %bitcast.4.order_ref, f32[192]{0:T(256)} %reshape.44.mix_ref, ...), custom_call_target="tpu_custom_call" | custom-call | flops 1073741824 | bytes 8127748 | tf_op jit(solution)/shard_map/forward/pallas_call | solution.py:40
  80.5 4.3 %collective-permute-done.8.refs_2_ = bf16[1,4,512,128]{3,2,1,0:T(8,128)(2,1)} collective-permute-done((bf16[1,4,512,128]{3,2,1,0:T(8,128)(2,1)}, bf16[1,4,512,128]{3,2,1,0:T(8,128)(2,1)}, u32[]{:S(2)}, u32[]{:S(2)}) %collective-permute-start.8) | collective-permute-done | bytes 524320 | tf_op jit(solution)/shard_map/ppermute | solution.py:637
  84.8 11.7 %all-to-all-done.1 = bf16[16,64,512]{2,1,0:T(8,128)(2,1)} async-done(((bf16[16,64,512]{2,1,0:T(8,128)(2,1)}), bf16[16,64,512]{2,1,0:T(8,128)(2,1)}, u32[]{:S(2)}, u32[]{:S(2)}) %all-to-all-start.1) | async-done | bytes 1048608 | tf_op jit(solution)/shard_map/all_to_all | solution.py:666
  97.3 7.6 %backward.1 = (bf16[384,2048]{1,0:T(8,128)(2,1)}, bf16[512,512]{1,0:T(8,128)(2,1)}, bf16[512,512]{1,0:T(8,128)(2,1)}, f32[512,512]{1,0:T(8,128)}, bf16[3,128,512]{2,1,0:T(8,128)(2,1)}, /*index=5*/f32[128,128]{1,0:T(8,128)}) custom-call(s32[1]{0:T(128)} %bitcast.4.order_ref, f32[192]{0:T(256)} %reshape.44.mix_ref, ...), custom_call_target="tpu_custom_call" | custom-call | flops 1610612736 | bytes 9635588 | tf_op jit(solution)/shard_map/backward/pallas_call | solution.py:40
  104.9 6.4 %all-to-all-start.3 = ((bf16[16,24,2048]{2,1,0:T(8,128)(2,1)}), bf16[16,24,2048]{2,1,0:T(8,128)(2,1)}, u32[]{:S(2)}, u32[]{:S(2)}) async-start(bf16[16,24,2048]{2,1,0:T(8,128)(2,1)} %bitcast.19), calls=%async_computation.3 | async-start | bytes 3145728 | tf_op jit(solution)/shard_map/all_to_all | solution.py:666
  112.9 1.8 %place_rows.1.placed_hbm = bf16[256,384]{1,0:T(8,128)(2,1)} custom-call(s32[1]{0:T(128)} %bitcast.me_ref, s32[32,128]{1,0:T(8,128)} %bitcast.23), custom_call_target="tpu_custom_call" | custom-call | flops 1048576 | bytes 212996 | tf_op jit(solution)/shard_map/place_rows/pallas_call | solution.py:40
  114.7 3.9 %mix_partials.1 = f32[192,128]{1,0:T(8,128)} custom-call(f32[512,512]{1,0:T(8,128)} %get-tuple-element.50.yg_hbm, f32[512,512]{1,0:T(8,128)} %get-tuple-element.51.yu_hbm, f32[512,512]{1,0:T(8,128)} %get-tuple-element.52.yd_hbm, bf16[3,128,512]{2,1,0:T(8,128)(2,1)} %get-tuple-element.48.refs_2_.d_hbm), custom_call_target="tpu_custom_call" | custom-call | flops 6291456 | bytes 3637248 | tf_op jit(solution)/shard_map/mix_partials/pallas_call | solution.py:40
  122.4 11.4 %collective-permute-done.12 = f32[1,3,4,4,4]{4,3,2,1,0:T(4,128)S(1)} collective-permute-done((f32[1,3,4,4,4]{4,3,2,1,0:T(4,128)S(1)}, f32[1,3,4,4,4]{4,3,2,1,0:T(4,128)S(1)}, u32[]{:S(2)}, u32[]{:S(2)}) %collective-permute-start.12) | collective-permute-done | bytes 800 | tf_op jit(solution)/shard_map/ppermute | solution.py:637
  135.2 6.9 %factor_grad.1 = f32[3,4,512,128]{3,2,1,0:T(8,128)} custom-call(f32[192]{0:T(256)} %reshape.44.mix_ref, bf16[512,512]{1,0:T(8,128)(2,1)} %get-tuple-element.46.refs_0_, bf16[512,512]{1,0:T(8,128)(2,1)} %get-tuple-element.47.refs_1_, bf16[3,128,512]{2,1,0:T(8,128)(2,1)} %get-tuple-element.48.refs_2_.d_hbm, bf16[512,512]{1,0:T(8,128)(2,1)} %copy-done.1, ...), custom_call_target="tpu_custom_call" | custom-call | flops 1610612736 | bytes 6030080 | tf_op jit(solution)/shard_map/factor_grad/pallas_call | solution.py:40
  142.1 5.5 %all-to-all-done.3 = bf16[16,24,2048]{2,1,0:T(8,128)(2,1)} async-done(((bf16[16,24,2048]{2,1,0:T(8,128)(2,1)}), bf16[16,24,2048]{2,1,0:T(8,128)(2,1)}, u32[]{:S(2)}, u32[]{:S(2)}) %all-to-all-start.3) | async-done | bytes 1572896 | tf_op jit(solution)/shard_map/all_to_all | solution.py:666
  147.6 3.1 %sum_rows.1 = bf16[128,4096]{1,0:T(8,128)(2,1)} custom-call(bf16[256,384]{1,0:T(8,128)(2,1)} %place_rows.1.placed_hbm, bf16[384,2048]{1,0:T(8,128)(2,1)} %bitcast.12.returned_ref), custom_call_target="tpu_custom_call" | custom-call | flops 402653184 | bytes 2818048 | tf_op jit(solution)/shard_map/sum_rows/pallas_call | solution.py:40
  (57 shorter events, 16.1 us)
Async XLA Ops:
  2.9 16.8 %collective-permute-start.4 = (bf16[128,512]{1,0:T(8,128)(2,1)}, bf16[128,512]{1,0:T(8,128)(2,1)S(1)}, u32[]{:S(2)}, u32[]{:S(2)}) collective-permute-start(bf16[128,512]{1,0:T(8,128)(2,1)} %get-tuple-element.36), channel_id=1, source_target_pairs={{0,4},{1,5},{2,6},{3,7},{4,0},{5,1},{6,2},{7,3},{8,12},{9,13},{10,... | collective-permute-start | bytes 393224 | tf_op jit(solution)/shard_map/ppermute | solution.py:672
  3.1 16.6 %collective-permute-start.5 = (bf16[128,512]{1,0:T(8,128)(2,1)}, bf16[128,512]{1,0:T(8,128)(2,1)S(1)}, u32[]{:S(2)}, u32[]{:S(2)}) collective-permute-start(bf16[128,512]{1,0:T(8,128)(2,1)} %get-tuple-element.37), channel_id=1, source_target_pairs={{0,5},{1,4},{2,7},{3,6},{4,1},{5,0},{6,3},{7,2},{8,13},{9,12},{10,... | collective-permute-start | bytes 393224 | tf_op jit(solution)/shard_map/ppermute | solution.py:672
  5.3 14.5 %collective-permute-start.6 = (bf16[128,512]{1,0:T(8,128)(2,1)}, bf16[128,512]{1,0:T(8,128)(2,1)S(1)}, u32[]{:S(2)}, u32[]{:S(2)}) collective-permute-start(bf16[128,512]{1,0:T(8,128)(2,1)} %get-tuple-element.38), channel_id=1, source_target_pairs={{0,6},{1,7},{2,4},{3,5},{4,2},{5,3},{6,0},{7,1},{8,14},{9,15},{10,... | collective-permute-start | bytes 393224 | tf_op jit(solution)/shard_map/ppermute | solution.py:672
  5.3 14.5 %collective-permute-start.7 = (bf16[128,512]{1,0:T(8,128)(2,1)}, bf16[128,512]{1,0:T(8,128)(2,1)S(1)}, u32[]{:S(2)}, u32[]{:S(2)}) collective-permute-start(bf16[128,512]{1,0:T(8,128)(2,1)} %get-tuple-element.39), channel_id=1, source_target_pairs={{0,7},{1,6},{2,5},{3,4},{4,3},{5,2},{6,1},{7,0},{8,15},{9,14},{10,... | collective-permute-start | bytes 393224 | tf_op jit(solution)/shard_map/ppermute | solution.py:672
  23.5 43.0 %all-to-all-start.2 = ((bf16[16,24,2048]{2,1,0:T(8,128)(2,1)}), bf16[16,24,2048]{2,1,0:T(8,128)(2,1)}, u32[]{:S(2)}, u32[]{:S(2)}) async-start(bf16[16,24,2048]{2,1,0:T(8,128)(2,1)} %bitcast.14), calls=%async_computation.2 | async-start | bytes 3145728 | tf_op jit(solution)/shard_map/all_to_all | solution.py:666
  30.1 4.4 %copy-start.10 = (bf16[128,512]{1,0:T(8,128)(2,1)S(1)}, bf16[128,512]{1,0:T(8,128)(2,1)}, u32[]{:S(2)}) copy-start(bf16[128,512]{1,0:T(8,128)(2,1)} %get-tuple-element.34) | copy-start | bytes 393220
  30.1 4.6 %copy-start.9 = (bf16[128,512]{1,0:T(8,128)(2,1)S(1)}, bf16[128,512]{1,0:T(8,128)(2,1)}, u32[]{:S(2)}) copy-start(bf16[128,512]{1,0:T(8,128)(2,1)} %get-tuple-element.35) | copy-start | bytes 393220
  32.6 24.8 %collective-permute-start = (bf16[2,4,512,128]{3,2,1,0:T(8,128)(2,1)}, bf16[2,4,512,128]{3,2,1,0:T(8,128)(2,1)}, u32[]{:S(2)}, u32[]{:S(2)}) collective-permute-start(bf16[2,4,512,128]{3,2,1,0:T(8,128)(2,1)} %get-tuple-element.31), channel_id=1, source_target_pairs={{0,16},{16,0},{1,17},{17,1},{2,18},{18,2},{3,19},{19,3},{4,20},{20... | collective-permute-start | bytes 3145736 | tf_op jit(solution)/shard_map/ppermute | solution.py:637
  33.9 2.4 %collective-permute-start.1 = (bf16[128,512]{1,0:T(8,128)(2,1)S(1)}, bf16[128,512]{1,0:T(8,128)(2,1)S(1)}, u32[]{:S(2)}, u32[]{:S(2)}) collective-permute-start(bf16[128,512]{1,0:T(8,128)(2,1)S(1)} %copy-done.11), channel_id=1, source_target_pairs={{0,1},{1,0},{2,3},{3,2},{4,5},{5,4},{6,7},{7,6},{8,9},{9,8},{10,11... | collective-permute-start | bytes 393224 | tf_op jit(solution)/shard_map/ppermute | solution.py:672
  34.5 8.1 %collective-permute-start.2 = (bf16[128,512]{1,0:T(8,128)(2,1)S(1)}, bf16[128,512]{1,0:T(8,128)(2,1)S(1)}, u32[]{:S(2)}, u32[]{:S(2)}) collective-permute-start(bf16[128,512]{1,0:T(8,128)(2,1)S(1)} %copy-done.10), channel_id=1, source_target_pairs={{0,2},{1,3},{2,0},{3,1},{4,6},{5,7},{6,4},{7,5},{8,10},{9,11},{10,... | collective-permute-start | bytes 393224 | tf_op jit(solution)/shard_map/ppermute | solution.py:672
  34.8 11.2 %collective-permute-start.3 = (bf16[128,512]{1,0:T(8,128)(2,1)S(1)}, bf16[128,512]{1,0:T(8,128)(2,1)S(1)}, u32[]{:S(2)}, u32[]{:S(2)}) collective-permute-start(bf16[128,512]{1,0:T(8,128)(2,1)S(1)} %copy-done.9), channel_id=1, source_target_pairs={{0,3},{1,2},{2,1},{3,0},{4,7},{5,6},{6,5},{7,4},{8,11},{9,10},{10,... | collective-permute-start | bytes 393224 | tf_op jit(solution)/shard_map/ppermute | solution.py:672
  36.2 21.1 %copy-start.12 = (bf16[128,512]{1,0:T(8,128)(2,1)}, bf16[128,512]{1,0:T(8,128)(2,1)S(1)}, u32[]{:S(2)}) copy-start(bf16[128,512]{1,0:T(8,128)(2,1)S(1)} %collective-permute-done.1.refs_2_) | copy-start | bytes 393220
  42.6 14.8 %copy-start.13 = (bf16[128,512]{1,0:T(8,128)(2,1)}, bf16[128,512]{1,0:T(8,128)(2,1)S(1)}, u32[]{:S(2)}) copy-start(bf16[128,512]{1,0:T(8,128)(2,1)S(1)} %collective-permute-done.2.refs_3_) | copy-start | bytes 393220
  46.0 11.4 %copy-start.14 = (bf16[128,512]{1,0:T(8,128)(2,1)}, bf16[128,512]{1,0:T(8,128)(2,1)S(1)}, u32[]{:S(2)}) copy-start(bf16[128,512]{1,0:T(8,128)(2,1)S(1)} %collective-permute-done.3.refs_4_) | copy-start | bytes 393220
  61.6 10.9 %copy-start.8 = (f32[1,3,4,4,4]{4,3,2,1,0:T(4,128)S(1)}, f32[1,3,4,4,4]{4,3,2,1,0:T(4,128)}, u32[]{:S(2)}) copy-start(f32[1,3,4,4,4]{4,3,2,1,0:T(4,128)} %param.9) | copy-start | bytes 2308
  66.5 30.0 %all-to-all-start.1 = ((bf16[16,64,512]{2,1,0:T(8,128)(2,1)}), bf16[16,64,512]{2,1,0:T(8,128)(2,1)}, u32[]{:S(2)}, u32[]{:S(2)}) async-start(bf16[16,64,512]{2,1,0:T(8,128)(2,1)} %bitcast.20), calls=%async_computation.1 | async-start | bytes 2097152 | tf_op jit(solution)/shard_map/all_to_all | solution.py:666
  71.4 13.5 %collective-permute-start.8 = (bf16[1,4,512,128]{3,2,1,0:T(8,128)(2,1)}, bf16[1,4,512,128]{3,2,1,0:T(8,128)(2,1)}, u32[]{:S(2)}, u32[]{:S(2)}) collective-permute-start(bf16[1,4,512,128]{3,2,1,0:T(8,128)(2,1)} %get-tuple-element.43), channel_id=1, source_target_pairs={{0,16},{16,0},{1,17},{17,1},{2,18},{18,2},{3,19},{19,3},{4,20},{20... | collective-permute-start | bytes 1572872 | tf_op jit(solution)/shard_map/ppermute | solution.py:637
  80.2 16.4 %collective-permute-start.9 = (bf16[512,512]{1,0:T(8,128)(2,1)}, bf16[512,512]{1,0:T(8,128)(2,1)S(1)}, u32[]{:S(2)}, u32[]{:S(2)}) collective-permute-start(bf16[512,512]{1,0:T(8,128)(2,1)} %get-tuple-element.44), channel_id=1, source_target_pairs={{0,16},{16,0},{1,17},{17,1},{2,18},{18,2},{3,19},{19,3},{4,20},{20... | collective-permute-start | bytes 1572872 | tf_op jit(solution)/shard_map/ppermute | solution.py:637
  104.9 7.7 %copy-start = (bf16[3,128,512]{2,1,0:T(8,128)(2,1)S(1)}, bf16[3,128,512]{2,1,0:T(8,128)(2,1)}, u32[]{:S(2)}) copy-start(bf16[3,128,512]{2,1,0:T(8,128)(2,1)} %get-tuple-element.48.refs_2_.d_hbm) | copy-start | bytes 1179652
  104.9 42.7 %all-to-all-start.3 = ((bf16[16,24,2048]{2,1,0:T(8,128)(2,1)}), bf16[16,24,2048]{2,1,0:T(8,128)(2,1)}, u32[]{:S(2)}, u32[]{:S(2)}) async-start(bf16[16,24,2048]{2,1,0:T(8,128)(2,1)} %bitcast.19), calls=%async_computation.3 | async-start | bytes 3145728 | tf_op jit(solution)/shard_map/all_to_all | solution.py:666
  111.3 23.1 %collective-permute-start.10 = (bf16[512,512]{1,0:T(8,128)(2,1)}, bf16[512,512]{1,0:T(8,128)(2,1)S(1)}, u32[]{:S(2)}, u32[]{:S(2)}) collective-permute-start(bf16[512,512]{1,0:T(8,128)(2,1)} %get-tuple-element.49), channel_id=1, source_target_pairs={{0,16},{16,0},{1,17},{17,1},{2,18},{18,2},{3,19},{19,3},{4,20},{20... | collective-permute-start | bytes 1572872 | tf_op jit(solution)/shard_map/ppermute | solution.py:637
  112.6 21.8 %collective-permute-start.11 = (bf16[3,128,512]{2,1,0:T(8,128)(2,1)S(1)}, bf16[3,128,512]{2,1,0:T(8,128)(2,1)}, u32[]{:S(2)}, u32[]{:S(2)}) collective-permute-start(bf16[3,128,512]{2,1,0:T(8,128)(2,1)S(1)} %copy-done), channel_id=1, source_target_pairs={{0,16},{16,0},{1,17},{17,1},{2,18},{18,2},{3,19},{19,3},{4,20},{20... | collective-permute-start | bytes 1179656 | tf_op jit(solution)/shard_map/ppermute | solution.py:637
  114.7 6.3 %copy-start.7 = (f32[128,128]{1,0:T(8,128)S(1)}, f32[128,128]{1,0:T(8,128)}, u32[]{:S(2)}) copy-start(f32[128,128]{1,0:T(8,128)} %get-tuple-element.53) | copy-start | bytes 196612
  119.7 14.1 %collective-permute-start.12 = (f32[1,3,4,4,4]{4,3,2,1,0:T(4,128)S(1)}, f32[1,3,4,4,4]{4,3,2,1,0:T(4,128)S(1)}, u32[]{:S(2)}, u32[]{:S(2)}) collective-permute-start(f32[1,3,4,4,4]{4,3,2,1,0:T(4,128)S(1)} %reshape.51), channel_id=1, source_target_pairs={{0,16},{16,0},{1,17},{17,1},{2,18},{18,2},{3,19},{19,3},{4,20},{20... | collective-permute-start | bytes 2312 | tf_op jit(solution)/shard_map/ppermute | solution.py:637
  (7 other events, 8.2 us)

commit v12 on v11

--- a/solution.py
+++ b/solution.py
@@ -68,7 +68,15 @@
     return [slice(c * chunk, (c + 1) * chunk) for c in range(part // chunk)]
 
 
-def index_body(cap, pieces, own_rows, block_len, chosen_ref, told_ref, slot_ref):
+def front_body(cap, pieces, own_rows, block_len, half, cross, me_ref, chosen_ref, *refs):
+    if cross:
+        source_ref, told_ref, slot_ref, cross_ref, held_ref, sems = refs
+        width = cross_ref.shape[1]
+        plane = lax.shift_right_logical(me_ref[0] & (half - 1), half.bit_length() - 2)
+        at = pl.ds(pl.multiple_of((1 - plane) * width, width), width)
+        load = begin(source_ref.at[:, at], held_ref, sems.at[0])
+    else:
+        told_ref, slot_ref = refs
     peers, rows = told_ref.shape[0] // 2, slot_ref.shape[1]
     blocks = [chosen_ref[b : b + 1, :] for b in range(chosen_ref.shape[0])]
     position = jnp.concatenate([x + b * block_len for b, x in enumerate(blocks)], axis=1)
@@ -88,6 +96,47 @@
     marked = jnp.where(twice == 2 * owner, local + 1, 0).astype(F32)
     asked = dot_nt(marked.astype(BF16), hit.astype(BF16)).astype(jnp.int32)
     told_ref[...] = jnp.where((twice & 1) == 1, jnp.concatenate(blocks, axis=1), asked)
+    if cross:
+        load.wait()
+        begin(held_ref, cross_ref, sems.at[1]).wait()
+
+
+def plane_columns(me, source, crossed, half):
+    own_rows, width = source.shape
+    part, count = width // half, half // 2
+
+    def body(me_ref, source_ref, crossed_ref, *refs):
+        outs, (held_ref, in_sem, out_sem) = refs[:count], refs[count:]
+        low = me_ref[0] & (half - 1)
+        plane = lax.shift_right_logical(low, half.bit_length() - 2)
+        wide = count * part
+        at = pl.ds(pl.multiple_of(plane * wide, wide), wide)
+        loads = [
+            begin(source_ref.at[:, at], held_ref.at[0], in_sem.at[0]),
+            begin(crossed_ref, held_ref.at[1], in_sem.at[1]),
+        ]
+        copies = []
+        for n, load in enumerate(loads):
+            load.wait()
+            for k in range(count):
+                share = (low & (count - 1)) ^ k
+                at = held_ref.at[n, :, pl.ds(pl.multiple_of(share * part, part), part)]
+                rows = pl.ds(n * own_rows, own_rows)
+                copies.append(begin(at, outs[k].at[rows], out_sem.at[n, k]))
+        wait_all(copies)
+
+    return call(
+        body,
+        [(shaped((2 * own_rows, part), BF16), HBM)] * count,
+        [(me, SMEM), (source, HBM), (crossed, HBM)],
+        "plane_columns",
+        0,
+        [
+            scratch_like((2, own_rows, count * part), BF16),
+            pltpu.SemaphoreType.DMA((2,)),
+            pltpu.SemaphoreType.DMA((2, count)),
+        ],
+    )
 
 
 def pick_matrix(cap, pieces, own_rows, requested):
@@ -153,38 +202,26 @@
     )[0]
 
 
-def spread_columns(me, sources, half, direct, name):
-    own_rows, width = sources[0].shape
-    count = len(sources)
+def spread_columns(source, half):
+    own_rows, width = source.shape
     part = width // half
-    tall = count * own_rows
-
-    def body(me_ref, *refs):
-        ins, outs = refs[:count], refs[count : -3]
-        held_ref, in_sem, out_sem = refs[-3:]
-        loads = [begin(ref, held_ref.at[n], in_sem.at[n]) for n, ref in enumerate(ins)]
-        low = me_ref[0] & (half - 1)
+
+    def body(source_ref, out_ref, held_ref, in_sem, out_sem):
+        begin(source_ref, held_ref, in_sem).wait()
         copies = []
-        for n, load in enumerate(loads):
-            load.wait()
-            for k in range(half):
-                share = low ^ k if direct else k
-                at = held_ref.at[n, :, pl.ds(pl.multiple_of(share * part, part), part)]
-                out, first = (outs[k], 0) if direct else (outs[0], k * tall)
-                rows = pl.ds(first + n * own_rows, own_rows)
-                copies.append(begin(at, out.at[rows], out_sem.at[n, k]))
+        for k in range(half):
+            at = held_ref.at[:, k * part : (k + 1) * part]
+            out = out_ref.at[k * own_rows : (k + 1) * own_rows]
+            copies.append(begin(at, out, out_sem.at[k]))
         wait_all(copies)
 
-    if direct:
-        outs = [(shaped((tall, part), BF16), HBM)] * half
-    else:
-        outs = [(shaped((half * tall, part), BF16), HBM)]
     scratch = [
-        scratch_like((count, own_rows, width), BF16),
-        pltpu.SemaphoreType.DMA((count,)),
-        pltpu.SemaphoreType.DMA((count, half)),
+        scratch_like((own_rows, width), BF16),
+        pltpu.SemaphoreType.DMA,
+        pltpu.SemaphoreType.DMA((half,)),
     ]
-    return call(body, outs, [(me, SMEM)] + [(x, HBM) for x in sources], name, 0, scratch)
+    outs = [(shaped((half * own_rows, part), BF16), HBM)]
+    return call(body, outs, [(source, HBM)], "spread_columns", 0, scratch)[0]
 
 
 def cut_factors(factors, first):
@@ -208,12 +245,11 @@
     return call(body, outs, [(factors, HBM)], "cut_factors", 0, scratch)
 
 
-def pick_rows(me, half, own_rows, which, chosen, shares, after, name):
+def pick_rows(me, half, own_rows, chosen, shares, after, name):
     peers, total = chosen.shape[0] // 2, chosen.shape[1]
     picks = total * half // peers
     part = shares[0].shape[1]
     block = half * own_rows
-    tall = sum(x.shape[0] for x in shares) // half
     batch = min(peers, 8)
 
     def body(me_ref, chosen_ref, *refs):
@@ -225,10 +261,10 @@
         loads = []
         for k in range(half):
             place = (me_ref[0] & (half - 1)) ^ k if len(parts) > 1 else k
-            share, first = (parts[k], 0) if len(parts) > 1 else (parts[0], k * tall)
-            first += which * own_rows
+            n, first = (k % len(parts), k // len(parts)) if len(parts) > 1 else (0, k)
+            at = parts[n].at[first * own_rows : (first + 1) * own_rows]
             target = rows_ref.at[pl.ds(pl.multiple_of(place * own_rows, own_rows), own_rows)]
-            loads.append(begin(share.at[first : first + own_rows], target, in_sem.at[k]))
+            loads.append(begin(at, target, in_sem.at[k]))
         block_at = lax.shift_right_logical(me_ref[0], half.bit_length() - 1)
         same = iota((picks, total), 0) + block_at * picks == iota((picks, total), 1)
         stores = []
@@ -641,8 +677,6 @@
     me = lax.axis_index("exp").astype(jnp.int32).reshape(1)
     group = lax.axis_index("seq").astype(jnp.int32).reshape(1)
     halves = [list(range(h, h + half)) for h in range(0, peers, half)]
-    near = [k for k in range(1, half) if k >= 4] + [k for k in range(1, half) if k < 4]
-
     if swap:
         cuts = [across(x) for x in cut_factors(factors[0], 2)]
         factor_parts = [factors[0]] + cuts
@@ -652,13 +686,17 @@
         factor_parts = [lax.all_gather(factors, "seq", axis=3, tiled=True)[0]]
         sides = 1
     sides_in = [(x, HBM) for x in factor_parts]
-    told, slot = call(
-        functools.partial(index_body, cap, pieces, own_rows, block_len),
-        [(shaped((2 * peers, rows), jnp.int32), VMEM), (shaped((1, rows), jnp.int32), VMEM)],
-        [(selection[0], VMEM)],
+    cross = [(shaped((own_rows, width // 2), BF16), HBM)] if direct else []
+    told, slot, *crossed = call(
+        functools.partial(front_body, cap, pieces, own_rows, block_len, half, direct),
+        [(shaped((2 * peers, rows), jnp.int32), VMEM), (shaped((1, rows), jnp.int32), VMEM)] + cross,
+        [(me, SMEM), (selection[0], VMEM)] + ([(cotangent, HBM)] if direct else []),
         "wanted_rows",
         1 << 20,
+        [scratch_like((own_rows, width // 2), BF16), dma((2,))] if direct else [],
     )
+    if direct:
+        crossed = [lax.ppermute(crossed[0], "exp", [(n, n ^ (half // 2)) for n in range(peers)])]
     chosen = lax.all_to_all(told, "exp", split_axis=0, concat_axis=0, tiled=True)
 
     def to_peers(array):
@@ -666,22 +704,20 @@
         array = lax.all_to_all(array, "exp", split_axis=0, concat_axis=0, tiled=True)
         return array.reshape(-1, array.shape[2])
 
-    def collect(shares):
-        if direct:
-            moved = {
-                k: lax.ppermute(shares[k], "exp", [(n, n ^ k) for n in range(peers)]) for k in near
-            }
-            return [shares[0]] + [moved[k] for k in range(1, half)]
-        array = shares[0].reshape(half, -1, shares[0].shape[1])
+    got_rows = to_peers(pick_slots(cap, pieces, chosen, tokens, crossed, "pick_tokens"))
+    if direct:
+        shares = plane_columns(me, cotangent, crossed[0], half)
+        shares = [shares[0]] + [
+            lax.ppermute(shares[k], "exp", [(n, n ^ k) for n in range(peers)])
+            for k in range(1, half // 2)
+        ]
+    else:
+        array = spread_columns(cotangent, half).reshape(half, own_rows, -1)
         array = lax.all_to_all(
             array, "exp", split_axis=0, concat_axis=0, axis_index_groups=halves, tiled=True
         )
-        return [array.reshape(shares[0].shape)]
-
-    shares = collect(spread_columns(me, [cotangent], half, direct, "spread_cotangent"))
-    early = shares[4:] if direct else []
-    got_rows = to_peers(pick_slots(cap, pieces, chosen, tokens, early, "pick_tokens"))
-    picked = pick_rows(me, half, own_rows, 0, chosen, shares, cuts[:1], "pick_cotangent")
+        shares = [array.reshape(half * own_rows, -1)]
+    picked = pick_rows(me, half, own_rows, chosen, shares, cuts[:1], "pick_cotangent")
     got_grads = to_peers(picked)
     placed = place_rows(cap, pieces, own_rows, me, half, chosen)
     gate = jax.nn.sigmoid(scores[0].reshape(-1).astype(F32) / 64.0)

time: 152 us -> 151 us (level)
  blocking collectives: 10.8 us -> 15.3 us
  starting transfers between devices: 30.3 us -> 26.2 us
  waiting for transfers between devices: 58.9 us -> 56.1 us
    ppermute x6, waiting for transfers between devices: 27.1 us -> 15.7 us  [across(): return lax.ppermute(array, 'seq', pair)]
    ppermute x7 -> x4, waiting for transfers between devices: 9.78 us -> 20.6 us  [the longest x3 20.6 us: shards(): lax.ppermute(shares[k], 'exp', [(n, n ^ k) for n in range(peers)])]
    all_to_all x1, blocking collectives: 10.8 us -> 15.3 us  [shards(): lax.all_to_all(told, 'exp', split_axis=0, concat_axis=0, tiled=True)]
    ppermute x7 -> x4, starting transfers between devices: 6.8 us -> 2.65 us  [the longest x3 2.42 us: shards(): lax.ppermute(shares[k], 'exp', [(n, n ^ k) for n in range(peers)])]
    all_to_all x3, waiting for transfers between devices: 22.1 us -> 19.9 us  [to_peers(): lax.all_to_all(array, 'exp', split_axis=0, concat_axis=0, tiled=True)]
    unnamed x30 -> x18, local copies, waits for them, and re-layouts: 2.39 us -> 3.1 us
  transfers between devices with their start and end apart: 16 -> 13, of which waited for: 8 -> 7; matrix products, arithmetic and copies ran while one was open for 3% -> 3% of each run, Pallas kernels for 18% -> 19%
where the time goes in v12:
time: 151 us; the launch traced here: 150 us
  waiting for transfers between devices  56.1 us (37%)
  Pallas kernels  45 us (30%)
  starting transfers between devices  26.2 us (17%)
  blocking collectives  15.3 us (10%)
  local copies, waits for them, and re-layouts  3.98 us (3%)
  other arithmetic  2.99 us (2%)
    pallas_call x11, Pallas kernels, call(): pl.pallas_call(body, out_shape=[x for x, _ in outs], in_specs=[place for...  45 us
    ppermute x3, waiting for transfers between devices, shards(): lax.ppermute(shares[k], 'exp', [(n, n ^ k) for n in range(peers)])  20.6 us
    all_to_all x3, waiting for transfers between devices, to_peers(): lax.all_to_all(array, 'exp', split_axis=0, concat_axis=0, tiled=True)  19.9 us
    all_to_all x3, starting transfers between devices, to_peers(): lax.all_to_all(array, 'exp', split_axis=0, concat_axis=0, tiled=True)  17.9 us
    ppermute x6, waiting for transfers between devices, across(): return lax.ppermute(array, 'seq', pair)  15.7 us
    all_to_all x1, blocking collectives, shards(): lax.all_to_all(told, 'exp', split_axis=0, concat_axis=0, tiled=True)  15.3 us
    ppermute x6, starting transfers between devices, across(): return lax.ppermute(array, 'seq', pair)  5.62 us
    unnamed x18, local copies, waits for them, and re-layouts  3.1 us
  transfers between devices with their start and end apart: 13, of which 7 were waited for; matrix products, arithmetic and copies ran while one was open for 3% of the time, Pallas kernels for 19%

profile of v12, /device:TPU:13, one launch (start us, length us, event | category | flops | bytes accessed | tf_op | source)
XLA Modules:
  0.0 150.4 jit_solution(9730323738703229815)
XLA Ops:
  0.6 3.1 %wanted_rows.1 = (s32[32,128]{1,0:T(8,128)}, s32[1,128]{1,0:T(1,128)}, bf16[128,2048]{1,0:T(8,128)(2,1)}) custom-call(s32[1]{0:T(128)} %bitcast.me_ref, s32[2,64]{1,0:T(2,128)} %bitcast.25, bf16[128,4096]{1,0:T(8,128)(2,1)} %source_ref.2), custom_call_target="tpu_custom_call" | custom-call | flops 1048576 | bytes 1590276 | tf_op jit(solution)/shard_map/wanted_rows/pallas_call | solution.py:40
  4.0 15.3 %all_to_all.26 = s32[16,2,128]{2,1,0:T(2,128)} all-to-all(s32[16,2,128]{2,1,0:T(2,128)} %bitcast.24), channel_id=1, replica_groups=mesh['seq'=2,'exp'=16] {'exp'}, dimensions={0} | all-to-all | bytes 32768 | tf_op jit(solution)/shard_map/all_to_all | solution.py:700
  20.1 2.9 %pick_tokens.1 = bf16[384,2048]{1,0:T(8,128)(2,1)} custom-call(s32[32,128]{1,0:T(8,128)} %bitcast.21, bf16[128,4096]{1,0:T(8,128)(2,1)} %source_ref.3, bf16[128,2048]{1,0:T(8,128)(2,1)} %copy-done), custom_call_target="tpu_custom_call" | custom-call | flops 402653184 | bytes 3162112 | tf_op jit(solution)/shard_map/pick_tokens/pallas_call | solution.py:40
  23.0 6.7 %all-to-all-start.2 = ((bf16[16,24,2048]{2,1,0:T(8,128)(2,1)}), bf16[16,24,2048]{2,1,0:T(8,128)(2,1)}, u32[]{:S(2)}, u32[]{:S(2)}) async-start(bf16[16,24,2048]{2,1,0:T(8,128)(2,1)} %bitcast.14), calls=%async_computation.2 | async-start | bytes 3145728 | tf_op jit(solution)/shard_map/all_to_all | solution.py:704
  29.7 2.4 %cut_factors.1 = (bf16[2,4,512,128]{3,2,1,0:T(8,128)(2,1)}, bf16[1,4,512,128]{3,2,1,0:T(8,128)(2,1)}) custom-call(bf16[3,4,512,128]{3,2,1,0:T(8,128)(2,1)} %bitcast.15), custom_call_target="tpu_custom_call" | custom-call | bytes 3145728 | tf_op jit(solution)/shard_map/cut_factors/pallas_call | solution.py:40
  32.1 1.3 collective-permute-start
  33.4 2.1 %plane_columns.1 = (bf16[256,512]{1,0:T(8,128)(2,1)}, bf16[256,512]{1,0:T(8,128)(2,1)}, bf16[256,512]{1,0:T(8,128)(2,1)}, bf16[256,512]{1,0:T(8,128)(2,1)}) custom-call(s32[1]{0:T(128)} %bitcast.me_ref, bf16[128,4096]{1,0:T(8,128)(2,1)} %source_ref.2, bf16[128,2048]{1,0:T(8,128)(2,1)} %copy-done), custom_call_target="tpu_custom_call" | custom-call | bytes 2621444 | tf_op jit(solution)/shard_map/plane_columns/pallas_call | solution.py:40
  36.5 1.4 collective-permute-start.4
  37.9 10.8 %collective-permute-done.3.refs_3_ = bf16[256,512]{1,0:T(8,128)(2,1)S(1)} collective-permute-done((bf16[256,512]{1,0:T(8,128)(2,1)}, bf16[256,512]{1,0:T(8,128)(2,1)S(1)}, u32[]{:S(2)}, u32[]{:S(2)}) %collective-permute-start.3) | collective-permute-done | bytes 262176 | tf_op jit(solution)/shard_map/ppermute | solution.py:711
  48.7 9.8 %collective-permute-done.4.refs_4_ = bf16[256,512]{1,0:T(8,128)(2,1)S(1)} collective-permute-done((bf16[256,512]{1,0:T(8,128)(2,1)}, bf16[256,512]{1,0:T(8,128)(2,1)S(1)}, u32[]{:S(2)}, u32[]{:S(2)}) %collective-permute-start.4) | collective-permute-done | bytes 262176 | tf_op jit(solution)/shard_map/ppermute | solution.py:711
  59.2 4.2 %pick_cotangent.1 = bf16[1024,512]{1,0:T(8,128)(2,1)} custom-call(s32[1]{0:T(128)} %bitcast.me_ref, s32[32,128]{1,0:T(8,128)} %bitcast.22, bf16[2,4,512,128]{3,2,1,0:T(8,128)(2,1)} %collective-permute-done.refs_0_.refs_1_, bf16[256,512]{1,0:T(8,128)(2,1)} %get-tuple-element.30.refs_1_, bf16[256,512]{1,0:T(8,128)(2,1)} %copy-done.6, ...), custom_call_target="tpu_custom_call" | custom-call | flops 1073741824 | bytes 3162116 | tf_op jit(solution)/shard_map/pick_cotangent/pallas_call | solution.py:40
  63.4 2.6 %all-to-all-done.2 = bf16[16,24,2048]{2,1,0:T(8,128)(2,1)} async-done(((bf16[16,24,2048]{2,1,0:T(8,128)(2,1)}), bf16[16,24,2048]{2,1,0:T(8,128)(2,1)}, u32[]{:S(2)}, u32[]{:S(2)}) %all-to-all-start.2) | async-done | bytes 1572896 | tf_op jit(solution)/shard_map/all_to_all | solution.py:704
  66.1 4.8 %all-to-all-start.1 = ((bf16[16,64,512]{2,1,0:T(8,128)(2,1)}), bf16[16,64,512]{2,1,0:T(8,128)(2,1)}, u32[]{:S(2)}, u32[]{:S(2)}) async-start(bf16[16,64,512]{2,1,0:T(8,128)(2,1)} %bitcast.20), calls=%async_computation.1 | async-start | bytes 2097152 | tf_op jit(solution)/shard_map/all_to_all | solution.py:704
  72.8 6.9 %forward.1 = (bf16[512,512]{1,0:T(8,128)(2,1)}, bf16[512,512]{1,0:T(8,128)(2,1)}, f32[512,512]{1,0:T(8,128)}, f32[512,512]{1,0:T(8,128)}, f32[128,512]{1,0:T(8,1...) custom-call(s32[1]{0:T(128)} %bitcast.4.order_ref, f32[192]{0:T(256)} %reshape.44.mix_ref, ...), custom_call_target="tpu_custom_call" | custom-call | flops 1073741824 | bytes 8127748 | tf_op jit(solution)/shard_map/forward/pallas_call | solution.py:40
  80.0 4.3 %collective-permute-done.5.refs_2_ = bf16[1,4,512,128]{3,2,1,0:T(8,128)(2,1)} collective-permute-done((bf16[1,4,512,128]{3,2,1,0:T(8,128)(2,1)}, bf16[1,4,512,128]{3,2,1,0:T(8,128)(2,1)}, u32[]{:S(2)}, u32[]{:S(2)}) %collective-permute-start.5) | collective-permute-done | bytes 524320 | tf_op jit(solution)/shard_map/ppermute | solution.py:673
  84.3 11.7 %all-to-all-done.1 = bf16[16,64,512]{2,1,0:T(8,128)(2,1)} async-done(((bf16[16,64,512]{2,1,0:T(8,128)(2,1)}), bf16[16,64,512]{2,1,0:T(8,128)(2,1)}, u32[]{:S(2)}, u32[]{:S(2)}) %all-to-all-start.1) | async-done | bytes 1048608 | tf_op jit(solution)/shard_map/all_to_all | solution.py:704
  96.8 7.6 %backward.1 = (bf16[384,2048]{1,0:T(8,128)(2,1)}, bf16[512,512]{1,0:T(8,128)(2,1)}, bf16[512,512]{1,0:T(8,128)(2,1)}, f32[512,512]{1,0:T(8,128)}, bf16[3,128,512]{2,1,0:T(8,128)(2,1)}, /*index=5*/f32[128,128]{1,0:T(8,128)}) custom-call(s32[1]{0:T(128)} %bitcast.4.order_ref, f32[192]{0:T(256)} %reshape.44.mix_ref, ...), custom_call_target="tpu_custom_call" | custom-call | flops 1610612736 | bytes 9635588 | tf_op jit(solution)/shard_map/backward/pallas_call | solution.py:40
  104.5 6.4 %all-to-all-start.3 = ((bf16[16,24,2048]{2,1,0:T(8,128)(2,1)}), bf16[16,24,2048]{2,1,0:T(8,128)(2,1)}, u32[]{:S(2)}, u32[]{:S(2)}) async-start(bf16[16,24,2048]{2,1,0:T(8,128)(2,1)} %bitcast.19), calls=%async_computation.3 | async-start | bytes 3145728 | tf_op jit(solution)/shard_map/all_to_all | solution.py:704
  112.4 1.8 %place_rows.1.placed_hbm = bf16[256,384]{1,0:T(8,128)(2,1)} custom-call(s32[1]{0:T(128)} %bitcast.me_ref, s32[32,128]{1,0:T(8,128)} %bitcast.23), custom_call_target="tpu_custom_call" | custom-call | flops 1048576 | bytes 212996 | tf_op jit(solution)/shard_map/place_rows/pallas_call | solution.py:40
  114.3 3.9 %mix_partials.1 = f32[192,128]{1,0:T(8,128)} custom-call(f32[512,512]{1,0:T(8,128)} %get-tuple-element.44.yg_hbm, f32[512,512]{1,0:T(8,128)} %get-tuple-element.45.yu_hbm, f32[512,512]{1,0:T(8,128)} %get-tuple-element.46.yd_hbm, bf16[3,128,512]{2,1,0:T(8,128)(2,1)} %get-tuple-element.42.refs_2_.d_hbm), custom_call_target="tpu_custom_call" | custom-call | flops 6291456 | bytes 3637248 | tf_op jit(solution)/shard_map/mix_partials/pallas_call | solution.py:40
  122.0 11.3 %collective-permute-done.9 = f32[1,3,4,4,4]{4,3,2,1,0:T(4,128)S(1)} collective-permute-done((f32[1,3,4,4,4]{4,3,2,1,0:T(4,128)S(1)}, f32[1,3,4,4,4]{4,3,2,1,0:T(4,128)S(1)}, u32[]{:S(2)}, u32[]{:S(2)}) %collective-permute-start.9) | collective-permute-done | bytes 800 | tf_op jit(solution)/shard_map/ppermute | solution.py:673
  134.8 6.9 %factor_grad.1 = f32[3,4,512,128]{3,2,1,0:T(8,128)} custom-call(f32[192]{0:T(256)} %reshape.44.mix_ref, bf16[512,512]{1,0:T(8,128)(2,1)} %get-tuple-element.40.refs_0_, bf16[512,512]{1,0:T(8,128)(2,1)} %get-tuple-element.41.refs_1_, bf16[3,128,512]{2,1,0:T(8,128)(2,1)} %get-tuple-element.42.refs_2_.d_hbm, bf16[512,512]{1,0:T(8,128)(2,1)} %copy-done.2, ...), custom_call_target="tpu_custom_call" | custom-call | flops 1610612736 | bytes 6030080 | tf_op jit(solution)/shard_map/factor_grad/pallas_call | solution.py:40
  141.6 5.5 %all-to-all-done.3 = bf16[16,24,2048]{2,1,0:T(8,128)(2,1)} async-done(((bf16[16,24,2048]{2,1,0:T(8,128)(2,1)}), bf16[16,24,2048]{2,1,0:T(8,128)(2,1)}, u32[]{:S(2)}, u32[]{:S(2)}) %all-to-all-start.3) | async-done | bytes 1572896 | tf_op jit(solution)/shard_map/all_to_all | solution.py:704
  147.2 3.1 %sum_rows.1 = bf16[128,4096]{1,0:T(8,128)(2,1)} custom-call(bf16[256,384]{1,0:T(8,128)(2,1)} %place_rows.1.placed_hbm, bf16[384,2048]{1,0:T(8,128)(2,1)} %bitcast.12.returned_ref), custom_call_target="tpu_custom_call" | custom-call | flops 402653184 | bytes 2818048 | tf_op jit(solution)/shard_map/sum_rows/pallas_call | solution.py:40
  (39 shorter events, 12.6 us)
Async XLA Ops:
  3.8 15.5 %collective-permute-start.1 = (bf16[128,2048]{1,0:T(8,128)(2,1)}, bf16[128,2048]{1,0:T(8,128)(2,1)S(1)}, u32[]{:S(2)}, u32[]{:S(2)}) collective-permute-start(bf16[128,2048]{1,0:T(8,128)(2,1)} %get-tuple-element.29), channel_id=1, source_target_pairs={{0,4},{1,5},{2,6},{3,7},{4,0},{5,1},{6,2},{7,3},{8,12},{9,13},{10,... | collective-permute-start | bytes 1572872 | tf_op jit(solution)/shard_map/ppermute | solution.py:699
  19.3 0.8 copy-start
  23.0 43.1 %all-to-all-start.2 = ((bf16[16,24,2048]{2,1,0:T(8,128)(2,1)}), bf16[16,24,2048]{2,1,0:T(8,128)(2,1)}, u32[]{:S(2)}, u32[]{:S(2)}) async-start(bf16[16,24,2048]{2,1,0:T(8,128)(2,1)} %bitcast.14), calls=%async_computation.2 | async-start | bytes 3145728 | tf_op jit(solution)/shard_map/all_to_all | solution.py:704
  32.1 26.4 %collective-permute-start = (bf16[2,4,512,128]{3,2,1,0:T(8,128)(2,1)}, bf16[2,4,512,128]{3,2,1,0:T(8,128)(2,1)}, u32[]{:S(2)}, u32[]{:S(2)}) collective-permute-start(bf16[2,4,512,128]{3,2,1,0:T(8,128)(2,1)} %get-tuple-element.28), channel_id=1, source_target_pairs={{0,16},{16,0},{1,17},{17,1},{2,18},{18,2},{3,19},{19,3},{4,20},{20... | collective-permute-start | bytes 3145736 | tf_op jit(solution)/shard_map/ppermute | solution.py:673
  35.5 2.4 %collective-permute-start.2 = (bf16[256,512]{1,0:T(8,128)(2,1)}, bf16[256,512]{1,0:T(8,128)(2,1)S(1)}, u32[]{:S(2)}, u32[]{:S(2)}) collective-permute-start(bf16[256,512]{1,0:T(8,128)(2,1)} %get-tuple-element.31), channel_id=1, source_target_pairs={{0,1},{1,0},{2,3},{3,2},{4,5},{5,4},{6,7},{7,6},{8,9},{9,8},{10,11... | collective-permute-start | bytes 786440 | tf_op jit(solution)/shard_map/ppermute | solution.py:711
  36.2 12.5 %collective-permute-start.3 = (bf16[256,512]{1,0:T(8,128)(2,1)}, bf16[256,512]{1,0:T(8,128)(2,1)S(1)}, u32[]{:S(2)}, u32[]{:S(2)}) collective-permute-start(bf16[256,512]{1,0:T(8,128)(2,1)} %get-tuple-element.32), channel_id=1, source_target_pairs={{0,2},{1,3},{2,0},{3,1},{4,6},{5,7},{6,4},{7,5},{8,10},{9,11},{10,... | collective-permute-start | bytes 786440 | tf_op jit(solution)/shard_map/ppermute | solution.py:711
  36.5 22.0 %collective-permute-start.4 = (bf16[256,512]{1,0:T(8,128)(2,1)}, bf16[256,512]{1,0:T(8,128)(2,1)S(1)}, u32[]{:S(2)}, u32[]{:S(2)}) collective-permute-start(bf16[256,512]{1,0:T(8,128)(2,1)} %get-tuple-element.33), channel_id=1, source_target_pairs={{0,3},{1,2},{2,1},{3,0},{4,7},{5,6},{6,5},{7,4},{8,11},{9,10},{10,... | collective-permute-start | bytes 786440 | tf_op jit(solution)/shard_map/ppermute | solution.py:711
  37.9 20.6 %copy-start.6 = (bf16[256,512]{1,0:T(8,128)(2,1)}, bf16[256,512]{1,0:T(8,128)(2,1)S(1)}, u32[]{:S(2)}) copy-start(bf16[256,512]{1,0:T(8,128)(2,1)S(1)} %collective-permute-done.2.refs_2_) | copy-start | bytes 786436
  48.7 9.8 %copy-start.7 = (bf16[256,512]{1,0:T(8,128)(2,1)}, bf16[256,512]{1,0:T(8,128)(2,1)S(1)}, u32[]{:S(2)}) copy-start(bf16[256,512]{1,0:T(8,128)(2,1)S(1)} %collective-permute-done.3.refs_3_) | copy-start | bytes 786436
  58.5 0.7 copy-start.8
  63.4 8.7 %copy-start.5 = (f32[1,3,4,4,4]{4,3,2,1,0:T(4,128)S(1)}, f32[1,3,4,4,4]{4,3,2,1,0:T(4,128)}, u32[]{:S(2)}) copy-start(f32[1,3,4,4,4]{4,3,2,1,0:T(4,128)} %param.9) | copy-start | bytes 2308
  66.1 30.0 %all-to-all-start.1 = ((bf16[16,64,512]{2,1,0:T(8,128)(2,1)}), bf16[16,64,512]{2,1,0:T(8,128)(2,1)}, u32[]{:S(2)}, u32[]{:S(2)}) async-start(bf16[16,64,512]{2,1,0:T(8,128)(2,1)} %bitcast.20), calls=%async_computation.1 | async-start | bytes 2097152 | tf_op jit(solution)/shard_map/all_to_all | solution.py:704
  70.9 13.5 %collective-permute-start.5 = (bf16[1,4,512,128]{3,2,1,0:T(8,128)(2,1)}, bf16[1,4,512,128]{3,2,1,0:T(8,128)(2,1)}, u32[]{:S(2)}, u32[]{:S(2)}) collective-permute-start(bf16[1,4,512,128]{3,2,1,0:T(8,128)(2,1)} %get-tuple-element.37), channel_id=1, source_target_pairs={{0,16},{16,0},{1,17},{17,1},{2,18},{18,2},{3,19},{19,3},{4,20},{20... | collective-permute-start | bytes 1572872 | tf_op jit(solution)/shard_map/ppermute | solution.py:673
  79.7 16.4 %collective-permute-start.6 = (bf16[512,512]{1,0:T(8,128)(2,1)}, bf16[512,512]{1,0:T(8,128)(2,1)S(1)}, u32[]{:S(2)}, u32[]{:S(2)}) collective-permute-start(bf16[512,512]{1,0:T(8,128)(2,1)} %get-tuple-element.38), channel_id=1, source_target_pairs={{0,16},{16,0},{1,17},{17,1},{2,18},{18,2},{3,19},{19,3},{4,20},{20... | collective-permute-start | bytes 1572872 | tf_op jit(solution)/shard_map/ppermute | solution.py:673
  96.0 0.8 copy-start.2
  104.5 7.7 %copy-start.1 = (bf16[3,128,512]{2,1,0:T(8,128)(2,1)S(1)}, bf16[3,128,512]{2,1,0:T(8,128)(2,1)}, u32[]{:S(2)}) copy-start(bf16[3,128,512]{2,1,0:T(8,128)(2,1)} %get-tuple-element.42.refs_2_.d_hbm) | copy-start | bytes 1179652
  104.5 42.7 %all-to-all-start.3 = ((bf16[16,24,2048]{2,1,0:T(8,128)(2,1)}), bf16[16,24,2048]{2,1,0:T(8,128)(2,1)}, u32[]{:S(2)}, u32[]{:S(2)}) async-start(bf16[16,24,2048]{2,1,0:T(8,128)(2,1)} %bitcast.19), calls=%async_computation.3 | async-start | bytes 3145728 | tf_op jit(solution)/shard_map/all_to_all | solution.py:704
  110.9 23.1 %collective-permute-start.7 = (bf16[512,512]{1,0:T(8,128)(2,1)}, bf16[512,512]{1,0:T(8,128)(2,1)S(1)}, u32[]{:S(2)}, u32[]{:S(2)}) collective-permute-start(bf16[512,512]{1,0:T(8,128)(2,1)} %get-tuple-element.43), channel_id=1, source_target_pairs={{0,16},{16,0},{1,17},{17,1},{2,18},{18,2},{3,19},{19,3},{4,20},{20... | collective-permute-start | bytes 1572872 | tf_op jit(solution)/shard_map/ppermute | solution.py:673
  112.2 21.8 %collective-permute-start.8 = (bf16[3,128,512]{2,1,0:T(8,128)(2,1)S(1)}, bf16[3,128,512]{2,1,0:T(8,128)(2,1)}, u32[]{:S(2)}, u32[]{:S(2)}) collective-permute-start(bf16[3,128,512]{2,1,0:T(8,128)(2,1)S(1)} %copy-done.1), channel_id=1, source_target_pairs={{0,16},{16,0},{1,17},{17,1},{2,18},{18,2},{3,19},{19,3},{4,20},{20... | collective-permute-start | bytes 1179656 | tf_op jit(solution)/shard_map/ppermute | solution.py:673
  114.3 6.3 %copy-start.4 = (f32[128,128]{1,0:T(8,128)S(1)}, f32[128,128]{1,0:T(8,128)}, u32[]{:S(2)}) copy-start(f32[128,128]{1,0:T(8,128)} %get-tuple-element.47) | copy-start | bytes 196612
  119.3 14.1 %collective-permute-start.9 = (f32[1,3,4,4,4]{4,3,2,1,0:T(4,128)S(1)}, f32[1,3,4,4,4]{4,3,2,1,0:T(4,128)S(1)}, u32[]{:S(2)}, u32[]{:S(2)}) collective-permute-start(f32[1,3,4,4,4]{4,3,2,1,0:T(4,128)S(1)} %reshape.51), channel_id=1, source_target_pairs={{0,16},{16,0},{1,17},{17,1},{2,18},{18,2},{3,19},{19,3},{4,20},{20... | collective-permute-start | bytes 2312 | tf_op jit(solution)/shard_map/ppermute | solution.py:673
  134.0 0.8 copy-start.3

commit v13 on v12

--- a/solution.py
+++ b/solution.py
@@ -70,8 +70,8 @@
 
 def front_body(cap, pieces, own_rows, block_len, half, cross, me_ref, chosen_ref, *refs):
     if cross:
-        source_ref, told_ref, slot_ref, cross_ref, held_ref, sems = refs
-        width = cross_ref.shape[1]
+        source_ref, told_ref, slot_ref, cross_ref, rest_ref, held_ref, sems = refs
+        width = held_ref.shape[1]
         plane = lax.shift_right_logical(me_ref[0] & (half - 1), half.bit_length() - 2)
         at = pl.ds(pl.multiple_of((1 - plane) * width, width), width)
         load = begin(source_ref.at[:, at], held_ref, sems.at[0])
@@ -98,14 +98,16 @@
     told_ref[...] = jnp.where((twice & 1) == 1, jnp.concatenate(blocks, axis=1), asked)
     if cross:
         load.wait()
-        begin(held_ref, cross_ref, sems.at[1]).wait()
-
-
-def plane_columns(me, source, crossed, half):
+        first = begin(held_ref.at[:, : width // 2], cross_ref, sems.at[1])
+        begin(held_ref.at[:, width // 2 :], rest_ref, sems.at[2]).wait()
+        first.wait()
+
+
+def plane_columns(me, source, crossed, rest, half):
     own_rows, width = source.shape
     part, count = width // half, half // 2
 
-    def body(me_ref, source_ref, crossed_ref, *refs):
+    def body(me_ref, source_ref, crossed_ref, rest_ref, *refs):
         outs, (held_ref, in_sem, out_sem) = refs[:count], refs[count:]
         low = me_ref[0] & (half - 1)
         plane = lax.shift_right_logical(low, half.bit_length() - 2)
@@ -113,11 +115,12 @@
         at = pl.ds(pl.multiple_of(plane * wide, wide), wide)
         loads = [
             begin(source_ref.at[:, at], held_ref.at[0], in_sem.at[0]),
-            begin(crossed_ref, held_ref.at[1], in_sem.at[1]),
+            begin(crossed_ref, held_ref.at[1, :, : wide // 2], in_sem.at[1]),
+            begin(rest_ref, held_ref.at[1, :, wide // 2 :], in_sem.at[2]),
         ]
         copies = []
-        for n, load in enumerate(loads):
-            load.wait()
+        for n in range(2):
+            wait_all(loads[n : 1 + 2 * n])
             for k in range(count):
                 share = (low & (count - 1)) ^ k
                 at = held_ref.at[n, :, pl.ds(pl.multiple_of(share * part, part), part)]
@@ -128,12 +131,12 @@
     return call(
         body,
         [(shaped((2 * own_rows, part), BF16), HBM)] * count,
-        [(me, SMEM), (source, HBM), (crossed, HBM)],
+        [(me, SMEM), (source, HBM), (crossed, HBM), (rest, HBM)],
         "plane_columns",
         0,
         [
             scratch_like((2, own_rows, count * part), BF16),
-            pltpu.SemaphoreType.DMA((2,)),
+            pltpu.SemaphoreType.DMA((3,)),
             pltpu.SemaphoreType.DMA((2, count)),
         ],
     )
@@ -686,17 +689,19 @@
         factor_parts = [lax.all_gather(factors, "seq", axis=3, tiled=True)[0]]
         sides = 1
     sides_in = [(x, HBM) for x in factor_parts]
-    cross = [(shaped((own_rows, width // 2), BF16), HBM)] if direct else []
+    cross = [(shaped((own_rows, width // 4), BF16), HBM)] * 2 if direct else []
     told, slot, *crossed = call(
         functools.partial(front_body, cap, pieces, own_rows, block_len, half, direct),
         [(shaped((2 * peers, rows), jnp.int32), VMEM), (shaped((1, rows), jnp.int32), VMEM)] + cross,
         [(me, SMEM), (selection[0], VMEM)] + ([(cotangent, HBM)] if direct else []),
         "wanted_rows",
         1 << 20,
-        [scratch_like((own_rows, width // 2), BF16), dma((2,))] if direct else [],
+        [scratch_like((own_rows, width // 2), BF16), dma((3,))] if direct else [],
     )
     if direct:
-        crossed = [lax.ppermute(crossed[0], "exp", [(n, n ^ (half // 2)) for n in range(peers)])]
+        crossed = [
+            lax.ppermute(x, "exp", [(n, n ^ (half // 2)) for n in range(peers)]) for x in crossed
+        ]
     chosen = lax.all_to_all(told, "exp", split_axis=0, concat_axis=0, tiled=True)
 
     def to_peers(array):
@@ -704,9 +709,9 @@
         array = lax.all_to_all(array, "exp", split_axis=0, concat_axis=0, tiled=True)
         return array.reshape(-1, array.shape[2])
 
-    got_rows = to_peers(pick_slots(cap, pieces, chosen, tokens, crossed, "pick_tokens"))
+    got_rows = to_peers(pick_slots(cap, pieces, chosen, tokens, crossed[:1], "pick_tokens"))
     if direct:
-        shares = plane_columns(me, cotangent, crossed[0], half)
+        shares = plane_columns(me, cotangent, *crossed, half)
         shares = [shares[0]] + [
             lax.ppermute(shares[k], "exp", [(n, n ^ k) for n in range(peers)])
             for k in range(1, half // 2)

time: 151 us -> 167 us (1.11)
  waiting for transfers between devices: 56.1 us -> 73.5 us
  blocking collectives: 15.3 us -> 11.2 us
  starting transfers between devices: 26.2 us -> 27.9 us
    ppermute x1 -> x2, waiting for transfers between devices: 0.01 us -> 28.3 us  [shards(): lax.ppermute(x, 'exp', [(n, n ^ half // 2) for n in range(peers)])]
    ppermute x3, waiting for transfers between devices: 20.6 us -> 12.2 us  [shards(): lax.ppermute(shares[k], 'exp', [(n, n ^ k) for n in range(peers)])]
    all_to_all x1, blocking collectives: 15.3 us -> 11.2 us  [shards(): lax.all_to_all(told, 'exp', split_axis=0, concat_axis=0, tiled=True)]
    all_to_all x3, waiting for transfers between devices: 19.9 us -> 17.2 us  [to_peers(): lax.all_to_all(array, 'exp', split_axis=0, concat_axis=0, tiled=True)]
    unnamed x18 -> x22, local copies, waits for them, and re-layouts: 3.1 us -> 3.73 us
  transfers between devices with their start and end apart: 13 -> 14, of which waited for: 7 -> 7; matrix products, arithmetic and copies ran while one was open for 3% -> 2% of each run, Pallas kernels for 19% -> 17%
where the time goes in v13:
time: 167 us; the launch traced here: 166 us
  waiting for transfers between devices  73.5 us (44%)
  Pallas kernels  45.1 us (27%)
  starting transfers between devices  27.9 us (17%)
  blocking collectives  11.2 us (7%)
  local copies, waits for them, and re-layouts  4.55 us (3%)
  other arithmetic  2.99 us (2%)
    pallas_call x11, Pallas kernels, call(): pl.pallas_call(body, out_shape=[x for x, _ in outs], in_specs=[place for...  45.1 us
    ppermute x2, waiting for transfers between devices, shards(): lax.ppermute(x, 'exp', [(n, n ^ half // 2) for n in range(peers)])  28.3 us
    all_to_all x3, starting transfers between devices, to_peers(): lax.all_to_all(array, 'exp', split_axis=0, concat_axis=0, tiled=True)  19.1 us
    all_to_all x3, waiting for transfers between devices, to_peers(): lax.all_to_all(array, 'exp', split_axis=0, concat_axis=0, tiled=True)  17.2 us
    ppermute x6, waiting for transfers between devices, across(): return lax.ppermute(array, 'seq', pair)  15.7 us
    ppermute x3, waiting for transfers between devices, shards(): lax.ppermute(shares[k], 'exp', [(n, n ^ k) for n in range(peers)])  12.2 us
    all_to_all x1, blocking collectives, shards(): lax.all_to_all(told, 'exp', split_axis=0, concat_axis=0, tiled=True)  11.2 us
    ppermute x6, starting transfers between devices, across(): return lax.ppermute(array, 'seq', pair)  5.63 us
  transfers between devices with their start and end apart: 14, of which 7 were waited for; matrix products, arithmetic and copies ran while one was open for 2% of the time, Pallas kernels for 17%

profile of v13, /device:TPU:13, one launch (start us, length us, event | category | flops | bytes accessed | tf_op | source)
XLA Modules:
  0.0 166.0 jit_solution(17085260618799746456)
XLA Ops:
  0.6 3.2 %wanted_rows.1 = (s32[32,128]{1,0:T(8,128)}, s32[1,128]{1,0:T(1,128)}, bf16[128,1024]{1,0:T(8,128)(2,1)}, bf16[128,1024]{1,0:T(8,128)(2,1)}) custom-call(s32[1]{0:T(128)} %bitcast.me_ref, s32[2,64]{1,0:T(2,128)} %bitcast.25, bf16[128,4096]{1,0:T(8,128)(2,1)} %source_ref.2), custom_call_target="tpu_custom_call" | custom-call | flops 1048576 | bytes 1590276 | tf_op jit(solution)/shard_map/wanted_rows/pallas_call | solution.py:40
  4.1 11.2 %all_to_all.26 = s32[16,2,128]{2,1,0:T(2,128)} all-to-all(s32[16,2,128]{2,1,0:T(2,128)} %bitcast.24), channel_id=1, replica_groups=mesh['seq'=2,'exp'=16] {'exp'}, dimensions={0} | all-to-all | bytes 32768 | tf_op jit(solution)/shard_map/all_to_all | solution.py:705
  15.9 2.9 %pick_tokens.1 = bf16[384,2048]{1,0:T(8,128)(2,1)} custom-call(s32[32,128]{1,0:T(8,128)} %bitcast.21, bf16[128,4096]{1,0:T(8,128)(2,1)} %source_ref.3, bf16[128,1024]{1,0:T(8,128)(2,1)} %copy-done.1), custom_call_target="tpu_custom_call" | custom-call | flops 402653184 | bytes 2899968 | tf_op jit(solution)/shard_map/pick_tokens/pallas_call | solution.py:40
  18.8 6.7 %all-to-all-start.2 = ((bf16[16,24,2048]{2,1,0:T(8,128)(2,1)}), bf16[16,24,2048]{2,1,0:T(8,128)(2,1)}, u32[]{:S(2)}, u32[]{:S(2)}) async-start(bf16[16,24,2048]{2,1,0:T(8,128)(2,1)} %bitcast.14), calls=%async_computation.2 | async-start | bytes 3145728 | tf_op jit(solution)/shard_map/all_to_all | solution.py:709
  25.5 2.4 %cut_factors.1 = (bf16[2,4,512,128]{3,2,1,0:T(8,128)(2,1)}, bf16[1,4,512,128]{3,2,1,0:T(8,128)(2,1)}) custom-call(bf16[3,4,512,128]{3,2,1,0:T(8,128)(2,1)} %bitcast.15), custom_call_target="tpu_custom_call" | custom-call | bytes 3145728 | tf_op jit(solution)/shard_map/cut_factors/pallas_call | solution.py:40
  28.0 1.3 collective-permute-start
  29.5 28.3 %collective-permute-done.2.rest_ref = bf16[128,1024]{1,0:T(8,128)(2,1)S(1)} collective-permute-done((bf16[128,1024]{1,0:T(8,128)(2,1)S(1)}, bf16[128,1024]{1,0:T(8,128)(2,1)S(1)}, u32[]{:S(2)}, u32[]{:S(2)}) %collective-permute-start.2) | collective-permute-done | bytes 262176 | tf_op jit(solution)/shard_map/ppermute | solution.py:703
  58.6 2.1 %plane_columns.1 = (bf16[256,512]{1,0:T(8,128)(2,1)}, bf16[256,512]{1,0:T(8,128)(2,1)}, bf16[256,512]{1,0:T(8,128)(2,1)}, bf16[256,512]{1,0:T(8,128)(2,1)}) custom-call(s32[1]{0:T(128)} %bitcast.me_ref, bf16[128,4096]{1,0:T(8,128)(2,1)} %source_ref.2, bf16[128,1024]{1,0:T(8,128)(2,1)} %copy-done.1, bf16[128,1024]{1,0:T(8,128)(2,1)} %copy-done.4), custom_call_target="tpu_custom_call" | custom-call | bytes 2621444 | tf_op jit(solution)/shard_map/plane_columns/pallas_call | solution.py:40
  61.7 1.6 collective-permute-start.5
  63.3 6.4 %collective-permute-done.4.refs_3_ = bf16[256,512]{1,0:T(8,128)(2,1)S(1)} collective-permute-done((bf16[256,512]{1,0:T(8,128)(2,1)}, bf16[256,512]{1,0:T(8,128)(2,1)S(1)}, u32[]{:S(2)}, u32[]{:S(2)}) %collective-permute-start.4) | collective-permute-done | bytes 262176 | tf_op jit(solution)/shard_map/ppermute | solution.py:716
  69.7 5.8 %collective-permute-done.5.refs_4_ = bf16[256,512]{1,0:T(8,128)(2,1)S(1)} collective-permute-done((bf16[256,512]{1,0:T(8,128)(2,1)}, bf16[256,512]{1,0:T(8,128)(2,1)S(1)}, u32[]{:S(2)}, u32[]{:S(2)}) %collective-permute-start.5) | collective-permute-done | bytes 262176 | tf_op jit(solution)/shard_map/ppermute | solution.py:716
  76.2 4.2 %pick_cotangent.1 = bf16[1024,512]{1,0:T(8,128)(2,1)} custom-call(s32[1]{0:T(128)} %bitcast.me_ref, s32[32,128]{1,0:T(8,128)} %bitcast.22, bf16[2,4,512,128]{3,2,1,0:T(8,128)(2,1)} %collective-permute-done.refs_0_.refs_1_, bf16[256,512]{1,0:T(8,128)(2,1)} %get-tuple-element.32.refs_1_, bf16[256,512]{1,0:T(8,128)(2,1)} %copy-done.8, ...), custom_call_target="tpu_custom_call" | custom-call | flops 1073741824 | bytes 3162116 | tf_op jit(solution)/shard_map/pick_cotangent/pallas_call | solution.py:40
  80.5 6.0 %all-to-all-start.1 = ((bf16[16,64,512]{2,1,0:T(8,128)(2,1)}), bf16[16,64,512]{2,1,0:T(8,128)(2,1)}, u32[]{:S(2)}, u32[]{:S(2)}) async-start(bf16[16,64,512]{2,1,0:T(8,128)(2,1)} %bitcast.20), calls=%async_computation.1 | async-start | bytes 2097152 | tf_op jit(solution)/shard_map/all_to_all | solution.py:709
  88.4 6.9 %forward.1 = (bf16[512,512]{1,0:T(8,128)(2,1)}, bf16[512,512]{1,0:T(8,128)(2,1)}, f32[512,512]{1,0:T(8,128)}, f32[512,512]{1,0:T(8,128)}, f32[128,512]{1,0:T(8,1...) custom-call(s32[1]{0:T(128)} %bitcast.4.order_ref, f32[192]{0:T(256)} %reshape.44.mix_ref, ...), custom_call_target="tpu_custom_call" | custom-call | flops 1073741824 | bytes 8127748 | tf_op jit(solution)/shard_map/forward/pallas_call | solution.py:40
  95.6 4.4 %collective-permute-done.6.refs_2_ = bf16[1,4,512,128]{3,2,1,0:T(8,128)(2,1)} collective-permute-done((bf16[1,4,512,128]{3,2,1,0:T(8,128)(2,1)}, bf16[1,4,512,128]{3,2,1,0:T(8,128)(2,1)}, u32[]{:S(2)}, u32[]{:S(2)}) %collective-permute-start.6) | collective-permute-done | bytes 524320 | tf_op jit(solution)/shard_map/ppermute | solution.py:676
  100.0 11.7 %all-to-all-done.1 = bf16[16,64,512]{2,1,0:T(8,128)(2,1)} async-done(((bf16[16,64,512]{2,1,0:T(8,128)(2,1)}), bf16[16,64,512]{2,1,0:T(8,128)(2,1)}, u32[]{:S(2)}, u32[]{:S(2)}) %all-to-all-start.1) | async-done | bytes 1048608 | tf_op jit(solution)/shard_map/all_to_all | solution.py:709
  112.5 7.6 %backward.1 = (bf16[384,2048]{1,0:T(8,128)(2,1)}, bf16[512,512]{1,0:T(8,128)(2,1)}, bf16[512,512]{1,0:T(8,128)(2,1)}, f32[512,512]{1,0:T(8,128)}, bf16[3,128,512]{2,1,0:T(8,128)(2,1)}, /*index=5*/f32[128,128]{1,0:T(8,128)}) custom-call(s32[1]{0:T(128)} %bitcast.4.order_ref, f32[192]{0:T(256)} %reshape.44.mix_ref, ...), custom_call_target="tpu_custom_call" | custom-call | flops 1610612736 | bytes 9635588 | tf_op jit(solution)/shard_map/backward/pallas_call | solution.py:40
  120.1 6.4 %all-to-all-start.3 = ((bf16[16,24,2048]{2,1,0:T(8,128)(2,1)}), bf16[16,24,2048]{2,1,0:T(8,128)(2,1)}, u32[]{:S(2)}, u32[]{:S(2)}) async-start(bf16[16,24,2048]{2,1,0:T(8,128)(2,1)} %bitcast.19), calls=%async_computation.3 | async-start | bytes 3145728 | tf_op jit(solution)/shard_map/all_to_all | solution.py:709
  128.1 1.9 %place_rows.1.placed_hbm = bf16[256,384]{1,0:T(8,128)(2,1)} custom-call(s32[1]{0:T(128)} %bitcast.me_ref, s32[32,128]{1,0:T(8,128)} %bitcast.23), custom_call_target="tpu_custom_call" | custom-call | flops 1048576 | bytes 212996 | tf_op jit(solution)/shard_map/place_rows/pallas_call | solution.py:40
  129.9 3.9 %mix_partials.1 = f32[192,128]{1,0:T(8,128)} custom-call(f32[512,512]{1,0:T(8,128)} %get-tuple-element.46.yg_hbm, f32[512,512]{1,0:T(8,128)} %get-tuple-element.47.yu_hbm, f32[512,512]{1,0:T(8,128)} %get-tuple-element.48.yd_hbm, bf16[3,128,512]{2,1,0:T(8,128)(2,1)} %get-tuple-element.44.refs_2_.d_hbm), custom_call_target="tpu_custom_call" | custom-call | flops 6291456 | bytes 3637248 | tf_op jit(solution)/shard_map/mix_partials/pallas_call | solution.py:40
  137.7 11.3 %collective-permute-done.10 = f32[1,3,4,4,4]{4,3,2,1,0:T(4,128)S(1)} collective-permute-done((f32[1,3,4,4,4]{4,3,2,1,0:T(4,128)S(1)}, f32[1,3,4,4,4]{4,3,2,1,0:T(4,128)S(1)}, u32[]{:S(2)}, u32[]{:S(2)}) %collective-permute-start.10) | collective-permute-done | bytes 800 | tf_op jit(solution)/shard_map/ppermute | solution.py:676
  150.4 6.9 %factor_grad.1 = f32[3,4,512,128]{3,2,1,0:T(8,128)} custom-call(f32[192]{0:T(256)} %reshape.44.mix_ref, bf16[512,512]{1,0:T(8,128)(2,1)} %get-tuple-element.42.refs_0_, bf16[512,512]{1,0:T(8,128)(2,1)} %get-tuple-element.43.refs_1_, bf16[3,128,512]{2,1,0:T(8,128)(2,1)} %get-tuple-element.44.refs_2_.d_hbm, bf16[512,512]{1,0:T(8,128)(2,1)} %copy-done.2, ...), custom_call_target="tpu_custom_call" | custom-call | flops 1610612736 | bytes 6030080 | tf_op jit(solution)/shard_map/factor_grad/pallas_call | solution.py:40
  157.3 5.5 %all-to-all-done.3 = bf16[16,24,2048]{2,1,0:T(8,128)(2,1)} async-done(((bf16[16,24,2048]{2,1,0:T(8,128)(2,1)}), bf16[16,24,2048]{2,1,0:T(8,128)(2,1)}, u32[]{:S(2)}, u32[]{:S(2)}) %all-to-all-start.3) | async-done | bytes 1572896 | tf_op jit(solution)/shard_map/all_to_all | solution.py:709
  162.8 3.1 %sum_rows.1 = bf16[128,4096]{1,0:T(8,128)(2,1)} custom-call(bf16[256,384]{1,0:T(8,128)(2,1)} %place_rows.1.placed_hbm, bf16[384,2048]{1,0:T(8,128)(2,1)} %bitcast.12.returned_ref), custom_call_target="tpu_custom_call" | custom-call | flops 402653184 | bytes 2818048 | tf_op jit(solution)/shard_map/sum_rows/pallas_call | solution.py:40
  (45 shorter events, 13.4 us)
Async XLA Ops:
  3.8 11.4 %collective-permute-start.1 = (bf16[128,1024]{1,0:T(8,128)(2,1)}, bf16[128,1024]{1,0:T(8,128)(2,1)S(1)}, u32[]{:S(2)}, u32[]{:S(2)}) collective-permute-start(bf16[128,1024]{1,0:T(8,128)(2,1)} %get-tuple-element.30), channel_id=1, source_target_pairs={{0,4},{1,5},{2,6},{3,7},{4,0},{5,1},{6,2},{7,3},{8,12},{9,13},{10,... | collective-permute-start | bytes 786440 | tf_op jit(solution)/shard_map/ppermute | solution.py:703
  15.2 0.7 copy-start.1
  18.8 61.6 %all-to-all-start.2 = ((bf16[16,24,2048]{2,1,0:T(8,128)(2,1)}), bf16[16,24,2048]{2,1,0:T(8,128)(2,1)}, u32[]{:S(2)}, u32[]{:S(2)}) async-start(bf16[16,24,2048]{2,1,0:T(8,128)(2,1)} %bitcast.14), calls=%async_computation.2 | async-start | bytes 3145728 | tf_op jit(solution)/shard_map/all_to_all | solution.py:709
  25.5 3.7 %copy-start.7 = (bf16[128,1024]{1,0:T(8,128)(2,1)S(1)}, bf16[128,1024]{1,0:T(8,128)(2,1)}, u32[]{:S(2)}) copy-start(bf16[128,1024]{1,0:T(8,128)(2,1)} %get-tuple-element.31) | copy-start | bytes 786436
  28.0 47.5 %collective-permute-start = (bf16[2,4,512,128]{3,2,1,0:T(8,128)(2,1)}, bf16[2,4,512,128]{3,2,1,0:T(8,128)(2,1)}, u32[]{:S(2)}, u32[]{:S(2)}) collective-permute-start(bf16[2,4,512,128]{3,2,1,0:T(8,128)(2,1)} %get-tuple-element.29), channel_id=1, source_target_pairs={{0,16},{16,0},{1,17},{17,1},{2,18},{18,2},{3,19},{19,3},{4,20},{20... | collective-permute-start | bytes 3145736 | tf_op jit(solution)/shard_map/ppermute | solution.py:676
  29.2 28.6 %collective-permute-start.2 = (bf16[128,1024]{1,0:T(8,128)(2,1)S(1)}, bf16[128,1024]{1,0:T(8,128)(2,1)S(1)}, u32[]{:S(2)}, u32[]{:S(2)}) collective-permute-start(bf16[128,1024]{1,0:T(8,128)(2,1)S(1)} %copy-done.7), channel_id=1, source_target_pairs={{0,4},{1,5},{2,6},{3,7},{4,0},{5,1},{6,2},{7,3},{8,12},{9,13},{10,... | collective-permute-start | bytes 786440 | tf_op jit(solution)/shard_map/ppermute | solution.py:703
  57.8 0.7 copy-start.4
  60.7 2.7 %collective-permute-start.3 = (bf16[256,512]{1,0:T(8,128)(2,1)}, bf16[256,512]{1,0:T(8,128)(2,1)S(1)}, u32[]{:S(2)}, u32[]{:S(2)}) collective-permute-start(bf16[256,512]{1,0:T(8,128)(2,1)} %get-tuple-element.33), channel_id=1, source_target_pairs={{0,1},{1,0},{2,3},{3,2},{4,5},{5,4},{6,7},{7,6},{8,9},{9,8},{10,11... | collective-permute-start | bytes 786440 | tf_op jit(solution)/shard_map/ppermute | solution.py:716
  61.6 8.1 %collective-permute-start.4 = (bf16[256,512]{1,0:T(8,128)(2,1)}, bf16[256,512]{1,0:T(8,128)(2,1)S(1)}, u32[]{:S(2)}, u32[]{:S(2)}) collective-permute-start(bf16[256,512]{1,0:T(8,128)(2,1)} %get-tuple-element.34), channel_id=1, source_target_pairs={{0,2},{1,3},{2,0},{3,1},{4,6},{5,7},{6,4},{7,5},{8,10},{9,11},{10,... | collective-permute-start | bytes 786440 | tf_op jit(solution)/shard_map/ppermute | solution.py:716
  61.7 13.8 %collective-permute-start.5 = (bf16[256,512]{1,0:T(8,128)(2,1)}, bf16[256,512]{1,0:T(8,128)(2,1)S(1)}, u32[]{:S(2)}, u32[]{:S(2)}) collective-permute-start(bf16[256,512]{1,0:T(8,128)(2,1)} %get-tuple-element.35), channel_id=1, source_target_pairs={{0,3},{1,2},{2,1},{3,0},{4,7},{5,6},{6,5},{7,4},{8,11},{9,10},{10,... | collective-permute-start | bytes 786440 | tf_op jit(solution)/shard_map/ppermute | solution.py:716
  63.3 12.2 %copy-start.8 = (bf16[256,512]{1,0:T(8,128)(2,1)}, bf16[256,512]{1,0:T(8,128)(2,1)S(1)}, u32[]{:S(2)}) copy-start(bf16[256,512]{1,0:T(8,128)(2,1)S(1)} %collective-permute-done.3.refs_2_) | copy-start | bytes 786436
  69.7 5.8 %copy-start.9 = (bf16[256,512]{1,0:T(8,128)(2,1)}, bf16[256,512]{1,0:T(8,128)(2,1)S(1)}, u32[]{:S(2)}) copy-start(bf16[256,512]{1,0:T(8,128)(2,1)S(1)} %collective-permute-done.4.refs_3_) | copy-start | bytes 786436
  80.4 7.3 %copy-start.6 = (f32[1,3,4,4,4]{4,3,2,1,0:T(4,128)S(1)}, f32[1,3,4,4,4]{4,3,2,1,0:T(4,128)}, u32[]{:S(2)}) copy-start(f32[1,3,4,4,4]{4,3,2,1,0:T(4,128)} %param.9) | copy-start | bytes 2308
  80.5 31.2 %all-to-all-start.1 = ((bf16[16,64,512]{2,1,0:T(8,128)(2,1)}), bf16[16,64,512]{2,1,0:T(8,128)(2,1)}, u32[]{:S(2)}, u32[]{:S(2)}) async-start(bf16[16,64,512]{2,1,0:T(8,128)(2,1)} %bitcast.20), calls=%async_computation.1 | async-start | bytes 2097152 | tf_op jit(solution)/shard_map/all_to_all | solution.py:709
  86.5 13.5 %collective-permute-start.6 = (bf16[1,4,512,128]{3,2,1,0:T(8,128)(2,1)}, bf16[1,4,512,128]{3,2,1,0:T(8,128)(2,1)}, u32[]{:S(2)}, u32[]{:S(2)}) collective-permute-start(bf16[1,4,512,128]{3,2,1,0:T(8,128)(2,1)} %get-tuple-element.39), channel_id=1, source_target_pairs={{0,16},{16,0},{1,17},{17,1},{2,18},{18,2},{3,19},{19,3},{4,20},{20... | collective-permute-start | bytes 1572872 | tf_op jit(solution)/shard_map/ppermute | solution.py:676
  95.3 16.4 %collective-permute-start.7 = (bf16[512,512]{1,0:T(8,128)(2,1)}, bf16[512,512]{1,0:T(8,128)(2,1)S(1)}, u32[]{:S(2)}, u32[]{:S(2)}) collective-permute-start(bf16[512,512]{1,0:T(8,128)(2,1)} %get-tuple-element.40), channel_id=1, source_target_pairs={{0,16},{16,0},{1,17},{17,1},{2,18},{18,2},{3,19},{19,3},{4,20},{20... | collective-permute-start | bytes 1572872 | tf_op jit(solution)/shard_map/ppermute | solution.py:676
  111.7 0.8 copy-start.2
  120.1 7.7 %copy-start = (bf16[3,128,512]{2,1,0:T(8,128)(2,1)S(1)}, bf16[3,128,512]{2,1,0:T(8,128)(2,1)}, u32[]{:S(2)}) copy-start(bf16[3,128,512]{2,1,0:T(8,128)(2,1)} %get-tuple-element.44.refs_2_.d_hbm) | copy-start | bytes 1179652
  120.1 42.7 %all-to-all-start.3 = ((bf16[16,24,2048]{2,1,0:T(8,128)(2,1)}), bf16[16,24,2048]{2,1,0:T(8,128)(2,1)}, u32[]{:S(2)}, u32[]{:S(2)}) async-start(bf16[16,24,2048]{2,1,0:T(8,128)(2,1)} %bitcast.19), calls=%async_computation.3 | async-start | bytes 3145728 | tf_op jit(solution)/shard_map/all_to_all | solution.py:709
  126.5 23.1 %collective-permute-start.8 = (bf16[512,512]{1,0:T(8,128)(2,1)}, bf16[512,512]{1,0:T(8,128)(2,1)S(1)}, u32[]{:S(2)}, u32[]{:S(2)}) collective-permute-start(bf16[512,512]{1,0:T(8,128)(2,1)} %get-tuple-element.45), channel_id=1, source_target_pairs={{0,16},{16,0},{1,17},{17,1},{2,18},{18,2},{3,19},{19,3},{4,20},{20... | collective-permute-start | bytes 1572872 | tf_op jit(solution)/shard_map/ppermute | solution.py:676
  127.8 21.8 %collective-permute-start.9 = (bf16[3,128,512]{2,1,0:T(8,128)(2,1)S(1)}, bf16[3,128,512]{2,1,0:T(8,128)(2,1)}, u32[]{:S(2)}, u32[]{:S(2)}) collective-permute-start(bf16[3,128,512]{2,1,0:T(8,128)(2,1)S(1)} %copy-done), channel_id=1, source_target_pairs={{0,16},{16,0},{1,17},{17,1},{2,18},{18,2},{3,19},{19,3},{4,20},{20... | collective-permute-start | bytes 1179656 | tf_op jit(solution)/shard_map/ppermute | solution.py:676
  129.9 6.3 %copy-start.5 = (f32[128,128]{1,0:T(8,128)S(1)}, f32[128,128]{1,0:T(8,128)}, u32[]{:S(2)}) copy-start(f32[128,128]{1,0:T(8,128)} %get-tuple-element.49) | copy-start | bytes 196612
  134.9 14.0 %collective-permute-start.10 = (f32[1,3,4,4,4]{4,3,2,1,0:T(4,128)S(1)}, f32[1,3,4,4,4]{4,3,2,1,0:T(4,128)S(1)}, u32[]{:S(2)}, u32[]{:S(2)}) collective-permute-start(f32[1,3,4,4,4]{4,3,2,1,0:T(4,128)S(1)} %reshape.51), channel_id=1, source_target_pairs={{0,16},{16,0},{1,17},{17,1},{2,18},{18,2},{3,19},{19,3},{4,20},{20... | collective-permute-start | bytes 2312 | tf_op jit(solution)/shard_map/ppermute | solution.py:676
  149.6 0.8 copy-start.3
  (1 other events, 0.7 us)

commit v14 on v12

--- a/solution.py
+++ b/solution.py
@@ -68,7 +68,7 @@
     return [slice(c * chunk, (c + 1) * chunk) for c in range(part // chunk)]
 
 
-def front_body(cap, pieces, own_rows, block_len, half, cross, me_ref, chosen_ref, *refs):
+def front_body(cap, pieces, back_pieces, own_rows, block_len, half, cross, me_ref, chosen_ref, *refs):
     if cross:
         source_ref, told_ref, slot_ref, cross_ref, held_ref, sems = refs
         width = cross_ref.shape[1]
@@ -87,7 +87,8 @@
     count = jnp.sum(mine, axis=1, keepdims=True)
     earlier = jnp.sum(jnp.where(peer < owner, count, 0.0), axis=0, keepdims=True).astype(jnp.int32)
     rank = iota((1, rows), 1) - earlier
-    slot_ref[...] = owner * (cap * pieces) + rank
+    slot_ref[0:1, :] = owner * (cap * pieces) + rank
+    slot_ref[1:2, :] = (owner ^ me_ref[0] if cross else owner) * (cap * back_pieces) + rank
     lane = iota((rows, rows), 0)
     hit = jnp.zeros((rows, rows), F32)
     for j in range(pieces):
@@ -298,7 +299,7 @@
     )[0]
 
 
-def place_rows(cap, pieces, own_rows, me, half, chosen):
+def place_rows(cap, pieces, own_rows, me, half, relative, chosen):
     peers, total = chosen.shape[0] // 2, chosen.shape[1]
     picks = total * half // peers
     group = cap * pieces
@@ -321,7 +322,8 @@
                 hit = jnp.where((place == rank + j * cap) & (rank >= 0) & (rank < cap), mine, 0)
                 row = jnp.sum(hit, axis=1, keepdims=True)
                 column = column + jnp.where(row > 0, row + j * own_rows, 0)
-            pick_ref[e * group : (e + 1) * group] = (
+            place_at = (me_ref[0] ^ e if relative else e) * group
+            pick_ref[pl.ds(pl.multiple_of(place_at, 8), group), :] = (
                 column == iota((group, pieces * own_rows), 1) + 1
             ).astype(F32)
         out_ref[...] = jnp.transpose(pick_ref[...]).astype(BF16)
@@ -337,20 +339,19 @@
 
 
 def sum_rows(pieces, placed, returned):
-    slots, part = returned.shape
+    count, (size, part) = len(returned), returned[0].shape
     own_rows = placed.shape[0] // pieces
     columns = chunks_of(part)
 
-    def body(placed_hbm, returned_ref, out_ref, place_ref, got_ref, sum_ref, in_sem, out_sem):
-        first = begin(placed_hbm, place_ref, in_sem.at[len(columns)])
-        loads = [
-            begin(returned_ref.at[:, at], got_ref.at[:, at], in_sem.at[n])
-            for n, at in enumerate(columns)
-        ]
-        first.wait()
+    def body(placed_hbm, *refs):
+        slabs, (out_ref, place_ref, got_ref, sum_ref, in_sem, out_sem) = refs[:count], refs[count:]
+        loads = [begin(placed_hbm, place_ref, in_sem.at[count])]
+        for n, slab in enumerate(slabs):
+            target = got_ref.at[n * size : (n + 1) * size]
+            loads.append(begin(slab, target, in_sem.at[n]))
+        wait_all(loads)
         stores = []
         for n, at in enumerate(columns):
-            loads[n].wait()
             summed = dot(place_ref[...], got_ref[:, at]).astype(BF16)
             for j in range(pieces):
                 wide = slice(j * part + at.start, j * part + at.stop)
@@ -363,14 +364,14 @@
     return call(
         body,
         [(shaped((own_rows, part * pieces), BF16), HBM)],
-        [(placed, HBM), (returned, HBM)],
+        [(placed, HBM)] + [(x, HBM) for x in returned],
         "sum_rows",
-        2 * slots * pieces * own_rows * part,
+        2 * count * size * pieces * own_rows * part,
         [
             scratch_like(placed.shape, BF16),
-            scratch_like((slots, part), BF16),
+            scratch_like((count * size, part), BF16),
             scratch_like((own_rows, part * pieces), BF16),
-            pltpu.SemaphoreType.DMA((len(columns) + 1,)),
+            pltpu.SemaphoreType.DMA((count + 1,)),
             pltpu.SemaphoreType.DMA((len(columns), pieces)),
         ],
     )[0]
@@ -498,7 +499,7 @@
     sides_in = [
         load_factor(order_ref, parts, m, side_ref.at[m], side_sem.at[m]) for m in range(2)
     ]
-    place = place_matrix(cap, pieces, got_ref.shape[0], slot_ref[...])
+    place = place_matrix(cap, pieces, got_ref.shape[0], slot_ref[0:1, :])
     stack_rows(pieces, place, loads, got_ref, x_ref)
     stores = store_parts(order_ref, x_ref, x_outs, out_sem)
     wait_all(sides_in[0])
@@ -525,16 +526,16 @@
 
 
 def backward_body(
-    cap, pieces, sides, after, order_ref, mix_ref, slot_hbm, score_hbm, got_hbm, act_hbm, slope_hbm, hid_hbm,
+    cap, pieces, slabs, sides, after, order_ref, mix_ref, slot_hbm, score_hbm, got_hbm, act_hbm, slope_hbm, hid_hbm,
     *refs,
 ):
     held = 3 if sides > 1 else 1
     parts, refs = refs[:held], refs[held + after :]
-    back_hbm, x_outs, refs = refs[0], refs[1 : 1 + sides], refs[1 + sides :]
+    backs, x_outs, refs = refs[:slabs], refs[slabs : slabs + sides], refs[slabs + sides :]
     y_hbm, d_hbm, inner_hbm = refs[:3]
     (
         down_ref, side_ref, x_ref, y_ref, d_ref, act_ref, slope_ref, hid_ref, z_ref, grad_ref,
-        back_ref, inner_ref, slot_ref, score_ref, got_sem, side_sem, in_sem, out_sem,
+        back_ref, inner_ref, slot_ref, score_ref, got_sem, side_sem, in_sem, out_sem, back_sem,
     ) = refs[3:]
     loads = load_rows(got_hbm, x_ref, got_sem)
     down_in = load_factor(order_ref, parts, 2, down_ref, side_sem.at[2])
@@ -560,7 +561,7 @@
     score = jnp.sum(jnp.where(same, score.astype(F32), 0.0), axis=1, keepdims=True)
     cols = hidden // NPHM
     gates = jnp.broadcast_to(jax.nn.sigmoid(score / 64.0), (rows, cols))
-    place = place_matrix(cap, pieces, back_ref.shape[0], slot_ref[...])
+    place = place_matrix(cap, pieces, back_ref.shape[0], slot_ref[1:2, :])
     strips = rows // STRIP
     tall = NPHM * STRIP
     wait_all(loads)
@@ -602,12 +603,15 @@
             wide = slice(start, start + at.stop - at.start)
             blocks += [grad_ref[rows_of(n, a), wide] for n in range(strips)]
         back_ref[:, at] = dot(place, jnp.concatenate(blocks, axis=0)).astype(BF16)
-        stores.append(begin(back_ref.at[:, at], back_hbm.at[:, at], out_sem.at[5 + k]))
+        for n, out in enumerate(backs):
+            size = out.shape[0]
+            source = back_ref.at[n * size : (n + 1) * size, at]
+            stores.append(begin(source, out.at[:, at], back_sem.at[n, k]))
     wait_all(stores)
 
 
-def factor_body(count_groups, mix_ref, *refs):
-    rows_in, refs = refs[: 3 * count_groups], refs[3 * count_groups :]
+def factor_body(count_groups, after, mix_ref, *refs):
+    rows_in, refs = refs[: 3 * count_groups], refs[3 * count_groups + after :]
     out_hbm, x_ref, g_ref, d_ref, z_ref, sum_ref, in_sem, out_sem = refs
     loads = []
     for n in range(count_groups):
@@ -629,7 +633,8 @@
     wait_all(stores)
 
 
-def mix_grad_body(yg_hbm, yu_hbm, yd_hbm, d_hbm, out_ref, y_ref, d_ref, sems):
+def mix_grad_body(yg_hbm, yu_hbm, yd_hbm, d_hbm, *refs):
+    out_ref, y_ref, d_ref, sems = refs[-4:]
     loads = [begin(d_hbm, d_ref, sems.at[3])]
     for m, source in enumerate((yg_hbm, yu_hbm, yd_hbm)):
         loads.append(begin(source, y_ref.at[m], sems.at[m]))
@@ -661,6 +666,10 @@
     slots = peers * cap * pieces
     part = width // pieces
     steps = len(chunks_of(part))
+    back_pieces = 2 * pieces if selection.shape[1] * 8 == peers else pieces
+    back_part = width // back_pieces
+    back_slots = peers * cap * back_pieces
+    back_steps = len(chunks_of(back_part))
     block_len = peers * SELECTED
     rows = selection.shape[1] * selection.shape[2]
     stacked = count * rows
@@ -688,8 +697,8 @@
     sides_in = [(x, HBM) for x in factor_parts]
     cross = [(shaped((own_rows, width // 2), BF16), HBM)] if direct else []
     told, slot, *crossed = call(
-        functools.partial(front_body, cap, pieces, own_rows, block_len, half, direct),
-        [(shaped((2 * peers, rows), jnp.int32), VMEM), (shaped((1, rows), jnp.int32), VMEM)] + cross,
+        functools.partial(front_body, cap, pieces, back_pieces, own_rows, block_len, half, direct),
+        [(shaped((2 * peers, rows), jnp.int32), VMEM), (shaped((2, rows), jnp.int32), VMEM)] + cross,
         [(me, SMEM), (selection[0], VMEM)] + ([(cotangent, HBM)] if direct else []),
         "wanted_rows",
         1 << 20,
@@ -719,7 +728,7 @@
         shares = [array.reshape(half * own_rows, -1)]
     picked = pick_rows(me, half, own_rows, chosen, shares, cuts[:1], "pick_cotangent")
     got_grads = to_peers(picked)
-    placed = place_rows(cap, pieces, own_rows, me, half, chosen)
+    placed = place_rows(cap, back_pieces, own_rows, me, half, direct, chosen)
     gate = jax.nn.sigmoid(scores[0].reshape(-1).astype(F32) / 64.0)
 
     product = 2 * stacked * depth * hidden
@@ -745,9 +754,10 @@
     x_parts, (y_gate, y_up, act, slope, hid) = outs[:sides], outs[sides:]
     x_rows = [x_parts[0]] + [across(x) for x in x_parts[1:]]
     after = x_rows[1:]
+    slabs = peers if direct else 1
     outs = call(
-        functools.partial(backward_body, cap, pieces, sides, len(after)),
-        [(shaped((slots, part), BF16), HBM)]
+        functools.partial(backward_body, cap, back_pieces, slabs, sides, len(after)),
+        [(shaped((back_slots // slabs, back_part), BF16), HBM)] * slabs
         + split
         + [mixed, (shaped((weights, rows, hidden), BF16), HBM), (shaped((rows, cols), F32), HBM)],
         [(group, SMEM), (mixing, SMEM), (slot, HBM), (scores[0], HBM), (got_grads, HBM)]
@@ -759,22 +769,35 @@
         [scratch_like((depth, hidden), BF16), scratch_like((depth, 2 * hidden), BF16)]
         + [stack_scratch, mixed_scratch, scratch_like((weights, rows, hidden), BF16)]
         + [flat_scratch] * 3
-        + [scratch_like((stacked, 2 * hidden), BF16), stack_scratch, back_scratch]
+        + [scratch_like((stacked, 2 * hidden), BF16), stack_scratch]
+        + [scratch_like((back_slots, back_part), BF16)]
         + [scratch_like((rows, cols), F32), scratch_like(slot.shape, jnp.int32)]
         + [scratch_like(scores.shape[1:], jnp.int32)]
-        + [dma((pieces_in,)), dma((weights, sides, count)), dma((5,)), dma((5 + steps,))],
+        + [dma((pieces_in,)), dma((weights, sides, count)), dma((5,)), dma((5,))]
+        + [dma((slabs, back_steps))],
     )
-    back, g_parts, (y_down, d_own, inner) = outs[0], outs[1 : 1 + sides], outs[1 + sides :]
-    returned = to_peers(back)
+    backs, outs = outs[:slabs], outs[slabs:]
+    g_parts, (y_down, d_own, inner) = outs[:sides], outs[sides:]
+    if direct:
+        order = [k for n in range(half) for k in (half + n, n)][:1]
+        order += [k for n in range(1, half) for k in (n, half + n)]
+        moved = {0: backs[0]}
+        for k in order:
+            moved[k] = lax.ppermute(backs[k], "exp", [(n, n ^ k) for n in range(peers)])
+        returned = [moved[k] for k in range(peers)]
+        soon, late = [moved[k] for k in order[:3]], [moved[k] for k in order[:11]]
+    else:
+        returned, soon, late = [to_peers(backs[0])], [], []
 
     d_rows = [d_own] + [across(d_own) for _ in x_parts[1:]]
     g_rows = [g_parts[0]] + [across(x) for x in g_parts[1:]]
     depth_here = depth // sides
     factor_grad = call(
-        functools.partial(factor_body, sides),
+        functools.partial(factor_body, sides, len(late)),
         [(shaped((weights, count, depth_here, cols), F32), HBM)],
         [(mixing, SMEM)]
-        + [(x, HBM) for n in range(sides) for x in (x_rows[n], g_rows[n], d_rows[n])],
+        + [(x, HBM) for n in range(sides) for x in (x_rows[n], g_rows[n], d_rows[n])]
+        + [(x, HBM) for x in late],
         "factor_grad",
         3 * product,
         [scratch_like((sides, stacked, depth_here), BF16)] * 2
@@ -789,7 +812,7 @@
     mix_rows = call(
         mix_grad_body,
         [(shaped((mixing.size, cols), F32), VMEM)],
-        [(x, HBM) for x in (y_gate, y_up, y_down, d_own)],
+        [(x, HBM) for x in [y_gate, y_up, y_down, d_own] + soon],
         "mix_partials",
         weights * 64 * 2 * rows * cols,
         [
@@ -807,7 +830,7 @@
         ).astype(F32)
         mix_grad = lax.psum(mix_part, "seq")
     gate_grad = (jnp.sum(inner, axis=1) * gate * (1.0 - gate)).reshape(selection.shape)
-    token_grad = sum_rows(pieces, placed, returned)
+    token_grad = sum_rows(back_pieces, placed, returned)
     return token_grad, factor_grad[None], mix_grad, gate_grad
 
 

time: 151 us -> 169 us (1.12)
  starting transfers between devices: 26.2 us -> 39 us
  Pallas kernels: 45 us -> 47.3 us
    ppermute x0 -> x15, starting transfers between devices: none -> 19.4 us  [shards(): moved[k] = lax.ppermute(backs[k], 'exp', [(n, n ^ k) for n in range(peers)])]
    ppermute x0 -> x15, waiting for transfers between devices: none -> 18.5 us  [shards(): moved[k] = lax.ppermute(backs[k], 'exp', [(n, n ^ k) for n in range(peers)])]
    ppermute x6, waiting for transfers between devices: 15.7 us -> 4.31 us  [across(): return lax.ppermute(array, 'seq', pair)]
    all_to_all x3 -> x2, starting transfers between devices: 17.9 us -> 11.4 us  [to_peers(): lax.all_to_all(array, 'exp', split_axis=0, concat_axis=0, tiled=True)]
    all_to_all x3 -> x2, waiting for transfers between devices: 19.9 us -> 14.3 us  [to_peers(): lax.all_to_all(array, 'exp', split_axis=0, concat_axis=0, tiled=True)]
    pallas_call x11, Pallas kernels: 45 us -> 47.3 us  [call(): pl.pallas_call(body, out_shape=[x for x, _ in outs], in_specs=[place for...]
  transfers between devices with their start and end apart: 13 -> 27, of which waited for: 7 -> 13; matrix products, arithmetic and copies ran while one was open for 3% -> 2% of each run, Pallas kernels for 19% -> 16%
where the time goes in v14:
time: 169 us; the launch traced here: 167 us
  waiting for transfers between devices  57.7 us (34%)
  Pallas kernels  47.3 us (28%)
  starting transfers between devices  39 us (23%)
  blocking collectives  15.2 us (9%)
  local copies, waits for them, and re-layouts  4.03 us (2%)
  other arithmetic  3.14 us (2%)
    pallas_call x11, Pallas kernels, call(): pl.pallas_call(body, out_shape=[x for x, _ in outs], in_specs=[place for...  47.3 us
    ppermute x3, waiting for transfers between devices, shards(): lax.ppermute(shares[k], 'exp', [(n, n ^ k) for n in range(peers)])  20.6 us
    ppermute x15, starting transfers between devices, shards(): moved[k] = lax.ppermute(backs[k], 'exp', [(n, n ^ k) for n in range(peers)])  19.4 us
    ppermute x15, waiting for transfers between devices, shards(): moved[k] = lax.ppermute(backs[k], 'exp', [(n, n ^ k) for n in range(peers)])  18.5 us
    all_to_all x1, blocking collectives, shards(): lax.all_to_all(told, 'exp', split_axis=0, concat_axis=0, tiled=True)  15.2 us
    all_to_all x2, waiting for transfers between devices, to_peers(): lax.all_to_all(array, 'exp', split_axis=0, concat_axis=0, tiled=True)  14.3 us
    all_to_all x2, starting transfers between devices, to_peers(): lax.all_to_all(array, 'exp', split_axis=0, concat_axis=0, tiled=True)  11.4 us
    ppermute x6, starting transfers between devices, across(): return lax.ppermute(array, 'seq', pair)  5.57 us
  transfers between devices with their start and end apart: 27, of which 13 were waited for; matrix products, arithmetic and copies ran while one was open for 2% of the time, Pallas kernels for 16%

profile of v14, /device:TPU:13, one launch (start us, length us, event | category | flops | bytes accessed | tf_op | source)
XLA Modules:
  0.0 167.3 jit_solution(2368550037151522860)
XLA Ops:
  0.6 3.1 %wanted_rows.1 = (s32[32,128]{1,0:T(8,128)}, s32[2,128]{1,0:T(2,128)}, bf16[128,2048]{1,0:T(8,128)(2,1)}) custom-call(s32[1]{0:T(128)} %bitcast.me_ref, s32[2,64]{1,0:T(2,128)} %bitcast.22, bf16[128,4096]{1,0:T(8,128)(2,1)} %source_ref.2), custom_call_target="tpu_custom_call" | custom-call | flops 1048576 | bytes 1590788 | tf_op jit(solution)/shard_map/wanted_rows/pallas_call | solution.py:40
  4.0 15.2 %all_to_all.21 = s32[16,2,128]{2,1,0:T(2,128)} all-to-all(s32[16,2,128]{2,1,0:T(2,128)} %bitcast.21), channel_id=1, replica_groups=mesh['seq'=2,'exp'=16] {'exp'}, dimensions={0} | all-to-all | bytes 32768 | tf_op jit(solution)/shard_map/all_to_all | solution.py:709
  20.1 2.9 %pick_tokens.1 = bf16[384,2048]{1,0:T(8,128)(2,1)} custom-call(s32[32,128]{1,0:T(8,128)} %bitcast.18, bf16[128,4096]{1,0:T(8,128)(2,1)} %source_ref.3, bf16[128,2048]{1,0:T(8,128)(2,1)} %copy-done), custom_call_target="tpu_custom_call" | custom-call | flops 402653184 | bytes 3162112 | tf_op jit(solution)/shard_map/pick_tokens/pallas_call | solution.py:40
  23.0 6.6 %all-to-all-start.2 = ((bf16[16,24,2048]{2,1,0:T(8,128)(2,1)}), bf16[16,24,2048]{2,1,0:T(8,128)(2,1)}, u32[]{:S(2)}, u32[]{:S(2)}) async-start(bf16[16,24,2048]{2,1,0:T(8,128)(2,1)} %bitcast.12), calls=%async_computation.2 | async-start | bytes 3145728 | tf_op jit(solution)/shard_map/all_to_all | solution.py:713
  29.6 2.4 %cut_factors.1 = (bf16[2,4,512,128]{3,2,1,0:T(8,128)(2,1)}, bf16[1,4,512,128]{3,2,1,0:T(8,128)(2,1)}) custom-call(bf16[3,4,512,128]{3,2,1,0:T(8,128)(2,1)} %bitcast.13), custom_call_target="tpu_custom_call" | custom-call | bytes 3145728 | tf_op jit(solution)/shard_map/cut_factors/pallas_call | solution.py:40
  33.2 2.1 %plane_columns.1 = (bf16[256,512]{1,0:T(8,128)(2,1)}, bf16[256,512]{1,0:T(8,128)(2,1)}, bf16[256,512]{1,0:T(8,128)(2,1)}, bf16[256,512]{1,0:T(8,128)(2,1)}) custom-call(s32[1]{0:T(128)} %bitcast.me_ref, bf16[128,4096]{1,0:T(8,128)(2,1)} %source_ref.2, bf16[128,2048]{1,0:T(8,128)(2,1)} %copy-done), custom_call_target="tpu_custom_call" | custom-call | bytes 2621444 | tf_op jit(solution)/shard_map/plane_columns/pallas_call | solution.py:40
  37.8 10.8 %collective-permute-done.3.refs_3_ = bf16[256,512]{1,0:T(8,128)(2,1)S(1)} collective-permute-done((bf16[256,512]{1,0:T(8,128)(2,1)}, bf16[256,512]{1,0:T(8,128)(2,1)S(1)}, u32[]{:S(2)}, u32[]{:S(2)}) %collective-permute-start.3) | collective-permute-done | bytes 262176 | tf_op jit(solution)/shard_map/ppermute | solution.py:720
  48.6 9.8 %collective-permute-done.4.refs_4_ = bf16[256,512]{1,0:T(8,128)(2,1)S(1)} collective-permute-done((bf16[256,512]{1,0:T(8,128)(2,1)}, bf16[256,512]{1,0:T(8,128)(2,1)S(1)}, u32[]{:S(2)}, u32[]{:S(2)}) %collective-permute-start.4) | collective-permute-done | bytes 262176 | tf_op jit(solution)/shard_map/ppermute | solution.py:720
  59.1 4.2 %pick_cotangent.1 = bf16[1024,512]{1,0:T(8,128)(2,1)} custom-call(s32[1]{0:T(128)} %bitcast.me_ref, s32[32,128]{1,0:T(8,128)} %bitcast.19, bf16[2,4,512,128]{3,2,1,0:T(8,128)(2,1)} %collective-permute-done.refs_0_.refs_1_, bf16[256,512]{1,0:T(8,128)(2,1)} %get-tuple-element.45.refs_1_, bf16[256,512]{1,0:T(8,128)(2,1)} %copy-done.9, ...), custom_call_target="tpu_custom_call" | custom-call | flops 1073741824 | bytes 3162116 | tf_op jit(solution)/shard_map/pick_cotangent/pallas_call | solution.py:40
  63.3 2.6 %all-to-all-done.2 = bf16[16,24,2048]{2,1,0:T(8,128)(2,1)} async-done(((bf16[16,24,2048]{2,1,0:T(8,128)(2,1)}), bf16[16,24,2048]{2,1,0:T(8,128)(2,1)}, u32[]{:S(2)}, u32[]{:S(2)}) %all-to-all-start.2) | async-done | bytes 1572896 | tf_op jit(solution)/shard_map/all_to_all | solution.py:713
  65.9 4.8 %all-to-all-start.1 = ((bf16[16,64,512]{2,1,0:T(8,128)(2,1)}), bf16[16,64,512]{2,1,0:T(8,128)(2,1)}, u32[]{:S(2)}, u32[]{:S(2)}) async-start(bf16[16,64,512]{2,1,0:T(8,128)(2,1)} %bitcast.17), calls=%async_computation.1 | async-start | bytes 2097152 | tf_op jit(solution)/shard_map/all_to_all | solution.py:713
  72.7 6.9 %forward.1 = (bf16[512,512]{1,0:T(8,128)(2,1)}, bf16[512,512]{1,0:T(8,128)(2,1)}, f32[512,512]{1,0:T(8,128)}, f32[512,512]{1,0:T(8,128)}, f32[128,512]{1,0:T(8,1...) custom-call(s32[1]{0:T(128)} %bitcast.4.order_ref, f32[192]{0:T(256)} %reshape.38.mix_ref, ...), custom_call_target="tpu_custom_call" | custom-call | flops 1073741824 | bytes 8128260 | tf_op jit(solution)/shard_map/forward/pallas_call | solution.py:40
  80.0 4.3 %collective-permute-done.5.refs_2_ = bf16[1,4,512,128]{3,2,1,0:T(8,128)(2,1)} collective-permute-done((bf16[1,4,512,128]{3,2,1,0:T(8,128)(2,1)}, bf16[1,4,512,128]{3,2,1,0:T(8,128)(2,1)}, u32[]{:S(2)}, u32[]{:S(2)}) %collective-permute-start.5) | collective-permute-done | bytes 524320 | tf_op jit(solution)/shard_map/ppermute | solution.py:682
  84.3 11.6 %all-to-all-done.1 = bf16[16,64,512]{2,1,0:T(8,128)(2,1)} async-done(((bf16[16,64,512]{2,1,0:T(8,128)(2,1)}), bf16[16,64,512]{2,1,0:T(8,128)(2,1)}, u32[]{:S(2)}, u32[]{:S(2)}) %all-to-all-start.1) | async-done | bytes 1048608 | tf_op jit(solution)/shard_map/all_to_all | solution.py:713
  96.7 8.4 %backward.1 = (bf16[48,1024]{1,0:T(8,128)(2,1)}, bf16[48,1024]{1,0:T(8,128)(2,1)}, bf16[48,1024]{1,0:T(8,128)(2,1)}, bf16[48,1024]{1,0:T(8,128)(2,1)}, bf16[48,1...) custom-call(s32[1]{0:T(128)} %bitcast.4.order_ref, ...), custom_call_target="tpu_custom_call" | custom-call | flops 1610612736 | bytes 9636100 | tf_op jit(solution)/shard_map/backward/pallas_call | solution.py:40
  110.6 2.0 %collective-permute-done.14.refs_8_.refs_6_.refs_0_ = bf16[48,1024]{1,0:T(8,128)(2,1)S(1)} collective-permute-done((bf16[48,1024]{1,0:T(8,128)(2,1)}, bf16[48,1024]{1,0:T(8,128)(2,1)S(1)}, u32[]{:S(2)}, u32[]{:S(2)}) %collective-permute-start.14) | collective-permute-done | bytes 98336 | tf_op jit(solution)/shard_map/ppermute | solution.py:786
  115.4 3.4 %collective-permute-start.16 = (bf16[48,1024]{1,0:T(8,128)(2,1)}, bf16[48,1024]{1,0:T(8,128)(2,1)}, u32[]{:S(2)}, u32[]{:S(2)}) collective-permute-start(bf16[48,1024]{1,0:T(8,128)(2,1)} %get-tuple-element.64), channel_id=1, source_target_pairs={{0,10},{1,11},{2,8},{3,9},{4,14},{5,15},{6,12},{7,13},{8,2},{9,3},... | collective-permute-start | bytes 294920 | tf_op jit(solution)/shard_map/ppermute | solution.py:786
  122.8 7.5 %collective-permute-done.17.refs_11_.refs_12_ = bf16[48,1024]{1,0:T(8,128)(2,1)} collective-permute-done((bf16[48,1024]{1,0:T(8,128)(2,1)}, bf16[48,1024]{1,0:T(8,128)(2,1)}, u32[]{:S(2)}, u32[]{:S(2)}) %collective-permute-start.17) | collective-permute-done | bytes 98336 | tf_op jit(solution)/shard_map/ppermute | solution.py:786
  130.3 2.5 %collective-permute-start.9 = (bf16[48,1024]{1,0:T(8,128)(2,1)}, bf16[48,1024]{1,0:T(8,128)(2,1)}, u32[]{:S(2)}, u32[]{:S(2)}) collective-permute-start(bf16[48,1024]{1,0:T(8,128)(2,1)} %get-tuple-element.57), channel_id=1, source_target_pairs={{0,3},{1,2},{2,1},{3,0},{4,7},{5,6},{6,5},{7,4},{8,11},{9,10},{10,... | collective-permute-start | bytes 294920 | tf_op jit(solution)/shard_map/ppermute | solution.py:786
  137.7 3.0 %place_rows.1.placed_hbm = bf16[512,768]{1,0:T(8,128)(2,1)} custom-call(s32[1]{0:T(128)} %bitcast.me_ref, s32[32,128]{1,0:T(8,128)} %bitcast.20), custom_call_target="tpu_custom_call" | custom-call | flops 1048576 | bytes 802820 | tf_op jit(solution)/shard_map/place_rows/pallas_call | solution.py:40
  145.6 3.9 %mix_partials.1 = f32[192,128]{1,0:T(8,128)} custom-call(f32[512,512]{1,0:T(8,128)} %get-tuple-element.74.yg_hbm, f32[512,512]{1,0:T(8,128)} %get-tuple-element.75.yu_hbm, f32[512,512]{1,0:T(8,128)} %get-tuple-element.76.yd_hbm, bf16[3,128,512]{2,1,0:T(8,128)(2,1)} %get-tuple-element.72.refs_2_.d_hbm, bf16[48,1024]{1,0:T(8,128)(2,1)} %copy-done.1, ...), custom_call_target="tpu_custom_call" | custom-call | flops 6291456 | bytes 3932160 | tf_op jit(solution)/shard_map/mix_partials/pallas_call | solution.py:40
  150.9 2.9 %collective-permute-done.20.refs_14_ = bf16[48,1024]{1,0:T(8,128)(2,1)} collective-permute-done((bf16[48,1024]{1,0:T(8,128)(2,1)}, bf16[48,1024]{1,0:T(8,128)(2,1)}, u32[]{:S(2)}, u32[]{:S(2)}) %collective-permute-start.20) | collective-permute-done | bytes 98336 | tf_op jit(solution)/shard_map/ppermute | solution.py:786
  155.4 3.5 %sum_rows.1 = bf16[128,4096]{1,0:T(8,128)(2,1)} custom-call(bf16[512,768]{1,0:T(8,128)(2,1)} %place_rows.1.placed_hbm, bf16[48,1024]{1,0:T(8,128)(2,1)} %get-tuple-element.54.refs_0_, bf16[48,1024]{1,0:T(8,128)(2,1)} %copy-done.3, bf16[48,1024]{1,0:T(8,128)(2,1)} %collective-permute-done.8.refs_2_.refs_9_, ...), custom_call_target="tpu_custom_call" | custom-call | flops 805306368 | bytes 3407872 | tf_op jit(solution)/shard_map/sum_rows/pallas_call | solution.py:40
  160.3 6.9 %factor_grad.1 = f32[3,4,512,128]{3,2,1,0:T(8,128)} custom-call(f32[192]{0:T(256)} %reshape.38.mix_ref, bf16[512,512]{1,0:T(8,128)(2,1)} %get-tuple-element.70.refs_0_, bf16[512,512]{1,0:T(8,128)(2,1)} %get-tuple-element.71.refs_1_, bf16[3,128,512]{2,1,0:T(8,128)(2,1)} %get-tuple-element.72.refs_2_.d_hbm, bf16[512,512]{1,0:T(8,128)(2,1)} %copy-done.4, ...), custom_call_target="tpu_custom_call" | custom-call | flops 1610612736 | bytes 7111424 | tf_op jit(solution)/shard_map/factor_grad/pallas_call | solution.py:40
  (73 shorter events, 35.1 us)
Async XLA Ops:
  3.8 15.5 %collective-permute-start.1 = (bf16[128,2048]{1,0:T(8,128)(2,1)}, bf16[128,2048]{1,0:T(8,128)(2,1)S(1)}, u32[]{:S(2)}, u32[]{:S(2)}) collective-permute-start(bf16[128,2048]{1,0:T(8,128)(2,1)} %get-tuple-element.44), channel_id=1, source_target_pairs={{0,4},{1,5},{2,6},{3,7},{4,0},{5,1},{6,2},{7,3},{8,12},{9,13},{10,... | collective-permute-start | bytes 1572872 | tf_op jit(solution)/shard_map/ppermute | solution.py:708
  23.0 43.0 %all-to-all-start.2 = ((bf16[16,24,2048]{2,1,0:T(8,128)(2,1)}), bf16[16,24,2048]{2,1,0:T(8,128)(2,1)}, u32[]{:S(2)}, u32[]{:S(2)}) async-start(bf16[16,24,2048]{2,1,0:T(8,128)(2,1)} %bitcast.12), calls=%async_computation.2 | async-start | bytes 3145728 | tf_op jit(solution)/shard_map/all_to_all | solution.py:713
  31.9 26.4 %collective-permute-start = (bf16[2,4,512,128]{3,2,1,0:T(8,128)(2,1)}, bf16[2,4,512,128]{3,2,1,0:T(8,128)(2,1)}, u32[]{:S(2)}, u32[]{:S(2)}) collective-permute-start(bf16[2,4,512,128]{3,2,1,0:T(8,128)(2,1)} %get-tuple-element.43), channel_id=1, source_target_pairs={{0,16},{16,0},{1,17},{17,1},{2,18},{18,2},{3,19},{19,3},{4,20},{20... | collective-permute-start | bytes 3145736 | tf_op jit(solution)/shard_map/ppermute | solution.py:682
  36.1 12.5 %collective-permute-start.3 = (bf16[256,512]{1,0:T(8,128)(2,1)}, bf16[256,512]{1,0:T(8,128)(2,1)S(1)}, u32[]{:S(2)}, u32[]{:S(2)}) collective-permute-start(bf16[256,512]{1,0:T(8,128)(2,1)} %get-tuple-element.47), channel_id=1, source_target_pairs={{0,2},{1,3},{2,0},{3,1},{4,6},{5,7},{6,4},{7,5},{8,10},{9,11},{10,... | collective-permute-start | bytes 786440 | tf_op jit(solution)/shard_map/ppermute | solution.py:720
  36.3 22.0 %collective-permute-start.4 = (bf16[256,512]{1,0:T(8,128)(2,1)}, bf16[256,512]{1,0:T(8,128)(2,1)S(1)}, u32[]{:S(2)}, u32[]{:S(2)}) collective-permute-start(bf16[256,512]{1,0:T(8,128)(2,1)} %get-tuple-element.48), channel_id=1, source_target_pairs={{0,3},{1,2},{2,1},{3,0},{4,7},{5,6},{6,5},{7,4},{8,11},{9,10},{10,... | collective-permute-start | bytes 786440 | tf_op jit(solution)/shard_map/ppermute | solution.py:720
  65.9 30.0 %all-to-all-start.1 = ((bf16[16,64,512]{2,1,0:T(8,128)(2,1)}), bf16[16,64,512]{2,1,0:T(8,128)(2,1)}, u32[]{:S(2)}, u32[]{:S(2)}) async-start(bf16[16,64,512]{2,1,0:T(8,128)(2,1)} %bitcast.17), calls=%async_computation.1 | async-start | bytes 2097152 | tf_op jit(solution)/shard_map/all_to_all | solution.py:713
  70.7 13.5 %collective-permute-start.5 = (bf16[1,4,512,128]{3,2,1,0:T(8,128)(2,1)}, bf16[1,4,512,128]{3,2,1,0:T(8,128)(2,1)}, u32[]{:S(2)}, u32[]{:S(2)}) collective-permute-start(bf16[1,4,512,128]{3,2,1,0:T(8,128)(2,1)} %get-tuple-element.52), channel_id=1, source_target_pairs={{0,16},{16,0},{1,17},{17,1},{2,18},{18,2},{3,19},{19,3},{4,20},{20... | collective-permute-start | bytes 1572872 | tf_op jit(solution)/shard_map/ppermute | solution.py:682
  79.6 16.3 %collective-permute-start.6 = (bf16[512,512]{1,0:T(8,128)(2,1)}, bf16[512,512]{1,0:T(8,128)(2,1)S(1)}, u32[]{:S(2)}, u32[]{:S(2)}) collective-permute-start(bf16[512,512]{1,0:T(8,128)(2,1)} %get-tuple-element.53), channel_id=1, source_target_pairs={{0,16},{16,0},{1,17},{17,1},{2,18},{18,2},{3,19},{19,3},{4,20},{20... | collective-permute-start | bytes 1572872 | tf_op jit(solution)/shard_map/ppermute | solution.py:682
  106.8 8.6 %collective-permute-start.15 = (bf16[48,1024]{1,0:T(8,128)(2,1)}, bf16[48,1024]{1,0:T(8,128)(2,1)S(1)}, u32[]{:S(2)}, u32[]{:S(2)}) collective-permute-start(bf16[48,1024]{1,0:T(8,128)(2,1)} %get-tuple-element.63), channel_id=1, source_target_pairs={{0,9},{1,8},{2,11},{3,10},{4,13},{5,12},{6,15},{7,14},{8,1},{9,0},... | collective-permute-start | bytes 294920 | tf_op jit(solution)/shard_map/ppermute | solution.py:786
  108.4 10.4 %collective-permute-start.7 = (bf16[48,1024]{1,0:T(8,128)(2,1)}, bf16[48,1024]{1,0:T(8,128)(2,1)S(1)}, u32[]{:S(2)}, u32[]{:S(2)}) collective-permute-start(bf16[48,1024]{1,0:T(8,128)(2,1)} %get-tuple-element.55), channel_id=1, source_target_pairs={{0,1},{1,0},{2,3},{3,2},{4,5},{5,4},{6,7},{7,6},{8,9},{9,8},{10,11... | collective-permute-start | bytes 294920 | tf_op jit(solution)/shard_map/ppermute | solution.py:786
  108.4 11.5 %collective-permute-start.10 = (bf16[48,1024]{1,0:T(8,128)(2,1)}, bf16[48,1024]{1,0:T(8,128)(2,1)S(1)}, u32[]{:S(2)}, u32[]{:S(2)}) collective-permute-start(bf16[48,1024]{1,0:T(8,128)(2,1)} %get-tuple-element.58), channel_id=1, source_target_pairs={{0,4},{1,5},{2,6},{3,7},{4,0},{5,1},{6,2},{7,3},{8,12},{9,13},{10,... | collective-permute-start | bytes 294920 | tf_op jit(solution)/shard_map/ppermute | solution.py:786
  108.7 11.3 %collective-permute-start.11 = (bf16[48,1024]{1,0:T(8,128)(2,1)}, bf16[48,1024]{1,0:T(8,128)(2,1)}, u32[]{:S(2)}, u32[]{:S(2)}) collective-permute-start(bf16[48,1024]{1,0:T(8,128)(2,1)} %get-tuple-element.59), channel_id=1, source_target_pairs={{0,5},{1,4},{2,7},{3,6},{4,1},{5,0},{6,3},{7,2},{8,13},{9,12},{10,... | collective-permute-start | bytes 294920 | tf_op jit(solution)/shard_map/ppermute | solution.py:786
  112.5 46.9 %collective-permute-start.22 = (bf16[512,512]{1,0:T(8,128)(2,1)}, bf16[512,512]{1,0:T(8,128)(2,1)S(1)}, u32[]{:S(2)}, u32[]{:S(2)}) collective-permute-start(bf16[512,512]{1,0:T(8,128)(2,1)} %get-tuple-element.73), channel_id=1, source_target_pairs={{0,16},{16,0},{1,17},{17,1},{2,18},{18,2},{3,19},{19,3},{4,20},{20... | collective-permute-start | bytes 1572872 | tf_op jit(solution)/shard_map/ppermute | solution.py:682
  118.8 11.5 %collective-permute-start.17 = (bf16[48,1024]{1,0:T(8,128)(2,1)}, bf16[48,1024]{1,0:T(8,128)(2,1)}, u32[]{:S(2)}, u32[]{:S(2)}) collective-permute-start(bf16[48,1024]{1,0:T(8,128)(2,1)} %get-tuple-element.65), channel_id=1, source_target_pairs={{0,11},{1,10},{2,9},{3,8},{4,15},{5,14},{6,13},{7,12},{8,3},{9,2},... | collective-permute-start | bytes 294920 | tf_op jit(solution)/shard_map/ppermute | solution.py:786
  119.9 14.1 %collective-permute-start.18 = (bf16[48,1024]{1,0:T(8,128)(2,1)}, bf16[48,1024]{1,0:T(8,128)(2,1)}, u32[]{:S(2)}, u32[]{:S(2)}) collective-permute-start(bf16[48,1024]{1,0:T(8,128)(2,1)} %get-tuple-element.66), channel_id=1, source_target_pairs={{0,12},{1,13},{2,14},{3,15},{4,8},{5,9},{6,10},{7,11},{8,4},{9,5},... | collective-permute-start | bytes 294920 | tf_op jit(solution)/shard_map/ppermute | solution.py:786
  120.0 16.5 %collective-permute-start.19 = (bf16[48,1024]{1,0:T(8,128)(2,1)}, bf16[48,1024]{1,0:T(8,128)(2,1)}, u32[]{:S(2)}, u32[]{:S(2)}) collective-permute-start(bf16[48,1024]{1,0:T(8,128)(2,1)} %get-tuple-element.67), channel_id=1, source_target_pairs={{0,13},{1,12},{2,15},{3,14},{4,9},{5,8},{6,11},{7,10},{8,5},{9,4},... | collective-permute-start | bytes 294920 | tf_op jit(solution)/shard_map/ppermute | solution.py:786
  121.9 19.8 %collective-permute-start.8 = (bf16[48,1024]{1,0:T(8,128)(2,1)}, bf16[48,1024]{1,0:T(8,128)(2,1)}, u32[]{:S(2)}, u32[]{:S(2)}) collective-permute-start(bf16[48,1024]{1,0:T(8,128)(2,1)} %get-tuple-element.56), channel_id=1, source_target_pairs={{0,2},{1,3},{2,0},{3,1},{4,6},{5,7},{6,4},{7,5},{8,10},{9,11},{10,... | collective-permute-start | bytes 294920 | tf_op jit(solution)/shard_map/ppermute | solution.py:786
  130.3 13.1 %collective-permute-start.9 = (bf16[48,1024]{1,0:T(8,128)(2,1)}, bf16[48,1024]{1,0:T(8,128)(2,1)}, u32[]{:S(2)}, u32[]{:S(2)}) collective-permute-start(bf16[48,1024]{1,0:T(8,128)(2,1)} %get-tuple-element.57), channel_id=1, source_target_pairs={{0,3},{1,2},{2,1},{3,0},{4,7},{5,6},{6,5},{7,4},{8,11},{9,10},{10,... | collective-permute-start | bytes 294920 | tf_op jit(solution)/shard_map/ppermute | solution.py:786
  134.0 10.2 %collective-permute-start.12 = (bf16[48,1024]{1,0:T(8,128)(2,1)}, bf16[48,1024]{1,0:T(8,128)(2,1)}, u32[]{:S(2)}, u32[]{:S(2)}) collective-permute-start(bf16[48,1024]{1,0:T(8,128)(2,1)} %get-tuple-element.60), channel_id=1, source_target_pairs={{0,6},{1,7},{2,4},{3,5},{4,2},{5,3},{6,0},{7,1},{8,14},{9,15},{10,... | collective-permute-start | bytes 294920 | tf_op jit(solution)/shard_map/ppermute | solution.py:786
  136.5 23.0 %collective-permute-start.23 = (bf16[3,128,512]{2,1,0:T(8,128)(2,1)}, bf16[3,128,512]{2,1,0:T(8,128)(2,1)}, u32[]{:S(2)}, u32[]{:S(2)}) collective-permute-start(bf16[3,128,512]{2,1,0:T(8,128)(2,1)} %get-tuple-element.72.refs_2_.d_hbm), channel_id=1, source_target_pairs={{0,16},{16,0},{1,17},{17,1},{2,18},{18,2},{3,19},{19,3},{4,20},{20... | collective-permute-start | bytes 1179656 | tf_op jit(solution)/shard_map/ppermute | solution.py:682
  141.7 8.9 %collective-permute-start.13 = (bf16[48,1024]{1,0:T(8,128)(2,1)}, bf16[48,1024]{1,0:T(8,128)(2,1)}, u32[]{:S(2)}, u32[]{:S(2)}) collective-permute-start(bf16[48,1024]{1,0:T(8,128)(2,1)} %get-tuple-element.61), channel_id=1, source_target_pairs={{0,7},{1,6},{2,5},{3,4},{4,3},{5,2},{6,1},{7,0},{8,15},{9,14},{10,... | collective-permute-start | bytes 294920 | tf_op jit(solution)/shard_map/ppermute | solution.py:786
  143.4 10.4 %collective-permute-start.20 = (bf16[48,1024]{1,0:T(8,128)(2,1)}, bf16[48,1024]{1,0:T(8,128)(2,1)}, u32[]{:S(2)}, u32[]{:S(2)}) collective-permute-start(bf16[48,1024]{1,0:T(8,128)(2,1)} %get-tuple-element.68), channel_id=1, source_target_pairs={{0,14},{1,15},{2,12},{3,13},{4,10},{5,11},{6,8},{7,9},{8,6},{9,7},... | collective-permute-start | bytes 294920 | tf_op jit(solution)/shard_map/ppermute | solution.py:786
  144.2 11.1 %collective-permute-start.21 = (bf16[48,1024]{1,0:T(8,128)(2,1)}, bf16[48,1024]{1,0:T(8,128)(2,1)}, u32[]{:S(2)}, u32[]{:S(2)}) collective-permute-start(bf16[48,1024]{1,0:T(8,128)(2,1)} %get-tuple-element.69), channel_id=1, source_target_pairs={{0,15},{1,14},{2,13},{3,12},{4,11},{5,10},{6,9},{7,8},{8,7},{9,6},... | collective-permute-start | bytes 294920 | tf_op jit(solution)/shard_map/ppermute | solution.py:786
  150.6 8.3 %collective-permute-start.24 = (f32[1,3,4,4,4]{4,3,2,1,0:T(4,128)S(1)}, f32[1,3,4,4,4]{4,3,2,1,0:T(4,128)S(1)}, u32[]{:S(2)}, u32[]{:S(2)}) collective-permute-start(f32[1,3,4,4,4]{4,3,2,1,0:T(4,128)S(1)} %reshape.43), channel_id=1, source_target_pairs={{0,16},{16,0},{1,17},{17,1},{2,18},{18,2},{3,19},{19,3},{4,20},{20... | collective-permute-start | bytes 2312 | tf_op jit(solution)/shard_map/ppermute | solution.py:682
  (15 other events, 226.1 us)

commit v15 on v12

--- a/solution.py
+++ b/solution.py
@@ -101,11 +101,12 @@
         begin(held_ref, cross_ref, sems.at[1]).wait()
 
 
-def plane_columns(me, source, crossed, half):
+def plane_columns(me, source, crossed, half, after):
     own_rows, width = source.shape
     part, count = width // half, half // 2
 
     def body(me_ref, source_ref, crossed_ref, *refs):
+        refs = refs[len(after) :]
         outs, (held_ref, in_sem, out_sem) = refs[:count], refs[count:]
         low = me_ref[0] & (half - 1)
         plane = lax.shift_right_logical(low, half.bit_length() - 2)
@@ -128,7 +129,7 @@
     return call(
         body,
         [(shaped((2 * own_rows, part), BF16), HBM)] * count,
-        [(me, SMEM), (source, HBM), (crossed, HBM)],
+        [(me, SMEM), (source, HBM), (crossed, HBM)] + [(x, HBM) for x in after],
         "plane_columns",
         0,
         [
@@ -222,27 +223,6 @@
     ]
     outs = [(shaped((half * own_rows, part), BF16), HBM)]
     return call(body, outs, [(source, HBM)], "spread_columns", 0, scratch)[0]
-
-
-def cut_factors(factors, first):
-    cuts = (slice(0, first), slice(first, factors.shape[0]))
-
-    def body(factors_ref, *refs):
-        outs, (held_ref, sems) = refs[:2], refs[2:]
-        loads = [
-            begin(factors_ref.at[at], held_ref.at[at], sems.at[0, n]) for n, at in enumerate(cuts)
-        ]
-        copies = []
-        for n, at in enumerate(cuts):
-            loads[n].wait()
-            copies.append(begin(held_ref.at[at], outs[n], sems.at[1, n]))
-        wait_all(copies)
-
-    outs = [
-        (shaped((at.stop - at.start,) + factors.shape[1:], BF16), HBM) for at in cuts
-    ]
-    scratch = [scratch_like(factors.shape, BF16), pltpu.SemaphoreType.DMA((2, 2))]
-    return call(body, outs, [(factors, HBM)], "cut_factors", 0, scratch)
 
 
 def pick_rows(me, half, own_rows, chosen, shares, after, name):
@@ -378,10 +358,7 @@
 
 def load_factor(order_ref, parts, m, target, sems):
     copies = []
-    sides = [parts[0].at[m]]
-    if len(parts) > 1:
-        first = parts[1].shape[0]
-        sides.append(parts[1].at[m] if m < first else parts[2].at[m - first])
+    sides = [part.at[m] for part in parts]
     for n, side in enumerate(sides):
         count, rows, cols = side.shape
         place = order_ref[0] ^ n if len(parts) > 1 else 0
@@ -488,8 +465,7 @@
 def forward_body(
     cap, pieces, sides, order_ref, mix_ref, slot_ref, got_hbm, *refs
 ):
-    held = 2 if sides > 1 else 1
-    parts, refs = refs[:held], refs[held:]
+    parts, refs = refs[:sides], refs[sides:]
     x_outs, refs = refs[:sides], refs[sides:]
     yg_hbm, yu_hbm, act_hbm, slope_hbm, hid_hbm = refs[:5]
     got_ref, side_ref, x_ref, yg_ref, yu_ref, act_ref, slope_ref, hid_ref = refs[5:13]
@@ -528,8 +504,7 @@
     cap, pieces, sides, after, order_ref, mix_ref, slot_hbm, score_hbm, got_hbm, act_hbm, slope_hbm, hid_hbm,
     *refs,
 ):
-    held = 3 if sides > 1 else 1
-    parts, refs = refs[:held], refs[held + after :]
+    parts, refs = refs[:sides], refs[sides + after :]
     back_hbm, x_outs, refs = refs[0], refs[1 : 1 + sides], refs[1 + sides :]
     y_hbm, d_hbm, inner_hbm = refs[:3]
     (
@@ -678,11 +653,9 @@
     group = lax.axis_index("seq").astype(jnp.int32).reshape(1)
     halves = [list(range(h, h + half)) for h in range(0, peers, half)]
     if swap:
-        cuts = [across(x) for x in cut_factors(factors[0], 2)]
-        factor_parts = [factors[0]] + cuts
+        factor_parts = [factors[0], across(factors)[0]]
         sides = 2
     else:
-        cuts = []
         factor_parts = [lax.all_gather(factors, "seq", axis=3, tiled=True)[0]]
         sides = 1
     sides_in = [(x, HBM) for x in factor_parts]
@@ -706,7 +679,7 @@
 
     got_rows = to_peers(pick_slots(cap, pieces, chosen, tokens, crossed, "pick_tokens"))
     if direct:
-        shares = plane_columns(me, cotangent, crossed[0], half)
+        shares = plane_columns(me, cotangent, crossed[0], half, factor_parts[1:])
         shares = [shares[0]] + [
             lax.ppermute(shares[k], "exp", [(n, n ^ k) for n in range(peers)])
             for k in range(1, half // 2)
@@ -717,7 +690,7 @@
             array, "exp", split_axis=0, concat_axis=0, axis_index_groups=halves, tiled=True
         )
         shares = [array.reshape(half * own_rows, -1)]
-    picked = pick_rows(me, half, own_rows, chosen, shares, cuts[:1], "pick_cotangent")
+    picked = pick_rows(me, half, own_rows, chosen, shares, [], "pick_cotangent")
     got_grads = to_peers(picked)
     placed = place_rows(cap, pieces, own_rows, me, half, chosen)
     gate = jax.nn.sigmoid(scores[0].reshape(-1).astype(F32) / 64.0)
@@ -735,7 +708,7 @@
     outs = call(
         functools.partial(forward_body, cap, pieces, sides),
         split + [mixed, mixed, flat, flat, flat],
-        [(group, SMEM), (mixing, SMEM), (slot, VMEM), (got_rows, HBM)] + sides_in[:2],
+        [(group, SMEM), (mixing, SMEM), (slot, VMEM), (got_rows, HBM)] + sides_in,
         "forward",
         2 * product,
         [back_scratch, scratch_like((2, depth, hidden), BF16), stack_scratch, mixed_scratch, mixed_scratch]

time: 151 us -> 173 us (1.15)
  waiting for transfers between devices: 56.1 us -> 79.7 us
  Pallas kernels: 45 us -> 42.6 us
    ppermute x6 -> x5, waiting for transfers between devices: 15.7 us -> 45.9 us  [across(): return lax.ppermute(array, 'seq', pair)]
    ppermute x3, waiting for transfers between devices: 20.6 us -> 12.2 us  [shards(): lax.ppermute(shares[k], 'exp', [(n, n ^ k) for n in range(peers)])]
    pallas_call x11 -> x10, Pallas kernels: 45 us -> 42.6 us  [call(): pl.pallas_call(body, out_shape=[x for x, _ in outs], in_specs=[place for...]
    all_to_all x3, waiting for transfers between devices: 19.9 us -> 21.7 us  [to_peers(): lax.all_to_all(array, 'exp', split_axis=0, concat_axis=0, tiled=True)]
    ppermute x6 -> x5, starting transfers between devices: 5.62 us -> 5.33 us  [across(): return lax.ppermute(array, 'seq', pair)]
  transfers between devices with their start and end apart: 13 -> 12, of which waited for: 7 -> 6; matrix products, arithmetic and copies ran while one was open for 3% -> 2% of each run, Pallas kernels for 19% -> 15%
where the time goes in v15:
time: 173 us; the launch traced here: 172 us
  waiting for transfers between devices  79.7 us (46%)
  Pallas kernels  42.6 us (25%)
  starting transfers between devices  26.4 us (15%)
  blocking collectives  15.3 us (9%)
  local copies, waits for them, and re-layouts  3.96 us (2%)
  other arithmetic  2.99 us (2%)
    ppermute x5, waiting for transfers between devices, across(): return lax.ppermute(array, 'seq', pair)  45.9 us
    pallas_call x10, Pallas kernels, call(): pl.pallas_call(body, out_shape=[x for x, _ in outs], in_specs=[place for...  42.6 us
    all_to_all x3, waiting for transfers between devices, to_peers(): lax.all_to_all(array, 'exp', split_axis=0, concat_axis=0, tiled=True)  21.7 us
    all_to_all x3, starting transfers between devices, to_peers(): lax.all_to_all(array, 'exp', split_axis=0, concat_axis=0, tiled=True)  17.9 us
    all_to_all x1, blocking collectives, shards(): lax.all_to_all(told, 'exp', split_axis=0, concat_axis=0, tiled=True)  15.3 us
    ppermute x3, waiting for transfers between devices, shards(): lax.ppermute(shares[k], 'exp', [(n, n ^ k) for n in range(peers)])  12.2 us
    ppermute x5, starting transfers between devices, across(): return lax.ppermute(array, 'seq', pair)  5.33 us
  transfers between devices with their start and end apart: 12, of which 6 were waited for; matrix products, arithmetic and copies ran while one was open for 2% of the time, Pallas kernels for 15%

profile of v15, /device:TPU:13, one launch (start us, length us, event | category | flops | bytes accessed | tf_op | source)
XLA Modules:
  0.0 171.8 jit_solution(894224407026964041)
XLA Ops:
  0.6 3.1 %wanted_rows.1 = (s32[32,128]{1,0:T(8,128)}, s32[1,128]{1,0:T(1,128)}, bf16[128,2048]{1,0:T(8,128)(2,1)}) custom-call(s32[1]{0:T(128)} %bitcast.me_ref, s32[2,64]{1,0:T(2,128)} %bitcast.25, bf16[128,4096]{1,0:T(8,128)(2,1)} %source_ref.2), custom_call_target="tpu_custom_call" | custom-call | flops 1048576 | bytes 1590276 | tf_op jit(solution)/shard_map/wanted_rows/pallas_call | solution.py:40
  4.0 15.3 %all_to_all.26 = s32[16,2,128]{2,1,0:T(2,128)} all-to-all(s32[16,2,128]{2,1,0:T(2,128)} %bitcast.24), channel_id=1, replica_groups=mesh['seq'=2,'exp'=16] {'exp'}, dimensions={0} | all-to-all | bytes 32768 | tf_op jit(solution)/shard_map/all_to_all | solution.py:673
  20.1 2.9 %pick_tokens.1 = bf16[384,2048]{1,0:T(8,128)(2,1)} custom-call(s32[32,128]{1,0:T(8,128)} %bitcast.21, bf16[128,4096]{1,0:T(8,128)(2,1)} %source_ref.3, bf16[128,2048]{1,0:T(8,128)(2,1)} %copy-done), custom_call_target="tpu_custom_call" | custom-call | flops 402653184 | bytes 3162112 | tf_op jit(solution)/shard_map/pick_tokens/pallas_call | solution.py:40
  23.0 6.8 %all-to-all-start.2 = ((bf16[16,24,2048]{2,1,0:T(8,128)(2,1)}), bf16[16,24,2048]{2,1,0:T(8,128)(2,1)}, u32[]{:S(2)}, u32[]{:S(2)}) async-start(bf16[16,24,2048]{2,1,0:T(8,128)(2,1)} %bitcast.15), calls=%async_computation.2 | async-start | bytes 3145728 | tf_op jit(solution)/shard_map/all_to_all | solution.py:677
  29.8 1.3 collective-permute-start.1
  31.1 34.5 %collective-permute-done.1 = bf16[1,3,4,512,128]{4,3,2,1,0:T(8,128)(2,1)} collective-permute-done((bf16[1,3,4,512,128]{4,3,2,1,0:T(8,128)(2,1)S(1)}, bf16[1,3,4,512,128]{4,3,2,1,0:T(8,128)(2,1)}, u32[]{:S(2)}, u32[]{:S(2)}) %collective-permute-start.1) | collective-permute-done | bytes 1572896 | tf_op jit(solution)/shard_map/ppermute | solution.py:648
  65.6 2.1 %plane_columns.1 = (bf16[256,512]{1,0:T(8,128)(2,1)}, bf16[256,512]{1,0:T(8,128)(2,1)}, bf16[256,512]{1,0:T(8,128)(2,1)}, bf16[256,512]{1,0:T(8,128)(2,1)}) custom-call(s32[1]{0:T(128)} %bitcast.me_ref, bf16[128,4096]{1,0:T(8,128)(2,1)} %source_ref.2, bf16[128,2048]{1,0:T(8,128)(2,1)} %copy-done, bf16[3,4,512,128]{3,2,1,0:T(8,128)(2,1)} %bitcast.6.refs_0_.refs_1_), custom_call_target="tpu_custom_call" | custom-call | bytes 4194308 | tf_op jit(solution)/shard_map/plane_columns/pallas_call | solution.py:40
  69.3 1.4 collective-permute-start.4
  70.7 6.4 %collective-permute-done.3.refs_2_ = bf16[256,512]{1,0:T(8,128)(2,1)S(1)} collective-permute-done((bf16[256,512]{1,0:T(8,128)(2,1)}, bf16[256,512]{1,0:T(8,128)(2,1)S(1)}, u32[]{:S(2)}, u32[]{:S(2)}) %collective-permute-start.3) | collective-permute-done | bytes 262176 | tf_op jit(solution)/shard_map/ppermute | solution.py:684
  77.1 5.8 %collective-permute-done.4.refs_3_ = bf16[256,512]{1,0:T(8,128)(2,1)S(1)} collective-permute-done((bf16[256,512]{1,0:T(8,128)(2,1)}, bf16[256,512]{1,0:T(8,128)(2,1)S(1)}, u32[]{:S(2)}, u32[]{:S(2)}) %collective-permute-start.4) | collective-permute-done | bytes 262176 | tf_op jit(solution)/shard_map/ppermute | solution.py:684
  83.5 4.2 %pick_cotangent.1 = bf16[1024,512]{1,0:T(8,128)(2,1)} custom-call(s32[1]{0:T(128)} %bitcast.me_ref, s32[32,128]{1,0:T(8,128)} %bitcast.22, bf16[256,512]{1,0:T(8,128)(2,1)} %get-tuple-element.27.refs_0_, bf16[256,512]{1,0:T(8,128)(2,1)} %copy-done.7, bf16[256,512]{1,0:T(8,128)(2,1)} %copy-done.8, bf16[256,512]{1,0:T(8,128)(2,1)} %copy-done.9), custom_call_target="tpu_custom_call" | custom-call | flops 1073741824 | bytes 2113540 | tf_op jit(solution)/shard_map/pick_cotangent/pallas_call | solution.py:40
  87.8 6.0 %all-to-all-start.1 = ((bf16[16,64,512]{2,1,0:T(8,128)(2,1)}), bf16[16,64,512]{2,1,0:T(8,128)(2,1)}, u32[]{:S(2)}, u32[]{:S(2)}) async-start(bf16[16,64,512]{2,1,0:T(8,128)(2,1)} %bitcast.20), calls=%async_computation.1 | async-start | bytes 2097152 | tf_op jit(solution)/shard_map/all_to_all | solution.py:677
  94.4 6.9 %forward.1 = (bf16[512,512]{1,0:T(8,128)(2,1)}, bf16[512,512]{1,0:T(8,128)(2,1)}, f32[512,512]{1,0:T(8,128)}, f32[512,512]{1,0:T(8,128)}, f32[128,512]{1,0:T(8,1...) custom-call(s32[1]{0:T(128)} %bitcast.4.order_ref, f32[192]{0:T(256)} %reshape.44.mix_ref, ...), custom_call_target="tpu_custom_call" | custom-call | flops 1073741824 | bytes 8652036 | tf_op jit(solution)/shard_map/forward/pallas_call | solution.py:40
  101.4 1.3 collective-permute-start.5
  102.6 16.1 %all-to-all-done.1 = bf16[16,64,512]{2,1,0:T(8,128)(2,1)} async-done(((bf16[16,64,512]{2,1,0:T(8,128)(2,1)}), bf16[16,64,512]{2,1,0:T(8,128)(2,1)}, u32[]{:S(2)}, u32[]{:S(2)}) %all-to-all-start.1) | async-done | bytes 1048608 | tf_op jit(solution)/shard_map/all_to_all | solution.py:677
  119.6 7.6 %backward.1 = (bf16[384,2048]{1,0:T(8,128)(2,1)}, bf16[512,512]{1,0:T(8,128)(2,1)}, bf16[512,512]{1,0:T(8,128)(2,1)}, f32[512,512]{1,0:T(8,128)}, bf16[3,128,512]{2,1,0:T(8,128)(2,1)}, /*index=5*/f32[128,128]{1,0:T(8,128)}) custom-call(s32[1]{0:T(128)} %bitcast.4.order_ref, f32[192]{0:T(256)} %reshape.44.mix_ref, ...), custom_call_target="tpu_custom_call" | custom-call | flops 1610612736 | bytes 9635588 | tf_op jit(solution)/shard_map/backward/pallas_call | solution.py:40
  127.2 5.1 %all-to-all-start.3 = ((bf16[16,24,2048]{2,1,0:T(8,128)(2,1)}), bf16[16,24,2048]{2,1,0:T(8,128)(2,1)}, u32[]{:S(2)}, u32[]{:S(2)}) async-start(bf16[16,24,2048]{2,1,0:T(8,128)(2,1)} %bitcast.17), calls=%async_computation.3 | async-start | bytes 3145728 | tf_op jit(solution)/shard_map/all_to_all | solution.py:677
  133.8 1.9 %place_rows.1.placed_hbm = bf16[256,384]{1,0:T(8,128)(2,1)} custom-call(s32[1]{0:T(128)} %bitcast.me_ref, s32[32,128]{1,0:T(8,128)} %bitcast.23), custom_call_target="tpu_custom_call" | custom-call | flops 1048576 | bytes 212996 | tf_op jit(solution)/shard_map/place_rows/pallas_call | solution.py:40
  135.7 3.9 %mix_partials.1 = f32[192,128]{1,0:T(8,128)} custom-call(f32[512,512]{1,0:T(8,128)} %get-tuple-element.40.yg_hbm, f32[512,512]{1,0:T(8,128)} %get-tuple-element.41.yu_hbm, f32[512,512]{1,0:T(8,128)} %get-tuple-element.42.yd_hbm, bf16[3,128,512]{2,1,0:T(8,128)(2,1)} %get-tuple-element.38.refs_2_.d_hbm), custom_call_target="tpu_custom_call" | custom-call | flops 6291456 | bytes 3637248 | tf_op jit(solution)/shard_map/mix_partials/pallas_call | solution.py:40
  142.1 1.3 subtract_multiply_fusion
  143.4 11.4 %collective-permute-done.8 = f32[1,3,4,4,4]{4,3,2,1,0:T(4,128)S(1)} collective-permute-done((f32[1,3,4,4,4]{4,3,2,1,0:T(4,128)S(1)}, f32[1,3,4,4,4]{4,3,2,1,0:T(4,128)S(1)}, u32[]{:S(2)}, u32[]{:S(2)}) %collective-permute-start.8) | collective-permute-done | bytes 800 | tf_op jit(solution)/shard_map/ppermute | solution.py:648
  156.2 6.9 %factor_grad.1 = f32[3,4,512,128]{3,2,1,0:T(8,128)} custom-call(f32[192]{0:T(256)} %reshape.44.mix_ref, bf16[512,512]{1,0:T(8,128)(2,1)} %get-tuple-element.36.refs_0_, bf16[512,512]{1,0:T(8,128)(2,1)} %get-tuple-element.37.refs_1_, bf16[3,128,512]{2,1,0:T(8,128)(2,1)} %get-tuple-element.38.refs_2_.d_hbm, bf16[512,512]{1,0:T(8,128)(2,1)} %copy-done.3, ...), custom_call_target="tpu_custom_call" | custom-call | flops 1610612736 | bytes 6030080 | tf_op jit(solution)/shard_map/factor_grad/pallas_call | solution.py:40
  163.0 5.5 %all-to-all-done.3 = bf16[16,24,2048]{2,1,0:T(8,128)(2,1)} async-done(((bf16[16,24,2048]{2,1,0:T(8,128)(2,1)}), bf16[16,24,2048]{2,1,0:T(8,128)(2,1)}, u32[]{:S(2)}, u32[]{:S(2)}) %all-to-all-start.3) | async-done | bytes 1572896 | tf_op jit(solution)/shard_map/all_to_all | solution.py:677
  168.6 3.1 %sum_rows.1 = bf16[128,4096]{1,0:T(8,128)(2,1)} custom-call(bf16[256,384]{1,0:T(8,128)(2,1)} %place_rows.1.placed_hbm, bf16[384,2048]{1,0:T(8,128)(2,1)} %bitcast.13.returned_ref), custom_call_target="tpu_custom_call" | custom-call | flops 402653184 | bytes 2818048 | tf_op jit(solution)/shard_map/sum_rows/pallas_call | solution.py:40
  (38 shorter events, 10.3 us)
Async XLA Ops:
  3.8 15.5 %collective-permute-start = (bf16[128,2048]{1,0:T(8,128)(2,1)}, bf16[128,2048]{1,0:T(8,128)(2,1)S(1)}, u32[]{:S(2)}, u32[]{:S(2)}) collective-permute-start(bf16[128,2048]{1,0:T(8,128)(2,1)} %get-tuple-element.26), channel_id=1, source_target_pairs={{0,4},{1,5},{2,6},{3,7},{4,0},{5,1},{6,2},{7,3},{8,12},{9,13},{10,... | collective-permute-start | bytes 1572872 | tf_op jit(solution)/shard_map/ppermute | solution.py:672
  19.3 0.8 copy-start
  23.0 6.8 %copy-start.2 = (bf16[1,3,4,512,128]{4,3,2,1,0:T(8,128)(2,1)S(1)}, bf16[1,3,4,512,128]{4,3,2,1,0:T(8,128)(2,1)}, u32[]{:S(2)}) copy-start(bf16[1,3,4,512,128]{4,3,2,1,0:T(8,128)(2,1)} %param.8) | copy-start | bytes 4718596
  23.0 64.8 %all-to-all-start.2 = ((bf16[16,24,2048]{2,1,0:T(8,128)(2,1)}), bf16[16,24,2048]{2,1,0:T(8,128)(2,1)}, u32[]{:S(2)}, u32[]{:S(2)}) async-start(bf16[16,24,2048]{2,1,0:T(8,128)(2,1)} %bitcast.15), calls=%async_computation.2 | async-start | bytes 3145728 | tf_op jit(solution)/shard_map/all_to_all | solution.py:677
  29.8 35.8 %collective-permute-start.1 = (bf16[1,3,4,512,128]{4,3,2,1,0:T(8,128)(2,1)S(1)}, bf16[1,3,4,512,128]{4,3,2,1,0:T(8,128)(2,1)}, u32[]{:S(2)}, u32[]{:S(2)}) collective-permute-start(bf16[1,3,4,512,128]{4,3,2,1,0:T(8,128)(2,1)S(1)} %copy-done.2), channel_id=1, source_target_pairs={{0,16},{16,0},{1,17},{17,1},{2,18},{18,2},{3,19},{19,3},{4,20},{20... | collective-permute-start | bytes 4718600 | tf_op jit(solution)/shard_map/ppermute | solution.py:648
  67.7 3.0 %collective-permute-start.2 = (bf16[256,512]{1,0:T(8,128)(2,1)}, bf16[256,512]{1,0:T(8,128)(2,1)S(1)}, u32[]{:S(2)}, u32[]{:S(2)}) collective-permute-start(bf16[256,512]{1,0:T(8,128)(2,1)} %get-tuple-element.28), channel_id=1, source_target_pairs={{0,1},{1,0},{2,3},{3,2},{4,5},{5,4},{6,7},{7,6},{8,9},{9,8},{10,11... | collective-permute-start | bytes 786440 | tf_op jit(solution)/shard_map/ppermute | solution.py:684
  69.0 8.1 %collective-permute-start.3 = (bf16[256,512]{1,0:T(8,128)(2,1)}, bf16[256,512]{1,0:T(8,128)(2,1)S(1)}, u32[]{:S(2)}, u32[]{:S(2)}) collective-permute-start(bf16[256,512]{1,0:T(8,128)(2,1)} %get-tuple-element.29), channel_id=1, source_target_pairs={{0,2},{1,3},{2,0},{3,1},{4,6},{5,7},{6,4},{7,5},{8,10},{9,11},{10,... | collective-permute-start | bytes 786440 | tf_op jit(solution)/shard_map/ppermute | solution.py:684
  69.3 13.6 %collective-permute-start.4 = (bf16[256,512]{1,0:T(8,128)(2,1)}, bf16[256,512]{1,0:T(8,128)(2,1)S(1)}, u32[]{:S(2)}, u32[]{:S(2)}) collective-permute-start(bf16[256,512]{1,0:T(8,128)(2,1)} %get-tuple-element.30), channel_id=1, source_target_pairs={{0,3},{1,2},{2,1},{3,0},{4,7},{5,6},{6,5},{7,4},{8,11},{9,10},{10,... | collective-permute-start | bytes 786440 | tf_op jit(solution)/shard_map/ppermute | solution.py:684
  70.7 12.2 %copy-start.7 = (bf16[256,512]{1,0:T(8,128)(2,1)}, bf16[256,512]{1,0:T(8,128)(2,1)S(1)}, u32[]{:S(2)}) copy-start(bf16[256,512]{1,0:T(8,128)(2,1)S(1)} %collective-permute-done.2.refs_1_) | copy-start | bytes 786436
  77.1 5.8 %copy-start.8 = (bf16[256,512]{1,0:T(8,128)(2,1)}, bf16[256,512]{1,0:T(8,128)(2,1)S(1)}, u32[]{:S(2)}) copy-start(bf16[256,512]{1,0:T(8,128)(2,1)S(1)} %collective-permute-done.3.refs_2_) | copy-start | bytes 786436
  82.9 0.7 copy-start.9
  87.8 6.0 %copy-start.6 = (f32[1,3,4,4,4]{4,3,2,1,0:T(4,128)S(1)}, f32[1,3,4,4,4]{4,3,2,1,0:T(4,128)}, u32[]{:S(2)}) copy-start(f32[1,3,4,4,4]{4,3,2,1,0:T(4,128)} %param.9) | copy-start | bytes 2308
  87.8 30.9 %all-to-all-start.1 = ((bf16[16,64,512]{2,1,0:T(8,128)(2,1)}), bf16[16,64,512]{2,1,0:T(8,128)(2,1)}, u32[]{:S(2)}, u32[]{:S(2)}) async-start(bf16[16,64,512]{2,1,0:T(8,128)(2,1)} %bitcast.20), calls=%async_computation.1 | async-start | bytes 2097152 | tf_op jit(solution)/shard_map/all_to_all | solution.py:677
  101.4 17.4 %collective-permute-start.5 = (bf16[512,512]{1,0:T(8,128)(2,1)}, bf16[512,512]{1,0:T(8,128)(2,1)S(1)}, u32[]{:S(2)}, u32[]{:S(2)}) collective-permute-start(bf16[512,512]{1,0:T(8,128)(2,1)} %get-tuple-element.34), channel_id=1, source_target_pairs={{0,16},{16,0},{1,17},{17,1},{2,18},{18,2},{3,19},{19,3},{4,20},{20... | collective-permute-start | bytes 1572872 | tf_op jit(solution)/shard_map/ppermute | solution.py:648
  118.8 0.8 copy-start.3
  127.2 6.4 %copy-start.1 = (bf16[3,128,512]{2,1,0:T(8,128)(2,1)S(1)}, bf16[3,128,512]{2,1,0:T(8,128)(2,1)}, u32[]{:S(2)}) copy-start(bf16[3,128,512]{2,1,0:T(8,128)(2,1)} %get-tuple-element.38.refs_2_.d_hbm) | copy-start | bytes 1179652
  127.2 41.4 %all-to-all-start.3 = ((bf16[16,24,2048]{2,1,0:T(8,128)(2,1)}), bf16[16,24,2048]{2,1,0:T(8,128)(2,1)}, u32[]{:S(2)}, u32[]{:S(2)}) async-start(bf16[16,24,2048]{2,1,0:T(8,128)(2,1)} %bitcast.17), calls=%async_computation.3 | async-start | bytes 3145728 | tf_op jit(solution)/shard_map/all_to_all | solution.py:677
  132.3 23.1 %collective-permute-start.6 = (bf16[512,512]{1,0:T(8,128)(2,1)}, bf16[512,512]{1,0:T(8,128)(2,1)S(1)}, u32[]{:S(2)}, u32[]{:S(2)}) collective-permute-start(bf16[512,512]{1,0:T(8,128)(2,1)} %get-tuple-element.39), channel_id=1, source_target_pairs={{0,16},{16,0},{1,17},{17,1},{2,18},{18,2},{3,19},{19,3},{4,20},{20... | collective-permute-start | bytes 1572872 | tf_op jit(solution)/shard_map/ppermute | solution.py:648
  133.5 21.8 %collective-permute-start.7 = (bf16[3,128,512]{2,1,0:T(8,128)(2,1)S(1)}, bf16[3,128,512]{2,1,0:T(8,128)(2,1)}, u32[]{:S(2)}, u32[]{:S(2)}) collective-permute-start(bf16[3,128,512]{2,1,0:T(8,128)(2,1)S(1)} %copy-done.1), channel_id=1, source_target_pairs={{0,16},{16,0},{1,17},{17,1},{2,18},{18,2},{3,19},{19,3},{4,20},{20... | collective-permute-start | bytes 1179656 | tf_op jit(solution)/shard_map/ppermute | solution.py:648
  135.7 6.3 %copy-start.5 = (f32[128,128]{1,0:T(8,128)S(1)}, f32[128,128]{1,0:T(8,128)}, u32[]{:S(2)}) copy-start(f32[128,128]{1,0:T(8,128)} %get-tuple-element.43) | copy-start | bytes 196612
  140.7 14.1 %collective-permute-start.8 = (f32[1,3,4,4,4]{4,3,2,1,0:T(4,128)S(1)}, f32[1,3,4,4,4]{4,3,2,1,0:T(4,128)S(1)}, u32[]{:S(2)}, u32[]{:S(2)}) collective-permute-start(f32[1,3,4,4,4]{4,3,2,1,0:T(4,128)S(1)} %reshape.51), channel_id=1, source_target_pairs={{0,16},{16,0},{1,17},{17,1},{2,18},{18,2},{3,19},{19,3},{4,20},{20... | collective-permute-start | bytes 2312 | tf_op jit(solution)/shard_map/ppermute | solution.py:648
  155.4 0.8 copy-start.4

commit v16 on v12

--- a/solution.py
+++ b/solution.py
@@ -68,15 +68,18 @@
     return [slice(c * chunk, (c + 1) * chunk) for c in range(part // chunk)]
 
 
-def front_body(cap, pieces, own_rows, block_len, half, cross, me_ref, chosen_ref, *refs):
+def front_body(cap, pieces, own_rows, block_len, half, cross, me_ref, chosen_hbm, *refs):
+    chosen_ref, told_ref, slot_ref, small_sem = refs[-4:]
+    small = begin(chosen_hbm, chosen_ref, small_sem.at[0])
     if cross:
-        source_ref, told_ref, slot_ref, cross_ref, held_ref, sems = refs
+        source_ref, told_hbm, slot_hbm, cross_ref, held_ref, sems = refs[:-4]
         width = cross_ref.shape[1]
         plane = lax.shift_right_logical(me_ref[0] & (half - 1), half.bit_length() - 2)
         at = pl.ds(pl.multiple_of((1 - plane) * width, width), width)
         load = begin(source_ref.at[:, at], held_ref, sems.at[0])
     else:
-        told_ref, slot_ref = refs
+        told_hbm, slot_hbm = refs[:-4]
+    small.wait()
     peers, rows = told_ref.shape[0] // 2, slot_ref.shape[1]
     blocks = [chosen_ref[b : b + 1, :] for b in range(chosen_ref.shape[0])]
     position = jnp.concatenate([x + b * block_len for b, x in enumerate(blocks)], axis=1)
@@ -96,9 +99,15 @@
     marked = jnp.where(twice == 2 * owner, local + 1, 0).astype(F32)
     asked = dot_nt(marked.astype(BF16), hit.astype(BF16)).astype(jnp.int32)
     told_ref[...] = jnp.where((twice & 1) == 1, jnp.concatenate(blocks, axis=1), asked)
+    stores = [
+        begin(told_ref, told_hbm, small_sem.at[1]),
+        begin(slot_ref, slot_hbm, small_sem.at[2]),
+    ]
     if cross:
         load.wait()
-        begin(held_ref, cross_ref, sems.at[1]).wait()
+        stores.append(begin(held_ref, cross_ref, sems.at[1]))
+    for store in stores:
+        store.wait()
 
 
 def plane_columns(me, source, crossed, half):
@@ -378,17 +387,18 @@
 
 def load_factor(order_ref, parts, m, target, sems):
     copies = []
-    sides = [parts[0].at[m]]
-    if len(parts) > 1:
-        first = parts[1].shape[0]
-        sides.append(parts[1].at[m] if m < first else parts[2].at[m - first])
-    for n, side in enumerate(sides):
-        count, rows, cols = side.shape
+    _, count, rows, cols = parts[0].shape
+    first = parts[1].shape[0] if len(parts) > 1 else 0
+    for n in range(2 if len(parts) > 1 else 1):
         place = order_ref[0] ^ n if len(parts) > 1 else 0
         start = pl.multiple_of(place * rows, rows)
         for i in range(count):
+            side = parts[0].at[m, i]
+            if n == 1:
+                flat = m * count + i
+                side = parts[1].at[flat] if flat < first else parts[2].at[flat - first]
             at = target.at[pl.ds(start, rows), i * cols : (i + 1) * cols]
-            copies.append(begin(side.at[i], at, sems.at[n, i]))
+            copies.append(begin(side, at, sems.at[n, i]))
     return copies
 
 
@@ -678,7 +688,8 @@
     group = lax.axis_index("seq").astype(jnp.int32).reshape(1)
     halves = [list(range(h, h + half)) for h in range(0, peers, half)]
     if swap:
-        cuts = [across(x) for x in cut_factors(factors[0], 2)]
+        flat_factors = factors[0].reshape(weights * count, depth_own, cols)
+        cuts = [across(x) for x in cut_factors(flat_factors, 10)]
         factor_parts = [factors[0]] + cuts
         sides = 2
     else:
@@ -689,11 +700,14 @@
     cross = [(shaped((own_rows, width // 2), BF16), HBM)] if direct else []
     told, slot, *crossed = call(
         functools.partial(front_body, cap, pieces, own_rows, block_len, half, direct),
-        [(shaped((2 * peers, rows), jnp.int32), VMEM), (shaped((1, rows), jnp.int32), VMEM)] + cross,
-        [(me, SMEM), (selection[0], VMEM)] + ([(cotangent, HBM)] if direct else []),
+        [(shaped((2 * peers, rows), jnp.int32), HBM), (shaped((1, rows), jnp.int32), HBM)] + cross,
+        [(me, SMEM), (selection[0], HBM)] + ([(cotangent, HBM)] if direct else []),
         "wanted_rows",
         1 << 20,
-        [scratch_like((own_rows, width // 2), BF16), dma((2,))] if direct else [],
+        ([scratch_like((own_rows, width // 2), BF16), dma((2,))] if direct else [])
+        + [scratch_like(selection.shape[1:], jnp.int32)]
+        + [scratch_like((2 * peers, rows), jnp.int32), scratch_like((1, rows), jnp.int32)]
+        + [dma((3,))],
     )
     if direct:
         crossed = [lax.ppermute(crossed[0], "exp", [(n, n ^ (half // 2)) for n in range(peers)])]

time: 151 us -> 155 us (1.026)
  waiting for transfers between devices: 56.1 us -> 59 us
  starting transfers between devices: 26.2 us -> 28.9 us
    ppermute x6, waiting for transfers between devices: 15.7 us -> 32.5 us  [across(): return lax.ppermute(array, 'seq', pair)]
    all_to_all x3, waiting for transfers between devices: 19.9 us -> 5.53 us  [to_peers(): lax.all_to_all(array, 'exp', split_axis=0, concat_axis=0, tiled=True)]
    all_to_all x3, starting transfers between devices: 17.9 us -> 20.6 us  [to_peers(): lax.all_to_all(array, 'exp', split_axis=0, concat_axis=0, tiled=True)]
  transfers between devices with their start and end apart: 13 -> 13, of which waited for: 7 -> 6; matrix products, arithmetic and copies ran while one was open for 3% -> 2% of each run, Pallas kernels for 19% -> 18%
where the time goes in v16:
time: 155 us; the launch traced here: 154 us
  waiting for transfers between devices  59 us (38%)
  Pallas kernels  43.9 us (28%)
  starting transfers between devices  28.9 us (19%)
  blocking collectives  15.3 us (10%)
  local copies, waits for them, and re-layouts  3.26 us (2%)
  other arithmetic  2.99 us (2%)
    pallas_call x11, Pallas kernels, call(): pl.pallas_call(body, out_shape=[x for x, _ in outs], in_specs=[place for...  43.9 us
    ppermute x6, waiting for transfers between devices, across(): return lax.ppermute(array, 'seq', pair)  32.5 us
    ppermute x3, waiting for transfers between devices, shards(): lax.ppermute(shares[k], 'exp', [(n, n ^ k) for n in range(peers)])  21 us
    all_to_all x3, starting transfers between devices, to_peers(): lax.all_to_all(array, 'exp', split_axis=0, concat_axis=0, tiled=True)  20.6 us
    all_to_all x1, blocking collectives, shards(): lax.all_to_all(told, 'exp', split_axis=0, concat_axis=0, tiled=True)  15.3 us
    ppermute x6, starting transfers between devices, across(): return lax.ppermute(array, 'seq', pair)  5.64 us
    all_to_all x3, waiting for transfers between devices, to_peers(): lax.all_to_all(array, 'exp', split_axis=0, concat_axis=0, tiled=True)  5.53 us
  transfers between devices with their start and end apart: 13, of which 6 were waited for; matrix products, arithmetic and copies ran while one was open for 2% of the time, Pallas kernels for 18%

profile of v16, /device:TPU:13, one launch (start us, length us, event | category | flops | bytes accessed | tf_op | source)
XLA Modules:
  0.0 154.3 jit_solution(4367973726047016154)
XLA Ops:
  0.6 1.9 %wanted_rows.1 = (s32[32,128]{1,0:T(8,128)}, s32[1,128]{1,0:T(1,128)}, bf16[128,2048]{1,0:T(8,128)(2,1)}) custom-call(s32[1]{0:T(128)} %bitcast.me_ref, s32[2,64]{1,0:T(2,128)} %bitcast.26, bf16[128,4096]{1,0:T(8,128)(2,1)} %source_ref.2), custom_call_target="tpu_custom_call" | custom-call | flops 1048576 | bytes 1590276 | tf_op jit(solution)/shard_map/wanted_rows/pallas_call | solution.py:40
  2.8 15.3 %all_to_all.26 = s32[16,2,128]{2,1,0:T(2,128)} all-to-all(s32[16,2,128]{2,1,0:T(2,128)} %bitcast.25), channel_id=1, replica_groups=mesh['seq'=2,'exp'=16] {'exp'}, dimensions={0} | all-to-all | bytes 32768 | tf_op jit(solution)/shard_map/all_to_all | solution.py:714
  18.8 2.9 %pick_tokens.1 = bf16[384,2048]{1,0:T(8,128)(2,1)} custom-call(s32[32,128]{1,0:T(8,128)} %bitcast.22, bf16[128,4096]{1,0:T(8,128)(2,1)} %source_ref.3, bf16[128,2048]{1,0:T(8,128)(2,1)} %copy-done), custom_call_target="tpu_custom_call" | custom-call | flops 402653184 | bytes 3162112 | tf_op jit(solution)/shard_map/pick_tokens/pallas_call | solution.py:40
  21.8 6.7 %all-to-all-start.2 = ((bf16[16,24,2048]{2,1,0:T(8,128)(2,1)}), bf16[16,24,2048]{2,1,0:T(8,128)(2,1)}, u32[]{:S(2)}, u32[]{:S(2)}) async-start(bf16[16,24,2048]{2,1,0:T(8,128)(2,1)} %bitcast.15), calls=%async_computation.2 | async-start | bytes 3145728 | tf_op jit(solution)/shard_map/all_to_all | solution.py:718
  28.4 2.5 %cut_factors.1 = (bf16[10,512,128]{2,1,0:T(8,128)(2,1)}, bf16[2,512,128]{2,1,0:T(8,128)(2,1)}) custom-call(bf16[12,512,128]{2,1,0:T(8,128)(2,1)} %bitcast.16), custom_call_target="tpu_custom_call" | custom-call | bytes 3145728 | tf_op jit(solution)/shard_map/cut_factors/pallas_call | solution.py:40
  30.9 1.3 collective-permute-start
  32.2 2.1 %plane_columns.1 = (bf16[256,512]{1,0:T(8,128)(2,1)}, bf16[256,512]{1,0:T(8,128)(2,1)}, bf16[256,512]{1,0:T(8,128)(2,1)}, bf16[256,512]{1,0:T(8,128)(2,1)}) custom-call(s32[1]{0:T(128)} %bitcast.me_ref, bf16[128,4096]{1,0:T(8,128)(2,1)} %source_ref.2, bf16[128,2048]{1,0:T(8,128)(2,1)} %copy-done), custom_call_target="tpu_custom_call" | custom-call | bytes 2621444 | tf_op jit(solution)/shard_map/plane_columns/pallas_call | solution.py:40
  35.4 1.4 collective-permute-start.4
  36.8 10.9 %collective-permute-done.3.refs_3_ = bf16[256,512]{1,0:T(8,128)(2,1)S(1)} collective-permute-done((bf16[256,512]{1,0:T(8,128)(2,1)}, bf16[256,512]{1,0:T(8,128)(2,1)S(1)}, u32[]{:S(2)}, u32[]{:S(2)}) %collective-permute-start.3) | collective-permute-done | bytes 262176 | tf_op jit(solution)/shard_map/ppermute | solution.py:725
  47.7 10.1 %collective-permute-done.4.refs_4_ = bf16[256,512]{1,0:T(8,128)(2,1)S(1)} collective-permute-done((bf16[256,512]{1,0:T(8,128)(2,1)}, bf16[256,512]{1,0:T(8,128)(2,1)S(1)}, u32[]{:S(2)}, u32[]{:S(2)}) %collective-permute-start.4) | collective-permute-done | bytes 262176 | tf_op jit(solution)/shard_map/ppermute | solution.py:725
  57.8 3.6 %collective-permute-done.refs_0_.refs_1_ = bf16[10,512,128]{2,1,0:T(8,128)(2,1)} collective-permute-done((bf16[10,512,128]{2,1,0:T(8,128)(2,1)}, bf16[10,512,128]{2,1,0:T(8,128)(2,1)}, u32[]{:S(2)}, u32[]{:S(2)}) %collective-permute-start) | collective-permute-done | bytes 1310752 | tf_op jit(solution)/shard_map/ppermute | solution.py:683
  61.3 4.2 %pick_cotangent.1 = bf16[1024,512]{1,0:T(8,128)(2,1)} custom-call(s32[1]{0:T(128)} %bitcast.me_ref, s32[32,128]{1,0:T(8,128)} %bitcast.23, bf16[10,512,128]{2,1,0:T(8,128)(2,1)} %collective-permute-done.refs_0_.refs_1_, bf16[256,512]{1,0:T(8,128)(2,1)} %get-tuple-element.30.refs_1_, bf16[256,512]{1,0:T(8,128)(2,1)} %copy-done.7, bf16[256,512]{1,0:T(8,128)(2,1)} %copy-done.8, ...), custom_call_target="tpu_custom_call" | custom-call | flops 1073741824 | bytes 3424260 | tf_op jit(solution)/shard_map/pick_cotangent/pallas_call | solution.py:40
  65.6 6.9 %all-to-all-start.1 = ((bf16[16,64,512]{2,1,0:T(8,128)(2,1)}), bf16[16,64,512]{2,1,0:T(8,128)(2,1)}, u32[]{:S(2)}, u32[]{:S(2)}) async-start(bf16[16,64,512]{2,1,0:T(8,128)(2,1)} %bitcast.21), calls=%async_computation.1 | async-start | bytes 2097152 | tf_op jit(solution)/shard_map/all_to_all | solution.py:718
  73.2 7.0 %forward.1 = (bf16[512,512]{1,0:T(8,128)(2,1)}, bf16[512,512]{1,0:T(8,128)(2,1)}, f32[512,512]{1,0:T(8,128)}, f32[512,512]{1,0:T(8,128)}, f32[128,512]{1,0:T(8,1...) custom-call(s32[1]{0:T(128)} %bitcast.4.order_ref, f32[192]{0:T(256)} %reshape.44.mix_ref, ...), custom_call_target="tpu_custom_call" | custom-call | flops 1073741824 | bytes 8389892 | tf_op jit(solution)/shard_map/forward/pallas_call | solution.py:40
  81.7 17.6 %collective-permute-done.5.refs_2_ = bf16[2,512,128]{2,1,0:T(8,128)(2,1)} collective-permute-done((bf16[2,512,128]{2,1,0:T(8,128)(2,1)S(1)}, bf16[2,512,128]{2,1,0:T(8,128)(2,1)}, u32[]{:S(2)}, u32[]{:S(2)}) %collective-permute-start.5) | collective-permute-done | bytes 262176 | tf_op jit(solution)/shard_map/ppermute | solution.py:683
  100.2 7.6 %backward.1 = (bf16[384,2048]{1,0:T(8,128)(2,1)}, bf16[512,512]{1,0:T(8,128)(2,1)}, bf16[512,512]{1,0:T(8,128)(2,1)}, f32[512,512]{1,0:T(8,128)}, bf16[3,128,512]{2,1,0:T(8,128)(2,1)}, /*index=5*/f32[128,128]{1,0:T(8,128)}) custom-call(s32[1]{0:T(128)} %bitcast.4.order_ref, f32[192]{0:T(256)} %reshape.44.mix_ref, ...), custom_call_target="tpu_custom_call" | custom-call | flops 1610612736 | bytes 9635588 | tf_op jit(solution)/shard_map/backward/pallas_call | solution.py:40
  107.7 7.0 %all-to-all-start.3 = ((bf16[16,24,2048]{2,1,0:T(8,128)(2,1)}), bf16[16,24,2048]{2,1,0:T(8,128)(2,1)}, u32[]{:S(2)}, u32[]{:S(2)}) async-start(bf16[16,24,2048]{2,1,0:T(8,128)(2,1)} %bitcast.20), calls=%async_computation.3 | async-start | bytes 3145728 | tf_op jit(solution)/shard_map/all_to_all | solution.py:718
  114.7 1.3 collective-permute-start.7
  116.3 1.9 %place_rows.1.placed_hbm = bf16[256,384]{1,0:T(8,128)(2,1)} custom-call(s32[1]{0:T(128)} %bitcast.me_ref, s32[32,128]{1,0:T(8,128)} %bitcast.24), custom_call_target="tpu_custom_call" | custom-call | flops 1048576 | bytes 212996 | tf_op jit(solution)/shard_map/place_rows/pallas_call | solution.py:40
  118.1 3.9 %mix_partials.1 = f32[192,128]{1,0:T(8,128)} custom-call(f32[512,512]{1,0:T(8,128)} %get-tuple-element.44.yg_hbm, f32[512,512]{1,0:T(8,128)} %get-tuple-element.45.yu_hbm, f32[512,512]{1,0:T(8,128)} %get-tuple-element.46.yd_hbm, bf16[3,128,512]{2,1,0:T(8,128)(2,1)} %get-tuple-element.42.refs_2_.d_hbm), custom_call_target="tpu_custom_call" | custom-call | flops 6291456 | bytes 3637248 | tf_op jit(solution)/shard_map/mix_partials/pallas_call | solution.py:40
  125.9 11.3 %collective-permute-done.9 = f32[1,3,4,4,4]{4,3,2,1,0:T(4,128)S(1)} collective-permute-done((f32[1,3,4,4,4]{4,3,2,1,0:T(4,128)S(1)}, f32[1,3,4,4,4]{4,3,2,1,0:T(4,128)S(1)}, u32[]{:S(2)}, u32[]{:S(2)}) %collective-permute-start.9) | collective-permute-done | bytes 800 | tf_op jit(solution)/shard_map/ppermute | solution.py:683
  138.6 6.9 %factor_grad.1 = f32[3,4,512,128]{3,2,1,0:T(8,128)} custom-call(f32[192]{0:T(256)} %reshape.44.mix_ref, bf16[512,512]{1,0:T(8,128)(2,1)} %get-tuple-element.40.refs_0_, bf16[512,512]{1,0:T(8,128)(2,1)} %get-tuple-element.41.refs_1_, bf16[3,128,512]{2,1,0:T(8,128)(2,1)} %get-tuple-element.42.refs_2_.d_hbm, bf16[512,512]{1,0:T(8,128)(2,1)} %copy-done.2, ...), custom_call_target="tpu_custom_call" | custom-call | flops 1610612736 | bytes 6030080 | tf_op jit(solution)/shard_map/factor_grad/pallas_call | solution.py:40
  145.5 5.5 %all-to-all-done.3 = bf16[16,24,2048]{2,1,0:T(8,128)(2,1)} async-done(((bf16[16,24,2048]{2,1,0:T(8,128)(2,1)}), bf16[16,24,2048]{2,1,0:T(8,128)(2,1)}, u32[]{:S(2)}, u32[]{:S(2)}) %all-to-all-start.3) | async-done | bytes 1572896 | tf_op jit(solution)/shard_map/all_to_all | solution.py:718
  151.0 3.1 %sum_rows.1 = bf16[128,4096]{1,0:T(8,128)(2,1)} custom-call(bf16[256,384]{1,0:T(8,128)(2,1)} %place_rows.1.placed_hbm, bf16[384,2048]{1,0:T(8,128)(2,1)} %bitcast.13.returned_ref), custom_call_target="tpu_custom_call" | custom-call | flops 402653184 | bytes 2818048 | tf_op jit(solution)/shard_map/sum_rows/pallas_call | solution.py:40
  (41 shorter events, 10.6 us)
Async XLA Ops:
  2.5 15.5 %collective-permute-start.1 = (bf16[128,2048]{1,0:T(8,128)(2,1)}, bf16[128,2048]{1,0:T(8,128)(2,1)S(1)}, u32[]{:S(2)}, u32[]{:S(2)}) collective-permute-start(bf16[128,2048]{1,0:T(8,128)(2,1)} %get-tuple-element.29), channel_id=1, source_target_pairs={{0,4},{1,5},{2,6},{3,7},{4,0},{5,1},{6,2},{7,3},{8,12},{9,13},{10,... | collective-permute-start | bytes 1572872 | tf_op jit(solution)/shard_map/ppermute | solution.py:713
  18.0 0.8 copy-start
  21.8 43.8 %all-to-all-start.2 = ((bf16[16,24,2048]{2,1,0:T(8,128)(2,1)}), bf16[16,24,2048]{2,1,0:T(8,128)(2,1)}, u32[]{:S(2)}, u32[]{:S(2)}) async-start(bf16[16,24,2048]{2,1,0:T(8,128)(2,1)} %bitcast.15), calls=%async_computation.2 | async-start | bytes 3145728 | tf_op jit(solution)/shard_map/all_to_all | solution.py:718
  30.9 30.4 %collective-permute-start = (bf16[10,512,128]{2,1,0:T(8,128)(2,1)}, bf16[10,512,128]{2,1,0:T(8,128)(2,1)}, u32[]{:S(2)}, u32[]{:S(2)}) collective-permute-start(bf16[10,512,128]{2,1,0:T(8,128)(2,1)} %get-tuple-element.28), channel_id=1, source_target_pairs={{0,16},{16,0},{1,17},{17,1},{2,18},{18,2},{3,19},{19,3},{4,20},{20... | collective-permute-start | bytes 3932168 | tf_op jit(solution)/shard_map/ppermute | solution.py:683
  34.4 2.4 %collective-permute-start.2 = (bf16[256,512]{1,0:T(8,128)(2,1)}, bf16[256,512]{1,0:T(8,128)(2,1)S(1)}, u32[]{:S(2)}, u32[]{:S(2)}) collective-permute-start(bf16[256,512]{1,0:T(8,128)(2,1)} %get-tuple-element.31), channel_id=1, source_target_pairs={{0,1},{1,0},{2,3},{3,2},{4,5},{5,4},{6,7},{7,6},{8,9},{9,8},{10,11... | collective-permute-start | bytes 786440 | tf_op jit(solution)/shard_map/ppermute | solution.py:725
  35.1 12.6 %collective-permute-start.3 = (bf16[256,512]{1,0:T(8,128)(2,1)}, bf16[256,512]{1,0:T(8,128)(2,1)S(1)}, u32[]{:S(2)}, u32[]{:S(2)}) collective-permute-start(bf16[256,512]{1,0:T(8,128)(2,1)} %get-tuple-element.32), channel_id=1, source_target_pairs={{0,2},{1,3},{2,0},{3,1},{4,6},{5,7},{6,4},{7,5},{8,10},{9,11},{10,... | collective-permute-start | bytes 786440 | tf_op jit(solution)/shard_map/ppermute | solution.py:725
  35.4 22.4 %collective-permute-start.4 = (bf16[256,512]{1,0:T(8,128)(2,1)}, bf16[256,512]{1,0:T(8,128)(2,1)S(1)}, u32[]{:S(2)}, u32[]{:S(2)}) collective-permute-start(bf16[256,512]{1,0:T(8,128)(2,1)} %get-tuple-element.33), channel_id=1, source_target_pairs={{0,3},{1,2},{2,1},{3,0},{4,7},{5,6},{6,5},{7,4},{8,11},{9,10},{10,... | collective-permute-start | bytes 786440 | tf_op jit(solution)/shard_map/ppermute | solution.py:725
  36.8 24.5 %copy-start.7 = (bf16[256,512]{1,0:T(8,128)(2,1)}, bf16[256,512]{1,0:T(8,128)(2,1)S(1)}, u32[]{:S(2)}) copy-start(bf16[256,512]{1,0:T(8,128)(2,1)S(1)} %collective-permute-done.2.refs_2_) | copy-start | bytes 786436
  47.7 13.7 %copy-start.8 = (bf16[256,512]{1,0:T(8,128)(2,1)}, bf16[256,512]{1,0:T(8,128)(2,1)S(1)}, u32[]{:S(2)}) copy-start(bf16[256,512]{1,0:T(8,128)(2,1)S(1)} %collective-permute-done.3.refs_3_) | copy-start | bytes 786436
  57.8 3.6 %copy-start.9 = (bf16[256,512]{1,0:T(8,128)(2,1)}, bf16[256,512]{1,0:T(8,128)(2,1)S(1)}, u32[]{:S(2)}) copy-start(bf16[256,512]{1,0:T(8,128)(2,1)S(1)} %collective-permute-done.4.refs_4_) | copy-start | bytes 786436
  65.6 6.9 %copy-start.5 = (f32[1,3,4,4,4]{4,3,2,1,0:T(4,128)S(1)}, f32[1,3,4,4,4]{4,3,2,1,0:T(4,128)}, u32[]{:S(2)}) copy-start(f32[1,3,4,4,4]{4,3,2,1,0:T(4,128)} %param.9) | copy-start | bytes 2308
  65.6 33.7 %all-to-all-start.1 = ((bf16[16,64,512]{2,1,0:T(8,128)(2,1)}), bf16[16,64,512]{2,1,0:T(8,128)(2,1)}, u32[]{:S(2)}, u32[]{:S(2)}) async-start(bf16[16,64,512]{2,1,0:T(8,128)(2,1)} %bitcast.21), calls=%async_computation.1 | async-start | bytes 2097152 | tf_op jit(solution)/shard_map/all_to_all | solution.py:718
  73.2 8.3 %copy-start.6 = (bf16[2,512,128]{2,1,0:T(8,128)(2,1)S(1)}, bf16[2,512,128]{2,1,0:T(8,128)(2,1)}, u32[]{:S(2)}) copy-start(bf16[2,512,128]{2,1,0:T(8,128)(2,1)} %get-tuple-element.37) | copy-start | bytes 786436
  80.2 19.2 %collective-permute-start.6 = (bf16[512,512]{1,0:T(8,128)(2,1)}, bf16[512,512]{1,0:T(8,128)(2,1)S(1)}, u32[]{:S(2)}, u32[]{:S(2)}) collective-permute-start(bf16[512,512]{1,0:T(8,128)(2,1)} %get-tuple-element.38), channel_id=1, source_target_pairs={{0,16},{16,0},{1,17},{17,1},{2,18},{18,2},{3,19},{19,3},{4,20},{20... | collective-permute-start | bytes 1572872 | tf_op jit(solution)/shard_map/ppermute | solution.py:683
  81.5 17.9 %collective-permute-start.5 = (bf16[2,512,128]{2,1,0:T(8,128)(2,1)S(1)}, bf16[2,512,128]{2,1,0:T(8,128)(2,1)}, u32[]{:S(2)}, u32[]{:S(2)}) collective-permute-start(bf16[2,512,128]{2,1,0:T(8,128)(2,1)S(1)} %copy-done.6), channel_id=1, source_target_pairs={{0,16},{16,0},{1,17},{17,1},{2,18},{18,2},{3,19},{19,3},{4,20},{20... | collective-permute-start | bytes 786440 | tf_op jit(solution)/shard_map/ppermute | solution.py:683
  99.3 0.8 copy-start.2
  107.7 8.3 %copy-start.1 = (bf16[3,128,512]{2,1,0:T(8,128)(2,1)S(1)}, bf16[3,128,512]{2,1,0:T(8,128)(2,1)}, u32[]{:S(2)}) copy-start(bf16[3,128,512]{2,1,0:T(8,128)(2,1)} %get-tuple-element.42.refs_2_.d_hbm) | copy-start | bytes 1179652
  107.7 43.3 %all-to-all-start.3 = ((bf16[16,24,2048]{2,1,0:T(8,128)(2,1)}), bf16[16,24,2048]{2,1,0:T(8,128)(2,1)}, u32[]{:S(2)}, u32[]{:S(2)}) async-start(bf16[16,24,2048]{2,1,0:T(8,128)(2,1)} %bitcast.20), calls=%async_computation.3 | async-start | bytes 3145728 | tf_op jit(solution)/shard_map/all_to_all | solution.py:718
  114.7 23.1 %collective-permute-start.7 = (bf16[512,512]{1,0:T(8,128)(2,1)}, bf16[512,512]{1,0:T(8,128)(2,1)S(1)}, u32[]{:S(2)}, u32[]{:S(2)}) collective-permute-start(bf16[512,512]{1,0:T(8,128)(2,1)} %get-tuple-element.43), channel_id=1, source_target_pairs={{0,16},{16,0},{1,17},{17,1},{2,18},{18,2},{3,19},{19,3},{4,20},{20... | collective-permute-start | bytes 1572872 | tf_op jit(solution)/shard_map/ppermute | solution.py:683
  116.0 21.8 %collective-permute-start.8 = (bf16[3,128,512]{2,1,0:T(8,128)(2,1)S(1)}, bf16[3,128,512]{2,1,0:T(8,128)(2,1)}, u32[]{:S(2)}, u32[]{:S(2)}) collective-permute-start(bf16[3,128,512]{2,1,0:T(8,128)(2,1)S(1)} %copy-done.1), channel_id=1, source_target_pairs={{0,16},{16,0},{1,17},{17,1},{2,18},{18,2},{3,19},{19,3},{4,20},{20... | collective-permute-start | bytes 1179656 | tf_op jit(solution)/shard_map/ppermute | solution.py:683
  118.1 6.3 %copy-start.4 = (f32[128,128]{1,0:T(8,128)S(1)}, f32[128,128]{1,0:T(8,128)}, u32[]{:S(2)}) copy-start(f32[128,128]{1,0:T(8,128)} %get-tuple-element.47) | copy-start | bytes 196612
  123.2 14.0 %collective-permute-start.9 = (f32[1,3,4,4,4]{4,3,2,1,0:T(4,128)S(1)}, f32[1,3,4,4,4]{4,3,2,1,0:T(4,128)S(1)}, u32[]{:S(2)}, u32[]{:S(2)}) collective-permute-start(f32[1,3,4,4,4]{4,3,2,1,0:T(4,128)S(1)} %reshape.51), channel_id=1, source_target_pairs={{0,16},{16,0},{1,17},{17,1},{2,18},{18,2},{3,19},{19,3},{4,20},{20... | collective-permute-start | bytes 2312 | tf_op jit(solution)/shard_map/ppermute | solution.py:683
  137.8 0.8 copy-start.3

commit v17 on v16

--- a/solution.py
+++ b/solution.py
@@ -689,7 +689,7 @@
     halves = [list(range(h, h + half)) for h in range(0, peers, half)]
     if swap:
         flat_factors = factors[0].reshape(weights * count, depth_own, cols)
-        cuts = [across(x) for x in cut_factors(flat_factors, 10)]
+        cuts = [across(x) for x in cut_factors(flat_factors, 2 * count)]
         factor_parts = [factors[0]] + cuts
         sides = 2
     else:

time: 155 us -> 150 us (0.968)
  starting transfers between devices: 28.9 us -> 26.1 us
  waiting for transfers between devices: 59 us -> 56.2 us
    ppermute x6, waiting for transfers between devices: 32.5 us -> 15.7 us  [across(): return lax.ppermute(array, 'seq', pair)]
    all_to_all x3, waiting for transfers between devices: 5.53 us -> 19.9 us  [to_peers(): lax.all_to_all(array, 'exp', split_axis=0, concat_axis=0, tiled=True)]
    all_to_all x3, starting transfers between devices: 20.6 us -> 17.9 us  [to_peers(): lax.all_to_all(array, 'exp', split_axis=0, concat_axis=0, tiled=True)]
  transfers between devices with their start and end apart: 13 -> 13, of which waited for: 6 -> 7; matrix products, arithmetic and copies ran while one was open for 2% -> 3% of each run, Pallas kernels for 18% -> 19%
where the time goes in v17:
time: 150 us; the launch traced here: 149 us
  waiting for transfers between devices  56.2 us (37%)
  Pallas kernels  43.7 us (29%)
  starting transfers between devices  26.1 us (17%)
  blocking collectives  15.3 us (10%)
  local copies, waits for them, and re-layouts  3.98 us (3%)
  other arithmetic  2.99 us (2%)
    pallas_call x11, Pallas kernels, call(): pl.pallas_call(body, out_shape=[x for x, _ in outs], in_specs=[place for...  43.7 us
    ppermute x3, waiting for transfers between devices, shards(): lax.ppermute(shares[k], 'exp', [(n, n ^ k) for n in range(peers)])  20.6 us
    all_to_all x3, waiting for transfers between devices, to_peers(): lax.all_to_all(array, 'exp', split_axis=0, concat_axis=0, tiled=True)  19.9 us
    all_to_all x3, starting transfers between devices, to_peers(): lax.all_to_all(array, 'exp', split_axis=0, concat_axis=0, tiled=True)  17.9 us
    ppermute x6, waiting for transfers between devices, across(): return lax.ppermute(array, 'seq', pair)  15.7 us
    all_to_all x1, blocking collectives, shards(): lax.all_to_all(told, 'exp', split_axis=0, concat_axis=0, tiled=True)  15.3 us
    ppermute x6, starting transfers between devices, across(): return lax.ppermute(array, 'seq', pair)  5.61 us
    unnamed x18, local copies, waits for them, and re-layouts  3.1 us
  transfers between devices with their start and end apart: 13, of which 7 were waited for; matrix products, arithmetic and copies ran while one was open for 3% of the time, Pallas kernels for 19%

profile of v17, /device:TPU:13, one launch (start us, length us, event | category | flops | bytes accessed | tf_op | source)
XLA Modules:
  0.0 149.2 jit_solution(4675130407331611797)
XLA Ops:
  0.6 1.9 %wanted_rows.1 = (s32[32,128]{1,0:T(8,128)}, s32[1,128]{1,0:T(1,128)}, bf16[128,2048]{1,0:T(8,128)(2,1)}) custom-call(s32[1]{0:T(128)} %bitcast.me_ref, s32[2,64]{1,0:T(2,128)} %bitcast.26, bf16[128,4096]{1,0:T(8,128)(2,1)} %source_ref.2), custom_call_target="tpu_custom_call" | custom-call | flops 1048576 | bytes 1590276 | tf_op jit(solution)/shard_map/wanted_rows/pallas_call | solution.py:40
  2.8 15.3 %all_to_all.26 = s32[16,2,128]{2,1,0:T(2,128)} all-to-all(s32[16,2,128]{2,1,0:T(2,128)} %bitcast.25), channel_id=1, replica_groups=mesh['seq'=2,'exp'=16] {'exp'}, dimensions={0} | all-to-all | bytes 32768 | tf_op jit(solution)/shard_map/all_to_all | solution.py:714
  18.8 2.9 %pick_tokens.1 = bf16[384,2048]{1,0:T(8,128)(2,1)} custom-call(s32[32,128]{1,0:T(8,128)} %bitcast.22, bf16[128,4096]{1,0:T(8,128)(2,1)} %source_ref.3, bf16[128,2048]{1,0:T(8,128)(2,1)} %copy-done), custom_call_target="tpu_custom_call" | custom-call | flops 402653184 | bytes 3162112 | tf_op jit(solution)/shard_map/pick_tokens/pallas_call | solution.py:40
  21.8 6.7 %all-to-all-start.2 = ((bf16[16,24,2048]{2,1,0:T(8,128)(2,1)}), bf16[16,24,2048]{2,1,0:T(8,128)(2,1)}, u32[]{:S(2)}, u32[]{:S(2)}) async-start(bf16[16,24,2048]{2,1,0:T(8,128)(2,1)} %bitcast.15), calls=%async_computation.2 | async-start | bytes 3145728 | tf_op jit(solution)/shard_map/all_to_all | solution.py:718
  28.4 2.4 %cut_factors.1 = (bf16[8,512,128]{2,1,0:T(8,128)(2,1)}, bf16[4,512,128]{2,1,0:T(8,128)(2,1)}) custom-call(bf16[12,512,128]{2,1,0:T(8,128)(2,1)} %bitcast.16), custom_call_target="tpu_custom_call" | custom-call | bytes 3145728 | tf_op jit(solution)/shard_map/cut_factors/pallas_call | solution.py:40
  30.8 1.3 collective-permute-start
  32.1 2.1 %plane_columns.1 = (bf16[256,512]{1,0:T(8,128)(2,1)}, bf16[256,512]{1,0:T(8,128)(2,1)}, bf16[256,512]{1,0:T(8,128)(2,1)}, bf16[256,512]{1,0:T(8,128)(2,1)}) custom-call(s32[1]{0:T(128)} %bitcast.me_ref, bf16[128,4096]{1,0:T(8,128)(2,1)} %source_ref.2, bf16[128,2048]{1,0:T(8,128)(2,1)} %copy-done), custom_call_target="tpu_custom_call" | custom-call | bytes 2621444 | tf_op jit(solution)/shard_map/plane_columns/pallas_call | solution.py:40
  35.2 1.4 collective-permute-start.4
  36.6 10.8 %collective-permute-done.3.refs_3_ = bf16[256,512]{1,0:T(8,128)(2,1)S(1)} collective-permute-done((bf16[256,512]{1,0:T(8,128)(2,1)}, bf16[256,512]{1,0:T(8,128)(2,1)S(1)}, u32[]{:S(2)}, u32[]{:S(2)}) %collective-permute-start.3) | collective-permute-done | bytes 262176 | tf_op jit(solution)/shard_map/ppermute | solution.py:725
  47.5 9.8 %collective-permute-done.4.refs_4_ = bf16[256,512]{1,0:T(8,128)(2,1)S(1)} collective-permute-done((bf16[256,512]{1,0:T(8,128)(2,1)}, bf16[256,512]{1,0:T(8,128)(2,1)S(1)}, u32[]{:S(2)}, u32[]{:S(2)}) %collective-permute-start.4) | collective-permute-done | bytes 262176 | tf_op jit(solution)/shard_map/ppermute | solution.py:725
  57.9 4.2 %pick_cotangent.1 = bf16[1024,512]{1,0:T(8,128)(2,1)} custom-call(s32[1]{0:T(128)} %bitcast.me_ref, s32[32,128]{1,0:T(8,128)} %bitcast.23, bf16[8,512,128]{2,1,0:T(8,128)(2,1)} %collective-permute-done.refs_0_.refs_1_, bf16[256,512]{1,0:T(8,128)(2,1)} %get-tuple-element.30.refs_1_, bf16[256,512]{1,0:T(8,128)(2,1)} %copy-done.6, bf16[256,512]{1,0:T(8,128)(2,1)} %copy-done.7, ...), custom_call_target="tpu_custom_call" | custom-call | flops 1073741824 | bytes 3162116 | tf_op jit(solution)/shard_map/pick_cotangent/pallas_call | solution.py:40
  62.2 2.6 %all-to-all-done.2 = bf16[16,24,2048]{2,1,0:T(8,128)(2,1)} async-done(((bf16[16,24,2048]{2,1,0:T(8,128)(2,1)}), bf16[16,24,2048]{2,1,0:T(8,128)(2,1)}, u32[]{:S(2)}, u32[]{:S(2)}) %all-to-all-start.2) | async-done | bytes 1572896 | tf_op jit(solution)/shard_map/all_to_all | solution.py:718
  64.8 4.8 %all-to-all-start.1 = ((bf16[16,64,512]{2,1,0:T(8,128)(2,1)}), bf16[16,64,512]{2,1,0:T(8,128)(2,1)}, u32[]{:S(2)}, u32[]{:S(2)}) async-start(bf16[16,64,512]{2,1,0:T(8,128)(2,1)} %bitcast.21), calls=%async_computation.1 | async-start | bytes 2097152 | tf_op jit(solution)/shard_map/all_to_all | solution.py:718
  71.5 6.9 %forward.1 = (bf16[512,512]{1,0:T(8,128)(2,1)}, bf16[512,512]{1,0:T(8,128)(2,1)}, f32[512,512]{1,0:T(8,128)}, f32[512,512]{1,0:T(8,128)}, f32[128,512]{1,0:T(8,1...) custom-call(s32[1]{0:T(128)} %bitcast.4.order_ref, f32[192]{0:T(256)} %reshape.44.mix_ref, ...), custom_call_target="tpu_custom_call" | custom-call | flops 1073741824 | bytes 8127748 | tf_op jit(solution)/shard_map/forward/pallas_call | solution.py:40
  78.8 4.3 %collective-permute-done.5.refs_2_ = bf16[4,512,128]{2,1,0:T(8,128)(2,1)} collective-permute-done((bf16[4,512,128]{2,1,0:T(8,128)(2,1)}, bf16[4,512,128]{2,1,0:T(8,128)(2,1)}, u32[]{:S(2)}, u32[]{:S(2)}) %collective-permute-start.5) | collective-permute-done | bytes 524320 | tf_op jit(solution)/shard_map/ppermute | solution.py:683
  83.1 11.7 %all-to-all-done.1 = bf16[16,64,512]{2,1,0:T(8,128)(2,1)} async-done(((bf16[16,64,512]{2,1,0:T(8,128)(2,1)}), bf16[16,64,512]{2,1,0:T(8,128)(2,1)}, u32[]{:S(2)}, u32[]{:S(2)}) %all-to-all-start.1) | async-done | bytes 1048608 | tf_op jit(solution)/shard_map/all_to_all | solution.py:718
  95.6 7.6 %backward.1 = (bf16[384,2048]{1,0:T(8,128)(2,1)}, bf16[512,512]{1,0:T(8,128)(2,1)}, bf16[512,512]{1,0:T(8,128)(2,1)}, f32[512,512]{1,0:T(8,128)}, bf16[3,128,512]{2,1,0:T(8,128)(2,1)}, /*index=5*/f32[128,128]{1,0:T(8,128)}) custom-call(s32[1]{0:T(128)} %bitcast.4.order_ref, f32[192]{0:T(256)} %reshape.44.mix_ref, ...), custom_call_target="tpu_custom_call" | custom-call | flops 1610612736 | bytes 9635588 | tf_op jit(solution)/shard_map/backward/pallas_call | solution.py:40
  103.2 6.4 %all-to-all-start.3 = ((bf16[16,24,2048]{2,1,0:T(8,128)(2,1)}), bf16[16,24,2048]{2,1,0:T(8,128)(2,1)}, u32[]{:S(2)}, u32[]{:S(2)}) async-start(bf16[16,24,2048]{2,1,0:T(8,128)(2,1)} %bitcast.20), calls=%async_computation.3 | async-start | bytes 3145728 | tf_op jit(solution)/shard_map/all_to_all | solution.py:718
  111.2 1.8 %place_rows.1.placed_hbm = bf16[256,384]{1,0:T(8,128)(2,1)} custom-call(s32[1]{0:T(128)} %bitcast.me_ref, s32[32,128]{1,0:T(8,128)} %bitcast.24), custom_call_target="tpu_custom_call" | custom-call | flops 1048576 | bytes 212996 | tf_op jit(solution)/shard_map/place_rows/pallas_call | solution.py:40
  113.0 3.9 %mix_partials.1 = f32[192,128]{1,0:T(8,128)} custom-call(f32[512,512]{1,0:T(8,128)} %get-tuple-element.44.yg_hbm, f32[512,512]{1,0:T(8,128)} %get-tuple-element.45.yu_hbm, f32[512,512]{1,0:T(8,128)} %get-tuple-element.46.yd_hbm, bf16[3,128,512]{2,1,0:T(8,128)(2,1)} %get-tuple-element.42.refs_2_.d_hbm), custom_call_target="tpu_custom_call" | custom-call | flops 6291456 | bytes 3637248 | tf_op jit(solution)/shard_map/mix_partials/pallas_call | solution.py:40
  120.8 11.4 %collective-permute-done.9 = f32[1,3,4,4,4]{4,3,2,1,0:T(4,128)S(1)} collective-permute-done((f32[1,3,4,4,4]{4,3,2,1,0:T(4,128)S(1)}, f32[1,3,4,4,4]{4,3,2,1,0:T(4,128)S(1)}, u32[]{:S(2)}, u32[]{:S(2)}) %collective-permute-start.9) | collective-permute-done | bytes 800 | tf_op jit(solution)/shard_map/ppermute | solution.py:683
  133.5 6.9 %factor_grad.1 = f32[3,4,512,128]{3,2,1,0:T(8,128)} custom-call(f32[192]{0:T(256)} %reshape.44.mix_ref, bf16[512,512]{1,0:T(8,128)(2,1)} %get-tuple-element.40.refs_0_, bf16[512,512]{1,0:T(8,128)(2,1)} %get-tuple-element.41.refs_1_, bf16[3,128,512]{2,1,0:T(8,128)(2,1)} %get-tuple-element.42.refs_2_.d_hbm, bf16[512,512]{1,0:T(8,128)(2,1)} %copy-done.2, ...), custom_call_target="tpu_custom_call" | custom-call | flops 1610612736 | bytes 6030080 | tf_op jit(solution)/shard_map/factor_grad/pallas_call | solution.py:40
  140.4 5.5 %all-to-all-done.3 = bf16[16,24,2048]{2,1,0:T(8,128)(2,1)} async-done(((bf16[16,24,2048]{2,1,0:T(8,128)(2,1)}), bf16[16,24,2048]{2,1,0:T(8,128)(2,1)}, u32[]{:S(2)}, u32[]{:S(2)}) %all-to-all-start.3) | async-done | bytes 1572896 | tf_op jit(solution)/shard_map/all_to_all | solution.py:718
  145.9 3.1 %sum_rows.1 = bf16[128,4096]{1,0:T(8,128)(2,1)} custom-call(bf16[256,384]{1,0:T(8,128)(2,1)} %place_rows.1.placed_hbm, bf16[384,2048]{1,0:T(8,128)(2,1)} %bitcast.13.returned_ref), custom_call_target="tpu_custom_call" | custom-call | flops 402653184 | bytes 2818048 | tf_op jit(solution)/shard_map/sum_rows/pallas_call | solution.py:40
  (39 shorter events, 12.5 us)
Async XLA Ops:
  2.5 15.5 %collective-permute-start.1 = (bf16[128,2048]{1,0:T(8,128)(2,1)}, bf16[128,2048]{1,0:T(8,128)(2,1)S(1)}, u32[]{:S(2)}, u32[]{:S(2)}) collective-permute-start(bf16[128,2048]{1,0:T(8,128)(2,1)} %get-tuple-element.29), channel_id=1, source_target_pairs={{0,4},{1,5},{2,6},{3,7},{4,0},{5,1},{6,2},{7,3},{8,12},{9,13},{10,... | collective-permute-start | bytes 1572872 | tf_op jit(solution)/shard_map/ppermute | solution.py:713
  18.0 0.8 copy-start
  21.8 43.1 %all-to-all-start.2 = ((bf16[16,24,2048]{2,1,0:T(8,128)(2,1)}), bf16[16,24,2048]{2,1,0:T(8,128)(2,1)}, u32[]{:S(2)}, u32[]{:S(2)}) async-start(bf16[16,24,2048]{2,1,0:T(8,128)(2,1)} %bitcast.15), calls=%async_computation.2 | async-start | bytes 3145728 | tf_op jit(solution)/shard_map/all_to_all | solution.py:718
  30.8 26.4 %collective-permute-start = (bf16[8,512,128]{2,1,0:T(8,128)(2,1)}, bf16[8,512,128]{2,1,0:T(8,128)(2,1)}, u32[]{:S(2)}, u32[]{:S(2)}) collective-permute-start(bf16[8,512,128]{2,1,0:T(8,128)(2,1)} %get-tuple-element.28), channel_id=1, source_target_pairs={{0,16},{16,0},{1,17},{17,1},{2,18},{18,2},{3,19},{19,3},{4,20},{20... | collective-permute-start | bytes 3145736 | tf_op jit(solution)/shard_map/ppermute | solution.py:683
  34.2 2.4 %collective-permute-start.2 = (bf16[256,512]{1,0:T(8,128)(2,1)}, bf16[256,512]{1,0:T(8,128)(2,1)S(1)}, u32[]{:S(2)}, u32[]{:S(2)}) collective-permute-start(bf16[256,512]{1,0:T(8,128)(2,1)} %get-tuple-element.31), channel_id=1, source_target_pairs={{0,1},{1,0},{2,3},{3,2},{4,5},{5,4},{6,7},{7,6},{8,9},{9,8},{10,11... | collective-permute-start | bytes 786440 | tf_op jit(solution)/shard_map/ppermute | solution.py:725
  34.9 12.5 %collective-permute-start.3 = (bf16[256,512]{1,0:T(8,128)(2,1)}, bf16[256,512]{1,0:T(8,128)(2,1)S(1)}, u32[]{:S(2)}, u32[]{:S(2)}) collective-permute-start(bf16[256,512]{1,0:T(8,128)(2,1)} %get-tuple-element.32), channel_id=1, source_target_pairs={{0,2},{1,3},{2,0},{3,1},{4,6},{5,7},{6,4},{7,5},{8,10},{9,11},{10,... | collective-permute-start | bytes 786440 | tf_op jit(solution)/shard_map/ppermute | solution.py:725
  35.2 22.0 %collective-permute-start.4 = (bf16[256,512]{1,0:T(8,128)(2,1)}, bf16[256,512]{1,0:T(8,128)(2,1)S(1)}, u32[]{:S(2)}, u32[]{:S(2)}) collective-permute-start(bf16[256,512]{1,0:T(8,128)(2,1)} %get-tuple-element.33), channel_id=1, source_target_pairs={{0,3},{1,2},{2,1},{3,0},{4,7},{5,6},{6,5},{7,4},{8,11},{9,10},{10,... | collective-permute-start | bytes 786440 | tf_op jit(solution)/shard_map/ppermute | solution.py:725
  36.6 20.6 %copy-start.6 = (bf16[256,512]{1,0:T(8,128)(2,1)}, bf16[256,512]{1,0:T(8,128)(2,1)S(1)}, u32[]{:S(2)}) copy-start(bf16[256,512]{1,0:T(8,128)(2,1)S(1)} %collective-permute-done.2.refs_2_) | copy-start | bytes 786436
  47.5 9.8 %copy-start.7 = (bf16[256,512]{1,0:T(8,128)(2,1)}, bf16[256,512]{1,0:T(8,128)(2,1)S(1)}, u32[]{:S(2)}) copy-start(bf16[256,512]{1,0:T(8,128)(2,1)S(1)} %collective-permute-done.3.refs_3_) | copy-start | bytes 786436
  57.2 0.7 copy-start.8
  62.2 8.7 %copy-start.5 = (f32[1,3,4,4,4]{4,3,2,1,0:T(4,128)S(1)}, f32[1,3,4,4,4]{4,3,2,1,0:T(4,128)}, u32[]{:S(2)}) copy-start(f32[1,3,4,4,4]{4,3,2,1,0:T(4,128)} %param.9) | copy-start | bytes 2308
  64.8 30.0 %all-to-all-start.1 = ((bf16[16,64,512]{2,1,0:T(8,128)(2,1)}), bf16[16,64,512]{2,1,0:T(8,128)(2,1)}, u32[]{:S(2)}, u32[]{:S(2)}) async-start(bf16[16,64,512]{2,1,0:T(8,128)(2,1)} %bitcast.21), calls=%async_computation.1 | async-start | bytes 2097152 | tf_op jit(solution)/shard_map/all_to_all | solution.py:718
  69.6 13.5 %collective-permute-start.5 = (bf16[4,512,128]{2,1,0:T(8,128)(2,1)}, bf16[4,512,128]{2,1,0:T(8,128)(2,1)}, u32[]{:S(2)}, u32[]{:S(2)}) collective-permute-start(bf16[4,512,128]{2,1,0:T(8,128)(2,1)} %get-tuple-element.37), channel_id=1, source_target_pairs={{0,16},{16,0},{1,17},{17,1},{2,18},{18,2},{3,19},{19,3},{4,20},{20... | collective-permute-start | bytes 1572872 | tf_op jit(solution)/shard_map/ppermute | solution.py:683
  78.4 16.4 %collective-permute-start.6 = (bf16[512,512]{1,0:T(8,128)(2,1)}, bf16[512,512]{1,0:T(8,128)(2,1)S(1)}, u32[]{:S(2)}, u32[]{:S(2)}) collective-permute-start(bf16[512,512]{1,0:T(8,128)(2,1)} %get-tuple-element.38), channel_id=1, source_target_pairs={{0,16},{16,0},{1,17},{17,1},{2,18},{18,2},{3,19},{19,3},{4,20},{20... | collective-permute-start | bytes 1572872 | tf_op jit(solution)/shard_map/ppermute | solution.py:683
  94.8 0.8 copy-start.2
  103.2 7.7 %copy-start.1 = (bf16[3,128,512]{2,1,0:T(8,128)(2,1)S(1)}, bf16[3,128,512]{2,1,0:T(8,128)(2,1)}, u32[]{:S(2)}) copy-start(bf16[3,128,512]{2,1,0:T(8,128)(2,1)} %get-tuple-element.42.refs_2_.d_hbm) | copy-start | bytes 1179652
  103.2 42.7 %all-to-all-start.3 = ((bf16[16,24,2048]{2,1,0:T(8,128)(2,1)}), bf16[16,24,2048]{2,1,0:T(8,128)(2,1)}, u32[]{:S(2)}, u32[]{:S(2)}) async-start(bf16[16,24,2048]{2,1,0:T(8,128)(2,1)} %bitcast.20), calls=%async_computation.3 | async-start | bytes 3145728 | tf_op jit(solution)/shard_map/all_to_all | solution.py:718
  109.6 23.1 %collective-permute-start.7 = (bf16[512,512]{1,0:T(8,128)(2,1)}, bf16[512,512]{1,0:T(8,128)(2,1)S(1)}, u32[]{:S(2)}, u32[]{:S(2)}) collective-permute-start(bf16[512,512]{1,0:T(8,128)(2,1)} %get-tuple-element.43), channel_id=1, source_target_pairs={{0,16},{16,0},{1,17},{17,1},{2,18},{18,2},{3,19},{19,3},{4,20},{20... | collective-permute-start | bytes 1572872 | tf_op jit(solution)/shard_map/ppermute | solution.py:683
  110.9 21.8 %collective-permute-start.8 = (bf16[3,128,512]{2,1,0:T(8,128)(2,1)S(1)}, bf16[3,128,512]{2,1,0:T(8,128)(2,1)}, u32[]{:S(2)}, u32[]{:S(2)}) collective-permute-start(bf16[3,128,512]{2,1,0:T(8,128)(2,1)S(1)} %copy-done.1), channel_id=1, source_target_pairs={{0,16},{16,0},{1,17},{17,1},{2,18},{18,2},{3,19},{19,3},{4,20},{20... | collective-permute-start | bytes 1179656 | tf_op jit(solution)/shard_map/ppermute | solution.py:683
  113.0 6.3 %copy-start.4 = (f32[128,128]{1,0:T(8,128)S(1)}, f32[128,128]{1,0:T(8,128)}, u32[]{:S(2)}) copy-start(f32[128,128]{1,0:T(8,128)} %get-tuple-element.47) | copy-start | bytes 196612
  118.0 14.1 %collective-permute-start.9 = (f32[1,3,4,4,4]{4,3,2,1,0:T(4,128)S(1)}, f32[1,3,4,4,4]{4,3,2,1,0:T(4,128)S(1)}, u32[]{:S(2)}, u32[]{:S(2)}) collective-permute-start(f32[1,3,4,4,4]{4,3,2,1,0:T(4,128)S(1)} %reshape.51), channel_id=1, source_target_pairs={{0,16},{16,0},{1,17},{17,1},{2,18},{18,2},{3,19},{19,3},{4,20},{20... | collective-permute-start | bytes 2312 | tf_op jit(solution)/shard_map/ppermute | solution.py:683
  132.7 0.8 copy-start.3

commit v18 on v17

--- a/solution.py
+++ b/solution.py
@@ -495,22 +495,33 @@
     return [d_ref[at, b * cols : (b + 1) * cols].astype(F32) for b in range(NPHM)]
 
 
-def forward_body(
-    cap, pieces, sides, order_ref, mix_ref, slot_ref, got_hbm, *refs
-):
+def order_body(cap, pieces, order_ref, slot_hbm, got_hbm, *refs):
+    x_outs, (got_ref, x_ref, slot_ref, got_sem, out_sem) = refs[:-5], refs[-5:]
+    small = begin(slot_hbm, slot_ref, got_sem.at[got_sem.shape[0] - 1])
+    loads = load_slots(got_hbm, got_ref, got_sem)
+    small.wait()
+    place = place_matrix(cap, pieces, got_ref.shape[0], slot_ref[...])
+    stack_rows(pieces, place, loads, got_ref, x_ref)
+    wait_all(store_parts(order_ref, x_ref, x_outs, out_sem))
+
+
+def forward_body(sides, order_ref, mix_ref, *refs):
+    x_parts, refs = refs[:sides], refs[sides:]
     held = 2 if sides > 1 else 1
     parts, refs = refs[:held], refs[held:]
-    x_outs, refs = refs[:sides], refs[sides:]
     yg_hbm, yu_hbm, act_hbm, slope_hbm, hid_hbm = refs[:5]
-    got_ref, side_ref, x_ref, yg_ref, yu_ref, act_ref, slope_ref, hid_ref = refs[5:13]
-    got_sem, side_sem, out_sem = refs[13:]
-    loads = load_slots(got_hbm, got_ref, got_sem)
+    side_ref, x_ref, yg_ref, yu_ref, act_ref, slope_ref, hid_ref = refs[5:12]
+    x_sem, side_sem, out_sem = refs[12:]
+    loads = []
+    for n, part in enumerate(x_parts):
+        size = part.shape[1]
+        start = pl.multiple_of((order_ref[0] ^ n) * size if sides > 1 else 0, size)
+        loads.append(begin(part, x_ref.at[:, pl.ds(start, size)], x_sem.at[n]))
     sides_in = [
         load_factor(order_ref, parts, m, side_ref.at[m], side_sem.at[m]) for m in range(2)
     ]
-    place = place_matrix(cap, pieces, got_ref.shape[0], slot_ref[...])
-    stack_rows(pieces, place, loads, got_ref, x_ref)
-    stores = store_parts(order_ref, x_ref, x_outs, out_sem)
+    wait_all(loads)
+    stores = []
     wait_all(sides_in[0])
     yg_ref[...] = dot(x_ref[...], side_ref[0])
     stores.append(begin(yg_ref, yg_hbm, out_sem.at[2]))
@@ -746,17 +757,25 @@
     mixed_scratch = scratch_like((stacked, hidden), F32)
     low_scratch = scratch_like((stacked, hidden), BF16)
     flat_scratch = scratch_like((rows, hidden), F32)
-    outs = call(
-        functools.partial(forward_body, cap, pieces, sides),
-        split + [mixed, mixed, flat, flat, flat],
-        [(group, SMEM), (mixing, SMEM), (slot, VMEM), (got_rows, HBM)] + sides_in[:2],
+    x_parts = call(
+        functools.partial(order_body, cap, pieces),
+        split,
+        [(group, SMEM), (slot, HBM), (got_rows, HBM)],
+        "order_rows",
+        product // 4,
+        [back_scratch, stack_scratch, scratch_like(slot.shape, jnp.int32)]
+        + [dma((steps + 1,)), dma((2,))],
+    )
+    y_gate, y_up, act, slope, hid = call(
+        functools.partial(forward_body, sides),
+        [mixed, mixed, flat, flat, flat],
+        [(group, SMEM), (mixing, SMEM)] + [(x, HBM) for x in x_parts] + sides_in[:2],
         "forward",
         2 * product,
-        [back_scratch, scratch_like((2, depth, hidden), BF16), stack_scratch, mixed_scratch, mixed_scratch]
+        [scratch_like((2, depth, hidden), BF16), stack_scratch, mixed_scratch, mixed_scratch]
         + [flat_scratch] * 3
-        + [dma((steps,)), dma((2, sides, count)), dma((7,))],
+        + [dma((2,)), dma((2, sides, count)), dma((7,))],
     )
-    x_parts, (y_gate, y_up, act, slope, hid) = outs[:sides], outs[sides:]
     x_rows = [x_parts[0]] + [across(x) for x in x_parts[1:]]
     after = x_rows[1:]
     outs = call(

time: 150 us -> 150 us (level)
  waiting for transfers between devices: 56.2 us -> 53.7 us
  Pallas kernels: 43.7 us -> 46.1 us
    ppermute x6, waiting for transfers between devices: 15.7 us -> 13.3 us  [across(): return lax.ppermute(array, 'seq', pair)]
    pallas_call x11 -> x12, Pallas kernels: 43.7 us -> 46.1 us  [call(): pl.pallas_call(body, out_shape=[x for x, _ in outs], in_specs=[place for...]
  transfers between devices with their start and end apart: 13 -> 13, of which waited for: 7 -> 7; matrix products, arithmetic and copies ran while one was open for 3% -> 3% of each run, Pallas kernels for 19% -> 21%
where the time goes in v18:
time: 150 us; the launch traced here: 149 us
  waiting for transfers between devices  53.7 us (36%)
  Pallas kernels  46.1 us (31%)
  starting transfers between devices  26.3 us (18%)
  blocking collectives  15.3 us (10%)
  local copies, waits for them, and re-layouts  3.96 us (3%)
  other arithmetic  2.99 us (2%)
    pallas_call x12, Pallas kernels, call(): pl.pallas_call(body, out_shape=[x for x, _ in outs], in_specs=[place for...  46.1 us
    ppermute x3, waiting for transfers between devices, shards(): lax.ppermute(shares[k], 'exp', [(n, n ^ k) for n in range(peers)])  20.6 us
    all_to_all x3, waiting for transfers between devices, to_peers(): lax.all_to_all(array, 'exp', split_axis=0, concat_axis=0, tiled=True)  19.9 us
    all_to_all x3, starting transfers between devices, to_peers(): lax.all_to_all(array, 'exp', split_axis=0, concat_axis=0, tiled=True)  18 us
    all_to_all x1, blocking collectives, shards(): lax.all_to_all(told, 'exp', split_axis=0, concat_axis=0, tiled=True)  15.3 us
    ppermute x6, waiting for transfers between devices, across(): return lax.ppermute(array, 'seq', pair)  13.3 us
    ppermute x6, starting transfers between devices, across(): return lax.ppermute(array, 'seq', pair)  5.61 us
    unnamed x18, local copies, waits for them, and re-layouts  3.08 us
  transfers between devices with their start and end apart: 13, of which 7 were waited for; matrix products, arithmetic and copies ran while one was open for 3% of the time, Pallas kernels for 21%

profile of v18, /device:TPU:13, one launch (start us, length us, event | category | flops | bytes accessed | tf_op | source)
XLA Modules:
  0.0 149.2 jit_solution(16061687007356215220)
XLA Ops:
  0.6 1.9 %wanted_rows.1 = (s32[32,128]{1,0:T(8,128)}, s32[1,128]{1,0:T(1,128)}, bf16[128,2048]{1,0:T(8,128)(2,1)}) custom-call(s32[1]{0:T(128)} %bitcast.me_ref, s32[2,64]{1,0:T(2,128)} %bitcast.26, bf16[128,4096]{1,0:T(8,128)(2,1)} %source_ref.2), custom_call_target="tpu_custom_call" | custom-call | flops 1048576 | bytes 1590276 | tf_op jit(solution)/shard_map/wanted_rows/pallas_call | solution.py:40
  2.8 15.3 %all_to_all.26 = s32[16,2,128]{2,1,0:T(2,128)} all-to-all(s32[16,2,128]{2,1,0:T(2,128)} %bitcast.25), channel_id=1, replica_groups=mesh['seq'=2,'exp'=16] {'exp'}, dimensions={0} | all-to-all | bytes 32768 | tf_op jit(solution)/shard_map/all_to_all | solution.py:725
  18.8 2.9 %pick_tokens.1 = bf16[384,2048]{1,0:T(8,128)(2,1)} custom-call(s32[32,128]{1,0:T(8,128)} %bitcast.22, bf16[128,4096]{1,0:T(8,128)(2,1)} %source_ref.3, bf16[128,2048]{1,0:T(8,128)(2,1)} %copy-done), custom_call_target="tpu_custom_call" | custom-call | flops 402653184 | bytes 3162112 | tf_op jit(solution)/shard_map/pick_tokens/pallas_call | solution.py:40
  21.8 6.7 %all-to-all-start.2 = ((bf16[16,24,2048]{2,1,0:T(8,128)(2,1)}), bf16[16,24,2048]{2,1,0:T(8,128)(2,1)}, u32[]{:S(2)}, u32[]{:S(2)}) async-start(bf16[16,24,2048]{2,1,0:T(8,128)(2,1)} %bitcast.15), calls=%async_computation.2 | async-start | bytes 3145728 | tf_op jit(solution)/shard_map/all_to_all | solution.py:729
  28.4 2.4 %cut_factors.1 = (bf16[8,512,128]{2,1,0:T(8,128)(2,1)}, bf16[4,512,128]{2,1,0:T(8,128)(2,1)}) custom-call(bf16[12,512,128]{2,1,0:T(8,128)(2,1)} %bitcast.17), custom_call_target="tpu_custom_call" | custom-call | bytes 3145728 | tf_op jit(solution)/shard_map/cut_factors/pallas_call | solution.py:40
  32.1 2.1 %plane_columns.1 = (bf16[256,512]{1,0:T(8,128)(2,1)}, bf16[256,512]{1,0:T(8,128)(2,1)}, bf16[256,512]{1,0:T(8,128)(2,1)}, bf16[256,512]{1,0:T(8,128)(2,1)}) custom-call(s32[1]{0:T(128)} %bitcast.me_ref, bf16[128,4096]{1,0:T(8,128)(2,1)} %source_ref.2, bf16[128,2048]{1,0:T(8,128)(2,1)} %copy-done), custom_call_target="tpu_custom_call" | custom-call | bytes 2621444 | tf_op jit(solution)/shard_map/plane_columns/pallas_call | solution.py:40
  35.2 1.4 collective-permute-start.4
  36.6 10.8 %collective-permute-done.3.refs_3_ = bf16[256,512]{1,0:T(8,128)(2,1)S(1)} collective-permute-done((bf16[256,512]{1,0:T(8,128)(2,1)}, bf16[256,512]{1,0:T(8,128)(2,1)S(1)}, u32[]{:S(2)}, u32[]{:S(2)}) %collective-permute-start.3) | collective-permute-done | bytes 262176 | tf_op jit(solution)/shard_map/ppermute | solution.py:736
  47.5 9.8 %collective-permute-done.4.refs_4_ = bf16[256,512]{1,0:T(8,128)(2,1)S(1)} collective-permute-done((bf16[256,512]{1,0:T(8,128)(2,1)}, bf16[256,512]{1,0:T(8,128)(2,1)S(1)}, u32[]{:S(2)}, u32[]{:S(2)}) %collective-permute-start.4) | collective-permute-done | bytes 262176 | tf_op jit(solution)/shard_map/ppermute | solution.py:736
  57.9 4.2 %pick_cotangent.1 = bf16[1024,512]{1,0:T(8,128)(2,1)} custom-call(s32[1]{0:T(128)} %bitcast.me_ref, s32[32,128]{1,0:T(8,128)} %bitcast.23, bf16[8,512,128]{2,1,0:T(8,128)(2,1)} %collective-permute-done.refs_0_.refs_3_.refs_1_, bf16[256,512]{1,0:T(8,128)(2,1)} %get-tuple-element.30.refs_1_, bf16[256,512]{1,0:T(8,128)(2,1)} %copy-done.6, ...), custom_call_target="tpu_custom_call" | custom-call | flops 1073741824 | bytes 3162116 | tf_op jit(solution)/shard_map/pick_cotangent/pallas_call | solution.py:40
  62.2 2.6 %all-to-all-done.2 = bf16[16,24,2048]{2,1,0:T(8,128)(2,1)} async-done(((bf16[16,24,2048]{2,1,0:T(8,128)(2,1)}), bf16[16,24,2048]{2,1,0:T(8,128)(2,1)}, u32[]{:S(2)}, u32[]{:S(2)}) %all-to-all-start.2) | async-done | bytes 1572896 | tf_op jit(solution)/shard_map/all_to_all | solution.py:729
  64.8 4.9 %all-to-all-start.1 = ((bf16[16,64,512]{2,1,0:T(8,128)(2,1)}), bf16[16,64,512]{2,1,0:T(8,128)(2,1)}, u32[]{:S(2)}, u32[]{:S(2)}) async-start(bf16[16,64,512]{2,1,0:T(8,128)(2,1)} %bitcast.21), calls=%async_computation.1 | async-start | bytes 2097152 | tf_op jit(solution)/shard_map/all_to_all | solution.py:729
  71.0 3.3 %order_rows.1 = (bf16[512,512]{1,0:T(8,128)(2,1)}, bf16[512,512]{1,0:T(8,128)(2,1)}) custom-call(s32[1]{0:T(128)} %bitcast.4.order_ref, s32[1,128]{1,0:T(1,128)} %get-tuple-element.27.slot_hbm, bf16[384,2048]{1,0:T(8,128)(2,1)} %bitcast.10.got_hbm), custom_call_target="tpu_custom_call" | custom-call | flops 134217728 | bytes 2621956 | tf_op jit(solution)/shard_map/order_rows/pallas_call | solution.py:40
  75.3 6.0 %forward.1 = (f32[512,512]{1,0:T(8,128)}, f32[512,512]{1,0:T(8,128)}, f32[128,512]{1,0:T(8,128)}, f32[128,512]{1,0:T(8,128)}, f32[128,512]{1,0:T(8,128)}) custom-call(s32[1]{0:T(128)} %bitcast.4.order_ref, f32[192]{0:T(256)} %reshape.44.mix_ref, bf16[512,512]{1,0:T(8,128)(2,1)} %get-tuple-element.34.refs_0_, bf16[512,512]{1,0:T(8,128)(2,1)} %get-tuple-element.35.refs_1_, ...), custom_call_target="tpu_custom_call" | custom-call | flops 1073741824 | bytes 6554372 | tf_op jit(solution)/shard_map/forward/pallas_call | solution.py:40
  81.3 1.9 %collective-permute-done.5.refs_2_ = bf16[4,512,128]{2,1,0:T(8,128)(2,1)} collective-permute-done((bf16[4,512,128]{2,1,0:T(8,128)(2,1)}, bf16[4,512,128]{2,1,0:T(8,128)(2,1)}, u32[]{:S(2)}, u32[]{:S(2)}) %collective-permute-start.5) | collective-permute-done | bytes 524320 | tf_op jit(solution)/shard_map/ppermute | solution.py:694
  83.2 11.7 %all-to-all-done.1 = bf16[16,64,512]{2,1,0:T(8,128)(2,1)} async-done(((bf16[16,64,512]{2,1,0:T(8,128)(2,1)}), bf16[16,64,512]{2,1,0:T(8,128)(2,1)}, u32[]{:S(2)}, u32[]{:S(2)}) %all-to-all-start.1) | async-done | bytes 1048608 | tf_op jit(solution)/shard_map/all_to_all | solution.py:729
  95.7 7.5 %backward.1 = (bf16[384,2048]{1,0:T(8,128)(2,1)}, bf16[512,512]{1,0:T(8,128)(2,1)}, bf16[512,512]{1,0:T(8,128)(2,1)}, f32[512,512]{1,0:T(8,128)}, bf16[3,128,512]{2,1,0:T(8,128)(2,1)}, /*index=5*/f32[128,128]{1,0:T(8,128)}) custom-call(s32[1]{0:T(128)} %bitcast.4.order_ref, f32[192]{0:T(256)} %reshape.44.mix_ref, s32[1,128]{1,0:T(1,128)} %get-tuple-element.27.slot_hbm, ...), custom_call_target="tpu_custom_call" | custom-call | flops 1610612736 | bytes 9635588 | tf_op jit(solution)/shard_map/backward/pallas_call | solution.py:40
  103.3 6.4 %all-to-all-start.3 = ((bf16[16,24,2048]{2,1,0:T(8,128)(2,1)}), bf16[16,24,2048]{2,1,0:T(8,128)(2,1)}, u32[]{:S(2)}, u32[]{:S(2)}) async-start(bf16[16,24,2048]{2,1,0:T(8,128)(2,1)} %bitcast.20), calls=%async_computation.3 | async-start | bytes 3145728 | tf_op jit(solution)/shard_map/all_to_all | solution.py:729
  111.2 1.8 %place_rows.1.placed_hbm = bf16[256,384]{1,0:T(8,128)(2,1)} custom-call(s32[1]{0:T(128)} %bitcast.me_ref, s32[32,128]{1,0:T(8,128)} %bitcast.24), custom_call_target="tpu_custom_call" | custom-call | flops 1048576 | bytes 212996 | tf_op jit(solution)/shard_map/place_rows/pallas_call | solution.py:40
  113.1 3.9 %mix_partials.1 = f32[192,128]{1,0:T(8,128)} custom-call(f32[512,512]{1,0:T(8,128)} %get-tuple-element.44.yg_hbm, f32[512,512]{1,0:T(8,128)} %get-tuple-element.45.yu_hbm, f32[512,512]{1,0:T(8,128)} %get-tuple-element.46.yd_hbm, bf16[3,128,512]{2,1,0:T(8,128)(2,1)} %get-tuple-element.42.refs_2_.d_hbm), custom_call_target="tpu_custom_call" | custom-call | flops 6291456 | bytes 3637248 | tf_op jit(solution)/shard_map/mix_partials/pallas_call | solution.py:40
  120.8 11.3 %collective-permute-done.9 = f32[1,3,4,4,4]{4,3,2,1,0:T(4,128)S(1)} collective-permute-done((f32[1,3,4,4,4]{4,3,2,1,0:T(4,128)S(1)}, f32[1,3,4,4,4]{4,3,2,1,0:T(4,128)S(1)}, u32[]{:S(2)}, u32[]{:S(2)}) %collective-permute-start.9) | collective-permute-done | bytes 800 | tf_op jit(solution)/shard_map/ppermute | solution.py:694
  133.6 6.9 %factor_grad.1 = f32[3,4,512,128]{3,2,1,0:T(8,128)} custom-call(f32[192]{0:T(256)} %reshape.44.mix_ref, bf16[512,512]{1,0:T(8,128)(2,1)} %get-tuple-element.34.refs_0_, bf16[512,512]{1,0:T(8,128)(2,1)} %get-tuple-element.41.refs_1_, bf16[3,128,512]{2,1,0:T(8,128)(2,1)} %get-tuple-element.42.refs_2_.d_hbm, bf16[512,512]{1,0:T(8,128)(2,1)} %copy-done.2, ...), custom_call_target="tpu_custom_call" | custom-call | flops 1610612736 | bytes 6030080 | tf_op jit(solution)/shard_map/factor_grad/pallas_call | solution.py:40
  140.4 5.5 %all-to-all-done.3 = bf16[16,24,2048]{2,1,0:T(8,128)(2,1)} async-done(((bf16[16,24,2048]{2,1,0:T(8,128)(2,1)}), bf16[16,24,2048]{2,1,0:T(8,128)(2,1)}, u32[]{:S(2)}, u32[]{:S(2)}) %all-to-all-start.3) | async-done | bytes 1572896 | tf_op jit(solution)/shard_map/all_to_all | solution.py:729
  146.0 3.1 %sum_rows.1 = bf16[128,4096]{1,0:T(8,128)(2,1)} custom-call(bf16[256,384]{1,0:T(8,128)(2,1)} %place_rows.1.placed_hbm, bf16[384,2048]{1,0:T(8,128)(2,1)} %bitcast.13.returned_ref), custom_call_target="tpu_custom_call" | custom-call | flops 402653184 | bytes 2818048 | tf_op jit(solution)/shard_map/sum_rows/pallas_call | solution.py:40
  (40 shorter events, 13.8 us)
Async XLA Ops:
  2.5 15.5 %collective-permute-start.1 = (bf16[128,2048]{1,0:T(8,128)(2,1)}, bf16[128,2048]{1,0:T(8,128)(2,1)S(1)}, u32[]{:S(2)}, u32[]{:S(2)}) collective-permute-start(bf16[128,2048]{1,0:T(8,128)(2,1)} %get-tuple-element.29), channel_id=1, source_target_pairs={{0,4},{1,5},{2,6},{3,7},{4,0},{5,1},{6,2},{7,3},{8,12},{9,13},{10,... | collective-permute-start | bytes 1572872 | tf_op jit(solution)/shard_map/ppermute | solution.py:724
  18.0 0.8 copy-start
  21.8 43.1 %all-to-all-start.2 = ((bf16[16,24,2048]{2,1,0:T(8,128)(2,1)}), bf16[16,24,2048]{2,1,0:T(8,128)(2,1)}, u32[]{:S(2)}, u32[]{:S(2)}) async-start(bf16[16,24,2048]{2,1,0:T(8,128)(2,1)} %bitcast.15), calls=%async_computation.2 | async-start | bytes 3145728 | tf_op jit(solution)/shard_map/all_to_all | solution.py:729
  30.8 26.4 %collective-permute-start = (bf16[8,512,128]{2,1,0:T(8,128)(2,1)}, bf16[8,512,128]{2,1,0:T(8,128)(2,1)}, u32[]{:S(2)}, u32[]{:S(2)}) collective-permute-start(bf16[8,512,128]{2,1,0:T(8,128)(2,1)} %get-tuple-element.28), channel_id=1, source_target_pairs={{0,16},{16,0},{1,17},{17,1},{2,18},{18,2},{3,19},{19,3},{4,20},{20... | collective-permute-start | bytes 3145736 | tf_op jit(solution)/shard_map/ppermute | solution.py:694
  34.2 2.4 %collective-permute-start.2 = (bf16[256,512]{1,0:T(8,128)(2,1)}, bf16[256,512]{1,0:T(8,128)(2,1)S(1)}, u32[]{:S(2)}, u32[]{:S(2)}) collective-permute-start(bf16[256,512]{1,0:T(8,128)(2,1)} %get-tuple-element.31), channel_id=1, source_target_pairs={{0,1},{1,0},{2,3},{3,2},{4,5},{5,4},{6,7},{7,6},{8,9},{9,8},{10,11... | collective-permute-start | bytes 786440 | tf_op jit(solution)/shard_map/ppermute | solution.py:736
  34.9 12.5 %collective-permute-start.3 = (bf16[256,512]{1,0:T(8,128)(2,1)}, bf16[256,512]{1,0:T(8,128)(2,1)S(1)}, u32[]{:S(2)}, u32[]{:S(2)}) collective-permute-start(bf16[256,512]{1,0:T(8,128)(2,1)} %get-tuple-element.32), channel_id=1, source_target_pairs={{0,2},{1,3},{2,0},{3,1},{4,6},{5,7},{6,4},{7,5},{8,10},{9,11},{10,... | collective-permute-start | bytes 786440 | tf_op jit(solution)/shard_map/ppermute | solution.py:736
  35.2 22.0 %collective-permute-start.4 = (bf16[256,512]{1,0:T(8,128)(2,1)}, bf16[256,512]{1,0:T(8,128)(2,1)S(1)}, u32[]{:S(2)}, u32[]{:S(2)}) collective-permute-start(bf16[256,512]{1,0:T(8,128)(2,1)} %get-tuple-element.33), channel_id=1, source_target_pairs={{0,3},{1,2},{2,1},{3,0},{4,7},{5,6},{6,5},{7,4},{8,11},{9,10},{10,... | collective-permute-start | bytes 786440 | tf_op jit(solution)/shard_map/ppermute | solution.py:736
  36.6 20.6 %copy-start.6 = (bf16[256,512]{1,0:T(8,128)(2,1)}, bf16[256,512]{1,0:T(8,128)(2,1)S(1)}, u32[]{:S(2)}) copy-start(bf16[256,512]{1,0:T(8,128)(2,1)S(1)} %collective-permute-done.2.refs_2_) | copy-start | bytes 786436
  47.5 9.8 %copy-start.7 = (bf16[256,512]{1,0:T(8,128)(2,1)}, bf16[256,512]{1,0:T(8,128)(2,1)S(1)}, u32[]{:S(2)}) copy-start(bf16[256,512]{1,0:T(8,128)(2,1)S(1)} %collective-permute-done.3.refs_3_) | copy-start | bytes 786436
  57.2 0.7 copy-start.8
  64.8 9.8 %copy-start.5 = (f32[1,3,4,4,4]{4,3,2,1,0:T(4,128)S(1)}, f32[1,3,4,4,4]{4,3,2,1,0:T(4,128)}, u32[]{:S(2)}) copy-start(f32[1,3,4,4,4]{4,3,2,1,0:T(4,128)} %param.9) | copy-start | bytes 2308
  64.8 30.1 %all-to-all-start.1 = ((bf16[16,64,512]{2,1,0:T(8,128)(2,1)}), bf16[16,64,512]{2,1,0:T(8,128)(2,1)}, u32[]{:S(2)}, u32[]{:S(2)}) async-start(bf16[16,64,512]{2,1,0:T(8,128)(2,1)} %bitcast.21), calls=%async_computation.1 | async-start | bytes 2097152 | tf_op jit(solution)/shard_map/all_to_all | solution.py:729
  69.8 13.5 %collective-permute-start.5 = (bf16[4,512,128]{2,1,0:T(8,128)(2,1)}, bf16[4,512,128]{2,1,0:T(8,128)(2,1)}, u32[]{:S(2)}, u32[]{:S(2)}) collective-permute-start(bf16[4,512,128]{2,1,0:T(8,128)(2,1)} %get-tuple-element.39), channel_id=1, source_target_pairs={{0,16},{16,0},{1,17},{17,1},{2,18},{18,2},{3,19},{19,3},{4,20},{20... | collective-permute-start | bytes 1572872 | tf_op jit(solution)/shard_map/ppermute | solution.py:694
  74.3 20.6 %collective-permute-start.6 = (bf16[512,512]{1,0:T(8,128)(2,1)}, bf16[512,512]{1,0:T(8,128)(2,1)S(1)}, u32[]{:S(2)}, u32[]{:S(2)}) collective-permute-start(bf16[512,512]{1,0:T(8,128)(2,1)} %get-tuple-element.35.refs_1_), channel_id=1, source_target_pairs={{0,16},{16,0},{1,17},{17,1},{2,18},{18,2},{3,19},{19,3},{4,20},{20... | collective-permute-start | bytes 1572872 | tf_op jit(solution)/shard_map/ppermute | solution.py:694
  94.9 0.8 copy-start.2
  103.3 7.7 %copy-start.1 = (bf16[3,128,512]{2,1,0:T(8,128)(2,1)S(1)}, bf16[3,128,512]{2,1,0:T(8,128)(2,1)}, u32[]{:S(2)}) copy-start(bf16[3,128,512]{2,1,0:T(8,128)(2,1)} %get-tuple-element.42.refs_2_.d_hbm) | copy-start | bytes 1179652
  103.3 42.7 %all-to-all-start.3 = ((bf16[16,24,2048]{2,1,0:T(8,128)(2,1)}), bf16[16,24,2048]{2,1,0:T(8,128)(2,1)}, u32[]{:S(2)}, u32[]{:S(2)}) async-start(bf16[16,24,2048]{2,1,0:T(8,128)(2,1)} %bitcast.20), calls=%async_computation.3 | async-start | bytes 3145728 | tf_op jit(solution)/shard_map/all_to_all | solution.py:729
  109.7 23.1 %collective-permute-start.7 = (bf16[512,512]{1,0:T(8,128)(2,1)}, bf16[512,512]{1,0:T(8,128)(2,1)S(1)}, u32[]{:S(2)}, u32[]{:S(2)}) collective-permute-start(bf16[512,512]{1,0:T(8,128)(2,1)} %get-tuple-element.43), channel_id=1, source_target_pairs={{0,16},{16,0},{1,17},{17,1},{2,18},{18,2},{3,19},{19,3},{4,20},{20... | collective-permute-start | bytes 1572872 | tf_op jit(solution)/shard_map/ppermute | solution.py:694
  111.0 21.8 %collective-permute-start.8 = (bf16[3,128,512]{2,1,0:T(8,128)(2,1)S(1)}, bf16[3,128,512]{2,1,0:T(8,128)(2,1)}, u32[]{:S(2)}, u32[]{:S(2)}) collective-permute-start(bf16[3,128,512]{2,1,0:T(8,128)(2,1)S(1)} %copy-done.1), channel_id=1, source_target_pairs={{0,16},{16,0},{1,17},{17,1},{2,18},{18,2},{3,19},{19,3},{4,20},{20... | collective-permute-start | bytes 1179656 | tf_op jit(solution)/shard_map/ppermute | solution.py:694
  113.1 6.3 %copy-start.4 = (f32[128,128]{1,0:T(8,128)S(1)}, f32[128,128]{1,0:T(8,128)}, u32[]{:S(2)}) copy-start(f32[128,128]{1,0:T(8,128)} %get-tuple-element.47) | copy-start | bytes 196612
  118.1 14.1 %collective-permute-start.9 = (f32[1,3,4,4,4]{4,3,2,1,0:T(4,128)S(1)}, f32[1,3,4,4,4]{4,3,2,1,0:T(4,128)S(1)}, u32[]{:S(2)}, u32[]{:S(2)}) collective-permute-start(f32[1,3,4,4,4]{4,3,2,1,0:T(4,128)S(1)} %reshape.51), channel_id=1, source_target_pairs={{0,16},{16,0},{1,17},{17,1},{2,18},{18,2},{3,19},{19,3},{4,20},{20... | collective-permute-start | bytes 2312 | tf_op jit(solution)/shard_map/ppermute | solution.py:694
  132.8 0.8 copy-start.3

commit v19 on v18

--- a/solution.py
+++ b/solution.py
@@ -700,7 +700,7 @@
     halves = [list(range(h, h + half)) for h in range(0, peers, half)]
     if swap:
         flat_factors = factors[0].reshape(weights * count, depth_own, cols)
-        cuts = [across(x) for x in cut_factors(flat_factors, 2 * count)]
+        cuts = [across(x) for x in cut_factors(flat_factors, 2 * count + 1)]
         factor_parts = [factors[0]] + cuts
         sides = 2
     else:

time: 150 us -> 151 us (level)
    ppermute x6, waiting for transfers between devices: 13.3 us -> 25.8 us  [across(): return lax.ppermute(array, 'seq', pair)]
    all_to_all x3, waiting for transfers between devices: 19.9 us -> 7.64 us  [to_peers(): lax.all_to_all(array, 'exp', split_axis=0, concat_axis=0, tiled=True)]
    unnamed x18 -> x20, local copies, waits for them, and re-layouts: 3.08 us -> 2.41 us
  transfers between devices with their start and end apart: 13 -> 13, of which waited for: 7 -> 7; matrix products, arithmetic and copies ran while one was open for 3% -> 3% of each run, Pallas kernels for 21% -> 20%
where the time goes in v19:
time: 151 us; the launch traced here: 150 us
  waiting for transfers between devices  54.4 us (36%)
  Pallas kernels  46.2 us (31%)
  starting transfers between devices  26.9 us (18%)
  blocking collectives  15.3 us (10%)
  local copies, waits for them, and re-layouts  3.31 us (2%)
  other arithmetic  2.99 us (2%)
    pallas_call x12, Pallas kernels, call(): pl.pallas_call(body, out_shape=[x for x, _ in outs], in_specs=[place for...  46.2 us
    ppermute x6, waiting for transfers between devices, across(): return lax.ppermute(array, 'seq', pair)  25.8 us
    ppermute x3, waiting for transfers between devices, shards(): lax.ppermute(shares[k], 'exp', [(n, n ^ k) for n in range(peers)])  21 us
    all_to_all x3, starting transfers between devices, to_peers(): lax.all_to_all(array, 'exp', split_axis=0, concat_axis=0, tiled=True)  18.6 us
    all_to_all x1, blocking collectives, shards(): lax.all_to_all(told, 'exp', split_axis=0, concat_axis=0, tiled=True)  15.3 us
    all_to_all x3, waiting for transfers between devices, to_peers(): lax.all_to_all(array, 'exp', split_axis=0, concat_axis=0, tiled=True)  7.64 us
    ppermute x6, starting transfers between devices, across(): return lax.ppermute(array, 'seq', pair)  5.63 us
  transfers between devices with their start and end apart: 13, of which 7 were waited for; matrix products, arithmetic and copies ran while one was open for 3% of the time, Pallas kernels for 20%

profile of v19, /device:TPU:13, one launch (start us, length us, event | category | flops | bytes accessed | tf_op | source)
XLA Modules:
  0.0 150.0 jit_solution(331247052933146156)
XLA Ops:
  0.6 1.9 %wanted_rows.1 = (s32[32,128]{1,0:T(8,128)}, s32[1,128]{1,0:T(1,128)}, bf16[128,2048]{1,0:T(8,128)(2,1)}) custom-call(s32[1]{0:T(128)} %bitcast.me_ref, s32[2,64]{1,0:T(2,128)} %bitcast.26, bf16[128,4096]{1,0:T(8,128)(2,1)} %source_ref.2), custom_call_target="tpu_custom_call" | custom-call | flops 1048576 | bytes 1590276 | tf_op jit(solution)/shard_map/wanted_rows/pallas_call | solution.py:40
  2.8 15.3 %all_to_all.26 = s32[16,2,128]{2,1,0:T(2,128)} all-to-all(s32[16,2,128]{2,1,0:T(2,128)} %bitcast.25), channel_id=1, replica_groups=mesh['seq'=2,'exp'=16] {'exp'}, dimensions={0} | all-to-all | bytes 32768 | tf_op jit(solution)/shard_map/all_to_all | solution.py:725
  18.8 2.9 %pick_tokens.1 = bf16[384,2048]{1,0:T(8,128)(2,1)} custom-call(s32[32,128]{1,0:T(8,128)} %bitcast.22, bf16[128,4096]{1,0:T(8,128)(2,1)} %source_ref.3, bf16[128,2048]{1,0:T(8,128)(2,1)} %copy-done), custom_call_target="tpu_custom_call" | custom-call | flops 402653184 | bytes 3162112 | tf_op jit(solution)/shard_map/pick_tokens/pallas_call | solution.py:40
  21.8 6.7 %all-to-all-start.2 = ((bf16[16,24,2048]{2,1,0:T(8,128)(2,1)}), bf16[16,24,2048]{2,1,0:T(8,128)(2,1)}, u32[]{:S(2)}, u32[]{:S(2)}) async-start(bf16[16,24,2048]{2,1,0:T(8,128)(2,1)} %bitcast.15), calls=%async_computation.2 | async-start | bytes 3145728 | tf_op jit(solution)/shard_map/all_to_all | solution.py:729
  28.4 2.5 %cut_factors.1 = (bf16[9,512,128]{2,1,0:T(8,128)(2,1)}, bf16[3,512,128]{2,1,0:T(8,128)(2,1)}) custom-call(bf16[12,512,128]{2,1,0:T(8,128)(2,1)} %bitcast.17), custom_call_target="tpu_custom_call" | custom-call | bytes 3145728 | tf_op jit(solution)/shard_map/cut_factors/pallas_call | solution.py:40
  30.9 1.3 collective-permute-start
  32.2 2.2 %plane_columns.1 = (bf16[256,512]{1,0:T(8,128)(2,1)}, bf16[256,512]{1,0:T(8,128)(2,1)}, bf16[256,512]{1,0:T(8,128)(2,1)}, bf16[256,512]{1,0:T(8,128)(2,1)}) custom-call(s32[1]{0:T(128)} %bitcast.me_ref, bf16[128,4096]{1,0:T(8,128)(2,1)} %source_ref.2, bf16[128,2048]{1,0:T(8,128)(2,1)} %copy-done), custom_call_target="tpu_custom_call" | custom-call | bytes 2621444 | tf_op jit(solution)/shard_map/plane_columns/pallas_call | solution.py:40
  35.3 1.4 collective-permute-start.4
  36.8 10.9 %collective-permute-done.3.refs_3_ = bf16[256,512]{1,0:T(8,128)(2,1)S(1)} collective-permute-done((bf16[256,512]{1,0:T(8,128)(2,1)}, bf16[256,512]{1,0:T(8,128)(2,1)S(1)}, u32[]{:S(2)}, u32[]{:S(2)}) %collective-permute-start.3) | collective-permute-done | bytes 262176 | tf_op jit(solution)/shard_map/ppermute | solution.py:736
  47.7 10.1 %collective-permute-done.4.refs_4_ = bf16[256,512]{1,0:T(8,128)(2,1)S(1)} collective-permute-done((bf16[256,512]{1,0:T(8,128)(2,1)}, bf16[256,512]{1,0:T(8,128)(2,1)S(1)}, u32[]{:S(2)}, u32[]{:S(2)}) %collective-permute-start.4) | collective-permute-done | bytes 262176 | tf_op jit(solution)/shard_map/ppermute | solution.py:736
  58.5 4.2 %pick_cotangent.1 = bf16[1024,512]{1,0:T(8,128)(2,1)} custom-call(s32[1]{0:T(128)} %bitcast.me_ref, s32[32,128]{1,0:T(8,128)} %bitcast.23, bf16[9,512,128]{2,1,0:T(8,128)(2,1)} %collective-permute-done.refs_0_.refs_3_.refs_1_, bf16[256,512]{1,0:T(8,128)(2,1)} %get-tuple-element.30.refs_1_, bf16[256,512]{1,0:T(8,128)(2,1)} %copy-done.7, ...), custom_call_target="tpu_custom_call" | custom-call | flops 1073741824 | bytes 3293188 | tf_op jit(solution)/shard_map/pick_cotangent/pallas_call | solution.py:40
  62.7 2.1 %all-to-all-done.2 = bf16[16,24,2048]{2,1,0:T(8,128)(2,1)} async-done(((bf16[16,24,2048]{2,1,0:T(8,128)(2,1)}), bf16[16,24,2048]{2,1,0:T(8,128)(2,1)}, u32[]{:S(2)}, u32[]{:S(2)}) %all-to-all-start.2) | async-done | bytes 1572896 | tf_op jit(solution)/shard_map/all_to_all | solution.py:729
  64.8 5.0 %all-to-all-start.1 = ((bf16[16,64,512]{2,1,0:T(8,128)(2,1)}), bf16[16,64,512]{2,1,0:T(8,128)(2,1)}, u32[]{:S(2)}, u32[]{:S(2)}) async-start(bf16[16,64,512]{2,1,0:T(8,128)(2,1)} %bitcast.21), calls=%async_computation.1 | async-start | bytes 2097152 | tf_op jit(solution)/shard_map/all_to_all | solution.py:729
  69.8 3.3 %order_rows.1 = (bf16[512,512]{1,0:T(8,128)(2,1)}, bf16[512,512]{1,0:T(8,128)(2,1)}) custom-call(s32[1]{0:T(128)} %bitcast.4.order_ref, s32[1,128]{1,0:T(1,128)} %get-tuple-element.27.slot_hbm, bf16[384,2048]{1,0:T(8,128)(2,1)} %bitcast.10.got_hbm), custom_call_target="tpu_custom_call" | custom-call | flops 134217728 | bytes 2621956 | tf_op jit(solution)/shard_map/order_rows/pallas_call | solution.py:40
  75.4 6.0 %forward.1 = (f32[512,512]{1,0:T(8,128)}, f32[512,512]{1,0:T(8,128)}, f32[128,512]{1,0:T(8,128)}, f32[128,512]{1,0:T(8,128)}, f32[128,512]{1,0:T(8,128)}) custom-call(s32[1]{0:T(128)} %bitcast.4.order_ref, f32[192]{0:T(256)} %reshape.44.mix_ref, bf16[512,512]{1,0:T(8,128)(2,1)} %get-tuple-element.34.refs_0_, bf16[512,512]{1,0:T(8,128)(2,1)} %get-tuple-element.35.refs_1_, ...), custom_call_target="tpu_custom_call" | custom-call | flops 1073741824 | bytes 6685444 | tf_op jit(solution)/shard_map/forward/pallas_call | solution.py:40
  81.3 13.7 %collective-permute-done.5.refs_2_ = bf16[3,512,128]{2,1,0:T(8,128)(2,1)} collective-permute-done((bf16[3,512,128]{2,1,0:T(8,128)(2,1)S(1)}, bf16[3,512,128]{2,1,0:T(8,128)(2,1)}, u32[]{:S(2)}, u32[]{:S(2)}) %collective-permute-start.5) | collective-permute-done | bytes 393248 | tf_op jit(solution)/shard_map/ppermute | solution.py:694
  95.9 7.6 %backward.1 = (bf16[384,2048]{1,0:T(8,128)(2,1)}, bf16[512,512]{1,0:T(8,128)(2,1)}, bf16[512,512]{1,0:T(8,128)(2,1)}, f32[512,512]{1,0:T(8,128)}, bf16[3,128,512]{2,1,0:T(8,128)(2,1)}, /*index=5*/f32[128,128]{1,0:T(8,128)}) custom-call(s32[1]{0:T(128)} %bitcast.4.order_ref, f32[192]{0:T(256)} %reshape.44.mix_ref, s32[1,128]{1,0:T(1,128)} %get-tuple-element.27.slot_hbm, ...), custom_call_target="tpu_custom_call" | custom-call | flops 1610612736 | bytes 9635588 | tf_op jit(solution)/shard_map/backward/pallas_call | solution.py:40
  103.5 7.0 %all-to-all-start.3 = ((bf16[16,24,2048]{2,1,0:T(8,128)(2,1)}), bf16[16,24,2048]{2,1,0:T(8,128)(2,1)}, u32[]{:S(2)}, u32[]{:S(2)}) async-start(bf16[16,24,2048]{2,1,0:T(8,128)(2,1)} %bitcast.20), calls=%async_computation.3 | async-start | bytes 3145728 | tf_op jit(solution)/shard_map/all_to_all | solution.py:729
  112.0 1.9 %place_rows.1.placed_hbm = bf16[256,384]{1,0:T(8,128)(2,1)} custom-call(s32[1]{0:T(128)} %bitcast.me_ref, s32[32,128]{1,0:T(8,128)} %bitcast.24), custom_call_target="tpu_custom_call" | custom-call | flops 1048576 | bytes 212996 | tf_op jit(solution)/shard_map/place_rows/pallas_call | solution.py:40
  113.8 3.9 %mix_partials.1 = f32[192,128]{1,0:T(8,128)} custom-call(f32[512,512]{1,0:T(8,128)} %get-tuple-element.44.yg_hbm, f32[512,512]{1,0:T(8,128)} %get-tuple-element.45.yu_hbm, f32[512,512]{1,0:T(8,128)} %get-tuple-element.46.yd_hbm, bf16[3,128,512]{2,1,0:T(8,128)(2,1)} %get-tuple-element.42.refs_2_.d_hbm), custom_call_target="tpu_custom_call" | custom-call | flops 6291456 | bytes 3637248 | tf_op jit(solution)/shard_map/mix_partials/pallas_call | solution.py:40
  121.6 11.3 %collective-permute-done.9 = f32[1,3,4,4,4]{4,3,2,1,0:T(4,128)S(1)} collective-permute-done((f32[1,3,4,4,4]{4,3,2,1,0:T(4,128)S(1)}, f32[1,3,4,4,4]{4,3,2,1,0:T(4,128)S(1)}, u32[]{:S(2)}, u32[]{:S(2)}) %collective-permute-start.9) | collective-permute-done | bytes 800 | tf_op jit(solution)/shard_map/ppermute | solution.py:694
  134.3 6.9 %factor_grad.1 = f32[3,4,512,128]{3,2,1,0:T(8,128)} custom-call(f32[192]{0:T(256)} %reshape.44.mix_ref, bf16[512,512]{1,0:T(8,128)(2,1)} %get-tuple-element.34.refs_0_, bf16[512,512]{1,0:T(8,128)(2,1)} %get-tuple-element.41.refs_1_, bf16[3,128,512]{2,1,0:T(8,128)(2,1)} %get-tuple-element.42.refs_2_.d_hbm, bf16[512,512]{1,0:T(8,128)(2,1)} %copy-done.2, ...), custom_call_target="tpu_custom_call" | custom-call | flops 1610612736 | bytes 6030080 | tf_op jit(solution)/shard_map/factor_grad/pallas_call | solution.py:40
  141.2 5.5 %all-to-all-done.3 = bf16[16,24,2048]{2,1,0:T(8,128)(2,1)} async-done(((bf16[16,24,2048]{2,1,0:T(8,128)(2,1)}), bf16[16,24,2048]{2,1,0:T(8,128)(2,1)}, u32[]{:S(2)}, u32[]{:S(2)}) %all-to-all-start.3) | async-done | bytes 1572896 | tf_op jit(solution)/shard_map/all_to_all | solution.py:729
  146.7 3.1 %sum_rows.1 = bf16[128,4096]{1,0:T(8,128)(2,1)} custom-call(bf16[256,384]{1,0:T(8,128)(2,1)} %place_rows.1.placed_hbm, bf16[384,2048]{1,0:T(8,128)(2,1)} %bitcast.13.returned_ref), custom_call_target="tpu_custom_call" | custom-call | flops 402653184 | bytes 2818048 | tf_op jit(solution)/shard_map/sum_rows/pallas_call | solution.py:40
  (42 shorter events, 12.6 us)
Async XLA Ops:
  2.5 15.5 %collective-permute-start.1 = (bf16[128,2048]{1,0:T(8,128)(2,1)}, bf16[128,2048]{1,0:T(8,128)(2,1)S(1)}, u32[]{:S(2)}, u32[]{:S(2)}) collective-permute-start(bf16[128,2048]{1,0:T(8,128)(2,1)} %get-tuple-element.29), channel_id=1, source_target_pairs={{0,4},{1,5},{2,6},{3,7},{4,0},{5,1},{6,2},{7,3},{8,12},{9,13},{10,... | collective-permute-start | bytes 1572872 | tf_op jit(solution)/shard_map/ppermute | solution.py:724
  18.0 0.8 copy-start
  21.8 43.1 %all-to-all-start.2 = ((bf16[16,24,2048]{2,1,0:T(8,128)(2,1)}), bf16[16,24,2048]{2,1,0:T(8,128)(2,1)}, u32[]{:S(2)}, u32[]{:S(2)}) async-start(bf16[16,24,2048]{2,1,0:T(8,128)(2,1)} %bitcast.15), calls=%async_computation.2 | async-start | bytes 3145728 | tf_op jit(solution)/shard_map/all_to_all | solution.py:729
  30.9 27.6 %collective-permute-start = (bf16[9,512,128]{2,1,0:T(8,128)(2,1)}, bf16[9,512,128]{2,1,0:T(8,128)(2,1)}, u32[]{:S(2)}, u32[]{:S(2)}) collective-permute-start(bf16[9,512,128]{2,1,0:T(8,128)(2,1)} %get-tuple-element.28), channel_id=1, source_target_pairs={{0,16},{16,0},{1,17},{17,1},{2,18},{18,2},{3,19},{19,3},{4,20},{20... | collective-permute-start | bytes 3538952 | tf_op jit(solution)/shard_map/ppermute | solution.py:694
  34.3 2.4 %collective-permute-start.2 = (bf16[256,512]{1,0:T(8,128)(2,1)}, bf16[256,512]{1,0:T(8,128)(2,1)S(1)}, u32[]{:S(2)}, u32[]{:S(2)}) collective-permute-start(bf16[256,512]{1,0:T(8,128)(2,1)} %get-tuple-element.31), channel_id=1, source_target_pairs={{0,1},{1,0},{2,3},{3,2},{4,5},{5,4},{6,7},{7,6},{8,9},{9,8},{10,11... | collective-permute-start | bytes 786440 | tf_op jit(solution)/shard_map/ppermute | solution.py:736
  35.1 12.6 %collective-permute-start.3 = (bf16[256,512]{1,0:T(8,128)(2,1)}, bf16[256,512]{1,0:T(8,128)(2,1)S(1)}, u32[]{:S(2)}, u32[]{:S(2)}) collective-permute-start(bf16[256,512]{1,0:T(8,128)(2,1)} %get-tuple-element.32), channel_id=1, source_target_pairs={{0,2},{1,3},{2,0},{3,1},{4,6},{5,7},{6,4},{7,5},{8,10},{9,11},{10,... | collective-permute-start | bytes 786440 | tf_op jit(solution)/shard_map/ppermute | solution.py:736
  35.3 22.4 %collective-permute-start.4 = (bf16[256,512]{1,0:T(8,128)(2,1)}, bf16[256,512]{1,0:T(8,128)(2,1)S(1)}, u32[]{:S(2)}, u32[]{:S(2)}) collective-permute-start(bf16[256,512]{1,0:T(8,128)(2,1)} %get-tuple-element.33), channel_id=1, source_target_pairs={{0,3},{1,2},{2,1},{3,0},{4,7},{5,6},{6,5},{7,4},{8,11},{9,10},{10,... | collective-permute-start | bytes 786440 | tf_op jit(solution)/shard_map/ppermute | solution.py:736
  36.8 21.7 %copy-start.7 = (bf16[256,512]{1,0:T(8,128)(2,1)}, bf16[256,512]{1,0:T(8,128)(2,1)S(1)}, u32[]{:S(2)}) copy-start(bf16[256,512]{1,0:T(8,128)(2,1)S(1)} %collective-permute-done.2.refs_2_) | copy-start | bytes 786436
  47.7 10.8 %copy-start.8 = (bf16[256,512]{1,0:T(8,128)(2,1)}, bf16[256,512]{1,0:T(8,128)(2,1)S(1)}, u32[]{:S(2)}) copy-start(bf16[256,512]{1,0:T(8,128)(2,1)S(1)} %collective-permute-done.3.refs_3_) | copy-start | bytes 786436
  57.8 0.7 copy-start.9
  64.8 9.6 %copy-start.6 = (bf16[3,512,128]{2,1,0:T(8,128)(2,1)S(1)}, bf16[3,512,128]{2,1,0:T(8,128)(2,1)}, u32[]{:S(2)}) copy-start(bf16[3,512,128]{2,1,0:T(8,128)(2,1)} %get-tuple-element.39) | copy-start | bytes 1179652
  64.8 9.8 %copy-start.5 = (f32[1,3,4,4,4]{4,3,2,1,0:T(4,128)S(1)}, f32[1,3,4,4,4]{4,3,2,1,0:T(4,128)}, u32[]{:S(2)}) copy-start(f32[1,3,4,4,4]{4,3,2,1,0:T(4,128)} %param.9) | copy-start | bytes 2308
  64.8 30.3 %all-to-all-start.1 = ((bf16[16,64,512]{2,1,0:T(8,128)(2,1)}), bf16[16,64,512]{2,1,0:T(8,128)(2,1)}, u32[]{:S(2)}, u32[]{:S(2)}) async-start(bf16[16,64,512]{2,1,0:T(8,128)(2,1)} %bitcast.21), calls=%async_computation.1 | async-start | bytes 2097152 | tf_op jit(solution)/shard_map/all_to_all | solution.py:729
  73.1 22.0 %collective-permute-start.6 = (bf16[512,512]{1,0:T(8,128)(2,1)}, bf16[512,512]{1,0:T(8,128)(2,1)S(1)}, u32[]{:S(2)}, u32[]{:S(2)}) collective-permute-start(bf16[512,512]{1,0:T(8,128)(2,1)} %get-tuple-element.35.refs_1_), channel_id=1, source_target_pairs={{0,16},{16,0},{1,17},{17,1},{2,18},{18,2},{3,19},{19,3},{4,20},{20... | collective-permute-start | bytes 1572872 | tf_op jit(solution)/shard_map/ppermute | solution.py:694
  74.4 20.7 %collective-permute-start.5 = (bf16[3,512,128]{2,1,0:T(8,128)(2,1)S(1)}, bf16[3,512,128]{2,1,0:T(8,128)(2,1)}, u32[]{:S(2)}, u32[]{:S(2)}) collective-permute-start(bf16[3,512,128]{2,1,0:T(8,128)(2,1)S(1)} %copy-done.6), channel_id=1, source_target_pairs={{0,16},{16,0},{1,17},{17,1},{2,18},{18,2},{3,19},{19,3},{4,20},{20... | collective-permute-start | bytes 1179656 | tf_op jit(solution)/shard_map/ppermute | solution.py:694
  95.1 0.8 copy-start.2
  103.4 8.3 %copy-start.1 = (bf16[3,128,512]{2,1,0:T(8,128)(2,1)S(1)}, bf16[3,128,512]{2,1,0:T(8,128)(2,1)}, u32[]{:S(2)}) copy-start(bf16[3,128,512]{2,1,0:T(8,128)(2,1)} %get-tuple-element.42.refs_2_.d_hbm) | copy-start | bytes 1179652
  103.5 43.3 %all-to-all-start.3 = ((bf16[16,24,2048]{2,1,0:T(8,128)(2,1)}), bf16[16,24,2048]{2,1,0:T(8,128)(2,1)}, u32[]{:S(2)}, u32[]{:S(2)}) async-start(bf16[16,24,2048]{2,1,0:T(8,128)(2,1)} %bitcast.20), calls=%async_computation.3 | async-start | bytes 3145728 | tf_op jit(solution)/shard_map/all_to_all | solution.py:729
  110.4 23.1 %collective-permute-start.7 = (bf16[512,512]{1,0:T(8,128)(2,1)}, bf16[512,512]{1,0:T(8,128)(2,1)S(1)}, u32[]{:S(2)}, u32[]{:S(2)}) collective-permute-start(bf16[512,512]{1,0:T(8,128)(2,1)} %get-tuple-element.43), channel_id=1, source_target_pairs={{0,16},{16,0},{1,17},{17,1},{2,18},{18,2},{3,19},{19,3},{4,20},{20... | collective-permute-start | bytes 1572872 | tf_op jit(solution)/shard_map/ppermute | solution.py:694
  111.7 21.8 %collective-permute-start.8 = (bf16[3,128,512]{2,1,0:T(8,128)(2,1)S(1)}, bf16[3,128,512]{2,1,0:T(8,128)(2,1)}, u32[]{:S(2)}, u32[]{:S(2)}) collective-permute-start(bf16[3,128,512]{2,1,0:T(8,128)(2,1)S(1)} %copy-done.1), channel_id=1, source_target_pairs={{0,16},{16,0},{1,17},{17,1},{2,18},{18,2},{3,19},{19,3},{4,20},{20... | collective-permute-start | bytes 1179656 | tf_op jit(solution)/shard_map/ppermute | solution.py:694
  113.8 6.3 %copy-start.4 = (f32[128,128]{1,0:T(8,128)S(1)}, f32[128,128]{1,0:T(8,128)}, u32[]{:S(2)}) copy-start(f32[128,128]{1,0:T(8,128)} %get-tuple-element.47) | copy-start | bytes 196612
  118.9 14.1 %collective-permute-start.9 = (f32[1,3,4,4,4]{4,3,2,1,0:T(4,128)S(1)}, f32[1,3,4,4,4]{4,3,2,1,0:T(4,128)S(1)}, u32[]{:S(2)}, u32[]{:S(2)}) collective-permute-start(f32[1,3,4,4,4]{4,3,2,1,0:T(4,128)S(1)} %reshape.51), channel_id=1, source_target_pairs={{0,16},{16,0},{1,17},{17,1},{2,18},{18,2},{3,19},{19,3},{4,20},{20... | collective-permute-start | bytes 2312 | tf_op jit(solution)/shard_map/ppermute | solution.py:694
  133.5 0.8 copy-start.3

commit v20 on v18

--- a/solution.py
+++ b/solution.py
@@ -495,6 +495,34 @@
     return [d_ref[at, b * cols : (b + 1) * cols].astype(F32) for b in range(NPHM)]
 
 
+def join_factors(group, parts, first, stop, name):
+    _, count, rows, cols = parts[0].shape
+    depth, hidden = rows * (2 if len(parts) > 1 else 1), count * cols
+    wide = (stop - first) * hidden
+
+    def body(order_ref, *refs):
+        ins, (out_ref, held_ref, sems, out_sem) = refs[: len(parts)], refs[len(parts) :]
+        loads = []
+        for m in range(first, stop):
+            target = held_ref.at[:, (m - first) * hidden : (m - first + 1) * hidden]
+            loads += load_factor(order_ref, ins, m, target, sems.at[m])
+        wait_all(loads)
+        begin(held_ref, out_ref, out_sem).wait()
+
+    return call(
+        body,
+        [(shaped((depth, wide), BF16), HBM)],
+        [(group, SMEM)] + [(x, HBM) for x in parts],
+        name,
+        0,
+        [
+            scratch_like((depth, wide), BF16),
+            pltpu.SemaphoreType.DMA((stop, 2, count)),
+            pltpu.SemaphoreType.DMA,
+        ],
+    )[0]
+
+
 def order_body(cap, pieces, order_ref, slot_hbm, got_hbm, *refs):
     x_outs, (got_ref, x_ref, slot_ref, got_sem, out_sem) = refs[:-5], refs[-5:]
     small = begin(slot_hbm, slot_ref, got_sem.at[got_sem.shape[0] - 1])
@@ -506,9 +534,7 @@
 
 
 def forward_body(sides, order_ref, mix_ref, *refs):
-    x_parts, refs = refs[:sides], refs[sides:]
-    held = 2 if sides > 1 else 1
-    parts, refs = refs[:held], refs[held:]
+    x_parts, side_hbm, refs = refs[:sides], refs[sides], refs[sides + 1 :]
     yg_hbm, yu_hbm, act_hbm, slope_hbm, hid_hbm = refs[:5]
     side_ref, x_ref, yg_ref, yu_ref, act_ref, slope_ref, hid_ref = refs[5:12]
     x_sem, side_sem, out_sem = refs[12:]
@@ -517,16 +543,14 @@
         size = part.shape[1]
         start = pl.multiple_of((order_ref[0] ^ n) * size if sides > 1 else 0, size)
         loads.append(begin(part, x_ref.at[:, pl.ds(start, size)], x_sem.at[n]))
-    sides_in = [
-        load_factor(order_ref, parts, m, side_ref.at[m], side_sem.at[m]) for m in range(2)
-    ]
+    side_in = begin(side_hbm, side_ref, side_sem)
     wait_all(loads)
     stores = []
-    wait_all(sides_in[0])
-    yg_ref[...] = dot(x_ref[...], side_ref[0])
+    side_in.wait()
+    hidden = yg_ref.shape[1]
+    yg_ref[...] = dot(x_ref[...], side_ref[:, :hidden])
     stores.append(begin(yg_ref, yg_hbm, out_sem.at[2]))
-    wait_all(sides_in[1])
-    yu_ref[...] = dot(x_ref[...], side_ref[1])
+    yu_ref[...] = dot(x_ref[...], side_ref[:, hidden:])
     stores.append(begin(yu_ref, yu_hbm, out_sem.at[3]))
     cols = yg_ref.shape[1] // NPHM
     for n in range(yg_ref.shape[0] // (NPHM * STRIP)):
@@ -549,8 +573,7 @@
     cap, pieces, sides, after, order_ref, mix_ref, slot_hbm, score_hbm, got_hbm, act_hbm, slope_hbm, hid_hbm,
     *refs,
 ):
-    held = 3 if sides > 1 else 1
-    parts, refs = refs[:held], refs[held + after :]
+    side_hbm, down_hbm, refs = refs[0], refs[1], refs[2 + after :]
     back_hbm, x_outs, refs = refs[0], refs[1 : 1 + sides], refs[1 + sides :]
     y_hbm, d_hbm, inner_hbm = refs[:3]
     (
@@ -558,7 +581,7 @@
         back_ref, inner_ref, slot_ref, score_ref, got_sem, side_sem, in_sem, out_sem,
     ) = refs[3:]
     loads = load_rows(got_hbm, x_ref, got_sem)
-    down_in = load_factor(order_ref, parts, 2, down_ref, side_sem.at[2])
+    down_in = [begin(down_hbm, down_ref, side_sem.at[0])]
     small_in = [
         begin(source, target, in_sem.at[n])
         for n, (source, target) in enumerate(((score_hbm, score_ref), (slot_hbm, slot_ref)))
@@ -570,10 +593,7 @@
         )
     ]
     hidden = d_ref.shape[2]
-    sides_in = []
-    for m in range(2):
-        target = side_ref.at[:, m * hidden : (m + 1) * hidden]
-        sides_in += load_factor(order_ref, parts, m, target, side_sem.at[m])
+    sides_in = [begin(side_hbm, side_ref, side_sem.at[1])]
     wait_all(small_in)
     score = jnp.concatenate([score_ref[b : b + 1, :] for b in range(score_ref.shape[0])], axis=1)
     rows = score.shape[1]
@@ -707,7 +727,6 @@
         cuts = []
         factor_parts = [lax.all_gather(factors, "seq", axis=3, tiled=True)[0]]
         sides = 1
-    sides_in = [(x, HBM) for x in factor_parts]
     cross = [(shaped((own_rows, width // 2), BF16), HBM)] if direct else []
     told, slot, *crossed = call(
         functools.partial(front_body, cap, pieces, own_rows, block_len, half, direct),
@@ -757,6 +776,8 @@
     mixed_scratch = scratch_like((stacked, hidden), F32)
     low_scratch = scratch_like((stacked, hidden), BF16)
     flat_scratch = scratch_like((rows, hidden), F32)
+    gate_up = join_factors(group, factor_parts[:2], 0, 2, "join_gate_up")
+    down = join_factors(group, factor_parts, 2, 3, "join_down")
     x_parts = call(
         functools.partial(order_body, cap, pieces),
         split,
@@ -769,12 +790,12 @@
     y_gate, y_up, act, slope, hid = call(
         functools.partial(forward_body, sides),
         [mixed, mixed, flat, flat, flat],
-        [(group, SMEM), (mixing, SMEM)] + [(x, HBM) for x in x_parts] + sides_in[:2],
+        [(group, SMEM), (mixing, SMEM)] + [(x, HBM) for x in x_parts] + [(gate_up, HBM)],
         "forward",
         2 * product,
-        [scratch_like((2, depth, hidden), BF16), stack_scratch, mixed_scratch, mixed_scratch]
+        [scratch_like((depth, 2 * hidden), BF16), stack_scratch, mixed_scratch, mixed_scratch]
         + [flat_scratch] * 3
-        + [dma((2,)), dma((2, sides, count)), dma((7,))],
+        + [dma((2,)), dma, dma((7,))],
     )
     x_rows = [x_parts[0]] + [across(x) for x in x_parts[1:]]
     after = x_rows[1:]
@@ -785,8 +806,7 @@
         + [mixed, (shaped((weights, rows, hidden), BF16), HBM), (shaped((rows, cols), F32), HBM)],
         [(group, SMEM), (mixing, SMEM), (slot, HBM), (scores[0], HBM), (got_grads, HBM)]
         + [(x, HBM) for x in (act, slope, hid)]
-        + sides_in
-        + [(x, HBM) for x in after],
+        + [(x, HBM) for x in [gate_up, down] + after],
         "backward",
         3 * product,
         [scratch_like((depth, hidden), BF16), scratch_like((depth, 2 * hidden), BF16)]
@@ -795,7 +815,7 @@
         + [scratch_like((stacked, 2 * hidden), BF16), stack_scratch, back_scratch]
         + [scratch_like((rows, cols), F32), scratch_like(slot.shape, jnp.int32)]
         + [scratch_like(scores.shape[1:], jnp.int32)]
-        + [dma((pieces_in,)), dma((weights, sides, count)), dma((5,)), dma((5 + steps,))],
+        + [dma((pieces_in,)), dma((2,)), dma((5,)), dma((5 + steps,))],
     )
     back, g_parts, (y_down, d_own, inner) = outs[0], outs[1 : 1 + sides], outs[1 + sides :]
     returned = to_peers(back)

time: 150 us -> 149 us (level)
  waiting for transfers between devices: 53.7 us -> 48.4 us
  Pallas kernels: 46.1 us -> 50.7 us
    all_to_all x3, waiting for transfers between devices: 19.9 us -> 11.5 us  [to_peers(): lax.all_to_all(array, 'exp', split_axis=0, concat_axis=0, tiled=True)]
    pallas_call x12 -> x14, Pallas kernels: 46.1 us -> 50.7 us  [call(): pl.pallas_call(body, out_shape=[x for x, _ in outs], in_specs=[place for...]
    ppermute x6, waiting for transfers between devices: 13.3 us -> 16.3 us  [across(): return lax.ppermute(array, 'seq', pair)]
  transfers between devices with their start and end apart: 13 -> 13, of which waited for: 7 -> 7; matrix products, arithmetic and copies ran while one was open for 3% -> 3% of each run, Pallas kernels for 21% -> 24%
where the time goes in v20:
time: 149 us
  Pallas kernels  50.7 us (34%)
  waiting for transfers between devices  48.4 us (32%)
  starting transfers between devices  26.3 us (18%)
  blocking collectives  15.3 us (10%)
  local copies, waits for them, and re-layouts  3.95 us (3%)
  other arithmetic  2.99 us (2%)
    pallas_call x14, Pallas kernels, call(): pl.pallas_call(body, out_shape=[x for x, _ in outs], in_specs=[place for...  50.7 us
    ppermute x3, waiting for transfers between devices, shards(): lax.ppermute(shares[k], 'exp', [(n, n ^ k) for n in range(peers)])  20.6 us
    all_to_all x3, starting transfers between devices, to_peers(): lax.all_to_all(array, 'exp', split_axis=0, concat_axis=0, tiled=True)  18 us
    ppermute x6, waiting for transfers between devices, across(): return lax.ppermute(array, 'seq', pair)  16.3 us
    all_to_all x1, blocking collectives, shards(): lax.all_to_all(told, 'exp', split_axis=0, concat_axis=0, tiled=True)  15.3 us
    all_to_all x3, waiting for transfers between devices, to_peers(): lax.all_to_all(array, 'exp', split_axis=0, concat_axis=0, tiled=True)  11.5 us
    ppermute x6, starting transfers between devices, across(): return lax.ppermute(array, 'seq', pair)  5.62 us
    unnamed x18, local copies, waits for them, and re-layouts  3.07 us
  transfers between devices with their start and end apart: 13, of which 7 were waited for; matrix products, arithmetic and copies ran while one was open for 3% of the time, Pallas kernels for 24%

profile of v20, /device:TPU:13, one launch (start us, length us, event | category | flops | bytes accessed | tf_op | source)
XLA Modules:
  0.0 148.6 jit_solution(13261610513165617385)
XLA Ops:
  0.6 1.9 %wanted_rows.1 = (s32[32,128]{1,0:T(8,128)}, s32[1,128]{1,0:T(1,128)}, bf16[128,2048]{1,0:T(8,128)(2,1)}) custom-call(s32[1]{0:T(128)} %bitcast.me_ref, s32[2,64]{1,0:T(2,128)} %bitcast.26, bf16[128,4096]{1,0:T(8,128)(2,1)} %source_ref.2), custom_call_target="tpu_custom_call" | custom-call | flops 1048576 | bytes 1590276 | tf_op jit(solution)/shard_map/wanted_rows/pallas_call | solution.py:40
  2.8 15.3 %all_to_all.26 = s32[16,2,128]{2,1,0:T(2,128)} all-to-all(s32[16,2,128]{2,1,0:T(2,128)} %bitcast.25), channel_id=1, replica_groups=mesh['seq'=2,'exp'=16] {'exp'}, dimensions={0} | all-to-all | bytes 32768 | tf_op jit(solution)/shard_map/all_to_all | solution.py:744
  18.8 2.9 %pick_tokens.1 = bf16[384,2048]{1,0:T(8,128)(2,1)} custom-call(s32[32,128]{1,0:T(8,128)} %bitcast.22, bf16[128,4096]{1,0:T(8,128)(2,1)} %source_ref.3, bf16[128,2048]{1,0:T(8,128)(2,1)} %copy-done), custom_call_target="tpu_custom_call" | custom-call | flops 402653184 | bytes 3162112 | tf_op jit(solution)/shard_map/pick_tokens/pallas_call | solution.py:40
  21.8 6.7 %all-to-all-start.2 = ((bf16[16,24,2048]{2,1,0:T(8,128)(2,1)}), bf16[16,24,2048]{2,1,0:T(8,128)(2,1)}, u32[]{:S(2)}, u32[]{:S(2)}) async-start(bf16[16,24,2048]{2,1,0:T(8,128)(2,1)} %bitcast.18), calls=%async_computation.2 | async-start | bytes 3145728 | tf_op jit(solution)/shard_map/all_to_all | solution.py:748
  28.4 2.4 %cut_factors.1 = (bf16[8,512,128]{2,1,0:T(8,128)(2,1)}, bf16[4,512,128]{2,1,0:T(8,128)(2,1)}) custom-call(bf16[12,512,128]{2,1,0:T(8,128)(2,1)} %bitcast.15), custom_call_target="tpu_custom_call" | custom-call | bytes 3145728 | tf_op jit(solution)/shard_map/cut_factors/pallas_call | solution.py:40
  32.1 2.1 %plane_columns.1 = (bf16[256,512]{1,0:T(8,128)(2,1)}, bf16[256,512]{1,0:T(8,128)(2,1)}, bf16[256,512]{1,0:T(8,128)(2,1)}, bf16[256,512]{1,0:T(8,128)(2,1)}) custom-call(s32[1]{0:T(128)} %bitcast.me_ref, bf16[128,4096]{1,0:T(8,128)(2,1)} %source_ref.2, bf16[128,2048]{1,0:T(8,128)(2,1)} %copy-done), custom_call_target="tpu_custom_call" | custom-call | bytes 2621444 | tf_op jit(solution)/shard_map/plane_columns/pallas_call | solution.py:40
  36.7 10.8 %collective-permute-done.3.refs_3_ = bf16[256,512]{1,0:T(8,128)(2,1)S(1)} collective-permute-done((bf16[256,512]{1,0:T(8,128)(2,1)}, bf16[256,512]{1,0:T(8,128)(2,1)S(1)}, u32[]{:S(2)}, u32[]{:S(2)}) %collective-permute-start.3) | collective-permute-done | bytes 262176 | tf_op jit(solution)/shard_map/ppermute | solution.py:755
  47.5 9.7 %collective-permute-done.4.refs_4_ = bf16[256,512]{1,0:T(8,128)(2,1)S(1)} collective-permute-done((bf16[256,512]{1,0:T(8,128)(2,1)}, bf16[256,512]{1,0:T(8,128)(2,1)S(1)}, u32[]{:S(2)}, u32[]{:S(2)}) %collective-permute-start.4) | collective-permute-done | bytes 262176 | tf_op jit(solution)/shard_map/ppermute | solution.py:755
  57.9 4.2 %pick_cotangent.1 = bf16[1024,512]{1,0:T(8,128)(2,1)} custom-call(s32[1]{0:T(128)} %bitcast.me_ref, s32[32,128]{1,0:T(8,128)} %bitcast.23, bf16[8,512,128]{2,1,0:T(8,128)(2,1)} %collective-permute-done.refs_0_.refs_1_, bf16[256,512]{1,0:T(8,128)(2,1)} %get-tuple-element.30.refs_1_, bf16[256,512]{1,0:T(8,128)(2,1)} %copy-done.6, bf16[256,512]{1,0:T(8,128)(2,1)} %copy-done.7, ...), custom_call_target="tpu_custom_call" | custom-call | flops 1073741824 | bytes 3162116 | tf_op jit(solution)/shard_map/pick_cotangent/pallas_call | solution.py:40
  62.2 2.6 %all-to-all-done.2 = bf16[16,24,2048]{2,1,0:T(8,128)(2,1)} async-done(((bf16[16,24,2048]{2,1,0:T(8,128)(2,1)}), bf16[16,24,2048]{2,1,0:T(8,128)(2,1)}, u32[]{:S(2)}, u32[]{:S(2)}) %all-to-all-start.2) | async-done | bytes 1572896 | tf_op jit(solution)/shard_map/all_to_all | solution.py:748
  64.8 4.9 %all-to-all-start.1 = ((bf16[16,64,512]{2,1,0:T(8,128)(2,1)}), bf16[16,64,512]{2,1,0:T(8,128)(2,1)}, u32[]{:S(2)}, u32[]{:S(2)}) async-start(bf16[16,64,512]{2,1,0:T(8,128)(2,1)} %bitcast.21), calls=%async_computation.1 | async-start | bytes 2097152 | tf_op jit(solution)/shard_map/all_to_all | solution.py:748
  71.0 3.3 %order_rows.1 = (bf16[512,512]{1,0:T(8,128)(2,1)}, bf16[512,512]{1,0:T(8,128)(2,1)}) custom-call(s32[1]{0:T(128)} %bitcast.4.order_ref, s32[1,128]{1,0:T(1,128)} %get-tuple-element.27.slot_hbm, bf16[384,2048]{1,0:T(8,128)(2,1)} %bitcast.10.got_hbm), custom_call_target="tpu_custom_call" | custom-call | flops 134217728 | bytes 2621956 | tf_op jit(solution)/shard_map/order_rows/pallas_call | solution.py:40
  75.2 3.1 %join_gate_up.1.refs_2_.refs_0_ = bf16[1024,1024]{1,0:T(8,128)(2,1)} custom-call(s32[1]{0:T(128)} %bitcast.4.order_ref, bf16[3,4,512,128]{3,2,1,0:T(8,128)(2,1)} %bitcast.16, bf16[8,512,128]{2,1,0:T(8,128)(2,1)} %collective-permute-done.refs_0_.refs_1_), custom_call_target="tpu_custom_call" | custom-call | bytes 4718596 | tf_op jit(solution)/shard_map/join_gate_up/pallas_call | solution.py:40
  78.3 4.9 %collective-permute-done.5.refs_2_ = bf16[4,512,128]{2,1,0:T(8,128)(2,1)} collective-permute-done((bf16[4,512,128]{2,1,0:T(8,128)(2,1)}, bf16[4,512,128]{2,1,0:T(8,128)(2,1)}, u32[]{:S(2)}, u32[]{:S(2)}) %collective-permute-start.5) | collective-permute-done | bytes 524320 | tf_op jit(solution)/shard_map/ppermute | solution.py:714
  83.2 2.5 %join_down.1.refs_1_ = bf16[1024,512]{1,0:T(8,128)(2,1)} custom-call(s32[1]{0:T(128)} %bitcast.4.order_ref, bf16[3,4,512,128]{3,2,1,0:T(8,128)(2,1)} %bitcast.17, bf16[8,512,128]{2,1,0:T(8,128)(2,1)} %collective-permute-done.refs_0_.refs_1_, bf16[4,512,128]{2,1,0:T(8,128)(2,1)} %collective-permute-done.5.refs_2_), custom_call_target="tpu_custom_call" | custom-call | bytes 4194308 | tf_op jit(solution)/shard_map/join_down/pallas_call | solution.py:40
  85.7 5.8 %forward.1 = (f32[512,512]{1,0:T(8,128)}, f32[512,512]{1,0:T(8,128)}, f32[128,512]{1,0:T(8,128)}, f32[128,512]{1,0:T(8,128)}, f32[128,512]{1,0:T(8,128)}) custom-call(s32[1]{0:T(128)} %bitcast.4.order_ref, f32[192]{0:T(256)} %reshape.44.mix_ref, bf16[512,512]{1,0:T(8,128)(2,1)} %get-tuple-element.34.refs_0_, bf16[512,512]{1,0:T(8,128)(2,1)} %get-tuple-element.35.refs_1_, ...), custom_call_target="tpu_custom_call" | custom-call | flops 1073741824 | bytes 6030084 | tf_op jit(solution)/shard_map/forward/pallas_call | solution.py:40
  91.5 3.4 %all-to-all-done.1 = bf16[16,64,512]{2,1,0:T(8,128)(2,1)} async-done(((bf16[16,64,512]{2,1,0:T(8,128)(2,1)}), bf16[16,64,512]{2,1,0:T(8,128)(2,1)}, u32[]{:S(2)}, u32[]{:S(2)}) %all-to-all-start.1) | async-done | bytes 1048608 | tf_op jit(solution)/shard_map/all_to_all | solution.py:748
  95.7 6.9 %backward.1 = (bf16[384,2048]{1,0:T(8,128)(2,1)}, bf16[512,512]{1,0:T(8,128)(2,1)}, bf16[512,512]{1,0:T(8,128)(2,1)}, f32[512,512]{1,0:T(8,128)}, bf16[3,128,512]{2,1,0:T(8,128)(2,1)}, /*index=5*/f32[128,128]{1,0:T(8,128)}) custom-call(s32[1]{0:T(128)} %bitcast.4.order_ref, f32[192]{0:T(256)} %reshape.44.mix_ref, s32[1,128]{1,0:T(1,128)} %get-tuple-element.27.slot_hbm, ...), custom_call_target="tpu_custom_call" | custom-call | flops 1610612736 | bytes 9635588 | tf_op jit(solution)/shard_map/backward/pallas_call | solution.py:40
  102.6 6.4 %all-to-all-start.3 = ((bf16[16,24,2048]{2,1,0:T(8,128)(2,1)}), bf16[16,24,2048]{2,1,0:T(8,128)(2,1)}, u32[]{:S(2)}, u32[]{:S(2)}) async-start(bf16[16,24,2048]{2,1,0:T(8,128)(2,1)} %bitcast.20), calls=%async_computation.3 | async-start | bytes 3145728 | tf_op jit(solution)/shard_map/all_to_all | solution.py:748
  112.4 3.9 %mix_partials.1 = f32[192,128]{1,0:T(8,128)} custom-call(f32[512,512]{1,0:T(8,128)} %get-tuple-element.44.yg_hbm, f32[512,512]{1,0:T(8,128)} %get-tuple-element.45.yu_hbm, f32[512,512]{1,0:T(8,128)} %get-tuple-element.46.yd_hbm, bf16[3,128,512]{2,1,0:T(8,128)(2,1)} %get-tuple-element.42.refs_2_.d_hbm), custom_call_target="tpu_custom_call" | custom-call | flops 6291456 | bytes 3637248 | tf_op jit(solution)/shard_map/mix_partials/pallas_call | solution.py:40
  120.2 11.4 %collective-permute-done.9 = f32[1,3,4,4,4]{4,3,2,1,0:T(4,128)S(1)} collective-permute-done((f32[1,3,4,4,4]{4,3,2,1,0:T(4,128)S(1)}, f32[1,3,4,4,4]{4,3,2,1,0:T(4,128)S(1)}, u32[]{:S(2)}, u32[]{:S(2)}) %collective-permute-start.9) | collective-permute-done | bytes 800 | tf_op jit(solution)/shard_map/ppermute | solution.py:714
  132.9 6.9 %factor_grad.1 = f32[3,4,512,128]{3,2,1,0:T(8,128)} custom-call(f32[192]{0:T(256)} %reshape.44.mix_ref, bf16[512,512]{1,0:T(8,128)(2,1)} %get-tuple-element.34.refs_0_, bf16[512,512]{1,0:T(8,128)(2,1)} %get-tuple-element.41.refs_1_, bf16[3,128,512]{2,1,0:T(8,128)(2,1)} %get-tuple-element.42.refs_2_.d_hbm, bf16[512,512]{1,0:T(8,128)(2,1)} %copy-done.2, ...), custom_call_target="tpu_custom_call" | custom-call | flops 1610612736 | bytes 6030080 | tf_op jit(solution)/shard_map/factor_grad/pallas_call | solution.py:40
  139.8 5.5 %all-to-all-done.3 = bf16[16,24,2048]{2,1,0:T(8,128)(2,1)} async-done(((bf16[16,24,2048]{2,1,0:T(8,128)(2,1)}), bf16[16,24,2048]{2,1,0:T(8,128)(2,1)}, u32[]{:S(2)}, u32[]{:S(2)}) %all-to-all-start.3) | async-done | bytes 1572896 | tf_op jit(solution)/shard_map/all_to_all | solution.py:748
  145.3 3.1 %sum_rows.1 = bf16[128,4096]{1,0:T(8,128)(2,1)} custom-call(bf16[256,384]{1,0:T(8,128)(2,1)} %place_rows.1.placed_hbm, bf16[384,2048]{1,0:T(8,128)(2,1)} %bitcast.13.returned_ref), custom_call_target="tpu_custom_call" | custom-call | flops 402653184 | bytes 2818048 | tf_op jit(solution)/shard_map/sum_rows/pallas_call | solution.py:40
  (42 shorter events, 17.1 us)
Async XLA Ops:
  2.5 15.5 %collective-permute-start.1 = (bf16[128,2048]{1,0:T(8,128)(2,1)}, bf16[128,2048]{1,0:T(8,128)(2,1)S(1)}, u32[]{:S(2)}, u32[]{:S(2)}) collective-permute-start(bf16[128,2048]{1,0:T(8,128)(2,1)} %get-tuple-element.29), channel_id=1, source_target_pairs={{0,4},{1,5},{2,6},{3,7},{4,0},{5,1},{6,2},{7,3},{8,12},{9,13},{10,... | collective-permute-start | bytes 1572872 | tf_op jit(solution)/shard_map/ppermute | solution.py:743
  18.0 0.8 copy-start
  21.8 43.1 %all-to-all-start.2 = ((bf16[16,24,2048]{2,1,0:T(8,128)(2,1)}), bf16[16,24,2048]{2,1,0:T(8,128)(2,1)}, u32[]{:S(2)}, u32[]{:S(2)}) async-start(bf16[16,24,2048]{2,1,0:T(8,128)(2,1)} %bitcast.18), calls=%async_computation.2 | async-start | bytes 3145728 | tf_op jit(solution)/shard_map/all_to_all | solution.py:748
  30.8 26.4 %collective-permute-start = (bf16[8,512,128]{2,1,0:T(8,128)(2,1)}, bf16[8,512,128]{2,1,0:T(8,128)(2,1)}, u32[]{:S(2)}, u32[]{:S(2)}) collective-permute-start(bf16[8,512,128]{2,1,0:T(8,128)(2,1)} %get-tuple-element.28), channel_id=1, source_target_pairs={{0,16},{16,0},{1,17},{17,1},{2,18},{18,2},{3,19},{19,3},{4,20},{20... | collective-permute-start | bytes 3145736 | tf_op jit(solution)/shard_map/ppermute | solution.py:714
  34.2 2.4 %collective-permute-start.2 = (bf16[256,512]{1,0:T(8,128)(2,1)}, bf16[256,512]{1,0:T(8,128)(2,1)S(1)}, u32[]{:S(2)}, u32[]{:S(2)}) collective-permute-start(bf16[256,512]{1,0:T(8,128)(2,1)} %get-tuple-element.31), channel_id=1, source_target_pairs={{0,1},{1,0},{2,3},{3,2},{4,5},{5,4},{6,7},{7,6},{8,9},{9,8},{10,11... | collective-permute-start | bytes 786440 | tf_op jit(solution)/shard_map/ppermute | solution.py:755
  34.9 12.6 %collective-permute-start.3 = (bf16[256,512]{1,0:T(8,128)(2,1)}, bf16[256,512]{1,0:T(8,128)(2,1)S(1)}, u32[]{:S(2)}, u32[]{:S(2)}) collective-permute-start(bf16[256,512]{1,0:T(8,128)(2,1)} %get-tuple-element.32), channel_id=1, source_target_pairs={{0,2},{1,3},{2,0},{3,1},{4,6},{5,7},{6,4},{7,5},{8,10},{9,11},{10,... | collective-permute-start | bytes 786440 | tf_op jit(solution)/shard_map/ppermute | solution.py:755
  35.2 22.0 %collective-permute-start.4 = (bf16[256,512]{1,0:T(8,128)(2,1)}, bf16[256,512]{1,0:T(8,128)(2,1)S(1)}, u32[]{:S(2)}, u32[]{:S(2)}) collective-permute-start(bf16[256,512]{1,0:T(8,128)(2,1)} %get-tuple-element.33), channel_id=1, source_target_pairs={{0,3},{1,2},{2,1},{3,0},{4,7},{5,6},{6,5},{7,4},{8,11},{9,10},{10,... | collective-permute-start | bytes 786440 | tf_op jit(solution)/shard_map/ppermute | solution.py:755
  36.7 20.6 %copy-start.6 = (bf16[256,512]{1,0:T(8,128)(2,1)}, bf16[256,512]{1,0:T(8,128)(2,1)S(1)}, u32[]{:S(2)}) copy-start(bf16[256,512]{1,0:T(8,128)(2,1)S(1)} %collective-permute-done.2.refs_2_) | copy-start | bytes 786436
  47.5 9.8 %copy-start.7 = (bf16[256,512]{1,0:T(8,128)(2,1)}, bf16[256,512]{1,0:T(8,128)(2,1)S(1)}, u32[]{:S(2)}) copy-start(bf16[256,512]{1,0:T(8,128)(2,1)S(1)} %collective-permute-done.3.refs_3_) | copy-start | bytes 786436
  57.2 0.7 copy-start.8
  64.8 9.7 %copy-start.5 = (f32[1,3,4,4,4]{4,3,2,1,0:T(4,128)S(1)}, f32[1,3,4,4,4]{4,3,2,1,0:T(4,128)}, u32[]{:S(2)}) copy-start(f32[1,3,4,4,4]{4,3,2,1,0:T(4,128)} %param.9) | copy-start | bytes 2308
  64.8 30.1 %all-to-all-start.1 = ((bf16[16,64,512]{2,1,0:T(8,128)(2,1)}), bf16[16,64,512]{2,1,0:T(8,128)(2,1)}, u32[]{:S(2)}, u32[]{:S(2)}) async-start(bf16[16,64,512]{2,1,0:T(8,128)(2,1)} %bitcast.21), calls=%async_computation.1 | async-start | bytes 2097152 | tf_op jit(solution)/shard_map/all_to_all | solution.py:748
  69.8 13.5 %collective-permute-start.5 = (bf16[4,512,128]{2,1,0:T(8,128)(2,1)}, bf16[4,512,128]{2,1,0:T(8,128)(2,1)}, u32[]{:S(2)}, u32[]{:S(2)}) collective-permute-start(bf16[4,512,128]{2,1,0:T(8,128)(2,1)} %get-tuple-element.39), channel_id=1, source_target_pairs={{0,16},{16,0},{1,17},{17,1},{2,18},{18,2},{3,19},{19,3},{4,20},{20... | collective-permute-start | bytes 1572872 | tf_op jit(solution)/shard_map/ppermute | solution.py:714
  74.2 20.7 %collective-permute-start.6 = (bf16[512,512]{1,0:T(8,128)(2,1)}, bf16[512,512]{1,0:T(8,128)(2,1)S(1)}, u32[]{:S(2)}, u32[]{:S(2)}) collective-permute-start(bf16[512,512]{1,0:T(8,128)(2,1)} %get-tuple-element.35.refs_1_), channel_id=1, source_target_pairs={{0,16},{16,0},{1,17},{17,1},{2,18},{18,2},{3,19},{19,3},{4,20},{20... | collective-permute-start | bytes 1572872 | tf_op jit(solution)/shard_map/ppermute | solution.py:714
  94.9 0.8 copy-start.2
  102.6 7.7 %copy-start.1 = (bf16[3,128,512]{2,1,0:T(8,128)(2,1)S(1)}, bf16[3,128,512]{2,1,0:T(8,128)(2,1)}, u32[]{:S(2)}) copy-start(bf16[3,128,512]{2,1,0:T(8,128)(2,1)} %get-tuple-element.42.refs_2_.d_hbm) | copy-start | bytes 1179652
  102.6 42.7 %all-to-all-start.3 = ((bf16[16,24,2048]{2,1,0:T(8,128)(2,1)}), bf16[16,24,2048]{2,1,0:T(8,128)(2,1)}, u32[]{:S(2)}, u32[]{:S(2)}) async-start(bf16[16,24,2048]{2,1,0:T(8,128)(2,1)} %bitcast.20), calls=%async_computation.3 | async-start | bytes 3145728 | tf_op jit(solution)/shard_map/all_to_all | solution.py:748
  109.0 23.1 %collective-permute-start.7 = (bf16[512,512]{1,0:T(8,128)(2,1)}, bf16[512,512]{1,0:T(8,128)(2,1)S(1)}, u32[]{:S(2)}, u32[]{:S(2)}) collective-permute-start(bf16[512,512]{1,0:T(8,128)(2,1)} %get-tuple-element.43), channel_id=1, source_target_pairs={{0,16},{16,0},{1,17},{17,1},{2,18},{18,2},{3,19},{19,3},{4,20},{20... | collective-permute-start | bytes 1572872 | tf_op jit(solution)/shard_map/ppermute | solution.py:714
  110.3 21.8 %collective-permute-start.8 = (bf16[3,128,512]{2,1,0:T(8,128)(2,1)S(1)}, bf16[3,128,512]{2,1,0:T(8,128)(2,1)}, u32[]{:S(2)}, u32[]{:S(2)}) collective-permute-start(bf16[3,128,512]{2,1,0:T(8,128)(2,1)S(1)} %copy-done.1), channel_id=1, source_target_pairs={{0,16},{16,0},{1,17},{17,1},{2,18},{18,2},{3,19},{19,3},{4,20},{20... | collective-permute-start | bytes 1179656 | tf_op jit(solution)/shard_map/ppermute | solution.py:714
  112.4 6.3 %copy-start.4 = (f32[128,128]{1,0:T(8,128)S(1)}, f32[128,128]{1,0:T(8,128)}, u32[]{:S(2)}) copy-start(f32[128,128]{1,0:T(8,128)} %get-tuple-element.47) | copy-start | bytes 196612
  117.4 14.1 %collective-permute-start.9 = (f32[1,3,4,4,4]{4,3,2,1,0:T(4,128)S(1)}, f32[1,3,4,4,4]{4,3,2,1,0:T(4,128)S(1)}, u32[]{:S(2)}, u32[]{:S(2)}) collective-permute-start(f32[1,3,4,4,4]{4,3,2,1,0:T(4,128)S(1)} %reshape.51), channel_id=1, source_target_pairs={{0,16},{16,0},{1,17},{17,1},{2,18},{18,2},{3,19},{19,3},{4,20},{20... | collective-permute-start | bytes 2312 | tf_op jit(solution)/shard_map/ppermute | solution.py:714
  132.1 0.8 copy-start.3

commit v21 on v20

--- a/solution.py
+++ b/solution.py
@@ -9,7 +9,7 @@
 
 SELECTED = 64
 NPHM = 4
-VMEM_LIMIT = 63 * 1024 * 1024
+VMEM_LIMIT = 65152 * 1024
 F32 = jnp.float32
 BF16 = jnp.bfloat16
 

time: 149 us -> 148 us (level)
  local copies, waits for them, and re-layouts: 3.95 us -> 0.9 us
  waiting for transfers between devices: 48.4 us -> 50.5 us
    unnamed x18 -> x8, local copies, waits for them, and re-layouts: 3.07 us -> 0.01 us
  transfers between devices with their start and end apart: 13 -> 13, of which waited for: 7 -> 7; matrix products, arithmetic and copies ran while one was open for 3% -> 2% of each run, Pallas kernels for 24% -> 25%
where the time goes in v21:
time: 148 us; the launch traced here: 147 us
  Pallas kernels  50.9 us (34%)
  waiting for transfers between devices  50.5 us (34%)
  starting transfers between devices  26.1 us (18%)
  blocking collectives  15.3 us (10%)
  other arithmetic  2.31 us (2%)
    pallas_call x14, Pallas kernels, call(): pl.pallas_call(body, out_shape=[x for x, _ in outs], in_specs=[place for...  50.9 us
    ppermute x3, waiting for transfers between devices, shards(): lax.ppermute(shares[k], 'exp', [(n, n ^ k) for n in range(peers)])  20.7 us
    all_to_all x3, starting transfers between devices, to_peers(): lax.all_to_all(array, 'exp', split_axis=0, concat_axis=0, tiled=True)  17.9 us
    ppermute x6, waiting for transfers between devices, across(): return lax.ppermute(array, 'seq', pair)  16.9 us
    all_to_all x1, blocking collectives, shards(): lax.all_to_all(told, 'exp', split_axis=0, concat_axis=0, tiled=True)  15.3 us
    all_to_all x3, waiting for transfers between devices, to_peers(): lax.all_to_all(array, 'exp', split_axis=0, concat_axis=0, tiled=True)  12.9 us
    ppermute x6, starting transfers between devices, across(): return lax.ppermute(array, 'seq', pair)  5.59 us
  transfers between devices with their start and end apart: 13, of which 7 were waited for; matrix products, arithmetic and copies ran while one was open for 2% of the time, Pallas kernels for 25%

profile of v21, /device:TPU:13, one launch (start us, length us, event | category | flops | bytes accessed | tf_op | source)
XLA Modules:
  0.0 147.0 jit_solution(14839219664882692468)
XLA Ops:
  0.6 1.9 %wanted_rows.1 = (s32[32,128]{1,0:T(8,128)}, s32[1,128]{1,0:T(1,128)}, bf16[128,2048]{1,0:T(8,128)(2,1)}) custom-call(s32[1]{0:T(128)} %bitcast.me_ref, s32[2,64]{1,0:T(2,128)} %bitcast.26, bf16[128,4096]{1,0:T(8,128)(2,1)} %source_ref.2), custom_call_target="tpu_custom_call" | custom-call | flops 1048576 | bytes 1590276 | tf_op jit(solution)/shard_map/wanted_rows/pallas_call | solution.py:40
  2.8 15.3 %all_to_all.26 = s32[16,2,128]{2,1,0:T(2,128)} all-to-all(s32[16,2,128]{2,1,0:T(2,128)} %bitcast.25), channel_id=1, replica_groups=mesh['seq'=2,'exp'=16] {'exp'}, dimensions={0} | all-to-all | bytes 32768 | tf_op jit(solution)/shard_map/all_to_all | solution.py:744
  18.0 2.9 %pick_tokens.1 = bf16[384,2048]{1,0:T(8,128)(2,1)} custom-call(s32[32,128]{1,0:T(8,128)} %bitcast.22, bf16[128,4096]{1,0:T(8,128)(2,1)} %source_ref.3, bf16[128,2048]{1,0:T(8,128)(2,1)} %collective-permute-done.1.crossed_ref.refs_0_), custom_call_target="tpu_custom_call" | custom-call | flops 402653184 | bytes 3162112 | tf_op jit(solution)/shard_map/pick_tokens/pallas_call | solution.py:40
  21.0 6.7 %all-to-all-start.2 = ((bf16[16,24,2048]{2,1,0:T(8,128)(2,1)}), bf16[16,24,2048]{2,1,0:T(8,128)(2,1)}, u32[]{:S(2)}, u32[]{:S(2)}) async-start(bf16[16,24,2048]{2,1,0:T(8,128)(2,1)} %bitcast.18), calls=%async_computation.2 | async-start | bytes 3145728 | tf_op jit(solution)/shard_map/all_to_all | solution.py:748
  27.6 2.4 %cut_factors.1 = (bf16[8,512,128]{2,1,0:T(8,128)(2,1)}, bf16[4,512,128]{2,1,0:T(8,128)(2,1)}) custom-call(bf16[12,512,128]{2,1,0:T(8,128)(2,1)} %bitcast.15), custom_call_target="tpu_custom_call" | custom-call | bytes 3145728 | tf_op jit(solution)/shard_map/cut_factors/pallas_call | solution.py:40
  31.3 2.1 %plane_columns.1 = (bf16[256,512]{1,0:T(8,128)(2,1)}, bf16[256,512]{1,0:T(8,128)(2,1)}, bf16[256,512]{1,0:T(8,128)(2,1)}, bf16[256,512]{1,0:T(8,128)(2,1)}) custom-call(s32[1]{0:T(128)} %bitcast.me_ref, bf16[128,4096]{1,0:T(8,128)(2,1)} %source_ref.2, bf16[128,2048]{1,0:T(8,128)(2,1)} %collective-permute-done.1.crossed_ref.refs_0_), custom_call_target="tpu_custom_call" | custom-call | bytes 2621444 | tf_op jit(solution)/shard_map/plane_columns/pallas_call | solution.py:40
  35.9 10.8 %collective-permute-done.3.refs_3_ = bf16[256,512]{1,0:T(8,128)(2,1)} collective-permute-done((bf16[256,512]{1,0:T(8,128)(2,1)}, bf16[256,512]{1,0:T(8,128)(2,1)}, u32[]{:S(2)}, u32[]{:S(2)}) %collective-permute-start.3) | collective-permute-done | bytes 262176 | tf_op jit(solution)/shard_map/ppermute | solution.py:755
  46.7 9.9 %collective-permute-done.4.refs_4_ = bf16[256,512]{1,0:T(8,128)(2,1)} collective-permute-done((bf16[256,512]{1,0:T(8,128)(2,1)}, bf16[256,512]{1,0:T(8,128)(2,1)}, u32[]{:S(2)}, u32[]{:S(2)}) %collective-permute-start.4) | collective-permute-done | bytes 262176 | tf_op jit(solution)/shard_map/ppermute | solution.py:755
  56.6 4.2 %pick_cotangent.1 = bf16[1024,512]{1,0:T(8,128)(2,1)} custom-call(s32[1]{0:T(128)} %bitcast.me_ref, s32[32,128]{1,0:T(8,128)} %bitcast.23, bf16[8,512,128]{2,1,0:T(8,128)(2,1)} %collective-permute-done.refs_0_.refs_1_, bf16[256,512]{1,0:T(8,128)(2,1)} %get-tuple-element.30.refs_1_, bf16[256,512]{1,0:T(8,128)(2,1)} %copy-done.3, ...), custom_call_target="tpu_custom_call" | custom-call | flops 1073741824 | bytes 3162116 | tf_op jit(solution)/shard_map/pick_cotangent/pallas_call | solution.py:40
  60.8 3.2 %all-to-all-done.2 = bf16[16,24,2048]{2,1,0:T(8,128)(2,1)} async-done(((bf16[16,24,2048]{2,1,0:T(8,128)(2,1)}), bf16[16,24,2048]{2,1,0:T(8,128)(2,1)}, u32[]{:S(2)}, u32[]{:S(2)}) %all-to-all-start.2) | async-done | bytes 1572896 | tf_op jit(solution)/shard_map/all_to_all | solution.py:748
  64.0 4.9 %all-to-all-start.1 = ((bf16[16,64,512]{2,1,0:T(8,128)(2,1)}), bf16[16,64,512]{2,1,0:T(8,128)(2,1)}, u32[]{:S(2)}, u32[]{:S(2)}) async-start(bf16[16,64,512]{2,1,0:T(8,128)(2,1)} %bitcast.21), calls=%async_computation.1 | async-start | bytes 2097152 | tf_op jit(solution)/shard_map/all_to_all | solution.py:748
  70.2 3.3 %order_rows.1 = (bf16[512,512]{1,0:T(8,128)(2,1)}, bf16[512,512]{1,0:T(8,128)(2,1)}) custom-call(s32[1]{0:T(128)} %bitcast.4.order_ref, s32[1,128]{1,0:T(1,128)} %get-tuple-element.27.slot_hbm, bf16[384,2048]{1,0:T(8,128)(2,1)} %bitcast.10.got_hbm), custom_call_target="tpu_custom_call" | custom-call | flops 134217728 | bytes 2621956 | tf_op jit(solution)/shard_map/order_rows/pallas_call | solution.py:40
  74.5 3.1 %join_gate_up.1.refs_2_.refs_0_ = bf16[1024,1024]{1,0:T(8,128)(2,1)} custom-call(s32[1]{0:T(128)} %bitcast.4.order_ref, bf16[3,4,512,128]{3,2,1,0:T(8,128)(2,1)} %bitcast.16, bf16[8,512,128]{2,1,0:T(8,128)(2,1)} %collective-permute-done.refs_0_.refs_1_), custom_call_target="tpu_custom_call" | custom-call | bytes 4718596 | tf_op jit(solution)/shard_map/join_gate_up/pallas_call | solution.py:40
  77.6 4.9 %collective-permute-done.5.refs_2_ = bf16[4,512,128]{2,1,0:T(8,128)(2,1)} collective-permute-done((bf16[4,512,128]{2,1,0:T(8,128)(2,1)}, bf16[4,512,128]{2,1,0:T(8,128)(2,1)}, u32[]{:S(2)}, u32[]{:S(2)}) %collective-permute-start.5) | collective-permute-done | bytes 524320 | tf_op jit(solution)/shard_map/ppermute | solution.py:714
  82.4 2.5 %join_down.1.refs_1_ = bf16[1024,512]{1,0:T(8,128)(2,1)} custom-call(s32[1]{0:T(128)} %bitcast.4.order_ref, bf16[3,4,512,128]{3,2,1,0:T(8,128)(2,1)} %bitcast.17, bf16[8,512,128]{2,1,0:T(8,128)(2,1)} %collective-permute-done.refs_0_.refs_1_, bf16[4,512,128]{2,1,0:T(8,128)(2,1)} %collective-permute-done.5.refs_2_), custom_call_target="tpu_custom_call" | custom-call | bytes 4194308 | tf_op jit(solution)/shard_map/join_down/pallas_call | solution.py:40
  85.0 5.9 %forward.1 = (f32[512,512]{1,0:T(8,128)}, f32[512,512]{1,0:T(8,128)}, f32[128,512]{1,0:T(8,128)}, f32[128,512]{1,0:T(8,128)}, f32[128,512]{1,0:T(8,128)}) custom-call(s32[1]{0:T(128)} %bitcast.4.order_ref, f32[192]{0:T(256)} %reshape.44.mix_ref, bf16[512,512]{1,0:T(8,128)(2,1)} %get-tuple-element.34.refs_0_, bf16[512,512]{1,0:T(8,128)(2,1)} %get-tuple-element.35.refs_1_, ...), custom_call_target="tpu_custom_call" | custom-call | flops 1073741824 | bytes 6030084 | tf_op jit(solution)/shard_map/forward/pallas_call | solution.py:40
  90.9 3.4 %all-to-all-done.1 = bf16[16,64,512]{2,1,0:T(8,128)(2,1)} async-done(((bf16[16,64,512]{2,1,0:T(8,128)(2,1)}), bf16[16,64,512]{2,1,0:T(8,128)(2,1)}, u32[]{:S(2)}, u32[]{:S(2)}) %all-to-all-start.1) | async-done | bytes 1048608 | tf_op jit(solution)/shard_map/all_to_all | solution.py:748
  94.3 6.9 %backward.1 = (bf16[384,2048]{1,0:T(8,128)(2,1)}, bf16[512,512]{1,0:T(8,128)(2,1)}, bf16[512,512]{1,0:T(8,128)(2,1)}, f32[512,512]{1,0:T(8,128)}, bf16[3,128,512]{2,1,0:T(8,128)(2,1)}, /*index=5*/f32[128,128]{1,0:T(8,128)}) custom-call(s32[1]{0:T(128)} %bitcast.4.order_ref, f32[192]{0:T(256)} %reshape.44.mix_ref, s32[1,128]{1,0:T(1,128)} %get-tuple-element.27.slot_hbm, ...), custom_call_target="tpu_custom_call" | custom-call | flops 1610612736 | bytes 9635588 | tf_op jit(solution)/shard_map/backward/pallas_call | solution.py:40
  101.2 6.3 %all-to-all-start.3 = ((bf16[16,24,2048]{2,1,0:T(8,128)(2,1)}), bf16[16,24,2048]{2,1,0:T(8,128)(2,1)}, u32[]{:S(2)}, u32[]{:S(2)}) async-start(bf16[16,24,2048]{2,1,0:T(8,128)(2,1)} %bitcast.20), calls=%async_computation.3 | async-start | bytes 3145728 | tf_op jit(solution)/shard_map/all_to_all | solution.py:748
  110.8 3.9 %mix_partials.1 = f32[192,128]{1,0:T(8,128)} custom-call(f32[512,512]{1,0:T(8,128)} %get-tuple-element.44.yg_hbm, f32[512,512]{1,0:T(8,128)} %get-tuple-element.45.yu_hbm, f32[512,512]{1,0:T(8,128)} %get-tuple-element.46.yd_hbm, bf16[3,128,512]{2,1,0:T(8,128)(2,1)} %get-tuple-element.42.refs_2_.d_hbm), custom_call_target="tpu_custom_call" | custom-call | flops 6291456 | bytes 3637248 | tf_op jit(solution)/shard_map/mix_partials/pallas_call | solution.py:40
  117.9 12.0 %collective-permute-done.9 = f32[1,3,4,4,4]{4,3,2,1,0:T(4,128)S(1)} collective-permute-done((f32[1,3,4,4,4]{4,3,2,1,0:T(4,128)S(1)}, f32[1,3,4,4,4]{4,3,2,1,0:T(4,128)S(1)}, u32[]{:S(2)}, u32[]{:S(2)}) %collective-permute-start.9) | collective-permute-done | bytes 800 | tf_op jit(solution)/shard_map/ppermute | solution.py:714
  130.6 6.9 %factor_grad.1 = f32[3,4,512,128]{3,2,1,0:T(8,128)} custom-call(f32[192]{0:T(256)} %reshape.44.mix_ref, bf16[512,512]{1,0:T(8,128)(2,1)} %get-tuple-element.34.refs_0_, bf16[512,512]{1,0:T(8,128)(2,1)} %get-tuple-element.41.refs_1_, bf16[3,128,512]{2,1,0:T(8,128)(2,1)} %get-tuple-element.42.refs_2_.d_hbm, ...), custom_call_target="tpu_custom_call" | custom-call | flops 1610612736 | bytes 6030080 | tf_op jit(solution)/shard_map/factor_grad/pallas_call | solution.py:40
  137.4 6.3 %all-to-all-done.3 = bf16[16,24,2048]{2,1,0:T(8,128)(2,1)} async-done(((bf16[16,24,2048]{2,1,0:T(8,128)(2,1)}), bf16[16,24,2048]{2,1,0:T(8,128)(2,1)}, u32[]{:S(2)}, u32[]{:S(2)}) %all-to-all-start.3) | async-done | bytes 1572896 | tf_op jit(solution)/shard_map/all_to_all | solution.py:748
  143.7 3.1 %sum_rows.1 = bf16[128,4096]{1,0:T(8,128)(2,1)} custom-call(bf16[256,384]{1,0:T(8,128)(2,1)} %place_rows.1.placed_hbm, bf16[384,2048]{1,0:T(8,128)(2,1)} %bitcast.13.returned_ref), custom_call_target="tpu_custom_call" | custom-call | flops 402653184 | bytes 2818048 | tf_op jit(solution)/shard_map/sum_rows/pallas_call | solution.py:40
  (32 shorter events, 13.3 us)
Async XLA Ops:
  2.5 15.5 %collective-permute-start.1 = (bf16[128,2048]{1,0:T(8,128)(2,1)}, bf16[128,2048]{1,0:T(8,128)(2,1)}, u32[]{:S(2)}, u32[]{:S(2)}) collective-permute-start(bf16[128,2048]{1,0:T(8,128)(2,1)} %get-tuple-element.29), channel_id=1, source_target_pairs={{0,4},{1,5},{2,6},{3,7},{4,0},{5,1},{6,2},{7,3},{8,12},{9,13},{10,... | collective-permute-start | bytes 1572872 | tf_op jit(solution)/shard_map/ppermute | solution.py:743
  21.0 43.1 %all-to-all-start.2 = ((bf16[16,24,2048]{2,1,0:T(8,128)(2,1)}), bf16[16,24,2048]{2,1,0:T(8,128)(2,1)}, u32[]{:S(2)}, u32[]{:S(2)}) async-start(bf16[16,24,2048]{2,1,0:T(8,128)(2,1)} %bitcast.18), calls=%async_computation.2 | async-start | bytes 3145728 | tf_op jit(solution)/shard_map/all_to_all | solution.py:748
  30.0 26.5 %collective-permute-start = (bf16[8,512,128]{2,1,0:T(8,128)(2,1)}, bf16[8,512,128]{2,1,0:T(8,128)(2,1)}, u32[]{:S(2)}, u32[]{:S(2)}) collective-permute-start(bf16[8,512,128]{2,1,0:T(8,128)(2,1)} %get-tuple-element.28), channel_id=1, source_target_pairs={{0,16},{16,0},{1,17},{17,1},{2,18},{18,2},{3,19},{19,3},{4,20},{20... | collective-permute-start | bytes 3145736 | tf_op jit(solution)/shard_map/ppermute | solution.py:714
  33.4 2.4 %collective-permute-start.2 = (bf16[256,512]{1,0:T(8,128)(2,1)}, bf16[256,512]{1,0:T(8,128)(2,1)S(1)}, u32[]{:S(2)}, u32[]{:S(2)}) collective-permute-start(bf16[256,512]{1,0:T(8,128)(2,1)} %get-tuple-element.31), channel_id=1, source_target_pairs={{0,1},{1,0},{2,3},{3,2},{4,5},{5,4},{6,7},{7,6},{8,9},{9,8},{10,11... | collective-permute-start | bytes 786440 | tf_op jit(solution)/shard_map/ppermute | solution.py:755
  34.1 12.5 %collective-permute-start.3 = (bf16[256,512]{1,0:T(8,128)(2,1)}, bf16[256,512]{1,0:T(8,128)(2,1)}, u32[]{:S(2)}, u32[]{:S(2)}) collective-permute-start(bf16[256,512]{1,0:T(8,128)(2,1)} %get-tuple-element.32), channel_id=1, source_target_pairs={{0,2},{1,3},{2,0},{3,1},{4,6},{5,7},{6,4},{7,5},{8,10},{9,11},{10,... | collective-permute-start | bytes 786440 | tf_op jit(solution)/shard_map/ppermute | solution.py:755
  34.4 22.1 %collective-permute-start.4 = (bf16[256,512]{1,0:T(8,128)(2,1)}, bf16[256,512]{1,0:T(8,128)(2,1)}, u32[]{:S(2)}, u32[]{:S(2)}) collective-permute-start(bf16[256,512]{1,0:T(8,128)(2,1)} %get-tuple-element.33), channel_id=1, source_target_pairs={{0,3},{1,2},{2,1},{3,0},{4,7},{5,6},{6,5},{7,4},{8,11},{9,10},{10,... | collective-permute-start | bytes 786440 | tf_op jit(solution)/shard_map/ppermute | solution.py:755
  35.9 20.7 %copy-start.3 = (bf16[256,512]{1,0:T(8,128)(2,1)}, bf16[256,512]{1,0:T(8,128)(2,1)S(1)}, u32[]{:S(2)}) copy-start(bf16[256,512]{1,0:T(8,128)(2,1)S(1)} %collective-permute-done.2.refs_2_) | copy-start | bytes 786436
  64.0 9.8 %copy-start.1 = (f32[1,3,4,4,4]{4,3,2,1,0:T(4,128)S(1)}, f32[1,3,4,4,4]{4,3,2,1,0:T(4,128)}, u32[]{:S(2)}) copy-start(f32[1,3,4,4,4]{4,3,2,1,0:T(4,128)} %param.9) | copy-start | bytes 2308
  64.0 30.2 %all-to-all-start.1 = ((bf16[16,64,512]{2,1,0:T(8,128)(2,1)}), bf16[16,64,512]{2,1,0:T(8,128)(2,1)}, u32[]{:S(2)}, u32[]{:S(2)}) async-start(bf16[16,64,512]{2,1,0:T(8,128)(2,1)} %bitcast.21), calls=%async_computation.1 | async-start | bytes 2097152 | tf_op jit(solution)/shard_map/all_to_all | solution.py:748
  69.0 13.5 %collective-permute-start.5 = (bf16[4,512,128]{2,1,0:T(8,128)(2,1)}, bf16[4,512,128]{2,1,0:T(8,128)(2,1)}, u32[]{:S(2)}, u32[]{:S(2)}) collective-permute-start(bf16[4,512,128]{2,1,0:T(8,128)(2,1)} %get-tuple-element.39), channel_id=1, source_target_pairs={{0,16},{16,0},{1,17},{17,1},{2,18},{18,2},{3,19},{19,3},{4,20},{20... | collective-permute-start | bytes 1572872 | tf_op jit(solution)/shard_map/ppermute | solution.py:714
  73.5 20.8 %collective-permute-start.6 = (bf16[512,512]{1,0:T(8,128)(2,1)}, bf16[512,512]{1,0:T(8,128)(2,1)}, u32[]{:S(2)}, u32[]{:S(2)}) collective-permute-start(bf16[512,512]{1,0:T(8,128)(2,1)} %get-tuple-element.35.refs_1_), channel_id=1, source_target_pairs={{0,16},{16,0},{1,17},{17,1},{2,18},{18,2},{3,19},{19,3},{4,20},{20... | collective-permute-start | bytes 1572872 | tf_op jit(solution)/shard_map/ppermute | solution.py:714
  101.2 42.6 %all-to-all-start.3 = ((bf16[16,24,2048]{2,1,0:T(8,128)(2,1)}), bf16[16,24,2048]{2,1,0:T(8,128)(2,1)}, u32[]{:S(2)}, u32[]{:S(2)}) async-start(bf16[16,24,2048]{2,1,0:T(8,128)(2,1)} %bitcast.20), calls=%async_computation.3 | async-start | bytes 3145728 | tf_op jit(solution)/shard_map/all_to_all | solution.py:748
  107.4 23.1 %collective-permute-start.7 = (bf16[512,512]{1,0:T(8,128)(2,1)}, bf16[512,512]{1,0:T(8,128)(2,1)}, u32[]{:S(2)}, u32[]{:S(2)}) collective-permute-start(bf16[512,512]{1,0:T(8,128)(2,1)} %get-tuple-element.43), channel_id=1, source_target_pairs={{0,16},{16,0},{1,17},{17,1},{2,18},{18,2},{3,19},{19,3},{4,20},{20... | collective-permute-start | bytes 1572872 | tf_op jit(solution)/shard_map/ppermute | solution.py:714
  108.7 21.8 %collective-permute-start.8 = (bf16[3,128,512]{2,1,0:T(8,128)(2,1)}, bf16[3,128,512]{2,1,0:T(8,128)(2,1)}, u32[]{:S(2)}, u32[]{:S(2)}) collective-permute-start(bf16[3,128,512]{2,1,0:T(8,128)(2,1)} %get-tuple-element.42.refs_2_.d_hbm), channel_id=1, source_target_pairs={{0,16},{16,0},{1,17},{17,1},{2,18},{18,2},{3,19},{19,3},{4,20},{20... | collective-permute-start | bytes 1179656 | tf_op jit(solution)/shard_map/ppermute | solution.py:714
  110.8 6.3 %copy-start = (f32[128,128]{1,0:T(8,128)S(1)}, f32[128,128]{1,0:T(8,128)}, u32[]{:S(2)}) copy-start(f32[128,128]{1,0:T(8,128)} %get-tuple-element.47) | copy-start | bytes 196612
  110.8 6.5 %copy-start.2 = (s32[1,2,64]{2,1,0:T(2,128)S(1)}, s32[1,2,64]{2,1,0:T(2,128)}, u32[]{:S(2)}) copy-start(s32[1,2,64]{2,1,0:T(2,128)} %param.11) | copy-start | bytes 1540
  115.9 14.1 %collective-permute-start.9 = (f32[1,3,4,4,4]{4,3,2,1,0:T(4,128)S(1)}, f32[1,3,4,4,4]{4,3,2,1,0:T(4,128)S(1)}, u32[]{:S(2)}, u32[]{:S(2)}) collective-permute-start(f32[1,3,4,4,4]{4,3,2,1,0:T(4,128)S(1)} %reshape.51), channel_id=1, source_target_pairs={{0,16},{16,0},{1,17},{17,1},{2,18},{18,2},{3,19},{19,3},{4,20},{20... | collective-permute-start | bytes 2312 | tf_op jit(solution)/shard_map/ppermute | solution.py:714
